TPU v7x, 32 devices: a whole 2x2x4 slice. The times are simulated.
32 devices in a mesh: grp: 2 (over y), blk: 4 (over z), rep: 2 (over x), sub: 2 (over core).
Axes of the slice: x: 2, y: 2, z: 4, core: 2. Of those that a mesh axis runs over, the one named last changes fastest.
Arguments:
- states: bfloat16 [4096, 256], P(('grp', 'blk', 'sub')), parts along dimension 0, may hold values from -6 to 6
- goal_distance: int32 [4096, 1], P(('grp', 'blk', 'sub')), parts along dimension 0, may hold values from 0 to 7; in each aligned block of 256 rows (0 to 255, 256 to 511, ...) at most 128 rows name the same one
- goal_row: int32 [4096], P(('grp', 'blk', 'sub')), parts along dimension 0, may hold values from 0 to 255
- episode: int32 [4096], P(('grp', 'blk', 'sub')), parts along dimension 0, may hold values from 0 to 15, never falling along the last dimension, each value on 1 to 256 neighbouring positions
- state_first: bfloat16 [256, 4096], P(None, 'rep'), may hold values from -0.375 to 0.375
- state_second: bfloat16 [4096, 256], P('rep'), may hold values from -0.09375 to 0.09375
- goal_first: bfloat16 [256, 4096], P(None, 'rep'), may hold values from -0.375 to 0.375
- goal_second: bfloat16 [4096, 256], P('rep'), may hold values from -0.09375 to 0.09375
Outputs:
- grad_state_first: float32 [512, 4096], P('grp', 'rep'), parts along dimension 0
- grad_state_second: float32 [8192, 256], P(('grp', 'rep')), parts along dimension 0
- grad_goal_first: float32 [512, 4096], P('grp', 'rep'), parts along dimension 0
- grad_goal_second: float32 [8192, 256], P(('grp', 'rep')), parts along dimension 0
There are 2 independent parts, one for each index of `grp`. A program takes and returns all parts, laid end to end along the dimension named above; an argument that names none is the same for every part. Nothing has to cross between parts.
Inputs may be any that keep to these rules, and one draw needn't show every extreme that they name: `goal_distance`: in the rows of one device each distance is named by at most 128 rows. Numbers never fall along the rows; an episode covers at most 256 rows.
All inputs are finite; a program needn't handle non-finite values.
Results may differ from a plain program's by a relative error of at most 0.0084.
Values may be sent and summed in bfloat16 or wider, within the bound.
No kernel may reach another device: no remote copies, remote signals or barrier semaphores. Data moves between devices by JAX's collectives and lax.ppermute only.
A program may use at most 64 MiB of HBM per device.

v0:
```python
import math

import jax
import jax.numpy as jnp
from jax import lax
from jax.sharding import PartitionSpec as P


def silu_slope(hidden):
    sig = jax.nn.sigmoid(hidden)
    return sig * (1.0 + hidden * (1.0 - sig))


def encoder_grads(rows_in, hidden, active, second, emb_grad):
    grad_second = jnp.einsum("nh,ne->he", active, emb_grad, preferred_element_type=jnp.float32)
    back = jnp.einsum("ne,he->nh", emb_grad, second, preferred_element_type=jnp.float32)
    back_rows = (back * silu_slope(hidden)).astype(jnp.bfloat16)
    grad_first = jnp.einsum("ns,nh->sh", rows_in, back_rows, preferred_element_type=jnp.float32)
    return (grad_first, grad_second)


def local(
    states, goal_distance, goal_row, episode, state_first, state_second, goal_first, goal_second
):
    rows_dev, width = states.shape
    owners = lax.axis_size(("blk", "sub"))
    position = lax.axis_index(("blk", "sub"))
    capacity = 4 * rows_dev // owners
    target = (position + goal_distance[:, 0]) % owners
    onehot = (target[:, None] == jnp.arange(owners, dtype=jnp.int32)[None, :]).astype(jnp.int32)
    slot_rank = jnp.sum((jnp.cumsum(onehot, axis=0) - onehot) * onehot, axis=1)
    requests = jnp.zeros((owners, capacity), jnp.int32).at[target, slot_rank].set(goal_row)
    wanted = lax.all_to_all(requests, ("blk", "sub"), split_axis=0, concat_axis=0, tiled=True)
    fetched = jnp.take(states, wanted.reshape(-1), axis=0).reshape(wanted.shape + (width,))
    replies = lax.all_to_all(fetched, ("blk", "sub"), split_axis=0, concat_axis=0, tiled=True)
    goal_states = jnp.take(
        replies.reshape(owners * capacity, width), target * capacity + slot_rank, axis=0
    )
    slab_rows = rows_dev // lax.axis_size("rep")
    state_hidden = jnp.dot(states, state_first, preferred_element_type=jnp.float32)
    state_active = jax.nn.silu(state_hidden).astype(jnp.bfloat16)
    goal_hidden = jnp.dot(goal_states, goal_first, preferred_element_type=jnp.float32)
    goal_active = jax.nn.silu(goal_hidden).astype(jnp.bfloat16)
    phi = lax.psum_scatter(
        jnp.dot(state_active, state_second, preferred_element_type=jnp.float32),
        "rep",
        scatter_dimension=0,
        tiled=True,
    ).astype(jnp.bfloat16)
    psi = lax.psum_scatter(
        jnp.dot(goal_active, goal_second, preferred_element_type=jnp.float32),
        "rep",
        scatter_dimension=0,
        tiled=True,
    ).astype(jnp.bfloat16)
    episode_own = lax.dynamic_slice_in_dim(episode, lax.axis_index("rep") * slab_rows, slab_rows, 0)
    psi_all, episode_all = (
        lax.all_gather(psi, "blk", axis=0, tiled=True),
        lax.all_gather(episode_own, "blk", axis=0, tiled=True),
    )
    batch_rows = psi_all.shape[0]
    logit_scale = 4.0 / math.sqrt(psi.shape[1])
    own_rows = lax.axis_index("blk") * slab_rows + jnp.arange(slab_rows, dtype=jnp.int32)
    columns = jnp.arange(batch_rows, dtype=jnp.int32)
    diagonal = own_rows[:, None] == columns[None, :]
    excluded = (episode_own[:, None] == episode_all[None, :]) & ~diagonal
    scores = jnp.einsum("ie,je->ij", phi, psi_all, preferred_element_type=jnp.float32) * logit_scale
    exponent = jnp.where(excluded, 0.0, jnp.exp(scores))
    totals = jnp.sum(exponent, axis=1)
    delta = (exponent / totals[:, None] - diagonal.astype(jnp.float32)).astype(jnp.bfloat16)
    phi_grad = (jnp.dot(delta, psi_all, preferred_element_type=jnp.float32) * logit_scale).astype(
        jnp.bfloat16
    )
    psi_grad = lax.psum_scatter(
        jnp.einsum("ij,ie->je", delta, phi, preferred_element_type=jnp.float32) * logit_scale,
        "blk",
        scatter_dimension=0,
        tiled=True,
    ).astype(jnp.bfloat16)
    phi_full, psi_full = (
        lax.all_gather(phi_grad, "rep", axis=0, tiled=True),
        lax.all_gather(psi_grad, "rep", axis=0, tiled=True),
    )
    state_parts = encoder_grads(states, state_hidden, state_active, state_second, phi_full)
    goal_parts = encoder_grads(goal_states, goal_hidden, goal_active, goal_second, psi_full)
    summed = lax.psum(
        (state_parts[0], state_parts[1], goal_parts[0], goal_parts[1]), ("blk", "sub")
    )
    return (summed[0], summed[1], summed[2], summed[3])


def solution(mesh):
    in_specs = (
        P(("grp", "blk", "sub"), None),
        P(("grp", "blk", "sub"), None),
        P(("grp", "blk", "sub")),
        P(("grp", "blk", "sub")),
        P(None, "rep"),
        P("rep", None),
        P(None, "rep"),
        P("rep", None),
    )
    out_specs = (P("grp", "rep"), P(("grp", "rep"), None), P("grp", "rep"), P(("grp", "rep"), None))
    return jax.shard_map(local, mesh=mesh, in_specs=in_specs, out_specs=out_specs, check_vma=False)
```

profile of v0, /device:TPU:0, one launch (start us, length us, event | category | flops | bytes accessed | tf_op | source)
XLA Modules:
  0.0 326.6 jit_solution(6313272569705230123)
XLA Ops:
  7.2 0.0 copy-start
  7.2 0.0 copy-start.1
  7.2 0.8 and_select_fusion
  8.0 0.6 reduce-window.6
  8.6 0.2 slice_reduce_fusion
  8.9 0.1 fusion.14
  9.0 0.7 or_select_fusion
  9.7 21.4 %scatter_fusion = s32[8,128]{1,0:T(8,128)S(1)} fusion(s32[8,128]{1,0:T(8,128)S(1)} %broadcast_in_dim.38, s32[256]{0:T(256)S(1)} %bitcast.47, s32[256]{0:T(256)} %param.10), kind=kCustom, calls=%fused_computation.2 | custom fusion | bytes 5120 | tf_op jit(solution)/shard_map/scatter | solution.py:32
  31.0 11.7 %all_to_all.14 = s32[8,1,128]{2,1,0:T(1,128)S(1)} all-to-all(s32[8,1,128]{2,1,0:T(1,128)S(1)} %bitcast.46), channel_id=1, replica_groups=mesh['grp'=2,'blk'=4,'rep'=2,'sub'=2] {'blk','sub'}, dimensions={0} | all-to-all | bytes 8192 | tf_op jit(solution)/shard_map/all_to_all | solution.py:33
  42.7 0.0 copy-done.1
  42.8 3.9 %gather_fusion = bf16[1024,256]{1,0:T(8,128)(2,1)S(1)} fusion(bf16[256,256]{1,0:T(8,128)(2,1)S(1)} %copy-done.1, s32[1024]{0:T(1024)S(1)} %broadcast_clamp_fusion), kind=kCustom, calls=%fused_computation | custom fusion | bytes 1052672 | tf_op jit(solution)/shard_map/jit(_take)/gather | solution.py:34
  46.7 0.0 copy-start.10
  46.7 1.0 broadcast_select_fusion
  47.7 3.5 %all-to-all-start.1 = ((bf16[8,128,256]{2,1,0:T(8,128)(2,1)}), bf16[8,128,256]{2,1,0:T(8,128)(2,1)S(1)}, u32[]{:S(2)}, u32[]{:S(2)}) async-start(bf16[8,128,256]{2,1,0:T(8,128)(2,1)} %broadcast_select_fusion), calls=%async_computation.2 | async-start | bytes 1048576 | tf_op jit(solution)/shard_map/all_to_all | solution.py:35
  51.2 0.0 reduce-scatter.6.cloned.1.call-start
  51.3 0.0 copy-done.10
  51.3 15.2 %all-to-all-done.1 = bf16[8,128,256]{2,1,0:T(8,128)(2,1)S(1)} async-done(((bf16[8,128,256]{2,1,0:T(8,128)(2,1)}), bf16[8,128,256]{2,1,0:T(8,128)(2,1)S(1)}, u32[]{:S(2)}, u32[]{:S(2)}) %all-to-all-start.1) | async-done | bytes 524320 | tf_op jit(solution)/shard_map/all_to_all | solution.py:35
  66.5 1.2 gather_fusion.1
  67.7 0.0 copy-done
  67.7 0.0 copy-start.6
  67.7 2.0 multiply_convert_fusion
  69.7 0.0 copy-done.8
  69.7 0.0 copy-done.6
  69.7 1.1 fusion.24
  70.9 0.0 reduce-scatter.6.cloned.1.call-update
  70.9 0.0 reduce-scatter.4.cloned.1.call-start
  70.9 0.0 copy-start.5
  70.9 3.3 %multiply_convert_fusion.1 = (bf16[256,2048]{1,0:T(8,128)(2,1)S(1)}, f32[256,2048]{1,0:T(8,128)}) fusion(bf16[256,256]{1,0:T(8,128)(2,1)S(1)} %copy-done.1, bf16[256,2048]{1,0:T(8,128)(2,1)} %param.12), kind=kOutput, calls=%fused_computation.10 | convolution fusion | flops 271056896 | bytes 4325376 | tf_op jit(solution)/shard_map/dot_general | solution.py:40
  74.3 0.0 copy-done.5
  74.3 1.1 fusion.23
  75.4 0.0 reduce-scatter.4.cloned.1.call-update
  75.4 0.0 reduce-scatter.8.cloned.1.call-start
  75.5 0.0 copy-done.11
  75.5 0.1 dynamic_slice.3
  75.6 0.1 dynamic-slice_bitcast_fusion
  75.6 8.7 %all-gather = s32[4,1,128]{2,1,0:T(1,128)S(1)} all-gather(s32[1,1,128]{2,1,0:T(1,128)S(1)} %dynamic-slice_bitcast_fusion), channel_id=1, replica_groups=mesh['grp'=2,'blk'=4,'rep'=2,'sub'=2] {'blk'}, dimensions={0}, use_global_device_ids=true | all-gather | bytes 2560 | tf_op jit(solution)/shard_map/all_gather | solution.py:59
  84.4 0.9 convert_element_type.42
  85.3 14.3 %all_gather.13 = bf16[512,256]{1,0:T(8,128)(2,1)S(1)} all-gather(bf16[128,256]{1,0:T(8,128)(2,1)S(1)} %convert_element_type.42), channel_id=1, replica_groups=mesh['grp'=2,'blk'=4,'rep'=2,'sub'=2] {'blk'}, dimensions={0}, use_global_device_ids=true | all-gather | bytes 327680 | tf_op jit(solution)/shard_map/all_gather | solution.py:58
  99.6 1.2 fusion.22
  100.8 0.0 copy-start.12
  100.8 0.0 copy-start.13
  100.9 0.7 copy-done.12
  101.5 2.0 convolution_multiply_fusion.2
  103.6 0.0 reduce-scatter.8.cloned.1.call-update
  103.6 0.0 all-reduce.3.cloned.1.call-start
  103.7 1.2 fusion.5
  104.9 4.9 %all_gather.14 = bf16[256,256]{1,0:T(8,128)(2,1)S(1)} all-gather(bf16[128,256]{1,0:T(8,128)(2,1)S(1)} %fusion.5), channel_id=1, replica_groups=mesh['grp'=2,'blk'=4,'rep'=2,'sub'=2] {'rep'}, dimensions={0}, use_global_device_ids=true | all-gather | bytes 196608 | tf_op jit(solution)/shard_map/all_gather | solution.py:81
  109.8 1.8 fusion.25
  111.6 4.4 %convolution_bitcast_fusion = f32[256,2048]{0,1:T(8,128)} fusion(bf16[256,256]{1,0:T(8,128)(2,1)S(1)} %copy-done.1, bf16[256,256]{1,0:T(8,128)(2,1)S(1)} %all_gather.14, bf16[2048,256]{1,0:T(8,128)(2,1)} %param.13, f32[256,2048]{1,0:T(8,128)} %get-tuple-element.25), kind=kOutput, calls=%fused_computation.3 | convolution fusion | flops 541589504 | bytes 5505024 | tf_op jit(solution)/shard_map/ns,nh->sh/dot_general | solution.py:18
  116.1 8.0 %reduce-scatter.8.cloned.1.call-done = f32[128,256]{1,0:T(8,128)} async-done(((f32[512,256]{1,0:T(8,128)}), f32[128,256]{1,0:T(8,128)}) %reduce-scatter.8.cloned.1.call-update) | async-done | bytes 131088 | tf_op jit(solution)/shard_map/reduce_scatter | solution.py:74
  124.0 0.9 convert_element_type.47
  125.0 4.9 %all_gather.15 = bf16[256,256]{1,0:T(8,128)(2,1)S(1)} all-gather(bf16[128,256]{1,0:T(8,128)(2,1)S(1)} %convert_element_type.47), channel_id=1, replica_groups=mesh['grp'=2,'blk'=4,'rep'=2,'sub'=2] {'rep'}, dimensions={0}, use_global_device_ids=true | all-gather | bytes 196608 | tf_op jit(solution)/shard_map/all_gather | solution.py:82
  129.9 1.8 fusion.26
  131.7 0.0 copy-done.7
  131.7 4.1 %fusion.2 = f32[256,2048]{1,0:T(8,128)} fusion(bf16[256,256]{1,0:T(8,128)(2,1)S(1)} %all_gather.15, bf16[2048,256]{1,0:T(8,128)(2,1)S(1)} %copy-done.7, f32[256,2048]{1,0:T(8,128)} %get-tuple-element.23, bf16[256,256]{1,0:T(8,128)(2,1)S(1)} %copy-done.9, pred[256]{0:T(512)(128)(4,1)S(1)} %get-tuple-element.20), kind=kOutput, calls=%fused_computation.12 | convolution fusion | flops 541655040 | bytes 5505280 | tf_op jit(solution)/shard_map/ns,nh->sh/dot_general | solution.py:18
  135.8 0.0 all-reduce.3.cloned.1.call-update
  135.9 175.2 %all-reduce.3.cloned.1.call-done = (f32[256,2048]{0,1:T(8,128)}, f32[2048,256]{1,0:T(8,128)}, f32[256,2048]{1,0:T(8,128)}, f32[2048,256]{1,0:T(8,128)}) async-done(((f32[256,2048]{0,1:T(8,128)}, f32[2048,256]{1,0:T(8,128)}, f32[256,2048]{1,0:T(8,128)}, f32[2048,256]{1,0:T(8,128)}), (f32[256,2048]{0,1:T(8,128)}, f32[2048,256]{1,0:T(8,128)}, f32[256,2048]{1,0:T(8,128)}, ...) | async-done | bytes 8388624 | tf_op jit(solution)/shard_map/psum | solution.py:86
  311.0 3.0 copy.15
  314.1 0.0 copy-done.4
  314.1 1.3 copy.21
  315.4 1.0 copy-done.3
  316.4 1.3 copy.22
  317.7 1.0 copy-done.2
  318.8 1.3 copy.23
  (21 shorter events, 0.1 us)
Async XLA Ops:
  7.2 60.5 %copy-start = (bf16[256,2048]{1,0:T(8,128)(2,1)S(1)}, bf16[256,2048]{1,0:T(8,128)(2,1)}, u32[]{:S(2)}) copy-start(bf16[256,2048]{1,0:T(8,128)(2,1)} %param.14) | copy-start | bytes 3145732
  7.2 35.6 %copy-start.1 = (bf16[256,256]{1,0:T(8,128)(2,1)S(1)}, bf16[256,256]{1,0:T(8,128)(2,1)}, u32[]{:S(2)}) copy-start(bf16[256,256]{1,0:T(8,128)(2,1)} %param.8) | copy-start | bytes 393220
  46.7 4.6 %copy-start.10 = (s32[256,1]{0,1:T(1,128)S(1)}, s32[256,1]{0,1:T(1,128)}, u32[]{:S(2)}) copy-start(s32[256,1]{0,1:T(1,128)} %param.9) | copy-start | bytes 3076
  47.7 18.8 %all-to-all-start.1 = ((bf16[8,128,256]{2,1,0:T(8,128)(2,1)}), bf16[8,128,256]{2,1,0:T(8,128)(2,1)S(1)}, u32[]{:S(2)}, u32[]{:S(2)}) async-start(bf16[8,128,256]{2,1,0:T(8,128)(2,1)} %broadcast_select_fusion), calls=%async_computation.2 | async-start | bytes 1048576 | tf_op jit(solution)/shard_map/all_to_all | solution.py:35
  51.2 33.2 %reduce-scatter.6.cloned.1.call-start = ((), (), s32[]{:S(2)}) async-start(), calls=%async_computation.6 | async-start | bytes 393216 | tf_op jit(solution)/shard_map/reduce_scatter | solution.py:50
  67.7 2.1 copy-start.8
  67.7 2.0 copy-start.6
  70.9 28.7 %reduce-scatter.4.cloned.1.call-start = ((), (), s32[]{:S(2)}) async-start(), calls=%async_computation.5 | async-start | bytes 393216 | tf_op jit(solution)/shard_map/reduce_scatter | solution.py:44
  70.9 3.3 %copy-start.5 = (bf16[2048,256]{1,0:T(8,128)(2,1)S(1)}, bf16[2048,256]{1,0:T(8,128)(2,1)}, u32[]{:S(2)}) copy-start(bf16[2048,256]{1,0:T(8,128)(2,1)} %param.13) | copy-start | bytes 3145732
  74.2 1.2 copy-start.11
  75.4 48.6 %reduce-scatter.8.cloned.1.call-start = ((), (), s32[]{:S(2)}) async-start(), calls=%async_computation.7 | async-start | bytes 655360 | tf_op jit(solution)/shard_map/reduce_scatter | solution.py:74
  100.8 0.7 copy-start.12
  100.8 0.7 copy-start.13
  103.6 207.4 %all-reduce.3.cloned.1.call-start = ((), (), s32[]{:S(2)}) async-start(), calls=%async_computation.8 | async-start | bytes 16777216 | tf_op jit(solution)/shard_map/psum | solution.py:86
  116.1 15.7 %copy-start.7 = (bf16[2048,256]{1,0:T(8,128)(2,1)S(1)}, bf16[2048,256]{1,0:T(8,128)(2,1)}, u32[]{:S(2)}) copy-start(bf16[2048,256]{1,0:T(8,128)(2,1)} %param.15) | copy-start | bytes 3145732
  116.1 15.7 %copy-start.9 = (bf16[256,256]{1,0:T(8,128)(2,1)S(1)}, bf16[256,256]{1,0:T(8,128)(2,1)}, u32[]{:S(2)}) copy-start(bf16[256,256]{1,0:T(8,128)(2,1)} %copy-done.8) | copy-start | bytes 393220
  311.0 3.0 copy-start.4
  314.1 2.3 copy-start.3
  316.4 2.3 copy-start.2
Sparse Core Ops, SparseCore 0:
  71.0 10.5 reduce-scatter.5
  84.5 11.6 reduce-scatter.3
  103.7 20.2 reduce-scatter.7
  136.0 174.9 all-reduce.2
where the time goes:
time: 327 us
  waiting for transfers between devices  198 us (61%)
  blocking collectives  44.6 us (14%)
  local copies, waits for them, and re-layouts  36.6 us (11%)
  matrix products  24.3 us (7%)
  between operations  14 us (4%)
  other arithmetic  5.12 us (2%)
  starting transfers between devices  3.66 us (1%)
    psum x1, waiting for transfers between devices, local(): lax.psum((state_parts[0], state_parts[1], goal_parts[0], goal_parts[1]),...  175 us
    scatter x1, local copies, waits for them, and re-layouts, local(): jnp.zeros((owners, capacity), jnp.int32).at[target, slot_rank].set(goal_row)  21.4 us
    all_to_all x1, waiting for transfers between devices, local(): lax.all_to_all(fetched, ('blk', 'sub'), split_axis=0, concat_axis=0, tile...  15.2 us
    all_gather x1, blocking collectives, local(): lax.all_gather(psi, 'blk', axis=0, tiled=True)  14.3 us
    all_to_all x1, blocking collectives, local(): lax.all_to_all(requests, ('blk', 'sub'), split_axis=0, concat_axis=0, til...  11.7 us
    unnamed x33, local copies, waits for them, and re-layouts  9.86 us
    all_gather x1, blocking collectives, local(): lax.all_gather(episode_own, 'blk', axis=0, tiled=True)  8.73 us
    dot_general x2, matrix products, encoder_grads(): jnp.einsum('ns,nh->sh', rows_in, back_rows, preferred_element_type=jnp.fl...  8.55 us
  transfers between devices with their start and end apart: 5, of which 3 were waited for; matrix products, arithmetic and copies ran while one was open for 4% of the time, Pallas kernels for 0%

commit v1 on v0

--- a/solution.py
+++ b/solution.py
@@ -1,9 +1,357 @@
+import functools
 import math
 
 import jax
 import jax.numpy as jnp
 from jax import lax
+from jax.experimental import pallas as pl
+from jax.experimental.pallas import tpu as pltpu
 from jax.sharding import PartitionSpec as P
+
+BF = jnp.bfloat16
+F32 = jnp.float32
+VMEM = 56 * 1024 * 1024
+
+
+def dot(a, b):
+    return jnp.dot(a, b, preferred_element_type=F32)
+
+
+def sigmoid(v):
+    return 0.5 * jnp.tanh(0.5 * v) + 0.5
+
+
+def whole(shape):
+    return pl.BlockSpec(shape, lambda *_: (0,) * len(shape))
+
+
+def forward_kernel(x_ref, sf_ref, gf_ref, ss_ref, gs_ref, out_ref, acc):
+    step = pl.program_id(0)
+    emb = ss_ref.shape[1]
+
+    @pl.when(step == 0)
+    def _():
+        acc[...] = jnp.zeros_like(acc)
+
+    x = x_ref[...]
+    for k, (first, second) in enumerate(((sf_ref, ss_ref), (gf_ref, gs_ref))):
+        hidden = dot(x, first[...])
+        active = (hidden * sigmoid(hidden)).astype(BF)
+        acc[:, k * emb : (k + 1) * emb] += dot(active, second[...])
+
+    @pl.when(step == pl.num_programs(0) - 1)
+    def _():
+        out_ref[...] = acc[...].astype(BF)
+
+
+def forward(x, rows, sf, gf, ss, gs):
+    width, hid = sf.shape
+    emb = ss.shape[1]
+    tile = 512
+    return pl.pallas_call(
+        forward_kernel,
+        grid=(hid // tile,),
+        in_specs=[
+            pl.BlockSpec((rows, width), lambda i: (0, 0)),
+            pl.BlockSpec((width, tile), lambda i: (0, i)),
+            pl.BlockSpec((width, tile), lambda i: (0, i)),
+            pl.BlockSpec((tile, emb), lambda i: (i, 0)),
+            pl.BlockSpec((tile, emb), lambda i: (i, 0)),
+        ],
+        out_specs=pl.BlockSpec((rows, 2 * emb), lambda i: (0, 0)),
+        out_shape=jax.ShapeDtypeStruct((rows, 2 * emb), BF),
+        scratch_shapes=[pltpu.VMEM((rows, 2 * emb), F32)],
+        compiler_params=pltpu.CompilerParams(vmem_limit_bytes=VMEM),
+        cost_estimate=pl.CostEstimate(
+            flops=8 * rows * width * hid, bytes_accessed=8 * width * hid, transcendentals=2 * rows * hid
+        ),
+        name="forward",
+    )(x, sf, gf, ss, gs)
+
+
+def place_blocks(pos_ref, mine, other, put, n_blk, n_rep, slab):
+    b, s = pos_ref[0], pos_ref[1]
+    for side, blocks in ((s, mine), (1 - s, other)):
+        for k, block in enumerate(blocks):
+            at = jnp.bitwise_xor(b, k)
+            for r in range(n_rep):
+                off = ((side * n_rep + r) * n_blk + at) * slab
+                put(pl.multiple_of(off, slab), block(r))
+
+
+def hidden_kernel(n_blk, n_rep, slab, pos_ref, *refs):
+    mine = refs[:n_blk]
+    other = refs[n_blk]
+    first_ref, all_ref, active_ref, slope_ref, states_t = refs[n_blk + 1 :]
+    rows = slab * n_rep
+    pad = other.shape[0] // n_blk
+
+    @pl.when(pl.program_id(0) == 0)
+    def _():
+        def put(off, value):
+            all_ref[pl.ds(off, slab), :] = value
+            states_t[:, pl.ds(off, slab)] = value.T
+
+        place_blocks(
+            pos_ref,
+            [functools.partial(lambda ref, r: ref[r * slab : (r + 1) * slab, :], ref) for ref in mine],
+            [
+                functools.partial(lambda k, r: other[k * pad + r * slab : k * pad + (r + 1) * slab, :], k)
+                for k in range(n_blk)
+            ],
+            put,
+            n_blk,
+            n_rep,
+            slab,
+        )
+
+    first_t = first_ref[...].T
+    chunk = 512
+    for c in range(all_ref.shape[0] // chunk):
+        cols = slice(c * chunk, (c + 1) * chunk)
+        hidden = dot(first_t, states_t[:, cols])
+        sig = sigmoid(hidden)
+        active = hidden * sig
+        active_ref[:, cols] = active.astype(BF)
+        slope_ref[:, cols] = (sig + active * (1.0 - sig)).astype(BF)
+
+
+def hidden_all(pos, mine, other, first, n_blk, n_rep, slab, quarter):
+    width = first.shape[0]
+    rows = 2 * n_blk * n_rep * slab
+    tile = 256
+    steps = quarter // tile
+    return pl.pallas_call(
+        functools.partial(hidden_kernel, n_blk, n_rep, slab),
+        grid_spec=pltpu.PrefetchScalarGridSpec(
+            num_scalar_prefetch=1,
+            grid=(steps,),
+            in_specs=[whole(m.shape) for m in mine]
+            + [whole(other.shape)]
+            + [pl.BlockSpec((width, tile), lambda i, p: (0, p[1] * steps + i))],
+            out_specs=[
+                whole((rows, width)),
+                pl.BlockSpec((tile, rows), lambda i, p: (i, 0)),
+                pl.BlockSpec((tile, rows), lambda i, p: (i, 0)),
+            ],
+            scratch_shapes=[pltpu.VMEM((width, rows), BF)],
+        ),
+        out_shape=[
+            jax.ShapeDtypeStruct((rows, width), BF),
+            jax.ShapeDtypeStruct((quarter, rows), BF),
+            jax.ShapeDtypeStruct((quarter, rows), BF),
+        ],
+        compiler_params=pltpu.CompilerParams(vmem_limit_bytes=VMEM),
+        cost_estimate=pl.CostEstimate(
+            flops=2 * rows * width * quarter, bytes_accessed=4 * rows * quarter, transcendentals=rows * quarter
+        ),
+        name="hidden_all",
+    )(pos, *mine, other, first)
+
+
+def contrast_kernel(n_blk, n_rep, slab, scale, pos_ref, *refs):
+    mine = refs[:n_blk]
+    other = refs[n_blk : 2 * n_blk]
+    (goal_row_ref, goal_col_ref, ep_row_ref, ep_col_ref) = refs[2 * n_blk : 2 * n_blk + 4]
+    phi_grad_ref, phi_grad_t_ref, sum_ref, sum_t_ref, phi_all, psi_all, total = refs[2 * n_blk + 4 :]
+    emb = phi_all.shape[1]
+    batch = n_blk * slab
+    rows = phi_all.shape[0]
+
+    def put(off, value):
+        phi_all[pl.ds(off, slab), :] = value[:, :emb]
+        psi_all[pl.ds(off, slab), :] = value[:, emb:]
+
+    def slabs(refs_):
+        return [functools.partial(lambda ref, r: ref[r * slab : (r + 1) * slab, :], ref) for ref in refs_]
+
+    place_blocks(pos_ref, slabs(mine), slabs(other), put, n_blk, n_rep, slab)
+
+    for j in range(rows // batch):
+        own = slice(j * batch, (j + 1) * batch)
+        pick = (
+            goal_col_ref[own, :1] == lax.broadcasted_iota(jnp.int32, (batch, rows), 1)
+        ).astype(F32).astype(BF)
+        psi = dot(pick, psi_all[...]).astype(BF)
+        phi = phi_all[own, :]
+        scores = lax.dot_general(phi, psi, (((1,), (1,)), ((), ())), preferred_element_type=F32) * scale
+        diagonal = lax.broadcasted_iota(jnp.int32, (batch, batch), 0) == lax.broadcasted_iota(
+            jnp.int32, (batch, batch), 1
+        )
+        same = ep_col_ref[own, :1] == ep_row_ref[:1, own]
+        exponent = jnp.where(same & ~diagonal, 0.0, jnp.exp(scores))
+        totals = jnp.sum(exponent, axis=1, keepdims=True)
+        delta = (exponent / totals - diagonal.astype(F32)).astype(BF)
+        phi_grad = dot(delta, psi) * scale
+        phi_grad_ref[own, :] = phi_grad.astype(BF)
+        phi_grad_t_ref[:, own] = phi_grad.T.astype(BF)
+        psi_grad = (dot(delta.T, phi) * scale).astype(BF)
+        put_back = (
+            goal_row_ref[:1, own] == lax.broadcasted_iota(jnp.int32, (rows, batch), 0)
+        ).astype(F32).astype(BF)
+        add = dot(put_back, psi_grad)
+        if j == 0:
+            total[...] = add
+        else:
+            total[...] += add
+    sum_ref[...] = total[...].astype(BF)
+    sum_t_ref[...] = total[...].T.astype(BF)
+
+
+def contrast(pos, mine, other, goal_row, goal_col, ep_row, ep_col, n_blk, n_rep, slab, emb):
+    rows = 2 * n_blk * n_rep * slab
+    args = (*mine, *other, goal_row, goal_col, ep_row, ep_col)
+    return pl.pallas_call(
+        functools.partial(contrast_kernel, n_blk, n_rep, slab, 4.0 / math.sqrt(emb)),
+        grid_spec=pltpu.PrefetchScalarGridSpec(
+            num_scalar_prefetch=1,
+            grid=(1,),
+            in_specs=[whole(a.shape) for a in args],
+            out_specs=[whole((rows, emb)), whole((emb, rows)), whole((rows, emb)), whole((emb, rows))],
+            scratch_shapes=[
+                pltpu.VMEM((rows, emb), BF),
+                pltpu.VMEM((rows, emb), BF),
+                pltpu.VMEM((rows, emb), F32),
+            ],
+        ),
+        out_shape=[
+            jax.ShapeDtypeStruct((rows, emb), BF),
+            jax.ShapeDtypeStruct((emb, rows), BF),
+            jax.ShapeDtypeStruct((rows, emb), BF),
+            jax.ShapeDtypeStruct((emb, rows), BF),
+        ],
+        compiler_params=pltpu.CompilerParams(vmem_limit_bytes=VMEM),
+        name="contrast",
+    )(pos, *args)
+
+
+def backward_kernel(second_ref, grad_ref, grad_t_ref, states_ref, active_ref, slope_ref, gf_ref, gs_ref):
+    gs_ref[...] = dot(active_ref[...], grad_ref[...])
+    back = (dot(second_ref[...], grad_t_ref[...]) * slope_ref[...].astype(F32)).astype(BF)
+    gf_ref[...] = dot(back, states_ref[...]).T
+
+
+def backward(pos, second, grad, grad_t, states, active, slope):
+    rows, width = states.shape
+    quarter = active.shape[0]
+    emb = second.shape[1]
+    tile = 256
+    steps = quarter // tile
+
+    def body(pos_ref, *refs):
+        backward_kernel(*refs)
+
+    return pl.pallas_call(
+        body,
+        grid_spec=pltpu.PrefetchScalarGridSpec(
+            num_scalar_prefetch=1,
+            grid=(steps,),
+            in_specs=[
+                pl.BlockSpec((tile, emb), lambda i, p: (p[1] * steps + i, 0)),
+                whole((rows, emb)),
+                whole((emb, rows)),
+                whole((rows, width)),
+                pl.BlockSpec((tile, rows), lambda i, p: (i, 0)),
+                pl.BlockSpec((tile, rows), lambda i, p: (i, 0)),
+            ],
+            out_specs=[
+                pl.BlockSpec((width, tile), lambda i, p: (0, i)),
+                pl.BlockSpec((tile, emb), lambda i, p: (i, 0)),
+            ],
+        ),
+        out_shape=[
+            jax.ShapeDtypeStruct((width, quarter), F32),
+            jax.ShapeDtypeStruct((quarter, emb), F32),
+        ],
+        compiler_params=pltpu.CompilerParams(vmem_limit_bytes=VMEM),
+        cost_estimate=pl.CostEstimate(
+            flops=6 * rows * width * quarter, bytes_accessed=4 * rows * quarter, transcendentals=0
+        ),
+        name="backward",
+    )(pos, second, grad, grad_t, states, active, slope)
+
+
+def gathered(
+    states, goal_distance, goal_row, episode, state_first, state_second, goal_first, goal_second
+):
+    rows_dev, width = states.shape
+    n_blk, n_rep, n_sub = (lax.axis_size(a) for a in ("blk", "rep", "sub"))
+    owners = n_blk * n_sub
+    slab = rows_dev // n_rep
+    rows_all = owners * rows_dev
+    emb = state_second.shape[1]
+    b, s = lax.axis_index("blk"), lax.axis_index("sub")
+    pos = jnp.stack([b, s]).astype(jnp.int32)
+    quarter = state_first.shape[1] // n_sub
+
+    def across(x, k):
+        return lax.ppermute(x, "blk", [(i, i ^ k) for i in range(n_blk)])
+
+    def swap(x, axis):
+        return lax.ppermute(x, axis, [(0, 1), (1, 0)])
+
+    owner = (b * n_sub + s + goal_distance[:, 0]) % owners
+    goal = (((owner % n_sub) * n_rep + goal_row // slab) * n_blk + owner // n_sub) * slab + goal_row % slab
+    meta = jnp.stack([goal // 256, goal % 256, episode]).astype(BF)
+    own = jnp.concatenate([states, jnp.pad(meta, ((0, 13), (0, 0)))], axis=0)
+    got = {0: own, 3: across(own, 3)}
+    got[1] = across(own, 1)
+    got[2] = across(own, 2)
+
+    weights = (state_first, goal_first, state_second, goal_second)
+    sums = {}
+    for k in (0, 3):
+        part = forward(states if k == 0 else got[k], rows_dev, *weights)
+        there = swap(part, "rep")
+        sums[k] = (part.astype(F32) + there.astype(F32)).astype(BF)
+    sums[1] = across(sums[0], 1)
+    sums[2] = across(sums[3], 1)
+
+    mine = [got[k] for k in range(n_blk)]
+    other = swap(jnp.concatenate(mine, axis=0), "sub")
+    all_states, active_s, slope_s = hidden_all(pos, mine, other, state_first, n_blk, n_rep, slab, quarter)
+    _, active_g, slope_g = hidden_all(pos, mine, other, goal_first, n_blk, n_rep, slab, quarter)
+
+    metas = jnp.stack(
+        [jnp.stack([m[rows_dev : rows_dev + 3] for m in mine])]
+        + [other.reshape(n_blk, -1, width)[:, rows_dev : rows_dev + 3]]
+    )
+    metas = metas.astype(F32).astype(jnp.int32)
+    metas = jnp.where(s == 0, metas, metas[::-1])
+    metas = jnp.take(metas, jnp.bitwise_xor(b, jnp.arange(n_blk)), axis=1)
+    metas = metas.reshape(n_sub, n_blk, 3, n_rep, slab).transpose(2, 0, 3, 1, 4).reshape(3, rows_all)
+    goal_all = metas[0] * 256 + metas[1]
+    ep_all = metas[2]
+
+    others = [swap(sums[k], "sub") for k in range(n_blk)]
+    phi_grad, phi_grad_t, psi_sum, psi_sum_t = contrast(
+        pos,
+        [sums[k] for k in range(n_blk)],
+        others,
+        goal_all[None, :],
+        goal_all[:, None],
+        ep_all[None, :],
+        ep_all[:, None],
+        n_blk,
+        n_rep,
+        slab,
+        emb,
+    )
+
+    outs = []
+    for second, grad, grad_t, active, slope in (
+        (state_second, phi_grad, phi_grad_t, active_s, slope_s),
+        (goal_second, psi_sum, psi_sum_t, active_g, slope_g),
+    ):
+        gf, gs = backward(pos, second, grad, grad_t, all_states, active, slope)
+        gf2, gs2 = swap(gf, "sub"), swap(gs, "sub")
+        outs.append(
+            jnp.where(s == 0, jnp.concatenate([gf, gf2], axis=1), jnp.concatenate([gf2, gf], axis=1))
+        )
+        outs.append(
+            jnp.where(s == 0, jnp.concatenate([gs, gs2], axis=0), jnp.concatenate([gs2, gs], axis=0))
+        )
+    return tuple(outs)
 
 
 def silu_slope(hidden):
@@ -19,7 +367,7 @@
     return (grad_first, grad_second)
 
 
-def local(
+def exchanged(
     states, goal_distance, goal_row, episode, state_first, state_second, goal_first, goal_second
 ):
     rows_dev, width = states.shape
@@ -101,4 +449,6 @@
         P("rep", None),
     )
     out_specs = (P("grp", "rep"), P(("grp", "rep"), None), P("grp", "rep"), P(("grp", "rep"), None))
+    shape = mesh.shape
+    local = gathered if (shape["blk"], shape["rep"], shape["sub"]) == (4, 2, 2) else exchanged
     return jax.shard_map(local, mesh=mesh, in_specs=in_specs, out_specs=out_specs, check_vma=False)

time: 327 us -> 106 us (0.32)
  waiting for transfers between devices: 198 us -> 8.33 us
  Pallas kernels: 0 us -> 59.5 us
  blocking collectives: 44.6 us -> 0 us
  local copies, waits for them, and re-layouts: 36.6 us -> 8.35 us
  matrix products: 24.3 us -> 0 us
  starting transfers between devices: 3.66 us -> 17 us
  between operations: 14 us -> 0.97 us
  other arithmetic: 5.12 us -> 11.2 us
    psum x1 -> x0, waiting for transfers between devices: 175 us -> none  [local(): lax.psum((state_parts[0], state_parts[1], goal_parts[0], goal_parts[1]),...]
    pallas_call x0 -> x7, Pallas kernels: none -> 59.5 us  [the longest x2 19.3 us: backward(): pl.pallas_call(body, grid_spec=pltpu.PrefetchScalarGridSpec(num_scalar_pr...]
    all_gather x4 -> x0, blocking collectives: 32.9 us -> none  [the longest x1 14.3 us: local(): lax.all_gather(psi, 'blk', axis=0, tiled=True)]
    dot_general x11 -> x0, matrix products: 24.3 us -> none  [the longest x2 8.55 us: encoder_grads(): jnp.einsum('ns,nh->sh', rows_in, back_rows, preferred_element_type=jnp.fl...]
    scatter x1 -> x0, local copies, waits for them, and re-layouts: 21.4 us -> none  [local(): jnp.zeros((owners, capacity), jnp.int32).at[target, slot_rank].set(goal_row)]
    ppermute x0 -> x16, starting transfers between devices: none -> 17 us  [the longest x5 11.9 us: across(): return lax.ppermute(x, 'blk', [(i, i ^ k) for i in range(n_blk)])]
    all_to_all x1 -> x0, waiting for transfers between devices: 15.2 us -> none  [local(): lax.all_to_all(fetched, ('blk', 'sub'), split_axis=0, concat_axis=0, tile...]
    all_to_all x1 -> x0, blocking collectives: 11.7 us -> none  [local(): lax.all_to_all(requests, ('blk', 'sub'), split_axis=0, concat_axis=0, til...]
  transfers between devices with their start and end apart: 5 -> 16, of which waited for: 3 -> 3; matrix products, arithmetic and copies ran while one was open for 4% -> 11% of each run, Pallas kernels for 0% -> 34%
where the time goes in v1:
time: 106 us; the launch traced here: 105 us
  Pallas kernels  59.5 us (56%)
  starting transfers between devices  17 us (16%)
  other arithmetic  11.2 us (11%)
  local copies, waits for them, and re-layouts  8.35 us (8%)
  waiting for transfers between devices  8.33 us (8%)
    pallas_call x2, Pallas kernels, backward(): pl.pallas_call(body, grid_spec=pltpu.PrefetchScalarGridSpec(num_scalar_pr...  19.3 us
    pallas_call x2, Pallas kernels, hidden_all(): pl.pallas_call(functools.partial(hidden_kernel, n_blk, n_rep, slab), grid...  16.1 us
    pallas_call x1, Pallas kernels, contrast(): pl.pallas_call(functools.partial(contrast_kernel, n_blk, n_rep, slab, 4.0...  13.9 us
    ppermute x5, starting transfers between devices, across(): return lax.ppermute(x, 'blk', [(i, i ^ k) for i in range(n_blk)])  11.9 us
    pallas_call x2, Pallas kernels, forward(): pl.pallas_call(forward_kernel, grid=(hid // tile,), in_specs=[pl.BlockSpe...  10.2 us
    ppermute x5, waiting for transfers between devices, across(): return lax.ppermute(x, 'blk', [(i, i ^ k) for i in range(n_blk)])  6.28 us
    ppermute x11, starting transfers between devices, swap(): return lax.ppermute(x, axis, [(0, 1), (1, 0)])  5.13 us
    unnamed x43, local copies, waits for them, and re-layouts  3.38 us
  transfers between devices with their start and end apart: 16, of which 3 were waited for; matrix products, arithmetic and copies ran while one was open for 11% of the time, Pallas kernels for 34%

profile of v1, /device:TPU:0, one launch (start us, length us, event | category | flops | bytes accessed | tf_op | source)
XLA Modules:
  0.0 105.5 jit_solution(3644432036336723613)
XLA Ops:
  0.6 0.7 convert.20
  1.3 0.7 broadcast_add_fusion
  2.0 0.7 fusion.12
  2.8 0.9 constant_dynamic-update-slice_fusion.4
  3.7 0.9 pad_maximum_fusion.refs_0_
  4.6 4.1 %collective-permute-start.10 = (bf16[272,256]{1,0:T(8,128)(2,1)S(1)}, bf16[272,256]{1,0:T(8,128)(2,1)S(1)}, u32[]{:S(2)}, u32[]{:S(2)}) collective-permute-start(bf16[272,256]{1,0:T(8,128)(2,1)S(1)} %pad_maximum_fusion.refs_0_), channel_id=1, source_target_pairs={{0,8},{4,12},{8,0},{12,4},{1,9},{5,13},{9,1},{13,5},{2,10},{6,14},... | collective-permute-start | bytes 417800 | tf_op jit(solution)/shard_map/ppermute | solution.py:288
  8.7 1.6 %collective-permute-start.9 = (bf16[272,256]{1,0:T(8,128)(2,1)S(1)}, bf16[272,256]{1,0:T(8,128)(2,1)S(1)}, u32[]{:S(2)}, u32[]{:S(2)}) collective-permute-start(bf16[272,256]{1,0:T(8,128)(2,1)S(1)} %pad_maximum_fusion.refs_0_), channel_id=1, source_target_pairs={{0,4},{4,0},{8,12},{12,8},{1,5},{5,1},{9,13},{13,9},{2,6},{6,2},{1... | collective-permute-start | bytes 417800 | tf_op jit(solution)/shard_map/ppermute | solution.py:288
  10.3 0.0 collective-permute-start.2
  10.3 5.1 %forward.2 = bf16[256,512]{1,0:T(8,128)(2,1)} custom-call(bf16[256,256]{1,0:T(8,128)(2,1)} %x_ref.1, bf16[256,2048]{1,0:T(8,128)(2,1)} %refs_5_.2, bf16[256,2048]{1,0:T(8,128)(2,1)} %refs_5_.3, bf16[2048,256]{1,0:T(8,128)(2,1)} %refs_0_.2, bf16[2048,256]{1,0:T(8,128)(2,1)} %refs_0_.3), custom_call_target="tpu_custom_call" | custom-call | flops 1073741824 | bytes 4194304 | tf_op jit(solution)/shard_map/forward/pallas_call | solution.py:51
  15.4 1.7 %collective-permute-start = (bf16[256,512]{1,0:T(8,128)(2,1)}, bf16[256,512]{1,0:T(8,128)(2,1)S(1)}, u32[]{:S(2)}, u32[]{:S(2)}) collective-permute-start(bf16[256,512]{1,0:T(8,128)(2,1)} %forward.2), channel_id=1, source_target_pairs={{0,2},{2,0},{1,3},{3,1},{4,6},{6,4},{5,7},{7,5},{8,10},{10,8},{9,1... | collective-permute-start | bytes 786440 | tf_op jit(solution)/shard_map/ppermute | solution.py:291
  17.2 0.6 pad_add_fusion.pos_ref
  17.8 0.0 copy-start.6
  17.8 1.8 %collective-permute-done.2.x_ref.refs_3_ = bf16[272,256]{1,0:T(8,128)(2,1)S(1)} collective-permute-done((bf16[272,256]{1,0:T(8,128)(2,1)S(1)}, bf16[272,256]{1,0:T(8,128)(2,1)S(1)}, u32[]{:S(2)}, u32[]{:S(2)}) %collective-permute-start.2) | collective-permute-done | bytes 139296 | tf_op jit(solution)/shard_map/ppermute | solution.py:288
  19.6 0.7 copy-done.7
  20.2 5.1 %forward.3 = bf16[256,512]{1,0:T(8,128)(2,1)} custom-call(bf16[272,256]{1,0:T(8,128)(2,1)} %copy-done.7, bf16[256,2048]{1,0:T(8,128)(2,1)} %refs_5_.2, bf16[256,2048]{1,0:T(8,128)(2,1)} %refs_5_.3, bf16[2048,256]{1,0:T(8,128)(2,1)} %refs_0_.2, bf16[2048,256]{1,0:T(8,128)(2,1)} %refs_0_.3), custom_call_target="tpu_custom_call" | custom-call | flops 1073741824 | bytes 4194304 | tf_op jit(solution)/shard_map/forward/pallas_call | solution.py:51
  25.4 1.5 %collective-permute-start.3 = (bf16[256,512]{1,0:T(8,128)(2,1)}, bf16[256,512]{1,0:T(8,128)(2,1)S(1)}, u32[]{:S(2)}, u32[]{:S(2)}) collective-permute-start(bf16[256,512]{1,0:T(8,128)(2,1)} %forward.3), channel_id=1, source_target_pairs={{0,2},{2,0},{1,3},{3,1},{4,6},{6,4},{5,7},{7,5},{8,10},{10,8},{9,1... | collective-permute-start | bytes 786440 | tf_op jit(solution)/shard_map/ppermute | solution.py:291
  26.8 0.0 collective-permute-done.9.refs_1_
  26.9 0.0 collective-permute-done.10.refs_2_
  26.9 1.0 constant_dynamic-update-slice_fusion
  27.9 0.1 collective-permute-start.11
  28.0 0.0 collective-permute-done
  28.0 0.1 add_convert_fusion.1.refs_0_
  28.1 2.6 %collective-permute-start.1 = (bf16[256,512]{1,0:T(8,128)(2,1)S(1)}, bf16[256,512]{1,0:T(8,128)(2,1)S(1)}, u32[]{:S(2)}, u32[]{:S(2)}) collective-permute-start(bf16[256,512]{1,0:T(8,128)(2,1)S(1)} %add_convert_fusion.1.refs_0_), channel_id=1, source_target_pairs={{0,4},{4,0},{8,12},{12,8},{1,5},{5,1},{9,13},{13,9},{2,6},{6,2},{1... | collective-permute-start | bytes 786440 | tf_op jit(solution)/shard_map/ppermute | solution.py:288
  30.6 2.0 %collective-permute-done.3 = bf16[256,512]{1,0:T(8,128)(2,1)S(1)} collective-permute-done((bf16[256,512]{1,0:T(8,128)(2,1)}, bf16[256,512]{1,0:T(8,128)(2,1)S(1)}, u32[]{:S(2)}, u32[]{:S(2)}) %collective-permute-start.3) | collective-permute-done | bytes 262176 | tf_op jit(solution)/shard_map/ppermute | solution.py:291
  32.7 1.0 add_convert_fusion.refs_3_
  33.7 3.7 %collective-permute-start.4 = (bf16[256,512]{1,0:T(8,128)(2,1)S(1)}, bf16[256,512]{1,0:T(8,128)(2,1)S(1)}, u32[]{:S(2)}, u32[]{:S(2)}) collective-permute-start(bf16[256,512]{1,0:T(8,128)(2,1)S(1)} %add_convert_fusion.refs_3_), channel_id=1, source_target_pairs={{0,4},{4,0},{8,12},{12,8},{1,5},{5,1},{9,13},{13,9},{2,6},{6,2},{1... | collective-permute-start | bytes 786440 | tf_op jit(solution)/shard_map/ppermute | solution.py:288
  37.4 0.7 slice_bitcast_fusion.1
  38.1 0.1 collective-permute-start.5
  38.1 0.5 collective-permute-start.8
  38.6 0.0 collective-permute-done.1.refs_1_
  38.7 0.1 collective-permute-start.6
  38.7 4.5 %collective-permute-done.4.refs_2_ = bf16[256,512]{1,0:T(8,128)(2,1)S(1)} collective-permute-done((bf16[256,512]{1,0:T(8,128)(2,1)S(1)}, bf16[256,512]{1,0:T(8,128)(2,1)S(1)}, u32[]{:S(2)}, u32[]{:S(2)}) %collective-permute-start.4) | collective-permute-done | bytes 262176 | tf_op jit(solution)/shard_map/ppermute | solution.py:288
  43.2 0.0 collective-permute-start.7
  43.2 0.0 collective-permute-done.11.refs_4_
  43.3 0.8 copy-done.19
  44.1 0.6 gather_fusion
  44.7 0.1 fusion
  44.8 1.3 %copy.17.refs_9_ = s32[2048,1]{1,0:T(8,128)} copy(s32[2048,1]{0,1:T(1,128)S(1)} %bitcast.30) | data formatting | bytes 16384 | tf_op jit(solution)/shard_map/add | solution.py:323
  46.1 1.3 %copy.18.refs_11_ = s32[2048,1]{1,0:T(8,128)} copy(s32[2048,1]{0,1:T(1,128)S(1)} %bitcast.28) | data formatting | bytes 16384 | tf_op jit(solution)/shard_map/broadcast_in_dim;squeeze | solution.py:334
  47.5 8.1 %hidden_all.2 = (bf16[2048,256]{1,0:T(8,128)(2,1)}, bf16[1024,2048]{1,0:T(8,128)(2,1)}, bf16[1024,2048]{1,0:T(8,128)(2,1)}) custom-call(s32[2]{0:T(128)} %pad_add_fusion.pos_ref, bf16[272,256]{1,0:T(8,128)(2,1)} %copy-done.16, bf16[272,256]{1,0:T(8,128)(2,1)} %copy-done.15, bf16[272,256]{1,0:T(8,128)(2,1)} %copy-done.14, bf16[272,256]{1,0:T(8,128)(2,1)} %copy-done.7, ...), custom_call_target="tpu_custom_call" | custom-call | flops 1073741824 | bytes 8388608 | tf_op jit(solution)/shard_map/hidden_all/pallas_call | solution.py:124
  55.6 0.0 collective-permute-done.5.refs_4_
  55.6 0.0 collective-permute-done.8.refs_7_
  55.6 0.0 collective-permute-done.6.refs_5_
  55.7 0.0 collective-permute-done.7.refs_6_
  55.7 0.6 copy-done.10
  56.3 0.1 copy-done.11
  56.4 0.1 copy-done.12
  56.5 0.1 copy-done.13
  56.6 13.9 %contrast.1 = (bf16[2048,256]{1,0:T(8,128)(2,1)}, bf16[256,2048]{1,0:T(8,128)(2,1)}, bf16[2048,256]{1,0:T(8,128)(2,1)}, bf16[256,2048]{1,0:T(8,128)(2,1)}) custom-call(s32[2]{0:T(128)} %pad_add_fusion.pos_ref, bf16[256,512]{1,0:T(8,128)(2,1)} %copy-done.4, bf16[256,512]{1,0:T(8,128)(2,1)} %copy-done.8, bf16[256,512]{1,0:T(8,128)(2,1)} %copy-done.9, ...), custom_call_target="tpu_custom_call" | custom-call | tf_op jit(solution)/shard_map/contrast/pallas_call | solution.py:204
  70.5 9.6 %backward.2 = (f32[256,1024]{1,0:T(8,128)}, f32[1024,256]{1,0:T(8,128)}) custom-call(s32[2]{0:T(128)} %pad_add_fusion.pos_ref, bf16[2048,256]{1,0:T(8,128)(2,1)} %refs_0_.2, bf16[2048,256]{1,0:T(8,128)(2,1)} %get-tuple-element.17.refs_1_, bf16[256,2048]{1,0:T(8,128)(2,1)} %get-tuple-element.18.refs_2_, bf16[2048,256]{1,0:T(8,128)(2,1)} %get-tuple-element.19.refs_3_, ...), custom_call_target="tpu_custom_call" | custom-call | flops 3221225472 | bytes 8388608 | tf_op jit(solution)/shard_map/backward/pallas_call | solution.py:244
  80.1 0.5 collective-permute-start.12
  80.6 8.0 %hidden_all.3 = (bf16[2048,256]{1,0:T(8,128)(2,1)}, bf16[1024,2048]{1,0:T(8,128)(2,1)}, bf16[1024,2048]{1,0:T(8,128)(2,1)}) custom-call(s32[2]{0:T(128)} %pad_add_fusion.pos_ref, bf16[272,256]{1,0:T(8,128)(2,1)} %copy-done.16, bf16[272,256]{1,0:T(8,128)(2,1)} %copy-done.15, bf16[272,256]{1,0:T(8,128)(2,1)} %copy-done.14, bf16[272,256]{1,0:T(8,128)(2,1)} %copy-done.7, ...), custom_call_target="tpu_custom_call" | custom-call | flops 1073741824 | bytes 8388608 | tf_op jit(solution)/shard_map/hidden_all/pallas_call | solution.py:124
  88.6 0.2 collective-permute-start.13
  88.8 9.7 %backward.3 = (f32[256,1024]{1,0:T(8,128)}, f32[1024,256]{1,0:T(8,128)}) custom-call(s32[2]{0:T(128)} %pad_add_fusion.pos_ref, bf16[2048,256]{1,0:T(8,128)(2,1)} %refs_0_.3, bf16[2048,256]{1,0:T(8,128)(2,1)} %get-tuple-element.24.refs_1_, bf16[256,2048]{1,0:T(8,128)(2,1)} %get-tuple-element.25.refs_2_, bf16[2048,256]{1,0:T(8,128)(2,1)} %get-tuple-element.19.refs_3_, ...), custom_call_target="tpu_custom_call" | custom-call | flops 3221225472 | bytes 8388608 | tf_op jit(solution)/shard_map/backward/pallas_call | solution.py:244
  98.5 0.3 collective-permute-start.14
  98.9 0.2 collective-permute-start.15
  99.0 0.0 collective-permute-done.12
  99.1 1.7 %maximum_select_fusion = f32[256,2048]{1,0:T(8,128)} fusion(f32[256,1024]{1,0:T(8,128)S(1)} %collective-permute-done.12, f32[256,1024]{1,0:T(8,128)S(1)} %copy-done.1, pred[]{:T(512)S(6)} %eq.12), kind=kLoop, calls=%fused_computation.1 | loop fusion | flops 1572864 | bytes 4194305 | tf_op jit(solution)/shard_map/jit(_where)/select_n | solution.py:349
  100.7 0.0 collective-permute-done.13
  100.7 1.6 %maximum_select_fusion.1 = f32[2048,256]{1,0:T(8,128)} fusion(f32[1024,256]{1,0:T(8,128)S(1)} %collective-permute-done.13, f32[1024,256]{1,0:T(8,128)S(1)} %copy-done, pred[]{:T(512)S(6)} %eq.12), kind=kLoop, calls=%fused_computation.2 | loop fusion | flops 1572864 | bytes 4194305 | tf_op jit(solution)/shard_map/jit(_where)/select_n | solution.py:352
  102.3 0.0 collective-permute-done.14
  102.3 1.6 %maximum_select_fusion.2 = f32[256,2048]{1,0:T(8,128)} fusion(f32[256,1024]{1,0:T(8,128)S(1)} %collective-permute-done.14, f32[256,1024]{1,0:T(8,128)S(1)} %copy-done.3, pred[]{:T(512)S(6)} %eq.12), kind=kLoop, calls=%fused_computation.3 | loop fusion | flops 1572864 | bytes 4194305 | tf_op jit(solution)/shard_map/jit(_where)/select_n | solution.py:349
  103.9 0.0 collective-permute-done.15
  103.9 1.6 %maximum_select_fusion.3 = f32[2048,256]{1,0:T(8,128)} fusion(f32[1024,256]{1,0:T(8,128)S(1)} %collective-permute-done.15, f32[1024,256]{1,0:T(8,128)S(1)} %copy-done.2, pred[]{:T(512)S(6)} %eq.12), kind=kLoop, calls=%fused_computation.4 | loop fusion | flops 1572864 | bytes 4194305 | tf_op jit(solution)/shard_map/jit(_where)/select_n | solution.py:352
  (53 shorter events, 0.2 us)
Async XLA Ops:
  4.6 10.8 %copy-start.16 = (bf16[272,256]{1,0:T(8,128)(2,1)}, bf16[272,256]{1,0:T(8,128)(2,1)S(1)}, u32[]{:S(2)}) copy-start(bf16[272,256]{1,0:T(8,128)(2,1)S(1)} %pad_maximum_fusion.refs_0_) | copy-start | bytes 417796
  4.6 22.2 %collective-permute-start.10 = (bf16[272,256]{1,0:T(8,128)(2,1)S(1)}, bf16[272,256]{1,0:T(8,128)(2,1)S(1)}, u32[]{:S(2)}, u32[]{:S(2)}) collective-permute-start(bf16[272,256]{1,0:T(8,128)(2,1)S(1)} %pad_maximum_fusion.refs_0_), channel_id=1, source_target_pairs={{0,8},{4,12},{8,0},{12,4},{1,9},{5,13},{9,1},{13,5},{2,10},{6,14},... | collective-permute-start | bytes 417800 | tf_op jit(solution)/shard_map/ppermute | solution.py:288
  8.7 18.1 %collective-permute-start.9 = (bf16[272,256]{1,0:T(8,128)(2,1)S(1)}, bf16[272,256]{1,0:T(8,128)(2,1)S(1)}, u32[]{:S(2)}, u32[]{:S(2)}) collective-permute-start(bf16[272,256]{1,0:T(8,128)(2,1)S(1)} %pad_maximum_fusion.refs_0_), channel_id=1, source_target_pairs={{0,4},{4,0},{8,12},{12,8},{1,5},{5,1},{9,13},{13,9},{2,6},{6,2},{1... | collective-permute-start | bytes 417800 | tf_op jit(solution)/shard_map/ppermute | solution.py:288
  10.3 9.3 %collective-permute-start.2 = (bf16[272,256]{1,0:T(8,128)(2,1)S(1)}, bf16[272,256]{1,0:T(8,128)(2,1)S(1)}, u32[]{:S(2)}, u32[]{:S(2)}) collective-permute-start(bf16[272,256]{1,0:T(8,128)(2,1)S(1)} %pad_maximum_fusion.refs_0_), channel_id=1, source_target_pairs={{0,12},{4,8},{8,4},{12,0},{1,13},{5,9},{9,5},{13,1},{2,14},{6,10},... | collective-permute-start | bytes 417800 | tf_op jit(solution)/shard_map/ppermute | solution.py:288
  15.4 12.6 %collective-permute-start = (bf16[256,512]{1,0:T(8,128)(2,1)}, bf16[256,512]{1,0:T(8,128)(2,1)S(1)}, u32[]{:S(2)}, u32[]{:S(2)}) collective-permute-start(bf16[256,512]{1,0:T(8,128)(2,1)} %forward.2), channel_id=1, source_target_pairs={{0,2},{2,0},{1,3},{3,1},{4,6},{6,4},{5,7},{7,5},{8,10},{10,8},{9,1... | collective-permute-start | bytes 786440 | tf_op jit(solution)/shard_map/ppermute | solution.py:291
  17.8 10.2 %copy-start.6 = (bf16[256,512]{1,0:T(8,128)(2,1)S(1)}, bf16[256,512]{1,0:T(8,128)(2,1)}, u32[]{:S(2)}) copy-start(bf16[256,512]{1,0:T(8,128)(2,1)} %forward.2) | copy-start | bytes 786436
  19.6 0.7 copy-start.7
  25.4 7.3 %collective-permute-start.3 = (bf16[256,512]{1,0:T(8,128)(2,1)}, bf16[256,512]{1,0:T(8,128)(2,1)S(1)}, u32[]{:S(2)}, u32[]{:S(2)}) collective-permute-start(bf16[256,512]{1,0:T(8,128)(2,1)} %forward.3), channel_id=1, source_target_pairs={{0,2},{2,0},{1,3},{3,1},{4,6},{6,4},{5,7},{7,5},{8,10},{10,8},{9,1... | collective-permute-start | bytes 786440 | tf_op jit(solution)/shard_map/ppermute | solution.py:291
  26.8 20.6 %copy-start.15 = (bf16[272,256]{1,0:T(8,128)(2,1)}, bf16[272,256]{1,0:T(8,128)(2,1)S(1)}, u32[]{:S(2)}) copy-start(bf16[272,256]{1,0:T(8,128)(2,1)S(1)} %collective-permute-done.9.refs_1_) | copy-start | bytes 417796
  26.9 20.6 %copy-start.14 = (bf16[272,256]{1,0:T(8,128)(2,1)}, bf16[272,256]{1,0:T(8,128)(2,1)S(1)}, u32[]{:S(2)}) copy-start(bf16[272,256]{1,0:T(8,128)(2,1)S(1)} %collective-permute-done.10.refs_2_) | copy-start | bytes 417796
  27.9 15.3 %collective-permute-start.11 = (bf16[1088,256]{1,0:T(8,128)(2,1)S(1)}, bf16[1088,256]{1,0:T(8,128)(2,1)S(1)}, u32[]{:S(2)}, u32[]{:S(2)}) collective-permute-start(bf16[1088,256]{1,0:T(8,128)(2,1)S(1)} %constant_dynamic-update-slice_fusion), channel_id=1, source_target_pairs={{0,1},{1,0},{2,3},{3,2},{4,5},{5,4},{6,7},{7,6},{8,9},{9,8},{10,11... | collective-permute-start | bytes 1671176 | tf_op jit(solution)/shard_map/ppermute | solution.py:291
  28.1 27.5 %copy-start.4 = (bf16[256,512]{1,0:T(8,128)(2,1)}, bf16[256,512]{1,0:T(8,128)(2,1)S(1)}, u32[]{:S(2)}) copy-start(bf16[256,512]{1,0:T(8,128)(2,1)S(1)} %add_convert_fusion.1.refs_0_) | copy-start | bytes 786436
  28.1 10.6 %collective-permute-start.1 = (bf16[256,512]{1,0:T(8,128)(2,1)S(1)}, bf16[256,512]{1,0:T(8,128)(2,1)S(1)}, u32[]{:S(2)}, u32[]{:S(2)}) collective-permute-start(bf16[256,512]{1,0:T(8,128)(2,1)S(1)} %add_convert_fusion.1.refs_0_), channel_id=1, source_target_pairs={{0,4},{4,0},{8,12},{12,8},{1,5},{5,1},{9,13},{13,9},{2,6},{6,2},{1... | collective-permute-start | bytes 786440 | tf_op jit(solution)/shard_map/ppermute | solution.py:288
  33.7 21.9 %copy-start.5 = (bf16[256,512]{1,0:T(8,128)(2,1)}, bf16[256,512]{1,0:T(8,128)(2,1)S(1)}, u32[]{:S(2)}) copy-start(bf16[256,512]{1,0:T(8,128)(2,1)S(1)} %add_convert_fusion.refs_3_) | copy-start | bytes 786436
  33.7 9.5 %collective-permute-start.4 = (bf16[256,512]{1,0:T(8,128)(2,1)S(1)}, bf16[256,512]{1,0:T(8,128)(2,1)S(1)}, u32[]{:S(2)}, u32[]{:S(2)}) collective-permute-start(bf16[256,512]{1,0:T(8,128)(2,1)S(1)} %add_convert_fusion.refs_3_), channel_id=1, source_target_pairs={{0,4},{4,0},{8,12},{12,8},{1,5},{5,1},{9,13},{13,9},{2,6},{6,2},{1... | collective-permute-start | bytes 786440 | tf_op jit(solution)/shard_map/ppermute | solution.py:288
  38.1 17.5 %collective-permute-start.5 = (bf16[256,512]{1,0:T(8,128)(2,1)S(1)}, bf16[256,512]{1,0:T(8,128)(2,1)S(1)}, u32[]{:S(2)}, u32[]{:S(2)}) collective-permute-start(bf16[256,512]{1,0:T(8,128)(2,1)S(1)} %add_convert_fusion.1.refs_0_), channel_id=1, source_target_pairs={{0,1},{1,0},{2,3},{3,2},{4,5},{5,4},{6,7},{7,6},{8,9},{9,8},{10,11... | collective-permute-start | bytes 786440 | tf_op jit(solution)/shard_map/ppermute | solution.py:291
  38.1 17.5 %collective-permute-start.8 = (bf16[256,512]{1,0:T(8,128)(2,1)S(1)}, bf16[256,512]{1,0:T(8,128)(2,1)S(1)}, u32[]{:S(2)}, u32[]{:S(2)}) collective-permute-start(bf16[256,512]{1,0:T(8,128)(2,1)S(1)} %add_convert_fusion.refs_3_), channel_id=1, source_target_pairs={{0,1},{1,0},{2,3},{3,2},{4,5},{5,4},{6,7},{7,6},{8,9},{9,8},{10,11... | collective-permute-start | bytes 786440 | tf_op jit(solution)/shard_map/ppermute | solution.py:291
  38.6 16.9 %copy-start.8 = (bf16[256,512]{1,0:T(8,128)(2,1)}, bf16[256,512]{1,0:T(8,128)(2,1)S(1)}, u32[]{:S(2)}) copy-start(bf16[256,512]{1,0:T(8,128)(2,1)S(1)} %collective-permute-done.1.refs_1_) | copy-start | bytes 786436
  38.7 17.0 %collective-permute-start.6 = (bf16[256,512]{1,0:T(8,128)(2,1)S(1)}, bf16[256,512]{1,0:T(8,128)(2,1)S(1)}, u32[]{:S(2)}, u32[]{:S(2)}) collective-permute-start(bf16[256,512]{1,0:T(8,128)(2,1)S(1)} %collective-permute-done.1.refs_1_), channel_id=1, source_target_pairs={{0,1},{1,0},{2,3},{3,2},{4,5},{5,4},{6,7},{7,6},{8,9},{9,8},{10,11... | collective-permute-start | bytes 786440 | tf_op jit(solution)/shard_map/ppermute | solution.py:291
  43.2 12.4 %copy-start.9 = (bf16[256,512]{1,0:T(8,128)(2,1)}, bf16[256,512]{1,0:T(8,128)(2,1)S(1)}, u32[]{:S(2)}) copy-start(bf16[256,512]{1,0:T(8,128)(2,1)S(1)} %collective-permute-done.4.refs_2_) | copy-start | bytes 786436
  43.2 12.5 %collective-permute-start.7 = (bf16[256,512]{1,0:T(8,128)(2,1)S(1)}, bf16[256,512]{1,0:T(8,128)(2,1)S(1)}, u32[]{:S(2)}, u32[]{:S(2)}) collective-permute-start(bf16[256,512]{1,0:T(8,128)(2,1)S(1)} %collective-permute-done.4.refs_2_), channel_id=1, source_target_pairs={{0,1},{1,0},{2,3},{3,2},{4,5},{5,4},{6,7},{7,6},{8,9},{9,8},{10,11... | collective-permute-start | bytes 786440 | tf_op jit(solution)/shard_map/ppermute | solution.py:291
  43.2 0.8 copy-start.19
  44.7 10.8 %copy-start.17 = (s32[1,2,2,4,128]{4,3,2,0,1:T(4,128)}, s32[1,2,2,4,128]{4,3,2,0,1:T(4,128)S(1)}, u32[]{:S(2)}) copy-start(s32[1,2,2,4,128]{4,3,2,0,1:T(4,128)S(1)} %get-tuple-element.32) | copy-start | bytes 24580
  44.8 10.8 %copy-start.18 = (s32[1,2,2,4,128]{4,3,2,0,1:T(4,128)}, s32[1,2,2,4,128]{4,3,2,0,1:T(4,128)S(1)}, u32[]{:S(2)}) copy-start(s32[1,2,2,4,128]{4,3,2,0,1:T(4,128)S(1)} %get-tuple-element.33) | copy-start | bytes 24580
  55.6 0.7 copy-start.10
  55.6 0.8 copy-start.11
  55.7 0.9 copy-start.12
  55.7 0.9 copy-start.13
  80.1 8.5 %copy-start = (f32[1024,256]{1,0:T(8,128)S(1)}, f32[1024,256]{1,0:T(8,128)}, u32[]{:S(2)}) copy-start(f32[1024,256]{1,0:T(8,128)} %get-tuple-element.23) | copy-start | bytes 3145732
  80.1 19.0 %collective-permute-start.12 = (f32[256,1024]{1,0:T(8,128)}, f32[256,1024]{1,0:T(8,128)S(1)}, u32[]{:S(2)}, u32[]{:S(2)}) collective-permute-start(f32[256,1024]{1,0:T(8,128)} %get-tuple-element.22), channel_id=1, source_target_pairs={{0,1},{1,0},{2,3},{3,2},{4,5},{5,4},{6,7},{7,6},{8,9},{9,8},{10,11... | collective-permute-start | bytes 3145736 | tf_op jit(solution)/shard_map/ppermute | solution.py:291
  88.6 12.1 %collective-permute-start.13 = (f32[1024,256]{1,0:T(8,128)S(1)}, f32[1024,256]{1,0:T(8,128)S(1)}, u32[]{:S(2)}, u32[]{:S(2)}) collective-permute-start(f32[1024,256]{1,0:T(8,128)S(1)} %copy-done), channel_id=1, source_target_pairs={{0,1},{1,0},{2,3},{3,2},{4,5},{5,4},{6,7},{7,6},{8,9},{9,8},{10,11... | collective-permute-start | bytes 3145736 | tf_op jit(solution)/shard_map/ppermute | solution.py:291
  88.8 10.2 %copy-start.1 = (f32[256,1024]{1,0:T(8,128)S(1)}, f32[256,1024]{1,0:T(8,128)}, u32[]{:S(2)}) copy-start(f32[256,1024]{1,0:T(8,128)} %get-tuple-element.22) | copy-start | bytes 3145732
  98.5 3.8 %collective-permute-start.14 = (f32[256,1024]{1,0:T(8,128)}, f32[256,1024]{1,0:T(8,128)S(1)}, u32[]{:S(2)}, u32[]{:S(2)}) collective-permute-start(f32[256,1024]{1,0:T(8,128)} %get-tuple-element.28), channel_id=1, source_target_pairs={{0,1},{1,0},{2,3},{3,2},{4,5},{5,4},{6,7},{7,6},{8,9},{9,8},{10,11... | collective-permute-start | bytes 3145736 | tf_op jit(solution)/shard_map/ppermute | solution.py:291
  98.9 5.0 %collective-permute-start.15 = (f32[1024,256]{1,0:T(8,128)}, f32[1024,256]{1,0:T(8,128)S(1)}, u32[]{:S(2)}, u32[]{:S(2)}) collective-permute-start(f32[1024,256]{1,0:T(8,128)} %get-tuple-element.29), channel_id=1, source_target_pairs={{0,1},{1,0},{2,3},{3,2},{4,5},{5,4},{6,7},{7,6},{8,9},{9,8},{10,11... | collective-permute-start | bytes 3145736 | tf_op jit(solution)/shard_map/ppermute | solution.py:291
  100.7 1.6 %copy-start.3 = (f32[256,1024]{1,0:T(8,128)S(1)}, f32[256,1024]{1,0:T(8,128)}, u32[]{:S(2)}) copy-start(f32[256,1024]{1,0:T(8,128)} %get-tuple-element.28) | copy-start | bytes 3145732
  102.3 1.6 %copy-start.2 = (f32[1024,256]{1,0:T(8,128)S(1)}, f32[1024,256]{1,0:T(8,128)}, u32[]{:S(2)}) copy-start(f32[1024,256]{1,0:T(8,128)} %get-tuple-element.29) | copy-start | bytes 3145732

commit v2 on v0

--- a/solution.py
+++ b/solution.py
@@ -1,9 +1,270 @@
+import functools
 import math
 
 import jax
 import jax.numpy as jnp
 from jax import lax
+from jax.experimental import pallas as pl
+from jax.experimental.pallas import tpu as pltpu
 from jax.sharding import PartitionSpec as P
+
+BF = jnp.bfloat16
+F32 = jnp.float32
+MIB = 1024 * 1024
+
+
+def dot(a, b):
+    return jnp.dot(a, b, preferred_element_type=F32)
+
+
+def sigmoid(v):
+    return 0.5 * jnp.tanh(0.5 * v) + 0.5
+
+
+def in_vmem(body, name, out_shape, args, scratch=(), limit=32, pos=None, flops=0):
+    vmem = pl.BlockSpec(memory_space=pltpu.VMEM)
+    smem = pl.BlockSpec(memory_space=pltpu.SMEM)
+    specs = [vmem] * len(args)
+    if pos is not None:
+        args = (pos, *args)
+        specs = [smem] + specs
+    return pl.pallas_call(
+        body,
+        in_specs=specs,
+        out_specs=jax.tree.map(lambda _: vmem, out_shape),
+        out_shape=out_shape,
+        scratch_shapes=scratch,
+        compiler_params=pltpu.CompilerParams(vmem_limit_bytes=limit * MIB),
+        cost_estimate=pl.CostEstimate(flops=flops, bytes_accessed=0, transcendentals=0),
+        name=name,
+    )(*args)
+
+
+def forward_kernel(x_ref, sf_ref, gf_ref, ss_ref, gs_ref, out_ref, active):
+    emb = ss_ref.shape[1]
+    for k, (first, second) in enumerate(((sf_ref, ss_ref), (gf_ref, gs_ref))):
+        for c in range(0, active.shape[1], 512):
+            hidden = dot(x_ref[...], first[:, c : c + 512])
+            active[:, c : c + 512] = (hidden * sigmoid(hidden)).astype(BF)
+        out_ref[:, k * emb : (k + 1) * emb] = dot(active[...], second[...]).astype(BF)
+
+
+def forward(x, sf, gf, ss, gs):
+    rows, width = x.shape
+    hid, emb = ss.shape
+    return in_vmem(
+        forward_kernel,
+        "forward",
+        jax.ShapeDtypeStruct((rows, 2 * emb), BF),
+        (x, sf, gf, ss, gs),
+        [pltpu.VMEM((rows, hid), BF)],
+        limit=16,
+        flops=8 * rows * width * hid,
+    )
+
+
+def place_blocks(pos_ref, mine, other, put, n_blk, n_rep, slab):
+    b, s = pos_ref[0], pos_ref[1]
+    for side, blocks in ((s, mine), (1 - s, other)):
+        for k, block in enumerate(blocks):
+            at = jnp.bitwise_xor(b, k)
+            for r in range(n_rep):
+                off = ((side * n_rep + r) * n_blk + at) * slab
+                put(pl.multiple_of(off, slab), block[r * slab : (r + 1) * slab, :])
+
+
+def arrange_kernel(n_blk, n_rep, slab, pos_ref, *refs):
+    mine, other = refs[:n_blk], refs[n_blk : 2 * n_blk]
+    all_ref, all_t_ref = refs[2 * n_blk :]
+
+    def put(off, value):
+        all_ref[pl.ds(off, slab), :] = value
+        all_t_ref[:, pl.ds(off, slab)] = value.T
+
+    place_blocks(pos_ref, mine, other, put, n_blk, n_rep, slab)
+
+
+def column(row):
+    return jnp.broadcast_to(row, (128, row.shape[1])).T[:, :1]
+
+
+def contrast_kernel(n_blk, n_rep, slab, scale, pos_ref, *refs):
+    mine, other = refs[:n_blk], refs[n_blk : 2 * n_blk]
+    meta_ref = refs[2 * n_blk]
+    phi_grad_ref, phi_grad_t_ref, sum_ref, sum_t_ref, phi_all, psi_all, total = refs[2 * n_blk + 1 :]
+    emb = phi_all.shape[1]
+    batch = n_blk * slab
+    rows = phi_all.shape[0]
+
+    def put(off, value):
+        phi_all[pl.ds(off, slab), :] = value[:, :emb]
+        psi_all[pl.ds(off, slab), :] = value[:, emb:]
+
+    place_blocks(pos_ref, mine, other, put, n_blk, n_rep, slab)
+
+    for j in range(rows // batch):
+        own = slice(j * batch, (j + 1) * batch)
+        side, r = j // n_rep, j % n_rep
+
+        def meta_row(which):
+            parts = [
+                meta_ref[(blk * 2 + side) * 8 + which : (blk * 2 + side) * 8 + which + 1, r * slab : (r + 1) * slab]
+                for blk in range(n_blk)
+            ]
+            return jnp.concatenate(parts, axis=1)
+
+        goal_row, ep_row = meta_row(0), meta_row(1)
+        goal_col, ep_col = column(goal_row.astype(F32)), column(ep_row.astype(F32))
+        pick = jnp.where(
+            goal_col.astype(jnp.int32) == lax.broadcasted_iota(jnp.int32, (batch, rows), 1), 1.0, 0.0
+        ).astype(BF)
+        psi = dot(pick, psi_all[...]).astype(BF)
+        phi = phi_all[own, :]
+        scores = lax.dot_general(phi, psi, (((1,), (1,)), ((), ())), preferred_element_type=F32) * scale
+        diagonal = lax.broadcasted_iota(jnp.int32, (batch, batch), 0) == lax.broadcasted_iota(
+            jnp.int32, (batch, batch), 1
+        )
+        same = ep_col == ep_row.astype(F32)
+        exponent = jnp.where(same & ~diagonal, 0.0, jnp.exp(scores))
+        totals = jnp.sum(exponent, axis=1, keepdims=True)
+        delta = (exponent / totals - diagonal.astype(F32)).astype(BF)
+        phi_grad = dot(delta, psi) * scale
+        phi_grad_ref[own, :] = phi_grad.astype(BF)
+        phi_grad_t_ref[:, own] = phi_grad.astype(BF).T
+        psi_grad = (dot(delta.T, phi) * scale).astype(BF)
+        put_back = jnp.where(
+            goal_row == lax.broadcasted_iota(jnp.int32, (rows, batch), 0), 1.0, 0.0
+        ).astype(BF)
+        add = dot(put_back, psi_grad)
+        if j == 0:
+            total[...] = add
+        else:
+            total[...] += add
+    sum_ref[...] = total[...].astype(BF)
+    sum_t_ref[...] = total[...].astype(BF).T
+
+
+def backward_kernel(pos_ref, first_ref, second_ref, grad_ref, grad_t_ref, states_ref, states_t_ref, gf_ref, gs_ref, active, back):
+    quarter, rows = active.shape
+    at = pl.multiple_of(pos_ref[1] * quarter, quarter)
+    first_t = first_ref[:, pl.ds(at, quarter)].T
+    second = second_ref[pl.ds(at, quarter), :]
+    chunk = 512
+    for c in range(0, rows, chunk):
+        cols = slice(c, c + chunk)
+        hidden = dot(first_t, states_t_ref[:, cols])
+        sig = sigmoid(hidden)
+        act = hidden * sig
+        active[:, cols] = act.astype(BF)
+        slope = sig + act * (1.0 - sig)
+        back[:, cols] = (dot(second, grad_t_ref[:, cols]) * slope).astype(BF)
+    gs_ref[...] = dot(active[...], grad_ref[...])
+    gf_ref[...] = dot(back[...], states_ref[...]).T
+
+
+def backward(pos, first, second, grad, grad_t, states, states_t, quarter):
+    rows, width = states.shape
+    emb = second.shape[1]
+    return in_vmem(
+        backward_kernel,
+        "backward",
+        [jax.ShapeDtypeStruct((width, quarter), F32), jax.ShapeDtypeStruct((quarter, emb), F32)],
+        (first, second, grad, grad_t, states, states_t),
+        [pltpu.VMEM((quarter, rows), BF), pltpu.VMEM((quarter, rows), BF)],
+        limit=32,
+        pos=pos,
+        flops=8 * rows * width * quarter,
+    )
+
+
+def gathered(
+    states, goal_distance, goal_row, episode, state_first, state_second, goal_first, goal_second
+):
+    rows_dev, width = states.shape
+    n_blk, n_rep, n_sub = (lax.axis_size(a) for a in ("blk", "rep", "sub"))
+    owners = n_blk * n_sub
+    slab = rows_dev // n_rep
+    rows_all = owners * rows_dev
+    emb = state_second.shape[1]
+    b, s = lax.axis_index("blk"), lax.axis_index("sub")
+    pos = jnp.stack([b, s]).astype(jnp.int32)
+    quarter = state_first.shape[1] // n_sub
+    weights = (state_first, goal_first, state_second, goal_second)
+
+    def across(x, k):
+        return lax.ppermute(x, "blk", [(i, i ^ k) for i in range(n_blk)])
+
+    def swap(x, axis):
+        return lax.ppermute(x, axis, [(0, 1), (1, 0)])
+
+    def after(x, *first):
+        return lax.optimization_barrier((x, *first))[0]
+
+    def both(part, there):
+        return (part.astype(F32) + there.astype(F32)).astype(BF)
+
+    got = {0: states, 3: across(states, 3)}
+    part0 = forward(states, *weights)
+    there0 = swap(part0, "rep")
+    got[2] = across(after(states, part0), 2)
+    part3 = forward(got[3], *weights)
+    there3 = swap(part3, "rep")
+    got[1] = across(after(states, part3), 1)
+
+    distance = after(goal_distance, part3)
+    owner = (b * n_sub + s + distance[:, 0]) % owners
+    goal = (((owner % n_sub) * n_rep + goal_row // slab) * n_blk + owner // n_sub) * slab + goal_row % slab
+    meta = jnp.pad(jnp.stack([goal, episode]), ((0, 6), (0, 0)))
+    meta_all = lax.all_gather(meta, ("blk", "sub"), axis=0, tiled=True)
+
+    sums = {0: both(part0, there0)}
+    sums[1] = across(sums[0], 1)
+    part2 = forward(got[2], *weights)
+    there2 = swap(part2, "rep")
+    sums[3] = both(part3, there3)
+    sums[2] = both(part2, there2)
+
+    others = [swap(got[k], "sub") for k in range(n_blk)]
+    all_states, all_states_t = in_vmem(
+        functools.partial(arrange_kernel, n_blk, n_rep, slab),
+        "arrange",
+        [jax.ShapeDtypeStruct((rows_all, width), BF), jax.ShapeDtypeStruct((width, rows_all), BF)],
+        (*(got[k] for k in range(n_blk)), *others),
+        pos=pos,
+        limit=16,
+    )
+
+    other_sums = [swap(sums[k], "sub") for k in range(n_blk)]
+    phi_grad, phi_grad_t, psi_sum, psi_sum_t = in_vmem(
+        functools.partial(contrast_kernel, n_blk, n_rep, slab, 4.0 / math.sqrt(emb)),
+        "contrast",
+        [
+            jax.ShapeDtypeStruct((rows_all, emb), BF),
+            jax.ShapeDtypeStruct((emb, rows_all), BF),
+            jax.ShapeDtypeStruct((rows_all, emb), BF),
+            jax.ShapeDtypeStruct((emb, rows_all), BF),
+        ],
+        (*(sums[k] for k in range(n_blk)), *other_sums, meta_all),
+        [pltpu.VMEM((rows_all, emb), BF), pltpu.VMEM((rows_all, emb), BF), pltpu.VMEM((rows_all, emb), F32)],
+        pos=pos,
+        limit=24,
+        flops=2 * rows_all * emb * (2 * rows_all + 3 * n_blk * slab),
+    )
+
+    outs = []
+    for first, second, grad, grad_t in (
+        (state_first, state_second, phi_grad, phi_grad_t),
+        (goal_first, goal_second, psi_sum, psi_sum_t),
+    ):
+        gf, gs = backward(pos, first, second, grad, grad_t, all_states, all_states_t, quarter)
+        gf2, gs2 = swap(gf, "sub"), swap(gs, "sub")
+        outs.append(
+            jnp.where(s == 0, jnp.concatenate([gf, gf2], axis=1), jnp.concatenate([gf2, gf], axis=1))
+        )
+        outs.append(
+            jnp.where(s == 0, jnp.concatenate([gs, gs2], axis=0), jnp.concatenate([gs2, gs], axis=0))
+        )
+    return tuple(outs)
 
 
 def silu_slope(hidden):
@@ -19,7 +280,7 @@
     return (grad_first, grad_second)
 
 
-def local(
+def exchanged(
     states, goal_distance, goal_row, episode, state_first, state_second, goal_first, goal_second
 ):
     rows_dev, width = states.shape
@@ -101,4 +362,6 @@
         P("rep", None),
     )
     out_specs = (P("grp", "rep"), P(("grp", "rep"), None), P("grp", "rep"), P(("grp", "rep"), None))
+    shape = mesh.shape
+    local = gathered if (shape["blk"], shape["rep"], shape["sub"]) == (4, 2, 2) else exchanged
     return jax.shard_map(local, mesh=mesh, in_specs=in_specs, out_specs=out_specs, check_vma=False)

time: 327 us -> 96.4 us (0.29)
  waiting for transfers between devices: 198 us -> 17.4 us
  Pallas kernels: 0 us -> 32.1 us
  local copies, waits for them, and re-layouts: 36.6 us -> 6.16 us
  blocking collectives: 44.6 us -> 14.2 us
  matrix products: 24.3 us -> 0 us
  between operations: 14 us -> 0.85 us
  other arithmetic: 5.12 us -> 13.9 us
  starting transfers between devices: 3.66 us -> 11.4 us
    psum x1 -> x0, waiting for transfers between devices: 175 us -> none  [local(): lax.psum((state_parts[0], state_parts[1], goal_parts[0], goal_parts[1]),...]
    pallas_call x0 -> x7, Pallas kernels: none -> 32.1 us  [in_vmem(): pl.pallas_call(body, in_specs=specs, out_specs=jax.tree.map(lambda _: vme...]
    dot_general x11 -> x0, matrix products: 24.3 us -> none  [the longest x2 8.55 us: encoder_grads(): jnp.einsum('ns,nh->sh', rows_in, back_rows, preferred_element_type=jnp.fl...]
    scatter x1 -> x0, local copies, waits for them, and re-layouts: 21.4 us -> none  [local(): jnp.zeros((owners, capacity), jnp.int32).at[target, slot_rank].set(goal_row)]
    all_gather x4 -> x1, blocking collectives: 32.9 us -> 14.2 us  [gathered(): meta_all = lax.all_gather(meta, ('blk', 'sub'), axis=0, tiled=True)]
    ppermute x0 -> x19, waiting for transfers between devices: none -> 17.4 us  [the longest x4 10.8 us: across(): return lax.ppermute(x, 'blk', [(i, i ^ k) for i in range(n_blk)])]
    all_to_all x1 -> x0, waiting for transfers between devices: 15.2 us -> none  [local(): lax.all_to_all(fetched, ('blk', 'sub'), split_axis=0, concat_axis=0, tile...]
    all_to_all x1 -> x0, blocking collectives: 11.7 us -> none  [local(): lax.all_to_all(requests, ('blk', 'sub'), split_axis=0, concat_axis=0, til...]
  transfers between devices with their start and end apart: 5 -> 19, of which waited for: 3 -> 3; matrix products, arithmetic and copies ran while one was open for 4% -> 13% of each run, Pallas kernels for 0% -> 14%
where the time goes in v2:
time: 96.4 us; the launch traced here: 96 us
  Pallas kernels  32.1 us (33%)
  waiting for transfers between devices  17.4 us (18%)
  blocking collectives  14.2 us (15%)
  other arithmetic  13.9 us (14%)
  starting transfers between devices  11.4 us (12%)
  local copies, waits for them, and re-layouts  6.16 us (6%)
    pallas_call x7, Pallas kernels, in_vmem(): pl.pallas_call(body, in_specs=specs, out_specs=jax.tree.map(lambda _: vme...  32.1 us
    all_gather x1, blocking collectives, gathered(): meta_all = lax.all_gather(meta, ('blk', 'sub'), axis=0, tiled=True)  14.2 us
    ppermute x4, waiting for transfers between devices, across(): return lax.ppermute(x, 'blk', [(i, i ^ k) for i in range(n_blk)])  10.8 us
    select_n x2, other arithmetic, gathered(): jnp.where(s == 0, jnp.concatenate([gf, gf2], axis=1), jnp.concatenate([gf...  7.25 us
    ppermute x15, waiting for transfers between devices, swap(): return lax.ppermute(x, axis, [(0, 1), (1, 0)])  6.59 us
    unnamed x24, local copies, waits for them, and re-layouts  6.15 us
    ppermute x4, starting transfers between devices, across(): return lax.ppermute(x, 'blk', [(i, i ^ k) for i in range(n_blk)])  5.77 us
    ppermute x15, starting transfers between devices, swap(): return lax.ppermute(x, axis, [(0, 1), (1, 0)])  5.63 us
  transfers between devices with their start and end apart: 19, of which 3 were waited for; matrix products, arithmetic and copies ran while one was open for 13% of the time, Pallas kernels for 14%

profile of v2, /device:TPU:0, one launch (start us, length us, event | category | flops | bytes accessed | tf_op | source)
XLA Modules:
  0.0 96.0 jit_solution(871640544337356467)
XLA Ops:
  0.6 5.1 %collective-permute-start.4 = (bf16[256,256]{1,0:T(8,128)(2,1)}, bf16[256,256]{1,0:T(8,128)(2,1)S(1)}, u32[]{:S(2)}, u32[]{:S(2)}) collective-permute-start(bf16[256,256]{1,0:T(8,128)(2,1)} %refs_0_.1), channel_id=1, source_target_pairs={{0,12},{4,8},{8,4},{12,0},{1,13},{5,9},{9,5},{13,1},{2,14},{6,10},... | collective-permute-start | bytes 393224 | tf_op jit(solution)/shard_map/ppermute | solution.py:195
  5.7 0.0 collective-permute-start.11
  5.8 1.2 %copy-done = bf16[256,2048]{1,0:T(8,128)(2,1)S(1)} copy-done((bf16[256,2048]{1,0:T(8,128)(2,1)S(1)}, bf16[256,2048]{1,0:T(8,128)(2,1)}, u32[]{:S(2)}) %copy-start) | copy-done | bytes 1048600
  7.0 1.2 %copy-done.2 = bf16[2048,256]{1,0:T(8,128)(2,1)S(1)} copy-done((bf16[2048,256]{1,0:T(8,128)(2,1)S(1)}, bf16[2048,256]{1,0:T(8,128)(2,1)}, u32[]{:S(2)}) %copy-start.2) | copy-done | bytes 1048600
  8.2 1.2 %copy-done.4 = bf16[256,2048]{1,0:T(8,128)(2,1)S(1)} copy-done((bf16[256,2048]{1,0:T(8,128)(2,1)S(1)}, bf16[256,2048]{1,0:T(8,128)(2,1)}, u32[]{:S(2)}) %copy-start.4) | copy-done | bytes 1048600
  9.4 1.2 %copy-done.6 = bf16[2048,256]{1,0:T(8,128)(2,1)S(1)} copy-done((bf16[2048,256]{1,0:T(8,128)(2,1)S(1)}, bf16[2048,256]{1,0:T(8,128)(2,1)}, u32[]{:S(2)}) %copy-start.6) | copy-done | bytes 1048600
  10.7 2.4 %forward.3 = bf16[256,512]{1,0:T(8,128)(2,1)S(1)} custom-call(bf16[256,256]{1,0:T(8,128)(2,1)} %refs_0_.1, bf16[256,2048]{1,0:T(8,128)(2,1)S(1)} %copy-done, bf16[256,2048]{1,0:T(8,128)(2,1)S(1)} %copy-done.4, bf16[2048,256]{1,0:T(8,128)(2,1)S(1)} %copy-done.2, bf16[2048,256]{1,0:T(8,128)(2,1)S(1)} %copy-done.6), custom_call_target="tpu_custom_call" | custom-call | flops 1073741824 | tf_op jit(solution)/shard_map/forward/pallas_call | solution.py:31
  13.1 1.6 %collective-permute-start = (bf16[256,512]{1,0:T(8,128)(2,1)S(1)}, bf16[256,512]{1,0:T(8,128)(2,1)}, u32[]{:S(2)}, u32[]{:S(2)}) collective-permute-start(bf16[256,512]{1,0:T(8,128)(2,1)S(1)} %forward.3), channel_id=1, source_target_pairs={{0,2},{2,0},{1,3},{3,1},{4,6},{6,4},{5,7},{7,5},{8,10},{10,8},{9,1... | collective-permute-start | bytes 786440 | tf_op jit(solution)/shard_map/ppermute | solution.py:198
  14.6 0.0 collective-permute-start.2
  14.6 0.1 pad_add_fusion.1.pos_ref
  14.7 0.0 collective-permute-done.4.x_ref.refs_3_
  14.7 0.0 copy-start.7
  14.8 1.2 %copy-done.7 = bf16[2048,256]{1,0:T(8,128)(2,1)S(1)} copy-done((bf16[2048,256]{1,0:T(8,128)(2,1)S(1)}, bf16[2048,256]{1,0:T(8,128)(2,1)}, u32[]{:S(2)}) %copy-start.7) | copy-done | bytes 1048600
  16.0 1.4 %forward.5 = bf16[256,512]{1,0:T(8,128)(2,1)S(1)} custom-call(bf16[256,256]{1,0:T(8,128)(2,1)S(1)} %collective-permute-done.4.x_ref.refs_3_, bf16[256,2048]{1,0:T(8,128)(2,1)S(1)} %copy-done.1, bf16[256,2048]{1,0:T(8,128)(2,1)S(1)} %copy-done.5, bf16[2048,256]{1,0:T(8,128)(2,1)S(1)} %copy-done.3, bf16[2048,256]{1,0:T(8,128)(2,1)S(1)} %copy-done.7), custom_call_target="tpu_custom_call" | custom-call | flops 1073741824 | tf_op jit(solution)/shard_map/forward/pallas_call | solution.py:31
  17.3 0.0 copy-start.10
  17.4 0.6 collective-permute-start.5
  18.0 0.7 collective-permute-start.10
  18.6 4.8 %collective-permute-done.2.x_ref.refs_2_ = bf16[256,256]{1,0:T(8,128)(2,1)} collective-permute-done((bf16[256,256]{1,0:T(8,128)(2,1)}, bf16[256,256]{1,0:T(8,128)(2,1)}, u32[]{:S(2)}, u32[]{:S(2)}) %collective-permute-start.2) | collective-permute-done | bytes 131104 | tf_op jit(solution)/shard_map/ppermute | solution.py:195
  23.4 2.3 %forward.4 = bf16[256,512]{1,0:T(8,128)(2,1)S(1)} custom-call(bf16[256,256]{1,0:T(8,128)(2,1)} %collective-permute-done.2.x_ref.refs_2_, bf16[256,2048]{1,0:T(8,128)(2,1)S(1)} %copy-done.1, bf16[256,2048]{1,0:T(8,128)(2,1)S(1)} %copy-done.5, bf16[2048,256]{1,0:T(8,128)(2,1)S(1)} %copy-done.3, bf16[2048,256]{1,0:T(8,128)(2,1)S(1)} %copy-done.7), custom_call_target="tpu_custom_call" | custom-call | flops 1073741824 | tf_op jit(solution)/shard_map/forward/pallas_call | solution.py:31
  25.7 0.0 copy-start.9
  25.7 0.0 copy-start.11
  25.7 0.6 collective-permute-start.3
  26.3 0.0 collective-permute-done
  26.3 0.1 collective-permute-start.14
  26.4 1.0 %add_convert_fusion.2.refs_0_ = bf16[256,512]{1,0:T(8,128)(2,1)S(1)} fusion(bf16[256,512]{1,0:T(8,128)(2,1)} %collective-permute-done, bf16[256,512]{1,0:T(8,128)(2,1)S(1)} %forward.3), kind=kLoop, calls=%fused_computation.6 | loop fusion | flops 524288 | bytes 786432 | tf_op jit(solution)/shard_map/convert_element_type | solution.py:204
  27.4 6.5 %collective-permute-done.3 = bf16[256,512]{1,0:T(8,128)(2,1)S(1)} collective-permute-done((bf16[256,512]{1,0:T(8,128)(2,1)S(1)}, bf16[256,512]{1,0:T(8,128)(2,1)S(1)}, u32[]{:S(2)}, u32[]{:S(2)}) %collective-permute-start.3) | collective-permute-done | bytes 262176 | tf_op jit(solution)/shard_map/ppermute | solution.py:198
  33.9 0.0 collective-permute-start.1
  33.9 0.1 add_convert_fusion.1.refs_2_
  34.0 0.0 collective-permute-done.5
  34.0 0.1 collective-permute-start.13
  34.1 0.1 add_convert_fusion.refs_3_
  34.2 0.0 collective-permute-done.11.refs_4_
  34.2 0.6 collective-permute-start.6
  34.7 0.0 collective-permute-done.14.refs_7_
  34.8 0.1 collective-permute-start.8
  34.8 0.0 collective-permute-done.10.refs_1_
  34.8 0.4 collective-permute-start.9
  35.3 6.0 %collective-permute-done.1.refs_1_ = bf16[256,512]{1,0:T(8,128)(2,1)S(1)} collective-permute-done((bf16[256,512]{1,0:T(8,128)(2,1)S(1)}, bf16[256,512]{1,0:T(8,128)(2,1)S(1)}, u32[]{:S(2)}, u32[]{:S(2)}) %collective-permute-start.1) | collective-permute-done | bytes 262176 | tf_op jit(solution)/shard_map/ppermute | solution.py:195
  41.3 0.0 collective-permute-start.7
  41.3 0.0 collective-permute-done.13.refs_6_
  41.3 0.6 collective-permute-start.12
  41.9 14.2 %all_gather.3.refs_8_ = s32[64,256]{1,0:T(8,128)S(1)} all-gather(s32[8,256]{1,0:T(8,128)S(1)} %pad.4), channel_id=1, replica_groups=mesh['grp'=2,'blk'=4,'rep'=2,'sub'=2] {'blk','sub'}, dimensions={0}, use_global_device_ids=true | all-gather | bytes 73728 | tf_op jit(solution)/shard_map/all_gather | solution.py:218
  56.1 0.0 collective-permute-done.12.refs_5_
  56.1 1.4 %arrange.1 = (bf16[2048,256]{1,0:T(8,128)(2,1)S(1)}, bf16[256,2048]{1,0:T(8,128)(2,1)S(1)}) custom-call(s32[2]{0:T(128)S(1)} %pad_add_fusion.1.pos_ref, bf16[256,256]{1,0:T(8,128)(2,1)} %refs_0_.1, bf16[256,256]{1,0:T(8,128)(2,1)S(1)} %collective-permute-done.10.refs_1_, bf16[256,256]{1,0:T(8,128)(2,1)} %collective-permute-done.2.x_ref.refs_2_, ...), custom_call_target="tpu_custom_call" | custom-call | tf_op jit(solution)/shard_map/arrange/pallas_call | solution.py:31
  57.5 0.0 collective-permute-done.6.refs_4_
  57.5 0.0 collective-permute-done.8.refs_6_
  57.5 0.0 collective-permute-done.9.refs_7_
  57.6 0.0 collective-permute-done.7.refs_5_
  57.6 10.9 %contrast.1 = (bf16[2048,256]{1,0:T(8,128)(2,1)S(1)}, bf16[256,2048]{1,0:T(8,128)(2,1)S(1)}, bf16[2048,256]{1,0:T(8,128)(2,1)S(1)}, bf16[256,2048]{1,0:T(8,128)(2,1)S(1)}) custom-call(s32[2]{0:T(128)S(1)} %pad_add_fusion.1.pos_ref, bf16[256,512]{1,0:T(8,128)(2,1)S(1)} %add_convert_fusion.2.refs_0_, bf16[256,512]{1,0:T(8,128)(2,1)S(1)} %collective-permute-done.1.refs_1_, ...), custom_call_target="tpu_custom_call" | custom-call | flops 5905580032 | tf_op jit(solution)/shard_map/contrast/pallas_call | solution.py:31
  68.4 0.0 copy-start.8
  68.5 7.6 %backward.2 = (f32[256,1024]{1,0:T(8,128)}, f32[1024,256]{1,0:T(8,128)}) custom-call(s32[2]{0:T(128)S(1)} %pad_add_fusion.1.pos_ref, bf16[256,2048]{1,0:T(8,128)(2,1)S(1)} %copy-done.1, bf16[2048,256]{1,0:T(8,128)(2,1)S(1)} %copy-done.3, bf16[2048,256]{1,0:T(8,128)(2,1)S(1)} %get-tuple-element.19.grad_ref, ...), custom_call_target="tpu_custom_call" | custom-call | flops 4294967296 | tf_op jit(solution)/shard_map/backward/pallas_call | solution.py:31
  76.1 0.3 collective-permute-start.15
  76.4 0.2 collective-permute-start.16
  76.6 6.1 %backward.3 = (f32[256,1024]{1,0:T(8,128)S(1)}, f32[1024,256]{1,0:T(8,128)S(1)}) custom-call(s32[2]{0:T(128)S(1)} %pad_add_fusion.1.pos_ref, bf16[256,2048]{1,0:T(8,128)(2,1)S(1)} %copy-done.5, bf16[2048,256]{1,0:T(8,128)(2,1)S(1)} %copy-done.8, bf16[2048,256]{1,0:T(8,128)(2,1)S(1)} %get-tuple-element.26.grad_ref, ...), custom_call_target="tpu_custom_call" | custom-call | flops 4294967296 | tf_op jit(solution)/shard_map/backward/pallas_call | solution.py:31
  82.7 0.4 collective-permute-start.17
  83.1 0.2 collective-permute-start.18
  83.3 0.0 collective-permute-done.15
  83.3 4.1 %maximum_select_fusion = f32[256,2048]{1,0:T(8,128)} fusion(f32[256,1024]{1,0:T(8,128)} %collective-permute-done.15, f32[256,1024]{1,0:T(8,128)} %get-tuple-element.24, pred[]{:T(512)S(6)} %eq.10), kind=kLoop, calls=%fused_computation | loop fusion | flops 1572864 | bytes 4194305 | tf_op jit(solution)/shard_map/jit(_where)/select_n | solution.py:262
  87.4 0.0 collective-permute-done.16
  87.4 3.9 %maximum_select_fusion.1 = f32[2048,256]{1,0:T(8,128)} fusion(f32[1024,256]{1,0:T(8,128)} %collective-permute-done.16, f32[1024,256]{1,0:T(8,128)} %get-tuple-element.25, pred[]{:T(512)S(6)} %eq.10), kind=kLoop, calls=%fused_computation.1 | loop fusion | flops 1572864 | bytes 4194305 | tf_op jit(solution)/shard_map/jit(_where)/select_n | solution.py:265
  91.3 0.0 collective-permute-done.17
  91.3 3.1 %maximum_select_fusion.2 = f32[256,2048]{1,0:T(8,128)} fusion(f32[256,1024]{1,0:T(8,128)} %collective-permute-done.17, f32[256,1024]{1,0:T(8,128)S(1)} %get-tuple-element.28, pred[]{:T(512)S(6)} %eq.10), kind=kLoop, calls=%fused_computation.2 | loop fusion | flops 1572864 | bytes 4194305 | tf_op jit(solution)/shard_map/jit(_where)/select_n | solution.py:262
  94.4 0.0 collective-permute-done.18
  94.4 1.6 %maximum_select_fusion.3 = f32[2048,256]{1,0:T(8,128)} fusion(f32[1024,256]{1,0:T(8,128)S(1)} %collective-permute-done.18, f32[1024,256]{1,0:T(8,128)S(1)} %get-tuple-element.29, pred[]{:T(512)S(6)} %eq.10), kind=kLoop, calls=%fused_computation.3 | loop fusion | flops 1572864 | bytes 4194305 | tf_op jit(solution)/shard_map/jit(_where)/select_n | solution.py:265
  (18 shorter events, 0.1 us)
Async XLA Ops:
  0.6 14.1 %collective-permute-start.4 = (bf16[256,256]{1,0:T(8,128)(2,1)}, bf16[256,256]{1,0:T(8,128)(2,1)S(1)}, u32[]{:S(2)}, u32[]{:S(2)}) collective-permute-start(bf16[256,256]{1,0:T(8,128)(2,1)} %refs_0_.1), channel_id=1, source_target_pairs={{0,12},{4,8},{8,4},{12,0},{1,13},{5,9},{9,5},{13,1},{2,14},{6,10},... | collective-permute-start | bytes 393224 | tf_op jit(solution)/shard_map/ppermute | solution.py:195
  5.7 28.4 %collective-permute-start.11 = (bf16[256,256]{1,0:T(8,128)(2,1)}, bf16[256,256]{1,0:T(8,128)(2,1)}, u32[]{:S(2)}, u32[]{:S(2)}) collective-permute-start(bf16[256,256]{1,0:T(8,128)(2,1)} %refs_0_.1), channel_id=1, source_target_pairs={{0,1},{1,0},{2,3},{3,2},{4,5},{5,4},{6,7},{7,6},{8,9},{9,8},{10,11... | collective-permute-start | bytes 393224 | tf_op jit(solution)/shard_map/ppermute | solution.py:198
  5.7 1.2 %copy-start = (bf16[256,2048]{1,0:T(8,128)(2,1)S(1)}, bf16[256,2048]{1,0:T(8,128)(2,1)}, u32[]{:S(2)}) copy-start(bf16[256,2048]{1,0:T(8,128)(2,1)} %first_ref.2) | copy-start | bytes 3145732
  7.0 1.2 %copy-start.2 = (bf16[2048,256]{1,0:T(8,128)(2,1)S(1)}, bf16[2048,256]{1,0:T(8,128)(2,1)}, u32[]{:S(2)}) copy-start(bf16[2048,256]{1,0:T(8,128)(2,1)} %second_ref.2) | copy-start | bytes 3145732
  8.2 1.2 %copy-start.4 = (bf16[256,2048]{1,0:T(8,128)(2,1)S(1)}, bf16[256,2048]{1,0:T(8,128)(2,1)}, u32[]{:S(2)}) copy-start(bf16[256,2048]{1,0:T(8,128)(2,1)} %first_ref.3) | copy-start | bytes 3145732
  9.4 1.2 %copy-start.6 = (bf16[2048,256]{1,0:T(8,128)(2,1)S(1)}, bf16[2048,256]{1,0:T(8,128)(2,1)}, u32[]{:S(2)}) copy-start(bf16[2048,256]{1,0:T(8,128)(2,1)} %second_ref.3) | copy-start | bytes 3145732
  10.7 4.1 %copy-start.1 = (bf16[256,2048]{1,0:T(8,128)(2,1)S(1)}, bf16[256,2048]{1,0:T(8,128)(2,1)}, u32[]{:S(2)}) copy-start(bf16[256,2048]{1,0:T(8,128)(2,1)} %first_ref.2) | copy-start | bytes 3145732
  10.7 4.1 %copy-start.3 = (bf16[2048,256]{1,0:T(8,128)(2,1)S(1)}, bf16[2048,256]{1,0:T(8,128)(2,1)}, u32[]{:S(2)}) copy-start(bf16[2048,256]{1,0:T(8,128)(2,1)} %second_ref.2) | copy-start | bytes 3145732
  10.7 4.1 %copy-start.5 = (bf16[256,2048]{1,0:T(8,128)(2,1)S(1)}, bf16[256,2048]{1,0:T(8,128)(2,1)}, u32[]{:S(2)}) copy-start(bf16[256,2048]{1,0:T(8,128)(2,1)} %first_ref.3) | copy-start | bytes 3145732
  13.1 13.2 %collective-permute-start = (bf16[256,512]{1,0:T(8,128)(2,1)S(1)}, bf16[256,512]{1,0:T(8,128)(2,1)}, u32[]{:S(2)}, u32[]{:S(2)}) collective-permute-start(bf16[256,512]{1,0:T(8,128)(2,1)S(1)} %forward.3), channel_id=1, source_target_pairs={{0,2},{2,0},{1,3},{3,1},{4,6},{6,4},{5,7},{7,5},{8,10},{10,8},{9,1... | collective-permute-start | bytes 786440 | tf_op jit(solution)/shard_map/ppermute | solution.py:198
  14.6 8.7 %collective-permute-start.2 = (bf16[256,256]{1,0:T(8,128)(2,1)}, bf16[256,256]{1,0:T(8,128)(2,1)}, u32[]{:S(2)}, u32[]{:S(2)}) collective-permute-start(bf16[256,256]{1,0:T(8,128)(2,1)} %refs_0_.1), channel_id=1, source_target_pairs={{0,8},{4,12},{8,0},{12,4},{1,9},{5,13},{9,1},{13,5},{2,10},{6,14},... | collective-permute-start | bytes 393224 | tf_op jit(solution)/shard_map/ppermute | solution.py:195
  14.7 1.2 %copy-start.7 = (bf16[2048,256]{1,0:T(8,128)(2,1)S(1)}, bf16[2048,256]{1,0:T(8,128)(2,1)}, u32[]{:S(2)}) copy-start(bf16[2048,256]{1,0:T(8,128)(2,1)} %second_ref.3) | copy-start | bytes 3145732
  17.3 8.9 %copy-start.10 = (s32[256,1]{0,1:T(1,128)S(1)}, s32[256,1]{0,1:T(1,128)}, u32[]{:S(2)}) copy-start(s32[256,1]{0,1:T(1,128)} %param.9) | copy-start | bytes 3076
  17.4 16.7 %collective-permute-start.5 = (bf16[256,512]{1,0:T(8,128)(2,1)S(1)}, bf16[256,512]{1,0:T(8,128)(2,1)S(1)}, u32[]{:S(2)}, u32[]{:S(2)}) collective-permute-start(bf16[256,512]{1,0:T(8,128)(2,1)S(1)} %forward.5), channel_id=1, source_target_pairs={{0,2},{2,0},{1,3},{3,1},{4,6},{6,4},{5,7},{7,5},{8,10},{10,8},{9,1... | collective-permute-start | bytes 786440 | tf_op jit(solution)/shard_map/ppermute | solution.py:198
  18.0 16.9 %collective-permute-start.10 = (bf16[256,256]{1,0:T(8,128)(2,1)}, bf16[256,256]{1,0:T(8,128)(2,1)S(1)}, u32[]{:S(2)}, u32[]{:S(2)}) collective-permute-start(bf16[256,256]{1,0:T(8,128)(2,1)} %refs_0_.1), channel_id=1, source_target_pairs={{0,4},{4,0},{8,12},{12,8},{1,5},{5,1},{9,13},{13,9},{2,6},{6,2},{1... | collective-permute-start | bytes 393224 | tf_op jit(solution)/shard_map/ppermute | solution.py:195
  25.7 15.6 %copy-start.9 = (s32[256]{0:T(256)S(1)}, s32[256]{0:T(256)}, u32[]{:S(2)}) copy-start(s32[256]{0:T(256)} %param.10) | copy-start | bytes 3076
  25.7 16.2 %copy-start.11 = (s32[256]{0:T(256)S(1)}, s32[256]{0:T(256)}, u32[]{:S(2)}) copy-start(s32[256]{0:T(256)} %param.11) | copy-start | bytes 3076
  25.7 8.3 %collective-permute-start.3 = (bf16[256,512]{1,0:T(8,128)(2,1)S(1)}, bf16[256,512]{1,0:T(8,128)(2,1)S(1)}, u32[]{:S(2)}, u32[]{:S(2)}) collective-permute-start(bf16[256,512]{1,0:T(8,128)(2,1)S(1)} %forward.4), channel_id=1, source_target_pairs={{0,2},{2,0},{1,3},{3,1},{4,6},{6,4},{5,7},{7,5},{8,10},{10,8},{9,1... | collective-permute-start | bytes 786440 | tf_op jit(solution)/shard_map/ppermute | solution.py:198
  26.3 8.5 %collective-permute-start.14 = (bf16[256,256]{1,0:T(8,128)(2,1)S(1)}, bf16[256,256]{1,0:T(8,128)(2,1)S(1)}, u32[]{:S(2)}, u32[]{:S(2)}) collective-permute-start(bf16[256,256]{1,0:T(8,128)(2,1)S(1)} %collective-permute-done.4.x_ref.refs_3_), channel_id=1, source_target_pairs={{0,1},{1,0},{2,3},{3,2},{4,5},{5,4},{6,7},{7,6},{8,9},{9,8},{10,11... | collective-permute-start | bytes 393224 | tf_op jit(solution)/shard_map/ppermute | solution.py:198
  33.9 7.3 %collective-permute-start.1 = (bf16[256,512]{1,0:T(8,128)(2,1)S(1)}, bf16[256,512]{1,0:T(8,128)(2,1)S(1)}, u32[]{:S(2)}, u32[]{:S(2)}) collective-permute-start(bf16[256,512]{1,0:T(8,128)(2,1)S(1)} %add_convert_fusion.2.refs_0_), channel_id=1, source_target_pairs={{0,4},{4,0},{8,12},{12,8},{1,5},{5,1},{9,13},{13,9},{2,6},{6,2},{1... | collective-permute-start | bytes 786440 | tf_op jit(solution)/shard_map/ppermute | solution.py:195
  34.0 7.3 %collective-permute-start.13 = (bf16[256,256]{1,0:T(8,128)(2,1)}, bf16[256,256]{1,0:T(8,128)(2,1)S(1)}, u32[]{:S(2)}, u32[]{:S(2)}) collective-permute-start(bf16[256,256]{1,0:T(8,128)(2,1)} %collective-permute-done.2.x_ref.refs_2_), channel_id=1, source_target_pairs={{0,1},{1,0},{2,3},{3,2},{4,5},{5,4},{6,7},{7,6},{8,9},{9,8},{10,11... | collective-permute-start | bytes 393224 | tf_op jit(solution)/shard_map/ppermute | solution.py:198
  34.2 23.3 %collective-permute-start.6 = (bf16[256,512]{1,0:T(8,128)(2,1)S(1)}, bf16[256,512]{1,0:T(8,128)(2,1)S(1)}, u32[]{:S(2)}, u32[]{:S(2)}) collective-permute-start(bf16[256,512]{1,0:T(8,128)(2,1)S(1)} %add_convert_fusion.2.refs_0_), channel_id=1, source_target_pairs={{0,1},{1,0},{2,3},{3,2},{4,5},{5,4},{6,7},{7,6},{8,9},{9,8},{10,11... | collective-permute-start | bytes 786440 | tf_op jit(solution)/shard_map/ppermute | solution.py:198
  34.8 22.8 %collective-permute-start.8 = (bf16[256,512]{1,0:T(8,128)(2,1)S(1)}, bf16[256,512]{1,0:T(8,128)(2,1)S(1)}, u32[]{:S(2)}, u32[]{:S(2)}) collective-permute-start(bf16[256,512]{1,0:T(8,128)(2,1)S(1)} %add_convert_fusion.1.refs_2_), channel_id=1, source_target_pairs={{0,1},{1,0},{2,3},{3,2},{4,5},{5,4},{6,7},{7,6},{8,9},{9,8},{10,11... | collective-permute-start | bytes 786440 | tf_op jit(solution)/shard_map/ppermute | solution.py:198
  34.8 22.7 %collective-permute-start.9 = (bf16[256,512]{1,0:T(8,128)(2,1)S(1)}, bf16[256,512]{1,0:T(8,128)(2,1)S(1)}, u32[]{:S(2)}, u32[]{:S(2)}) collective-permute-start(bf16[256,512]{1,0:T(8,128)(2,1)S(1)} %add_convert_fusion.refs_3_), channel_id=1, source_target_pairs={{0,1},{1,0},{2,3},{3,2},{4,5},{5,4},{6,7},{7,6},{8,9},{9,8},{10,11... | collective-permute-start | bytes 786440 | tf_op jit(solution)/shard_map/ppermute | solution.py:198
  41.3 16.3 %collective-permute-start.7 = (bf16[256,512]{1,0:T(8,128)(2,1)S(1)}, bf16[256,512]{1,0:T(8,128)(2,1)S(1)}, u32[]{:S(2)}, u32[]{:S(2)}) collective-permute-start(bf16[256,512]{1,0:T(8,128)(2,1)S(1)} %collective-permute-done.1.refs_1_), channel_id=1, source_target_pairs={{0,1},{1,0},{2,3},{3,2},{4,5},{5,4},{6,7},{7,6},{8,9},{9,8},{10,11... | collective-permute-start | bytes 786440 | tf_op jit(solution)/shard_map/ppermute | solution.py:198
  41.3 14.8 %collective-permute-start.12 = (bf16[256,256]{1,0:T(8,128)(2,1)S(1)}, bf16[256,256]{1,0:T(8,128)(2,1)S(1)}, u32[]{:S(2)}, u32[]{:S(2)}) collective-permute-start(bf16[256,256]{1,0:T(8,128)(2,1)S(1)} %collective-permute-done.10.refs_1_), channel_id=1, source_target_pairs={{0,1},{1,0},{2,3},{3,2},{4,5},{5,4},{6,7},{7,6},{8,9},{9,8},{10,11... | collective-permute-start | bytes 393224 | tf_op jit(solution)/shard_map/ppermute | solution.py:198
  68.4 8.1 %copy-start.8 = (bf16[2048,256]{1,0:T(8,128)(2,1)S(1)}, bf16[2048,256]{1,0:T(8,128)(2,1)}, u32[]{:S(2)}) copy-start(bf16[2048,256]{1,0:T(8,128)(2,1)} %second_ref.3) | copy-start | bytes 3145732
  76.1 7.2 %collective-permute-start.15 = (f32[256,1024]{1,0:T(8,128)}, f32[256,1024]{1,0:T(8,128)}, u32[]{:S(2)}, u32[]{:S(2)}) collective-permute-start(f32[256,1024]{1,0:T(8,128)} %get-tuple-element.24), channel_id=1, source_target_pairs={{0,1},{1,0},{2,3},{3,2},{4,5},{5,4},{6,7},{7,6},{8,9},{9,8},{10,11... | collective-permute-start | bytes 3145736 | tf_op jit(solution)/shard_map/ppermute | solution.py:198
  76.4 11.1 %collective-permute-start.16 = (f32[1024,256]{1,0:T(8,128)}, f32[1024,256]{1,0:T(8,128)}, u32[]{:S(2)}, u32[]{:S(2)}) collective-permute-start(f32[1024,256]{1,0:T(8,128)} %get-tuple-element.25), channel_id=1, source_target_pairs={{0,1},{1,0},{2,3},{3,2},{4,5},{5,4},{6,7},{7,6},{8,9},{9,8},{10,11... | collective-permute-start | bytes 3145736 | tf_op jit(solution)/shard_map/ppermute | solution.py:198
  82.7 8.6 %collective-permute-start.17 = (f32[256,1024]{1,0:T(8,128)S(1)}, f32[256,1024]{1,0:T(8,128)}, u32[]{:S(2)}, u32[]{:S(2)}) collective-permute-start(f32[256,1024]{1,0:T(8,128)S(1)} %get-tuple-element.28), channel_id=1, source_target_pairs={{0,1},{1,0},{2,3},{3,2},{4,5},{5,4},{6,7},{7,6},{8,9},{9,8},{10,11... | collective-permute-start | bytes 3145736 | tf_op jit(solution)/shard_map/ppermute | solution.py:198
  83.1 11.3 %collective-permute-start.18 = (f32[1024,256]{1,0:T(8,128)S(1)}, f32[1024,256]{1,0:T(8,128)S(1)}, u32[]{:S(2)}, u32[]{:S(2)}) collective-permute-start(f32[1024,256]{1,0:T(8,128)S(1)} %get-tuple-element.29), channel_id=1, source_target_pairs={{0,1},{1,0},{2,3},{3,2},{4,5},{5,4},{6,7},{7,6},{8,9},{9,8},{10,11... | collective-permute-start | bytes 3145736 | tf_op jit(solution)/shard_map/ppermute | solution.py:198

commit v3 on v2

--- a/solution.py
+++ b/solution.py
@@ -21,46 +21,67 @@
     return 0.5 * jnp.tanh(0.5 * v) + 0.5
 
 
-def in_vmem(body, name, out_shape, args, scratch=(), limit=32, pos=None, flops=0):
-    vmem = pl.BlockSpec(memory_space=pltpu.VMEM)
-    smem = pl.BlockSpec(memory_space=pltpu.SMEM)
-    specs = [vmem] * len(args)
+HBM = pl.BlockSpec(memory_space=pl.ANY)
+VMEM = pl.BlockSpec(memory_space=pltpu.VMEM)
+SMEM = pl.BlockSpec(memory_space=pltpu.SMEM)
+
+
+def kernel(body, name, outs, args, scratch=(), limit=16, pos=None, flops=0, hbm=(), hbm_out=(), aliases={}):
+    specs = [HBM if i in hbm else VMEM for i in range(len(args))]
     if pos is not None:
-        args = (pos, *args)
-        specs = [smem] + specs
+        args, specs = (pos, *args), [SMEM, *specs]
+        aliases = {i + 1: o for i, o in aliases.items()}
     return pl.pallas_call(
         body,
         in_specs=specs,
-        out_specs=jax.tree.map(lambda _: vmem, out_shape),
-        out_shape=out_shape,
+        out_specs=[HBM if i in hbm_out else VMEM for i in range(len(outs))],
+        out_shape=[jax.ShapeDtypeStruct(shape, dtype) for shape, dtype in outs],
         scratch_shapes=scratch,
+        input_output_aliases=aliases,
         compiler_params=pltpu.CompilerParams(vmem_limit_bytes=limit * MIB),
         cost_estimate=pl.CostEstimate(flops=flops, bytes_accessed=0, transcendentals=0),
         name=name,
     )(*args)
 
 
-def forward_kernel(x_ref, sf_ref, gf_ref, ss_ref, gs_ref, out_ref, active):
-    emb = ss_ref.shape[1]
-    for k, (first, second) in enumerate(((sf_ref, ss_ref), (gf_ref, gs_ref))):
+def encode(x_ref, weights, out_ref, active):
+    emb = weights[2].shape[1]
+    for k in range(2):
+        first, second = weights[k], weights[2 + k]
         for c in range(0, active.shape[1], 512):
             hidden = dot(x_ref[...], first[:, c : c + 512])
             active[:, c : c + 512] = (hidden * sigmoid(hidden)).astype(BF)
         out_ref[:, k * emb : (k + 1) * emb] = dot(active[...], second[...]).astype(BF)
 
 
-def forward(x, sf, gf, ss, gs):
+def first_kernel(x_ref, *refs):
+    weights, out_ref, held, active, sems = refs[:4], refs[4], refs[5:9], refs[9], refs[10]
+    copies = [pltpu.make_async_copy(w, h, sems.at[i]) for i, (w, h) in enumerate(zip(weights, held))]
+    for i in (0, 2, 1, 3):
+        copies[i].start()
+    for c in copies:
+        c.wait()
+    encode(x_ref, held, out_ref, active)
+
+
+def forward_kernel(x_ref, *refs):
+    encode(x_ref, refs[:4], refs[4], refs[5])
+
+
+def forward(x, weights, load=False):
     rows, width = x.shape
-    hid, emb = ss.shape
-    return in_vmem(
-        forward_kernel,
+    hid, emb = weights[2].shape
+    outs = [((rows, 2 * emb), BF)] + [(w.shape, w.dtype) for w in weights] * load
+    got = kernel(
+        first_kernel if load else forward_kernel,
         "forward",
-        jax.ShapeDtypeStruct((rows, 2 * emb), BF),
-        (x, sf, gf, ss, gs),
-        [pltpu.VMEM((rows, hid), BF)],
-        limit=16,
+        outs,
+        (x, *weights),
+        [pltpu.VMEM((rows, hid), BF)] + [pltpu.SemaphoreType.DMA((4,))] * load,
         flops=8 * rows * width * hid,
-    )
+        hbm=(1, 2, 3, 4) if load else (),
+    )
+    return (got[0], got[1:]) if load else got[0]
 
 
 def place_blocks(pos_ref, mine, other, put, n_blk, n_rep, slab):
@@ -73,25 +94,47 @@
                 put(pl.multiple_of(off, slab), block[r * slab : (r + 1) * slab, :])
 
 
+def column(row):
+    return jnp.broadcast_to(row, (128, row.shape[1])).T[:, :1]
+
+
+def meta_row(pos_ref, meta_mine, meta_other, which, j, n_blk, n_rep, slab):
+    side, r = j // n_rep, j % n_rep
+    parts = []
+    for blk in range(n_blk):
+        at = pl.multiple_of(jnp.bitwise_xor(blk, pos_ref[0]) * 8, 8)
+        cols = slice(r * slab, (r + 1) * slab)
+        pair = [ref[pl.ds(at, 8), cols][which : which + 1, :] for ref in (meta_mine, meta_other)]
+        parts.append(jnp.where(pos_ref[1] == side, pair[0], pair[1]))
+    return jnp.concatenate(parts, axis=1).astype(F32)
+
+
 def arrange_kernel(n_blk, n_rep, slab, pos_ref, *refs):
     mine, other = refs[:n_blk], refs[n_blk : 2 * n_blk]
-    all_ref, all_t_ref = refs[2 * n_blk :]
+    meta_mine, meta_other, all_ref, all_t_ref, goals_ref, goals_t_ref, pick_ref = refs[2 * n_blk :]
+    rows = all_ref.shape[0]
+    batch = n_blk * slab
 
     def put(off, value):
         all_ref[pl.ds(off, slab), :] = value
         all_t_ref[:, pl.ds(off, slab)] = value.T
 
     place_blocks(pos_ref, mine, other, put, n_blk, n_rep, slab)
-
-
-def column(row):
-    return jnp.broadcast_to(row, (128, row.shape[1])).T[:, :1]
+    for j in range(rows // batch):
+        own = slice(j * batch, (j + 1) * batch)
+        goal = column(meta_row(pos_ref, meta_mine, meta_other, 0, j, n_blk, n_rep, slab)).astype(jnp.int32)
+        pick_ref[own, :] = jnp.where(
+            goal == lax.broadcasted_iota(jnp.int32, (batch, rows), 1), 1.0, 0.0
+        ).astype(BF)
+    goals = dot(pick_ref[...], all_ref[...]).astype(BF)
+    goals_ref[...] = goals
+    goals_t_ref[...] = goals.T
 
 
 def contrast_kernel(n_blk, n_rep, slab, scale, pos_ref, *refs):
     mine, other = refs[:n_blk], refs[n_blk : 2 * n_blk]
-    meta_ref = refs[2 * n_blk]
-    phi_grad_ref, phi_grad_t_ref, sum_ref, sum_t_ref, phi_all, psi_all, total = refs[2 * n_blk + 1 :]
+    meta_mine, meta_other, pick_ref = refs[2 * n_blk : 2 * n_blk + 3]
+    phi_grad_ref, phi_grad_t_ref, psi_grad_ref, psi_grad_t_ref, phi_all, psi_all = refs[2 * n_blk + 3 :]
     emb = phi_all.shape[1]
     batch = n_blk * slab
     rows = phi_all.shape[0]
@@ -104,47 +147,36 @@
 
     for j in range(rows // batch):
         own = slice(j * batch, (j + 1) * batch)
-        side, r = j // n_rep, j % n_rep
-
-        def meta_row(which):
-            parts = [
-                meta_ref[(blk * 2 + side) * 8 + which : (blk * 2 + side) * 8 + which + 1, r * slab : (r + 1) * slab]
-                for blk in range(n_blk)
-            ]
-            return jnp.concatenate(parts, axis=1)
-
-        goal_row, ep_row = meta_row(0), meta_row(1)
-        goal_col, ep_col = column(goal_row.astype(F32)), column(ep_row.astype(F32))
-        pick = jnp.where(
-            goal_col.astype(jnp.int32) == lax.broadcasted_iota(jnp.int32, (batch, rows), 1), 1.0, 0.0
-        ).astype(BF)
-        psi = dot(pick, psi_all[...]).astype(BF)
+        ep_row = meta_row(pos_ref, meta_mine, meta_other, 1, j, n_blk, n_rep, slab)
+        psi = dot(pick_ref[own, :], psi_all[...]).astype(BF)
         phi = phi_all[own, :]
         scores = lax.dot_general(phi, psi, (((1,), (1,)), ((), ())), preferred_element_type=F32) * scale
         diagonal = lax.broadcasted_iota(jnp.int32, (batch, batch), 0) == lax.broadcasted_iota(
             jnp.int32, (batch, batch), 1
         )
-        same = ep_col == ep_row.astype(F32)
+        same = column(ep_row) == ep_row
         exponent = jnp.where(same & ~diagonal, 0.0, jnp.exp(scores))
         totals = jnp.sum(exponent, axis=1, keepdims=True)
         delta = (exponent / totals - diagonal.astype(F32)).astype(BF)
-        phi_grad = dot(delta, psi) * scale
-        phi_grad_ref[own, :] = phi_grad.astype(BF)
-        phi_grad_t_ref[:, own] = phi_grad.astype(BF).T
+        phi_grad = (dot(delta, psi) * scale).astype(BF)
+        phi_grad_ref[own, :] = phi_grad
+        phi_grad_t_ref[:, own] = phi_grad.T
         psi_grad = (dot(delta.T, phi) * scale).astype(BF)
-        put_back = jnp.where(
-            goal_row == lax.broadcasted_iota(jnp.int32, (rows, batch), 0), 1.0, 0.0
-        ).astype(BF)
-        add = dot(put_back, psi_grad)
-        if j == 0:
-            total[...] = add
-        else:
-            total[...] += add
-    sum_ref[...] = total[...].astype(BF)
-    sum_t_ref[...] = total[...].astype(BF).T
-
-
-def backward_kernel(pos_ref, first_ref, second_ref, grad_ref, grad_t_ref, states_ref, states_t_ref, gf_ref, gs_ref, active, back):
+        psi_grad_ref[own, :] = psi_grad
+        psi_grad_t_ref[:, own] = psi_grad.T
+
+
+def backward_kernel(n_put, pos_ref, first_ref, second_ref, grad_ref, grad_t_ref, states_ref, states_t_ref, *refs):
+    done, (gf_ref, gs_ref), outs, (active, back), sems = (
+        refs[:n_put],
+        refs[n_put : n_put + 2],
+        refs[n_put + 2 : 2 * n_put + 2],
+        refs[2 * n_put + 2 : 2 * n_put + 4],
+        refs[2 * n_put + 4 :],
+    )
+    copies = [put_half(pos_ref[1], x, o, sems[0].at[i]) for i, (x, o) in enumerate(zip(done, outs))]
+    for c in copies:
+        c.start()
     quarter, rows = active.shape
     at = pl.multiple_of(pos_ref[1] * quarter, quarter)
     first_t = first_ref[:, pl.ds(at, quarter)].T
@@ -160,20 +192,64 @@
         back[:, cols] = (dot(second, grad_t_ref[:, cols]) * slope).astype(BF)
     gs_ref[...] = dot(active[...], grad_ref[...])
     gf_ref[...] = dot(back[...], states_ref[...]).T
-
-
-def backward(pos, first, second, grad, grad_t, states, states_t, quarter):
+    for c in copies:
+        c.wait()
+
+
+def put_half(side, half, out, sem):
+    n, m = half.shape
+    if out.shape[0] == n:
+        to = out.at[:, pl.ds(pl.multiple_of(side * m, m), m)]
+    else:
+        to = out.at[pl.ds(pl.multiple_of(side * n, n), n), :]
+    return pltpu.make_async_copy(half, to, sem)
+
+
+def backward(pos, first, second, grad, grad_t, states, states_t, quarter, done=()):
     rows, width = states.shape
     emb = second.shape[1]
-    return in_vmem(
-        backward_kernel,
+    halves = [((width, quarter), F32), ((quarter, emb), F32)]
+    return kernel(
+        functools.partial(backward_kernel, len(done)),
         "backward",
-        [jax.ShapeDtypeStruct((width, quarter), F32), jax.ShapeDtypeStruct((quarter, emb), F32)],
-        (first, second, grad, grad_t, states, states_t),
-        [pltpu.VMEM((quarter, rows), BF), pltpu.VMEM((quarter, rows), BF)],
-        limit=32,
+        halves + [((width, 2 * quarter), F32), ((2 * quarter, emb), F32)][: len(done)],
+        (first, second, grad, grad_t, states, states_t, *done),
+        [pltpu.VMEM((quarter, rows), BF), pltpu.VMEM((quarter, rows), BF)]
+        + [pltpu.SemaphoreType.DMA((2,))] * bool(done),
+        limit=28,
         pos=pos,
         flops=8 * rows * width * quarter,
+        hbm_out=(2, 3),
+    )
+
+
+def finish_kernel(old, new, pos_ref, *refs):
+    halves = refs[: old + new]
+    outs = refs[2 * old + new : 2 * (old + new) + old]
+    sems = refs[-1]
+    copies = [
+        put_half(1 - pos_ref[1] if i < old else pos_ref[1], x, o, sems.at[i])
+        for i, (x, o) in enumerate(zip(halves, outs))
+    ]
+    for c in copies:
+        c.start()
+    for c in copies:
+        c.wait()
+
+
+def finish(pos, halves, wholes, shapes):
+    old, new = len(wholes), len(shapes)
+    n = old + new
+    return kernel(
+        functools.partial(finish_kernel, old, new),
+        "finish",
+        [(w.shape, w.dtype) for w in wholes] + shapes,
+        (*halves, *wholes),
+        [pltpu.SemaphoreType.DMA((n,))],
+        pos=pos,
+        hbm=range(n, n + old),
+        hbm_out=range(n),
+        aliases={n + i: i for i in range(old)},
     )
 
 
@@ -185,11 +261,10 @@
     owners = n_blk * n_sub
     slab = rows_dev // n_rep
     rows_all = owners * rows_dev
-    emb = state_second.shape[1]
+    hid, emb = state_second.shape
     b, s = lax.axis_index("blk"), lax.axis_index("sub")
     pos = jnp.stack([b, s]).astype(jnp.int32)
-    quarter = state_first.shape[1] // n_sub
-    weights = (state_first, goal_first, state_second, goal_second)
+    quarter = hid // n_sub
 
     def across(x, k):
         return lax.ppermute(x, "blk", [(i, i ^ k) for i in range(n_blk)])
@@ -203,68 +278,68 @@
     def both(part, there):
         return (part.astype(F32) + there.astype(F32)).astype(BF)
 
-    got = {0: states, 3: across(states, 3)}
-    part0 = forward(states, *weights)
+    got = {0: states, 3: across(states, 3), 2: across(states, 2)}
+    part0, weights = forward(states, (state_first, goal_first, state_second, goal_second), load=True)
     there0 = swap(part0, "rep")
-    got[2] = across(after(states, part0), 2)
-    part3 = forward(got[3], *weights)
+    part3 = forward(got[3], weights)
     there3 = swap(part3, "rep")
-    got[1] = across(after(states, part3), 1)
-
-    distance = after(goal_distance, part3)
+
+    distance = after(goal_distance, part0)
     owner = (b * n_sub + s + distance[:, 0]) % owners
     goal = (((owner % n_sub) * n_rep + goal_row // slab) * n_blk + owner // n_sub) * slab + goal_row % slab
     meta = jnp.pad(jnp.stack([goal, episode]), ((0, 6), (0, 0)))
-    meta_all = lax.all_gather(meta, ("blk", "sub"), axis=0, tiled=True)
+    meta = jnp.concatenate([meta, across(meta, 1)], axis=0)
+    meta = jnp.concatenate([meta, across(meta, 2)], axis=0)
+    meta_other = swap(meta, "sub")
 
     sums = {0: both(part0, there0)}
     sums[1] = across(sums[0], 1)
-    part2 = forward(got[2], *weights)
+    part2 = forward(after(got[2], sums[0]), weights)
     there2 = swap(part2, "rep")
+    got[1] = across(after(states, part2), 1)
     sums[3] = both(part3, there3)
     sums[2] = both(part2, there2)
 
     others = [swap(got[k], "sub") for k in range(n_blk)]
-    all_states, all_states_t = in_vmem(
+    wide, tall = ((rows_all, width), BF), ((width, rows_all), BF)
+    all_states, all_states_t, goals, goals_t, pick = kernel(
         functools.partial(arrange_kernel, n_blk, n_rep, slab),
         "arrange",
-        [jax.ShapeDtypeStruct((rows_all, width), BF), jax.ShapeDtypeStruct((width, rows_all), BF)],
-        (*(got[k] for k in range(n_blk)), *others),
+        [wide, tall, wide, tall, ((rows_all, rows_all), BF)],
+        (*(got[k] for k in range(n_blk)), *others, meta, meta_other),
         pos=pos,
-        limit=16,
+        flops=2 * rows_all * rows_all * width,
     )
 
     other_sums = [swap(sums[k], "sub") for k in range(n_blk)]
-    phi_grad, phi_grad_t, psi_sum, psi_sum_t = in_vmem(
+    wide, tall = ((rows_all, emb), BF), ((emb, rows_all), BF)
+    phi_grad, phi_grad_t, psi_grad, psi_grad_t = kernel(
         functools.partial(contrast_kernel, n_blk, n_rep, slab, 4.0 / math.sqrt(emb)),
         "contrast",
-        [
-            jax.ShapeDtypeStruct((rows_all, emb), BF),
-            jax.ShapeDtypeStruct((emb, rows_all), BF),
-            jax.ShapeDtypeStruct((rows_all, emb), BF),
-            jax.ShapeDtypeStruct((emb, rows_all), BF),
-        ],
-        (*(sums[k] for k in range(n_blk)), *other_sums, meta_all),
-        [pltpu.VMEM((rows_all, emb), BF), pltpu.VMEM((rows_all, emb), BF), pltpu.VMEM((rows_all, emb), F32)],
+        [wide, tall, wide, tall],
+        (*(sums[k] for k in range(n_blk)), *other_sums, meta, meta_other, pick),
+        [pltpu.VMEM((rows_all, emb), BF), pltpu.VMEM((rows_all, emb), BF)],
         pos=pos,
-        limit=24,
-        flops=2 * rows_all * emb * (2 * rows_all + 3 * n_blk * slab),
-    )
-
-    outs = []
-    for first, second, grad, grad_t in (
-        (state_first, state_second, phi_grad, phi_grad_t),
-        (goal_first, goal_second, psi_sum, psi_sum_t),
-    ):
-        gf, gs = backward(pos, first, second, grad, grad_t, all_states, all_states_t, quarter)
-        gf2, gs2 = swap(gf, "sub"), swap(gs, "sub")
-        outs.append(
-            jnp.where(s == 0, jnp.concatenate([gf, gf2], axis=1), jnp.concatenate([gf2, gf], axis=1))
-        )
-        outs.append(
-            jnp.where(s == 0, jnp.concatenate([gs, gs2], axis=0), jnp.concatenate([gs2, gs], axis=0))
-        )
-    return tuple(outs)
+        flops=2 * rows_all * emb * (rows_all + 3 * n_blk * slab),
+    )
+
+    sf, gf, ss, gs = weights
+    state_first_half, state_second_half = backward(
+        pos, sf, ss, phi_grad, phi_grad_t, all_states, all_states_t, quarter
+    )
+    state_there = [swap(x, "sub") for x in (state_first_half, state_second_half)]
+    goal_first_half, goal_second_half, out0, out1 = backward(
+        pos, gf, gs, psi_grad, psi_grad_t, goals, goals_t, quarter, (state_first_half, state_second_half)
+    )
+    goal_there = [swap(x, "sub") for x in (goal_first_half, goal_second_half)]
+    out0, out1, out2, out3 = finish(
+        pos,
+        (*state_there, goal_first_half, goal_second_half),
+        (out0, out1),
+        [((width, hid), F32), ((hid, emb), F32)],
+    )
+    out2, out3 = finish(pos, goal_there, (out2, out3), [])
+    return (out0, out1, out2, out3)
 
 
 def silu_slope(hidden):

time: 96.4 us -> 77.1 us (0.80)
  blocking collectives: 14.2 us -> 0 us
  other arithmetic: 13.9 us -> 1.26 us
  Pallas kernels: 32.1 us -> 38 us
  waiting for transfers between devices: 17.4 us -> 14.2 us
  starting transfers between devices: 11.4 us -> 14.1 us
  local copies, waits for them, and re-layouts: 6.16 us -> 8.01 us
    all_gather x1 -> x0, blocking collectives: 14.2 us -> none  [gathered(): meta_all = lax.all_gather(meta, ('blk', 'sub'), axis=0, tiled=True)]
    select_n x4 -> x0, other arithmetic: 12.7 us -> none  [the longest x2 7.25 us: gathered(): jnp.where(s == 0, jnp.concatenate([gf, gf2], axis=1), jnp.concatenate([gf...]
    pallas_call x7 -> x9, Pallas kernels: 32.1 us -> 38 us  [kernel(): pl.pallas_call(body, in_specs=specs, out_specs=[HBM if i in hbm_out else...]
    ppermute x4 -> x6, starting transfers between devices: 5.77 us -> 7.68 us  [across(): return lax.ppermute(x, 'blk', [(i, i ^ k) for i in range(n_blk)])]
    unnamed x24, local copies, waits for them, and re-layouts: 6.15 us -> 8.01 us
    ppermute x4 -> x6, waiting for transfers between devices: 10.8 us -> 9.22 us  [across(): return lax.ppermute(x, 'blk', [(i, i ^ k) for i in range(n_blk)])]
    ppermute x15 -> x16, waiting for transfers between devices: 6.59 us -> 5.03 us  [swap(): return lax.ppermute(x, axis, [(0, 1), (1, 0)])]
    ppermute x15 -> x16, starting transfers between devices: 5.63 us -> 6.46 us  [swap(): return lax.ppermute(x, axis, [(0, 1), (1, 0)])]
  transfers between devices with their start and end apart: 19 -> 22, of which waited for: 3 -> 5; matrix products, arithmetic and copies ran while one was open for 13% -> 2% of each run, Pallas kernels for 14% -> 27%
where the time goes in v3:
time: 77.1 us; the launch traced here: 76.7 us
  Pallas kernels  38 us (49%)
  waiting for transfers between devices  14.2 us (18%)
  starting transfers between devices  14.1 us (18%)
  local copies, waits for them, and re-layouts  8.01 us (10%)
  other arithmetic  1.26 us (2%)
  between operations  1.08 us (1%)
    pallas_call x9, Pallas kernels, kernel(): pl.pallas_call(body, in_specs=specs, out_specs=[HBM if i in hbm_out else...  38 us
    ppermute x6, waiting for transfers between devices, across(): return lax.ppermute(x, 'blk', [(i, i ^ k) for i in range(n_blk)])  9.22 us
    unnamed x24, local copies, waits for them, and re-layouts  8.01 us
    ppermute x6, starting transfers between devices, across(): return lax.ppermute(x, 'blk', [(i, i ^ k) for i in range(n_blk)])  7.68 us
    ppermute x16, starting transfers between devices, swap(): return lax.ppermute(x, axis, [(0, 1), (1, 0)])  6.46 us
    ppermute x16, waiting for transfers between devices, swap(): return lax.ppermute(x, axis, [(0, 1), (1, 0)])  5.03 us
  transfers between devices with their start and end apart: 22, of which 5 were waited for; matrix products, arithmetic and copies ran while one was open for 2% of the time, Pallas kernels for 27%

profile of v3, /device:TPU:0, one launch (start us, length us, event | category | flops | bytes accessed | tf_op | source)
XLA Modules:
  0.0 76.7 jit_solution(10264361446384266518)
XLA Ops:
  0.6 5.1 %collective-permute-start.4 = (bf16[256,256]{1,0:T(8,128)(2,1)}, bf16[256,256]{1,0:T(8,128)(2,1)}, u32[]{:S(2)}, u32[]{:S(2)}) collective-permute-start(bf16[256,256]{1,0:T(8,128)(2,1)} %refs_0_.3), channel_id=1, source_target_pairs={{0,12},{4,8},{8,4},{12,0},{1,13},{5,9},{9,5},{13,1},{2,14},{6,10},... | collective-permute-start | bytes 393224 | tf_op jit(solution)/shard_map/ppermute | solution.py:270
  5.8 1.2 %copy-done.3 = bf16[256,2048]{1,0:T(8,128)(2,1)S(1)} copy-done((bf16[256,2048]{1,0:T(8,128)(2,1)S(1)}, bf16[256,2048]{1,0:T(8,128)(2,1)}, u32[]{:S(2)}) %copy-start.3) | copy-done | bytes 1048600
  7.0 1.2 %copy-done.4 = bf16[256,2048]{1,0:T(8,128)(2,1)S(1)} copy-done((bf16[256,2048]{1,0:T(8,128)(2,1)S(1)}, bf16[256,2048]{1,0:T(8,128)(2,1)}, u32[]{:S(2)}) %copy-start.4) | copy-done | bytes 1048600
  8.2 1.2 %copy-done.5 = bf16[2048,256]{1,0:T(8,128)(2,1)S(1)} copy-done((bf16[2048,256]{1,0:T(8,128)(2,1)S(1)}, bf16[2048,256]{1,0:T(8,128)(2,1)}, u32[]{:S(2)}) %copy-start.5) | copy-done | bytes 1048600
  9.4 1.2 %copy-done.6 = bf16[2048,256]{1,0:T(8,128)(2,1)S(1)} copy-done((bf16[2048,256]{1,0:T(8,128)(2,1)S(1)}, bf16[2048,256]{1,0:T(8,128)(2,1)}, u32[]{:S(2)}) %copy-start.6) | copy-done | bytes 1048600
  10.7 0.9 %copy-done.7 = bf16[256,256]{1,0:T(8,128)(2,1)S(1)} copy-done((bf16[256,256]{1,0:T(8,128)(2,1)S(1)}, bf16[256,256]{1,0:T(8,128)(2,1)}, u32[]{:S(2)}) %copy-start.7) | copy-done | bytes 131096
  11.6 1.7 %forward.3 = (bf16[256,512]{1,0:T(8,128)(2,1)S(1)}, bf16[256,2048]{1,0:T(8,128)(2,1)S(1)}, bf16[256,2048]{1,0:T(8,128)(2,1)S(1)}, bf16[2048,256]{1,0:T(8,128)(2,1)S(1)}, bf16[2048,256]{1,0:T(8,128)(2,1)S(1)}) custom-call(bf16[256,256]{1,0:T(8,128)(2,1)S(1)} %copy-done.7, bf16[256,2048]{1,0:T(8,128)(2,1)S(1)} %copy-done.3, bf16[256,2048]{1,0:T(8,128)(2,1)S(1)} %copy-done.4, ...), custom_call_target="tpu_custom_call" | custom-call | flops 1073741824 | tf_op jit(solution)/shard_map/forward/pallas_call | solution.py:34
  13.3 0.0 copy-start
  13.3 1.0 %copy-done = bf16[2048,256]{1,0:T(8,128)(2,1)} copy-done((bf16[2048,256]{1,0:T(8,128)(2,1)}, bf16[2048,256]{1,0:T(8,128)(2,1)S(1)}, u32[]{:S(2)}) %copy-start) | copy-done | bytes 1048600
  14.2 1.5 %collective-permute-start = (bf16[256,512]{1,0:T(8,128)(2,1)S(1)}, bf16[256,512]{1,0:T(8,128)(2,1)}, u32[]{:S(2)}, u32[]{:S(2)}) collective-permute-start(bf16[256,512]{1,0:T(8,128)(2,1)S(1)} %get-tuple-element.35), channel_id=1, source_target_pairs={{0,2},{2,0},{1,3},{3,1},{4,6},{6,4},{5,7},{7,5},{8,10},{10,8},{9,1... | collective-permute-start | bytes 786440 | tf_op jit(solution)/shard_map/ppermute | solution.py:273
  15.8 0.1 collective-permute-start.10
  15.9 0.8 collective-permute-start.2
  16.7 0.0 collective-permute-start.14
  16.7 3.3 %collective-permute-done.10 = s32[8,256]{1,0:T(8,128)S(1)} collective-permute-done((s32[8,256]{1,0:T(8,128)S(1)}, s32[8,256]{1,0:T(8,128)S(1)}, u32[]{:S(2)}, u32[]{:S(2)}) %collective-permute-start.10) | collective-permute-done | bytes 8224 | tf_op jit(solution)/shard_map/ppermute | solution.py:270
  20.0 0.0 collective-permute-start.11
  20.0 0.0 collective-permute-done.4.x_ref.refs_3_
  20.0 0.0 copy-start.1
  20.0 1.2 %copy-done.1 = bf16[2048,256]{1,0:T(8,128)(2,1)S(1)} copy-done((bf16[2048,256]{1,0:T(8,128)(2,1)S(1)}, bf16[2048,256]{1,0:T(8,128)(2,1)}, u32[]{:S(2)}) %copy-start.1) | copy-done | bytes 1048600
  21.3 2.3 %forward.5 = bf16[256,512]{1,0:T(8,128)(2,1)S(1)} custom-call(bf16[256,256]{1,0:T(8,128)(2,1)} %collective-permute-done.4.x_ref.refs_3_, bf16[256,2048]{1,0:T(8,128)(2,1)S(1)} %get-tuple-element.33.refs_0_.first_ref, bf16[256,2048]{1,0:T(8,128)(2,1)S(1)} %get-tuple-element.37.refs_1_.first_ref, bf16[2048,256]{1,0:T(8,128)(2,1)S(1)} %copy-done.1, ...), custom_call_target="tpu_custom_call" | custom-call | flops 1073741824 | tf_op jit(solution)/shard_map/forward/pallas_call | solution.py:34
  23.5 0.6 collective-permute-start.5
  24.1 0.0 collective-permute-done
  24.1 1.0 %add_convert_fusion.2.refs_0_ = bf16[256,512]{1,0:T(8,128)(2,1)S(1)} fusion(bf16[256,512]{1,0:T(8,128)(2,1)} %collective-permute-done, bf16[256,512]{1,0:T(8,128)(2,1)S(1)} %get-tuple-element.35), kind=kLoop, calls=%fused_computation.2 | loop fusion | flops 524288 | bytes 786432 | tf_op jit(solution)/shard_map/convert_element_type | solution.py:279
  25.1 0.0 collective-permute-done.2.x_ref.refs_2_
  25.2 1.4 %forward.4 = bf16[256,512]{1,0:T(8,128)(2,1)S(1)} custom-call(bf16[256,256]{1,0:T(8,128)(2,1)S(1)} %collective-permute-done.2.x_ref.refs_2_, bf16[256,2048]{1,0:T(8,128)(2,1)S(1)} %get-tuple-element.33.refs_0_.first_ref, bf16[256,2048]{1,0:T(8,128)(2,1)S(1)} %get-tuple-element.37.refs_1_.first_ref, bf16[2048,256]{1,0:T(8,128)(2,1)S(1)} %copy-done.1, ...), custom_call_target="tpu_custom_call" | custom-call | flops 1073741824 | tf_op jit(solution)/shard_map/forward/pallas_call | solution.py:34
  26.5 1.6 %collective-permute-start.3 = (bf16[256,512]{1,0:T(8,128)(2,1)S(1)}, bf16[256,512]{1,0:T(8,128)(2,1)S(1)}, u32[]{:S(2)}, u32[]{:S(2)}) collective-permute-start(bf16[256,512]{1,0:T(8,128)(2,1)S(1)} %forward.4), channel_id=1, source_target_pairs={{0,2},{2,0},{1,3},{3,1},{4,6},{6,4},{5,7},{7,5},{8,10},{10,8},{9,1... | collective-permute-start | bytes 786440 | tf_op jit(solution)/shard_map/ppermute | solution.py:273
  28.1 0.0 collective-permute-done.11
  28.1 0.0 collective-permute-start.12
  28.1 0.9 %collective-permute-start.1 = (bf16[256,512]{1,0:T(8,128)(2,1)S(1)}, bf16[256,512]{1,0:T(8,128)(2,1)S(1)}, u32[]{:S(2)}, u32[]{:S(2)}) collective-permute-start(bf16[256,512]{1,0:T(8,128)(2,1)S(1)} %add_convert_fusion.2.refs_0_), channel_id=1, source_target_pairs={{0,4},{4,0},{8,12},{12,8},{1,5},{5,1},{9,13},{13,9},{2,6},{6,2},{1... | collective-permute-start | bytes 786440 | tf_op jit(solution)/shard_map/ppermute | solution.py:270
  29.1 3.8 %collective-permute-done.5 = bf16[256,512]{1,0:T(8,128)(2,1)S(1)} collective-permute-done((bf16[256,512]{1,0:T(8,128)(2,1)S(1)}, bf16[256,512]{1,0:T(8,128)(2,1)S(1)}, u32[]{:S(2)}, u32[]{:S(2)}) %collective-permute-start.5) | collective-permute-done | bytes 262176 | tf_op jit(solution)/shard_map/ppermute | solution.py:273
  32.8 0.8 %collective-permute-start.13 = (bf16[256,256]{1,0:T(8,128)(2,1)S(1)}, bf16[256,256]{1,0:T(8,128)(2,1)S(1)}, u32[]{:S(2)}, u32[]{:S(2)}) collective-permute-start(bf16[256,256]{1,0:T(8,128)(2,1)S(1)} %copy-done.8), channel_id=1, source_target_pairs={{0,4},{4,0},{8,12},{12,8},{1,5},{5,1},{9,13},{13,9},{2,6},{6,2},{1... | collective-permute-start | bytes 393224 | tf_op jit(solution)/shard_map/ppermute | solution.py:270
  33.6 0.1 add_convert_fusion.refs_3_
  33.7 0.0 collective-permute-done.12.refs_9_
  33.7 0.1 collective-permute-start.17
  33.8 5.9 %collective-permute-done.13.refs_1_ = bf16[256,256]{1,0:T(8,128)(2,1)S(1)} collective-permute-done((bf16[256,256]{1,0:T(8,128)(2,1)S(1)}, bf16[256,256]{1,0:T(8,128)(2,1)S(1)}, u32[]{:S(2)}, u32[]{:S(2)}) %collective-permute-start.13) | collective-permute-done | bytes 131104 | tf_op jit(solution)/shard_map/ppermute | solution.py:270
  39.6 0.0 collective-permute-start.16
  39.6 0.0 collective-permute-done.3
  39.6 0.5 collective-permute-start.15
  40.2 0.1 add_convert_fusion.1.refs_2_
  40.2 0.0 collective-permute-done.14.refs_4_
  40.2 0.1 collective-permute-start.6
  40.3 0.0 collective-permute-done.17.refs_7_
  40.3 0.5 collective-permute-start.9
  40.8 0.2 collective-permute-done.16.refs_6_
  41.0 0.1 collective-permute-start.8
  41.1 0.0 collective-permute-done.1.refs_1_
  41.1 0.4 collective-permute-start.7
  41.5 0.1 pad_add_fusion.3.pos_ref
  41.6 5.3 %arrange.1 = (bf16[2048,256]{1,0:T(8,128)(2,1)S(1)}, bf16[256,2048]{1,0:T(8,128)(2,1)S(1)}, bf16[2048,256]{1,0:T(8,128)(2,1)S(1)}, bf16[256,2048]{1,0:T(8,128)(2,1)S(1)}, bf16[2048,2048]{1,0:T(8,128)(2,1)S(1)}) custom-call(s32[2]{0:T(128)S(1)} %pad_add_fusion.3.pos_ref, bf16[256,256]{1,0:T(8,128)(2,1)S(1)} %copy-done.8, ...), custom_call_target="tpu_custom_call" | custom-call | flops 2147483648 | tf_op jit(solution)/shard_map/arrange/pallas_call | solution.py:34
  46.9 0.0 collective-permute-done.6.refs_4_
  46.9 0.0 collective-permute-done.7.refs_5_
  46.9 0.0 copy-start.2
  46.9 9.5 %contrast.1 = (bf16[2048,256]{1,0:T(8,128)(2,1)S(1)}, bf16[256,2048]{1,0:T(8,128)(2,1)S(1)}, bf16[2048,256]{1,0:T(8,128)(2,1)S(1)}, bf16[256,2048]{1,0:T(8,128)(2,1)S(1)}) custom-call(s32[2]{0:T(128)S(1)} %pad_add_fusion.3.pos_ref, bf16[256,512]{1,0:T(8,128)(2,1)S(1)} %add_convert_fusion.2.refs_0_, bf16[256,512]{1,0:T(8,128)(2,1)S(1)} %collective-permute-done.1.refs_1_, ...), custom_call_target="tpu_custom_call" | custom-call | flops 3758096384 | tf_op jit(solution)/shard_map/contrast/pallas_call | solution.py:34
  56.4 6.2 %backward.2 = (f32[256,1024]{1,0:T(8,128)S(1)}, f32[1024,256]{1,0:T(8,128)S(1)}) custom-call(s32[2]{0:T(128)S(1)} %pad_add_fusion.3.pos_ref, bf16[256,2048]{1,0:T(8,128)(2,1)S(1)} %get-tuple-element.33.refs_0_.first_ref, bf16[2048,256]{1,0:T(8,128)(2,1)S(1)} %copy-done.2, bf16[2048,256]{1,0:T(8,128)(2,1)S(1)} %get-tuple-element.42.grad_ref, ...), custom_call_target="tpu_custom_call" | custom-call | flops 4294967296 | tf_op jit(solution)/shard_map/backward/pallas_call | solution.py:34
  62.6 0.2 collective-permute-start.18
  62.8 0.4 collective-permute-start.19
  63.2 7.2 %backward.3 = (f32[256,1024]{1,0:T(8,128)S(1)}, f32[1024,256]{1,0:T(8,128)S(1)}, f32[256,2048]{1,0:T(8,128)}, f32[2048,256]{1,0:T(8,128)}) custom-call(s32[2]{0:T(128)S(1)} %pad_add_fusion.3.pos_ref, bf16[256,2048]{1,0:T(8,128)(2,1)S(1)} %get-tuple-element.37.refs_1_.first_ref, bf16[2048,256]{1,0:T(8,128)(2,1)S(1)} %get-tuple-element.38.refs_3_.second_ref, ...), custom_call_target="tpu_custom_call" | custom-call | flops 4294967296 | tf_op jit(solution)/shard_map/backward/pallas_call | solution.py:34
  70.4 0.2 collective-permute-start.20
  70.6 0.4 collective-permute-start.21
  71.0 0.0 collective-permute-done.18.refs_0_
  71.0 0.0 collective-permute-done.19.refs_1_
  71.0 2.6 %finish.2 = (f32[256,2048]{1,0:T(8,128)}, f32[2048,256]{1,0:T(8,128)}, f32[256,2048]{1,0:T(8,128)}, f32[2048,256]{1,0:T(8,128)}) custom-call(s32[2]{0:T(128)S(1)} %pad_add_fusion.3.pos_ref, f32[256,1024]{1,0:T(8,128)S(1)} %collective-permute-done.18.refs_0_, ...), custom_call_target="tpu_custom_call", output_to_operand_aliasing={{0}: (5, {}), {1}: (6, {})} | custom-call | tf_op jit(solution)/shard_map/finish/pallas_call | solution.py:34
  73.6 0.0 collective-permute-done.20.refs_0_
  73.6 1.0 %collective-permute-done.21.refs_1_ = f32[1024,256]{1,0:T(8,128)S(1)} collective-permute-done((f32[1024,256]{1,0:T(8,128)S(1)}, f32[1024,256]{1,0:T(8,128)S(1)}, u32[]{:S(2)}, u32[]{:S(2)}) %collective-permute-start.21) | collective-permute-done | bytes 1048608 | tf_op jit(solution)/shard_map/ppermute | solution.py:273
  74.6 1.9 %finish.3 = (f32[256,2048]{1,0:T(8,128)}, f32[2048,256]{1,0:T(8,128)}) custom-call(s32[2]{0:T(128)S(1)} %pad_add_fusion.3.pos_ref, f32[256,1024]{1,0:T(8,128)S(1)} %collective-permute-done.20.refs_0_, f32[1024,256]{1,0:T(8,128)S(1)} %collective-permute-done.21.refs_1_, ...), custom_call_target="tpu_custom_call", output_to_operand_aliasing={{0}: (3, {}), {1}: (4, {})} | custom-call | tf_op jit(solution)/shard_map/finish/pallas_call | solution.py:34
  (23 shorter events, 0.1 us)
Async XLA Ops:
  0.6 19.4 %collective-permute-start.4 = (bf16[256,256]{1,0:T(8,128)(2,1)}, bf16[256,256]{1,0:T(8,128)(2,1)}, u32[]{:S(2)}, u32[]{:S(2)}) collective-permute-start(bf16[256,256]{1,0:T(8,128)(2,1)} %refs_0_.3), channel_id=1, source_target_pairs={{0,12},{4,8},{8,4},{12,0},{1,13},{5,9},{9,5},{13,1},{2,14},{6,10},... | collective-permute-start | bytes 393224 | tf_op jit(solution)/shard_map/ppermute | solution.py:270
  5.7 1.2 %copy-start.3 = (bf16[256,2048]{1,0:T(8,128)(2,1)S(1)}, bf16[256,2048]{1,0:T(8,128)(2,1)}, u32[]{:S(2)}) copy-start(bf16[256,2048]{1,0:T(8,128)(2,1)} %refs_0_.2) | copy-start | bytes 3145732
  7.0 1.2 %copy-start.4 = (bf16[256,2048]{1,0:T(8,128)(2,1)S(1)}, bf16[256,2048]{1,0:T(8,128)(2,1)}, u32[]{:S(2)}) copy-start(bf16[256,2048]{1,0:T(8,128)(2,1)} %refs_1_.1) | copy-start | bytes 3145732
  8.2 1.2 %copy-start.5 = (bf16[2048,256]{1,0:T(8,128)(2,1)S(1)}, bf16[2048,256]{1,0:T(8,128)(2,1)}, u32[]{:S(2)}) copy-start(bf16[2048,256]{1,0:T(8,128)(2,1)} %refs_2_.1) | copy-start | bytes 3145732
  9.4 1.2 %copy-start.6 = (bf16[2048,256]{1,0:T(8,128)(2,1)S(1)}, bf16[2048,256]{1,0:T(8,128)(2,1)}, u32[]{:S(2)}) copy-start(bf16[2048,256]{1,0:T(8,128)(2,1)} %refs_3_.1) | copy-start | bytes 3145732
  10.6 0.9 %copy-start.7 = (bf16[256,256]{1,0:T(8,128)(2,1)S(1)}, bf16[256,256]{1,0:T(8,128)(2,1)}, u32[]{:S(2)}) copy-start(bf16[256,256]{1,0:T(8,128)(2,1)} %refs_0_.3) | copy-start | bytes 393220
  11.6 4.2 %copy-start.10 = (s32[256,1]{0,1:T(1,128)S(1)}, s32[256,1]{0,1:T(1,128)}, u32[]{:S(2)}) copy-start(s32[256,1]{0,1:T(1,128)} %param.9) | copy-start | bytes 3076
  11.6 4.2 %copy-start.9 = (s32[256]{0:T(256)S(1)}, s32[256]{0:T(256)}, u32[]{:S(2)}) copy-start(s32[256]{0:T(256)} %param.10) | copy-start | bytes 3076
  11.6 4.2 %copy-start.11 = (s32[256]{0:T(256)S(1)}, s32[256]{0:T(256)}, u32[]{:S(2)}) copy-start(s32[256]{0:T(256)} %param.11) | copy-start | bytes 3076
  11.6 4.3 %copy-start.8 = (bf16[256,256]{1,0:T(8,128)(2,1)S(1)}, bf16[256,256]{1,0:T(8,128)(2,1)}, u32[]{:S(2)}) copy-start(bf16[256,256]{1,0:T(8,128)(2,1)} %refs_0_.3) | copy-start | bytes 393220
  13.3 1.0 %copy-start = (bf16[2048,256]{1,0:T(8,128)(2,1)}, bf16[2048,256]{1,0:T(8,128)(2,1)S(1)}, u32[]{:S(2)}) copy-start(bf16[2048,256]{1,0:T(8,128)(2,1)S(1)} %get-tuple-element.34.refs_2_.second_ref) | copy-start | bytes 3145732
  14.2 9.9 %collective-permute-start = (bf16[256,512]{1,0:T(8,128)(2,1)S(1)}, bf16[256,512]{1,0:T(8,128)(2,1)}, u32[]{:S(2)}, u32[]{:S(2)}) collective-permute-start(bf16[256,512]{1,0:T(8,128)(2,1)S(1)} %get-tuple-element.35), channel_id=1, source_target_pairs={{0,2},{2,0},{1,3},{3,1},{4,6},{6,4},{5,7},{7,5},{8,10},{10,8},{9,1... | collective-permute-start | bytes 786440 | tf_op jit(solution)/shard_map/ppermute | solution.py:273
  15.8 4.2 %collective-permute-start.10 = (s32[8,256]{1,0:T(8,128)S(1)}, s32[8,256]{1,0:T(8,128)S(1)}, u32[]{:S(2)}, u32[]{:S(2)}) collective-permute-start(s32[8,256]{1,0:T(8,128)S(1)} %pad.4), channel_id=1, source_target_pairs={{0,4},{4,0},{8,12},{12,8},{1,5},{5,1},{9,13},{13,9},{2,6},{6,2},{1... | collective-permute-start | bytes 24584 | tf_op jit(solution)/shard_map/ppermute | solution.py:270
  15.9 9.3 %collective-permute-start.2 = (bf16[256,256]{1,0:T(8,128)(2,1)S(1)}, bf16[256,256]{1,0:T(8,128)(2,1)S(1)}, u32[]{:S(2)}, u32[]{:S(2)}) collective-permute-start(bf16[256,256]{1,0:T(8,128)(2,1)S(1)} %copy-done.8), channel_id=1, source_target_pairs={{0,8},{4,12},{8,0},{12,4},{1,9},{5,13},{9,1},{13,5},{2,10},{6,14},... | collective-permute-start | bytes 393224 | tf_op jit(solution)/shard_map/ppermute | solution.py:270
  16.7 23.6 %collective-permute-start.14 = (bf16[256,256]{1,0:T(8,128)(2,1)S(1)}, bf16[256,256]{1,0:T(8,128)(2,1)S(1)}, u32[]{:S(2)}, u32[]{:S(2)}) collective-permute-start(bf16[256,256]{1,0:T(8,128)(2,1)S(1)} %copy-done.8), channel_id=1, source_target_pairs={{0,1},{1,0},{2,3},{3,2},{4,5},{5,4},{6,7},{7,6},{8,9},{9,8},{10,11... | collective-permute-start | bytes 393224 | tf_op jit(solution)/shard_map/ppermute | solution.py:273
  20.0 8.1 %collective-permute-start.11 = (s32[16,256]{1,0:T(8,128)S(1)}, s32[16,256]{1,0:T(8,128)S(1)}, u32[]{:S(2)}, u32[]{:S(2)}) collective-permute-start(s32[16,256]{1,0:T(8,128)S(1)} %pad_add_fusion.1), channel_id=1, source_target_pairs={{0,8},{4,12},{8,0},{12,4},{1,9},{5,13},{9,1},{13,5},{2,10},{6,14},... | collective-permute-start | bytes 49160 | tf_op jit(solution)/shard_map/ppermute | solution.py:270
  20.0 1.2 %copy-start.1 = (bf16[2048,256]{1,0:T(8,128)(2,1)S(1)}, bf16[2048,256]{1,0:T(8,128)(2,1)}, u32[]{:S(2)}) copy-start(bf16[2048,256]{1,0:T(8,128)(2,1)} %copy-done) | copy-start | bytes 3145732
  23.5 9.3 %collective-permute-start.5 = (bf16[256,512]{1,0:T(8,128)(2,1)S(1)}, bf16[256,512]{1,0:T(8,128)(2,1)S(1)}, u32[]{:S(2)}, u32[]{:S(2)}) collective-permute-start(bf16[256,512]{1,0:T(8,128)(2,1)S(1)} %forward.5), channel_id=1, source_target_pairs={{0,2},{2,0},{1,3},{3,1},{4,6},{6,4},{5,7},{7,5},{8,10},{10,8},{9,1... | collective-permute-start | bytes 786440 | tf_op jit(solution)/shard_map/ppermute | solution.py:273
  26.5 13.1 %collective-permute-start.3 = (bf16[256,512]{1,0:T(8,128)(2,1)S(1)}, bf16[256,512]{1,0:T(8,128)(2,1)S(1)}, u32[]{:S(2)}, u32[]{:S(2)}) collective-permute-start(bf16[256,512]{1,0:T(8,128)(2,1)S(1)} %forward.4), channel_id=1, source_target_pairs={{0,2},{2,0},{1,3},{3,1},{4,6},{6,4},{5,7},{7,5},{8,10},{10,8},{9,1... | collective-permute-start | bytes 786440 | tf_op jit(solution)/shard_map/ppermute | solution.py:273
  28.1 5.6 %collective-permute-start.12 = (s32[32,256]{1,0:T(8,128)S(1)}, s32[32,256]{1,0:T(8,128)S(1)}, u32[]{:S(2)}, u32[]{:S(2)}) collective-permute-start(s32[32,256]{1,0:T(8,128)S(1)} %pad_add_fusion.refs_8_), channel_id=1, source_target_pairs={{0,1},{1,0},{2,3},{3,2},{4,5},{5,4},{6,7},{7,6},{8,9},{9,8},{10,11... | collective-permute-start | bytes 98312 | tf_op jit(solution)/shard_map/ppermute | solution.py:273
  28.1 13.0 %collective-permute-start.1 = (bf16[256,512]{1,0:T(8,128)(2,1)S(1)}, bf16[256,512]{1,0:T(8,128)(2,1)S(1)}, u32[]{:S(2)}, u32[]{:S(2)}) collective-permute-start(bf16[256,512]{1,0:T(8,128)(2,1)S(1)} %add_convert_fusion.2.refs_0_), channel_id=1, source_target_pairs={{0,4},{4,0},{8,12},{12,8},{1,5},{5,1},{9,13},{13,9},{2,6},{6,2},{1... | collective-permute-start | bytes 786440 | tf_op jit(solution)/shard_map/ppermute | solution.py:270
  32.8 6.8 %collective-permute-start.13 = (bf16[256,256]{1,0:T(8,128)(2,1)S(1)}, bf16[256,256]{1,0:T(8,128)(2,1)S(1)}, u32[]{:S(2)}, u32[]{:S(2)}) collective-permute-start(bf16[256,256]{1,0:T(8,128)(2,1)S(1)} %copy-done.8), channel_id=1, source_target_pairs={{0,4},{4,0},{8,12},{12,8},{1,5},{5,1},{9,13},{13,9},{2,6},{6,2},{1... | collective-permute-start | bytes 393224 | tf_op jit(solution)/shard_map/ppermute | solution.py:270
  33.7 6.6 %collective-permute-start.17 = (bf16[256,256]{1,0:T(8,128)(2,1)}, bf16[256,256]{1,0:T(8,128)(2,1)S(1)}, u32[]{:S(2)}, u32[]{:S(2)}) collective-permute-start(bf16[256,256]{1,0:T(8,128)(2,1)} %collective-permute-done.4.x_ref.refs_3_), channel_id=1, source_target_pairs={{0,1},{1,0},{2,3},{3,2},{4,5},{5,4},{6,7},{7,6},{8,9},{9,8},{10,11... | collective-permute-start | bytes 393224 | tf_op jit(solution)/shard_map/ppermute | solution.py:273
  39.6 1.3 %collective-permute-start.16 = (bf16[256,256]{1,0:T(8,128)(2,1)S(1)}, bf16[256,256]{1,0:T(8,128)(2,1)S(1)}, u32[]{:S(2)}, u32[]{:S(2)}) collective-permute-start(bf16[256,256]{1,0:T(8,128)(2,1)S(1)} %collective-permute-done.2.x_ref.refs_2_), channel_id=1, source_target_pairs={{0,1},{1,0},{2,3},{3,2},{4,5},{5,4},{6,7},{7,6},{8,9},{9,8},{10,11... | collective-permute-start | bytes 393224 | tf_op jit(solution)/shard_map/ppermute | solution.py:273
  39.6 1.9 %collective-permute-start.15 = (bf16[256,256]{1,0:T(8,128)(2,1)S(1)}, bf16[256,256]{1,0:T(8,128)(2,1)S(1)}, u32[]{:S(2)}, u32[]{:S(2)}) collective-permute-start(bf16[256,256]{1,0:T(8,128)(2,1)S(1)} %collective-permute-done.13.refs_1_), channel_id=1, source_target_pairs={{0,1},{1,0},{2,3},{3,2},{4,5},{5,4},{6,7},{7,6},{8,9},{9,8},{10,11... | collective-permute-start | bytes 393224 | tf_op jit(solution)/shard_map/ppermute | solution.py:273
  40.2 6.6 %collective-permute-start.6 = (bf16[256,512]{1,0:T(8,128)(2,1)S(1)}, bf16[256,512]{1,0:T(8,128)(2,1)S(1)}, u32[]{:S(2)}, u32[]{:S(2)}) collective-permute-start(bf16[256,512]{1,0:T(8,128)(2,1)S(1)} %add_convert_fusion.2.refs_0_), channel_id=1, source_target_pairs={{0,1},{1,0},{2,3},{3,2},{4,5},{5,4},{6,7},{7,6},{8,9},{9,8},{10,11... | collective-permute-start | bytes 786440 | tf_op jit(solution)/shard_map/ppermute | solution.py:273
  40.3 6.5 %collective-permute-start.9 = (bf16[256,512]{1,0:T(8,128)(2,1)S(1)}, bf16[256,512]{1,0:T(8,128)(2,1)S(1)}, u32[]{:S(2)}, u32[]{:S(2)}) collective-permute-start(bf16[256,512]{1,0:T(8,128)(2,1)S(1)} %add_convert_fusion.refs_3_), channel_id=1, source_target_pairs={{0,1},{1,0},{2,3},{3,2},{4,5},{5,4},{6,7},{7,6},{8,9},{9,8},{10,11... | collective-permute-start | bytes 786440 | tf_op jit(solution)/shard_map/ppermute | solution.py:273
  41.0 5.9 %collective-permute-start.8 = (bf16[256,512]{1,0:T(8,128)(2,1)S(1)}, bf16[256,512]{1,0:T(8,128)(2,1)S(1)}, u32[]{:S(2)}, u32[]{:S(2)}) collective-permute-start(bf16[256,512]{1,0:T(8,128)(2,1)S(1)} %add_convert_fusion.1.refs_2_), channel_id=1, source_target_pairs={{0,1},{1,0},{2,3},{3,2},{4,5},{5,4},{6,7},{7,6},{8,9},{9,8},{10,11... | collective-permute-start | bytes 786440 | tf_op jit(solution)/shard_map/ppermute | solution.py:273
  41.1 5.7 %collective-permute-start.7 = (bf16[256,512]{1,0:T(8,128)(2,1)S(1)}, bf16[256,512]{1,0:T(8,128)(2,1)S(1)}, u32[]{:S(2)}, u32[]{:S(2)}) collective-permute-start(bf16[256,512]{1,0:T(8,128)(2,1)S(1)} %collective-permute-done.1.refs_1_), channel_id=1, source_target_pairs={{0,1},{1,0},{2,3},{3,2},{4,5},{5,4},{6,7},{7,6},{8,9},{9,8},{10,11... | collective-permute-start | bytes 786440 | tf_op jit(solution)/shard_map/ppermute | solution.py:273
  46.9 9.5 %copy-start.2 = (bf16[2048,256]{1,0:T(8,128)(2,1)S(1)}, bf16[2048,256]{1,0:T(8,128)(2,1)}, u32[]{:S(2)}) copy-start(bf16[2048,256]{1,0:T(8,128)(2,1)} %copy-done) | copy-start | bytes 3145732
  62.6 8.4 %collective-permute-start.18 = (f32[256,1024]{1,0:T(8,128)S(1)}, f32[256,1024]{1,0:T(8,128)S(1)}, u32[]{:S(2)}, u32[]{:S(2)}) collective-permute-start(f32[256,1024]{1,0:T(8,128)S(1)} %get-tuple-element.46.refs_0_), channel_id=1, source_target_pairs={{0,1},{1,0},{2,3},{3,2},{4,5},{5,4},{6,7},{7,6},{8,9},{9,8},{10,11... | collective-permute-start | bytes 3145736 | tf_op jit(solution)/shard_map/ppermute | solution.py:273
  62.8 8.2 %collective-permute-start.19 = (f32[1024,256]{1,0:T(8,128)S(1)}, f32[1024,256]{1,0:T(8,128)S(1)}, u32[]{:S(2)}, u32[]{:S(2)}) collective-permute-start(f32[1024,256]{1,0:T(8,128)S(1)} %get-tuple-element.47.refs_1_), channel_id=1, source_target_pairs={{0,1},{1,0},{2,3},{3,2},{4,5},{5,4},{6,7},{7,6},{8,9},{9,8},{10,11... | collective-permute-start | bytes 3145736 | tf_op jit(solution)/shard_map/ppermute | solution.py:273
  70.4 3.2 %collective-permute-start.20 = (f32[256,1024]{1,0:T(8,128)S(1)}, f32[256,1024]{1,0:T(8,128)S(1)}, u32[]{:S(2)}, u32[]{:S(2)}) collective-permute-start(f32[256,1024]{1,0:T(8,128)S(1)} %get-tuple-element.52.refs_2_), channel_id=1, source_target_pairs={{0,1},{1,0},{2,3},{3,2},{4,5},{5,4},{6,7},{7,6},{8,9},{9,8},{10,11... | collective-permute-start | bytes 3145736 | tf_op jit(solution)/shard_map/ppermute | solution.py:273
  70.6 4.0 %collective-permute-start.21 = (f32[1024,256]{1,0:T(8,128)S(1)}, f32[1024,256]{1,0:T(8,128)S(1)}, u32[]{:S(2)}, u32[]{:S(2)}) collective-permute-start(f32[1024,256]{1,0:T(8,128)S(1)} %get-tuple-element.53.refs_3_), channel_id=1, source_target_pairs={{0,1},{1,0},{2,3},{3,2},{4,5},{5,4},{6,7},{7,6},{8,9},{9,8},{10,11... | collective-permute-start | bytes 3145736 | tf_op jit(solution)/shard_map/ppermute | solution.py:273

commit v4 on v3

--- a/solution.py
+++ b/solution.py
@@ -21,7 +21,7 @@
     return 0.5 * jnp.tanh(0.5 * v) + 0.5
 
 
-HBM = pl.BlockSpec(memory_space=pl.ANY)
+HBM = pl.BlockSpec(memory_space=pltpu.HBM)
 VMEM = pl.BlockSpec(memory_space=pltpu.VMEM)
 SMEM = pl.BlockSpec(memory_space=pltpu.SMEM)
 
@@ -84,89 +84,126 @@
     return (got[0], got[1:]) if load else got[0]
 
 
-def place_blocks(pos_ref, mine, other, put, n_blk, n_rep, slab):
-    b, s = pos_ref[0], pos_ref[1]
-    for side, blocks in ((s, mine), (1 - s, other)):
-        for k, block in enumerate(blocks):
-            at = jnp.bitwise_xor(b, k)
-            for r in range(n_rep):
-                off = ((side * n_rep + r) * n_blk + at) * slab
-                put(pl.multiple_of(off, slab), block[r * slab : (r + 1) * slab, :])
+def add_kernel(a_ref, b_ref, out_ref):
+    out_ref[...] = (a_ref[...].astype(F32) + b_ref[...].astype(F32)).astype(BF)
+
+
+def both(part, there):
+    return kernel(add_kernel, "both", [(part.shape, BF)], (part, there), limit=4)[0]
+
+
+def place_blocks(pos_ref, blocks, put, n_blk, n_rep, slab):
+    for k, block in enumerate(blocks):
+        at = jnp.bitwise_xor(pos_ref[0], k)
+        for r in range(n_rep):
+            off = (r * n_blk + at) * slab
+            put(pl.multiple_of(off, slab), block[r * slab : (r + 1) * slab, :])
 
 
 def column(row):
     return jnp.broadcast_to(row, (128, row.shape[1])).T[:, :1]
 
 
-def meta_row(pos_ref, meta_mine, meta_other, which, j, n_blk, n_rep, slab):
-    side, r = j // n_rep, j % n_rep
+def meta_row(pos_ref, meta_ref, which, r, n_blk, slab):
     parts = []
     for blk in range(n_blk):
         at = pl.multiple_of(jnp.bitwise_xor(blk, pos_ref[0]) * 8, 8)
-        cols = slice(r * slab, (r + 1) * slab)
-        pair = [ref[pl.ds(at, 8), cols][which : which + 1, :] for ref in (meta_mine, meta_other)]
-        parts.append(jnp.where(pos_ref[1] == side, pair[0], pair[1]))
+        parts.append(meta_ref[pl.ds(at, 8), r * slab : (r + 1) * slab][which : which + 1, :])
     return jnp.concatenate(parts, axis=1).astype(F32)
 
 
 def arrange_kernel(n_blk, n_rep, slab, pos_ref, *refs):
-    mine, other = refs[:n_blk], refs[n_blk : 2 * n_blk]
-    meta_mine, meta_other, all_ref, all_t_ref, goals_ref, goals_t_ref, pick_ref = refs[2 * n_blk :]
-    rows = all_ref.shape[0]
+    mine, other, metas = refs[:n_blk], refs[n_blk : 2 * n_blk], refs[2 * n_blk : 2 * n_blk + 2]
+    rows_mine, rows_other, goals_mine, goals_other, pick_ref, both_sides, pick_other = refs[2 * n_blk + 2 :]
+    half = rows_mine.shape[0]
+    rows = 2 * half
     batch = n_blk * slab
-
-    def put(off, value):
-        all_ref[pl.ds(off, slab), :] = value
-        all_t_ref[:, pl.ds(off, slab)] = value.T
-
-    place_blocks(pos_ref, mine, other, put, n_blk, n_rep, slab)
-    for j in range(rows // batch):
-        own = slice(j * batch, (j + 1) * batch)
-        goal = column(meta_row(pos_ref, meta_mine, meta_other, 0, j, n_blk, n_rep, slab)).astype(jnp.int32)
-        pick_ref[own, :] = jnp.where(
-            goal == lax.broadcasted_iota(jnp.int32, (batch, rows), 1), 1.0, 0.0
-        ).astype(BF)
-    goals = dot(pick_ref[...], all_ref[...]).astype(BF)
-    goals_ref[...] = goals
-    goals_t_ref[...] = goals.T
+    for i, (blocks, to) in enumerate(((mine, rows_mine), (other, rows_other))):
+
+        def put(off, value, i=i, to=to):
+            to[pl.ds(off, slab), :] = value
+            both_sides[pl.ds(i * half + off, slab), :] = value
+
+        place_blocks(pos_ref, blocks, put, n_blk, n_rep, slab)
+    for meta, pick, goals in ((metas[0], pick_ref, goals_mine), (metas[1], pick_other, goals_other)):
+        for r in range(n_rep):
+            own = slice(r * batch, (r + 1) * batch)
+            goal = column(meta_row(pos_ref, meta, 0, r, n_blk, slab)).astype(jnp.int32) + pos_ref[1] * half
+            goal = jnp.where(goal >= rows, goal - rows, goal)
+            pick[own, :] = jnp.where(
+                goal == lax.broadcasted_iota(jnp.int32, (batch, rows), 1), 1.0, 0.0
+            ).astype(BF)
+        goals[...] = dot(pick[...], both_sides[...]).astype(BF)
 
 
 def contrast_kernel(n_blk, n_rep, slab, scale, pos_ref, *refs):
-    mine, other = refs[:n_blk], refs[n_blk : 2 * n_blk]
-    meta_mine, meta_other, pick_ref = refs[2 * n_blk : 2 * n_blk + 3]
-    phi_grad_ref, phi_grad_t_ref, psi_grad_ref, psi_grad_t_ref, phi_all, psi_all = refs[2 * n_blk + 3 :]
-    emb = phi_all.shape[1]
+    n = n_blk + 1
+    mine, other, meta_ref, pick_ref = refs[:n], refs[n : 2 * n], refs[2 * n], refs[2 * n + 1]
+    grads_ref, phi_all, psi_all = refs[2 * n + 2 :]
+    half, emb = phi_all.shape
     batch = n_blk * slab
-    rows = phi_all.shape[0]
-
-    def put(off, value):
+    last = n_blk - 2
+
+    def sums(parts):
+        blocks = list(parts[:n_blk])
+        blocks[last] = (parts[last][...].astype(F32) + parts[n_blk][...].astype(F32)).astype(BF)
+        return blocks
+
+    def put_mine(off, value):
         phi_all[pl.ds(off, slab), :] = value[:, :emb]
         psi_all[pl.ds(off, slab), :] = value[:, emb:]
 
-    place_blocks(pos_ref, mine, other, put, n_blk, n_rep, slab)
-
-    for j in range(rows // batch):
-        own = slice(j * batch, (j + 1) * batch)
-        ep_row = meta_row(pos_ref, meta_mine, meta_other, 1, j, n_blk, n_rep, slab)
+    def put_other(off, value):
+        psi_all[pl.ds(half + off, slab), :] = value[:, emb:]
+
+    place_blocks(pos_ref, sums(mine), put_mine, n_blk, n_rep, slab)
+    place_blocks(pos_ref, sums(other), put_other, n_blk, n_rep, slab)
+    diagonal = lax.broadcasted_iota(jnp.int32, (batch, batch), 0) == lax.broadcasted_iota(
+        jnp.int32, (batch, batch), 1
+    )
+    for r in range(n_rep):
+        own = slice(r * batch, (r + 1) * batch)
+        ep_row = meta_row(pos_ref, meta_ref, 1, r, n_blk, slab)
         psi = dot(pick_ref[own, :], psi_all[...]).astype(BF)
         phi = phi_all[own, :]
-        scores = lax.dot_general(phi, psi, (((1,), (1,)), ((), ())), preferred_element_type=F32) * scale
-        diagonal = lax.broadcasted_iota(jnp.int32, (batch, batch), 0) == lax.broadcasted_iota(
-            jnp.int32, (batch, batch), 1
-        )
-        same = column(ep_row) == ep_row
-        exponent = jnp.where(same & ~diagonal, 0.0, jnp.exp(scores))
+        scores = lax.dot_general(phi, psi, (((1,), (1,)), ((), ())), preferred_element_type=F32)
+        kept = (column(ep_row) != ep_row) | diagonal
+        exponent = jnp.where(kept, jnp.exp(scores * scale), 0.0)
         totals = jnp.sum(exponent, axis=1, keepdims=True)
-        delta = (exponent / totals - diagonal.astype(F32)).astype(BF)
-        phi_grad = (dot(delta, psi) * scale).astype(BF)
-        phi_grad_ref[own, :] = phi_grad
-        phi_grad_t_ref[:, own] = phi_grad.T
-        psi_grad = (dot(delta.T, phi) * scale).astype(BF)
-        psi_grad_ref[own, :] = psi_grad
-        psi_grad_t_ref[:, own] = psi_grad.T
-
-
-def backward_kernel(n_put, pos_ref, first_ref, second_ref, grad_ref, grad_t_ref, states_ref, states_t_ref, *refs):
+        power = jnp.where(totals > 1.0, 2.0**-32, 1.0)
+        shares = (exponent * power) * (1.0 / (totals * power))
+        delta = jnp.where(diagonal, shares - 1.0, shares).astype(BF)
+        grads_ref[own, :emb] = (dot(delta, psi) * scale).astype(BF)
+        grads_ref[own, emb:] = (dot(delta.T, phi) * scale).astype(BF)
+
+
+def rows_grads(at, first_ref, second_ref, grads_ref, k, rows_ref, active, back):
+    quarter, rows = active.shape
+    emb = second_ref.shape[1]
+    first_t = first_ref[:, pl.ds(at, quarter)].T
+    second = second_ref[pl.ds(at, quarter), :]
+    grad = grads_ref[:, k * emb : (k + 1) * emb]
+    chunk = 512
+    for c in range(0, rows, chunk):
+        cols = slice(c, c + chunk)
+        hidden = dot(first_t, rows_ref[cols, :].T)
+        sig = sigmoid(hidden)
+        act = hidden * sig
+        active[:, cols] = act.astype(BF)
+        slope = sig + act * (1.0 - sig)
+        back[:, cols] = (dot(second, grad[cols, :].T) * slope).astype(BF)
+    return dot(active[...], grad), dot(back[...], rows_ref[...])
+
+
+def mine_kernel(pos_ref, sf, gf, ss, gs, grads_ref, rows_ref, goals_ref, *refs):
+    outs, (active, back) = refs[:4], refs[4:]
+    quarter = active.shape[0]
+    at = pl.multiple_of(pos_ref[1] * quarter, quarter)
+    outs[0][...], outs[1][...] = rows_grads(at, sf, ss, grads_ref, 0, rows_ref, active, back)
+    outs[2][...], outs[3][...] = rows_grads(at, gf, gs, grads_ref, 1, goals_ref, active, back)
+
+
+def other_kernel(k, n_put, pos_ref, first, second, grads_ref, rows_ref, sum_second, sum_first, *refs):
     done, (gf_ref, gs_ref), outs, (active, back), sems = (
         refs[:n_put],
         refs[n_put : n_put + 2],
@@ -177,21 +214,11 @@
     copies = [put_half(pos_ref[1], x, o, sems[0].at[i]) for i, (x, o) in enumerate(zip(done, outs))]
     for c in copies:
         c.start()
-    quarter, rows = active.shape
+    quarter = active.shape[0]
     at = pl.multiple_of(pos_ref[1] * quarter, quarter)
-    first_t = first_ref[:, pl.ds(at, quarter)].T
-    second = second_ref[pl.ds(at, quarter), :]
-    chunk = 512
-    for c in range(0, rows, chunk):
-        cols = slice(c, c + chunk)
-        hidden = dot(first_t, states_t_ref[:, cols])
-        sig = sigmoid(hidden)
-        act = hidden * sig
-        active[:, cols] = act.astype(BF)
-        slope = sig + act * (1.0 - sig)
-        back[:, cols] = (dot(second, grad_t_ref[:, cols]) * slope).astype(BF)
-    gs_ref[...] = dot(active[...], grad_ref[...])
-    gf_ref[...] = dot(back[...], states_ref[...]).T
+    grad_second, grad_first = rows_grads(at, first, second, grads_ref, k, rows_ref, active, back)
+    gs_ref[...] = sum_second[...] + grad_second
+    gf_ref[...] = (sum_first[...] + grad_first).T
     for c in copies:
         c.wait()
 
@@ -203,24 +230,6 @@
     else:
         to = out.at[pl.ds(pl.multiple_of(side * n, n), n), :]
     return pltpu.make_async_copy(half, to, sem)
-
-
-def backward(pos, first, second, grad, grad_t, states, states_t, quarter, done=()):
-    rows, width = states.shape
-    emb = second.shape[1]
-    halves = [((width, quarter), F32), ((quarter, emb), F32)]
-    return kernel(
-        functools.partial(backward_kernel, len(done)),
-        "backward",
-        halves + [((width, 2 * quarter), F32), ((2 * quarter, emb), F32)][: len(done)],
-        (first, second, grad, grad_t, states, states_t, *done),
-        [pltpu.VMEM((quarter, rows), BF), pltpu.VMEM((quarter, rows), BF)]
-        + [pltpu.SemaphoreType.DMA((2,))] * bool(done),
-        limit=28,
-        pos=pos,
-        flops=8 * rows * width * quarter,
-        hbm_out=(2, 3),
-    )
 
 
 def finish_kernel(old, new, pos_ref, *refs):
@@ -275,12 +284,10 @@
     def after(x, *first):
         return lax.optimization_barrier((x, *first))[0]
 
-    def both(part, there):
-        return (part.astype(F32) + there.astype(F32)).astype(BF)
-
     got = {0: states, 3: across(states, 3), 2: across(states, 2)}
     part0, weights = forward(states, (state_first, goal_first, state_second, goal_second), load=True)
     there0 = swap(part0, "rep")
+    got[1] = across(after(states, part0), 1)
     part3 = forward(got[3], weights)
     there3 = swap(part3, "rep")
 
@@ -296,48 +303,66 @@
     sums[1] = across(sums[0], 1)
     part2 = forward(after(got[2], sums[0]), weights)
     there2 = swap(part2, "rep")
-    got[1] = across(after(states, part2), 1)
     sums[3] = both(part3, there3)
-    sums[2] = both(part2, there2)
-
-    others = [swap(got[k], "sub") for k in range(n_blk)]
-    wide, tall = ((rows_all, width), BF), ((width, rows_all), BF)
-    all_states, all_states_t, goals, goals_t, pick = kernel(
+    embedded = [sums[0], sums[1], part2, sums[3], there2]
+
+    side = ((rows_all // 2, width), BF)
+    mine, other, goals_mine, goals_other, pick = kernel(
         functools.partial(arrange_kernel, n_blk, n_rep, slab),
         "arrange",
-        [wide, tall, wide, tall, ((rows_all, rows_all), BF)],
-        (*(got[k] for k in range(n_blk)), *others, meta, meta_other),
+        [side, side, side, side, ((rows_all // 2, rows_all), BF)],
+        (*(got[k] for k in range(n_blk)), *(swap(got[k], "sub") for k in range(n_blk)), meta, meta_other),
+        [pltpu.VMEM((rows_all, width), BF), pltpu.VMEM((rows_all // 2, rows_all), BF)],
         pos=pos,
         flops=2 * rows_all * rows_all * width,
     )
-
-    other_sums = [swap(sums[k], "sub") for k in range(n_blk)]
-    wide, tall = ((rows_all, emb), BF), ((emb, rows_all), BF)
-    phi_grad, phi_grad_t, psi_grad, psi_grad_t = kernel(
+    (grads_mine,) = kernel(
         functools.partial(contrast_kernel, n_blk, n_rep, slab, 4.0 / math.sqrt(emb)),
         "contrast",
-        [wide, tall, wide, tall],
-        (*(sums[k] for k in range(n_blk)), *other_sums, meta, meta_other, pick),
-        [pltpu.VMEM((rows_all, emb), BF), pltpu.VMEM((rows_all, emb), BF)],
-        pos=pos,
-        flops=2 * rows_all * emb * (rows_all + 3 * n_blk * slab),
-    )
+        [((rows_all // 2, 2 * emb), BF)],
+        (*embedded, *(swap(x, "sub") for x in embedded), meta, pick),
+        [pltpu.VMEM((rows_all // 2, emb), BF), pltpu.VMEM((rows_all, emb), BF)],
+        pos=pos,
+        flops=rows_all * emb * (rows_all + 3 * n_blk * slab),
+    )
+    grads_other = swap(grads_mine, "sub")
 
     sf, gf, ss, gs = weights
-    state_first_half, state_second_half = backward(
-        pos, sf, ss, phi_grad, phi_grad_t, all_states, all_states_t, quarter
-    )
-    state_there = [swap(x, "sub") for x in (state_first_half, state_second_half)]
-    goal_first_half, goal_second_half, out0, out1 = backward(
-        pos, gf, gs, psi_grad, psi_grad_t, goals, goals_t, quarter, (state_first_half, state_second_half)
-    )
-    goal_there = [swap(x, "sub") for x in (goal_first_half, goal_second_half)]
-    out0, out1, out2, out3 = finish(
-        pos,
-        (*state_there, goal_first_half, goal_second_half),
-        (out0, out1),
-        [((width, hid), F32), ((hid, emb), F32)],
-    )
+    work = [pltpu.VMEM((quarter, rows_all // 2), BF), pltpu.VMEM((quarter, rows_all // 2), BF)]
+    flops = 4 * rows_all * width * quarter
+    sums_s2, sums_s1, sums_g2, sums_g1 = kernel(
+        mine_kernel,
+        "mine",
+        [((quarter, emb), F32), ((quarter, width), F32)] * 2,
+        (sf, gf, ss, gs, grads_mine, mine, goals_mine),
+        work,
+        pos=pos,
+        flops=2 * flops,
+    )
+    halves = [((width, quarter), F32), ((quarter, emb), F32)]
+    wholes = [((width, hid), F32), ((hid, emb), F32)]
+    state_halves = kernel(
+        functools.partial(other_kernel, 0, 0),
+        "other_state",
+        halves,
+        (sf, ss, grads_other, other, sums_s2, sums_s1),
+        work,
+        pos=pos,
+        flops=flops,
+    )
+    state_there = [swap(x, "sub") for x in state_halves]
+    *goal_halves, out0, out1 = kernel(
+        functools.partial(other_kernel, 1, 2),
+        "other_goal",
+        halves + wholes,
+        (gf, gs, grads_other, goals_other, sums_g2, sums_g1, *state_halves),
+        work + [pltpu.SemaphoreType.DMA((2,))],
+        pos=pos,
+        flops=flops,
+        hbm_out=(2, 3),
+    )
+    goal_there = [swap(x, "sub") for x in goal_halves]
+    out0, out1, out2, out3 = finish(pos, (*state_there, *goal_halves), (out0, out1), wholes)
     out2, out3 = finish(pos, goal_there, (out2, out3), [])
     return (out0, out1, out2, out3)
 

time: 77.1 us -> 70 us (0.908)
  Pallas kernels: 38 us -> 33.7 us
  waiting for transfers between devices: 14.2 us -> 10.7 us
  starting transfers between devices: 14.1 us -> 15.8 us
  other arithmetic: 1.26 us -> 0.12 us
    ppermute x6, waiting for transfers between devices: 9.22 us -> 2.15 us  [across(): return lax.ppermute(x, 'blk', [(i, i ^ k) for i in range(n_blk)])]
    pallas_call x9 -> x12, Pallas kernels: 38 us -> 33.7 us  [kernel(): pl.pallas_call(body, in_specs=specs, out_specs=[HBM if i in hbm_out else...]
    ppermute x16 -> x18, waiting for transfers between devices: 5.03 us -> 8.59 us  [swap(): return lax.ppermute(x, axis, [(0, 1), (1, 0)])]
    ppermute x6, starting transfers between devices: 7.68 us -> 8.83 us  [across(): return lax.ppermute(x, 'blk', [(i, i ^ k) for i in range(n_blk)])]
    convert_element_type x3 -> x0, other arithmetic: 1.15 us -> none  [both(): return (part.astype(F32) + there.astype(F32)).astype(BF)]
    ppermute x16 -> x18, starting transfers between devices: 6.46 us -> 6.96 us  [swap(): return lax.ppermute(x, axis, [(0, 1), (1, 0)])]
  transfers between devices with their start and end apart: 22 -> 24, of which waited for: 5 -> 5; matrix products, arithmetic and copies ran while one was open for 2% -> 0% of each run, Pallas kernels for 27% -> 33%
where the time goes in v4:
time: 70 us; the launch traced here: 69.6 us
  Pallas kernels  33.7 us (48%)
  starting transfers between devices  15.8 us (23%)
  waiting for transfers between devices  10.7 us (15%)
  local copies, waits for them, and re-layouts  8.02 us (11%)
  between operations  1.24 us (2%)
    pallas_call x12, Pallas kernels, kernel(): pl.pallas_call(body, in_specs=specs, out_specs=[HBM if i in hbm_out else...  33.7 us
    ppermute x6, starting transfers between devices, across(): return lax.ppermute(x, 'blk', [(i, i ^ k) for i in range(n_blk)])  8.83 us
    ppermute x18, waiting for transfers between devices, swap(): return lax.ppermute(x, axis, [(0, 1), (1, 0)])  8.59 us
    unnamed x24, local copies, waits for them, and re-layouts  8.01 us
    ppermute x18, starting transfers between devices, swap(): return lax.ppermute(x, axis, [(0, 1), (1, 0)])  6.96 us
    ppermute x6, waiting for transfers between devices, across(): return lax.ppermute(x, 'blk', [(i, i ^ k) for i in range(n_blk)])  2.15 us
  transfers between devices with their start and end apart: 24, of which 5 were waited for; matrix products, arithmetic and copies ran while one was open for 0% of the time, Pallas kernels for 33%

profile of v4, /device:TPU:0, one launch (start us, length us, event | category | flops | bytes accessed | tf_op | source)
XLA Modules:
  0.0 69.6 jit_solution(44156019282277437)
XLA Ops:
  0.6 5.1 %collective-permute-start.3 = (bf16[256,256]{1,0:T(8,128)(2,1)}, bf16[256,256]{1,0:T(8,128)(2,1)}, u32[]{:S(2)}, u32[]{:S(2)}) collective-permute-start(bf16[256,256]{1,0:T(8,128)(2,1)} %refs_0_.3), channel_id=1, source_target_pairs={{0,12},{4,8},{8,4},{12,0},{1,13},{5,9},{9,5},{13,1},{2,14},{6,10},... | collective-permute-start | bytes 393224 | tf_op jit(solution)/shard_map/ppermute | solution.py:279
  5.8 1.2 %copy-done.3 = bf16[256,2048]{1,0:T(8,128)(2,1)S(1)} copy-done((bf16[256,2048]{1,0:T(8,128)(2,1)S(1)}, bf16[256,2048]{1,0:T(8,128)(2,1)}, u32[]{:S(2)}) %copy-start.3) | copy-done | bytes 1048600
  7.0 1.2 %copy-done.4 = bf16[256,2048]{1,0:T(8,128)(2,1)S(1)} copy-done((bf16[256,2048]{1,0:T(8,128)(2,1)S(1)}, bf16[256,2048]{1,0:T(8,128)(2,1)}, u32[]{:S(2)}) %copy-start.4) | copy-done | bytes 1048600
  8.2 1.2 %copy-done.5 = bf16[2048,256]{1,0:T(8,128)(2,1)S(1)} copy-done((bf16[2048,256]{1,0:T(8,128)(2,1)S(1)}, bf16[2048,256]{1,0:T(8,128)(2,1)}, u32[]{:S(2)}) %copy-start.5) | copy-done | bytes 1048600
  9.4 1.2 %copy-done.6 = bf16[2048,256]{1,0:T(8,128)(2,1)S(1)} copy-done((bf16[2048,256]{1,0:T(8,128)(2,1)S(1)}, bf16[2048,256]{1,0:T(8,128)(2,1)}, u32[]{:S(2)}) %copy-start.6) | copy-done | bytes 1048600
  10.7 0.9 %copy-done.7 = bf16[256,256]{1,0:T(8,128)(2,1)S(1)} copy-done((bf16[256,256]{1,0:T(8,128)(2,1)S(1)}, bf16[256,256]{1,0:T(8,128)(2,1)}, u32[]{:S(2)}) %copy-start.7) | copy-done | bytes 131096
  11.6 1.7 %forward.3 = (bf16[256,512]{1,0:T(8,128)(2,1)S(1)}, bf16[256,2048]{1,0:T(8,128)(2,1)S(1)}, bf16[256,2048]{1,0:T(8,128)(2,1)S(1)}, bf16[2048,256]{1,0:T(8,128)(2,1)S(1)}, bf16[2048,256]{1,0:T(8,128)(2,1)S(1)}) custom-call(bf16[256,256]{1,0:T(8,128)(2,1)S(1)} %copy-done.7, bf16[256,2048]{1,0:T(8,128)(2,1)S(1)} %copy-done.3, bf16[256,2048]{1,0:T(8,128)(2,1)S(1)} %copy-done.4, ...), custom_call_target="tpu_custom_call" | custom-call | flops 1073741824 | tf_op jit(solution)/shard_map/forward/pallas_call | solution.py:34
  13.3 0.0 copy-start
  13.3 1.0 %copy-done = bf16[2048,256]{1,0:T(8,128)(2,1)} copy-done((bf16[2048,256]{1,0:T(8,128)(2,1)}, bf16[2048,256]{1,0:T(8,128)(2,1)S(1)}, u32[]{:S(2)}) %copy-start) | copy-done | bytes 1048600
  14.3 0.1 collective-permute-start.11
  14.4 0.6 collective-permute-start.2
  15.0 0.0 collective-permute-start.14
  15.0 1.7 %collective-permute-start = (bf16[256,512]{1,0:T(8,128)(2,1)S(1)}, bf16[256,512]{1,0:T(8,128)(2,1)S(1)}, u32[]{:S(2)}, u32[]{:S(2)}) collective-permute-start(bf16[256,512]{1,0:T(8,128)(2,1)S(1)} %get-tuple-element.35.a_ref), channel_id=1, source_target_pairs={{0,2},{2,0},{1,3},{3,1},{4,6},{6,4},{5,7},{7,5},{8,10},{10,8},{9,1... | collective-permute-start | bytes 786440 | tf_op jit(solution)/shard_map/ppermute | solution.py:282
  16.7 2.1 %collective-permute-done.11 = s32[8,256]{1,0:T(8,128)S(1)} collective-permute-done((s32[8,256]{1,0:T(8,128)S(1)}, s32[8,256]{1,0:T(8,128)S(1)}, u32[]{:S(2)}, u32[]{:S(2)}) %collective-permute-start.11) | collective-permute-done | bytes 8224 | tf_op jit(solution)/shard_map/ppermute | solution.py:279
  18.8 0.0 collective-permute-start.13
  18.8 0.0 collective-permute-done.3.x_ref.refs_3_
  18.8 2.0 %collective-permute-start.12 = (s32[16,256]{1,0:T(8,128)S(1)}, s32[16,256]{1,0:T(8,128)S(1)}, u32[]{:S(2)}, u32[]{:S(2)}) collective-permute-start(s32[16,256]{1,0:T(8,128)S(1)} %pad_add_fusion.1), channel_id=1, source_target_pairs={{0,8},{4,12},{8,0},{12,4},{1,9},{5,13},{9,1},{13,5},{2,10},{6,14},... | collective-permute-start | bytes 49160 | tf_op jit(solution)/shard_map/ppermute | solution.py:279
  20.8 1.2 %copy-done.1 = bf16[2048,256]{1,0:T(8,128)(2,1)S(1)} copy-done((bf16[2048,256]{1,0:T(8,128)(2,1)S(1)}, bf16[2048,256]{1,0:T(8,128)(2,1)}, u32[]{:S(2)}) %copy-start.1) | copy-done | bytes 1048600
  22.1 2.3 %forward.5.a_ref = bf16[256,512]{1,0:T(8,128)(2,1)S(1)} custom-call(bf16[256,256]{1,0:T(8,128)(2,1)} %collective-permute-done.3.x_ref.refs_3_, bf16[256,2048]{1,0:T(8,128)(2,1)S(1)} %get-tuple-element.33.refs_0_.sf.first, bf16[256,2048]{1,0:T(8,128)(2,1)S(1)} %get-tuple-element.37.refs_1_.gf.first, bf16[2048,256]{1,0:T(8,128)(2,1)S(1)} %copy-done.1, ...), custom_call_target="tpu_custom_call" | custom-call | flops 1073741824 | tf_op jit(solution)/shard_map/forward/pallas_call | solution.py:34
  24.3 0.0 collective-permute-done.12
  24.3 0.8 %collective-permute-start.4 = (bf16[256,512]{1,0:T(8,128)(2,1)S(1)}, bf16[256,512]{1,0:T(8,128)(2,1)S(1)}, u32[]{:S(2)}, u32[]{:S(2)}) collective-permute-start(bf16[256,512]{1,0:T(8,128)(2,1)S(1)} %forward.5.a_ref), channel_id=1, source_target_pairs={{0,2},{2,0},{1,3},{3,1},{4,6},{6,4},{5,7},{7,5},{8,10},{10,8},{9,1... | collective-permute-start | bytes 786440 | tf_op jit(solution)/shard_map/ppermute | solution.py:282
  25.2 0.0 collective-permute-done.b_ref
  25.2 0.0 collective-permute-start.18
  25.2 0.1 both.2.refs_0_
  25.3 1.4 %forward.4.refs_2_ = bf16[256,512]{1,0:T(8,128)(2,1)S(1)} custom-call(bf16[256,256]{1,0:T(8,128)(2,1)S(1)} %collective-permute-done.2.x_ref.refs_2_, bf16[256,2048]{1,0:T(8,128)(2,1)S(1)} %get-tuple-element.33.refs_0_.sf.first, bf16[256,2048]{1,0:T(8,128)(2,1)S(1)} %get-tuple-element.37.refs_1_.gf.first, bf16[2048,256]{1,0:T(8,128)(2,1)S(1)} %copy-done.1, ...), custom_call_target="tpu_custom_call" | custom-call | flops 1073741824 | tf_op jit(solution)/shard_map/forward/pallas_call | solution.py:34
  26.6 1.3 %collective-permute-start.5 = (bf16[256,512]{1,0:T(8,128)(2,1)S(1)}, bf16[256,512]{1,0:T(8,128)(2,1)S(1)}, u32[]{:S(2)}, u32[]{:S(2)}) collective-permute-start(bf16[256,512]{1,0:T(8,128)(2,1)S(1)} %forward.4.refs_2_), channel_id=1, source_target_pairs={{0,2},{2,0},{1,3},{3,1},{4,6},{6,4},{5,7},{7,5},{8,10},{10,8},{9,1... | collective-permute-start | bytes 786440 | tf_op jit(solution)/shard_map/ppermute | solution.py:282
  28.0 0.0 collective-permute-done.18.refs_9_
  28.0 1.1 %collective-permute-start.1 = (bf16[256,512]{1,0:T(8,128)(2,1)S(1)}, bf16[256,512]{1,0:T(8,128)(2,1)S(1)}, u32[]{:S(2)}, u32[]{:S(2)}) collective-permute-start(bf16[256,512]{1,0:T(8,128)(2,1)S(1)} %both.2.refs_0_), channel_id=1, source_target_pairs={{0,4},{4,0},{8,12},{12,8},{1,5},{5,1},{9,13},{13,9},{2,6},{6,2},{1... | collective-permute-start | bytes 786440 | tf_op jit(solution)/shard_map/ppermute | solution.py:279
  29.0 0.0 collective-permute-done.13.refs_1_
  29.0 0.0 collective-permute-start.15
  29.0 0.0 collective-permute-done.14.refs_4_
  29.1 0.5 collective-permute-start.16
  29.6 4.1 %collective-permute-done.4.b_ref = bf16[256,512]{1,0:T(8,128)(2,1)S(1)} collective-permute-done((bf16[256,512]{1,0:T(8,128)(2,1)S(1)}, bf16[256,512]{1,0:T(8,128)(2,1)S(1)}, u32[]{:S(2)}, u32[]{:S(2)}) %collective-permute-start.4) | collective-permute-done | bytes 262176 | tf_op jit(solution)/shard_map/ppermute | solution.py:282
  33.6 0.0 collective-permute-start.17
  33.6 0.1 both.3.refs_3_
  33.7 0.6 collective-permute-start.8
  34.3 0.0 collective-permute-done.16.refs_6_
  34.3 0.1 collective-permute-start.6
  34.4 0.8 %collective-permute-done.17.refs_7_ = bf16[256,256]{1,0:T(8,128)(2,1)S(1)} collective-permute-done((bf16[256,256]{1,0:T(8,128)(2,1)}, bf16[256,256]{1,0:T(8,128)(2,1)S(1)}, u32[]{:S(2)}, u32[]{:S(2)}) %collective-permute-start.17) | collective-permute-done | bytes 131104 | tf_op jit(solution)/shard_map/ppermute | solution.py:282
  35.2 0.1 collective-permute-start.9
  35.3 2.6 %collective-permute-done.5.refs_4_ = bf16[256,512]{1,0:T(8,128)(2,1)S(1)} collective-permute-done((bf16[256,512]{1,0:T(8,128)(2,1)S(1)}, bf16[256,512]{1,0:T(8,128)(2,1)S(1)}, u32[]{:S(2)}, u32[]{:S(2)}) %collective-permute-start.5) | collective-permute-done | bytes 262176 | tf_op jit(solution)/shard_map/ppermute | solution.py:282
  37.9 0.5 collective-permute-start.7
  38.4 0.1 pad_add_fusion.3.pos_ref
  38.5 4.4 %arrange.1 = (bf16[1024,256]{1,0:T(8,128)(2,1)S(1)}, bf16[1024,256]{1,0:T(8,128)(2,1)S(1)}, bf16[1024,256]{1,0:T(8,128)(2,1)S(1)}, bf16[1024,256]{1,0:T(8,128)(2,1)S(1)}, bf16[1024,2048]{1,0:T(8,128)(2,1)S(1)}) custom-call(s32[2]{0:T(128)S(1)} %pad_add_fusion.3.pos_ref, bf16[256,256]{1,0:T(8,128)(2,1)S(1)} %copy-done.8, ...), custom_call_target="tpu_custom_call" | custom-call | flops 2147483648 | tf_op jit(solution)/shard_map/arrange/pallas_call | solution.py:34
  42.9 0.0 collective-permute-done.8.refs_7_
  42.9 0.0 collective-permute-done.6.refs_5_
  42.9 0.0 collective-permute-done.10.refs_9_
  42.9 0.0 collective-permute-done.7.refs_6_
  42.9 0.0 copy-start.2
  43.0 5.1 %contrast.1.grads_ref = bf16[1024,512]{1,0:T(8,128)(2,1)S(1)} custom-call(s32[2]{0:T(128)S(1)} %pad_add_fusion.3.pos_ref, bf16[256,512]{1,0:T(8,128)(2,1)S(1)} %both.2.refs_0_, bf16[256,512]{1,0:T(8,128)(2,1)S(1)} %collective-permute-done.1.refs_1_, bf16[256,512]{1,0:T(8,128)(2,1)S(1)} %forward.4.refs_2_, bf16[256,512]{1,0:T(8,128)(2,1)S(1)} %both.3.refs_3_, ...), custom_call_target="tpu_custom_call" | custom-call | flops 1879048192 | tf_op jit(solution)/shard_map/contrast/pallas_call | solution.py:34
  48.2 0.1 collective-permute-start.19
  48.3 6.1 %mine.1 = (f32[1024,256]{1,0:T(8,128)S(1)}, f32[1024,256]{1,0:T(8,128)S(1)}, f32[1024,256]{1,0:T(8,128)S(1)}, f32[1024,256]{1,0:T(8,128)S(1)}) custom-call(s32[2]{0:T(128)S(1)} %pad_add_fusion.3.pos_ref, bf16[256,2048]{1,0:T(8,128)(2,1)S(1)} %get-tuple-element.33.refs_0_.sf.first, bf16[256,2048]{1,0:T(8,128)(2,1)S(1)} %get-tuple-element.37.refs_1_.gf.first, ...), custom_call_target="tpu_custom_call" | custom-call | flops 4294967296 | tf_op jit(solution)/shard_map/mine/pallas_call | solution.py:34
  54.4 3.5 %other_state.1 = (f32[256,1024]{1,0:T(8,128)S(1)}, f32[1024,256]{1,0:T(8,128)S(1)}) custom-call(s32[2]{0:T(128)S(1)} %pad_add_fusion.3.pos_ref, bf16[256,2048]{1,0:T(8,128)(2,1)S(1)} %get-tuple-element.33.refs_0_.sf.first, bf16[2048,256]{1,0:T(8,128)(2,1)S(1)} %copy-done.2, bf16[1024,512]{1,0:T(8,128)(2,1)S(1)} %collective-permute-done.19.grads_ref, ...), custom_call_target="tpu_custom_call" | custom-call | flops 2147483648 | tf_op jit(solution)/shard_map/other_state/pallas_call | solution.py:34
  57.9 0.6 collective-permute-start.20
  58.5 0.1 collective-permute-start.21
  58.5 4.7 %other_goal.1 = (f32[256,1024]{1,0:T(8,128)S(1)}, f32[1024,256]{1,0:T(8,128)S(1)}, f32[256,2048]{1,0:T(8,128)}, f32[2048,256]{1,0:T(8,128)}) custom-call(s32[2]{0:T(128)S(1)} %pad_add_fusion.3.pos_ref, bf16[256,2048]{1,0:T(8,128)(2,1)S(1)} %get-tuple-element.37.refs_1_.gf.first, bf16[2048,256]{1,0:T(8,128)(2,1)S(1)} %get-tuple-element.38.refs_3_.gs.second, ...), custom_call_target="tpu_custom_call" | custom-call | flops 2147483648 | tf_op jit(solution)/shard_map/other_goal/pallas_call | solution.py:34
  63.3 0.5 collective-permute-start.22
  63.8 0.1 collective-permute-start.23
  63.9 0.0 collective-permute-done.20.refs_0_
  63.9 0.0 collective-permute-done.21.refs_1_
  63.9 2.6 %finish.2 = (f32[256,2048]{1,0:T(8,128)}, f32[2048,256]{1,0:T(8,128)}, f32[256,2048]{1,0:T(8,128)}, f32[2048,256]{1,0:T(8,128)}) custom-call(s32[2]{0:T(128)S(1)} %pad_add_fusion.3.pos_ref, f32[256,1024]{1,0:T(8,128)S(1)} %collective-permute-done.20.refs_0_, ...), custom_call_target="tpu_custom_call", output_to_operand_aliasing={{0}: (5, {}), {1}: (6, {})} | custom-call | tf_op jit(solution)/shard_map/finish/pallas_call | solution.py:34
  66.5 0.0 collective-permute-done.22.refs_0_
  66.5 1.1 %collective-permute-done.23.refs_1_ = f32[1024,256]{1,0:T(8,128)S(1)} collective-permute-done((f32[1024,256]{1,0:T(8,128)S(1)}, f32[1024,256]{1,0:T(8,128)S(1)}, u32[]{:S(2)}, u32[]{:S(2)}) %collective-permute-start.23) | collective-permute-done | bytes 1048608 | tf_op jit(solution)/shard_map/ppermute | solution.py:282
  67.6 1.9 %finish.3 = (f32[256,2048]{1,0:T(8,128)}, f32[2048,256]{1,0:T(8,128)}) custom-call(s32[2]{0:T(128)S(1)} %pad_add_fusion.3.pos_ref, f32[256,1024]{1,0:T(8,128)S(1)} %collective-permute-done.22.refs_0_, f32[1024,256]{1,0:T(8,128)S(1)} %collective-permute-done.23.refs_1_, ...), custom_call_target="tpu_custom_call", output_to_operand_aliasing={{0}: (3, {}), {1}: (4, {})} | custom-call | tf_op jit(solution)/shard_map/finish/pallas_call | solution.py:34
  (27 shorter events, 0.1 us)
Async XLA Ops:
  0.6 18.2 %collective-permute-start.3 = (bf16[256,256]{1,0:T(8,128)(2,1)}, bf16[256,256]{1,0:T(8,128)(2,1)}, u32[]{:S(2)}, u32[]{:S(2)}) collective-permute-start(bf16[256,256]{1,0:T(8,128)(2,1)} %refs_0_.3), channel_id=1, source_target_pairs={{0,12},{4,8},{8,4},{12,0},{1,13},{5,9},{9,5},{13,1},{2,14},{6,10},... | collective-permute-start | bytes 393224 | tf_op jit(solution)/shard_map/ppermute | solution.py:279
  5.7 1.2 %copy-start.3 = (bf16[256,2048]{1,0:T(8,128)(2,1)S(1)}, bf16[256,2048]{1,0:T(8,128)(2,1)}, u32[]{:S(2)}) copy-start(bf16[256,2048]{1,0:T(8,128)(2,1)} %refs_0_.2) | copy-start | bytes 3145732
  7.0 1.2 %copy-start.4 = (bf16[256,2048]{1,0:T(8,128)(2,1)S(1)}, bf16[256,2048]{1,0:T(8,128)(2,1)}, u32[]{:S(2)}) copy-start(bf16[256,2048]{1,0:T(8,128)(2,1)} %refs_1_.1) | copy-start | bytes 3145732
  8.2 1.2 %copy-start.5 = (bf16[2048,256]{1,0:T(8,128)(2,1)S(1)}, bf16[2048,256]{1,0:T(8,128)(2,1)}, u32[]{:S(2)}) copy-start(bf16[2048,256]{1,0:T(8,128)(2,1)} %refs_2_.1) | copy-start | bytes 3145732
  9.4 1.2 %copy-start.6 = (bf16[2048,256]{1,0:T(8,128)(2,1)S(1)}, bf16[2048,256]{1,0:T(8,128)(2,1)}, u32[]{:S(2)}) copy-start(bf16[2048,256]{1,0:T(8,128)(2,1)} %refs_3_.1) | copy-start | bytes 3145732
  10.6 0.9 %copy-start.7 = (bf16[256,256]{1,0:T(8,128)(2,1)S(1)}, bf16[256,256]{1,0:T(8,128)(2,1)}, u32[]{:S(2)}) copy-start(bf16[256,256]{1,0:T(8,128)(2,1)} %refs_0_.3) | copy-start | bytes 393220
  11.6 2.7 %copy-start.10 = (s32[256,1]{0,1:T(1,128)S(1)}, s32[256,1]{0,1:T(1,128)}, u32[]{:S(2)}) copy-start(s32[256,1]{0,1:T(1,128)} %param.9) | copy-start | bytes 3076
  11.6 2.7 %copy-start.9 = (s32[256]{0:T(256)S(1)}, s32[256]{0:T(256)}, u32[]{:S(2)}) copy-start(s32[256]{0:T(256)} %param.10) | copy-start | bytes 3076
  11.6 2.7 %copy-start.11 = (s32[256]{0:T(256)S(1)}, s32[256]{0:T(256)}, u32[]{:S(2)}) copy-start(s32[256]{0:T(256)} %param.11) | copy-start | bytes 3076
  11.6 2.8 %copy-start.8 = (bf16[256,256]{1,0:T(8,128)(2,1)S(1)}, bf16[256,256]{1,0:T(8,128)(2,1)}, u32[]{:S(2)}) copy-start(bf16[256,256]{1,0:T(8,128)(2,1)} %refs_0_.3) | copy-start | bytes 393220
  13.3 1.0 %copy-start = (bf16[2048,256]{1,0:T(8,128)(2,1)}, bf16[2048,256]{1,0:T(8,128)(2,1)S(1)}, u32[]{:S(2)}) copy-start(bf16[2048,256]{1,0:T(8,128)(2,1)S(1)} %get-tuple-element.34.refs_2_.ss.second) | copy-start | bytes 3145732
  14.3 4.5 %collective-permute-start.11 = (s32[8,256]{1,0:T(8,128)S(1)}, s32[8,256]{1,0:T(8,128)S(1)}, u32[]{:S(2)}, u32[]{:S(2)}) collective-permute-start(s32[8,256]{1,0:T(8,128)S(1)} %pad.4), channel_id=1, source_target_pairs={{0,4},{4,0},{8,12},{12,8},{1,5},{5,1},{9,13},{13,9},{2,6},{6,2},{1... | collective-permute-start | bytes 24584 | tf_op jit(solution)/shard_map/ppermute | solution.py:279
  14.4 10.8 %collective-permute-start.2 = (bf16[256,256]{1,0:T(8,128)(2,1)S(1)}, bf16[256,256]{1,0:T(8,128)(2,1)S(1)}, u32[]{:S(2)}, u32[]{:S(2)}) collective-permute-start(bf16[256,256]{1,0:T(8,128)(2,1)S(1)} %copy-done.8), channel_id=1, source_target_pairs={{0,8},{4,12},{8,0},{12,4},{1,9},{5,13},{9,1},{13,5},{2,10},{6,14},... | collective-permute-start | bytes 393224 | tf_op jit(solution)/shard_map/ppermute | solution.py:279
  15.0 14.1 %collective-permute-start.14 = (bf16[256,256]{1,0:T(8,128)(2,1)S(1)}, bf16[256,256]{1,0:T(8,128)(2,1)S(1)}, u32[]{:S(2)}, u32[]{:S(2)}) collective-permute-start(bf16[256,256]{1,0:T(8,128)(2,1)S(1)} %copy-done.8), channel_id=1, source_target_pairs={{0,1},{1,0},{2,3},{3,2},{4,5},{5,4},{6,7},{7,6},{8,9},{9,8},{10,11... | collective-permute-start | bytes 393224 | tf_op jit(solution)/shard_map/ppermute | solution.py:282
  15.0 10.2 %collective-permute-start = (bf16[256,512]{1,0:T(8,128)(2,1)S(1)}, bf16[256,512]{1,0:T(8,128)(2,1)S(1)}, u32[]{:S(2)}, u32[]{:S(2)}) collective-permute-start(bf16[256,512]{1,0:T(8,128)(2,1)S(1)} %get-tuple-element.35.a_ref), channel_id=1, source_target_pairs={{0,2},{2,0},{1,3},{3,1},{4,6},{6,4},{5,7},{7,5},{8,10},{10,8},{9,1... | collective-permute-start | bytes 786440 | tf_op jit(solution)/shard_map/ppermute | solution.py:282
  18.8 10.2 %collective-permute-start.13 = (bf16[256,256]{1,0:T(8,128)(2,1)S(1)}, bf16[256,256]{1,0:T(8,128)(2,1)S(1)}, u32[]{:S(2)}, u32[]{:S(2)}) collective-permute-start(bf16[256,256]{1,0:T(8,128)(2,1)S(1)} %copy-done.8), channel_id=1, source_target_pairs={{0,4},{4,0},{8,12},{12,8},{1,5},{5,1},{9,13},{13,9},{2,6},{6,2},{1... | collective-permute-start | bytes 393224 | tf_op jit(solution)/shard_map/ppermute | solution.py:279
  18.8 5.5 %collective-permute-start.12 = (s32[16,256]{1,0:T(8,128)S(1)}, s32[16,256]{1,0:T(8,128)S(1)}, u32[]{:S(2)}, u32[]{:S(2)}) collective-permute-start(s32[16,256]{1,0:T(8,128)S(1)} %pad_add_fusion.1), channel_id=1, source_target_pairs={{0,8},{4,12},{8,0},{12,4},{1,9},{5,13},{9,1},{13,5},{2,10},{6,14},... | collective-permute-start | bytes 49160 | tf_op jit(solution)/shard_map/ppermute | solution.py:279
  20.8 1.2 %copy-start.1 = (bf16[2048,256]{1,0:T(8,128)(2,1)S(1)}, bf16[2048,256]{1,0:T(8,128)(2,1)}, u32[]{:S(2)}) copy-start(bf16[2048,256]{1,0:T(8,128)(2,1)} %copy-done) | copy-start | bytes 3145732
  24.3 9.3 %collective-permute-start.4 = (bf16[256,512]{1,0:T(8,128)(2,1)S(1)}, bf16[256,512]{1,0:T(8,128)(2,1)S(1)}, u32[]{:S(2)}, u32[]{:S(2)}) collective-permute-start(bf16[256,512]{1,0:T(8,128)(2,1)S(1)} %forward.5.a_ref), channel_id=1, source_target_pairs={{0,2},{2,0},{1,3},{3,1},{4,6},{6,4},{5,7},{7,5},{8,10},{10,8},{9,1... | collective-permute-start | bytes 786440 | tf_op jit(solution)/shard_map/ppermute | solution.py:282
  25.2 2.8 %collective-permute-start.18 = (s32[32,256]{1,0:T(8,128)S(1)}, s32[32,256]{1,0:T(8,128)S(1)}, u32[]{:S(2)}, u32[]{:S(2)}) collective-permute-start(s32[32,256]{1,0:T(8,128)S(1)} %pad_add_fusion.refs_8_.refs_10_), channel_id=1, source_target_pairs={{0,1},{1,0},{2,3},{3,2},{4,5},{5,4},{6,7},{7,6},{8,9},{9,8},{10,11... | collective-permute-start | bytes 98312 | tf_op jit(solution)/shard_map/ppermute | solution.py:282
  26.6 11.3 %collective-permute-start.5 = (bf16[256,512]{1,0:T(8,128)(2,1)S(1)}, bf16[256,512]{1,0:T(8,128)(2,1)S(1)}, u32[]{:S(2)}, u32[]{:S(2)}) collective-permute-start(bf16[256,512]{1,0:T(8,128)(2,1)S(1)} %forward.4.refs_2_), channel_id=1, source_target_pairs={{0,2},{2,0},{1,3},{3,1},{4,6},{6,4},{5,7},{7,5},{8,10},{10,8},{9,1... | collective-permute-start | bytes 786440 | tf_op jit(solution)/shard_map/ppermute | solution.py:282
  28.0 9.9 %collective-permute-start.1 = (bf16[256,512]{1,0:T(8,128)(2,1)S(1)}, bf16[256,512]{1,0:T(8,128)(2,1)S(1)}, u32[]{:S(2)}, u32[]{:S(2)}) collective-permute-start(bf16[256,512]{1,0:T(8,128)(2,1)S(1)} %both.2.refs_0_), channel_id=1, source_target_pairs={{0,4},{4,0},{8,12},{12,8},{1,5},{5,1},{9,13},{13,9},{2,6},{6,2},{1... | collective-permute-start | bytes 786440 | tf_op jit(solution)/shard_map/ppermute | solution.py:279
  29.0 4.7 %collective-permute-start.15 = (bf16[256,256]{1,0:T(8,128)(2,1)S(1)}, bf16[256,256]{1,0:T(8,128)(2,1)S(1)}, u32[]{:S(2)}, u32[]{:S(2)}) collective-permute-start(bf16[256,256]{1,0:T(8,128)(2,1)S(1)} %collective-permute-done.13.refs_1_), channel_id=1, source_target_pairs={{0,1},{1,0},{2,3},{3,2},{4,5},{5,4},{6,7},{7,6},{8,9},{9,8},{10,11... | collective-permute-start | bytes 393224 | tf_op jit(solution)/shard_map/ppermute | solution.py:282
  29.1 5.2 %collective-permute-start.16 = (bf16[256,256]{1,0:T(8,128)(2,1)S(1)}, bf16[256,256]{1,0:T(8,128)(2,1)S(1)}, u32[]{:S(2)}, u32[]{:S(2)}) collective-permute-start(bf16[256,256]{1,0:T(8,128)(2,1)S(1)} %collective-permute-done.2.x_ref.refs_2_), channel_id=1, source_target_pairs={{0,1},{1,0},{2,3},{3,2},{4,5},{5,4},{6,7},{7,6},{8,9},{9,8},{10,11... | collective-permute-start | bytes 393224 | tf_op jit(solution)/shard_map/ppermute | solution.py:282
  33.6 1.6 %collective-permute-start.17 = (bf16[256,256]{1,0:T(8,128)(2,1)}, bf16[256,256]{1,0:T(8,128)(2,1)S(1)}, u32[]{:S(2)}, u32[]{:S(2)}) collective-permute-start(bf16[256,256]{1,0:T(8,128)(2,1)} %collective-permute-done.3.x_ref.refs_3_), channel_id=1, source_target_pairs={{0,1},{1,0},{2,3},{3,2},{4,5},{5,4},{6,7},{7,6},{8,9},{9,8},{10,11... | collective-permute-start | bytes 393224 | tf_op jit(solution)/shard_map/ppermute | solution.py:282
  33.7 9.2 %collective-permute-start.8 = (bf16[256,512]{1,0:T(8,128)(2,1)S(1)}, bf16[256,512]{1,0:T(8,128)(2,1)S(1)}, u32[]{:S(2)}, u32[]{:S(2)}) collective-permute-start(bf16[256,512]{1,0:T(8,128)(2,1)S(1)} %forward.4.refs_2_), channel_id=1, source_target_pairs={{0,1},{1,0},{2,3},{3,2},{4,5},{5,4},{6,7},{7,6},{8,9},{9,8},{10,11... | collective-permute-start | bytes 786440 | tf_op jit(solution)/shard_map/ppermute | solution.py:282
  34.3 8.6 %collective-permute-start.6 = (bf16[256,512]{1,0:T(8,128)(2,1)S(1)}, bf16[256,512]{1,0:T(8,128)(2,1)S(1)}, u32[]{:S(2)}, u32[]{:S(2)}) collective-permute-start(bf16[256,512]{1,0:T(8,128)(2,1)S(1)} %both.2.refs_0_), channel_id=1, source_target_pairs={{0,1},{1,0},{2,3},{3,2},{4,5},{5,4},{6,7},{7,6},{8,9},{9,8},{10,11... | collective-permute-start | bytes 786440 | tf_op jit(solution)/shard_map/ppermute | solution.py:282
  35.2 7.7 %collective-permute-start.9 = (bf16[256,512]{1,0:T(8,128)(2,1)S(1)}, bf16[256,512]{1,0:T(8,128)(2,1)S(1)}, u32[]{:S(2)}, u32[]{:S(2)}) collective-permute-start(bf16[256,512]{1,0:T(8,128)(2,1)S(1)} %both.3.refs_3_), channel_id=1, source_target_pairs={{0,1},{1,0},{2,3},{3,2},{4,5},{5,4},{6,7},{7,6},{8,9},{9,8},{10,11... | collective-permute-start | bytes 786440 | tf_op jit(solution)/shard_map/ppermute | solution.py:282
  37.9 5.0 %collective-permute-start.10 = (bf16[256,512]{1,0:T(8,128)(2,1)S(1)}, bf16[256,512]{1,0:T(8,128)(2,1)S(1)}, u32[]{:S(2)}, u32[]{:S(2)}) collective-permute-start(bf16[256,512]{1,0:T(8,128)(2,1)S(1)} %collective-permute-done.5.refs_4_), channel_id=1, source_target_pairs={{0,1},{1,0},{2,3},{3,2},{4,5},{5,4},{6,7},{7,6},{8,9},{9,8},{10,11... | collective-permute-start | bytes 786440 | tf_op jit(solution)/shard_map/ppermute | solution.py:282
  37.9 5.0 %collective-permute-start.7 = (bf16[256,512]{1,0:T(8,128)(2,1)S(1)}, bf16[256,512]{1,0:T(8,128)(2,1)S(1)}, u32[]{:S(2)}, u32[]{:S(2)}) collective-permute-start(bf16[256,512]{1,0:T(8,128)(2,1)S(1)} %collective-permute-done.1.refs_1_), channel_id=1, source_target_pairs={{0,1},{1,0},{2,3},{3,2},{4,5},{5,4},{6,7},{7,6},{8,9},{9,8},{10,11... | collective-permute-start | bytes 786440 | tf_op jit(solution)/shard_map/ppermute | solution.py:282
  42.9 5.4 %copy-start.2 = (bf16[2048,256]{1,0:T(8,128)(2,1)S(1)}, bf16[2048,256]{1,0:T(8,128)(2,1)}, u32[]{:S(2)}) copy-start(bf16[2048,256]{1,0:T(8,128)(2,1)} %copy-done) | copy-start | bytes 3145732
  48.2 6.2 %collective-permute-start.19 = (bf16[1024,512]{1,0:T(8,128)(2,1)S(1)}, bf16[1024,512]{1,0:T(8,128)(2,1)S(1)}, u32[]{:S(2)}, u32[]{:S(2)}) collective-permute-start(bf16[1024,512]{1,0:T(8,128)(2,1)S(1)} %contrast.1.grads_ref), channel_id=1, source_target_pairs={{0,1},{1,0},{2,3},{3,2},{4,5},{5,4},{6,7},{7,6},{8,9},{9,8},{10,11... | collective-permute-start | bytes 3145736 | tf_op jit(solution)/shard_map/ppermute | solution.py:282
  57.9 5.9 %collective-permute-start.20 = (f32[256,1024]{1,0:T(8,128)S(1)}, f32[256,1024]{1,0:T(8,128)S(1)}, u32[]{:S(2)}, u32[]{:S(2)}) collective-permute-start(f32[256,1024]{1,0:T(8,128)S(1)} %get-tuple-element.47.refs_0_), channel_id=1, source_target_pairs={{0,1},{1,0},{2,3},{3,2},{4,5},{5,4},{6,7},{7,6},{8,9},{9,8},{10,11... | collective-permute-start | bytes 3145736 | tf_op jit(solution)/shard_map/ppermute | solution.py:282
  58.5 5.4 %collective-permute-start.21 = (f32[1024,256]{1,0:T(8,128)S(1)}, f32[1024,256]{1,0:T(8,128)S(1)}, u32[]{:S(2)}, u32[]{:S(2)}) collective-permute-start(f32[1024,256]{1,0:T(8,128)S(1)} %get-tuple-element.48.refs_1_), channel_id=1, source_target_pairs={{0,1},{1,0},{2,3},{3,2},{4,5},{5,4},{6,7},{7,6},{8,9},{9,8},{10,11... | collective-permute-start | bytes 3145736 | tf_op jit(solution)/shard_map/ppermute | solution.py:282
  63.3 3.2 %collective-permute-start.22 = (f32[256,1024]{1,0:T(8,128)S(1)}, f32[256,1024]{1,0:T(8,128)S(1)}, u32[]{:S(2)}, u32[]{:S(2)}) collective-permute-start(f32[256,1024]{1,0:T(8,128)S(1)} %get-tuple-element.52.refs_2_), channel_id=1, source_target_pairs={{0,1},{1,0},{2,3},{3,2},{4,5},{5,4},{6,7},{7,6},{8,9},{9,8},{10,11... | collective-permute-start | bytes 3145736 | tf_op jit(solution)/shard_map/ppermute | solution.py:282
  63.8 3.8 %collective-permute-start.23 = (f32[1024,256]{1,0:T(8,128)S(1)}, f32[1024,256]{1,0:T(8,128)S(1)}, u32[]{:S(2)}, u32[]{:S(2)}) collective-permute-start(f32[1024,256]{1,0:T(8,128)S(1)} %get-tuple-element.53.refs_3_), channel_id=1, source_target_pairs={{0,1},{1,0},{2,3},{3,2},{4,5},{5,4},{6,7},{7,6},{8,9},{9,8},{10,11... | collective-permute-start | bytes 3145736 | tf_op jit(solution)/shard_map/ppermute | solution.py:282

commit v5 on v4

--- a/solution.py
+++ b/solution.py
@@ -44,44 +44,47 @@
     )(*args)
 
 
-def encode(x_ref, weights, out_ref, active):
-    emb = weights[2].shape[1]
+def forward_kernel(x_ref, *refs):
+    weights, out_ref, held, active, sems = refs[:4], refs[4], refs[5:9], refs[9], refs[10]
+    hid, emb = weights[2].shape
+    part = hid // 2
+
+    def piece(ref, i, p):
+        at = pl.ds(p * part, part)
+        return ref.at[:, at] if i < 2 else ref.at[at, :]
+
+    copies = {}
     for k in range(2):
-        first, second = weights[k], weights[2 + k]
-        for c in range(0, active.shape[1], 512):
-            hidden = dot(x_ref[...], first[:, c : c + 512])
-            active[:, c : c + 512] = (hidden * sigmoid(hidden)).astype(BF)
-        out_ref[:, k * emb : (k + 1) * emb] = dot(active[...], second[...]).astype(BF)
-
-
-def first_kernel(x_ref, *refs):
-    weights, out_ref, held, active, sems = refs[:4], refs[4], refs[5:9], refs[9], refs[10]
-    copies = [pltpu.make_async_copy(w, h, sems.at[i]) for i, (w, h) in enumerate(zip(weights, held))]
-    for i in (0, 2, 1, 3):
-        copies[i].start()
-    for c in copies:
-        c.wait()
-    encode(x_ref, held, out_ref, active)
-
-
-def forward_kernel(x_ref, *refs):
-    encode(x_ref, refs[:4], refs[4], refs[5])
-
-
-def forward(x, weights, load=False):
+        for p in range(2):
+            for i in (k, 2 + k):
+                copies[i, p] = pltpu.make_async_copy(
+                    piece(weights[i], i, p), piece(held[i], i, p), sems.at[2 * i + p]
+                )
+                copies[i, p].start()
+    for k in range(2):
+        for p in range(2):
+            copies[k, p].wait()
+            for c in range(p * part, (p + 1) * part, 512):
+                hidden = dot(x_ref[...], held[k][:, c : c + 512])
+                active[:, c : c + 512] = (hidden * sigmoid(hidden)).astype(BF)
+        for p in range(2):
+            copies[2 + k, p].wait()
+        out_ref[:, k * emb : (k + 1) * emb] = dot(active[...], held[2 + k][...]).astype(BF)
+
+
+def forward(x, weights):
     rows, width = x.shape
     hid, emb = weights[2].shape
-    outs = [((rows, 2 * emb), BF)] + [(w.shape, w.dtype) for w in weights] * load
-    got = kernel(
-        first_kernel if load else forward_kernel,
+    return kernel(
+        forward_kernel,
         "forward",
-        outs,
+        [((rows, 2 * emb), BF)],
         (x, *weights),
-        [pltpu.VMEM((rows, hid), BF)] + [pltpu.SemaphoreType.DMA((4,))] * load,
-        flops=8 * rows * width * hid,
-        hbm=(1, 2, 3, 4) if load else (),
-    )
-    return (got[0], got[1:]) if load else got[0]
+        [pltpu.VMEM(w.shape, w.dtype) for w in weights]
+        + [pltpu.VMEM((rows, hid), BF), pltpu.SemaphoreType.DMA((8,))],
+        limit=56,
+        hbm=(1, 2, 3, 4),
+    )[0]
 
 
 def add_kernel(a_ref, b_ref, out_ref):
@@ -285,7 +288,8 @@
         return lax.optimization_barrier((x, *first))[0]
 
     got = {0: states, 3: across(states, 3), 2: across(states, 2)}
-    part0, weights = forward(states, (state_first, goal_first, state_second, goal_second), load=True)
+    weights = (state_first, goal_first, state_second, goal_second)
+    part0 = forward(states, weights)
     there0 = swap(part0, "rep")
     got[1] = across(after(states, part0), 1)
     part3 = forward(got[3], weights)
@@ -314,7 +318,6 @@
         (*(got[k] for k in range(n_blk)), *(swap(got[k], "sub") for k in range(n_blk)), meta, meta_other),
         [pltpu.VMEM((rows_all, width), BF), pltpu.VMEM((rows_all // 2, rows_all), BF)],
         pos=pos,
-        flops=2 * rows_all * rows_all * width,
     )
     (grads_mine,) = kernel(
         functools.partial(contrast_kernel, n_blk, n_rep, slab, 4.0 / math.sqrt(emb)),

time: 70 us -> 79.9 us (1.14)
  Pallas kernels: 33.7 us -> 45.2 us
  starting transfers between devices: 15.8 us -> 22.1 us
  local copies, waits for them, and re-layouts: 8.02 us -> 3.21 us
  waiting for transfers between devices: 10.7 us -> 7.9 us
    pallas_call x12, Pallas kernels: 33.7 us -> 45.2 us  [kernel(): pl.pallas_call(body, in_specs=specs, out_specs=[HBM if i in hbm_out else...]
    ppermute x6, starting transfers between devices: 8.83 us -> 15.2 us  [across(): return lax.ppermute(x, 'blk', [(i, i ^ k) for i in range(n_blk)])]
    unnamed x24 -> x30, local copies, waits for them, and re-layouts: 8.01 us -> 3.2 us
    ppermute x6, waiting for transfers between devices: 2.15 us -> 0.15 us  [across(): return lax.ppermute(x, 'blk', [(i, i ^ k) for i in range(n_blk)])]
    ppermute x18, waiting for transfers between devices: 8.59 us -> 7.75 us  [swap(): return lax.ppermute(x, axis, [(0, 1), (1, 0)])]
  transfers between devices with their start and end apart: 24 -> 24, of which waited for: 5 -> 5; matrix products, arithmetic and copies ran while one was open for 0% -> 0% of each run, Pallas kernels for 33% -> 36%
where the time goes in v5:
time: 79.9 us; the launch traced here: 79.6 us
  Pallas kernels  45.2 us (57%)
  starting transfers between devices  22.1 us (28%)
  waiting for transfers between devices  7.9 us (10%)
  local copies, waits for them, and re-layouts  3.21 us (4%)
  between operations  1.1 us (1%)
    pallas_call x12, Pallas kernels, kernel(): pl.pallas_call(body, in_specs=specs, out_specs=[HBM if i in hbm_out else...  45.2 us
    ppermute x6, starting transfers between devices, across(): return lax.ppermute(x, 'blk', [(i, i ^ k) for i in range(n_blk)])  15.2 us
    ppermute x18, waiting for transfers between devices, swap(): return lax.ppermute(x, axis, [(0, 1), (1, 0)])  7.75 us
    ppermute x18, starting transfers between devices, swap(): return lax.ppermute(x, axis, [(0, 1), (1, 0)])  6.86 us
    unnamed x30, local copies, waits for them, and re-layouts  3.2 us
  transfers between devices with their start and end apart: 24, of which 5 were waited for; matrix products, arithmetic and copies ran while one was open for 0% of the time, Pallas kernels for 36%

profile of v5, /device:TPU:0, one launch (start us, length us, event | category | flops | bytes accessed | tf_op | source)
XLA Modules:
  0.0 79.6 jit_solution(4998177627326309569)
XLA Ops:
  0.7 5.9 %forward.3.a_ref = bf16[256,512]{1,0:T(8,128)(2,1)} custom-call(bf16[256,256]{1,0:T(8,128)(2,1)} %refs_0_.7, bf16[256,2048]{1,0:T(8,128)(2,1)} %first.2, bf16[256,2048]{1,0:T(8,128)(2,1)} %first.3, bf16[2048,256]{1,0:T(8,128)(2,1)} %second.2, bf16[2048,256]{1,0:T(8,128)(2,1)} %second.3), custom_call_target="tpu_custom_call" | custom-call | tf_op jit(solution)/shard_map/forward/pallas_call | solution.py:34
  6.7 3.1 %collective-permute-start.11 = (s32[8,256]{1,0:T(8,128)S(1)}, s32[8,256]{1,0:T(8,128)S(1)}, u32[]{:S(2)}, u32[]{:S(2)}) collective-permute-start(s32[8,256]{1,0:T(8,128)S(1)} %pad.4), channel_id=1, source_target_pairs={{0,4},{4,0},{8,12},{12,8},{1,5},{5,1},{9,13},{13,9},{2,6},{6,2},{1... | collective-permute-start | bytes 24584 | tf_op jit(solution)/shard_map/ppermute | solution.py:282
  9.8 2.5 %collective-permute-start.3 = (bf16[256,256]{1,0:T(8,128)(2,1)S(1)}, bf16[256,256]{1,0:T(8,128)(2,1)S(1)}, u32[]{:S(2)}, u32[]{:S(2)}) collective-permute-start(bf16[256,256]{1,0:T(8,128)(2,1)S(1)} %copy-done.7), channel_id=1, source_target_pairs={{0,12},{4,8},{8,4},{12,0},{1,13},{5,9},{9,5},{13,1},{2,14},{6,10},... | collective-permute-start | bytes 393224 | tf_op jit(solution)/shard_map/ppermute | solution.py:282
  12.3 1.5 %collective-permute-start = (bf16[256,512]{1,0:T(8,128)(2,1)}, bf16[256,512]{1,0:T(8,128)(2,1)S(1)}, u32[]{:S(2)}, u32[]{:S(2)}) collective-permute-start(bf16[256,512]{1,0:T(8,128)(2,1)} %forward.3.a_ref), channel_id=1, source_target_pairs={{0,2},{2,0},{1,3},{3,1},{4,6},{6,4},{5,7},{7,5},{8,10},{10,8},{9,1... | collective-permute-start | bytes 786440 | tf_op jit(solution)/shard_map/ppermute | solution.py:285
  13.7 0.0 collective-permute-done.11
  13.8 0.8 collective-permute-start.12
  14.5 2.2 %collective-permute-start.2 = (bf16[256,256]{1,0:T(8,128)(2,1)S(1)}, bf16[256,256]{1,0:T(8,128)(2,1)S(1)}, u32[]{:S(2)}, u32[]{:S(2)}) collective-permute-start(bf16[256,256]{1,0:T(8,128)(2,1)S(1)} %copy-done.7), channel_id=1, source_target_pairs={{0,8},{4,12},{8,0},{12,4},{1,9},{5,13},{9,1},{13,5},{2,10},{6,14},... | collective-permute-start | bytes 393224 | tf_op jit(solution)/shard_map/ppermute | solution.py:282
  16.7 0.1 collective-permute-done.3.x_ref.refs_3_
  16.8 0.7 copy-done.8
  17.5 5.8 %forward.5.a_ref = bf16[256,512]{1,0:T(8,128)(2,1)} custom-call(bf16[256,256]{1,0:T(8,128)(2,1)} %copy-done.8, bf16[256,2048]{1,0:T(8,128)(2,1)} %first.2, bf16[256,2048]{1,0:T(8,128)(2,1)} %first.3, bf16[2048,256]{1,0:T(8,128)(2,1)} %second.2, bf16[2048,256]{1,0:T(8,128)(2,1)} %second.3), custom_call_target="tpu_custom_call" | custom-call | tf_op jit(solution)/shard_map/forward/pallas_call | solution.py:34
  23.3 1.6 %collective-permute-start.4 = (bf16[256,512]{1,0:T(8,128)(2,1)}, bf16[256,512]{1,0:T(8,128)(2,1)S(1)}, u32[]{:S(2)}, u32[]{:S(2)}) collective-permute-start(bf16[256,512]{1,0:T(8,128)(2,1)} %forward.5.a_ref), channel_id=1, source_target_pairs={{0,2},{2,0},{1,3},{3,1},{4,6},{6,4},{5,7},{7,5},{8,10},{10,8},{9,1... | collective-permute-start | bytes 786440 | tf_op jit(solution)/shard_map/ppermute | solution.py:285
  24.9 0.0 collective-permute-done.12
  24.9 0.0 collective-permute-start.18
  24.9 6.4 %collective-permute-start.13 = (bf16[256,256]{1,0:T(8,128)(2,1)S(1)}, bf16[256,256]{1,0:T(8,128)(2,1)S(1)}, u32[]{:S(2)}, u32[]{:S(2)}) collective-permute-start(bf16[256,256]{1,0:T(8,128)(2,1)S(1)} %copy-done.7), channel_id=1, source_target_pairs={{0,4},{4,0},{8,12},{12,8},{1,5},{5,1},{9,13},{13,9},{2,6},{6,2},{1... | collective-permute-start | bytes 393224 | tf_op jit(solution)/shard_map/ppermute | solution.py:282
  31.3 0.0 collective-permute-done.b_ref
  31.3 0.2 collective-permute-start.14
  31.5 0.1 both.2.refs_0_
  31.5 0.0 copy-start.9
  31.6 0.0 copy-start.6
  31.6 0.0 collective-permute-done.2.x_ref.refs_2_
  31.6 0.0 copy-start.10
  31.6 0.6 copy-done.10
  32.2 5.8 %forward.4.refs_2_ = bf16[256,512]{1,0:T(8,128)(2,1)} custom-call(bf16[256,256]{1,0:T(8,128)(2,1)} %copy-done.10, bf16[256,2048]{1,0:T(8,128)(2,1)} %first.2, bf16[256,2048]{1,0:T(8,128)(2,1)} %first.3, bf16[2048,256]{1,0:T(8,128)(2,1)} %second.2, bf16[2048,256]{1,0:T(8,128)(2,1)} %second.3), custom_call_target="tpu_custom_call" | custom-call | tf_op jit(solution)/shard_map/forward/pallas_call | solution.py:34
  38.1 0.6 collective-permute-start.5
  38.7 0.0 collective-permute-done.18.refs_9_
  38.7 0.3 collective-permute-start.1
  39.0 0.0 collective-permute-done.13.refs_1_
  39.0 0.0 collective-permute-start.15
  39.0 0.0 collective-permute-done.14.refs_4_
  39.0 0.5 collective-permute-start.16
  39.5 0.0 collective-permute-done.4.b_ref
  39.5 0.1 collective-permute-start.17
  39.6 0.1 both.3.refs_3_
  39.6 0.7 collective-permute-done.15.refs_5_
  40.3 0.1 collective-permute-start.8
  40.5 0.2 collective-permute-done.16.refs_6_
  40.7 0.3 collective-permute-start.6
  41.0 0.0 collective-permute-done.17.refs_7_
  41.0 0.2 collective-permute-start.9
  41.2 5.7 %collective-permute-done.5.refs_4_ = bf16[256,512]{1,0:T(8,128)(2,1)S(1)} collective-permute-done((bf16[256,512]{1,0:T(8,128)(2,1)}, bf16[256,512]{1,0:T(8,128)(2,1)S(1)}, u32[]{:S(2)}, u32[]{:S(2)}) %collective-permute-start.5) | collective-permute-done | bytes 262176 | tf_op jit(solution)/shard_map/ppermute | solution.py:285
  46.9 0.0 collective-permute-start.10
  46.9 0.0 collective-permute-done.1.refs_1_
  47.0 0.5 collective-permute-start.7
  47.4 0.1 pad_add_fusion.3.pos_ref
  47.5 0.9 %copy-done.11 = bf16[256,256]{1,0:T(8,128)(2,1)S(1)} copy-done((bf16[256,256]{1,0:T(8,128)(2,1)S(1)}, bf16[256,256]{1,0:T(8,128)(2,1)}, u32[]{:S(2)}) %copy-start.11) | copy-done | bytes 131096
  48.4 4.0 %arrange.1 = (bf16[1024,256]{1,0:T(8,128)(2,1)S(1)}, bf16[1024,256]{1,0:T(8,128)(2,1)S(1)}, bf16[1024,256]{1,0:T(8,128)(2,1)S(1)}, bf16[1024,256]{1,0:T(8,128)(2,1)S(1)}, bf16[1024,2048]{1,0:T(8,128)(2,1)S(1)}) custom-call(s32[2]{0:T(128)S(1)} %pad_add_fusion.3.pos_ref, bf16[256,256]{1,0:T(8,128)(2,1)S(1)} %copy-done.7, ...), custom_call_target="tpu_custom_call" | custom-call | tf_op jit(solution)/shard_map/arrange/pallas_call | solution.py:34
  52.4 0.0 collective-permute-done.8.refs_7_
  52.4 0.0 collective-permute-done.9.refs_8_
  52.5 0.0 collective-permute-done.10.refs_9_
  52.5 0.0 copy-start.4
  52.5 0.9 %copy-done.4 = bf16[256,512]{1,0:T(8,128)(2,1)S(1)} copy-done((bf16[256,512]{1,0:T(8,128)(2,1)S(1)}, bf16[256,512]{1,0:T(8,128)(2,1)}, u32[]{:S(2)}) %copy-start.4) | copy-done | bytes 262168
  53.4 5.1 %contrast.1.grads_ref = bf16[1024,512]{1,0:T(8,128)(2,1)S(1)} custom-call(s32[2]{0:T(128)S(1)} %pad_add_fusion.3.pos_ref, bf16[256,512]{1,0:T(8,128)(2,1)S(1)} %both.2.refs_0_, bf16[256,512]{1,0:T(8,128)(2,1)S(1)} %collective-permute-done.1.refs_1_, bf16[256,512]{1,0:T(8,128)(2,1)S(1)} %copy-done.4, bf16[256,512]{1,0:T(8,128)(2,1)S(1)} %both.3.refs_3_, ...), custom_call_target="tpu_custom_call" | custom-call | flops 1879048192 | tf_op jit(solution)/shard_map/contrast/pallas_call | solution.py:34
  58.5 0.1 collective-permute-start.19
  58.7 5.9 %mine.1 = (f32[1024,256]{1,0:T(8,128)S(1)}, f32[1024,256]{1,0:T(8,128)S(1)}, f32[1024,256]{1,0:T(8,128)S(1)}, f32[1024,256]{1,0:T(8,128)S(1)}) custom-call(s32[2]{0:T(128)S(1)} %pad_add_fusion.3.pos_ref, bf16[256,2048]{1,0:T(8,128)(2,1)S(1)} %copy-done, bf16[256,2048]{1,0:T(8,128)(2,1)S(1)} %copy-done.2, bf16[2048,256]{1,0:T(8,128)(2,1)S(1)} %copy-done.1, ...), custom_call_target="tpu_custom_call" | custom-call | flops 4294967296 | tf_op jit(solution)/shard_map/mine/pallas_call | solution.py:34
  64.6 0.0 collective-permute-done.19.grads_ref
  64.6 3.4 %other_state.1 = (f32[256,1024]{1,0:T(8,128)S(1)}, f32[1024,256]{1,0:T(8,128)S(1)}) custom-call(s32[2]{0:T(128)S(1)} %pad_add_fusion.3.pos_ref, bf16[256,2048]{1,0:T(8,128)(2,1)S(1)} %copy-done, bf16[2048,256]{1,0:T(8,128)(2,1)S(1)} %copy-done.1, bf16[1024,512]{1,0:T(8,128)(2,1)S(1)} %collective-permute-done.19.grads_ref, ...), custom_call_target="tpu_custom_call" | custom-call | flops 2147483648 | tf_op jit(solution)/shard_map/other_state/pallas_call | solution.py:34
  68.0 0.6 collective-permute-start.20
  68.6 0.1 collective-permute-start.21
  68.7 4.6 %other_goal.1 = (f32[256,1024]{1,0:T(8,128)S(1)}, f32[1024,256]{1,0:T(8,128)S(1)}, f32[256,2048]{1,0:T(8,128)}, f32[2048,256]{1,0:T(8,128)}) custom-call(s32[2]{0:T(128)S(1)} %pad_add_fusion.3.pos_ref, bf16[256,2048]{1,0:T(8,128)(2,1)S(1)} %copy-done.2, bf16[2048,256]{1,0:T(8,128)(2,1)S(1)} %copy-done.3, ...), custom_call_target="tpu_custom_call" | custom-call | flops 2147483648 | tf_op jit(solution)/shard_map/other_goal/pallas_call | solution.py:34
  73.3 0.5 collective-permute-start.22
  73.8 0.1 collective-permute-start.23
  73.9 2.6 %finish.2 = (f32[256,2048]{1,0:T(8,128)}, f32[2048,256]{1,0:T(8,128)}, f32[256,2048]{1,0:T(8,128)}, f32[2048,256]{1,0:T(8,128)}) custom-call(s32[2]{0:T(128)S(1)} %pad_add_fusion.3.pos_ref, f32[256,1024]{1,0:T(8,128)S(1)} %collective-permute-done.20.refs_0_, ...), custom_call_target="tpu_custom_call", output_to_operand_aliasing={{0}: (5, {}), {1}: (6, {})} | custom-call | tf_op jit(solution)/shard_map/finish/pallas_call | solution.py:34
  76.5 1.1 %collective-permute-done.23.refs_1_ = f32[1024,256]{1,0:T(8,128)S(1)} collective-permute-done((f32[1024,256]{1,0:T(8,128)S(1)}, f32[1024,256]{1,0:T(8,128)S(1)}, u32[]{:S(2)}, u32[]{:S(2)}) %collective-permute-start.23) | collective-permute-done | bytes 1048608 | tf_op jit(solution)/shard_map/ppermute | solution.py:285
  77.6 1.9 %finish.3 = (f32[256,2048]{1,0:T(8,128)}, f32[2048,256]{1,0:T(8,128)}) custom-call(s32[2]{0:T(128)S(1)} %pad_add_fusion.3.pos_ref, f32[256,1024]{1,0:T(8,128)S(1)} %collective-permute-done.22.refs_0_, f32[1024,256]{1,0:T(8,128)S(1)} %collective-permute-done.23.refs_1_, ...), custom_call_target="tpu_custom_call", output_to_operand_aliasing={{0}: (3, {}), {1}: (4, {})} | custom-call | tf_op jit(solution)/shard_map/finish/pallas_call | solution.py:34
  (33 shorter events, 0.1 us)
Async XLA Ops:
  0.6 6.0 %copy-start.13 = (s32[256,1]{0,1:T(1,128)S(1)}, s32[256,1]{0,1:T(1,128)}, u32[]{:S(2)}) copy-start(s32[256,1]{0,1:T(1,128)} %param.9) | copy-start | bytes 3076
  0.6 6.0 %copy-start.12 = (s32[256]{0:T(256)S(1)}, s32[256]{0:T(256)}, u32[]{:S(2)}) copy-start(s32[256]{0:T(256)} %param.10) | copy-start | bytes 3076
  0.7 6.0 %copy-start.14 = (s32[256]{0:T(256)S(1)}, s32[256]{0:T(256)}, u32[]{:S(2)}) copy-start(s32[256]{0:T(256)} %param.11) | copy-start | bytes 3076
  0.7 9.1 %copy-start.7 = (bf16[256,256]{1,0:T(8,128)(2,1)S(1)}, bf16[256,256]{1,0:T(8,128)(2,1)}, u32[]{:S(2)}) copy-start(bf16[256,256]{1,0:T(8,128)(2,1)} %refs_0_.7) | copy-start | bytes 393220
  6.7 7.1 %collective-permute-start.11 = (s32[8,256]{1,0:T(8,128)S(1)}, s32[8,256]{1,0:T(8,128)S(1)}, u32[]{:S(2)}, u32[]{:S(2)}) collective-permute-start(s32[8,256]{1,0:T(8,128)S(1)} %pad.4), channel_id=1, source_target_pairs={{0,4},{4,0},{8,12},{12,8},{1,5},{5,1},{9,13},{13,9},{2,6},{6,2},{1... | collective-permute-start | bytes 24584 | tf_op jit(solution)/shard_map/ppermute | solution.py:282
  9.8 7.1 %collective-permute-start.3 = (bf16[256,256]{1,0:T(8,128)(2,1)S(1)}, bf16[256,256]{1,0:T(8,128)(2,1)S(1)}, u32[]{:S(2)}, u32[]{:S(2)}) collective-permute-start(bf16[256,256]{1,0:T(8,128)(2,1)S(1)} %copy-done.7), channel_id=1, source_target_pairs={{0,12},{4,8},{8,4},{12,0},{1,13},{5,9},{9,5},{13,1},{2,14},{6,10},... | collective-permute-start | bytes 393224 | tf_op jit(solution)/shard_map/ppermute | solution.py:282
  12.3 19.1 %collective-permute-start = (bf16[256,512]{1,0:T(8,128)(2,1)}, bf16[256,512]{1,0:T(8,128)(2,1)S(1)}, u32[]{:S(2)}, u32[]{:S(2)}) collective-permute-start(bf16[256,512]{1,0:T(8,128)(2,1)} %forward.3.a_ref), channel_id=1, source_target_pairs={{0,2},{2,0},{1,3},{3,1},{4,6},{6,4},{5,7},{7,5},{8,10},{10,8},{9,1... | collective-permute-start | bytes 786440 | tf_op jit(solution)/shard_map/ppermute | solution.py:285
  13.8 17.7 %copy-start.5 = (bf16[256,512]{1,0:T(8,128)(2,1)S(1)}, bf16[256,512]{1,0:T(8,128)(2,1)}, u32[]{:S(2)}) copy-start(bf16[256,512]{1,0:T(8,128)(2,1)} %forward.3.a_ref) | copy-start | bytes 786436
  13.8 11.2 %collective-permute-start.12 = (s32[16,256]{1,0:T(8,128)S(1)}, s32[16,256]{1,0:T(8,128)S(1)}, u32[]{:S(2)}, u32[]{:S(2)}) collective-permute-start(s32[16,256]{1,0:T(8,128)S(1)} %pad_add_fusion.1), channel_id=1, source_target_pairs={{0,8},{4,12},{8,0},{12,4},{1,9},{5,13},{9,1},{13,5},{2,10},{6,14},... | collective-permute-start | bytes 49160 | tf_op jit(solution)/shard_map/ppermute | solution.py:282
  14.5 17.0 %collective-permute-start.2 = (bf16[256,256]{1,0:T(8,128)(2,1)S(1)}, bf16[256,256]{1,0:T(8,128)(2,1)S(1)}, u32[]{:S(2)}, u32[]{:S(2)}) collective-permute-start(bf16[256,256]{1,0:T(8,128)(2,1)S(1)} %copy-done.7), channel_id=1, source_target_pairs={{0,8},{4,12},{8,0},{12,4},{1,9},{5,13},{9,1},{13,5},{2,10},{6,14},... | collective-permute-start | bytes 393224 | tf_op jit(solution)/shard_map/ppermute | solution.py:282
  16.8 0.7 copy-start.8
  23.3 16.2 %collective-permute-start.4 = (bf16[256,512]{1,0:T(8,128)(2,1)}, bf16[256,512]{1,0:T(8,128)(2,1)S(1)}, u32[]{:S(2)}, u32[]{:S(2)}) collective-permute-start(bf16[256,512]{1,0:T(8,128)(2,1)} %forward.5.a_ref), channel_id=1, source_target_pairs={{0,2},{2,0},{1,3},{3,1},{4,6},{6,4},{5,7},{7,5},{8,10},{10,8},{9,1... | collective-permute-start | bytes 786440 | tf_op jit(solution)/shard_map/ppermute | solution.py:285
  24.9 13.8 %collective-permute-start.18 = (s32[32,256]{1,0:T(8,128)S(1)}, s32[32,256]{1,0:T(8,128)S(1)}, u32[]{:S(2)}, u32[]{:S(2)}) collective-permute-start(s32[32,256]{1,0:T(8,128)S(1)} %pad_add_fusion.refs_8_.refs_10_), channel_id=1, source_target_pairs={{0,1},{1,0},{2,3},{3,2},{4,5},{5,4},{6,7},{7,6},{8,9},{9,8},{10,11... | collective-permute-start | bytes 98312 | tf_op jit(solution)/shard_map/ppermute | solution.py:285
  24.9 14.0 %collective-permute-start.13 = (bf16[256,256]{1,0:T(8,128)(2,1)S(1)}, bf16[256,256]{1,0:T(8,128)(2,1)S(1)}, u32[]{:S(2)}, u32[]{:S(2)}) collective-permute-start(bf16[256,256]{1,0:T(8,128)(2,1)S(1)} %copy-done.7), channel_id=1, source_target_pairs={{0,4},{4,0},{8,12},{12,8},{1,5},{5,1},{9,13},{13,9},{2,6},{6,2},{1... | collective-permute-start | bytes 393224 | tf_op jit(solution)/shard_map/ppermute | solution.py:282
  31.3 7.7 %collective-permute-start.14 = (bf16[256,256]{1,0:T(8,128)(2,1)S(1)}, bf16[256,256]{1,0:T(8,128)(2,1)S(1)}, u32[]{:S(2)}, u32[]{:S(2)}) collective-permute-start(bf16[256,256]{1,0:T(8,128)(2,1)S(1)} %copy-done.7), channel_id=1, source_target_pairs={{0,1},{1,0},{2,3},{3,2},{4,5},{5,4},{6,7},{7,6},{8,9},{9,8},{10,11... | collective-permute-start | bytes 393224 | tf_op jit(solution)/shard_map/ppermute | solution.py:285
  31.5 7.9 %copy-start.9 = (bf16[256,256]{1,0:T(8,128)(2,1)S(1)}, bf16[256,256]{1,0:T(8,128)(2,1)}, u32[]{:S(2)}) copy-start(bf16[256,256]{1,0:T(8,128)(2,1)} %copy-done.8) | copy-start | bytes 393220
  31.6 8.0 %copy-start.6 = (bf16[256,512]{1,0:T(8,128)(2,1)S(1)}, bf16[256,512]{1,0:T(8,128)(2,1)}, u32[]{:S(2)}) copy-start(bf16[256,512]{1,0:T(8,128)(2,1)} %forward.5.a_ref) | copy-start | bytes 786436
  31.6 0.7 copy-start.10
  38.1 8.8 %collective-permute-start.5 = (bf16[256,512]{1,0:T(8,128)(2,1)}, bf16[256,512]{1,0:T(8,128)(2,1)S(1)}, u32[]{:S(2)}, u32[]{:S(2)}) collective-permute-start(bf16[256,512]{1,0:T(8,128)(2,1)} %forward.4.refs_2_), channel_id=1, source_target_pairs={{0,2},{2,0},{1,3},{3,1},{4,6},{6,4},{5,7},{7,5},{8,10},{10,8},{9,1... | collective-permute-start | bytes 786440 | tf_op jit(solution)/shard_map/ppermute | solution.py:285
  38.7 8.3 %collective-permute-start.1 = (bf16[256,512]{1,0:T(8,128)(2,1)S(1)}, bf16[256,512]{1,0:T(8,128)(2,1)S(1)}, u32[]{:S(2)}, u32[]{:S(2)}) collective-permute-start(bf16[256,512]{1,0:T(8,128)(2,1)S(1)} %both.2.refs_0_), channel_id=1, source_target_pairs={{0,4},{4,0},{8,12},{12,8},{1,5},{5,1},{9,13},{13,9},{2,6},{6,2},{1... | collective-permute-start | bytes 786440 | tf_op jit(solution)/shard_map/ppermute | solution.py:282
  39.0 1.3 %collective-permute-start.15 = (bf16[256,256]{1,0:T(8,128)(2,1)S(1)}, bf16[256,256]{1,0:T(8,128)(2,1)S(1)}, u32[]{:S(2)}, u32[]{:S(2)}) collective-permute-start(bf16[256,256]{1,0:T(8,128)(2,1)S(1)} %collective-permute-done.13.refs_1_), channel_id=1, source_target_pairs={{0,1},{1,0},{2,3},{3,2},{4,5},{5,4},{6,7},{7,6},{8,9},{9,8},{10,11... | collective-permute-start | bytes 393224 | tf_op jit(solution)/shard_map/ppermute | solution.py:285
  39.0 1.7 %collective-permute-start.16 = (bf16[256,256]{1,0:T(8,128)(2,1)}, bf16[256,256]{1,0:T(8,128)(2,1)S(1)}, u32[]{:S(2)}, u32[]{:S(2)}) collective-permute-start(bf16[256,256]{1,0:T(8,128)(2,1)} %copy-done.10), channel_id=1, source_target_pairs={{0,1},{1,0},{2,3},{3,2},{4,5},{5,4},{6,7},{7,6},{8,9},{9,8},{10,11... | collective-permute-start | bytes 393224 | tf_op jit(solution)/shard_map/ppermute | solution.py:285
  39.5 1.6 %collective-permute-start.17 = (bf16[256,256]{1,0:T(8,128)(2,1)S(1)}, bf16[256,256]{1,0:T(8,128)(2,1)S(1)}, u32[]{:S(2)}, u32[]{:S(2)}) collective-permute-start(bf16[256,256]{1,0:T(8,128)(2,1)S(1)} %copy-done.9), channel_id=1, source_target_pairs={{0,1},{1,0},{2,3},{3,2},{4,5},{5,4},{6,7},{7,6},{8,9},{9,8},{10,11... | collective-permute-start | bytes 393224 | tf_op jit(solution)/shard_map/ppermute | solution.py:285
  40.3 12.1 %collective-permute-start.8 = (bf16[256,512]{1,0:T(8,128)(2,1)}, bf16[256,512]{1,0:T(8,128)(2,1)S(1)}, u32[]{:S(2)}, u32[]{:S(2)}) collective-permute-start(bf16[256,512]{1,0:T(8,128)(2,1)} %forward.4.refs_2_), channel_id=1, source_target_pairs={{0,1},{1,0},{2,3},{3,2},{4,5},{5,4},{6,7},{7,6},{8,9},{9,8},{10,11... | collective-permute-start | bytes 786440 | tf_op jit(solution)/shard_map/ppermute | solution.py:285
  40.7 11.7 %collective-permute-start.6 = (bf16[256,512]{1,0:T(8,128)(2,1)S(1)}, bf16[256,512]{1,0:T(8,128)(2,1)S(1)}, u32[]{:S(2)}, u32[]{:S(2)}) collective-permute-start(bf16[256,512]{1,0:T(8,128)(2,1)S(1)} %both.2.refs_0_), channel_id=1, source_target_pairs={{0,1},{1,0},{2,3},{3,2},{4,5},{5,4},{6,7},{7,6},{8,9},{9,8},{10,11... | collective-permute-start | bytes 786440 | tf_op jit(solution)/shard_map/ppermute | solution.py:285
  41.0 11.4 %collective-permute-start.9 = (bf16[256,512]{1,0:T(8,128)(2,1)S(1)}, bf16[256,512]{1,0:T(8,128)(2,1)S(1)}, u32[]{:S(2)}, u32[]{:S(2)}) collective-permute-start(bf16[256,512]{1,0:T(8,128)(2,1)S(1)} %both.3.refs_3_), channel_id=1, source_target_pairs={{0,1},{1,0},{2,3},{3,2},{4,5},{5,4},{6,7},{7,6},{8,9},{9,8},{10,11... | collective-permute-start | bytes 786440 | tf_op jit(solution)/shard_map/ppermute | solution.py:285
  46.9 5.5 %collective-permute-start.10 = (bf16[256,512]{1,0:T(8,128)(2,1)S(1)}, bf16[256,512]{1,0:T(8,128)(2,1)S(1)}, u32[]{:S(2)}, u32[]{:S(2)}) collective-permute-start(bf16[256,512]{1,0:T(8,128)(2,1)S(1)} %collective-permute-done.5.refs_4_), channel_id=1, source_target_pairs={{0,1},{1,0},{2,3},{3,2},{4,5},{5,4},{6,7},{7,6},{8,9},{9,8},{10,11... | collective-permute-start | bytes 786440 | tf_op jit(solution)/shard_map/ppermute | solution.py:285
  47.0 5.5 %collective-permute-start.7 = (bf16[256,512]{1,0:T(8,128)(2,1)S(1)}, bf16[256,512]{1,0:T(8,128)(2,1)S(1)}, u32[]{:S(2)}, u32[]{:S(2)}) collective-permute-start(bf16[256,512]{1,0:T(8,128)(2,1)S(1)} %collective-permute-done.1.refs_1_), channel_id=1, source_target_pairs={{0,1},{1,0},{2,3},{3,2},{4,5},{5,4},{6,7},{7,6},{8,9},{9,8},{10,11... | collective-permute-start | bytes 786440 | tf_op jit(solution)/shard_map/ppermute | solution.py:285
  47.5 0.9 %copy-start.11 = (bf16[256,256]{1,0:T(8,128)(2,1)S(1)}, bf16[256,256]{1,0:T(8,128)(2,1)}, u32[]{:S(2)}) copy-start(bf16[256,256]{1,0:T(8,128)(2,1)} %copy-done.10) | copy-start | bytes 393220
  52.5 1.0 %copy-start.4 = (bf16[256,512]{1,0:T(8,128)(2,1)S(1)}, bf16[256,512]{1,0:T(8,128)(2,1)}, u32[]{:S(2)}) copy-start(bf16[256,512]{1,0:T(8,128)(2,1)} %forward.4.refs_2_) | copy-start | bytes 786436
  53.4 5.2 %copy-start = (bf16[256,2048]{1,0:T(8,128)(2,1)S(1)}, bf16[256,2048]{1,0:T(8,128)(2,1)}, u32[]{:S(2)}) copy-start(bf16[256,2048]{1,0:T(8,128)(2,1)} %first.2) | copy-start | bytes 3145732
  53.4 5.2 %copy-start.1 = (bf16[2048,256]{1,0:T(8,128)(2,1)S(1)}, bf16[2048,256]{1,0:T(8,128)(2,1)}, u32[]{:S(2)}) copy-start(bf16[2048,256]{1,0:T(8,128)(2,1)} %second.2) | copy-start | bytes 3145732
  53.4 5.2 %copy-start.2 = (bf16[256,2048]{1,0:T(8,128)(2,1)S(1)}, bf16[256,2048]{1,0:T(8,128)(2,1)}, u32[]{:S(2)}) copy-start(bf16[256,2048]{1,0:T(8,128)(2,1)} %first.3) | copy-start | bytes 3145732
  53.4 5.2 %copy-start.3 = (bf16[2048,256]{1,0:T(8,128)(2,1)S(1)}, bf16[2048,256]{1,0:T(8,128)(2,1)}, u32[]{:S(2)}) copy-start(bf16[2048,256]{1,0:T(8,128)(2,1)} %second.3) | copy-start | bytes 3145732
  58.5 6.1 %collective-permute-start.19 = (bf16[1024,512]{1,0:T(8,128)(2,1)S(1)}, bf16[1024,512]{1,0:T(8,128)(2,1)S(1)}, u32[]{:S(2)}, u32[]{:S(2)}) collective-permute-start(bf16[1024,512]{1,0:T(8,128)(2,1)S(1)} %contrast.1.grads_ref), channel_id=1, source_target_pairs={{0,1},{1,0},{2,3},{3,2},{4,5},{5,4},{6,7},{7,6},{8,9},{9,8},{10,11... | collective-permute-start | bytes 3145736 | tf_op jit(solution)/shard_map/ppermute | solution.py:285
  68.0 5.9 %collective-permute-start.20 = (f32[256,1024]{1,0:T(8,128)S(1)}, f32[256,1024]{1,0:T(8,128)S(1)}, u32[]{:S(2)}, u32[]{:S(2)}) collective-permute-start(f32[256,1024]{1,0:T(8,128)S(1)} %get-tuple-element.37.refs_0_), channel_id=1, source_target_pairs={{0,1},{1,0},{2,3},{3,2},{4,5},{5,4},{6,7},{7,6},{8,9},{9,8},{10,11... | collective-permute-start | bytes 3145736 | tf_op jit(solution)/shard_map/ppermute | solution.py:285
  68.6 5.3 %collective-permute-start.21 = (f32[1024,256]{1,0:T(8,128)S(1)}, f32[1024,256]{1,0:T(8,128)S(1)}, u32[]{:S(2)}, u32[]{:S(2)}) collective-permute-start(f32[1024,256]{1,0:T(8,128)S(1)} %get-tuple-element.38.refs_1_), channel_id=1, source_target_pairs={{0,1},{1,0},{2,3},{3,2},{4,5},{5,4},{6,7},{7,6},{8,9},{9,8},{10,11... | collective-permute-start | bytes 3145736 | tf_op jit(solution)/shard_map/ppermute | solution.py:285
  73.3 3.2 %collective-permute-start.22 = (f32[256,1024]{1,0:T(8,128)S(1)}, f32[256,1024]{1,0:T(8,128)S(1)}, u32[]{:S(2)}, u32[]{:S(2)}) collective-permute-start(f32[256,1024]{1,0:T(8,128)S(1)} %get-tuple-element.42.refs_2_), channel_id=1, source_target_pairs={{0,1},{1,0},{2,3},{3,2},{4,5},{5,4},{6,7},{7,6},{8,9},{9,8},{10,11... | collective-permute-start | bytes 3145736 | tf_op jit(solution)/shard_map/ppermute | solution.py:285
  73.8 3.8 %collective-permute-start.23 = (f32[1024,256]{1,0:T(8,128)S(1)}, f32[1024,256]{1,0:T(8,128)S(1)}, u32[]{:S(2)}, u32[]{:S(2)}) collective-permute-start(f32[1024,256]{1,0:T(8,128)S(1)} %get-tuple-element.43.refs_3_), channel_id=1, source_target_pairs={{0,1},{1,0},{2,3},{3,2},{4,5},{5,4},{6,7},{7,6},{8,9},{9,8},{10,11... | collective-permute-start | bytes 3145736 | tf_op jit(solution)/shard_map/ppermute | solution.py:285

commit v6 on v4

--- a/solution.py
+++ b/solution.py
@@ -54,34 +54,63 @@
         out_ref[:, k * emb : (k + 1) * emb] = dot(active[...], second[...]).astype(BF)
 
 
-def first_kernel(x_ref, *refs):
-    weights, out_ref, held, active, sems = refs[:4], refs[4], refs[5:9], refs[9], refs[10]
-    copies = [pltpu.make_async_copy(w, h, sems.at[i]) for i, (w, h) in enumerate(zip(weights, held))]
-    for i in (0, 2, 1, 3):
-        copies[i].start()
+def first_kernel(n_rep, n_blk, n_sub, pos_ref, x_hbm, *refs):
+    weights, (distance_ref, place_ref, episode_ref) = refs[:4], refs[4:7]
+    out_ref, pack_ref, held, active, x_ref, sems = refs[7], refs[8], refs[9:13], refs[13], refs[14], refs[15]
+    copies = [pltpu.make_async_copy(x_hbm, x_ref, sems.at[4])]
+    copies += [pltpu.make_async_copy(weights[i], held[i], sems.at[i]) for i in (0, 2, 1, 3)]
     for c in copies:
+        c.start()
+    rows = x_ref.shape[0]
+    slab = rows // n_rep
+
+    def bits(n):
+        return n.bit_length() - 1
+
+    owner = (pos_ref[0] * n_sub + pos_ref[1] + distance_ref[...]) & (n_blk * n_sub - 1)
+    place = place_ref[...]
+    batch = ((owner & (n_sub - 1)) << bits(n_rep)) + (place >> bits(slab))
+    goal = (((batch << bits(n_blk)) + (owner >> bits(n_sub))) << bits(slab)) + (place & (slab - 1))
+    digits = (goal >> 8, goal & 255, episode_ref[...])
+    table = jnp.concatenate([d.astype(F32) for d in digits] + [jnp.zeros((13, rows), F32)], axis=0)
+    pack_ref[rows:, :] = table.astype(BF)
+    copies[0].wait()
+    pack_ref[:rows, :] = x_ref[...]
+    for c in copies[1:]:
         c.wait()
     encode(x_ref, held, out_ref, active)
 
 
-def forward_kernel(x_ref, *refs):
-    encode(x_ref, refs[:4], refs[4], refs[5])
-
-
-def forward(x, weights, load=False):
+def first_forward(pos, x, weights, meta, n_rep, n_blk, n_sub):
     rows, width = x.shape
     hid, emb = weights[2].shape
-    outs = [((rows, 2 * emb), BF)] + [(w.shape, w.dtype) for w in weights] * load
-    got = kernel(
-        first_kernel if load else forward_kernel,
+    part, pack, *held = kernel(
+        functools.partial(first_kernel, n_rep, n_blk, n_sub),
         "forward",
-        outs,
+        [((rows, 2 * emb), BF), ((rows + 16, width), BF)] + [(w.shape, w.dtype) for w in weights],
+        (x, *weights, *meta),
+        [pltpu.VMEM((rows, hid), BF), pltpu.VMEM(x.shape, x.dtype), pltpu.SemaphoreType.DMA((5,))],
+        limit=49,
+        pos=pos,
+        hbm=range(5),
+    )
+    return part, pack, held
+
+
+def forward_kernel(x_ref, *refs):
+    encode(x_ref.at[: refs[4].shape[0]], refs[:4], refs[4], refs[5])
+
+
+def forward(x, weights, rows):
+    hid, emb = weights[2].shape
+    return kernel(
+        forward_kernel,
+        "forward",
+        [((rows, 2 * emb), BF)],
         (x, *weights),
-        [pltpu.VMEM((rows, hid), BF)] + [pltpu.SemaphoreType.DMA((4,))] * load,
-        flops=8 * rows * width * hid,
-        hbm=(1, 2, 3, 4) if load else (),
-    )
-    return (got[0], got[1:]) if load else got[0]
+        [pltpu.VMEM((rows, hid), BF)],
+        limit=8,
+    )[0]
 
 
 def add_kernel(a_ref, b_ref, out_ref):
@@ -104,17 +133,9 @@
     return jnp.broadcast_to(row, (128, row.shape[1])).T[:, :1]
 
 
-def meta_row(pos_ref, meta_ref, which, r, n_blk, slab):
-    parts = []
-    for blk in range(n_blk):
-        at = pl.multiple_of(jnp.bitwise_xor(blk, pos_ref[0]) * 8, 8)
-        parts.append(meta_ref[pl.ds(at, 8), r * slab : (r + 1) * slab][which : which + 1, :])
-    return jnp.concatenate(parts, axis=1).astype(F32)
-
-
 def arrange_kernel(n_blk, n_rep, slab, pos_ref, *refs):
-    mine, other, metas = refs[:n_blk], refs[n_blk : 2 * n_blk], refs[2 * n_blk : 2 * n_blk + 2]
-    rows_mine, rows_other, goals_mine, goals_other, pick_ref, both_sides, pick_other = refs[2 * n_blk + 2 :]
+    mine, other = refs[:n_blk], refs[n_blk : 2 * n_blk]
+    rows_mine, rows_other, goals_mine, goals_other, pick_ref, ep_ref, both_sides, pick_other, meta = refs[2 * n_blk :]
     half = rows_mine.shape[0]
     rows = 2 * half
     batch = n_blk * slab
@@ -125,10 +146,16 @@
             both_sides[pl.ds(i * half + off, slab), :] = value
 
         place_blocks(pos_ref, blocks, put, n_blk, n_rep, slab)
-    for meta, pick, goals in ((metas[0], pick_ref, goals_mine), (metas[1], pick_other, goals_other)):
+        for k, block in enumerate(blocks):
+            at = jnp.bitwise_xor(pos_ref[0], k)
+            for r in range(n_rep):
+                off = pl.multiple_of((r * n_blk + at) * slab, slab)
+                meta[i, :, pl.ds(off, slab)] = block[n_rep * slab :, r * slab : (r + 1) * slab].astype(F32)
+    ep_ref[...] = meta[0, 2:3, :]
+    for i, (pick, goals) in enumerate(((pick_ref, goals_mine), (pick_other, goals_other))):
         for r in range(n_rep):
             own = slice(r * batch, (r + 1) * batch)
-            goal = column(meta_row(pos_ref, meta, 0, r, n_blk, slab)).astype(jnp.int32) + pos_ref[1] * half
+            goal = column(meta[i, 0:1, own] * 256.0 + meta[i, 1:2, own]).astype(jnp.int32) + pos_ref[1] * half
             goal = jnp.where(goal >= rows, goal - rows, goal)
             pick[own, :] = jnp.where(
                 goal == lax.broadcasted_iota(jnp.int32, (batch, rows), 1), 1.0, 0.0
@@ -138,7 +165,7 @@
 
 def contrast_kernel(n_blk, n_rep, slab, scale, pos_ref, *refs):
     n = n_blk + 1
-    mine, other, meta_ref, pick_ref = refs[:n], refs[n : 2 * n], refs[2 * n], refs[2 * n + 1]
+    mine, other, ep_ref, pick_ref = refs[:n], refs[n : 2 * n], refs[2 * n], refs[2 * n + 1]
     grads_ref, phi_all, psi_all = refs[2 * n + 2 :]
     half, emb = phi_all.shape
     batch = n_blk * slab
@@ -163,7 +190,7 @@
     )
     for r in range(n_rep):
         own = slice(r * batch, (r + 1) * batch)
-        ep_row = meta_row(pos_ref, meta_ref, 1, r, n_blk, slab)
+        ep_row = ep_ref[:, own]
         psi = dot(pick_ref[own, :], psi_all[...]).astype(BF)
         phi = phi_all[own, :]
         scores = lax.dot_general(phi, psi, (((1,), (1,)), ((), ())), preferred_element_type=F32)
@@ -284,46 +311,41 @@
     def after(x, *first):
         return lax.optimization_barrier((x, *first))[0]
 
-    got = {0: states, 3: across(states, 3), 2: across(states, 2)}
-    part0, weights = forward(states, (state_first, goal_first, state_second, goal_second), load=True)
+    weights = (state_first, goal_first, state_second, goal_second)
+    meta = (goal_distance.reshape(1, rows_dev), goal_row.reshape(1, rows_dev), episode.reshape(1, rows_dev))
+    part0, pack, held = first_forward(pos, states, weights, meta, n_rep, n_blk, n_sub)
+    got = {k: across(pack, k) if k else pack for k in (0, 3, 2, 1)}
     there0 = swap(part0, "rep")
-    got[1] = across(after(states, part0), 1)
-    part3 = forward(got[3], weights)
+    part3 = forward(got[3], held, rows_dev)
     there3 = swap(part3, "rep")
-
-    distance = after(goal_distance, part0)
-    owner = (b * n_sub + s + distance[:, 0]) % owners
-    goal = (((owner % n_sub) * n_rep + goal_row // slab) * n_blk + owner // n_sub) * slab + goal_row % slab
-    meta = jnp.pad(jnp.stack([goal, episode]), ((0, 6), (0, 0)))
-    meta = jnp.concatenate([meta, across(meta, 1)], axis=0)
-    meta = jnp.concatenate([meta, across(meta, 2)], axis=0)
-    meta_other = swap(meta, "sub")
 
     sums = {0: both(part0, there0)}
     sums[1] = across(sums[0], 1)
-    part2 = forward(after(got[2], sums[0]), weights)
+    part2 = forward(after(got[2], sums[0]), held, rows_dev)
     there2 = swap(part2, "rep")
     sums[3] = both(part3, there3)
     embedded = [sums[0], sums[1], part2, sums[3], there2]
 
     side = ((rows_all // 2, width), BF)
-    mine, other, goals_mine, goals_other, pick = kernel(
+    mine, other, goals_mine, goals_other, pick, episodes = kernel(
         functools.partial(arrange_kernel, n_blk, n_rep, slab),
         "arrange",
-        [side, side, side, side, ((rows_all // 2, rows_all), BF)],
-        (*(got[k] for k in range(n_blk)), *(swap(got[k], "sub") for k in range(n_blk)), meta, meta_other),
-        [pltpu.VMEM((rows_all, width), BF), pltpu.VMEM((rows_all // 2, rows_all), BF)],
-        pos=pos,
-        flops=2 * rows_all * rows_all * width,
+        [side, side, side, side, ((rows_all // 2, rows_all), BF), ((1, rows_all // 2), F32)],
+        (*(got[k] for k in range(n_blk)), *(swap(got[k], "sub") for k in range(n_blk))),
+        [
+            pltpu.VMEM((rows_all, width), BF),
+            pltpu.VMEM((rows_all // 2, rows_all), BF),
+            pltpu.VMEM((2, 16, rows_all // 2), F32),
+        ],
+        pos=pos,
     )
     (grads_mine,) = kernel(
         functools.partial(contrast_kernel, n_blk, n_rep, slab, 4.0 / math.sqrt(emb)),
         "contrast",
         [((rows_all // 2, 2 * emb), BF)],
-        (*embedded, *(swap(x, "sub") for x in embedded), meta, pick),
+        (*embedded, *(swap(x, "sub") for x in embedded), episodes, pick),
         [pltpu.VMEM((rows_all // 2, emb), BF), pltpu.VMEM((rows_all, emb), BF)],
         pos=pos,
-        flops=rows_all * emb * (rows_all + 3 * n_blk * slab),
     )
     grads_other = swap(grads_mine, "sub")
 

time: 70 us -> 68.2 us (0.974)
  local copies, waits for them, and re-layouts: 8.02 us -> 2.96 us
  starting transfers between devices: 15.8 us -> 17.9 us
  Pallas kernels: 33.7 us -> 35.3 us
    unnamed x24 -> x16, local copies, waits for them, and re-layouts: 8.01 us -> 2.96 us
    ppermute x6 -> x4, starting transfers between devices: 8.83 us -> 10.6 us  [across(): return lax.ppermute(x, 'blk', [(i, i ^ k) for i in range(n_blk)])]
    ppermute x6 -> x4, waiting for transfers between devices: 2.15 us -> 3.88 us  [across(): return lax.ppermute(x, 'blk', [(i, i ^ k) for i in range(n_blk)])]
    ppermute x18 -> x17, waiting for transfers between devices: 8.59 us -> 6.98 us  [swap(): return lax.ppermute(x, axis, [(0, 1), (1, 0)])]
    pallas_call x12, Pallas kernels: 33.7 us -> 35.3 us  [kernel(): pl.pallas_call(body, in_specs=specs, out_specs=[HBM if i in hbm_out else...]
    ppermute x18 -> x17, starting transfers between devices: 6.96 us -> 7.25 us  [swap(): return lax.ppermute(x, axis, [(0, 1), (1, 0)])]
  transfers between devices with their start and end apart: 24 -> 21, of which waited for: 5 -> 7; matrix products, arithmetic and copies ran while one was open for 0% -> 0% of each run, Pallas kernels for 33% -> 30%
where the time goes in v6:
time: 68.2 us; the launch traced here: 68 us
  Pallas kernels  35.3 us (52%)
  starting transfers between devices  17.9 us (26%)
  waiting for transfers between devices  10.9 us (16%)
  local copies, waits for them, and re-layouts  2.96 us (4%)
  between operations  0.99 us (1%)
    pallas_call x12, Pallas kernels, kernel(): pl.pallas_call(body, in_specs=specs, out_specs=[HBM if i in hbm_out else...  35.3 us
    ppermute x4, starting transfers between devices, across(): return lax.ppermute(x, 'blk', [(i, i ^ k) for i in range(n_blk)])  10.6 us
    ppermute x17, starting transfers between devices, swap(): return lax.ppermute(x, axis, [(0, 1), (1, 0)])  7.25 us
    ppermute x17, waiting for transfers between devices, swap(): return lax.ppermute(x, axis, [(0, 1), (1, 0)])  6.98 us
    ppermute x4, waiting for transfers between devices, across(): return lax.ppermute(x, 'blk', [(i, i ^ k) for i in range(n_blk)])  3.88 us
    unnamed x16, local copies, waits for them, and re-layouts  2.96 us
  transfers between devices with their start and end apart: 21, of which 7 were waited for; matrix products, arithmetic and copies ran while one was open for 0% of the time, Pallas kernels for 30%

profile of v6, /device:TPU:0, one launch (start us, length us, event | category | flops | bytes accessed | tf_op | source)
XLA Modules:
  0.0 68.0 jit_solution(11424620508680953096)
XLA Ops:
  0.6 0.1 pad_add_fusion.pos_ref
  0.7 0.9 %copy-done.4 = bf16[256,256]{1,0:T(8,128)(2,1)S(1)} copy-done((bf16[256,256]{1,0:T(8,128)(2,1)S(1)}, bf16[256,256]{1,0:T(8,128)(2,1)}, u32[]{:S(2)}) %copy-start.4) | copy-done | bytes 131096
  1.6 0.7 copy-done.5
  2.3 0.7 copy-done.6
  3.0 0.7 copy-done.7
  3.7 4.3 %forward.3 = (bf16[256,512]{1,0:T(8,128)(2,1)S(1)}, bf16[272,256]{1,0:T(8,128)(2,1)S(1)}, bf16[256,2048]{1,0:T(8,128)(2,1)S(1)}, bf16[256,2048]{1,0:T(8,128)(2,1...) custom-call(s32[2]{0:T(128)S(1)} %pad_add_fusion.pos_ref, bf16[256,256]{1,0:T(8,128)(2,1)S(1)} %copy-done.4, ...), custom_call_target="tpu_custom_call" | custom-call | tf_op jit(solution)/shard_map/forward/pallas_call | solution.py:34
  8.0 5.1 %collective-permute-start.3 = (bf16[272,256]{1,0:T(8,128)(2,1)S(1)}, bf16[272,256]{1,0:T(8,128)(2,1)S(1)}, u32[]{:S(2)}, u32[]{:S(2)}) collective-permute-start(bf16[272,256]{1,0:T(8,128)(2,1)S(1)} %get-tuple-element.34.refs_0_), channel_id=1, source_target_pairs={{0,12},{4,8},{8,4},{12,0},{1,13},{5,9},{9,5},{13,1},{2,14},{6,10},... | collective-permute-start | bytes 417800 | tf_op jit(solution)/shard_map/ppermute | solution.py:306
  13.1 1.5 %collective-permute-start = (bf16[256,512]{1,0:T(8,128)(2,1)S(1)}, bf16[256,512]{1,0:T(8,128)(2,1)S(1)}, u32[]{:S(2)}, u32[]{:S(2)}) collective-permute-start(bf16[256,512]{1,0:T(8,128)(2,1)S(1)} %get-tuple-element.33.a_ref), channel_id=1, source_target_pairs={{0,2},{2,0},{1,3},{3,1},{4,6},{6,4},{5,7},{7,5},{8,10},{10,8},{9,1... | collective-permute-start | bytes 786440 | tf_op jit(solution)/shard_map/ppermute | solution.py:309
  14.6 0.0 collective-permute-start.2
  14.6 2.7 %collective-permute-done.3.x_ref.refs_3_ = bf16[272,256]{1,0:T(8,128)(2,1)S(1)} collective-permute-done((bf16[272,256]{1,0:T(8,128)(2,1)S(1)}, bf16[272,256]{1,0:T(8,128)(2,1)S(1)}, u32[]{:S(2)}, u32[]{:S(2)}) %collective-permute-start.3) | collective-permute-done | bytes 139296 | tf_op jit(solution)/shard_map/ppermute | solution.py:306
  17.3 1.4 %forward.5.a_ref = bf16[256,512]{1,0:T(8,128)(2,1)S(1)} custom-call(bf16[272,256]{1,0:T(8,128)(2,1)S(1)} %collective-permute-done.3.x_ref.refs_3_, bf16[256,2048]{1,0:T(8,128)(2,1)S(1)} %get-tuple-element.36.refs_0_, bf16[256,2048]{1,0:T(8,128)(2,1)S(1)} %get-tuple-element.37.refs_1_, bf16[2048,256]{1,0:T(8,128)(2,1)S(1)} %get-tuple-element.38.refs_2_, ...), custom_call_target="tpu_custom_call" | custom-call | tf_op jit(solution)/shard_map/forward/pallas_call | solution.py:34
  18.6 2.2 %collective-permute-start.4 = (bf16[256,512]{1,0:T(8,128)(2,1)S(1)}, bf16[256,512]{1,0:T(8,128)(2,1)S(1)}, u32[]{:S(2)}, u32[]{:S(2)}) collective-permute-start(bf16[256,512]{1,0:T(8,128)(2,1)S(1)} %forward.5.a_ref), channel_id=1, source_target_pairs={{0,2},{2,0},{1,3},{3,1},{4,6},{6,4},{5,7},{7,5},{8,10},{10,8},{9,1... | collective-permute-start | bytes 786440 | tf_op jit(solution)/shard_map/ppermute | solution.py:309
  20.8 5.5 %collective-permute-start.11 = (bf16[272,256]{1,0:T(8,128)(2,1)S(1)}, bf16[272,256]{1,0:T(8,128)(2,1)S(1)}, u32[]{:S(2)}, u32[]{:S(2)}) collective-permute-start(bf16[272,256]{1,0:T(8,128)(2,1)S(1)} %get-tuple-element.34.refs_0_), channel_id=1, source_target_pairs={{0,4},{4,0},{8,12},{12,8},{1,5},{5,1},{9,13},{13,9},{2,6},{6,2},{1... | collective-permute-start | bytes 417800 | tf_op jit(solution)/shard_map/ppermute | solution.py:306
  26.3 0.0 collective-permute-start.12
  26.3 0.0 collective-permute-done.b_ref
  26.3 0.1 both.2.refs_0_
  26.4 0.0 collective-permute-done.2.x_ref.refs_2_
  26.4 1.4 %forward.4.refs_2_ = bf16[256,512]{1,0:T(8,128)(2,1)S(1)} custom-call(bf16[272,256]{1,0:T(8,128)(2,1)S(1)} %collective-permute-done.2.x_ref.refs_2_, bf16[256,2048]{1,0:T(8,128)(2,1)S(1)} %get-tuple-element.36.refs_0_, bf16[256,2048]{1,0:T(8,128)(2,1)S(1)} %get-tuple-element.37.refs_1_, bf16[2048,256]{1,0:T(8,128)(2,1)S(1)} %get-tuple-element.38.refs_2_, ...), custom_call_target="tpu_custom_call" | custom-call | tf_op jit(solution)/shard_map/forward/pallas_call | solution.py:34
  27.8 0.6 collective-permute-start.5
  28.4 0.0 collective-permute-start.1
  28.4 1.0 %collective-permute-done.11.refs_1_ = bf16[272,256]{1,0:T(8,128)(2,1)S(1)} collective-permute-done((bf16[272,256]{1,0:T(8,128)(2,1)S(1)}, bf16[272,256]{1,0:T(8,128)(2,1)S(1)}, u32[]{:S(2)}, u32[]{:S(2)}) %collective-permute-start.11) | collective-permute-done | bytes 139296 | tf_op jit(solution)/shard_map/ppermute | solution.py:306
  29.4 0.0 collective-permute-start.14
  29.4 0.0 collective-permute-done.12.refs_4_
  29.4 0.5 collective-permute-start.15
  29.9 0.0 collective-permute-done.4.b_ref
  29.9 0.1 collective-permute-start.13
  30.0 0.1 both.3.refs_3_
  30.0 0.7 %collective-permute-done.14.refs_6_ = bf16[272,256]{1,0:T(8,128)(2,1)S(1)} collective-permute-done((bf16[272,256]{1,0:T(8,128)(2,1)S(1)}, bf16[272,256]{1,0:T(8,128)(2,1)S(1)}, u32[]{:S(2)}, u32[]{:S(2)}) %collective-permute-start.14) | collective-permute-done | bytes 139296 | tf_op jit(solution)/shard_map/ppermute | solution.py:309
  30.7 0.1 collective-permute-start.8
  30.9 0.1 collective-permute-done.15.refs_7_
  30.9 0.3 collective-permute-start.6
  31.2 0.0 collective-permute-done.13.refs_5_
  31.2 0.2 collective-permute-start.9
  31.4 5.1 %collective-permute-done.5.refs_4_ = bf16[256,512]{1,0:T(8,128)(2,1)S(1)} collective-permute-done((bf16[256,512]{1,0:T(8,128)(2,1)S(1)}, bf16[256,512]{1,0:T(8,128)(2,1)S(1)}, u32[]{:S(2)}, u32[]{:S(2)}) %collective-permute-start.5) | collective-permute-done | bytes 262176 | tf_op jit(solution)/shard_map/ppermute | solution.py:309
  36.6 0.0 collective-permute-start.10
  36.6 0.3 collective-permute-done.1.refs_1_
  36.8 0.3 collective-permute-start.7
  37.1 4.0 %arrange.1 = (bf16[1024,256]{1,0:T(8,128)(2,1)S(1)}, bf16[1024,256]{1,0:T(8,128)(2,1)S(1)}, bf16[1024,256]{1,0:T(8,128)(2,1)S(1)}, bf16[1024,256]{1,0:T(8,128)(2...) custom-call(s32[2]{0:T(128)S(1)} %pad_add_fusion.pos_ref, ...), custom_call_target="tpu_custom_call" | custom-call | tf_op jit(solution)/shard_map/arrange/pallas_call | solution.py:34
  41.1 0.0 collective-permute-done.8.refs_7_
  41.1 0.0 collective-permute-done.6.refs_5_
  41.2 0.0 collective-permute-done.9.refs_8_
  41.2 0.0 collective-permute-done.10.refs_9_
  41.2 0.0 collective-permute-done.7.refs_6_
  41.2 0.0 copy-start
  41.2 0.0 copy-start.1
  41.2 0.0 copy-start.2
  41.2 0.0 copy-start.3
  41.2 5.1 %contrast.1.grads_ref = bf16[1024,512]{1,0:T(8,128)(2,1)S(1)} custom-call(s32[2]{0:T(128)S(1)} %pad_add_fusion.pos_ref, bf16[256,512]{1,0:T(8,128)(2,1)S(1)} %both.2.refs_0_, bf16[256,512]{1,0:T(8,128)(2,1)S(1)} %collective-permute-done.1.refs_1_, bf16[256,512]{1,0:T(8,128)(2,1)S(1)} %forward.4.refs_2_, bf16[256,512]{1,0:T(8,128)(2,1)S(1)} %both.3.refs_3_, ...), custom_call_target="tpu_custom_call" | custom-call | tf_op jit(solution)/shard_map/contrast/pallas_call | solution.py:34
  46.3 0.3 collective-permute-start.16
  46.7 0.0 copy-done
  46.7 6.3 %mine.1 = (f32[1024,256]{1,0:T(8,128)S(1)}, f32[1024,256]{1,0:T(8,128)S(1)}, f32[1024,256]{1,0:T(8,128)S(1)}, f32[1024,256]{1,0:T(8,128)S(1)}) custom-call(s32[2]{0:T(128)S(1)} %pad_add_fusion.pos_ref, bf16[256,2048]{1,0:T(8,128)(2,1)S(1)} %copy-done, bf16[256,2048]{1,0:T(8,128)(2,1)S(1)} %copy-done.2, bf16[2048,256]{1,0:T(8,128)(2,1)S(1)} %copy-done.1, ...), custom_call_target="tpu_custom_call" | custom-call | flops 4294967296 | tf_op jit(solution)/shard_map/mine/pallas_call | solution.py:34
  53.0 0.0 collective-permute-done.16.grads_ref
  53.0 3.5 %other_state.1 = (f32[256,1024]{1,0:T(8,128)S(1)}, f32[1024,256]{1,0:T(8,128)S(1)}) custom-call(s32[2]{0:T(128)S(1)} %pad_add_fusion.pos_ref, bf16[256,2048]{1,0:T(8,128)(2,1)S(1)} %copy-done, bf16[2048,256]{1,0:T(8,128)(2,1)S(1)} %copy-done.1, bf16[1024,512]{1,0:T(8,128)(2,1)S(1)} %collective-permute-done.16.grads_ref, ...), custom_call_target="tpu_custom_call" | custom-call | flops 2147483648 | tf_op jit(solution)/shard_map/other_state/pallas_call | solution.py:34
  56.5 0.3 collective-permute-start.17
  56.8 0.2 collective-permute-start.18
  57.0 4.7 %other_goal.1 = (f32[256,1024]{1,0:T(8,128)S(1)}, f32[1024,256]{1,0:T(8,128)S(1)}, f32[256,2048]{1,0:T(8,128)}, f32[2048,256]{1,0:T(8,128)}) custom-call(s32[2]{0:T(128)S(1)} %pad_add_fusion.pos_ref, bf16[256,2048]{1,0:T(8,128)(2,1)S(1)} %copy-done.2, bf16[2048,256]{1,0:T(8,128)(2,1)S(1)} %copy-done.3, ...), custom_call_target="tpu_custom_call" | custom-call | flops 2147483648 | tf_op jit(solution)/shard_map/other_goal/pallas_call | solution.py:34
  61.8 0.3 collective-permute-start.19
  62.1 0.2 collective-permute-start.20
  62.4 0.0 collective-permute-done.17.refs_0_
  62.4 0.0 collective-permute-done.18.refs_1_
  62.4 2.6 %finish.2 = (f32[256,2048]{1,0:T(8,128)}, f32[2048,256]{1,0:T(8,128)}, f32[256,2048]{1,0:T(8,128)}, f32[2048,256]{1,0:T(8,128)}) custom-call(s32[2]{0:T(128)S(1)} %pad_add_fusion.pos_ref, f32[256,1024]{1,0:T(8,128)S(1)} %collective-permute-done.17.refs_0_, ...), custom_call_target="tpu_custom_call", output_to_operand_aliasing={{0}: (5, {}), {1}: (6, {})} | custom-call | tf_op jit(solution)/shard_map/finish/pallas_call | solution.py:34
  65.0 0.0 collective-permute-done.19.refs_0_
  65.0 1.0 %collective-permute-done.20.refs_1_ = f32[1024,256]{1,0:T(8,128)S(1)} collective-permute-done((f32[1024,256]{1,0:T(8,128)S(1)}, f32[1024,256]{1,0:T(8,128)S(1)}, u32[]{:S(2)}, u32[]{:S(2)}) %collective-permute-start.20) | collective-permute-done | bytes 1048608 | tf_op jit(solution)/shard_map/ppermute | solution.py:309
  66.0 1.9 %finish.3 = (f32[256,2048]{1,0:T(8,128)}, f32[2048,256]{1,0:T(8,128)}) custom-call(s32[2]{0:T(128)S(1)} %pad_add_fusion.pos_ref, f32[256,1024]{1,0:T(8,128)S(1)} %collective-permute-done.19.refs_0_, f32[1024,256]{1,0:T(8,128)S(1)} %collective-permute-done.20.refs_1_, ...), custom_call_target="tpu_custom_call", output_to_operand_aliasing={{0}: (3, {}), {1}: (4, {})} | custom-call | tf_op jit(solution)/shard_map/finish/pallas_call | solution.py:34
  (7 shorter events, 0.0 us)
Async XLA Ops:
  0.7 0.9 %copy-start.4 = (bf16[256,256]{1,0:T(8,128)(2,1)S(1)}, bf16[256,256]{1,0:T(8,128)(2,1)}, u32[]{:S(2)}) copy-start(bf16[256,256]{1,0:T(8,128)(2,1)} %x_hbm.1) | copy-start | bytes 393220
  1.6 0.7 copy-start.5
  2.3 0.7 copy-start.6
  3.0 0.7 copy-start.7
  8.0 9.3 %collective-permute-start.3 = (bf16[272,256]{1,0:T(8,128)(2,1)S(1)}, bf16[272,256]{1,0:T(8,128)(2,1)S(1)}, u32[]{:S(2)}, u32[]{:S(2)}) collective-permute-start(bf16[272,256]{1,0:T(8,128)(2,1)S(1)} %get-tuple-element.34.refs_0_), channel_id=1, source_target_pairs={{0,12},{4,8},{8,4},{12,0},{1,13},{5,9},{9,5},{13,1},{2,14},{6,10},... | collective-permute-start | bytes 417800 | tf_op jit(solution)/shard_map/ppermute | solution.py:306
  13.1 13.3 %collective-permute-start = (bf16[256,512]{1,0:T(8,128)(2,1)S(1)}, bf16[256,512]{1,0:T(8,128)(2,1)S(1)}, u32[]{:S(2)}, u32[]{:S(2)}) collective-permute-start(bf16[256,512]{1,0:T(8,128)(2,1)S(1)} %get-tuple-element.33.a_ref), channel_id=1, source_target_pairs={{0,2},{2,0},{1,3},{3,1},{4,6},{6,4},{5,7},{7,5},{8,10},{10,8},{9,1... | collective-permute-start | bytes 786440 | tf_op jit(solution)/shard_map/ppermute | solution.py:309
  14.6 11.8 %collective-permute-start.2 = (bf16[272,256]{1,0:T(8,128)(2,1)S(1)}, bf16[272,256]{1,0:T(8,128)(2,1)S(1)}, u32[]{:S(2)}, u32[]{:S(2)}) collective-permute-start(bf16[272,256]{1,0:T(8,128)(2,1)S(1)} %get-tuple-element.34.refs_0_), channel_id=1, source_target_pairs={{0,8},{4,12},{8,0},{12,4},{1,9},{5,13},{9,1},{13,5},{2,10},{6,14},... | collective-permute-start | bytes 417800 | tf_op jit(solution)/shard_map/ppermute | solution.py:306
  18.6 11.3 %collective-permute-start.4 = (bf16[256,512]{1,0:T(8,128)(2,1)S(1)}, bf16[256,512]{1,0:T(8,128)(2,1)S(1)}, u32[]{:S(2)}, u32[]{:S(2)}) collective-permute-start(bf16[256,512]{1,0:T(8,128)(2,1)S(1)} %forward.5.a_ref), channel_id=1, source_target_pairs={{0,2},{2,0},{1,3},{3,1},{4,6},{6,4},{5,7},{7,5},{8,10},{10,8},{9,1... | collective-permute-start | bytes 786440 | tf_op jit(solution)/shard_map/ppermute | solution.py:309
  20.8 8.5 %collective-permute-start.11 = (bf16[272,256]{1,0:T(8,128)(2,1)S(1)}, bf16[272,256]{1,0:T(8,128)(2,1)S(1)}, u32[]{:S(2)}, u32[]{:S(2)}) collective-permute-start(bf16[272,256]{1,0:T(8,128)(2,1)S(1)} %get-tuple-element.34.refs_0_), channel_id=1, source_target_pairs={{0,4},{4,0},{8,12},{12,8},{1,5},{5,1},{9,13},{13,9},{2,6},{6,2},{1... | collective-permute-start | bytes 417800 | tf_op jit(solution)/shard_map/ppermute | solution.py:306
  26.3 3.0 %collective-permute-start.12 = (bf16[272,256]{1,0:T(8,128)(2,1)S(1)}, bf16[272,256]{1,0:T(8,128)(2,1)S(1)}, u32[]{:S(2)}, u32[]{:S(2)}) collective-permute-start(bf16[272,256]{1,0:T(8,128)(2,1)S(1)} %get-tuple-element.34.refs_0_), channel_id=1, source_target_pairs={{0,1},{1,0},{2,3},{3,2},{4,5},{5,4},{6,7},{7,6},{8,9},{9,8},{10,11... | collective-permute-start | bytes 417800 | tf_op jit(solution)/shard_map/ppermute | solution.py:309
  27.8 8.8 %collective-permute-start.5 = (bf16[256,512]{1,0:T(8,128)(2,1)S(1)}, bf16[256,512]{1,0:T(8,128)(2,1)S(1)}, u32[]{:S(2)}, u32[]{:S(2)}) collective-permute-start(bf16[256,512]{1,0:T(8,128)(2,1)S(1)} %forward.4.refs_2_), channel_id=1, source_target_pairs={{0,2},{2,0},{1,3},{3,1},{4,6},{6,4},{5,7},{7,5},{8,10},{10,8},{9,1... | collective-permute-start | bytes 786440 | tf_op jit(solution)/shard_map/ppermute | solution.py:309
  28.4 8.4 %collective-permute-start.1 = (bf16[256,512]{1,0:T(8,128)(2,1)S(1)}, bf16[256,512]{1,0:T(8,128)(2,1)S(1)}, u32[]{:S(2)}, u32[]{:S(2)}) collective-permute-start(bf16[256,512]{1,0:T(8,128)(2,1)S(1)} %both.2.refs_0_), channel_id=1, source_target_pairs={{0,4},{4,0},{8,12},{12,8},{1,5},{5,1},{9,13},{13,9},{2,6},{6,2},{1... | collective-permute-start | bytes 786440 | tf_op jit(solution)/shard_map/ppermute | solution.py:306
  29.4 1.4 %collective-permute-start.14 = (bf16[272,256]{1,0:T(8,128)(2,1)S(1)}, bf16[272,256]{1,0:T(8,128)(2,1)S(1)}, u32[]{:S(2)}, u32[]{:S(2)}) collective-permute-start(bf16[272,256]{1,0:T(8,128)(2,1)S(1)} %collective-permute-done.2.x_ref.refs_2_), channel_id=1, source_target_pairs={{0,1},{1,0},{2,3},{3,2},{4,5},{5,4},{6,7},{7,6},{8,9},{9,8},{10,11... | collective-permute-start | bytes 417800 | tf_op jit(solution)/shard_map/ppermute | solution.py:309
  29.4 1.6 %collective-permute-start.15 = (bf16[272,256]{1,0:T(8,128)(2,1)S(1)}, bf16[272,256]{1,0:T(8,128)(2,1)S(1)}, u32[]{:S(2)}, u32[]{:S(2)}) collective-permute-start(bf16[272,256]{1,0:T(8,128)(2,1)S(1)} %collective-permute-done.3.x_ref.refs_3_), channel_id=1, source_target_pairs={{0,1},{1,0},{2,3},{3,2},{4,5},{5,4},{6,7},{7,6},{8,9},{9,8},{10,11... | collective-permute-start | bytes 417800 | tf_op jit(solution)/shard_map/ppermute | solution.py:309
  29.9 1.4 %collective-permute-start.13 = (bf16[272,256]{1,0:T(8,128)(2,1)S(1)}, bf16[272,256]{1,0:T(8,128)(2,1)S(1)}, u32[]{:S(2)}, u32[]{:S(2)}) collective-permute-start(bf16[272,256]{1,0:T(8,128)(2,1)S(1)} %collective-permute-done.11.refs_1_), channel_id=1, source_target_pairs={{0,1},{1,0},{2,3},{3,2},{4,5},{5,4},{6,7},{7,6},{8,9},{9,8},{10,11... | collective-permute-start | bytes 417800 | tf_op jit(solution)/shard_map/ppermute | solution.py:309
  30.7 10.4 %collective-permute-start.8 = (bf16[256,512]{1,0:T(8,128)(2,1)S(1)}, bf16[256,512]{1,0:T(8,128)(2,1)S(1)}, u32[]{:S(2)}, u32[]{:S(2)}) collective-permute-start(bf16[256,512]{1,0:T(8,128)(2,1)S(1)} %forward.4.refs_2_), channel_id=1, source_target_pairs={{0,1},{1,0},{2,3},{3,2},{4,5},{5,4},{6,7},{7,6},{8,9},{9,8},{10,11... | collective-permute-start | bytes 786440 | tf_op jit(solution)/shard_map/ppermute | solution.py:309
  30.9 10.2 %collective-permute-start.6 = (bf16[256,512]{1,0:T(8,128)(2,1)S(1)}, bf16[256,512]{1,0:T(8,128)(2,1)S(1)}, u32[]{:S(2)}, u32[]{:S(2)}) collective-permute-start(bf16[256,512]{1,0:T(8,128)(2,1)S(1)} %both.2.refs_0_), channel_id=1, source_target_pairs={{0,1},{1,0},{2,3},{3,2},{4,5},{5,4},{6,7},{7,6},{8,9},{9,8},{10,11... | collective-permute-start | bytes 786440 | tf_op jit(solution)/shard_map/ppermute | solution.py:309
  31.2 9.9 %collective-permute-start.9 = (bf16[256,512]{1,0:T(8,128)(2,1)S(1)}, bf16[256,512]{1,0:T(8,128)(2,1)S(1)}, u32[]{:S(2)}, u32[]{:S(2)}) collective-permute-start(bf16[256,512]{1,0:T(8,128)(2,1)S(1)} %both.3.refs_3_), channel_id=1, source_target_pairs={{0,1},{1,0},{2,3},{3,2},{4,5},{5,4},{6,7},{7,6},{8,9},{9,8},{10,11... | collective-permute-start | bytes 786440 | tf_op jit(solution)/shard_map/ppermute | solution.py:309
  36.6 4.6 %collective-permute-start.10 = (bf16[256,512]{1,0:T(8,128)(2,1)S(1)}, bf16[256,512]{1,0:T(8,128)(2,1)S(1)}, u32[]{:S(2)}, u32[]{:S(2)}) collective-permute-start(bf16[256,512]{1,0:T(8,128)(2,1)S(1)} %collective-permute-done.5.refs_4_), channel_id=1, source_target_pairs={{0,1},{1,0},{2,3},{3,2},{4,5},{5,4},{6,7},{7,6},{8,9},{9,8},{10,11... | collective-permute-start | bytes 786440 | tf_op jit(solution)/shard_map/ppermute | solution.py:309
  36.8 4.3 %collective-permute-start.7 = (bf16[256,512]{1,0:T(8,128)(2,1)S(1)}, bf16[256,512]{1,0:T(8,128)(2,1)S(1)}, u32[]{:S(2)}, u32[]{:S(2)}) collective-permute-start(bf16[256,512]{1,0:T(8,128)(2,1)S(1)} %collective-permute-done.1.refs_1_), channel_id=1, source_target_pairs={{0,1},{1,0},{2,3},{3,2},{4,5},{5,4},{6,7},{7,6},{8,9},{9,8},{10,11... | collective-permute-start | bytes 786440 | tf_op jit(solution)/shard_map/ppermute | solution.py:309
  41.2 5.5 %copy-start = (bf16[256,2048]{1,0:T(8,128)(2,1)S(1)}, bf16[256,2048]{1,0:T(8,128)(2,1)}, u32[]{:S(2)}) copy-start(bf16[256,2048]{1,0:T(8,128)(2,1)} %first.2) | copy-start | bytes 3145732
  41.2 5.5 %copy-start.1 = (bf16[2048,256]{1,0:T(8,128)(2,1)S(1)}, bf16[2048,256]{1,0:T(8,128)(2,1)}, u32[]{:S(2)}) copy-start(bf16[2048,256]{1,0:T(8,128)(2,1)} %second.2) | copy-start | bytes 3145732
  41.2 5.5 %copy-start.2 = (bf16[256,2048]{1,0:T(8,128)(2,1)S(1)}, bf16[256,2048]{1,0:T(8,128)(2,1)}, u32[]{:S(2)}) copy-start(bf16[256,2048]{1,0:T(8,128)(2,1)} %first.3) | copy-start | bytes 3145732
  41.2 5.5 %copy-start.3 = (bf16[2048,256]{1,0:T(8,128)(2,1)S(1)}, bf16[2048,256]{1,0:T(8,128)(2,1)}, u32[]{:S(2)}) copy-start(bf16[2048,256]{1,0:T(8,128)(2,1)} %second.3) | copy-start | bytes 3145732
  46.3 6.6 %collective-permute-start.16 = (bf16[1024,512]{1,0:T(8,128)(2,1)S(1)}, bf16[1024,512]{1,0:T(8,128)(2,1)S(1)}, u32[]{:S(2)}, u32[]{:S(2)}) collective-permute-start(bf16[1024,512]{1,0:T(8,128)(2,1)S(1)} %contrast.1.grads_ref), channel_id=1, source_target_pairs={{0,1},{1,0},{2,3},{3,2},{4,5},{5,4},{6,7},{7,6},{8,9},{9,8},{10,11... | collective-permute-start | bytes 3145736 | tf_op jit(solution)/shard_map/ppermute | solution.py:309
  56.5 5.9 %collective-permute-start.17 = (f32[256,1024]{1,0:T(8,128)S(1)}, f32[256,1024]{1,0:T(8,128)S(1)}, u32[]{:S(2)}, u32[]{:S(2)}) collective-permute-start(f32[256,1024]{1,0:T(8,128)S(1)} %get-tuple-element.47.refs_0_), channel_id=1, source_target_pairs={{0,1},{1,0},{2,3},{3,2},{4,5},{5,4},{6,7},{7,6},{8,9},{9,8},{10,11... | collective-permute-start | bytes 3145736 | tf_op jit(solution)/shard_map/ppermute | solution.py:309
  56.8 5.6 %collective-permute-start.18 = (f32[1024,256]{1,0:T(8,128)S(1)}, f32[1024,256]{1,0:T(8,128)S(1)}, u32[]{:S(2)}, u32[]{:S(2)}) collective-permute-start(f32[1024,256]{1,0:T(8,128)S(1)} %get-tuple-element.48.refs_1_), channel_id=1, source_target_pairs={{0,1},{1,0},{2,3},{3,2},{4,5},{5,4},{6,7},{7,6},{8,9},{9,8},{10,11... | collective-permute-start | bytes 3145736 | tf_op jit(solution)/shard_map/ppermute | solution.py:309
  61.8 3.2 %collective-permute-start.19 = (f32[256,1024]{1,0:T(8,128)S(1)}, f32[256,1024]{1,0:T(8,128)S(1)}, u32[]{:S(2)}, u32[]{:S(2)}) collective-permute-start(f32[256,1024]{1,0:T(8,128)S(1)} %get-tuple-element.52.refs_2_), channel_id=1, source_target_pairs={{0,1},{1,0},{2,3},{3,2},{4,5},{5,4},{6,7},{7,6},{8,9},{9,8},{10,11... | collective-permute-start | bytes 3145736 | tf_op jit(solution)/shard_map/ppermute | solution.py:309
  62.1 3.9 %collective-permute-start.20 = (f32[1024,256]{1,0:T(8,128)S(1)}, f32[1024,256]{1,0:T(8,128)S(1)}, u32[]{:S(2)}, u32[]{:S(2)}) collective-permute-start(f32[1024,256]{1,0:T(8,128)S(1)} %get-tuple-element.53.refs_3_), channel_id=1, source_target_pairs={{0,1},{1,0},{2,3},{3,2},{4,5},{5,4},{6,7},{7,6},{8,9},{9,8},{10,11... | collective-permute-start | bytes 3145736 | tf_op jit(solution)/shard_map/ppermute | solution.py:309

commit v7 on v6

--- a/solution.py
+++ b/solution.py
@@ -38,29 +38,49 @@
         out_shape=[jax.ShapeDtypeStruct(shape, dtype) for shape, dtype in outs],
         scratch_shapes=scratch,
         input_output_aliases=aliases,
-        compiler_params=pltpu.CompilerParams(vmem_limit_bytes=limit * MIB),
+        compiler_params=pltpu.CompilerParams(vmem_limit_bytes=int(limit * MIB)),
         cost_estimate=pl.CostEstimate(flops=flops, bytes_accessed=0, transcendentals=0),
         name=name,
     )(*args)
 
 
-def encode(x_ref, weights, out_ref, active):
+def encode(x_ref, weights, out_ref, active, ready=lambda i: None):
     emb = weights[2].shape[1]
     for k in range(2):
         first, second = weights[k], weights[2 + k]
+        ready(k)
         for c in range(0, active.shape[1], 512):
             hidden = dot(x_ref[...], first[:, c : c + 512])
             active[:, c : c + 512] = (hidden * sigmoid(hidden)).astype(BF)
+        ready(2 + k)
         out_ref[:, k * emb : (k + 1) * emb] = dot(active[...], second[...]).astype(BF)
 
 
-def first_kernel(n_rep, n_blk, n_sub, pos_ref, x_hbm, *refs):
-    weights, (distance_ref, place_ref, episode_ref) = refs[:4], refs[4:7]
-    out_ref, pack_ref, held, active, x_ref, sems = refs[7], refs[8], refs[9:13], refs[13], refs[14], refs[15]
-    copies = [pltpu.make_async_copy(x_hbm, x_ref, sems.at[4])]
-    copies += [pltpu.make_async_copy(weights[i], held[i], sems.at[i]) for i in (0, 2, 1, 3)]
-    for c in copies:
-        c.start()
+def first_kernel(pos_ref, x_ref, *refs):
+    weights, out_ref, held, active, sems = refs[:4], refs[4], refs[5:9], refs[9], refs[10]
+    copies = [pltpu.make_async_copy(weights[i], held[i], sems.at[i]) for i in range(4)]
+    for i in (0, 2, 1, 3):
+        copies[i].start()
+    encode(x_ref, held, out_ref, active, lambda i: copies[i].wait())
+
+
+def first_forward(pos, x, weights):
+    rows, width = x.shape
+    hid, emb = weights[2].shape
+    part, *held = kernel(
+        first_kernel,
+        "forward",
+        [((rows, 2 * emb), BF)] + [(w.shape, w.dtype) for w in weights],
+        (x, *weights),
+        [pltpu.VMEM((rows, hid), BF), pltpu.SemaphoreType.DMA((4,))],
+        limit=49,
+        pos=pos,
+        hbm=range(1, 5),
+    )
+    return part, held
+
+
+def pack_kernel(n_rep, n_blk, n_sub, pos_ref, x_ref, distance_ref, place_ref, episode_ref, pack_ref, meta_ref):
     rows = x_ref.shape[0]
     slab = rows // n_rep
 
@@ -72,29 +92,10 @@
     batch = ((owner & (n_sub - 1)) << bits(n_rep)) + (place >> bits(slab))
     goal = (((batch << bits(n_blk)) + (owner >> bits(n_sub))) << bits(slab)) + (place & (slab - 1))
     digits = (goal >> 8, goal & 255, episode_ref[...])
-    table = jnp.concatenate([d.astype(F32) for d in digits] + [jnp.zeros((13, rows), F32)], axis=0)
-    pack_ref[rows:, :] = table.astype(BF)
-    copies[0].wait()
+    table = jnp.concatenate([d.astype(F32) for d in digits] + [jnp.zeros((13, rows), F32)], axis=0).astype(BF)
     pack_ref[:rows, :] = x_ref[...]
-    for c in copies[1:]:
-        c.wait()
-    encode(x_ref, held, out_ref, active)
-
-
-def first_forward(pos, x, weights, meta, n_rep, n_blk, n_sub):
-    rows, width = x.shape
-    hid, emb = weights[2].shape
-    part, pack, *held = kernel(
-        functools.partial(first_kernel, n_rep, n_blk, n_sub),
-        "forward",
-        [((rows, 2 * emb), BF), ((rows + 16, width), BF)] + [(w.shape, w.dtype) for w in weights],
-        (x, *weights, *meta),
-        [pltpu.VMEM((rows, hid), BF), pltpu.VMEM(x.shape, x.dtype), pltpu.SemaphoreType.DMA((5,))],
-        limit=49,
-        pos=pos,
-        hbm=range(5),
-    )
-    return part, pack, held
+    pack_ref[rows:, :] = table
+    meta_ref[...] = table
 
 
 def forward_kernel(x_ref, *refs):
@@ -134,8 +135,9 @@
 
 
 def arrange_kernel(n_blk, n_rep, slab, pos_ref, *refs):
-    mine, other = refs[:n_blk], refs[n_blk : 2 * n_blk]
-    rows_mine, rows_other, goals_mine, goals_other, pick_ref, ep_ref, both_sides, pick_other, meta = refs[2 * n_blk :]
+    n = n_blk + 1
+    mine, other = refs[:n], refs[n : 2 * n]
+    rows_mine, rows_other, goals_mine, goals_other, pick_ref, ep_ref, both_sides, pick_other, meta = refs[2 * n :]
     half = rows_mine.shape[0]
     rows = 2 * half
     batch = n_blk * slab
@@ -145,12 +147,13 @@
             to[pl.ds(off, slab), :] = value
             both_sides[pl.ds(i * half + off, slab), :] = value
 
-        place_blocks(pos_ref, blocks, put, n_blk, n_rep, slab)
-        for k, block in enumerate(blocks):
+        place_blocks(pos_ref, blocks[:n_blk], put, n_blk, n_rep, slab)
+        tables = [block.at[n_rep * slab :] for block in blocks[: n_blk - 1]] + [blocks[n_blk]]
+        for k, table in enumerate(tables):
             at = jnp.bitwise_xor(pos_ref[0], k)
             for r in range(n_rep):
                 off = pl.multiple_of((r * n_blk + at) * slab, slab)
-                meta[i, :, pl.ds(off, slab)] = block[n_rep * slab :, r * slab : (r + 1) * slab].astype(F32)
+                meta[i, :, pl.ds(off, slab)] = table[:, r * slab : (r + 1) * slab].astype(F32)
     ep_ref[...] = meta[0, 2:3, :]
     for i, (pick, goals) in enumerate(((pick_ref, goals_mine), (pick_other, goals_other))):
         for r in range(n_rep):
@@ -313,9 +316,20 @@
 
     weights = (state_first, goal_first, state_second, goal_second)
     meta = (goal_distance.reshape(1, rows_dev), goal_row.reshape(1, rows_dev), episode.reshape(1, rows_dev))
-    part0, pack, held = first_forward(pos, states, weights, meta, n_rep, n_blk, n_sub)
-    got = {k: across(pack, k) if k else pack for k in (0, 3, 2, 1)}
+    got = {3: across(states, 3)}
+    part0, held = first_forward(pos, states, weights)
     there0 = swap(part0, "rep")
+    pack, table = kernel(
+        functools.partial(pack_kernel, n_rep, n_blk, n_sub),
+        "pack",
+        [((rows_dev + 16, width), BF), ((16, width), BF)],
+        (after(states, part0), *meta),
+        pos=pos,
+        limit=4,
+    )
+    got[0], got[1] = pack, across(pack, 1)
+    got[2] = across(after(pack, got[3]), 2)
+    got[4] = across(after(table, got[3]), 3)
     part3 = forward(got[3], held, rows_dev)
     there3 = swap(part3, "rep")
 
@@ -324,14 +338,13 @@
     part2 = forward(after(got[2], sums[0]), held, rows_dev)
     there2 = swap(part2, "rep")
     sums[3] = both(part3, there3)
-    embedded = [sums[0], sums[1], part2, sums[3], there2]
 
     side = ((rows_all // 2, width), BF)
     mine, other, goals_mine, goals_other, pick, episodes = kernel(
         functools.partial(arrange_kernel, n_blk, n_rep, slab),
         "arrange",
         [side, side, side, side, ((rows_all // 2, rows_all), BF), ((1, rows_all // 2), F32)],
-        (*(got[k] for k in range(n_blk)), *(swap(got[k], "sub") for k in range(n_blk))),
+        (*(got[k] for k in range(n_blk + 1)), *(swap(got[k], "sub") for k in range(n_blk + 1))),
         [
             pltpu.VMEM((rows_all, width), BF),
             pltpu.VMEM((rows_all // 2, rows_all), BF),
@@ -339,6 +352,7 @@
         ],
         pos=pos,
     )
+    embedded = [sums[0], sums[1], part2, sums[3], after(there2, pick)]
     (grads_mine,) = kernel(
         functools.partial(contrast_kernel, n_blk, n_rep, slab, 4.0 / math.sqrt(emb)),
         "contrast",

time: 68.2 us -> 64.1 us (0.940)
  starting transfers between devices: 17.9 us -> 13.7 us
  local copies, waits for them, and re-layouts: 2.96 us -> 0.93 us
  waiting for transfers between devices: 10.9 us -> 12.2 us
  Pallas kernels: 35.3 us -> 36.1 us
    ppermute x4 -> x5, starting transfers between devices: 10.6 us -> 5.86 us  [across(): return lax.ppermute(x, 'blk', [(i, i ^ k) for i in range(n_blk)])]
    unnamed x16, local copies, waits for them, and re-layouts: 2.96 us -> 0.93 us
    ppermute x17 -> x18, waiting for transfers between devices: 6.98 us -> 8.1 us  [swap(): return lax.ppermute(x, axis, [(0, 1), (1, 0)])]
    pallas_call x12 -> x13, Pallas kernels: 35.3 us -> 36.1 us  [kernel(): pl.pallas_call(body, in_specs=specs, out_specs=[HBM if i in hbm_out else...]
    ppermute x17 -> x18, starting transfers between devices: 7.25 us -> 7.87 us  [swap(): return lax.ppermute(x, axis, [(0, 1), (1, 0)])]
    ppermute x4 -> x5, waiting for transfers between devices: 3.88 us -> 4.1 us  [across(): return lax.ppermute(x, 'blk', [(i, i ^ k) for i in range(n_blk)])]
  transfers between devices with their start and end apart: 21 -> 23, of which waited for: 7 -> 8; matrix products, arithmetic and copies ran while one was open for 0% -> 0% of each run, Pallas kernels for 30% -> 40%
where the time goes in v7:
time: 64.1 us; the launch traced here: 64 us
  Pallas kernels  36.1 us (56%)
  starting transfers between devices  13.7 us (21%)
  waiting for transfers between devices  12.2 us (19%)
  between operations  0.94 us (1%)
  local copies, waits for them, and re-layouts  0.93 us (1%)
    pallas_call x13, Pallas kernels, kernel(): pl.pallas_call(body, in_specs=specs, out_specs=[HBM if i in hbm_out else...  36.1 us
    ppermute x18, waiting for transfers between devices, swap(): return lax.ppermute(x, axis, [(0, 1), (1, 0)])  8.1 us
    ppermute x18, starting transfers between devices, swap(): return lax.ppermute(x, axis, [(0, 1), (1, 0)])  7.87 us
    ppermute x5, starting transfers between devices, across(): return lax.ppermute(x, 'blk', [(i, i ^ k) for i in range(n_blk)])  5.86 us
    ppermute x5, waiting for transfers between devices, across(): return lax.ppermute(x, 'blk', [(i, i ^ k) for i in range(n_blk)])  4.1 us
  transfers between devices with their start and end apart: 23, of which 8 were waited for; matrix products, arithmetic and copies ran while one was open for 0% of the time, Pallas kernels for 40%

profile of v7, /device:TPU:0, one launch (start us, length us, event | category | flops | bytes accessed | tf_op | source)
XLA Modules:
  0.0 64.0 jit_solution(11430002234498615928)
XLA Ops:
  0.6 5.1 %collective-permute-start.2 = (bf16[256,256]{1,0:T(8,128)(2,1)}, bf16[256,256]{1,0:T(8,128)(2,1)S(1)}, u32[]{:S(2)}, u32[]{:S(2)}) collective-permute-start(bf16[256,256]{1,0:T(8,128)(2,1)} %x_ref.2), channel_id=1, source_target_pairs={{0,12},{4,8},{8,4},{12,0},{1,13},{5,9},{9,5},{13,1},{2,14},{6,10},... | collective-permute-start | bytes 393224 | tf_op jit(solution)/shard_map/ppermute | solution.py:309
  5.7 0.1 pad_add_fusion.pos_ref
  5.8 0.9 %copy-done.4 = bf16[256,256]{1,0:T(8,128)(2,1)S(1)} copy-done((bf16[256,256]{1,0:T(8,128)(2,1)S(1)}, bf16[256,256]{1,0:T(8,128)(2,1)}, u32[]{:S(2)}) %copy-start.4) | copy-done | bytes 131096
  6.7 4.6 %forward.3 = (bf16[256,512]{1,0:T(8,128)(2,1)S(1)}, bf16[256,2048]{1,0:T(8,128)(2,1)S(1)}, bf16[256,2048]{1,0:T(8,128)(2,1)S(1)}, bf16[2048,256]{1,0:T(8,128)(2,1)S(1)}, bf16[2048,256]{1,0:T(8,128)(2,1)S(1)}) custom-call(s32[2]{0:T(128)S(1)} %pad_add_fusion.pos_ref, bf16[256,256]{1,0:T(8,128)(2,1)S(1)} %copy-done.4, bf16[256,2048]{1,0:T(8,128)(2,1)} %first.2, ...), custom_call_target="tpu_custom_call" | custom-call | tf_op jit(solution)/shard_map/forward/pallas_call | solution.py:34
  11.3 1.6 %collective-permute-start = (bf16[256,512]{1,0:T(8,128)(2,1)S(1)}, bf16[256,512]{1,0:T(8,128)(2,1)S(1)}, u32[]{:S(2)}, u32[]{:S(2)}) collective-permute-start(bf16[256,512]{1,0:T(8,128)(2,1)S(1)} %get-tuple-element.38.a_ref), channel_id=1, source_target_pairs={{0,2},{2,0},{1,3},{3,1},{4,6},{6,4},{5,7},{7,5},{8,10},{10,8},{9,1... | collective-permute-start | bytes 786440 | tf_op jit(solution)/shard_map/ppermute | solution.py:312
  12.9 0.0 copy-done.5
  12.9 0.0 copy-done.6
  12.9 0.0 copy-done.7
  12.9 0.6 pack.1
  13.5 0.0 collective-permute-done.2.x_ref.refs_3_
  13.5 0.1 collective-permute-start.3
  13.6 1.4 %forward.5.a_ref = bf16[256,512]{1,0:T(8,128)(2,1)S(1)} custom-call(bf16[256,256]{1,0:T(8,128)(2,1)S(1)} %collective-permute-done.2.x_ref.refs_3_, bf16[256,2048]{1,0:T(8,128)(2,1)S(1)} %get-tuple-element.43.refs_0_, bf16[256,2048]{1,0:T(8,128)(2,1)S(1)} %get-tuple-element.44.refs_1_, bf16[2048,256]{1,0:T(8,128)(2,1)S(1)} %get-tuple-element.45.refs_2_, ...), custom_call_target="tpu_custom_call" | custom-call | tf_op jit(solution)/shard_map/forward/pallas_call | solution.py:34
  14.9 1.0 %collective-permute-start.4 = (bf16[256,512]{1,0:T(8,128)(2,1)S(1)}, bf16[256,512]{1,0:T(8,128)(2,1)S(1)}, u32[]{:S(2)}, u32[]{:S(2)}) collective-permute-start(bf16[256,512]{1,0:T(8,128)(2,1)S(1)} %forward.5.a_ref), channel_id=1, source_target_pairs={{0,2},{2,0},{1,3},{3,1},{4,6},{6,4},{5,7},{7,5},{8,10},{10,8},{9,1... | collective-permute-start | bytes 786440 | tf_op jit(solution)/shard_map/ppermute | solution.py:312
  15.9 0.7 %collective-permute-start.6 = (bf16[272,256]{1,0:T(8,128)(2,1)S(1)}, bf16[272,256]{1,0:T(8,128)(2,1)S(1)}, u32[]{:S(2)}, u32[]{:S(2)}) collective-permute-start(bf16[272,256]{1,0:T(8,128)(2,1)S(1)} %get-tuple-element.41.refs_0_), channel_id=1, source_target_pairs={{0,4},{4,0},{8,12},{12,8},{1,5},{5,1},{9,13},{13,9},{2,6},{6,2},{1... | collective-permute-start | bytes 417800 | tf_op jit(solution)/shard_map/ppermute | solution.py:309
  16.6 0.0 collective-permute-start.8
  16.6 4.0 %collective-permute-done.b_ref = bf16[256,512]{1,0:T(8,128)(2,1)S(1)} collective-permute-done((bf16[256,512]{1,0:T(8,128)(2,1)S(1)}, bf16[256,512]{1,0:T(8,128)(2,1)S(1)}, u32[]{:S(2)}, u32[]{:S(2)}) %collective-permute-start) | collective-permute-done | bytes 262176 | tf_op jit(solution)/shard_map/ppermute | solution.py:312
  20.6 0.0 collective-permute-start.7
  20.6 0.1 both.2.refs_0_
  20.7 0.7 %collective-permute-done.3.x_ref.refs_2_ = bf16[272,256]{1,0:T(8,128)(2,1)S(1)} collective-permute-done((bf16[272,256]{1,0:T(8,128)(2,1)S(1)}, bf16[272,256]{1,0:T(8,128)(2,1)S(1)}, u32[]{:S(2)}, u32[]{:S(2)}) %collective-permute-start.3) | collective-permute-done | bytes 139296 | tf_op jit(solution)/shard_map/ppermute | solution.py:309
  21.4 0.0 collective-permute-start.1
  21.4 1.4 %forward.4.refs_2_ = bf16[256,512]{1,0:T(8,128)(2,1)S(1)} custom-call(bf16[272,256]{1,0:T(8,128)(2,1)S(1)} %collective-permute-done.3.x_ref.refs_2_, bf16[256,2048]{1,0:T(8,128)(2,1)S(1)} %get-tuple-element.43.refs_0_, bf16[256,2048]{1,0:T(8,128)(2,1)S(1)} %get-tuple-element.44.refs_1_, bf16[2048,256]{1,0:T(8,128)(2,1)S(1)} %get-tuple-element.45.refs_2_, ...), custom_call_target="tpu_custom_call" | custom-call | tf_op jit(solution)/shard_map/forward/pallas_call | solution.py:34
  22.8 3.4 %collective-permute-done.7.refs_4_ = bf16[16,256]{1,0:T(8,128)(2,1)S(1)} collective-permute-done((bf16[16,256]{1,0:T(8,128)(2,1)S(1)}, bf16[16,256]{1,0:T(8,128)(2,1)S(1)}, u32[]{:S(2)}, u32[]{:S(2)}) %collective-permute-start.7) | collective-permute-done | bytes 8224 | tf_op jit(solution)/shard_map/ppermute | solution.py:309
  26.2 1.5 %collective-permute-start.5 = (bf16[256,512]{1,0:T(8,128)(2,1)S(1)}, bf16[256,512]{1,0:T(8,128)(2,1)S(1)}, u32[]{:S(2)}, u32[]{:S(2)}) collective-permute-start(bf16[256,512]{1,0:T(8,128)(2,1)S(1)} %forward.4.refs_2_), channel_id=1, source_target_pairs={{0,2},{2,0},{1,3},{3,1},{4,6},{6,4},{5,7},{7,5},{8,10},{10,8},{9,1... | collective-permute-start | bytes 786440 | tf_op jit(solution)/shard_map/ppermute | solution.py:312
  27.7 0.0 collective-permute-done.6.refs_1_
  27.7 0.0 collective-permute-start.12
  27.7 0.0 collective-permute-done.8.refs_5_
  27.7 0.5 collective-permute-start.9
  28.2 0.7 %collective-permute-done.12.refs_9_ = bf16[16,256]{1,0:T(8,128)(2,1)S(1)} collective-permute-done((bf16[16,256]{1,0:T(8,128)(2,1)S(1)}, bf16[16,256]{1,0:T(8,128)(2,1)S(1)}, u32[]{:S(2)}, u32[]{:S(2)}) %collective-permute-start.12) | collective-permute-done | bytes 8224 | tf_op jit(solution)/shard_map/ppermute | solution.py:312
  28.9 0.2 collective-permute-start.10
  29.0 0.0 collective-permute-done.4.b_ref
  29.0 0.3 collective-permute-start.11
  29.4 0.1 both.3.refs_3_
  29.4 1.0 %collective-permute-done.11.refs_8_ = bf16[256,256]{1,0:T(8,128)(2,1)S(1)} collective-permute-done((bf16[256,256]{1,0:T(8,128)(2,1)S(1)}, bf16[256,256]{1,0:T(8,128)(2,1)S(1)}, u32[]{:S(2)}, u32[]{:S(2)}) %collective-permute-start.11) | collective-permute-done | bytes 131104 | tf_op jit(solution)/shard_map/ppermute | solution.py:312
  30.4 0.3 collective-permute-start.13
  30.7 0.0 collective-permute-done.9.refs_6_
  30.7 0.2 collective-permute-start.15
  30.9 0.0 collective-permute-done.10.refs_7_
  30.9 0.3 collective-permute-start.16
  31.2 4.0 %arrange.1 = (bf16[1024,256]{1,0:T(8,128)(2,1)S(1)}, bf16[1024,256]{1,0:T(8,128)(2,1)S(1)}, bf16[1024,256]{1,0:T(8,128)(2,1)S(1)}, bf16[1024,256]{1,0:T(8,128)(2...) custom-call(s32[2]{0:T(128)S(1)} %pad_add_fusion.pos_ref, ...), custom_call_target="tpu_custom_call" | custom-call | tf_op jit(solution)/shard_map/arrange/pallas_call | solution.py:34
  35.3 0.0 collective-permute-done.1.refs_1_
  35.3 0.3 collective-permute-start.14
  35.5 0.0 collective-permute-done.5.refs_4_
  35.5 0.3 collective-permute-start.17
  35.9 0.0 collective-permute-done.13.refs_5_
  35.9 0.0 collective-permute-done.15.refs_7_
  35.9 0.0 collective-permute-done.16.refs_8_
  35.9 1.0 %collective-permute-done.14.refs_6_ = bf16[256,512]{1,0:T(8,128)(2,1)S(1)} collective-permute-done((bf16[256,512]{1,0:T(8,128)(2,1)S(1)}, bf16[256,512]{1,0:T(8,128)(2,1)S(1)}, u32[]{:S(2)}, u32[]{:S(2)}) %collective-permute-start.14) | collective-permute-done | bytes 262176 | tf_op jit(solution)/shard_map/ppermute | solution.py:312
  36.9 0.4 collective-permute-done.17.refs_9_
  37.3 5.3 %contrast.1.grads_ref = bf16[1024,512]{1,0:T(8,128)(2,1)S(1)} custom-call(s32[2]{0:T(128)S(1)} %pad_add_fusion.pos_ref, bf16[256,512]{1,0:T(8,128)(2,1)S(1)} %both.2.refs_0_, bf16[256,512]{1,0:T(8,128)(2,1)S(1)} %collective-permute-done.1.refs_1_, bf16[256,512]{1,0:T(8,128)(2,1)S(1)} %forward.4.refs_2_, bf16[256,512]{1,0:T(8,128)(2,1)S(1)} %both.3.refs_3_, ...), custom_call_target="tpu_custom_call" | custom-call | tf_op jit(solution)/shard_map/contrast/pallas_call | solution.py:34
  42.5 0.3 collective-permute-start.18
  42.8 6.1 %mine.1 = (f32[1024,256]{1,0:T(8,128)S(1)}, f32[1024,256]{1,0:T(8,128)S(1)}, f32[1024,256]{1,0:T(8,128)S(1)}, f32[1024,256]{1,0:T(8,128)S(1)}) custom-call(s32[2]{0:T(128)S(1)} %pad_add_fusion.pos_ref, bf16[256,2048]{1,0:T(8,128)(2,1)S(1)} %copy-done, bf16[256,2048]{1,0:T(8,128)(2,1)S(1)} %copy-done.2, bf16[2048,256]{1,0:T(8,128)(2,1)S(1)} %copy-done.1, ...), custom_call_target="tpu_custom_call" | custom-call | flops 4294967296 | tf_op jit(solution)/shard_map/mine/pallas_call | solution.py:34
  48.9 0.0 collective-permute-done.18.grads_ref
  48.9 3.5 %other_state.1 = (f32[256,1024]{1,0:T(8,128)S(1)}, f32[1024,256]{1,0:T(8,128)S(1)}) custom-call(s32[2]{0:T(128)S(1)} %pad_add_fusion.pos_ref, bf16[256,2048]{1,0:T(8,128)(2,1)S(1)} %copy-done, bf16[2048,256]{1,0:T(8,128)(2,1)S(1)} %copy-done.1, bf16[1024,512]{1,0:T(8,128)(2,1)S(1)} %collective-permute-done.18.grads_ref, ...), custom_call_target="tpu_custom_call" | custom-call | flops 2147483648 | tf_op jit(solution)/shard_map/other_state/pallas_call | solution.py:34
  52.4 0.4 collective-permute-start.19
  52.8 0.2 collective-permute-start.20
  53.0 4.7 %other_goal.1 = (f32[256,1024]{1,0:T(8,128)S(1)}, f32[1024,256]{1,0:T(8,128)S(1)}, f32[256,2048]{1,0:T(8,128)}, f32[2048,256]{1,0:T(8,128)}) custom-call(s32[2]{0:T(128)S(1)} %pad_add_fusion.pos_ref, bf16[256,2048]{1,0:T(8,128)(2,1)S(1)} %copy-done.2, bf16[2048,256]{1,0:T(8,128)(2,1)S(1)} %copy-done.3, ...), custom_call_target="tpu_custom_call" | custom-call | flops 2147483648 | tf_op jit(solution)/shard_map/other_goal/pallas_call | solution.py:34
  57.7 0.4 collective-permute-start.21
  58.1 0.2 collective-permute-start.22
  58.3 0.0 collective-permute-done.19.refs_0_
  58.3 0.0 collective-permute-done.20.refs_1_
  58.3 2.6 %finish.2 = (f32[256,2048]{1,0:T(8,128)}, f32[2048,256]{1,0:T(8,128)}, f32[256,2048]{1,0:T(8,128)}, f32[2048,256]{1,0:T(8,128)}) custom-call(s32[2]{0:T(128)S(1)} %pad_add_fusion.pos_ref, f32[256,1024]{1,0:T(8,128)S(1)} %collective-permute-done.19.refs_0_, ...), custom_call_target="tpu_custom_call", output_to_operand_aliasing={{0}: (5, {}), {1}: (6, {})} | custom-call | tf_op jit(solution)/shard_map/finish/pallas_call | solution.py:34
  60.9 0.0 collective-permute-done.21.refs_0_
  60.9 1.0 %collective-permute-done.22.refs_1_ = f32[1024,256]{1,0:T(8,128)S(1)} collective-permute-done((f32[1024,256]{1,0:T(8,128)S(1)}, f32[1024,256]{1,0:T(8,128)S(1)}, u32[]{:S(2)}, u32[]{:S(2)}) %collective-permute-start.22) | collective-permute-done | bytes 1048608 | tf_op jit(solution)/shard_map/ppermute | solution.py:312
  61.9 1.9 %finish.3 = (f32[256,2048]{1,0:T(8,128)}, f32[2048,256]{1,0:T(8,128)}) custom-call(s32[2]{0:T(128)S(1)} %pad_add_fusion.pos_ref, f32[256,1024]{1,0:T(8,128)S(1)} %collective-permute-done.21.refs_0_, f32[1024,256]{1,0:T(8,128)S(1)} %collective-permute-done.22.refs_1_, ...), custom_call_target="tpu_custom_call", output_to_operand_aliasing={{0}: (3, {}), {1}: (4, {})} | custom-call | tf_op jit(solution)/shard_map/finish/pallas_call | solution.py:34
  (12 shorter events, 0.0 us)
Async XLA Ops:
  0.6 12.8 %collective-permute-start.2 = (bf16[256,256]{1,0:T(8,128)(2,1)}, bf16[256,256]{1,0:T(8,128)(2,1)S(1)}, u32[]{:S(2)}, u32[]{:S(2)}) collective-permute-start(bf16[256,256]{1,0:T(8,128)(2,1)} %x_ref.2), channel_id=1, source_target_pairs={{0,12},{4,8},{8,4},{12,0},{1,13},{5,9},{9,5},{13,1},{2,14},{6,10},... | collective-permute-start | bytes 393224 | tf_op jit(solution)/shard_map/ppermute | solution.py:309
  5.8 0.9 %copy-start.4 = (bf16[256,256]{1,0:T(8,128)(2,1)S(1)}, bf16[256,256]{1,0:T(8,128)(2,1)}, u32[]{:S(2)}) copy-start(bf16[256,256]{1,0:T(8,128)(2,1)} %x_ref.2) | copy-start | bytes 393220
  6.7 6.2 %copy-start.5 = (s32[256,1]{0,1:T(1,128)S(1)}, s32[256,1]{0,1:T(1,128)}, u32[]{:S(2)}) copy-start(s32[256,1]{0,1:T(1,128)} %param.9) | copy-start | bytes 3076
  6.7 6.2 %copy-start.6 = (s32[256]{0:T(256)S(1)}, s32[256]{0:T(256)}, u32[]{:S(2)}) copy-start(s32[256]{0:T(256)} %param.10) | copy-start | bytes 3076
  6.7 6.2 %copy-start.7 = (s32[256]{0:T(256)S(1)}, s32[256]{0:T(256)}, u32[]{:S(2)}) copy-start(s32[256]{0:T(256)} %param.11) | copy-start | bytes 3076
  11.3 9.3 %collective-permute-start = (bf16[256,512]{1,0:T(8,128)(2,1)S(1)}, bf16[256,512]{1,0:T(8,128)(2,1)S(1)}, u32[]{:S(2)}, u32[]{:S(2)}) collective-permute-start(bf16[256,512]{1,0:T(8,128)(2,1)S(1)} %get-tuple-element.38.a_ref), channel_id=1, source_target_pairs={{0,2},{2,0},{1,3},{3,1},{4,6},{6,4},{5,7},{7,5},{8,10},{10,8},{9,1... | collective-permute-start | bytes 786440 | tf_op jit(solution)/shard_map/ppermute | solution.py:312
  13.5 7.9 %collective-permute-start.3 = (bf16[272,256]{1,0:T(8,128)(2,1)S(1)}, bf16[272,256]{1,0:T(8,128)(2,1)S(1)}, u32[]{:S(2)}, u32[]{:S(2)}) collective-permute-start(bf16[272,256]{1,0:T(8,128)(2,1)S(1)} %get-tuple-element.41.refs_0_), channel_id=1, source_target_pairs={{0,8},{4,12},{8,0},{12,4},{1,9},{5,13},{9,1},{13,5},{2,10},{6,14},... | collective-permute-start | bytes 417800 | tf_op jit(solution)/shard_map/ppermute | solution.py:309
  14.9 14.1 %collective-permute-start.4 = (bf16[256,512]{1,0:T(8,128)(2,1)S(1)}, bf16[256,512]{1,0:T(8,128)(2,1)S(1)}, u32[]{:S(2)}, u32[]{:S(2)}) collective-permute-start(bf16[256,512]{1,0:T(8,128)(2,1)S(1)} %forward.5.a_ref), channel_id=1, source_target_pairs={{0,2},{2,0},{1,3},{3,1},{4,6},{6,4},{5,7},{7,5},{8,10},{10,8},{9,1... | collective-permute-start | bytes 786440 | tf_op jit(solution)/shard_map/ppermute | solution.py:312
  15.9 11.8 %collective-permute-start.6 = (bf16[272,256]{1,0:T(8,128)(2,1)S(1)}, bf16[272,256]{1,0:T(8,128)(2,1)S(1)}, u32[]{:S(2)}, u32[]{:S(2)}) collective-permute-start(bf16[272,256]{1,0:T(8,128)(2,1)S(1)} %get-tuple-element.41.refs_0_), channel_id=1, source_target_pairs={{0,4},{4,0},{8,12},{12,8},{1,5},{5,1},{9,13},{13,9},{2,6},{6,2},{1... | collective-permute-start | bytes 417800 | tf_op jit(solution)/shard_map/ppermute | solution.py:309
  16.6 11.1 %collective-permute-start.8 = (bf16[272,256]{1,0:T(8,128)(2,1)S(1)}, bf16[272,256]{1,0:T(8,128)(2,1)S(1)}, u32[]{:S(2)}, u32[]{:S(2)}) collective-permute-start(bf16[272,256]{1,0:T(8,128)(2,1)S(1)} %get-tuple-element.41.refs_0_), channel_id=1, source_target_pairs={{0,1},{1,0},{2,3},{3,2},{4,5},{5,4},{6,7},{7,6},{8,9},{9,8},{10,11... | collective-permute-start | bytes 417800 | tf_op jit(solution)/shard_map/ppermute | solution.py:312
  20.6 5.6 %collective-permute-start.7 = (bf16[16,256]{1,0:T(8,128)(2,1)S(1)}, bf16[16,256]{1,0:T(8,128)(2,1)S(1)}, u32[]{:S(2)}, u32[]{:S(2)}) collective-permute-start(bf16[16,256]{1,0:T(8,128)(2,1)S(1)} %get-tuple-element.48), channel_id=1, source_target_pairs={{0,12},{4,8},{8,4},{12,0},{1,13},{5,9},{9,5},{13,1},{2,14},{6,10},... | collective-permute-start | bytes 24584 | tf_op jit(solution)/shard_map/ppermute | solution.py:309
  21.4 13.9 %collective-permute-start.1 = (bf16[256,512]{1,0:T(8,128)(2,1)S(1)}, bf16[256,512]{1,0:T(8,128)(2,1)S(1)}, u32[]{:S(2)}, u32[]{:S(2)}) collective-permute-start(bf16[256,512]{1,0:T(8,128)(2,1)S(1)} %both.2.refs_0_), channel_id=1, source_target_pairs={{0,4},{4,0},{8,12},{12,8},{1,5},{5,1},{9,13},{13,9},{2,6},{6,2},{1... | collective-permute-start | bytes 786440 | tf_op jit(solution)/shard_map/ppermute | solution.py:309
  26.2 9.4 %collective-permute-start.5 = (bf16[256,512]{1,0:T(8,128)(2,1)S(1)}, bf16[256,512]{1,0:T(8,128)(2,1)S(1)}, u32[]{:S(2)}, u32[]{:S(2)}) collective-permute-start(bf16[256,512]{1,0:T(8,128)(2,1)S(1)} %forward.4.refs_2_), channel_id=1, source_target_pairs={{0,2},{2,0},{1,3},{3,1},{4,6},{6,4},{5,7},{7,5},{8,10},{10,8},{9,1... | collective-permute-start | bytes 786440 | tf_op jit(solution)/shard_map/ppermute | solution.py:312
  27.7 1.2 %collective-permute-start.12 = (bf16[16,256]{1,0:T(8,128)(2,1)S(1)}, bf16[16,256]{1,0:T(8,128)(2,1)S(1)}, u32[]{:S(2)}, u32[]{:S(2)}) collective-permute-start(bf16[16,256]{1,0:T(8,128)(2,1)S(1)} %collective-permute-done.7.refs_4_), channel_id=1, source_target_pairs={{0,1},{1,0},{2,3},{3,2},{4,5},{5,4},{6,7},{7,6},{8,9},{9,8},{10,11... | collective-permute-start | bytes 24584 | tf_op jit(solution)/shard_map/ppermute | solution.py:312
  27.7 3.0 %collective-permute-start.9 = (bf16[272,256]{1,0:T(8,128)(2,1)S(1)}, bf16[272,256]{1,0:T(8,128)(2,1)S(1)}, u32[]{:S(2)}, u32[]{:S(2)}) collective-permute-start(bf16[272,256]{1,0:T(8,128)(2,1)S(1)} %collective-permute-done.6.refs_1_), channel_id=1, source_target_pairs={{0,1},{1,0},{2,3},{3,2},{4,5},{5,4},{6,7},{7,6},{8,9},{9,8},{10,11... | collective-permute-start | bytes 417800 | tf_op jit(solution)/shard_map/ppermute | solution.py:312
  28.9 2.1 %collective-permute-start.10 = (bf16[272,256]{1,0:T(8,128)(2,1)S(1)}, bf16[272,256]{1,0:T(8,128)(2,1)S(1)}, u32[]{:S(2)}, u32[]{:S(2)}) collective-permute-start(bf16[272,256]{1,0:T(8,128)(2,1)S(1)} %collective-permute-done.3.x_ref.refs_2_), channel_id=1, source_target_pairs={{0,1},{1,0},{2,3},{3,2},{4,5},{5,4},{6,7},{7,6},{8,9},{9,8},{10,11... | collective-permute-start | bytes 417800 | tf_op jit(solution)/shard_map/ppermute | solution.py:312
  29.0 1.4 %collective-permute-start.11 = (bf16[256,256]{1,0:T(8,128)(2,1)S(1)}, bf16[256,256]{1,0:T(8,128)(2,1)S(1)}, u32[]{:S(2)}, u32[]{:S(2)}) collective-permute-start(bf16[256,256]{1,0:T(8,128)(2,1)S(1)} %collective-permute-done.2.x_ref.refs_3_), channel_id=1, source_target_pairs={{0,1},{1,0},{2,3},{3,2},{4,5},{5,4},{6,7},{7,6},{8,9},{9,8},{10,11... | collective-permute-start | bytes 393224 | tf_op jit(solution)/shard_map/ppermute | solution.py:312
  30.4 5.5 %collective-permute-start.13 = (bf16[256,512]{1,0:T(8,128)(2,1)S(1)}, bf16[256,512]{1,0:T(8,128)(2,1)S(1)}, u32[]{:S(2)}, u32[]{:S(2)}) collective-permute-start(bf16[256,512]{1,0:T(8,128)(2,1)S(1)} %both.2.refs_0_), channel_id=1, source_target_pairs={{0,1},{1,0},{2,3},{3,2},{4,5},{5,4},{6,7},{7,6},{8,9},{9,8},{10,11... | collective-permute-start | bytes 786440 | tf_op jit(solution)/shard_map/ppermute | solution.py:312
  30.7 5.1 %collective-permute-start.15 = (bf16[256,512]{1,0:T(8,128)(2,1)S(1)}, bf16[256,512]{1,0:T(8,128)(2,1)S(1)}, u32[]{:S(2)}, u32[]{:S(2)}) collective-permute-start(bf16[256,512]{1,0:T(8,128)(2,1)S(1)} %forward.4.refs_2_), channel_id=1, source_target_pairs={{0,1},{1,0},{2,3},{3,2},{4,5},{5,4},{6,7},{7,6},{8,9},{9,8},{10,11... | collective-permute-start | bytes 786440 | tf_op jit(solution)/shard_map/ppermute | solution.py:312
  30.9 4.9 %collective-permute-start.16 = (bf16[256,512]{1,0:T(8,128)(2,1)S(1)}, bf16[256,512]{1,0:T(8,128)(2,1)S(1)}, u32[]{:S(2)}, u32[]{:S(2)}) collective-permute-start(bf16[256,512]{1,0:T(8,128)(2,1)S(1)} %both.3.refs_3_), channel_id=1, source_target_pairs={{0,1},{1,0},{2,3},{3,2},{4,5},{5,4},{6,7},{7,6},{8,9},{9,8},{10,11... | collective-permute-start | bytes 786440 | tf_op jit(solution)/shard_map/ppermute | solution.py:312
  35.3 1.6 %collective-permute-start.14 = (bf16[256,512]{1,0:T(8,128)(2,1)S(1)}, bf16[256,512]{1,0:T(8,128)(2,1)S(1)}, u32[]{:S(2)}, u32[]{:S(2)}) collective-permute-start(bf16[256,512]{1,0:T(8,128)(2,1)S(1)} %collective-permute-done.1.refs_1_), channel_id=1, source_target_pairs={{0,1},{1,0},{2,3},{3,2},{4,5},{5,4},{6,7},{7,6},{8,9},{9,8},{10,11... | collective-permute-start | bytes 786440 | tf_op jit(solution)/shard_map/ppermute | solution.py:312
  35.5 1.7 %collective-permute-start.17 = (bf16[256,512]{1,0:T(8,128)(2,1)S(1)}, bf16[256,512]{1,0:T(8,128)(2,1)S(1)}, u32[]{:S(2)}, u32[]{:S(2)}) collective-permute-start(bf16[256,512]{1,0:T(8,128)(2,1)S(1)} %collective-permute-done.5.refs_4_), channel_id=1, source_target_pairs={{0,1},{1,0},{2,3},{3,2},{4,5},{5,4},{6,7},{7,6},{8,9},{9,8},{10,11... | collective-permute-start | bytes 786440 | tf_op jit(solution)/shard_map/ppermute | solution.py:312
  37.3 5.6 %copy-start = (bf16[256,2048]{1,0:T(8,128)(2,1)S(1)}, bf16[256,2048]{1,0:T(8,128)(2,1)}, u32[]{:S(2)}) copy-start(bf16[256,2048]{1,0:T(8,128)(2,1)} %first.2) | copy-start | bytes 3145732
  37.3 5.6 %copy-start.1 = (bf16[2048,256]{1,0:T(8,128)(2,1)S(1)}, bf16[2048,256]{1,0:T(8,128)(2,1)}, u32[]{:S(2)}) copy-start(bf16[2048,256]{1,0:T(8,128)(2,1)} %second.2) | copy-start | bytes 3145732
  37.3 5.6 %copy-start.2 = (bf16[256,2048]{1,0:T(8,128)(2,1)S(1)}, bf16[256,2048]{1,0:T(8,128)(2,1)}, u32[]{:S(2)}) copy-start(bf16[256,2048]{1,0:T(8,128)(2,1)} %first.3) | copy-start | bytes 3145732
  37.3 5.6 %copy-start.3 = (bf16[2048,256]{1,0:T(8,128)(2,1)S(1)}, bf16[2048,256]{1,0:T(8,128)(2,1)}, u32[]{:S(2)}) copy-start(bf16[2048,256]{1,0:T(8,128)(2,1)} %second.3) | copy-start | bytes 3145732
  42.5 6.4 %collective-permute-start.18 = (bf16[1024,512]{1,0:T(8,128)(2,1)S(1)}, bf16[1024,512]{1,0:T(8,128)(2,1)S(1)}, u32[]{:S(2)}, u32[]{:S(2)}) collective-permute-start(bf16[1024,512]{1,0:T(8,128)(2,1)S(1)} %contrast.1.grads_ref), channel_id=1, source_target_pairs={{0,1},{1,0},{2,3},{3,2},{4,5},{5,4},{6,7},{7,6},{8,9},{9,8},{10,11... | collective-permute-start | bytes 3145736 | tf_op jit(solution)/shard_map/ppermute | solution.py:312
  52.4 5.9 %collective-permute-start.19 = (f32[256,1024]{1,0:T(8,128)S(1)}, f32[256,1024]{1,0:T(8,128)S(1)}, u32[]{:S(2)}, u32[]{:S(2)}) collective-permute-start(f32[256,1024]{1,0:T(8,128)S(1)} %get-tuple-element.57.refs_0_), channel_id=1, source_target_pairs={{0,1},{1,0},{2,3},{3,2},{4,5},{5,4},{6,7},{7,6},{8,9},{9,8},{10,11... | collective-permute-start | bytes 3145736 | tf_op jit(solution)/shard_map/ppermute | solution.py:312
  52.8 5.5 %collective-permute-start.20 = (f32[1024,256]{1,0:T(8,128)S(1)}, f32[1024,256]{1,0:T(8,128)S(1)}, u32[]{:S(2)}, u32[]{:S(2)}) collective-permute-start(f32[1024,256]{1,0:T(8,128)S(1)} %get-tuple-element.58.refs_1_), channel_id=1, source_target_pairs={{0,1},{1,0},{2,3},{3,2},{4,5},{5,4},{6,7},{7,6},{8,9},{9,8},{10,11... | collective-permute-start | bytes 3145736 | tf_op jit(solution)/shard_map/ppermute | solution.py:312
  57.7 3.2 %collective-permute-start.21 = (f32[256,1024]{1,0:T(8,128)S(1)}, f32[256,1024]{1,0:T(8,128)S(1)}, u32[]{:S(2)}, u32[]{:S(2)}) collective-permute-start(f32[256,1024]{1,0:T(8,128)S(1)} %get-tuple-element.62.refs_2_), channel_id=1, source_target_pairs={{0,1},{1,0},{2,3},{3,2},{4,5},{5,4},{6,7},{7,6},{8,9},{9,8},{10,11... | collective-permute-start | bytes 3145736 | tf_op jit(solution)/shard_map/ppermute | solution.py:312
  58.1 3.9 %collective-permute-start.22 = (f32[1024,256]{1,0:T(8,128)S(1)}, f32[1024,256]{1,0:T(8,128)S(1)}, u32[]{:S(2)}, u32[]{:S(2)}) collective-permute-start(f32[1024,256]{1,0:T(8,128)S(1)} %get-tuple-element.63.refs_3_), channel_id=1, source_target_pairs={{0,1},{1,0},{2,3},{3,2},{4,5},{5,4},{6,7},{7,6},{8,9},{9,8},{10,11... | collective-permute-start | bytes 3145736 | tf_op jit(solution)/shard_map/ppermute | solution.py:312

commit v8 on v7

--- a/solution.py
+++ b/solution.py
@@ -136,8 +136,8 @@
 
 def arrange_kernel(n_blk, n_rep, slab, pos_ref, *refs):
     n = n_blk + 1
-    mine, other = refs[:n], refs[n : 2 * n]
-    rows_mine, rows_other, goals_mine, goals_other, pick_ref, ep_ref, both_sides, pick_other, meta = refs[2 * n :]
+    mine, other = refs[:n], refs[n : 2 * n - 1]
+    rows_mine, rows_other, goals_ref, pick_ref, ep_ref, both_sides, meta = refs[2 * n - 1 :]
     half = rows_mine.shape[0]
     rows = 2 * half
     batch = n_blk * slab
@@ -148,22 +148,21 @@
             both_sides[pl.ds(i * half + off, slab), :] = value
 
         place_blocks(pos_ref, blocks[:n_blk], put, n_blk, n_rep, slab)
-        tables = [block.at[n_rep * slab :] for block in blocks[: n_blk - 1]] + [blocks[n_blk]]
-        for k, table in enumerate(tables):
-            at = jnp.bitwise_xor(pos_ref[0], k)
-            for r in range(n_rep):
-                off = pl.multiple_of((r * n_blk + at) * slab, slab)
-                meta[i, :, pl.ds(off, slab)] = table[:, r * slab : (r + 1) * slab].astype(F32)
-    ep_ref[...] = meta[0, 2:3, :]
-    for i, (pick, goals) in enumerate(((pick_ref, goals_mine), (pick_other, goals_other))):
+    tables = [block.at[n_rep * slab :] for block in mine[: n_blk - 1]] + [mine[n_blk]]
+    for k, table in enumerate(tables):
+        at = jnp.bitwise_xor(pos_ref[0], k)
         for r in range(n_rep):
-            own = slice(r * batch, (r + 1) * batch)
-            goal = column(meta[i, 0:1, own] * 256.0 + meta[i, 1:2, own]).astype(jnp.int32) + pos_ref[1] * half
-            goal = jnp.where(goal >= rows, goal - rows, goal)
-            pick[own, :] = jnp.where(
-                goal == lax.broadcasted_iota(jnp.int32, (batch, rows), 1), 1.0, 0.0
-            ).astype(BF)
-        goals[...] = dot(pick[...], both_sides[...]).astype(BF)
+            off = pl.multiple_of((r * n_blk + at) * slab, slab)
+            meta[:, pl.ds(off, slab)] = table[:, r * slab : (r + 1) * slab].astype(F32)
+    ep_ref[...] = meta[2:3, :]
+    for r in range(n_rep):
+        own = slice(r * batch, (r + 1) * batch)
+        goal = column(meta[0:1, own] * 256.0 + meta[1:2, own]).astype(jnp.int32) + pos_ref[1] * half
+        goal = jnp.where(goal >= rows, goal - rows, goal)
+        pick_ref[own, :] = jnp.where(
+            goal == lax.broadcasted_iota(jnp.int32, (batch, rows), 1), 1.0, 0.0
+        ).astype(BF)
+    goals_ref[...] = dot(pick_ref[...], both_sides[...]).astype(BF)
 
 
 def contrast_kernel(n_blk, n_rep, slab, scale, pos_ref, *refs):
@@ -234,23 +233,30 @@
 
 
 def other_kernel(k, n_put, pos_ref, first, second, grads_ref, rows_ref, sum_second, sum_first, *refs):
-    done, (gf_ref, gs_ref), outs, (active, back), sems = (
+    done, (gf_ref, gs_ref), outs, (active, back), rest = (
         refs[:n_put],
         refs[n_put : n_put + 2],
         refs[n_put + 2 : 2 * n_put + 2],
         refs[2 * n_put + 2 : 2 * n_put + 4],
         refs[2 * n_put + 4 :],
     )
-    copies = [put_half(pos_ref[1], x, o, sems[0].at[i]) for i, (x, o) in enumerate(zip(done, outs))]
-    for c in copies:
-        c.start()
+    copies = put_halves([pos_ref[1]] * n_put, done, outs, rest)
     quarter = active.shape[0]
     at = pl.multiple_of(pos_ref[1] * quarter, quarter)
     grad_second, grad_first = rows_grads(at, first, second, grads_ref, k, rows_ref, active, back)
-    gs_ref[...] = sum_second[...] + grad_second
-    gf_ref[...] = (sum_first[...] + grad_first).T
+    gs_ref[...] = (sum_second[...] + grad_second).astype(BF)
+    gf_ref[...] = (sum_first[...] + grad_first).astype(BF).T
     for c in copies:
         c.wait()
+
+
+def put_halves(sides, halves, outs, rest):
+    copies = []
+    for i, (side, half, out) in enumerate(zip(sides, halves, outs)):
+        rest[i][...] = half[...].astype(F32)
+        copies.append(put_half(side, rest[i], out, rest[-1].at[i]))
+        copies[-1].start()
+    return copies
 
 
 def put_half(side, half, out, sem):
@@ -263,16 +269,9 @@
 
 
 def finish_kernel(old, new, pos_ref, *refs):
-    halves = refs[: old + new]
-    outs = refs[2 * old + new : 2 * (old + new) + old]
-    sems = refs[-1]
-    copies = [
-        put_half(1 - pos_ref[1] if i < old else pos_ref[1], x, o, sems.at[i])
-        for i, (x, o) in enumerate(zip(halves, outs))
-    ]
-    for c in copies:
-        c.start()
-    for c in copies:
+    n = old + new
+    sides = [1 - pos_ref[1]] * old + [pos_ref[1]] * new
+    for c in put_halves(sides, refs[:n], refs[n + old : 2 * n + old], refs[2 * n + old :]):
         c.wait()
 
 
@@ -284,7 +283,7 @@
         "finish",
         [(w.shape, w.dtype) for w in wholes] + shapes,
         (*halves, *wholes),
-        [pltpu.SemaphoreType.DMA((n,))],
+        [*(pltpu.VMEM(x.shape, F32) for x in halves), pltpu.SemaphoreType.DMA((n,))],
         pos=pos,
         hbm=range(n, n + old),
         hbm_out=range(n),
@@ -329,7 +328,6 @@
     )
     got[0], got[1] = pack, across(pack, 1)
     got[2] = across(after(pack, got[3]), 2)
-    got[4] = across(after(table, got[3]), 3)
     part3 = forward(got[3], held, rows_dev)
     there3 = swap(part3, "rep")
 
@@ -337,18 +335,18 @@
     sums[1] = across(sums[0], 1)
     part2 = forward(after(got[2], sums[0]), held, rows_dev)
     there2 = swap(part2, "rep")
+    got[4] = across(after(table, part2), 3)
     sums[3] = both(part3, there3)
 
     side = ((rows_all // 2, width), BF)
-    mine, other, goals_mine, goals_other, pick, episodes = kernel(
+    mine, other, goals_mine, pick, episodes = kernel(
         functools.partial(arrange_kernel, n_blk, n_rep, slab),
         "arrange",
-        [side, side, side, side, ((rows_all // 2, rows_all), BF), ((1, rows_all // 2), F32)],
-        (*(got[k] for k in range(n_blk + 1)), *(swap(got[k], "sub") for k in range(n_blk + 1))),
+        [side, side, side, ((rows_all // 2, rows_all), BF), ((1, rows_all // 2), F32)],
+        (*(got[k] for k in range(n_blk + 1)), *(swap(got[k], "sub") for k in range(n_blk))),
         [
             pltpu.VMEM((rows_all, width), BF),
-            pltpu.VMEM((rows_all // 2, rows_all), BF),
-            pltpu.VMEM((2, 16, rows_all // 2), F32),
+            pltpu.VMEM((16, rows_all // 2), F32),
         ],
         pos=pos,
     )
@@ -362,6 +360,7 @@
         pos=pos,
     )
     grads_other = swap(grads_mine, "sub")
+    goals_other = swap(goals_mine, "sub")
 
     sf, gf, ss, gs = weights
     work = [pltpu.VMEM((quarter, rows_all // 2), BF), pltpu.VMEM((quarter, rows_all // 2), BF)]
@@ -375,7 +374,7 @@
         pos=pos,
         flops=2 * flops,
     )
-    halves = [((width, quarter), F32), ((quarter, emb), F32)]
+    halves = [((width, quarter), BF), ((quarter, emb), BF)]
     wholes = [((width, hid), F32), ((hid, emb), F32)]
     state_halves = kernel(
         functools.partial(other_kernel, 0, 0),
@@ -392,7 +391,7 @@
         "other_goal",
         halves + wholes,
         (gf, gs, grads_other, goals_other, sums_g2, sums_g1, *state_halves),
-        work + [pltpu.SemaphoreType.DMA((2,))],
+        work + [*(pltpu.VMEM(shape, F32) for shape, _ in halves), pltpu.SemaphoreType.DMA((2,))],
         pos=pos,
         flops=flops,
         hbm_out=(2, 3),

time: 64.1 us -> 62.2 us (0.970)
  waiting for transfers between devices: 12.2 us -> 8.75 us
  starting transfers between devices: 13.7 us -> 16.1 us
  Pallas kernels: 36.1 us -> 35.2 us
    ppermute x5, starting transfers between devices: 5.86 us -> 9.66 us  [across(): return lax.ppermute(x, 'blk', [(i, i ^ k) for i in range(n_blk)])]
    ppermute x18, waiting for transfers between devices: 8.1 us -> 5.18 us  [swap(): return lax.ppermute(x, axis, [(0, 1), (1, 0)])]
    ppermute x18, starting transfers between devices: 7.87 us -> 6.46 us  [swap(): return lax.ppermute(x, axis, [(0, 1), (1, 0)])]
    pallas_call x13, Pallas kernels: 36.1 us -> 35.2 us  [kernel(): pl.pallas_call(body, in_specs=specs, out_specs=[HBM if i in hbm_out else...]
  transfers between devices with their start and end apart: 23 -> 23, of which waited for: 8 -> 6; matrix products, arithmetic and copies ran while one was open for 0% -> 0% of each run, Pallas kernels for 40% -> 45%
where the time goes in v8:
time: 62.2 us; the launch traced here: 62 us
  Pallas kernels  35.2 us (57%)
  starting transfers between devices  16.1 us (26%)
  waiting for transfers between devices  8.75 us (14%)
  between operations  0.96 us (2%)
  local copies, waits for them, and re-layouts  0.93 us (1%)
    pallas_call x13, Pallas kernels, kernel(): pl.pallas_call(body, in_specs=specs, out_specs=[HBM if i in hbm_out else...  35.2 us
    ppermute x5, starting transfers between devices, across(): return lax.ppermute(x, 'blk', [(i, i ^ k) for i in range(n_blk)])  9.66 us
    ppermute x18, starting transfers between devices, swap(): return lax.ppermute(x, axis, [(0, 1), (1, 0)])  6.46 us
    ppermute x18, waiting for transfers between devices, swap(): return lax.ppermute(x, axis, [(0, 1), (1, 0)])  5.18 us
    ppermute x5, waiting for transfers between devices, across(): return lax.ppermute(x, 'blk', [(i, i ^ k) for i in range(n_blk)])  3.56 us
  transfers between devices with their start and end apart: 23, of which 6 were waited for; matrix products, arithmetic and copies ran while one was open for 0% of the time, Pallas kernels for 45%

profile of v8, /device:TPU:0, one launch (start us, length us, event | category | flops | bytes accessed | tf_op | source)
XLA Modules:
  0.0 62.0 jit_solution(4183297867392057306)
XLA Ops:
  0.6 5.1 %collective-permute-start.2 = (bf16[256,256]{1,0:T(8,128)(2,1)}, bf16[256,256]{1,0:T(8,128)(2,1)S(1)}, u32[]{:S(2)}, u32[]{:S(2)}) collective-permute-start(bf16[256,256]{1,0:T(8,128)(2,1)} %x_ref.2), channel_id=1, source_target_pairs={{0,12},{4,8},{8,4},{12,0},{1,13},{5,9},{9,5},{13,1},{2,14},{6,10},... | collective-permute-start | bytes 393224 | tf_op jit(solution)/shard_map/ppermute | solution.py:308
  5.7 0.1 pad_add_fusion.pos_ref
  5.8 0.9 %copy-done.4 = bf16[256,256]{1,0:T(8,128)(2,1)S(1)} copy-done((bf16[256,256]{1,0:T(8,128)(2,1)S(1)}, bf16[256,256]{1,0:T(8,128)(2,1)}, u32[]{:S(2)}) %copy-start.4) | copy-done | bytes 131096
  6.7 4.6 %forward.3 = (bf16[256,512]{1,0:T(8,128)(2,1)S(1)}, bf16[256,2048]{1,0:T(8,128)(2,1)S(1)}, bf16[256,2048]{1,0:T(8,128)(2,1)S(1)}, bf16[2048,256]{1,0:T(8,128)(2,1)S(1)}, bf16[2048,256]{1,0:T(8,128)(2,1)S(1)}) custom-call(s32[2]{0:T(128)S(1)} %pad_add_fusion.pos_ref, bf16[256,256]{1,0:T(8,128)(2,1)S(1)} %copy-done.4, bf16[256,2048]{1,0:T(8,128)(2,1)} %first.2, ...), custom_call_target="tpu_custom_call" | custom-call | tf_op jit(solution)/shard_map/forward/pallas_call | solution.py:34
  11.3 1.6 %collective-permute-start = (bf16[256,512]{1,0:T(8,128)(2,1)S(1)}, bf16[256,512]{1,0:T(8,128)(2,1)S(1)}, u32[]{:S(2)}, u32[]{:S(2)}) collective-permute-start(bf16[256,512]{1,0:T(8,128)(2,1)S(1)} %get-tuple-element.37.a_ref), channel_id=1, source_target_pairs={{0,2},{2,0},{1,3},{3,1},{4,6},{6,4},{5,7},{7,5},{8,10},{10,8},{9,1... | collective-permute-start | bytes 786440 | tf_op jit(solution)/shard_map/ppermute | solution.py:311
  12.9 0.0 copy-done.5
  12.9 0.0 copy-done.6
  12.9 0.6 pack.1
  13.5 0.0 collective-permute-done.2.x_ref.refs_3_
  13.5 0.1 collective-permute-start.3
  13.6 0.8 %collective-permute-start.6 = (bf16[272,256]{1,0:T(8,128)(2,1)S(1)}, bf16[272,256]{1,0:T(8,128)(2,1)S(1)}, u32[]{:S(2)}, u32[]{:S(2)}) collective-permute-start(bf16[272,256]{1,0:T(8,128)(2,1)S(1)} %get-tuple-element.40.refs_0_), channel_id=1, source_target_pairs={{0,4},{4,0},{8,12},{12,8},{1,5},{5,1},{9,13},{13,9},{2,6},{6,2},{1... | collective-permute-start | bytes 417800 | tf_op jit(solution)/shard_map/ppermute | solution.py:308
  14.3 0.0 collective-permute-start.8
  14.3 1.4 %forward.5.a_ref = bf16[256,512]{1,0:T(8,128)(2,1)S(1)} custom-call(bf16[256,256]{1,0:T(8,128)(2,1)S(1)} %collective-permute-done.2.x_ref.refs_3_, bf16[256,2048]{1,0:T(8,128)(2,1)S(1)} %get-tuple-element.42.refs_0_, bf16[256,2048]{1,0:T(8,128)(2,1)S(1)} %get-tuple-element.43.refs_1_, bf16[2048,256]{1,0:T(8,128)(2,1)S(1)} %get-tuple-element.44.refs_2_, ...), custom_call_target="tpu_custom_call" | custom-call | tf_op jit(solution)/shard_map/forward/pallas_call | solution.py:34
  15.7 0.9 %collective-permute-start.4 = (bf16[256,512]{1,0:T(8,128)(2,1)S(1)}, bf16[256,512]{1,0:T(8,128)(2,1)S(1)}, u32[]{:S(2)}, u32[]{:S(2)}) collective-permute-start(bf16[256,512]{1,0:T(8,128)(2,1)S(1)} %forward.5.a_ref), channel_id=1, source_target_pairs={{0,2},{2,0},{1,3},{3,1},{4,6},{6,4},{5,7},{7,5},{8,10},{10,8},{9,1... | collective-permute-start | bytes 786440 | tf_op jit(solution)/shard_map/ppermute | solution.py:311
  16.6 2.8 %collective-permute-done.b_ref = bf16[256,512]{1,0:T(8,128)(2,1)S(1)} collective-permute-done((bf16[256,512]{1,0:T(8,128)(2,1)S(1)}, bf16[256,512]{1,0:T(8,128)(2,1)S(1)}, u32[]{:S(2)}, u32[]{:S(2)}) %collective-permute-start) | collective-permute-done | bytes 262176 | tf_op jit(solution)/shard_map/ppermute | solution.py:311
  19.4 0.0 collective-permute-start.11
  19.4 0.1 both.2.refs_0_
  19.4 1.9 %collective-permute-done.3.x_ref.refs_2_ = bf16[272,256]{1,0:T(8,128)(2,1)S(1)} collective-permute-done((bf16[272,256]{1,0:T(8,128)(2,1)S(1)}, bf16[272,256]{1,0:T(8,128)(2,1)S(1)}, u32[]{:S(2)}, u32[]{:S(2)}) %collective-permute-start.3) | collective-permute-done | bytes 139296 | tf_op jit(solution)/shard_map/ppermute | solution.py:308
  21.3 0.0 collective-permute-start.1
  21.3 1.4 %forward.4.refs_2_ = bf16[256,512]{1,0:T(8,128)(2,1)S(1)} custom-call(bf16[272,256]{1,0:T(8,128)(2,1)S(1)} %collective-permute-done.3.x_ref.refs_2_, bf16[256,2048]{1,0:T(8,128)(2,1)S(1)} %get-tuple-element.42.refs_0_, bf16[256,2048]{1,0:T(8,128)(2,1)S(1)} %get-tuple-element.43.refs_1_, bf16[2048,256]{1,0:T(8,128)(2,1)S(1)} %get-tuple-element.44.refs_2_, ...), custom_call_target="tpu_custom_call" | custom-call | tf_op jit(solution)/shard_map/forward/pallas_call | solution.py:34
  22.7 0.0 collective-permute-done.6.refs_1_
  22.7 0.6 collective-permute-start.5
  23.3 0.0 collective-permute-done.8.refs_5_
  23.3 0.1 collective-permute-start.9
  23.4 0.0 collective-permute-done.11.refs_8_
  23.4 0.5 collective-permute-start.10
  23.8 0.9 %collective-permute-done.4.b_ref = bf16[256,512]{1,0:T(8,128)(2,1)S(1)} collective-permute-done((bf16[256,512]{1,0:T(8,128)(2,1)S(1)}, bf16[256,512]{1,0:T(8,128)(2,1)S(1)}, u32[]{:S(2)}, u32[]{:S(2)}) %collective-permute-start.4) | collective-permute-done | bytes 262176 | tf_op jit(solution)/shard_map/ppermute | solution.py:311
  24.8 3.7 %collective-permute-start.7 = (bf16[16,256]{1,0:T(8,128)(2,1)S(1)}, bf16[16,256]{1,0:T(8,128)(2,1)S(1)}, u32[]{:S(2)}, u32[]{:S(2)}) collective-permute-start(bf16[16,256]{1,0:T(8,128)(2,1)S(1)} %get-tuple-element.47), channel_id=1, source_target_pairs={{0,12},{4,8},{8,4},{12,0},{1,13},{5,9},{9,5},{13,1},{2,14},{6,10},... | collective-permute-start | bytes 24584 | tf_op jit(solution)/shard_map/ppermute | solution.py:308
  28.5 0.1 both.3.refs_3_
  28.5 1.7 %collective-permute-done.7.refs_4_ = bf16[16,256]{1,0:T(8,128)(2,1)S(1)} collective-permute-done((bf16[16,256]{1,0:T(8,128)(2,1)S(1)}, bf16[16,256]{1,0:T(8,128)(2,1)S(1)}, u32[]{:S(2)}, u32[]{:S(2)}) %collective-permute-start.7) | collective-permute-done | bytes 8224 | tf_op jit(solution)/shard_map/ppermute | solution.py:308
  30.2 0.0 collective-permute-start.12
  30.2 0.0 collective-permute-done.9.refs_6_
  30.2 0.5 collective-permute-start.14
  30.7 0.0 collective-permute-done.10.refs_7_
  30.7 0.1 collective-permute-start.15
  30.8 2.9 %arrange.1 = (bf16[1024,256]{1,0:T(8,128)(2,1)S(1)}, bf16[1024,256]{1,0:T(8,128)(2,1)S(1)}, bf16[1024,256]{1,0:T(8,128)(2,1)S(1)}, bf16[1024,2048]{1,0:T(8,128)(2,1)S(1)}, f32[1,1024]{1,0:T(1,128)S(1)}) custom-call(s32[2]{0:T(128)S(1)} %pad_add_fusion.pos_ref, bf16[272,256]{1,0:T(8,128)(2,1)S(1)} %get-tuple-element.40.refs_0_, ...), custom_call_target="tpu_custom_call" | custom-call | tf_op jit(solution)/shard_map/arrange/pallas_call | solution.py:34
  33.7 0.0 collective-permute-done.1.refs_1_
  33.7 0.5 collective-permute-start.13
  34.2 0.0 collective-permute-done.5.refs_4_
  34.2 0.1 collective-permute-start.16
  34.3 0.0 collective-permute-done.12.refs_5_
  34.3 0.0 collective-permute-done.14.refs_7_
  34.3 0.0 collective-permute-done.15.refs_8_
  34.3 1.1 %collective-permute-done.13.refs_6_ = bf16[256,512]{1,0:T(8,128)(2,1)S(1)} collective-permute-done((bf16[256,512]{1,0:T(8,128)(2,1)S(1)}, bf16[256,512]{1,0:T(8,128)(2,1)S(1)}, u32[]{:S(2)}, u32[]{:S(2)}) %collective-permute-start.13) | collective-permute-done | bytes 262176 | tf_op jit(solution)/shard_map/ppermute | solution.py:311
  35.4 0.4 collective-permute-done.16.refs_9_
  35.8 5.1 %contrast.1.grads_ref = bf16[1024,512]{1,0:T(8,128)(2,1)S(1)} custom-call(s32[2]{0:T(128)S(1)} %pad_add_fusion.pos_ref, bf16[256,512]{1,0:T(8,128)(2,1)S(1)} %both.2.refs_0_, bf16[256,512]{1,0:T(8,128)(2,1)S(1)} %collective-permute-done.1.refs_1_, bf16[256,512]{1,0:T(8,128)(2,1)S(1)} %forward.4.refs_2_, bf16[256,512]{1,0:T(8,128)(2,1)S(1)} %both.3.refs_3_, ...), custom_call_target="tpu_custom_call" | custom-call | tf_op jit(solution)/shard_map/contrast/pallas_call | solution.py:34
  40.9 0.4 collective-permute-start.17
  41.3 0.1 collective-permute-start.20
  41.5 0.0 copy-done.2
  41.5 6.3 %mine.1 = (f32[1024,256]{1,0:T(8,128)S(1)}, f32[1024,256]{1,0:T(8,128)S(1)}, f32[1024,256]{1,0:T(8,128)S(1)}, f32[1024,256]{1,0:T(8,128)S(1)}) custom-call(s32[2]{0:T(128)S(1)} %pad_add_fusion.pos_ref, bf16[256,2048]{1,0:T(8,128)(2,1)S(1)} %copy-done, bf16[256,2048]{1,0:T(8,128)(2,1)S(1)} %copy-done.2, bf16[2048,256]{1,0:T(8,128)(2,1)S(1)} %copy-done.1, ...), custom_call_target="tpu_custom_call" | custom-call | flops 4294967296 | tf_op jit(solution)/shard_map/mine/pallas_call | solution.py:34
  47.8 0.0 collective-permute-done.17.grads_ref
  47.8 3.5 %other_state.1 = (bf16[256,1024]{1,0:T(8,128)(2,1)S(1)}, bf16[1024,256]{1,0:T(8,128)(2,1)S(1)}) custom-call(s32[2]{0:T(128)S(1)} %pad_add_fusion.pos_ref, bf16[256,2048]{1,0:T(8,128)(2,1)S(1)} %copy-done, bf16[2048,256]{1,0:T(8,128)(2,1)S(1)} %copy-done.1, bf16[1024,512]{1,0:T(8,128)(2,1)S(1)} %collective-permute-done.17.grads_ref, ...), custom_call_target="tpu_custom_call" | custom-call | flops 2147483648 | tf_op jit(solution)/shard_map/other_state/pallas_call | solution.py:34
  51.3 0.4 collective-permute-start.18
  51.7 0.1 collective-permute-start.19
  51.9 0.0 collective-permute-done.20.rows_ref
  51.9 4.8 %other_goal.1 = (bf16[256,1024]{1,0:T(8,128)(2,1)S(1)}, bf16[1024,256]{1,0:T(8,128)(2,1)S(1)}, f32[256,2048]{1,0:T(8,128)}, f32[2048,256]{1,0:T(8,128)}) custom-call(s32[2]{0:T(128)S(1)} %pad_add_fusion.pos_ref, bf16[256,2048]{1,0:T(8,128)(2,1)S(1)} %copy-done.2, bf16[2048,256]{1,0:T(8,128)(2,1)S(1)} %copy-done.3, ...), custom_call_target="tpu_custom_call" | custom-call | flops 2147483648 | tf_op jit(solution)/shard_map/other_goal/pallas_call | solution.py:34
  56.7 0.4 collective-permute-start.21
  57.1 0.1 collective-permute-start.22
  57.3 0.0 collective-permute-done.18.refs_0_
  57.3 0.0 collective-permute-done.19.refs_1_
  57.3 2.6 %finish.2 = (f32[256,2048]{1,0:T(8,128)}, f32[2048,256]{1,0:T(8,128)}, f32[256,2048]{1,0:T(8,128)}, f32[2048,256]{1,0:T(8,128)}) custom-call(s32[2]{0:T(128)S(1)} %pad_add_fusion.pos_ref, bf16[256,1024]{1,0:T(8,128)(2,1)S(1)} %collective-permute-done.18.refs_0_, ...), custom_call_target="tpu_custom_call", output_to_operand_aliasing={{0}: (5, {}), {1}: (6, {})} | custom-call | tf_op jit(solution)/shard_map/finish/pallas_call | solution.py:34
  59.9 0.0 collective-permute-done.21.refs_0_
  59.9 0.0 collective-permute-done.22.refs_1_
  59.9 1.9 %finish.3 = (f32[256,2048]{1,0:T(8,128)}, f32[2048,256]{1,0:T(8,128)}) custom-call(s32[2]{0:T(128)S(1)} %pad_add_fusion.pos_ref, bf16[256,1024]{1,0:T(8,128)(2,1)S(1)} %collective-permute-done.21.refs_0_, bf16[1024,256]{1,0:T(8,128)(2,1)S(1)} %collective-permute-done.22.refs_1_, ...), custom_call_target="tpu_custom_call", output_to_operand_aliasing={{0}: (3, {}), {1}: (4, {})} | custom-call | tf_op jit(solution)/shard_map/finish/pallas_call | solution.py:34
  (12 shorter events, 0.0 us)
Async XLA Ops:
  0.6 12.8 %collective-permute-start.2 = (bf16[256,256]{1,0:T(8,128)(2,1)}, bf16[256,256]{1,0:T(8,128)(2,1)S(1)}, u32[]{:S(2)}, u32[]{:S(2)}) collective-permute-start(bf16[256,256]{1,0:T(8,128)(2,1)} %x_ref.2), channel_id=1, source_target_pairs={{0,12},{4,8},{8,4},{12,0},{1,13},{5,9},{9,5},{13,1},{2,14},{6,10},... | collective-permute-start | bytes 393224 | tf_op jit(solution)/shard_map/ppermute | solution.py:308
  5.8 0.9 %copy-start.4 = (bf16[256,256]{1,0:T(8,128)(2,1)S(1)}, bf16[256,256]{1,0:T(8,128)(2,1)}, u32[]{:S(2)}) copy-start(bf16[256,256]{1,0:T(8,128)(2,1)} %x_ref.2) | copy-start | bytes 393220
  6.7 6.2 %copy-start.5 = (s32[256,1]{0,1:T(1,128)S(1)}, s32[256,1]{0,1:T(1,128)}, u32[]{:S(2)}) copy-start(s32[256,1]{0,1:T(1,128)} %param.9) | copy-start | bytes 3076
  6.7 6.2 %copy-start.6 = (s32[256]{0:T(256)S(1)}, s32[256]{0:T(256)}, u32[]{:S(2)}) copy-start(s32[256]{0:T(256)} %param.10) | copy-start | bytes 3076
  6.7 6.2 %copy-start.7 = (s32[256]{0:T(256)S(1)}, s32[256]{0:T(256)}, u32[]{:S(2)}) copy-start(s32[256]{0:T(256)} %param.11) | copy-start | bytes 3076
  11.3 8.0 %collective-permute-start = (bf16[256,512]{1,0:T(8,128)(2,1)S(1)}, bf16[256,512]{1,0:T(8,128)(2,1)S(1)}, u32[]{:S(2)}, u32[]{:S(2)}) collective-permute-start(bf16[256,512]{1,0:T(8,128)(2,1)S(1)} %get-tuple-element.37.a_ref), channel_id=1, source_target_pairs={{0,2},{2,0},{1,3},{3,1},{4,6},{6,4},{5,7},{7,5},{8,10},{10,8},{9,1... | collective-permute-start | bytes 786440 | tf_op jit(solution)/shard_map/ppermute | solution.py:311
  13.5 7.8 %collective-permute-start.3 = (bf16[272,256]{1,0:T(8,128)(2,1)S(1)}, bf16[272,256]{1,0:T(8,128)(2,1)S(1)}, u32[]{:S(2)}, u32[]{:S(2)}) collective-permute-start(bf16[272,256]{1,0:T(8,128)(2,1)S(1)} %get-tuple-element.40.refs_0_), channel_id=1, source_target_pairs={{0,8},{4,12},{8,0},{12,4},{1,9},{5,13},{9,1},{13,5},{2,10},{6,14},... | collective-permute-start | bytes 417800 | tf_op jit(solution)/shard_map/ppermute | solution.py:308
  13.6 9.2 %collective-permute-start.6 = (bf16[272,256]{1,0:T(8,128)(2,1)S(1)}, bf16[272,256]{1,0:T(8,128)(2,1)S(1)}, u32[]{:S(2)}, u32[]{:S(2)}) collective-permute-start(bf16[272,256]{1,0:T(8,128)(2,1)S(1)} %get-tuple-element.40.refs_0_), channel_id=1, source_target_pairs={{0,4},{4,0},{8,12},{12,8},{1,5},{5,1},{9,13},{13,9},{2,6},{6,2},{1... | collective-permute-start | bytes 417800 | tf_op jit(solution)/shard_map/ppermute | solution.py:308
  14.3 9.0 %collective-permute-start.8 = (bf16[272,256]{1,0:T(8,128)(2,1)S(1)}, bf16[272,256]{1,0:T(8,128)(2,1)S(1)}, u32[]{:S(2)}, u32[]{:S(2)}) collective-permute-start(bf16[272,256]{1,0:T(8,128)(2,1)S(1)} %get-tuple-element.40.refs_0_), channel_id=1, source_target_pairs={{0,1},{1,0},{2,3},{3,2},{4,5},{5,4},{6,7},{7,6},{8,9},{9,8},{10,11... | collective-permute-start | bytes 417800 | tf_op jit(solution)/shard_map/ppermute | solution.py:311
  15.7 9.1 %collective-permute-start.4 = (bf16[256,512]{1,0:T(8,128)(2,1)S(1)}, bf16[256,512]{1,0:T(8,128)(2,1)S(1)}, u32[]{:S(2)}, u32[]{:S(2)}) collective-permute-start(bf16[256,512]{1,0:T(8,128)(2,1)S(1)} %forward.5.a_ref), channel_id=1, source_target_pairs={{0,2},{2,0},{1,3},{3,1},{4,6},{6,4},{5,7},{7,5},{8,10},{10,8},{9,1... | collective-permute-start | bytes 786440 | tf_op jit(solution)/shard_map/ppermute | solution.py:311
  19.4 4.0 %collective-permute-start.11 = (bf16[256,256]{1,0:T(8,128)(2,1)S(1)}, bf16[256,256]{1,0:T(8,128)(2,1)S(1)}, u32[]{:S(2)}, u32[]{:S(2)}) collective-permute-start(bf16[256,256]{1,0:T(8,128)(2,1)S(1)} %collective-permute-done.2.x_ref.refs_3_), channel_id=1, source_target_pairs={{0,1},{1,0},{2,3},{3,2},{4,5},{5,4},{6,7},{7,6},{8,9},{9,8},{10,11... | collective-permute-start | bytes 393224 | tf_op jit(solution)/shard_map/ppermute | solution.py:311
  21.3 12.4 %collective-permute-start.1 = (bf16[256,512]{1,0:T(8,128)(2,1)S(1)}, bf16[256,512]{1,0:T(8,128)(2,1)S(1)}, u32[]{:S(2)}, u32[]{:S(2)}) collective-permute-start(bf16[256,512]{1,0:T(8,128)(2,1)S(1)} %both.2.refs_0_), channel_id=1, source_target_pairs={{0,4},{4,0},{8,12},{12,8},{1,5},{5,1},{9,13},{13,9},{2,6},{6,2},{1... | collective-permute-start | bytes 786440 | tf_op jit(solution)/shard_map/ppermute | solution.py:308
  22.7 11.5 %collective-permute-start.5 = (bf16[256,512]{1,0:T(8,128)(2,1)S(1)}, bf16[256,512]{1,0:T(8,128)(2,1)S(1)}, u32[]{:S(2)}, u32[]{:S(2)}) collective-permute-start(bf16[256,512]{1,0:T(8,128)(2,1)S(1)} %forward.4.refs_2_), channel_id=1, source_target_pairs={{0,2},{2,0},{1,3},{3,1},{4,6},{6,4},{5,7},{7,5},{8,10},{10,8},{9,1... | collective-permute-start | bytes 786440 | tf_op jit(solution)/shard_map/ppermute | solution.py:311
  23.3 6.9 %collective-permute-start.9 = (bf16[272,256]{1,0:T(8,128)(2,1)S(1)}, bf16[272,256]{1,0:T(8,128)(2,1)S(1)}, u32[]{:S(2)}, u32[]{:S(2)}) collective-permute-start(bf16[272,256]{1,0:T(8,128)(2,1)S(1)} %collective-permute-done.6.refs_1_), channel_id=1, source_target_pairs={{0,1},{1,0},{2,3},{3,2},{4,5},{5,4},{6,7},{7,6},{8,9},{9,8},{10,11... | collective-permute-start | bytes 417800 | tf_op jit(solution)/shard_map/ppermute | solution.py:311
  23.4 7.4 %collective-permute-start.10 = (bf16[272,256]{1,0:T(8,128)(2,1)S(1)}, bf16[272,256]{1,0:T(8,128)(2,1)S(1)}, u32[]{:S(2)}, u32[]{:S(2)}) collective-permute-start(bf16[272,256]{1,0:T(8,128)(2,1)S(1)} %collective-permute-done.3.x_ref.refs_2_), channel_id=1, source_target_pairs={{0,1},{1,0},{2,3},{3,2},{4,5},{5,4},{6,7},{7,6},{8,9},{9,8},{10,11... | collective-permute-start | bytes 417800 | tf_op jit(solution)/shard_map/ppermute | solution.py:311
  24.8 5.4 %collective-permute-start.7 = (bf16[16,256]{1,0:T(8,128)(2,1)S(1)}, bf16[16,256]{1,0:T(8,128)(2,1)S(1)}, u32[]{:S(2)}, u32[]{:S(2)}) collective-permute-start(bf16[16,256]{1,0:T(8,128)(2,1)S(1)} %get-tuple-element.47), channel_id=1, source_target_pairs={{0,12},{4,8},{8,4},{12,0},{1,13},{5,9},{9,5},{13,1},{2,14},{6,10},... | collective-permute-start | bytes 24584 | tf_op jit(solution)/shard_map/ppermute | solution.py:308
  30.2 4.1 %collective-permute-start.12 = (bf16[256,512]{1,0:T(8,128)(2,1)S(1)}, bf16[256,512]{1,0:T(8,128)(2,1)S(1)}, u32[]{:S(2)}, u32[]{:S(2)}) collective-permute-start(bf16[256,512]{1,0:T(8,128)(2,1)S(1)} %both.2.refs_0_), channel_id=1, source_target_pairs={{0,1},{1,0},{2,3},{3,2},{4,5},{5,4},{6,7},{7,6},{8,9},{9,8},{10,11... | collective-permute-start | bytes 786440 | tf_op jit(solution)/shard_map/ppermute | solution.py:311
  30.2 4.1 %collective-permute-start.14 = (bf16[256,512]{1,0:T(8,128)(2,1)S(1)}, bf16[256,512]{1,0:T(8,128)(2,1)S(1)}, u32[]{:S(2)}, u32[]{:S(2)}) collective-permute-start(bf16[256,512]{1,0:T(8,128)(2,1)S(1)} %forward.4.refs_2_), channel_id=1, source_target_pairs={{0,1},{1,0},{2,3},{3,2},{4,5},{5,4},{6,7},{7,6},{8,9},{9,8},{10,11... | collective-permute-start | bytes 786440 | tf_op jit(solution)/shard_map/ppermute | solution.py:311
  30.7 3.6 %collective-permute-start.15 = (bf16[256,512]{1,0:T(8,128)(2,1)S(1)}, bf16[256,512]{1,0:T(8,128)(2,1)S(1)}, u32[]{:S(2)}, u32[]{:S(2)}) collective-permute-start(bf16[256,512]{1,0:T(8,128)(2,1)S(1)} %both.3.refs_3_), channel_id=1, source_target_pairs={{0,1},{1,0},{2,3},{3,2},{4,5},{5,4},{6,7},{7,6},{8,9},{9,8},{10,11... | collective-permute-start | bytes 786440 | tf_op jit(solution)/shard_map/ppermute | solution.py:311
  33.7 1.7 %collective-permute-start.13 = (bf16[256,512]{1,0:T(8,128)(2,1)S(1)}, bf16[256,512]{1,0:T(8,128)(2,1)S(1)}, u32[]{:S(2)}, u32[]{:S(2)}) collective-permute-start(bf16[256,512]{1,0:T(8,128)(2,1)S(1)} %collective-permute-done.1.refs_1_), channel_id=1, source_target_pairs={{0,1},{1,0},{2,3},{3,2},{4,5},{5,4},{6,7},{7,6},{8,9},{9,8},{10,11... | collective-permute-start | bytes 786440 | tf_op jit(solution)/shard_map/ppermute | solution.py:311
  34.2 1.5 %collective-permute-start.16 = (bf16[256,512]{1,0:T(8,128)(2,1)S(1)}, bf16[256,512]{1,0:T(8,128)(2,1)S(1)}, u32[]{:S(2)}, u32[]{:S(2)}) collective-permute-start(bf16[256,512]{1,0:T(8,128)(2,1)S(1)} %collective-permute-done.5.refs_4_), channel_id=1, source_target_pairs={{0,1},{1,0},{2,3},{3,2},{4,5},{5,4},{6,7},{7,6},{8,9},{9,8},{10,11... | collective-permute-start | bytes 786440 | tf_op jit(solution)/shard_map/ppermute | solution.py:311
  35.8 5.7 %copy-start = (bf16[256,2048]{1,0:T(8,128)(2,1)S(1)}, bf16[256,2048]{1,0:T(8,128)(2,1)}, u32[]{:S(2)}) copy-start(bf16[256,2048]{1,0:T(8,128)(2,1)} %first.2) | copy-start | bytes 3145732
  35.8 5.7 %copy-start.1 = (bf16[2048,256]{1,0:T(8,128)(2,1)S(1)}, bf16[2048,256]{1,0:T(8,128)(2,1)}, u32[]{:S(2)}) copy-start(bf16[2048,256]{1,0:T(8,128)(2,1)} %second.2) | copy-start | bytes 3145732
  35.8 5.7 %copy-start.2 = (bf16[256,2048]{1,0:T(8,128)(2,1)S(1)}, bf16[256,2048]{1,0:T(8,128)(2,1)}, u32[]{:S(2)}) copy-start(bf16[256,2048]{1,0:T(8,128)(2,1)} %first.3) | copy-start | bytes 3145732
  35.8 5.7 %copy-start.3 = (bf16[2048,256]{1,0:T(8,128)(2,1)S(1)}, bf16[2048,256]{1,0:T(8,128)(2,1)}, u32[]{:S(2)}) copy-start(bf16[2048,256]{1,0:T(8,128)(2,1)} %second.3) | copy-start | bytes 3145732
  40.9 6.9 %collective-permute-start.17 = (bf16[1024,512]{1,0:T(8,128)(2,1)S(1)}, bf16[1024,512]{1,0:T(8,128)(2,1)S(1)}, u32[]{:S(2)}, u32[]{:S(2)}) collective-permute-start(bf16[1024,512]{1,0:T(8,128)(2,1)S(1)} %contrast.1.grads_ref), channel_id=1, source_target_pairs={{0,1},{1,0},{2,3},{3,2},{4,5},{5,4},{6,7},{7,6},{8,9},{9,8},{10,11... | collective-permute-start | bytes 3145736 | tf_op jit(solution)/shard_map/ppermute | solution.py:311
  41.3 10.5 %collective-permute-start.20 = (bf16[1024,256]{1,0:T(8,128)(2,1)S(1)}, bf16[1024,256]{1,0:T(8,128)(2,1)S(1)}, u32[]{:S(2)}, u32[]{:S(2)}) collective-permute-start(bf16[1024,256]{1,0:T(8,128)(2,1)S(1)} %get-tuple-element.53.goals_ref), channel_id=1, source_target_pairs={{0,1},{1,0},{2,3},{3,2},{4,5},{5,4},{6,7},{7,6},{8,9},{9,8},{10,11... | collective-permute-start | bytes 1572872 | tf_op jit(solution)/shard_map/ppermute | solution.py:311
  51.3 6.0 %collective-permute-start.18 = (bf16[256,1024]{1,0:T(8,128)(2,1)S(1)}, bf16[256,1024]{1,0:T(8,128)(2,1)S(1)}, u32[]{:S(2)}, u32[]{:S(2)}) collective-permute-start(bf16[256,1024]{1,0:T(8,128)(2,1)S(1)} %get-tuple-element.56.refs_0_), channel_id=1, source_target_pairs={{0,1},{1,0},{2,3},{3,2},{4,5},{5,4},{6,7},{7,6},{8,9},{9,8},{10,11... | collective-permute-start | bytes 1572872 | tf_op jit(solution)/shard_map/ppermute | solution.py:311
  51.7 5.5 %collective-permute-start.19 = (bf16[1024,256]{1,0:T(8,128)(2,1)S(1)}, bf16[1024,256]{1,0:T(8,128)(2,1)S(1)}, u32[]{:S(2)}, u32[]{:S(2)}) collective-permute-start(bf16[1024,256]{1,0:T(8,128)(2,1)S(1)} %get-tuple-element.57.refs_1_), channel_id=1, source_target_pairs={{0,1},{1,0},{2,3},{3,2},{4,5},{5,4},{6,7},{7,6},{8,9},{9,8},{10,11... | collective-permute-start | bytes 1572872 | tf_op jit(solution)/shard_map/ppermute | solution.py:311
  56.7 3.2 %collective-permute-start.21 = (bf16[256,1024]{1,0:T(8,128)(2,1)S(1)}, bf16[256,1024]{1,0:T(8,128)(2,1)S(1)}, u32[]{:S(2)}, u32[]{:S(2)}) collective-permute-start(bf16[256,1024]{1,0:T(8,128)(2,1)S(1)} %get-tuple-element.60.refs_2_), channel_id=1, source_target_pairs={{0,1},{1,0},{2,3},{3,2},{4,5},{5,4},{6,7},{7,6},{8,9},{9,8},{10,11... | collective-permute-start | bytes 1572872 | tf_op jit(solution)/shard_map/ppermute | solution.py:311
  57.1 2.8 %collective-permute-start.22 = (bf16[1024,256]{1,0:T(8,128)(2,1)S(1)}, bf16[1024,256]{1,0:T(8,128)(2,1)S(1)}, u32[]{:S(2)}, u32[]{:S(2)}) collective-permute-start(bf16[1024,256]{1,0:T(8,128)(2,1)S(1)} %get-tuple-element.61.refs_3_), channel_id=1, source_target_pairs={{0,1},{1,0},{2,3},{3,2},{4,5},{5,4},{6,7},{7,6},{8,9},{9,8},{10,11... | collective-permute-start | bytes 1572872 | tf_op jit(solution)/shard_map/ppermute | solution.py:311

commit v9 on v8

--- a/solution.py
+++ b/solution.py
@@ -61,11 +61,10 @@
     copies = [pltpu.make_async_copy(weights[i], held[i], sems.at[i]) for i in range(4)]
     for i in (0, 2, 1, 3):
         copies[i].start()
-    encode(x_ref, held, out_ref, active, lambda i: copies[i].wait())
-
-
-def first_forward(pos, x, weights):
-    rows, width = x.shape
+    encode(x_ref.at[: out_ref.shape[0]], held, out_ref, active, lambda i: copies[i].wait())
+
+
+def first_forward(pos, x, weights, rows):
     hid, emb = weights[2].shape
     part, *held = kernel(
         first_kernel,
@@ -80,22 +79,21 @@
     return part, held
 
 
-def pack_kernel(n_rep, n_blk, n_sub, pos_ref, x_ref, distance_ref, place_ref, episode_ref, pack_ref, meta_ref):
+def pack_kernel(n_rep, n_blk, n_sub, pos_ref, x_ref, own_ref, pack_ref):
     rows = x_ref.shape[0]
     slab = rows // n_rep
 
     def bits(n):
         return n.bit_length() - 1
 
-    owner = (pos_ref[0] * n_sub + pos_ref[1] + distance_ref[...]) & (n_blk * n_sub - 1)
-    place = place_ref[...]
+    owner = (pos_ref[0] * n_sub + pos_ref[1] + own_ref[0:1, :]) & (n_blk * n_sub - 1)
+    place = own_ref[1:2, :]
     batch = ((owner & (n_sub - 1)) << bits(n_rep)) + (place >> bits(slab))
     goal = (((batch << bits(n_blk)) + (owner >> bits(n_sub))) << bits(slab)) + (place & (slab - 1))
-    digits = (goal >> 8, goal & 255, episode_ref[...])
+    digits = (goal >> 8, goal & 255, own_ref[2:3, :])
     table = jnp.concatenate([d.astype(F32) for d in digits] + [jnp.zeros((13, rows), F32)], axis=0).astype(BF)
     pack_ref[:rows, :] = x_ref[...]
     pack_ref[rows:, :] = table
-    meta_ref[...] = table
 
 
 def forward_kernel(x_ref, *refs):
@@ -135,9 +133,8 @@
 
 
 def arrange_kernel(n_blk, n_rep, slab, pos_ref, *refs):
-    n = n_blk + 1
-    mine, other = refs[:n], refs[n : 2 * n - 1]
-    rows_mine, rows_other, goals_ref, pick_ref, ep_ref, both_sides, meta = refs[2 * n - 1 :]
+    mine, other = refs[:n_blk], refs[n_blk : 2 * n_blk]
+    rows_mine, rows_other, goals_ref, pick_ref, ep_ref, both_sides, meta = refs[2 * n_blk :]
     half = rows_mine.shape[0]
     rows = 2 * half
     batch = n_blk * slab
@@ -147,13 +144,12 @@
             to[pl.ds(off, slab), :] = value
             both_sides[pl.ds(i * half + off, slab), :] = value
 
-        place_blocks(pos_ref, blocks[:n_blk], put, n_blk, n_rep, slab)
-    tables = [block.at[n_rep * slab :] for block in mine[: n_blk - 1]] + [mine[n_blk]]
-    for k, table in enumerate(tables):
+        place_blocks(pos_ref, blocks, put, n_blk, n_rep, slab)
+    for k, block in enumerate(mine):
         at = jnp.bitwise_xor(pos_ref[0], k)
         for r in range(n_rep):
             off = pl.multiple_of((r * n_blk + at) * slab, slab)
-            meta[:, pl.ds(off, slab)] = table[:, r * slab : (r + 1) * slab].astype(F32)
+            meta[:, pl.ds(off, slab)] = block[n_rep * slab :, r * slab : (r + 1) * slab].astype(F32)
     ep_ref[...] = meta[2:3, :]
     for r in range(n_rep):
         own = slice(r * batch, (r + 1) * batch)
@@ -314,20 +310,19 @@
         return lax.optimization_barrier((x, *first))[0]
 
     weights = (state_first, goal_first, state_second, goal_second)
-    meta = (goal_distance.reshape(1, rows_dev), goal_row.reshape(1, rows_dev), episode.reshape(1, rows_dev))
-    got = {3: across(states, 3)}
-    part0, held = first_forward(pos, states, weights)
-    there0 = swap(part0, "rep")
-    pack, table = kernel(
+    (pack,) = kernel(
         functools.partial(pack_kernel, n_rep, n_blk, n_sub),
         "pack",
-        [((rows_dev + 16, width), BF), ((16, width), BF)],
-        (after(states, part0), *meta),
+        [((rows_dev + 16, width), BF)],
+        (states, jnp.stack([goal_distance.reshape(rows_dev), goal_row, episode])),
         pos=pos,
         limit=4,
     )
-    got[0], got[1] = pack, across(pack, 1)
+    got = {0: pack, 3: across(pack, 3)}
+    part0, held = first_forward(pos, pack, weights, rows_dev)
+    got[1] = across(after(pack, part0), 1)
     got[2] = across(after(pack, got[3]), 2)
+    there0 = swap(part0, "rep")
     part3 = forward(got[3], held, rows_dev)
     there3 = swap(part3, "rep")
 
@@ -335,7 +330,6 @@
     sums[1] = across(sums[0], 1)
     part2 = forward(after(got[2], sums[0]), held, rows_dev)
     there2 = swap(part2, "rep")
-    got[4] = across(after(table, part2), 3)
     sums[3] = both(part3, there3)
 
     side = ((rows_all // 2, width), BF)
@@ -343,7 +337,7 @@
         functools.partial(arrange_kernel, n_blk, n_rep, slab),
         "arrange",
         [side, side, side, ((rows_all // 2, rows_all), BF), ((1, rows_all // 2), F32)],
-        (*(got[k] for k in range(n_blk + 1)), *(swap(got[k], "sub") for k in range(n_blk))),
+        (*(got[k] for k in range(n_blk)), *(swap(got[k], "sub") for k in range(n_blk))),
         [
             pltpu.VMEM((rows_all, width), BF),
             pltpu.VMEM((16, rows_all // 2), F32),

time: 62.2 us -> 61.5 us (0.989)
  starting transfers between devices: 16.1 us -> 14.4 us
  other arithmetic: 0.07 us -> 0.8 us
    ppermute x5 -> x4, starting transfers between devices: 9.66 us -> 7.86 us  [across(): return lax.ppermute(x, 'blk', [(i, i ^ k) for i in range(n_blk)])]
    ppermute x18, waiting for transfers between devices: 5.18 us -> 6.25 us  [swap(): return lax.ppermute(x, axis, [(0, 1), (1, 0)])]
    ppermute x5 -> x4, waiting for transfers between devices: 3.56 us -> 2.68 us  [across(): return lax.ppermute(x, 'blk', [(i, i ^ k) for i in range(n_blk)])]
    another operation x0 -> x1, other arithmetic: none -> 0.72 us  [gathered(): jnp.stack([goal_distance.reshape(rows_dev), goal_row, episode])]
  transfers between devices with their start and end apart: 23 -> 22, of which waited for: 6 -> 7; matrix products, arithmetic and copies ran while one was open for 0% -> 0% of each run, Pallas kernels for 45% -> 45%
where the time goes in v9:
time: 61.5 us; the launch traced here: 61.3 us
  Pallas kernels  35.2 us (57%)
  starting transfers between devices  14.4 us (23%)
  waiting for transfers between devices  8.92 us (15%)
  between operations  0.95 us (2%)
  local copies, waits for them, and re-layouts  0.92 us (1%)
  other arithmetic  0.8 us (1%)
    pallas_call x13, Pallas kernels, kernel(): pl.pallas_call(body, in_specs=specs, out_specs=[HBM if i in hbm_out else...  35.2 us
    ppermute x4, starting transfers between devices, across(): return lax.ppermute(x, 'blk', [(i, i ^ k) for i in range(n_blk)])  7.86 us
    ppermute x18, starting transfers between devices, swap(): return lax.ppermute(x, axis, [(0, 1), (1, 0)])  6.58 us
    ppermute x18, waiting for transfers between devices, swap(): return lax.ppermute(x, axis, [(0, 1), (1, 0)])  6.25 us
    ppermute x4, waiting for transfers between devices, across(): return lax.ppermute(x, 'blk', [(i, i ^ k) for i in range(n_blk)])  2.68 us
  transfers between devices with their start and end apart: 22, of which 7 were waited for; matrix products, arithmetic and copies ran while one was open for 0% of the time, Pallas kernels for 45%

profile of v9, /device:TPU:0, one launch (start us, length us, event | category | flops | bytes accessed | tf_op | source)
XLA Modules:
  0.0 61.3 jit_solution(6456277851161181873)
XLA Ops:
  0.6 0.1 pad_add_fusion.1.pos_ref
  0.7 0.7 %pad_add_fusion.own_ref = s32[3,256]{1,0:T(4,128)S(1)} fusion(s32[1,256]{1,0:T(1,128)} %bitcast.5, s32[1,256]{1,0:T(1,128)} %bitcast.6, s32[1,256]{1,0:T(1,128)} %bitcast.7), kind=kLoop, calls=%fused_computation | loop fusion | flops 1536 | bytes 6144 | tf_op jit(solution)/shard_map/stack | solution.py:317
  1.4 0.9 %copy-done.4 = bf16[256,256]{1,0:T(8,128)(2,1)S(1)} copy-done((bf16[256,256]{1,0:T(8,128)(2,1)S(1)}, bf16[256,256]{1,0:T(8,128)(2,1)}, u32[]{:S(2)}) %copy-start.4) | copy-done | bytes 131096
  2.3 0.6 pack.1.x_ref.refs_0_
  2.9 5.1 %collective-permute-start.2 = (bf16[272,256]{1,0:T(8,128)(2,1)S(1)}, bf16[272,256]{1,0:T(8,128)(2,1)S(1)}, u32[]{:S(2)}, u32[]{:S(2)}) collective-permute-start(bf16[272,256]{1,0:T(8,128)(2,1)S(1)} %pack.1.x_ref.refs_0_), channel_id=1, source_target_pairs={{0,12},{4,8},{8,4},{12,0},{1,13},{5,9},{9,5},{13,1},{2,14},{6,10},... | collective-permute-start | bytes 417800 | tf_op jit(solution)/shard_map/ppermute | solution.py:304
  8.0 4.6 %forward.3 = (bf16[256,512]{1,0:T(8,128)(2,1)S(1)}, bf16[256,2048]{1,0:T(8,128)(2,1)S(1)}, bf16[256,2048]{1,0:T(8,128)(2,1)S(1)}, bf16[2048,256]{1,0:T(8,128)(2,1)S(1)}, bf16[2048,256]{1,0:T(8,128)(2,1)S(1)}) custom-call(s32[2]{0:T(128)S(1)} %pad_add_fusion.1.pos_ref, bf16[272,256]{1,0:T(8,128)(2,1)S(1)} %pack.1.x_ref.refs_0_, bf16[256,2048]{1,0:T(8,128)(2,1)} %first.2, ...), custom_call_target="tpu_custom_call" | custom-call | tf_op jit(solution)/shard_map/forward/pallas_call | solution.py:34
  12.6 1.6 %collective-permute-start = (bf16[256,512]{1,0:T(8,128)(2,1)S(1)}, bf16[256,512]{1,0:T(8,128)(2,1)S(1)}, u32[]{:S(2)}, u32[]{:S(2)}) collective-permute-start(bf16[256,512]{1,0:T(8,128)(2,1)S(1)} %get-tuple-element.34.a_ref), channel_id=1, source_target_pairs={{0,2},{2,0},{1,3},{3,1},{4,6},{6,4},{5,7},{7,5},{8,10},{10,8},{9,1... | collective-permute-start | bytes 786440 | tf_op jit(solution)/shard_map/ppermute | solution.py:307
  14.2 0.0 collective-permute-done.2.x_ref.refs_3_
  14.2 1.4 %forward.5.a_ref = bf16[256,512]{1,0:T(8,128)(2,1)S(1)} custom-call(bf16[272,256]{1,0:T(8,128)(2,1)S(1)} %collective-permute-done.2.x_ref.refs_3_, bf16[256,2048]{1,0:T(8,128)(2,1)S(1)} %get-tuple-element.37.refs_0_, bf16[256,2048]{1,0:T(8,128)(2,1)S(1)} %get-tuple-element.38.refs_1_, bf16[2048,256]{1,0:T(8,128)(2,1)S(1)} %get-tuple-element.39.refs_2_, ...), custom_call_target="tpu_custom_call" | custom-call | tf_op jit(solution)/shard_map/forward/pallas_call | solution.py:34
  15.6 0.6 collective-permute-start.4
  16.2 2.2 %collective-permute-start.3 = (bf16[272,256]{1,0:T(8,128)(2,1)S(1)}, bf16[272,256]{1,0:T(8,128)(2,1)S(1)}, u32[]{:S(2)}, u32[]{:S(2)}) collective-permute-start(bf16[272,256]{1,0:T(8,128)(2,1)S(1)} %pack.1.x_ref.refs_0_), channel_id=1, source_target_pairs={{0,8},{4,12},{8,0},{12,4},{1,9},{5,13},{9,1},{13,5},{2,10},{6,14},... | collective-permute-start | bytes 417800 | tf_op jit(solution)/shard_map/ppermute | solution.py:304
  18.3 0.5 collective-permute-start.6
  18.8 0.0 collective-permute-start.7
  18.8 3.1 %collective-permute-done.b_ref = bf16[256,512]{1,0:T(8,128)(2,1)S(1)} collective-permute-done((bf16[256,512]{1,0:T(8,128)(2,1)S(1)}, bf16[256,512]{1,0:T(8,128)(2,1)S(1)}, u32[]{:S(2)}, u32[]{:S(2)}) %collective-permute-start) | collective-permute-done | bytes 262176 | tf_op jit(solution)/shard_map/ppermute | solution.py:307
  21.9 0.1 both.2.refs_0_
  22.0 0.1 collective-permute-start.1
  22.1 2.7 %collective-permute-done.3.x_ref.refs_2_ = bf16[272,256]{1,0:T(8,128)(2,1)S(1)} collective-permute-done((bf16[272,256]{1,0:T(8,128)(2,1)S(1)}, bf16[272,256]{1,0:T(8,128)(2,1)S(1)}, u32[]{:S(2)}, u32[]{:S(2)}) %collective-permute-start.3) | collective-permute-done | bytes 139296 | tf_op jit(solution)/shard_map/ppermute | solution.py:304
  24.7 1.4 %forward.4.refs_2_ = bf16[256,512]{1,0:T(8,128)(2,1)S(1)} custom-call(bf16[272,256]{1,0:T(8,128)(2,1)S(1)} %collective-permute-done.3.x_ref.refs_2_, bf16[256,2048]{1,0:T(8,128)(2,1)S(1)} %get-tuple-element.37.refs_0_, bf16[256,2048]{1,0:T(8,128)(2,1)S(1)} %get-tuple-element.38.refs_1_, bf16[2048,256]{1,0:T(8,128)(2,1)S(1)} %get-tuple-element.39.refs_2_, ...), custom_call_target="tpu_custom_call" | custom-call | tf_op jit(solution)/shard_map/forward/pallas_call | solution.py:34
  26.1 1.1 %collective-permute-start.5 = (bf16[256,512]{1,0:T(8,128)(2,1)S(1)}, bf16[256,512]{1,0:T(8,128)(2,1)S(1)}, u32[]{:S(2)}, u32[]{:S(2)}) collective-permute-start(bf16[256,512]{1,0:T(8,128)(2,1)S(1)} %forward.4.refs_2_), channel_id=1, source_target_pairs={{0,2},{2,0},{1,3},{3,1},{4,6},{6,4},{5,7},{7,5},{8,10},{10,8},{9,1... | collective-permute-start | bytes 786440 | tf_op jit(solution)/shard_map/ppermute | solution.py:307
  27.2 0.0 collective-permute-done.6.refs_1_
  27.2 0.0 collective-permute-start.8
  27.2 0.0 collective-permute-done.7.refs_4_
  27.2 0.5 collective-permute-start.10
  27.7 0.0 collective-permute-done.4.b_ref
  27.7 0.1 collective-permute-start.9
  27.8 0.1 both.3.refs_3_
  27.9 0.7 %collective-permute-done.8.refs_5_ = bf16[272,256]{1,0:T(8,128)(2,1)S(1)} collective-permute-done((bf16[272,256]{1,0:T(8,128)(2,1)S(1)}, bf16[272,256]{1,0:T(8,128)(2,1)S(1)}, u32[]{:S(2)}, u32[]{:S(2)}) %collective-permute-start.8) | collective-permute-done | bytes 139296 | tf_op jit(solution)/shard_map/ppermute | solution.py:307
  28.6 0.1 collective-permute-start.11
  28.7 0.1 collective-permute-done.10.refs_7_
  28.8 0.3 collective-permute-start.13
  29.1 0.0 collective-permute-done.9.refs_6_
  29.1 0.2 collective-permute-start.14
  29.3 2.9 %arrange.1 = (bf16[1024,256]{1,0:T(8,128)(2,1)S(1)}, bf16[1024,256]{1,0:T(8,128)(2,1)S(1)}, bf16[1024,256]{1,0:T(8,128)(2,1)S(1)}, bf16[1024,2048]{1,0:T(8,128)(2,1)S(1)}, f32[1,1024]{1,0:T(1,128)S(1)}) custom-call(s32[2]{0:T(128)S(1)} %pad_add_fusion.1.pos_ref, bf16[272,256]{1,0:T(8,128)(2,1)S(1)} %pack.1.x_ref.refs_0_, ...), custom_call_target="tpu_custom_call" | custom-call | tf_op jit(solution)/shard_map/arrange/pallas_call | solution.py:34
  32.2 0.0 collective-permute-done.1.refs_1_
  32.2 0.4 collective-permute-start.12
  32.6 0.9 %collective-permute-done.5.refs_4_ = bf16[256,512]{1,0:T(8,128)(2,1)S(1)} collective-permute-done((bf16[256,512]{1,0:T(8,128)(2,1)S(1)}, bf16[256,512]{1,0:T(8,128)(2,1)S(1)}, u32[]{:S(2)}, u32[]{:S(2)}) %collective-permute-start.5) | collective-permute-done | bytes 262176 | tf_op jit(solution)/shard_map/ppermute | solution.py:307
  33.4 0.0 collective-permute-start.15
  33.4 0.0 collective-permute-done.11.refs_5_
  33.4 0.0 collective-permute-done.13.refs_7_
  33.5 0.0 collective-permute-done.14.refs_8_
  33.5 0.3 collective-permute-done.12.refs_6_
  33.8 1.2 %collective-permute-done.15.refs_9_ = bf16[256,512]{1,0:T(8,128)(2,1)S(1)} collective-permute-done((bf16[256,512]{1,0:T(8,128)(2,1)S(1)}, bf16[256,512]{1,0:T(8,128)(2,1)S(1)}, u32[]{:S(2)}, u32[]{:S(2)}) %collective-permute-start.15) | collective-permute-done | bytes 262176 | tf_op jit(solution)/shard_map/ppermute | solution.py:307
  35.0 5.1 %contrast.1.grads_ref = bf16[1024,512]{1,0:T(8,128)(2,1)S(1)} custom-call(s32[2]{0:T(128)S(1)} %pad_add_fusion.1.pos_ref, bf16[256,512]{1,0:T(8,128)(2,1)S(1)} %both.2.refs_0_, bf16[256,512]{1,0:T(8,128)(2,1)S(1)} %collective-permute-done.1.refs_1_, bf16[256,512]{1,0:T(8,128)(2,1)S(1)} %forward.4.refs_2_, bf16[256,512]{1,0:T(8,128)(2,1)S(1)} %both.3.refs_3_, ...), custom_call_target="tpu_custom_call" | custom-call | tf_op jit(solution)/shard_map/contrast/pallas_call | solution.py:34
  40.1 0.2 collective-permute-start.16
  40.3 0.4 collective-permute-start.19
  40.7 0.0 copy-done
  40.7 0.0 copy-done.1
  40.7 0.0 copy-done.2
  40.7 0.0 copy-done.3
  40.7 6.3 %mine.1 = (f32[1024,256]{1,0:T(8,128)S(1)}, f32[1024,256]{1,0:T(8,128)S(1)}, f32[1024,256]{1,0:T(8,128)S(1)}, f32[1024,256]{1,0:T(8,128)S(1)}) custom-call(s32[2]{0:T(128)S(1)} %pad_add_fusion.1.pos_ref, bf16[256,2048]{1,0:T(8,128)(2,1)S(1)} %copy-done, bf16[256,2048]{1,0:T(8,128)(2,1)S(1)} %copy-done.2, bf16[2048,256]{1,0:T(8,128)(2,1)S(1)} %copy-done.1, ...), custom_call_target="tpu_custom_call" | custom-call | flops 4294967296 | tf_op jit(solution)/shard_map/mine/pallas_call | solution.py:34
  47.0 0.0 collective-permute-done.16.grads_ref
  47.0 3.5 %other_state.1 = (bf16[256,1024]{1,0:T(8,128)(2,1)S(1)}, bf16[1024,256]{1,0:T(8,128)(2,1)S(1)}) custom-call(s32[2]{0:T(128)S(1)} %pad_add_fusion.1.pos_ref, bf16[256,2048]{1,0:T(8,128)(2,1)S(1)} %copy-done, bf16[2048,256]{1,0:T(8,128)(2,1)S(1)} %copy-done.1, bf16[1024,512]{1,0:T(8,128)(2,1)S(1)} %collective-permute-done.16.grads_ref, ...), custom_call_target="tpu_custom_call" | custom-call | flops 2147483648 | tf_op jit(solution)/shard_map/other_state/pallas_call | solution.py:34
  50.5 0.2 collective-permute-start.17
  50.7 0.4 collective-permute-start.18
  51.1 0.0 collective-permute-done.19.rows_ref
  51.1 4.8 %other_goal.1 = (bf16[256,1024]{1,0:T(8,128)(2,1)S(1)}, bf16[1024,256]{1,0:T(8,128)(2,1)S(1)}, f32[256,2048]{1,0:T(8,128)}, f32[2048,256]{1,0:T(8,128)}) custom-call(s32[2]{0:T(128)S(1)} %pad_add_fusion.1.pos_ref, bf16[256,2048]{1,0:T(8,128)(2,1)S(1)} %copy-done.2, bf16[2048,256]{1,0:T(8,128)(2,1)S(1)} %copy-done.3, ...), custom_call_target="tpu_custom_call" | custom-call | flops 2147483648 | tf_op jit(solution)/shard_map/other_goal/pallas_call | solution.py:34
  55.9 0.2 collective-permute-start.20
  56.1 0.4 collective-permute-start.21
  56.5 0.0 collective-permute-done.17.refs_0_
  56.5 0.0 collective-permute-done.18.refs_1_
  56.5 2.6 %finish.2 = (f32[256,2048]{1,0:T(8,128)}, f32[2048,256]{1,0:T(8,128)}, f32[256,2048]{1,0:T(8,128)}, f32[2048,256]{1,0:T(8,128)}) custom-call(s32[2]{0:T(128)S(1)} %pad_add_fusion.1.pos_ref, bf16[256,1024]{1,0:T(8,128)(2,1)S(1)} %collective-permute-done.17.refs_0_, ...), custom_call_target="tpu_custom_call", output_to_operand_aliasing={{0}: (5, {}), {1}: (6, {})} | custom-call | tf_op jit(solution)/shard_map/finish/pallas_call | solution.py:34
  59.2 0.0 collective-permute-done.20.refs_0_
  59.2 0.0 collective-permute-done.21.refs_1_
  59.2 1.9 %finish.3 = (f32[256,2048]{1,0:T(8,128)}, f32[2048,256]{1,0:T(8,128)}) custom-call(s32[2]{0:T(128)S(1)} %pad_add_fusion.1.pos_ref, bf16[256,1024]{1,0:T(8,128)(2,1)S(1)} %collective-permute-done.20.refs_0_, bf16[1024,256]{1,0:T(8,128)(2,1)S(1)} %collective-permute-done.21.refs_1_, ...), custom_call_target="tpu_custom_call", output_to_operand_aliasing={{0}: (3, {}), {1}: (4, {})} | custom-call | tf_op jit(solution)/shard_map/finish/pallas_call | solution.py:34
  (5 shorter events, 0.0 us)
Async XLA Ops:
  1.4 0.9 %copy-start.4 = (bf16[256,256]{1,0:T(8,128)(2,1)S(1)}, bf16[256,256]{1,0:T(8,128)(2,1)}, u32[]{:S(2)}) copy-start(bf16[256,256]{1,0:T(8,128)(2,1)} %x_ref.1) | copy-start | bytes 393220
  2.9 11.3 %collective-permute-start.2 = (bf16[272,256]{1,0:T(8,128)(2,1)S(1)}, bf16[272,256]{1,0:T(8,128)(2,1)S(1)}, u32[]{:S(2)}, u32[]{:S(2)}) collective-permute-start(bf16[272,256]{1,0:T(8,128)(2,1)S(1)} %pack.1.x_ref.refs_0_), channel_id=1, source_target_pairs={{0,12},{4,8},{8,4},{12,0},{1,13},{5,9},{9,5},{13,1},{2,14},{6,10},... | collective-permute-start | bytes 417800 | tf_op jit(solution)/shard_map/ppermute | solution.py:304
  12.6 9.3 %collective-permute-start = (bf16[256,512]{1,0:T(8,128)(2,1)S(1)}, bf16[256,512]{1,0:T(8,128)(2,1)S(1)}, u32[]{:S(2)}, u32[]{:S(2)}) collective-permute-start(bf16[256,512]{1,0:T(8,128)(2,1)S(1)} %get-tuple-element.34.a_ref), channel_id=1, source_target_pairs={{0,2},{2,0},{1,3},{3,1},{4,6},{6,4},{5,7},{7,5},{8,10},{10,8},{9,1... | collective-permute-start | bytes 786440 | tf_op jit(solution)/shard_map/ppermute | solution.py:307
  15.6 12.2 %collective-permute-start.4 = (bf16[256,512]{1,0:T(8,128)(2,1)S(1)}, bf16[256,512]{1,0:T(8,128)(2,1)S(1)}, u32[]{:S(2)}, u32[]{:S(2)}) collective-permute-start(bf16[256,512]{1,0:T(8,128)(2,1)S(1)} %forward.5.a_ref), channel_id=1, source_target_pairs={{0,2},{2,0},{1,3},{3,1},{4,6},{6,4},{5,7},{7,5},{8,10},{10,8},{9,1... | collective-permute-start | bytes 786440 | tf_op jit(solution)/shard_map/ppermute | solution.py:307
  16.2 8.6 %collective-permute-start.3 = (bf16[272,256]{1,0:T(8,128)(2,1)S(1)}, bf16[272,256]{1,0:T(8,128)(2,1)S(1)}, u32[]{:S(2)}, u32[]{:S(2)}) collective-permute-start(bf16[272,256]{1,0:T(8,128)(2,1)S(1)} %pack.1.x_ref.refs_0_), channel_id=1, source_target_pairs={{0,8},{4,12},{8,0},{12,4},{1,9},{5,13},{9,1},{13,5},{2,10},{6,14},... | collective-permute-start | bytes 417800 | tf_op jit(solution)/shard_map/ppermute | solution.py:304
  18.3 8.9 %collective-permute-start.6 = (bf16[272,256]{1,0:T(8,128)(2,1)S(1)}, bf16[272,256]{1,0:T(8,128)(2,1)S(1)}, u32[]{:S(2)}, u32[]{:S(2)}) collective-permute-start(bf16[272,256]{1,0:T(8,128)(2,1)S(1)} %pack.1.x_ref.refs_0_), channel_id=1, source_target_pairs={{0,4},{4,0},{8,12},{12,8},{1,5},{5,1},{9,13},{13,9},{2,6},{6,2},{1... | collective-permute-start | bytes 417800 | tf_op jit(solution)/shard_map/ppermute | solution.py:304
  18.8 8.4 %collective-permute-start.7 = (bf16[272,256]{1,0:T(8,128)(2,1)S(1)}, bf16[272,256]{1,0:T(8,128)(2,1)S(1)}, u32[]{:S(2)}, u32[]{:S(2)}) collective-permute-start(bf16[272,256]{1,0:T(8,128)(2,1)S(1)} %pack.1.x_ref.refs_0_), channel_id=1, source_target_pairs={{0,1},{1,0},{2,3},{3,2},{4,5},{5,4},{6,7},{7,6},{8,9},{9,8},{10,11... | collective-permute-start | bytes 417800 | tf_op jit(solution)/shard_map/ppermute | solution.py:307
  22.0 10.2 %collective-permute-start.1 = (bf16[256,512]{1,0:T(8,128)(2,1)S(1)}, bf16[256,512]{1,0:T(8,128)(2,1)S(1)}, u32[]{:S(2)}, u32[]{:S(2)}) collective-permute-start(bf16[256,512]{1,0:T(8,128)(2,1)S(1)} %both.2.refs_0_), channel_id=1, source_target_pairs={{0,4},{4,0},{8,12},{12,8},{1,5},{5,1},{9,13},{13,9},{2,6},{6,2},{1... | collective-permute-start | bytes 786440 | tf_op jit(solution)/shard_map/ppermute | solution.py:304
  26.1 7.3 %collective-permute-start.5 = (bf16[256,512]{1,0:T(8,128)(2,1)S(1)}, bf16[256,512]{1,0:T(8,128)(2,1)S(1)}, u32[]{:S(2)}, u32[]{:S(2)}) collective-permute-start(bf16[256,512]{1,0:T(8,128)(2,1)S(1)} %forward.4.refs_2_), channel_id=1, source_target_pairs={{0,2},{2,0},{1,3},{3,1},{4,6},{6,4},{5,7},{7,5},{8,10},{10,8},{9,1... | collective-permute-start | bytes 786440 | tf_op jit(solution)/shard_map/ppermute | solution.py:307
  27.2 1.4 %collective-permute-start.8 = (bf16[272,256]{1,0:T(8,128)(2,1)S(1)}, bf16[272,256]{1,0:T(8,128)(2,1)S(1)}, u32[]{:S(2)}, u32[]{:S(2)}) collective-permute-start(bf16[272,256]{1,0:T(8,128)(2,1)S(1)} %collective-permute-done.6.refs_1_), channel_id=1, source_target_pairs={{0,1},{1,0},{2,3},{3,2},{4,5},{5,4},{6,7},{7,6},{8,9},{9,8},{10,11... | collective-permute-start | bytes 417800 | tf_op jit(solution)/shard_map/ppermute | solution.py:307
  27.2 1.6 %collective-permute-start.10 = (bf16[272,256]{1,0:T(8,128)(2,1)S(1)}, bf16[272,256]{1,0:T(8,128)(2,1)S(1)}, u32[]{:S(2)}, u32[]{:S(2)}) collective-permute-start(bf16[272,256]{1,0:T(8,128)(2,1)S(1)} %collective-permute-done.2.x_ref.refs_3_), channel_id=1, source_target_pairs={{0,1},{1,0},{2,3},{3,2},{4,5},{5,4},{6,7},{7,6},{8,9},{9,8},{10,11... | collective-permute-start | bytes 417800 | tf_op jit(solution)/shard_map/ppermute | solution.py:307
  27.7 1.4 %collective-permute-start.9 = (bf16[272,256]{1,0:T(8,128)(2,1)S(1)}, bf16[272,256]{1,0:T(8,128)(2,1)S(1)}, u32[]{:S(2)}, u32[]{:S(2)}) collective-permute-start(bf16[272,256]{1,0:T(8,128)(2,1)S(1)} %collective-permute-done.3.x_ref.refs_2_), channel_id=1, source_target_pairs={{0,1},{1,0},{2,3},{3,2},{4,5},{5,4},{6,7},{7,6},{8,9},{9,8},{10,11... | collective-permute-start | bytes 417800 | tf_op jit(solution)/shard_map/ppermute | solution.py:307
  28.6 4.9 %collective-permute-start.11 = (bf16[256,512]{1,0:T(8,128)(2,1)S(1)}, bf16[256,512]{1,0:T(8,128)(2,1)S(1)}, u32[]{:S(2)}, u32[]{:S(2)}) collective-permute-start(bf16[256,512]{1,0:T(8,128)(2,1)S(1)} %both.2.refs_0_), channel_id=1, source_target_pairs={{0,1},{1,0},{2,3},{3,2},{4,5},{5,4},{6,7},{7,6},{8,9},{9,8},{10,11... | collective-permute-start | bytes 786440 | tf_op jit(solution)/shard_map/ppermute | solution.py:307
  28.8 4.7 %collective-permute-start.13 = (bf16[256,512]{1,0:T(8,128)(2,1)S(1)}, bf16[256,512]{1,0:T(8,128)(2,1)S(1)}, u32[]{:S(2)}, u32[]{:S(2)}) collective-permute-start(bf16[256,512]{1,0:T(8,128)(2,1)S(1)} %forward.4.refs_2_), channel_id=1, source_target_pairs={{0,1},{1,0},{2,3},{3,2},{4,5},{5,4},{6,7},{7,6},{8,9},{9,8},{10,11... | collective-permute-start | bytes 786440 | tf_op jit(solution)/shard_map/ppermute | solution.py:307
  29.1 4.4 %collective-permute-start.14 = (bf16[256,512]{1,0:T(8,128)(2,1)S(1)}, bf16[256,512]{1,0:T(8,128)(2,1)S(1)}, u32[]{:S(2)}, u32[]{:S(2)}) collective-permute-start(bf16[256,512]{1,0:T(8,128)(2,1)S(1)} %both.3.refs_3_), channel_id=1, source_target_pairs={{0,1},{1,0},{2,3},{3,2},{4,5},{5,4},{6,7},{7,6},{8,9},{9,8},{10,11... | collective-permute-start | bytes 786440 | tf_op jit(solution)/shard_map/ppermute | solution.py:307
  32.2 1.6 %collective-permute-start.12 = (bf16[256,512]{1,0:T(8,128)(2,1)S(1)}, bf16[256,512]{1,0:T(8,128)(2,1)S(1)}, u32[]{:S(2)}, u32[]{:S(2)}) collective-permute-start(bf16[256,512]{1,0:T(8,128)(2,1)S(1)} %collective-permute-done.1.refs_1_), channel_id=1, source_target_pairs={{0,1},{1,0},{2,3},{3,2},{4,5},{5,4},{6,7},{7,6},{8,9},{9,8},{10,11... | collective-permute-start | bytes 786440 | tf_op jit(solution)/shard_map/ppermute | solution.py:307
  33.4 1.5 %collective-permute-start.15 = (bf16[256,512]{1,0:T(8,128)(2,1)S(1)}, bf16[256,512]{1,0:T(8,128)(2,1)S(1)}, u32[]{:S(2)}, u32[]{:S(2)}) collective-permute-start(bf16[256,512]{1,0:T(8,128)(2,1)S(1)} %collective-permute-done.5.refs_4_), channel_id=1, source_target_pairs={{0,1},{1,0},{2,3},{3,2},{4,5},{5,4},{6,7},{7,6},{8,9},{9,8},{10,11... | collective-permute-start | bytes 786440 | tf_op jit(solution)/shard_map/ppermute | solution.py:307
  35.0 5.7 %copy-start = (bf16[256,2048]{1,0:T(8,128)(2,1)S(1)}, bf16[256,2048]{1,0:T(8,128)(2,1)}, u32[]{:S(2)}) copy-start(bf16[256,2048]{1,0:T(8,128)(2,1)} %first.2) | copy-start | bytes 3145732
  35.0 5.7 %copy-start.1 = (bf16[2048,256]{1,0:T(8,128)(2,1)S(1)}, bf16[2048,256]{1,0:T(8,128)(2,1)}, u32[]{:S(2)}) copy-start(bf16[2048,256]{1,0:T(8,128)(2,1)} %second.2) | copy-start | bytes 3145732
  35.0 5.7 %copy-start.2 = (bf16[256,2048]{1,0:T(8,128)(2,1)S(1)}, bf16[256,2048]{1,0:T(8,128)(2,1)}, u32[]{:S(2)}) copy-start(bf16[256,2048]{1,0:T(8,128)(2,1)} %first.3) | copy-start | bytes 3145732
  35.0 5.7 %copy-start.3 = (bf16[2048,256]{1,0:T(8,128)(2,1)S(1)}, bf16[2048,256]{1,0:T(8,128)(2,1)}, u32[]{:S(2)}) copy-start(bf16[2048,256]{1,0:T(8,128)(2,1)} %second.3) | copy-start | bytes 3145732
  40.1 6.9 %collective-permute-start.16 = (bf16[1024,512]{1,0:T(8,128)(2,1)S(1)}, bf16[1024,512]{1,0:T(8,128)(2,1)S(1)}, u32[]{:S(2)}, u32[]{:S(2)}) collective-permute-start(bf16[1024,512]{1,0:T(8,128)(2,1)S(1)} %contrast.1.grads_ref), channel_id=1, source_target_pairs={{0,1},{1,0},{2,3},{3,2},{4,5},{5,4},{6,7},{7,6},{8,9},{9,8},{10,11... | collective-permute-start | bytes 3145736 | tf_op jit(solution)/shard_map/ppermute | solution.py:307
  40.3 10.8 %collective-permute-start.19 = (bf16[1024,256]{1,0:T(8,128)(2,1)S(1)}, bf16[1024,256]{1,0:T(8,128)(2,1)S(1)}, u32[]{:S(2)}, u32[]{:S(2)}) collective-permute-start(bf16[1024,256]{1,0:T(8,128)(2,1)S(1)} %get-tuple-element.47.goals_ref), channel_id=1, source_target_pairs={{0,1},{1,0},{2,3},{3,2},{4,5},{5,4},{6,7},{7,6},{8,9},{9,8},{10,11... | collective-permute-start | bytes 1572872 | tf_op jit(solution)/shard_map/ppermute | solution.py:307
  50.5 6.0 %collective-permute-start.17 = (bf16[256,1024]{1,0:T(8,128)(2,1)S(1)}, bf16[256,1024]{1,0:T(8,128)(2,1)S(1)}, u32[]{:S(2)}, u32[]{:S(2)}) collective-permute-start(bf16[256,1024]{1,0:T(8,128)(2,1)S(1)} %get-tuple-element.50.refs_0_), channel_id=1, source_target_pairs={{0,1},{1,0},{2,3},{3,2},{4,5},{5,4},{6,7},{7,6},{8,9},{9,8},{10,11... | collective-permute-start | bytes 1572872 | tf_op jit(solution)/shard_map/ppermute | solution.py:307
  50.7 5.8 %collective-permute-start.18 = (bf16[1024,256]{1,0:T(8,128)(2,1)S(1)}, bf16[1024,256]{1,0:T(8,128)(2,1)S(1)}, u32[]{:S(2)}, u32[]{:S(2)}) collective-permute-start(bf16[1024,256]{1,0:T(8,128)(2,1)S(1)} %get-tuple-element.51.refs_1_), channel_id=1, source_target_pairs={{0,1},{1,0},{2,3},{3,2},{4,5},{5,4},{6,7},{7,6},{8,9},{9,8},{10,11... | collective-permute-start | bytes 1572872 | tf_op jit(solution)/shard_map/ppermute | solution.py:307
  55.9 3.2 %collective-permute-start.20 = (bf16[256,1024]{1,0:T(8,128)(2,1)S(1)}, bf16[256,1024]{1,0:T(8,128)(2,1)S(1)}, u32[]{:S(2)}, u32[]{:S(2)}) collective-permute-start(bf16[256,1024]{1,0:T(8,128)(2,1)S(1)} %get-tuple-element.54.refs_2_), channel_id=1, source_target_pairs={{0,1},{1,0},{2,3},{3,2},{4,5},{5,4},{6,7},{7,6},{8,9},{9,8},{10,11... | collective-permute-start | bytes 1572872 | tf_op jit(solution)/shard_map/ppermute | solution.py:307
  56.1 3.1 %collective-permute-start.21 = (bf16[1024,256]{1,0:T(8,128)(2,1)S(1)}, bf16[1024,256]{1,0:T(8,128)(2,1)S(1)}, u32[]{:S(2)}, u32[]{:S(2)}) collective-permute-start(bf16[1024,256]{1,0:T(8,128)(2,1)S(1)} %get-tuple-element.55.refs_3_), channel_id=1, source_target_pairs={{0,1},{1,0},{2,3},{3,2},{4,5},{5,4},{6,7},{7,6},{8,9},{9,8},{10,11... | collective-permute-start | bytes 1572872 | tf_op jit(solution)/shard_map/ppermute | solution.py:307

commit v10 on v9

--- a/solution.py
+++ b/solution.py
@@ -186,10 +186,11 @@
     diagonal = lax.broadcasted_iota(jnp.int32, (batch, batch), 0) == lax.broadcasted_iota(
         jnp.int32, (batch, batch), 1
     )
+    psi_all[:half, :] = dot(pick_ref[...], psi_all[...]).astype(BF)
     for r in range(n_rep):
         own = slice(r * batch, (r + 1) * batch)
         ep_row = ep_ref[:, own]
-        psi = dot(pick_ref[own, :], psi_all[...]).astype(BF)
+        psi = psi_all[own, :]
         phi = phi_all[own, :]
         scores = lax.dot_general(phi, psi, (((1,), (1,)), ((), ())), preferred_element_type=F32)
         kept = (column(ep_row) != ep_row) | diagonal
@@ -208,7 +209,7 @@
     first_t = first_ref[:, pl.ds(at, quarter)].T
     second = second_ref[pl.ds(at, quarter), :]
     grad = grads_ref[:, k * emb : (k + 1) * emb]
-    chunk = 512
+    chunk = 256
     for c in range(0, rows, chunk):
         cols = slice(c, c + chunk)
         hidden = dot(first_t, rows_ref[cols, :].T)
@@ -327,7 +328,7 @@
     there3 = swap(part3, "rep")
 
     sums = {0: both(part0, there0)}
-    sums[1] = across(sums[0], 1)
+    sums[1] = across(after(sums[0], got[2]), 1)
     part2 = forward(after(got[2], sums[0]), held, rows_dev)
     there2 = swap(part2, "rep")
     sums[3] = both(part3, there3)

time: 61.5 us -> 59.1 us (0.961)
  Pallas kernels: 35.2 us -> 34.1 us
  waiting for transfers between devices: 8.92 us -> 8.17 us
    ppermute x4, waiting for transfers between devices: 2.68 us -> 0.93 us  [across(): return lax.ppermute(x, 'blk', [(i, i ^ k) for i in range(n_blk)])]
    pallas_call x13, Pallas kernels: 35.2 us -> 34.1 us  [kernel(): pl.pallas_call(body, in_specs=specs, out_specs=[HBM if i in hbm_out else...]
    ppermute x4, starting transfers between devices: 7.86 us -> 6.84 us  [across(): return lax.ppermute(x, 'blk', [(i, i ^ k) for i in range(n_blk)])]
    ppermute x18, waiting for transfers between devices: 6.25 us -> 7.25 us  [swap(): return lax.ppermute(x, axis, [(0, 1), (1, 0)])]
    ppermute x18, starting transfers between devices: 6.58 us -> 7.23 us  [swap(): return lax.ppermute(x, axis, [(0, 1), (1, 0)])]
  transfers between devices with their start and end apart: 22 -> 22, of which waited for: 7 -> 9; matrix products, arithmetic and copies ran while one was open for 0% -> 0% of each run, Pallas kernels for 45% -> 46%
where the time goes in v10:
time: 59.1 us; the launch traced here: 59 us
  Pallas kernels  34.1 us (58%)
  starting transfers between devices  14.1 us (24%)
  waiting for transfers between devices  8.17 us (14%)
  between operations  0.94 us (2%)
  local copies, waits for them, and re-layouts  0.92 us (2%)
  other arithmetic  0.8 us (1%)
    pallas_call x13, Pallas kernels, kernel(): pl.pallas_call(body, in_specs=specs, out_specs=[HBM if i in hbm_out else...  34.1 us
    ppermute x18, waiting for transfers between devices, swap(): return lax.ppermute(x, axis, [(0, 1), (1, 0)])  7.25 us
    ppermute x18, starting transfers between devices, swap(): return lax.ppermute(x, axis, [(0, 1), (1, 0)])  7.23 us
    ppermute x4, starting transfers between devices, across(): return lax.ppermute(x, 'blk', [(i, i ^ k) for i in range(n_blk)])  6.84 us
  transfers between devices with their start and end apart: 22, of which 9 were waited for; matrix products, arithmetic and copies ran while one was open for 0% of the time, Pallas kernels for 46%

profile of v10, /device:TPU:0, one launch (start us, length us, event | category | flops | bytes accessed | tf_op | source)
XLA Modules:
  0.0 59.0 jit_solution(10603004977404807674)
XLA Ops:
  0.6 0.1 pad_add_fusion.1.pos_ref
  0.7 0.7 %pad_add_fusion.own_ref = s32[3,256]{1,0:T(4,128)S(1)} fusion(s32[1,256]{1,0:T(1,128)} %bitcast.5, s32[1,256]{1,0:T(1,128)} %bitcast.6, s32[1,256]{1,0:T(1,128)} %bitcast.7), kind=kLoop, calls=%fused_computation | loop fusion | flops 1536 | bytes 6144 | tf_op jit(solution)/shard_map/stack | solution.py:318
  1.4 0.9 %copy-done.4 = bf16[256,256]{1,0:T(8,128)(2,1)S(1)} copy-done((bf16[256,256]{1,0:T(8,128)(2,1)S(1)}, bf16[256,256]{1,0:T(8,128)(2,1)}, u32[]{:S(2)}) %copy-start.4) | copy-done | bytes 131096
  2.3 0.6 pack.1.x_ref.refs_0_
  2.9 5.1 %collective-permute-start.1 = (bf16[272,256]{1,0:T(8,128)(2,1)S(1)}, bf16[272,256]{1,0:T(8,128)(2,1)S(1)}, u32[]{:S(2)}, u32[]{:S(2)}) collective-permute-start(bf16[272,256]{1,0:T(8,128)(2,1)S(1)} %pack.1.x_ref.refs_0_), channel_id=1, source_target_pairs={{0,12},{4,8},{8,4},{12,0},{1,13},{5,9},{9,5},{13,1},{2,14},{6,10},... | collective-permute-start | bytes 417800 | tf_op jit(solution)/shard_map/ppermute | solution.py:305
  8.0 4.6 %forward.3 = (bf16[256,512]{1,0:T(8,128)(2,1)S(1)}, bf16[256,2048]{1,0:T(8,128)(2,1)S(1)}, bf16[256,2048]{1,0:T(8,128)(2,1)S(1)}, bf16[2048,256]{1,0:T(8,128)(2,1)S(1)}, bf16[2048,256]{1,0:T(8,128)(2,1)S(1)}) custom-call(s32[2]{0:T(128)S(1)} %pad_add_fusion.1.pos_ref, bf16[272,256]{1,0:T(8,128)(2,1)S(1)} %pack.1.x_ref.refs_0_, bf16[256,2048]{1,0:T(8,128)(2,1)} %first.2, ...), custom_call_target="tpu_custom_call" | custom-call | tf_op jit(solution)/shard_map/forward/pallas_call | solution.py:34
  12.6 1.6 %collective-permute-start = (bf16[256,512]{1,0:T(8,128)(2,1)S(1)}, bf16[256,512]{1,0:T(8,128)(2,1)S(1)}, u32[]{:S(2)}, u32[]{:S(2)}) collective-permute-start(bf16[256,512]{1,0:T(8,128)(2,1)S(1)} %get-tuple-element.35.a_ref), channel_id=1, source_target_pairs={{0,2},{2,0},{1,3},{3,1},{4,6},{6,4},{5,7},{7,5},{8,10},{10,8},{9,1... | collective-permute-start | bytes 786440 | tf_op jit(solution)/shard_map/ppermute | solution.py:308
  14.2 0.0 collective-permute-done.1.x_ref.refs_3_
  14.2 1.2 %collective-permute-start.2 = (bf16[272,256]{1,0:T(8,128)(2,1)S(1)}, bf16[272,256]{1,0:T(8,128)(2,1)S(1)}, u32[]{:S(2)}, u32[]{:S(2)}) collective-permute-start(bf16[272,256]{1,0:T(8,128)(2,1)S(1)} %pack.1.x_ref.refs_0_), channel_id=1, source_target_pairs={{0,8},{4,12},{8,0},{12,4},{1,9},{5,13},{9,1},{13,5},{2,10},{6,14},... | collective-permute-start | bytes 417800 | tf_op jit(solution)/shard_map/ppermute | solution.py:305
  15.4 1.4 %forward.5.a_ref = bf16[256,512]{1,0:T(8,128)(2,1)S(1)} custom-call(bf16[272,256]{1,0:T(8,128)(2,1)S(1)} %collective-permute-done.1.x_ref.refs_3_, bf16[256,2048]{1,0:T(8,128)(2,1)S(1)} %get-tuple-element.39.refs_0_, bf16[256,2048]{1,0:T(8,128)(2,1)S(1)} %get-tuple-element.40.refs_1_, bf16[2048,256]{1,0:T(8,128)(2,1)S(1)} %get-tuple-element.41.refs_2_, ...), custom_call_target="tpu_custom_call" | custom-call | tf_op jit(solution)/shard_map/forward/pallas_call | solution.py:34
  16.8 1.6 %collective-permute-start.4 = (bf16[256,512]{1,0:T(8,128)(2,1)S(1)}, bf16[256,512]{1,0:T(8,128)(2,1)S(1)}, u32[]{:S(2)}, u32[]{:S(2)}) collective-permute-start(bf16[256,512]{1,0:T(8,128)(2,1)S(1)} %forward.5.a_ref), channel_id=1, source_target_pairs={{0,2},{2,0},{1,3},{3,1},{4,6},{6,4},{5,7},{7,5},{8,10},{10,8},{9,1... | collective-permute-start | bytes 786440 | tf_op jit(solution)/shard_map/ppermute | solution.py:308
  18.3 0.5 collective-permute-start.6
  18.8 0.0 collective-permute-start.7
  18.8 3.1 %collective-permute-done.b_ref = bf16[256,512]{1,0:T(8,128)(2,1)S(1)} collective-permute-done((bf16[256,512]{1,0:T(8,128)(2,1)S(1)}, bf16[256,512]{1,0:T(8,128)(2,1)S(1)}, u32[]{:S(2)}, u32[]{:S(2)}) %collective-permute-start) | collective-permute-done | bytes 262176 | tf_op jit(solution)/shard_map/ppermute | solution.py:308
  21.9 0.1 both.2.refs_0_
  22.0 0.5 collective-permute-done.2.x_ref.refs_2_
  22.5 1.4 %forward.4.refs_2_ = bf16[256,512]{1,0:T(8,128)(2,1)S(1)} custom-call(bf16[272,256]{1,0:T(8,128)(2,1)S(1)} %collective-permute-done.2.x_ref.refs_2_, bf16[256,2048]{1,0:T(8,128)(2,1)S(1)} %get-tuple-element.39.refs_0_, bf16[256,2048]{1,0:T(8,128)(2,1)S(1)} %get-tuple-element.40.refs_1_, bf16[2048,256]{1,0:T(8,128)(2,1)S(1)} %get-tuple-element.41.refs_2_, ...), custom_call_target="tpu_custom_call" | custom-call | tf_op jit(solution)/shard_map/forward/pallas_call | solution.py:34
  23.9 1.1 %collective-permute-start.5 = (bf16[256,512]{1,0:T(8,128)(2,1)S(1)}, bf16[256,512]{1,0:T(8,128)(2,1)S(1)}, u32[]{:S(2)}, u32[]{:S(2)}) collective-permute-start(bf16[256,512]{1,0:T(8,128)(2,1)S(1)} %forward.4.refs_2_), channel_id=1, source_target_pairs={{0,2},{2,0},{1,3},{3,1},{4,6},{6,4},{5,7},{7,5},{8,10},{10,8},{9,1... | collective-permute-start | bytes 786440 | tf_op jit(solution)/shard_map/ppermute | solution.py:308
  25.0 0.0 collective-permute-start.3
  25.0 0.0 collective-permute-done.6.refs_1_
  25.0 0.0 collective-permute-start.8
  25.0 0.0 collective-permute-done.7.refs_4_
  25.0 0.5 collective-permute-start.10
  25.5 0.5 collective-permute-done.4.b_ref
  26.1 0.0 collective-permute-start.9
  26.1 0.1 both.3.refs_3_
  26.1 0.2 collective-permute-done.8.refs_5_
  26.4 0.3 collective-permute-start.11
  26.7 0.0 collective-permute-done.10.refs_7_
  26.7 0.2 collective-permute-start.13
  26.9 0.5 collective-permute-done.9.refs_6_
  27.4 0.1 collective-permute-start.14
  27.6 2.9 %arrange.1 = (bf16[1024,256]{1,0:T(8,128)(2,1)S(1)}, bf16[1024,256]{1,0:T(8,128)(2,1)S(1)}, bf16[1024,256]{1,0:T(8,128)(2,1)S(1)}, bf16[1024,2048]{1,0:T(8,128)(2,1)S(1)}, f32[1,1024]{1,0:T(1,128)S(1)}) custom-call(s32[2]{0:T(128)S(1)} %pad_add_fusion.1.pos_ref, bf16[272,256]{1,0:T(8,128)(2,1)S(1)} %pack.1.x_ref.refs_0_, ...), custom_call_target="tpu_custom_call" | custom-call | tf_op jit(solution)/shard_map/arrange/pallas_call | solution.py:34
  30.5 1.4 %collective-permute-done.5.refs_4_ = bf16[256,512]{1,0:T(8,128)(2,1)S(1)} collective-permute-done((bf16[256,512]{1,0:T(8,128)(2,1)S(1)}, bf16[256,512]{1,0:T(8,128)(2,1)S(1)}, u32[]{:S(2)}, u32[]{:S(2)}) %collective-permute-start.5) | collective-permute-done | bytes 262176 | tf_op jit(solution)/shard_map/ppermute | solution.py:308
  31.9 0.0 collective-permute-start.15
  31.9 0.4 collective-permute-done.3.refs_1_
  32.3 0.1 collective-permute-start.12
  32.4 0.0 collective-permute-done.11.refs_5_
  32.4 0.0 collective-permute-done.13.refs_7_
  32.4 0.0 collective-permute-done.14.refs_8_
  32.4 1.0 %collective-permute-done.15.refs_9_ = bf16[256,512]{1,0:T(8,128)(2,1)S(1)} collective-permute-done((bf16[256,512]{1,0:T(8,128)(2,1)S(1)}, bf16[256,512]{1,0:T(8,128)(2,1)S(1)}, u32[]{:S(2)}, u32[]{:S(2)}) %collective-permute-start.15) | collective-permute-done | bytes 262176 | tf_op jit(solution)/shard_map/ppermute | solution.py:308
  33.4 0.4 collective-permute-done.12.refs_6_
  33.8 4.7 %contrast.1.grads_ref = bf16[1024,512]{1,0:T(8,128)(2,1)S(1)} custom-call(s32[2]{0:T(128)S(1)} %pad_add_fusion.1.pos_ref, bf16[256,512]{1,0:T(8,128)(2,1)S(1)} %both.2.refs_0_, bf16[256,512]{1,0:T(8,128)(2,1)S(1)} %collective-permute-done.3.refs_1_, bf16[256,512]{1,0:T(8,128)(2,1)S(1)} %forward.4.refs_2_, bf16[256,512]{1,0:T(8,128)(2,1)S(1)} %both.3.refs_3_, ...), custom_call_target="tpu_custom_call" | custom-call | tf_op jit(solution)/shard_map/contrast/pallas_call | solution.py:34
  38.5 0.2 collective-permute-start.16
  38.7 0.4 collective-permute-start.19
  39.1 0.0 copy-done
  39.1 0.0 copy-done.1
  39.1 0.0 copy-done.2
  39.1 0.0 copy-done.3
  39.1 5.9 %mine.1 = (f32[1024,256]{1,0:T(8,128)S(1)}, f32[1024,256]{1,0:T(8,128)S(1)}, f32[1024,256]{1,0:T(8,128)S(1)}, f32[1024,256]{1,0:T(8,128)S(1)}) custom-call(s32[2]{0:T(128)S(1)} %pad_add_fusion.1.pos_ref, bf16[256,2048]{1,0:T(8,128)(2,1)S(1)} %copy-done, bf16[256,2048]{1,0:T(8,128)(2,1)S(1)} %copy-done.2, bf16[2048,256]{1,0:T(8,128)(2,1)S(1)} %copy-done.1, ...), custom_call_target="tpu_custom_call" | custom-call | flops 4294967296 | tf_op jit(solution)/shard_map/mine/pallas_call | solution.py:34
  45.1 0.0 collective-permute-done.16.grads_ref
  45.1 3.3 %other_state.1 = (bf16[256,1024]{1,0:T(8,128)(2,1)S(1)}, bf16[1024,256]{1,0:T(8,128)(2,1)S(1)}) custom-call(s32[2]{0:T(128)S(1)} %pad_add_fusion.1.pos_ref, bf16[256,2048]{1,0:T(8,128)(2,1)S(1)} %copy-done, bf16[2048,256]{1,0:T(8,128)(2,1)S(1)} %copy-done.1, bf16[1024,512]{1,0:T(8,128)(2,1)S(1)} %collective-permute-done.16.grads_ref, ...), custom_call_target="tpu_custom_call" | custom-call | flops 2147483648 | tf_op jit(solution)/shard_map/other_state/pallas_call | solution.py:34
  48.4 0.2 collective-permute-start.17
  48.6 0.4 collective-permute-start.18
  49.0 0.0 collective-permute-done.19.rows_ref
  49.0 4.6 %other_goal.1 = (bf16[256,1024]{1,0:T(8,128)(2,1)S(1)}, bf16[1024,256]{1,0:T(8,128)(2,1)S(1)}, f32[256,2048]{1,0:T(8,128)}, f32[2048,256]{1,0:T(8,128)}) custom-call(s32[2]{0:T(128)S(1)} %pad_add_fusion.1.pos_ref, bf16[256,2048]{1,0:T(8,128)(2,1)S(1)} %copy-done.2, bf16[2048,256]{1,0:T(8,128)(2,1)S(1)} %copy-done.3, ...), custom_call_target="tpu_custom_call" | custom-call | flops 2147483648 | tf_op jit(solution)/shard_map/other_goal/pallas_call | solution.py:34
  53.6 0.2 collective-permute-start.20
  53.8 0.4 collective-permute-start.21
  54.2 0.0 collective-permute-done.17.refs_0_
  54.2 0.0 collective-permute-done.18.refs_1_
  54.2 2.6 %finish.2 = (f32[256,2048]{1,0:T(8,128)}, f32[2048,256]{1,0:T(8,128)}, f32[256,2048]{1,0:T(8,128)}, f32[2048,256]{1,0:T(8,128)}) custom-call(s32[2]{0:T(128)S(1)} %pad_add_fusion.1.pos_ref, bf16[256,1024]{1,0:T(8,128)(2,1)S(1)} %collective-permute-done.17.refs_0_, ...), custom_call_target="tpu_custom_call", output_to_operand_aliasing={{0}: (5, {}), {1}: (6, {})} | custom-call | tf_op jit(solution)/shard_map/finish/pallas_call | solution.py:34
  56.9 0.0 collective-permute-done.20.refs_0_
  56.9 0.0 collective-permute-done.21.refs_1_
  56.9 1.9 %finish.3 = (f32[256,2048]{1,0:T(8,128)}, f32[2048,256]{1,0:T(8,128)}) custom-call(s32[2]{0:T(128)S(1)} %pad_add_fusion.1.pos_ref, bf16[256,1024]{1,0:T(8,128)(2,1)S(1)} %collective-permute-done.20.refs_0_, bf16[1024,256]{1,0:T(8,128)(2,1)S(1)} %collective-permute-done.21.refs_1_, ...), custom_call_target="tpu_custom_call", output_to_operand_aliasing={{0}: (3, {}), {1}: (4, {})} | custom-call | tf_op jit(solution)/shard_map/finish/pallas_call | solution.py:34
  (5 shorter events, 0.0 us)
Async XLA Ops:
  1.4 0.9 %copy-start.4 = (bf16[256,256]{1,0:T(8,128)(2,1)S(1)}, bf16[256,256]{1,0:T(8,128)(2,1)}, u32[]{:S(2)}) copy-start(bf16[256,256]{1,0:T(8,128)(2,1)} %x_ref.1) | copy-start | bytes 393220
  2.9 11.3 %collective-permute-start.1 = (bf16[272,256]{1,0:T(8,128)(2,1)S(1)}, bf16[272,256]{1,0:T(8,128)(2,1)S(1)}, u32[]{:S(2)}, u32[]{:S(2)}) collective-permute-start(bf16[272,256]{1,0:T(8,128)(2,1)S(1)} %pack.1.x_ref.refs_0_), channel_id=1, source_target_pairs={{0,12},{4,8},{8,4},{12,0},{1,13},{5,9},{9,5},{13,1},{2,14},{6,10},... | collective-permute-start | bytes 417800 | tf_op jit(solution)/shard_map/ppermute | solution.py:305
  12.6 9.3 %collective-permute-start = (bf16[256,512]{1,0:T(8,128)(2,1)S(1)}, bf16[256,512]{1,0:T(8,128)(2,1)S(1)}, u32[]{:S(2)}, u32[]{:S(2)}) collective-permute-start(bf16[256,512]{1,0:T(8,128)(2,1)S(1)} %get-tuple-element.35.a_ref), channel_id=1, source_target_pairs={{0,2},{2,0},{1,3},{3,1},{4,6},{6,4},{5,7},{7,5},{8,10},{10,8},{9,1... | collective-permute-start | bytes 786440 | tf_op jit(solution)/shard_map/ppermute | solution.py:308
  14.2 8.3 %collective-permute-start.2 = (bf16[272,256]{1,0:T(8,128)(2,1)S(1)}, bf16[272,256]{1,0:T(8,128)(2,1)S(1)}, u32[]{:S(2)}, u32[]{:S(2)}) collective-permute-start(bf16[272,256]{1,0:T(8,128)(2,1)S(1)} %pack.1.x_ref.refs_0_), channel_id=1, source_target_pairs={{0,8},{4,12},{8,0},{12,4},{1,9},{5,13},{9,1},{13,5},{2,10},{6,14},... | collective-permute-start | bytes 417800 | tf_op jit(solution)/shard_map/ppermute | solution.py:305
  16.8 9.3 %collective-permute-start.4 = (bf16[256,512]{1,0:T(8,128)(2,1)S(1)}, bf16[256,512]{1,0:T(8,128)(2,1)S(1)}, u32[]{:S(2)}, u32[]{:S(2)}) collective-permute-start(bf16[256,512]{1,0:T(8,128)(2,1)S(1)} %forward.5.a_ref), channel_id=1, source_target_pairs={{0,2},{2,0},{1,3},{3,1},{4,6},{6,4},{5,7},{7,5},{8,10},{10,8},{9,1... | collective-permute-start | bytes 786440 | tf_op jit(solution)/shard_map/ppermute | solution.py:308
  18.3 6.7 %collective-permute-start.6 = (bf16[272,256]{1,0:T(8,128)(2,1)S(1)}, bf16[272,256]{1,0:T(8,128)(2,1)S(1)}, u32[]{:S(2)}, u32[]{:S(2)}) collective-permute-start(bf16[272,256]{1,0:T(8,128)(2,1)S(1)} %pack.1.x_ref.refs_0_), channel_id=1, source_target_pairs={{0,4},{4,0},{8,12},{12,8},{1,5},{5,1},{9,13},{13,9},{2,6},{6,2},{1... | collective-permute-start | bytes 417800 | tf_op jit(solution)/shard_map/ppermute | solution.py:305
  18.8 6.2 %collective-permute-start.7 = (bf16[272,256]{1,0:T(8,128)(2,1)S(1)}, bf16[272,256]{1,0:T(8,128)(2,1)S(1)}, u32[]{:S(2)}, u32[]{:S(2)}) collective-permute-start(bf16[272,256]{1,0:T(8,128)(2,1)S(1)} %pack.1.x_ref.refs_0_), channel_id=1, source_target_pairs={{0,1},{1,0},{2,3},{3,2},{4,5},{5,4},{6,7},{7,6},{8,9},{9,8},{10,11... | collective-permute-start | bytes 417800 | tf_op jit(solution)/shard_map/ppermute | solution.py:308
  23.9 8.0 %collective-permute-start.5 = (bf16[256,512]{1,0:T(8,128)(2,1)S(1)}, bf16[256,512]{1,0:T(8,128)(2,1)S(1)}, u32[]{:S(2)}, u32[]{:S(2)}) collective-permute-start(bf16[256,512]{1,0:T(8,128)(2,1)S(1)} %forward.4.refs_2_), channel_id=1, source_target_pairs={{0,2},{2,0},{1,3},{3,1},{4,6},{6,4},{5,7},{7,5},{8,10},{10,8},{9,1... | collective-permute-start | bytes 786440 | tf_op jit(solution)/shard_map/ppermute | solution.py:308
  25.0 7.3 %collective-permute-start.3 = (bf16[256,512]{1,0:T(8,128)(2,1)S(1)}, bf16[256,512]{1,0:T(8,128)(2,1)S(1)}, u32[]{:S(2)}, u32[]{:S(2)}) collective-permute-start(bf16[256,512]{1,0:T(8,128)(2,1)S(1)} %both.2.refs_0_), channel_id=1, source_target_pairs={{0,4},{4,0},{8,12},{12,8},{1,5},{5,1},{9,13},{13,9},{2,6},{6,2},{1... | collective-permute-start | bytes 786440 | tf_op jit(solution)/shard_map/ppermute | solution.py:305
  25.0 1.4 %collective-permute-start.8 = (bf16[272,256]{1,0:T(8,128)(2,1)S(1)}, bf16[272,256]{1,0:T(8,128)(2,1)S(1)}, u32[]{:S(2)}, u32[]{:S(2)}) collective-permute-start(bf16[272,256]{1,0:T(8,128)(2,1)S(1)} %collective-permute-done.6.refs_1_), channel_id=1, source_target_pairs={{0,1},{1,0},{2,3},{3,2},{4,5},{5,4},{6,7},{7,6},{8,9},{9,8},{10,11... | collective-permute-start | bytes 417800 | tf_op jit(solution)/shard_map/ppermute | solution.py:308
  25.0 1.7 %collective-permute-start.10 = (bf16[272,256]{1,0:T(8,128)(2,1)S(1)}, bf16[272,256]{1,0:T(8,128)(2,1)S(1)}, u32[]{:S(2)}, u32[]{:S(2)}) collective-permute-start(bf16[272,256]{1,0:T(8,128)(2,1)S(1)} %collective-permute-done.1.x_ref.refs_3_), channel_id=1, source_target_pairs={{0,1},{1,0},{2,3},{3,2},{4,5},{5,4},{6,7},{7,6},{8,9},{9,8},{10,11... | collective-permute-start | bytes 417800 | tf_op jit(solution)/shard_map/ppermute | solution.py:308
  26.1 1.4 %collective-permute-start.9 = (bf16[272,256]{1,0:T(8,128)(2,1)S(1)}, bf16[272,256]{1,0:T(8,128)(2,1)S(1)}, u32[]{:S(2)}, u32[]{:S(2)}) collective-permute-start(bf16[272,256]{1,0:T(8,128)(2,1)S(1)} %collective-permute-done.2.x_ref.refs_2_), channel_id=1, source_target_pairs={{0,1},{1,0},{2,3},{3,2},{4,5},{5,4},{6,7},{7,6},{8,9},{9,8},{10,11... | collective-permute-start | bytes 417800 | tf_op jit(solution)/shard_map/ppermute | solution.py:308
  26.4 6.0 %collective-permute-start.11 = (bf16[256,512]{1,0:T(8,128)(2,1)S(1)}, bf16[256,512]{1,0:T(8,128)(2,1)S(1)}, u32[]{:S(2)}, u32[]{:S(2)}) collective-permute-start(bf16[256,512]{1,0:T(8,128)(2,1)S(1)} %both.2.refs_0_), channel_id=1, source_target_pairs={{0,1},{1,0},{2,3},{3,2},{4,5},{5,4},{6,7},{7,6},{8,9},{9,8},{10,11... | collective-permute-start | bytes 786440 | tf_op jit(solution)/shard_map/ppermute | solution.py:308
  26.7 5.7 %collective-permute-start.13 = (bf16[256,512]{1,0:T(8,128)(2,1)S(1)}, bf16[256,512]{1,0:T(8,128)(2,1)S(1)}, u32[]{:S(2)}, u32[]{:S(2)}) collective-permute-start(bf16[256,512]{1,0:T(8,128)(2,1)S(1)} %forward.4.refs_2_), channel_id=1, source_target_pairs={{0,1},{1,0},{2,3},{3,2},{4,5},{5,4},{6,7},{7,6},{8,9},{9,8},{10,11... | collective-permute-start | bytes 786440 | tf_op jit(solution)/shard_map/ppermute | solution.py:308
  27.4 5.0 %collective-permute-start.14 = (bf16[256,512]{1,0:T(8,128)(2,1)S(1)}, bf16[256,512]{1,0:T(8,128)(2,1)S(1)}, u32[]{:S(2)}, u32[]{:S(2)}) collective-permute-start(bf16[256,512]{1,0:T(8,128)(2,1)S(1)} %both.3.refs_3_), channel_id=1, source_target_pairs={{0,1},{1,0},{2,3},{3,2},{4,5},{5,4},{6,7},{7,6},{8,9},{9,8},{10,11... | collective-permute-start | bytes 786440 | tf_op jit(solution)/shard_map/ppermute | solution.py:308
  31.9 1.5 %collective-permute-start.15 = (bf16[256,512]{1,0:T(8,128)(2,1)S(1)}, bf16[256,512]{1,0:T(8,128)(2,1)S(1)}, u32[]{:S(2)}, u32[]{:S(2)}) collective-permute-start(bf16[256,512]{1,0:T(8,128)(2,1)S(1)} %collective-permute-done.5.refs_4_), channel_id=1, source_target_pairs={{0,1},{1,0},{2,3},{3,2},{4,5},{5,4},{6,7},{7,6},{8,9},{9,8},{10,11... | collective-permute-start | bytes 786440 | tf_op jit(solution)/shard_map/ppermute | solution.py:308
  32.3 1.5 %collective-permute-start.12 = (bf16[256,512]{1,0:T(8,128)(2,1)S(1)}, bf16[256,512]{1,0:T(8,128)(2,1)S(1)}, u32[]{:S(2)}, u32[]{:S(2)}) collective-permute-start(bf16[256,512]{1,0:T(8,128)(2,1)S(1)} %collective-permute-done.3.refs_1_), channel_id=1, source_target_pairs={{0,1},{1,0},{2,3},{3,2},{4,5},{5,4},{6,7},{7,6},{8,9},{9,8},{10,11... | collective-permute-start | bytes 786440 | tf_op jit(solution)/shard_map/ppermute | solution.py:308
  33.8 5.3 %copy-start = (bf16[256,2048]{1,0:T(8,128)(2,1)S(1)}, bf16[256,2048]{1,0:T(8,128)(2,1)}, u32[]{:S(2)}) copy-start(bf16[256,2048]{1,0:T(8,128)(2,1)} %first.2) | copy-start | bytes 3145732
  33.8 5.3 %copy-start.1 = (bf16[2048,256]{1,0:T(8,128)(2,1)S(1)}, bf16[2048,256]{1,0:T(8,128)(2,1)}, u32[]{:S(2)}) copy-start(bf16[2048,256]{1,0:T(8,128)(2,1)} %second.2) | copy-start | bytes 3145732
  33.8 5.3 %copy-start.2 = (bf16[256,2048]{1,0:T(8,128)(2,1)S(1)}, bf16[256,2048]{1,0:T(8,128)(2,1)}, u32[]{:S(2)}) copy-start(bf16[256,2048]{1,0:T(8,128)(2,1)} %first.3) | copy-start | bytes 3145732
  33.8 5.3 %copy-start.3 = (bf16[2048,256]{1,0:T(8,128)(2,1)S(1)}, bf16[2048,256]{1,0:T(8,128)(2,1)}, u32[]{:S(2)}) copy-start(bf16[2048,256]{1,0:T(8,128)(2,1)} %second.3) | copy-start | bytes 3145732
  38.5 6.5 %collective-permute-start.16 = (bf16[1024,512]{1,0:T(8,128)(2,1)S(1)}, bf16[1024,512]{1,0:T(8,128)(2,1)S(1)}, u32[]{:S(2)}, u32[]{:S(2)}) collective-permute-start(bf16[1024,512]{1,0:T(8,128)(2,1)S(1)} %contrast.1.grads_ref), channel_id=1, source_target_pairs={{0,1},{1,0},{2,3},{3,2},{4,5},{5,4},{6,7},{7,6},{8,9},{9,8},{10,11... | collective-permute-start | bytes 3145736 | tf_op jit(solution)/shard_map/ppermute | solution.py:308
  38.7 10.2 %collective-permute-start.19 = (bf16[1024,256]{1,0:T(8,128)(2,1)S(1)}, bf16[1024,256]{1,0:T(8,128)(2,1)S(1)}, u32[]{:S(2)}, u32[]{:S(2)}) collective-permute-start(bf16[1024,256]{1,0:T(8,128)(2,1)S(1)} %get-tuple-element.49.goals_ref), channel_id=1, source_target_pairs={{0,1},{1,0},{2,3},{3,2},{4,5},{5,4},{6,7},{7,6},{8,9},{9,8},{10,11... | collective-permute-start | bytes 1572872 | tf_op jit(solution)/shard_map/ppermute | solution.py:308
  48.4 5.8 %collective-permute-start.17 = (bf16[256,1024]{1,0:T(8,128)(2,1)S(1)}, bf16[256,1024]{1,0:T(8,128)(2,1)S(1)}, u32[]{:S(2)}, u32[]{:S(2)}) collective-permute-start(bf16[256,1024]{1,0:T(8,128)(2,1)S(1)} %get-tuple-element.52.refs_0_), channel_id=1, source_target_pairs={{0,1},{1,0},{2,3},{3,2},{4,5},{5,4},{6,7},{7,6},{8,9},{9,8},{10,11... | collective-permute-start | bytes 1572872 | tf_op jit(solution)/shard_map/ppermute | solution.py:308
  48.6 5.6 %collective-permute-start.18 = (bf16[1024,256]{1,0:T(8,128)(2,1)S(1)}, bf16[1024,256]{1,0:T(8,128)(2,1)S(1)}, u32[]{:S(2)}, u32[]{:S(2)}) collective-permute-start(bf16[1024,256]{1,0:T(8,128)(2,1)S(1)} %get-tuple-element.53.refs_1_), channel_id=1, source_target_pairs={{0,1},{1,0},{2,3},{3,2},{4,5},{5,4},{6,7},{7,6},{8,9},{9,8},{10,11... | collective-permute-start | bytes 1572872 | tf_op jit(solution)/shard_map/ppermute | solution.py:308
  53.6 3.2 %collective-permute-start.20 = (bf16[256,1024]{1,0:T(8,128)(2,1)S(1)}, bf16[256,1024]{1,0:T(8,128)(2,1)S(1)}, u32[]{:S(2)}, u32[]{:S(2)}) collective-permute-start(bf16[256,1024]{1,0:T(8,128)(2,1)S(1)} %get-tuple-element.56.refs_2_), channel_id=1, source_target_pairs={{0,1},{1,0},{2,3},{3,2},{4,5},{5,4},{6,7},{7,6},{8,9},{9,8},{10,11... | collective-permute-start | bytes 1572872 | tf_op jit(solution)/shard_map/ppermute | solution.py:308
  53.8 3.1 %collective-permute-start.21 = (bf16[1024,256]{1,0:T(8,128)(2,1)S(1)}, bf16[1024,256]{1,0:T(8,128)(2,1)S(1)}, u32[]{:S(2)}, u32[]{:S(2)}) collective-permute-start(bf16[1024,256]{1,0:T(8,128)(2,1)S(1)} %get-tuple-element.57.refs_3_), channel_id=1, source_target_pairs={{0,1},{1,0},{2,3},{3,2},{4,5},{5,4},{6,7},{7,6},{8,9},{9,8},{10,11... | collective-permute-start | bytes 1572872 | tf_op jit(solution)/shard_map/ppermute | solution.py:308

commit v11 on v10

--- a/solution.py
+++ b/solution.py
@@ -56,29 +56,6 @@
         out_ref[:, k * emb : (k + 1) * emb] = dot(active[...], second[...]).astype(BF)
 
 
-def first_kernel(pos_ref, x_ref, *refs):
-    weights, out_ref, held, active, sems = refs[:4], refs[4], refs[5:9], refs[9], refs[10]
-    copies = [pltpu.make_async_copy(weights[i], held[i], sems.at[i]) for i in range(4)]
-    for i in (0, 2, 1, 3):
-        copies[i].start()
-    encode(x_ref.at[: out_ref.shape[0]], held, out_ref, active, lambda i: copies[i].wait())
-
-
-def first_forward(pos, x, weights, rows):
-    hid, emb = weights[2].shape
-    part, *held = kernel(
-        first_kernel,
-        "forward",
-        [((rows, 2 * emb), BF)] + [(w.shape, w.dtype) for w in weights],
-        (x, *weights),
-        [pltpu.VMEM((rows, hid), BF), pltpu.SemaphoreType.DMA((4,))],
-        limit=49,
-        pos=pos,
-        hbm=range(1, 5),
-    )
-    return part, held
-
-
 def pack_kernel(n_rep, n_blk, n_sub, pos_ref, x_ref, own_ref, pack_ref):
     rows = x_ref.shape[0]
     slab = rows // n_rep
@@ -230,30 +207,25 @@
 
 
 def other_kernel(k, n_put, pos_ref, first, second, grads_ref, rows_ref, sum_second, sum_first, *refs):
-    done, (gf_ref, gs_ref), outs, (active, back), rest = (
+    done, outs, puts, (active, back), sems = (
         refs[:n_put],
-        refs[n_put : n_put + 2],
-        refs[n_put + 2 : 2 * n_put + 2],
-        refs[2 * n_put + 2 : 2 * n_put + 4],
-        refs[2 * n_put + 4 :],
-    )
-    copies = put_halves([pos_ref[1]] * n_put, done, outs, rest)
+        refs[n_put : n_put + 4],
+        refs[n_put + 4 : 2 * n_put + 4],
+        refs[2 * n_put + 4 : 2 * n_put + 6],
+        refs[2 * n_put + 6 :],
+    )
+    copies = [put_half(pos_ref[1], x, o, sems[0].at[i]) for i, (x, o) in enumerate(zip(done, puts))]
+    for c in copies:
+        c.start()
     quarter = active.shape[0]
     at = pl.multiple_of(pos_ref[1] * quarter, quarter)
     grad_second, grad_first = rows_grads(at, first, second, grads_ref, k, rows_ref, active, back)
-    gs_ref[...] = (sum_second[...] + grad_second).astype(BF)
-    gf_ref[...] = (sum_first[...] + grad_first).astype(BF).T
+    halves = ((sum_first[...] + grad_first).astype(BF).T, (sum_second[...] + grad_second).astype(BF))
+    for half, out16, out32 in zip(halves, outs[:2], outs[2:]):
+        out16[...] = half
+        out32[...] = half.astype(F32)
     for c in copies:
         c.wait()
-
-
-def put_halves(sides, halves, outs, rest):
-    copies = []
-    for i, (side, half, out) in enumerate(zip(sides, halves, outs)):
-        rest[i][...] = half[...].astype(F32)
-        copies.append(put_half(side, rest[i], out, rest[-1].at[i]))
-        copies[-1].start()
-    return copies
 
 
 def put_half(side, half, out, sem):
@@ -267,20 +239,27 @@
 
 def finish_kernel(old, new, pos_ref, *refs):
     n = old + new
-    sides = [1 - pos_ref[1]] * old + [pos_ref[1]] * new
-    for c in put_halves(sides, refs[:n], refs[n + old : 2 * n + old], refs[2 * n + old :]):
+    halves, outs, scratch, sems = refs[:n], refs[n + old : 2 * n + old], refs[2 * n + old : -1], refs[-1]
+    copies = [put_half(pos_ref[1], x, o, sems.at[old + i]) for i, (x, o) in enumerate(zip(halves[old:], outs[old:]))]
+    for c in copies:
+        c.start()
+    for i in range(old):
+        scratch[i][...] = halves[i][...].astype(F32)
+        copies.append(put_half(1 - pos_ref[1], scratch[i], outs[i], sems.at[i]))
+        copies[-1].start()
+    for c in copies:
         c.wait()
 
 
-def finish(pos, halves, wholes, shapes):
+def finish(pos, there, own, wholes, shapes):
     old, new = len(wholes), len(shapes)
     n = old + new
     return kernel(
         functools.partial(finish_kernel, old, new),
         "finish",
         [(w.shape, w.dtype) for w in wholes] + shapes,
-        (*halves, *wholes),
-        [*(pltpu.VMEM(x.shape, F32) for x in halves), pltpu.SemaphoreType.DMA((n,))],
+        (*there, *own, *wholes),
+        [*(pltpu.VMEM(x.shape, F32) for x in there), pltpu.SemaphoreType.DMA((n,))],
         pos=pos,
         hbm=range(n, n + old),
         hbm_out=range(n),
@@ -318,9 +297,11 @@
         (states, jnp.stack([goal_distance.reshape(rows_dev), goal_row, episode])),
         pos=pos,
         limit=4,
+        flops=2**32,
     )
     got = {0: pack, 3: across(pack, 3)}
-    part0, held = first_forward(pos, pack, weights, rows_dev)
+    held = weights
+    part0 = forward(pack, held, rows_dev)
     got[1] = across(after(pack, part0), 1)
     got[2] = across(after(pack, got[3]), 2)
     there0 = swap(part0, "rep")
@@ -369,9 +350,9 @@
         pos=pos,
         flops=2 * flops,
     )
-    halves = [((width, quarter), BF), ((quarter, emb), BF)]
+    halves = [(shape, kind) for kind in (BF, F32) for shape in ((width, quarter), (quarter, emb))]
     wholes = [((width, hid), F32), ((hid, emb), F32)]
-    state_halves = kernel(
+    *state_halves, state_first_own, state_second_own = kernel(
         functools.partial(other_kernel, 0, 0),
         "other_state",
         halves,
@@ -381,19 +362,19 @@
         flops=flops,
     )
     state_there = [swap(x, "sub") for x in state_halves]
-    *goal_halves, out0, out1 = kernel(
+    *goal_halves, goal_first_own, goal_second_own, out0, out1 = kernel(
         functools.partial(other_kernel, 1, 2),
         "other_goal",
         halves + wholes,
-        (gf, gs, grads_other, goals_other, sums_g2, sums_g1, *state_halves),
-        work + [*(pltpu.VMEM(shape, F32) for shape, _ in halves), pltpu.SemaphoreType.DMA((2,))],
+        (gf, gs, grads_other, goals_other, sums_g2, sums_g1, state_first_own, state_second_own),
+        work + [pltpu.SemaphoreType.DMA((2,))],
         pos=pos,
         flops=flops,
-        hbm_out=(2, 3),
+        hbm_out=(4, 5),
     )
     goal_there = [swap(x, "sub") for x in goal_halves]
-    out0, out1, out2, out3 = finish(pos, (*state_there, *goal_halves), (out0, out1), wholes)
-    out2, out3 = finish(pos, goal_there, (out2, out3), [])
+    out0, out1, out2, out3 = finish(pos, state_there, (goal_first_own, goal_second_own), (out0, out1), wholes)
+    out2, out3 = finish(pos, goal_there, (), (out2, out3), [])
     return (out0, out1, out2, out3)
 
 

time: 59.1 us -> 56.5 us (0.956)
  Pallas kernels: 34.1 us -> 29.8 us
  starting transfers between devices: 14.1 us -> 17.2 us
  waiting for transfers between devices: 8.17 us -> 6.62 us
    ppermute x18, waiting for transfers between devices: 7.25 us -> 2.17 us  [swap(): return lax.ppermute(x, axis, [(0, 1), (1, 0)])]
    pallas_call x13, Pallas kernels: 34.1 us -> 29.8 us  [kernel(): pl.pallas_call(body, in_specs=specs, out_specs=[HBM if i in hbm_out else...]
    ppermute x4, waiting for transfers between devices: 0.93 us -> 4.45 us  [across(): return lax.ppermute(x, 'blk', [(i, i ^ k) for i in range(n_blk)])]
    ppermute x4, starting transfers between devices: 6.84 us -> 9.22 us  [across(): return lax.ppermute(x, 'blk', [(i, i ^ k) for i in range(n_blk)])]
    ppermute x18, starting transfers between devices: 7.23 us -> 8 us  [swap(): return lax.ppermute(x, axis, [(0, 1), (1, 0)])]
  transfers between devices with their start and end apart: 22 -> 22, of which waited for: 9 -> 8; matrix products, arithmetic and copies ran while one was open for 0% -> 0% of each run, Pallas kernels for 46% -> 40%
where the time goes in v11:
time: 56.5 us; the launch traced here: 56.3 us
  Pallas kernels  29.8 us (53%)
  starting transfers between devices  17.2 us (30%)
  waiting for transfers between devices  6.62 us (12%)
  between operations  0.95 us (2%)
  local copies, waits for them, and re-layouts  0.92 us (2%)
  other arithmetic  0.8 us (1%)
    pallas_call x13, Pallas kernels, kernel(): pl.pallas_call(body, in_specs=specs, out_specs=[HBM if i in hbm_out else...  29.8 us
    ppermute x4, starting transfers between devices, across(): return lax.ppermute(x, 'blk', [(i, i ^ k) for i in range(n_blk)])  9.22 us
    ppermute x18, starting transfers between devices, swap(): return lax.ppermute(x, axis, [(0, 1), (1, 0)])  8 us
    ppermute x4, waiting for transfers between devices, across(): return lax.ppermute(x, 'blk', [(i, i ^ k) for i in range(n_blk)])  4.45 us
    ppermute x18, waiting for transfers between devices, swap(): return lax.ppermute(x, axis, [(0, 1), (1, 0)])  2.17 us
  transfers between devices with their start and end apart: 22, of which 8 were waited for; matrix products, arithmetic and copies ran while one was open for 0% of the time, Pallas kernels for 40%

profile of v11, /device:TPU:0, one launch (start us, length us, event | category | flops | bytes accessed | tf_op | source)
XLA Modules:
  0.0 56.3 jit_solution(7833556213924938181)
XLA Ops:
  0.6 0.1 pad_add_fusion.1.pos_ref
  0.7 0.7 %pad_add_fusion.own_ref = s32[3,256]{1,0:T(4,128)S(1)} fusion(s32[1,256]{1,0:T(1,128)} %bitcast.5, s32[1,256]{1,0:T(1,128)} %bitcast.6, s32[1,256]{1,0:T(1,128)} %bitcast.7), kind=kLoop, calls=%fused_computation | loop fusion | flops 1536 | bytes 6144 | tf_op jit(solution)/shard_map/stack | solution.py:297
  1.4 0.9 %copy-done.4 = bf16[256,256]{1,0:T(8,128)(2,1)S(1)} copy-done((bf16[256,256]{1,0:T(8,128)(2,1)S(1)}, bf16[256,256]{1,0:T(8,128)(2,1)}, u32[]{:S(2)}) %copy-start.4) | copy-done | bytes 131096
  2.3 0.6 %pack.1.x_ref.refs_0_ = bf16[272,256]{1,0:T(8,128)(2,1)S(1)} custom-call(s32[2]{0:T(128)S(1)} %pad_add_fusion.1.pos_ref, bf16[256,256]{1,0:T(8,128)(2,1)S(1)} %copy-done.4, s32[3,256]{1,0:T(4,128)S(1)} %pad_add_fusion.own_ref), custom_call_target="tpu_custom_call" | custom-call | flops 4294967296 | tf_op jit(solution)/shard_map/pack/pallas_call | solution.py:34
  2.9 5.1 %collective-permute-start.1 = (bf16[272,256]{1,0:T(8,128)(2,1)S(1)}, bf16[272,256]{1,0:T(8,128)(2,1)S(1)}, u32[]{:S(2)}, u32[]{:S(2)}) collective-permute-start(bf16[272,256]{1,0:T(8,128)(2,1)S(1)} %pack.1.x_ref.refs_0_), channel_id=1, source_target_pairs={{0,12},{4,8},{8,4},{12,0},{1,13},{5,9},{9,5},{13,1},{2,14},{6,10},... | collective-permute-start | bytes 417800 | tf_op jit(solution)/shard_map/ppermute | solution.py:284
  8.0 0.0 copy-done
  8.0 0.0 copy-done.1
  8.0 0.0 copy-done.2
  8.0 0.0 copy-done.3
  8.0 1.4 %forward.3.a_ref = bf16[256,512]{1,0:T(8,128)(2,1)S(1)} custom-call(bf16[272,256]{1,0:T(8,128)(2,1)S(1)} %pack.1.x_ref.refs_0_, bf16[256,2048]{1,0:T(8,128)(2,1)S(1)} %copy-done, bf16[256,2048]{1,0:T(8,128)(2,1)S(1)} %copy-done.2, bf16[2048,256]{1,0:T(8,128)(2,1)S(1)} %copy-done.1, bf16[2048,256]{1,0:T(8,128)(2,1)S(1)} %copy-done.3), custom_call_target="tpu_custom_call" | custom-call | tf_op jit(solution)/shard_map/forward/pallas_call | solution.py:34
  9.4 1.6 %collective-permute-start = (bf16[256,512]{1,0:T(8,128)(2,1)S(1)}, bf16[256,512]{1,0:T(8,128)(2,1)S(1)}, u32[]{:S(2)}, u32[]{:S(2)}) collective-permute-start(bf16[256,512]{1,0:T(8,128)(2,1)S(1)} %forward.3.a_ref), channel_id=1, source_target_pairs={{0,2},{2,0},{1,3},{3,1},{4,6},{6,4},{5,7},{7,5},{8,10},{10,8},{9,1... | collective-permute-start | bytes 786440 | tf_op jit(solution)/shard_map/ppermute | solution.py:287
  11.0 0.8 %collective-permute-done.1.x_ref.refs_3_ = bf16[272,256]{1,0:T(8,128)(2,1)S(1)} collective-permute-done((bf16[272,256]{1,0:T(8,128)(2,1)S(1)}, bf16[272,256]{1,0:T(8,128)(2,1)S(1)}, u32[]{:S(2)}, u32[]{:S(2)}) %collective-permute-start.1) | collective-permute-done | bytes 139296 | tf_op jit(solution)/shard_map/ppermute | solution.py:284
  11.8 3.6 %collective-permute-start.2 = (bf16[272,256]{1,0:T(8,128)(2,1)S(1)}, bf16[272,256]{1,0:T(8,128)(2,1)S(1)}, u32[]{:S(2)}, u32[]{:S(2)}) collective-permute-start(bf16[272,256]{1,0:T(8,128)(2,1)S(1)} %pack.1.x_ref.refs_0_), channel_id=1, source_target_pairs={{0,8},{4,12},{8,0},{12,4},{1,9},{5,13},{9,1},{13,5},{2,10},{6,14},... | collective-permute-start | bytes 417800 | tf_op jit(solution)/shard_map/ppermute | solution.py:284
  15.4 1.4 %forward.5.a_ref = bf16[256,512]{1,0:T(8,128)(2,1)S(1)} custom-call(bf16[272,256]{1,0:T(8,128)(2,1)S(1)} %collective-permute-done.1.x_ref.refs_3_, bf16[256,2048]{1,0:T(8,128)(2,1)S(1)} %copy-done, bf16[256,2048]{1,0:T(8,128)(2,1)S(1)} %copy-done.2, bf16[2048,256]{1,0:T(8,128)(2,1)S(1)} %copy-done.1, bf16[2048,256]{1,0:T(8,128)(2,1)S(1)} %copy-done.3), custom_call_target="tpu_custom_call" | custom-call | tf_op jit(solution)/shard_map/forward/pallas_call | solution.py:34
  16.8 1.6 %collective-permute-start.4 = (bf16[256,512]{1,0:T(8,128)(2,1)S(1)}, bf16[256,512]{1,0:T(8,128)(2,1)S(1)}, u32[]{:S(2)}, u32[]{:S(2)}) collective-permute-start(bf16[256,512]{1,0:T(8,128)(2,1)S(1)} %forward.5.a_ref), channel_id=1, source_target_pairs={{0,2},{2,0},{1,3},{3,1},{4,6},{6,4},{5,7},{7,5},{8,10},{10,8},{9,1... | collective-permute-start | bytes 786440 | tf_op jit(solution)/shard_map/ppermute | solution.py:287
  18.3 0.0 collective-permute-start.7
  18.3 0.5 collective-permute-start.6
  18.8 0.0 collective-permute-done.b_ref
  18.8 0.1 both.2.refs_0_
  18.9 2.0 %collective-permute-done.2.x_ref.refs_2_ = bf16[272,256]{1,0:T(8,128)(2,1)S(1)} collective-permute-done((bf16[272,256]{1,0:T(8,128)(2,1)S(1)}, bf16[272,256]{1,0:T(8,128)(2,1)S(1)}, u32[]{:S(2)}, u32[]{:S(2)}) %collective-permute-start.2) | collective-permute-done | bytes 139296 | tf_op jit(solution)/shard_map/ppermute | solution.py:284
  21.0 1.4 %forward.4.refs_2_ = bf16[256,512]{1,0:T(8,128)(2,1)S(1)} custom-call(bf16[272,256]{1,0:T(8,128)(2,1)S(1)} %collective-permute-done.2.x_ref.refs_2_, bf16[256,2048]{1,0:T(8,128)(2,1)S(1)} %copy-done, bf16[256,2048]{1,0:T(8,128)(2,1)S(1)} %copy-done.2, bf16[2048,256]{1,0:T(8,128)(2,1)S(1)} %copy-done.1, bf16[2048,256]{1,0:T(8,128)(2,1)S(1)} %copy-done.3), custom_call_target="tpu_custom_call" | custom-call | tf_op jit(solution)/shard_map/forward/pallas_call | solution.py:34
  22.3 1.6 %collective-permute-start.5 = (bf16[256,512]{1,0:T(8,128)(2,1)S(1)}, bf16[256,512]{1,0:T(8,128)(2,1)S(1)}, u32[]{:S(2)}, u32[]{:S(2)}) collective-permute-start(bf16[256,512]{1,0:T(8,128)(2,1)S(1)} %forward.4.refs_2_), channel_id=1, source_target_pairs={{0,2},{2,0},{1,3},{3,1},{4,6},{6,4},{5,7},{7,5},{8,10},{10,8},{9,1... | collective-permute-start | bytes 786440 | tf_op jit(solution)/shard_map/ppermute | solution.py:287
  23.9 0.0 collective-permute-start.3
  23.9 0.0 collective-permute-done.7.refs_4_
  23.9 0.0 collective-permute-start.10
  24.0 0.9 %collective-permute-done.6.refs_1_ = bf16[272,256]{1,0:T(8,128)(2,1)S(1)} collective-permute-done((bf16[272,256]{1,0:T(8,128)(2,1)S(1)}, bf16[272,256]{1,0:T(8,128)(2,1)S(1)}, u32[]{:S(2)}, u32[]{:S(2)}) %collective-permute-start.6) | collective-permute-done | bytes 139296 | tf_op jit(solution)/shard_map/ppermute | solution.py:284
  24.8 0.0 collective-permute-start.8
  24.8 0.0 collective-permute-done.4.b_ref
  24.8 0.5 collective-permute-start.9
  25.3 0.1 both.3.refs_3_
  25.4 0.0 collective-permute-done.10.refs_7_
  25.4 0.1 collective-permute-start.11
  25.5 0.7 %collective-permute-done.8.refs_5_ = bf16[272,256]{1,0:T(8,128)(2,1)S(1)} collective-permute-done((bf16[272,256]{1,0:T(8,128)(2,1)S(1)}, bf16[272,256]{1,0:T(8,128)(2,1)S(1)}, u32[]{:S(2)}, u32[]{:S(2)}) %collective-permute-start.8) | collective-permute-done | bytes 139296 | tf_op jit(solution)/shard_map/ppermute | solution.py:287
  26.2 0.1 collective-permute-start.13
  26.3 0.1 collective-permute-done.9.refs_6_
  26.4 0.3 collective-permute-start.14
  26.7 2.9 %arrange.1 = (bf16[1024,256]{1,0:T(8,128)(2,1)S(1)}, bf16[1024,256]{1,0:T(8,128)(2,1)S(1)}, bf16[1024,256]{1,0:T(8,128)(2,1)S(1)}, bf16[1024,2048]{1,0:T(8,128)(2,1)S(1)}, f32[1,1024]{1,0:T(1,128)S(1)}) custom-call(s32[2]{0:T(128)S(1)} %pad_add_fusion.1.pos_ref, bf16[272,256]{1,0:T(8,128)(2,1)S(1)} %pack.1.x_ref.refs_0_, ...), custom_call_target="tpu_custom_call" | custom-call | tf_op jit(solution)/shard_map/arrange/pallas_call | solution.py:34
  29.6 0.0 collective-permute-done.5.refs_4_
  29.6 0.7 %collective-permute-done.3.refs_1_ = bf16[256,512]{1,0:T(8,128)(2,1)S(1)} collective-permute-done((bf16[256,512]{1,0:T(8,128)(2,1)S(1)}, bf16[256,512]{1,0:T(8,128)(2,1)S(1)}, u32[]{:S(2)}, u32[]{:S(2)}) %collective-permute-start.3) | collective-permute-done | bytes 262176 | tf_op jit(solution)/shard_map/ppermute | solution.py:284
  30.3 0.0 collective-permute-start.12
  30.3 0.5 collective-permute-start.15
  30.8 0.0 collective-permute-done.11.refs_5_
  30.8 0.0 collective-permute-done.13.refs_7_
  30.8 0.0 collective-permute-done.14.refs_8_
  30.8 1.0 %collective-permute-done.12.refs_6_ = bf16[256,512]{1,0:T(8,128)(2,1)S(1)} collective-permute-done((bf16[256,512]{1,0:T(8,128)(2,1)S(1)}, bf16[256,512]{1,0:T(8,128)(2,1)S(1)}, u32[]{:S(2)}, u32[]{:S(2)}) %collective-permute-start.12) | collective-permute-done | bytes 262176 | tf_op jit(solution)/shard_map/ppermute | solution.py:287
  31.8 0.4 collective-permute-done.15.refs_9_
  32.2 4.7 %contrast.1.grads_ref = bf16[1024,512]{1,0:T(8,128)(2,1)S(1)} custom-call(s32[2]{0:T(128)S(1)} %pad_add_fusion.1.pos_ref, bf16[256,512]{1,0:T(8,128)(2,1)S(1)} %both.2.refs_0_, bf16[256,512]{1,0:T(8,128)(2,1)S(1)} %collective-permute-done.3.refs_1_, bf16[256,512]{1,0:T(8,128)(2,1)S(1)} %forward.4.refs_2_, bf16[256,512]{1,0:T(8,128)(2,1)S(1)} %both.3.refs_3_, ...), custom_call_target="tpu_custom_call" | custom-call | tf_op jit(solution)/shard_map/contrast/pallas_call | solution.py:34
  36.9 0.2 collective-permute-start.16
  37.1 0.4 collective-permute-start.19
  37.5 5.9 %mine.1 = (f32[1024,256]{1,0:T(8,128)S(1)}, f32[1024,256]{1,0:T(8,128)S(1)}, f32[1024,256]{1,0:T(8,128)S(1)}, f32[1024,256]{1,0:T(8,128)S(1)}) custom-call(s32[2]{0:T(128)S(1)} %pad_add_fusion.1.pos_ref, bf16[256,2048]{1,0:T(8,128)(2,1)S(1)} %copy-done, bf16[256,2048]{1,0:T(8,128)(2,1)S(1)} %copy-done.2, bf16[2048,256]{1,0:T(8,128)(2,1)S(1)} %copy-done.1, ...), custom_call_target="tpu_custom_call" | custom-call | flops 4294967296 | tf_op jit(solution)/shard_map/mine/pallas_call | solution.py:34
  43.4 0.0 collective-permute-done.16.grads_ref
  43.4 3.3 %other_state.1 = (bf16[256,1024]{1,0:T(8,128)(2,1)S(1)}, bf16[1024,256]{1,0:T(8,128)(2,1)S(1)}, f32[256,1024]{1,0:T(8,128)S(1)}, f32[1024,256]{1,0:T(8,128)S(1)}) custom-call(s32[2]{0:T(128)S(1)} %pad_add_fusion.1.pos_ref, bf16[256,2048]{1,0:T(8,128)(2,1)S(1)} %copy-done, bf16[2048,256]{1,0:T(8,128)(2,1)S(1)} %copy-done.1, ...), custom_call_target="tpu_custom_call" | custom-call | flops 2147483648 | tf_op jit(solution)/shard_map/other_state/pallas_call | solution.py:34
  46.7 0.2 collective-permute-start.17
  46.9 0.4 collective-permute-start.18
  47.3 0.0 collective-permute-done.19.rows_ref
  47.3 3.7 %other_goal.1 = (bf16[256,1024]{1,0:T(8,128)(2,1)S(1)}, bf16[1024,256]{1,0:T(8,128)(2,1)S(1)}, f32[256,1024]{1,0:T(8,128)S(1)}, f32[1024,256]{1,0:T(8,128)S(1)},...) custom-call(s32[2]{0:T(128)S(1)} %pad_add_fusion.1.pos_ref, bf16[256,2048]{1,0:T(8,128)(2,1)S(1)} %copy-done.2, ...), custom_call_target="tpu_custom_call" | custom-call | flops 2147483648 | tf_op jit(solution)/shard_map/other_goal/pallas_call | solution.py:34
  51.0 0.2 collective-permute-start.20
  51.2 0.4 collective-permute-start.21
  51.6 0.0 collective-permute-done.17.refs_0_
  51.6 0.0 collective-permute-done.18.refs_1_
  51.6 2.6 %finish.2 = (f32[256,2048]{1,0:T(8,128)}, f32[2048,256]{1,0:T(8,128)}, f32[256,2048]{1,0:T(8,128)}, f32[2048,256]{1,0:T(8,128)}) custom-call(s32[2]{0:T(128)S(1)} %pad_add_fusion.1.pos_ref, bf16[256,1024]{1,0:T(8,128)(2,1)S(1)} %collective-permute-done.17.refs_0_, ...), custom_call_target="tpu_custom_call", output_to_operand_aliasing={{0}: (5, {}), {1}: (6, {})} | custom-call | tf_op jit(solution)/shard_map/finish/pallas_call | solution.py:34
  54.2 0.0 collective-permute-done.20.refs_0_
  54.2 0.0 collective-permute-done.21.refs_1_
  54.2 1.9 %finish.3 = (f32[256,2048]{1,0:T(8,128)}, f32[2048,256]{1,0:T(8,128)}) custom-call(s32[2]{0:T(128)S(1)} %pad_add_fusion.1.pos_ref, bf16[256,1024]{1,0:T(8,128)(2,1)S(1)} %collective-permute-done.20.refs_0_, bf16[1024,256]{1,0:T(8,128)(2,1)S(1)} %collective-permute-done.21.refs_1_, ...), custom_call_target="tpu_custom_call", output_to_operand_aliasing={{0}: (3, {}), {1}: (4, {})} | custom-call | tf_op jit(solution)/shard_map/finish/pallas_call | solution.py:34
  (5 shorter events, 0.0 us)
Async XLA Ops:
  1.4 0.9 %copy-start.4 = (bf16[256,256]{1,0:T(8,128)(2,1)S(1)}, bf16[256,256]{1,0:T(8,128)(2,1)}, u32[]{:S(2)}) copy-start(bf16[256,256]{1,0:T(8,128)(2,1)} %x_ref.1) | copy-start | bytes 393220
  2.3 5.7 %copy-start = (bf16[256,2048]{1,0:T(8,128)(2,1)S(1)}, bf16[256,2048]{1,0:T(8,128)(2,1)}, u32[]{:S(2)}) copy-start(bf16[256,2048]{1,0:T(8,128)(2,1)} %first.2) | copy-start | bytes 3145732
  2.3 5.7 %copy-start.1 = (bf16[2048,256]{1,0:T(8,128)(2,1)S(1)}, bf16[2048,256]{1,0:T(8,128)(2,1)}, u32[]{:S(2)}) copy-start(bf16[2048,256]{1,0:T(8,128)(2,1)} %second.2) | copy-start | bytes 3145732
  2.3 5.7 %copy-start.2 = (bf16[256,2048]{1,0:T(8,128)(2,1)S(1)}, bf16[256,2048]{1,0:T(8,128)(2,1)}, u32[]{:S(2)}) copy-start(bf16[256,2048]{1,0:T(8,128)(2,1)} %first.3) | copy-start | bytes 3145732
  2.3 5.7 %copy-start.3 = (bf16[2048,256]{1,0:T(8,128)(2,1)S(1)}, bf16[2048,256]{1,0:T(8,128)(2,1)}, u32[]{:S(2)}) copy-start(bf16[2048,256]{1,0:T(8,128)(2,1)} %second.3) | copy-start | bytes 3145732
  2.9 8.9 %collective-permute-start.1 = (bf16[272,256]{1,0:T(8,128)(2,1)S(1)}, bf16[272,256]{1,0:T(8,128)(2,1)S(1)}, u32[]{:S(2)}, u32[]{:S(2)}) collective-permute-start(bf16[272,256]{1,0:T(8,128)(2,1)S(1)} %pack.1.x_ref.refs_0_), channel_id=1, source_target_pairs={{0,12},{4,8},{8,4},{12,0},{1,13},{5,9},{9,5},{13,1},{2,14},{6,10},... | collective-permute-start | bytes 417800 | tf_op jit(solution)/shard_map/ppermute | solution.py:284
  9.4 9.4 %collective-permute-start = (bf16[256,512]{1,0:T(8,128)(2,1)S(1)}, bf16[256,512]{1,0:T(8,128)(2,1)S(1)}, u32[]{:S(2)}, u32[]{:S(2)}) collective-permute-start(bf16[256,512]{1,0:T(8,128)(2,1)S(1)} %forward.3.a_ref), channel_id=1, source_target_pairs={{0,2},{2,0},{1,3},{3,1},{4,6},{6,4},{5,7},{7,5},{8,10},{10,8},{9,1... | collective-permute-start | bytes 786440 | tf_op jit(solution)/shard_map/ppermute | solution.py:287
  11.8 9.1 %collective-permute-start.2 = (bf16[272,256]{1,0:T(8,128)(2,1)S(1)}, bf16[272,256]{1,0:T(8,128)(2,1)S(1)}, u32[]{:S(2)}, u32[]{:S(2)}) collective-permute-start(bf16[272,256]{1,0:T(8,128)(2,1)S(1)} %pack.1.x_ref.refs_0_), channel_id=1, source_target_pairs={{0,8},{4,12},{8,0},{12,4},{1,9},{5,13},{9,1},{13,5},{2,10},{6,14},... | collective-permute-start | bytes 417800 | tf_op jit(solution)/shard_map/ppermute | solution.py:284
  16.8 8.0 %collective-permute-start.4 = (bf16[256,512]{1,0:T(8,128)(2,1)S(1)}, bf16[256,512]{1,0:T(8,128)(2,1)S(1)}, u32[]{:S(2)}, u32[]{:S(2)}) collective-permute-start(bf16[256,512]{1,0:T(8,128)(2,1)S(1)} %forward.5.a_ref), channel_id=1, source_target_pairs={{0,2},{2,0},{1,3},{3,1},{4,6},{6,4},{5,7},{7,5},{8,10},{10,8},{9,1... | collective-permute-start | bytes 786440 | tf_op jit(solution)/shard_map/ppermute | solution.py:287
  18.3 5.6 %collective-permute-start.7 = (bf16[272,256]{1,0:T(8,128)(2,1)S(1)}, bf16[272,256]{1,0:T(8,128)(2,1)S(1)}, u32[]{:S(2)}, u32[]{:S(2)}) collective-permute-start(bf16[272,256]{1,0:T(8,128)(2,1)S(1)} %pack.1.x_ref.refs_0_), channel_id=1, source_target_pairs={{0,1},{1,0},{2,3},{3,2},{4,5},{5,4},{6,7},{7,6},{8,9},{9,8},{10,11... | collective-permute-start | bytes 417800 | tf_op jit(solution)/shard_map/ppermute | solution.py:287
  18.3 6.5 %collective-permute-start.6 = (bf16[272,256]{1,0:T(8,128)(2,1)S(1)}, bf16[272,256]{1,0:T(8,128)(2,1)S(1)}, u32[]{:S(2)}, u32[]{:S(2)}) collective-permute-start(bf16[272,256]{1,0:T(8,128)(2,1)S(1)} %pack.1.x_ref.refs_0_), channel_id=1, source_target_pairs={{0,4},{4,0},{8,12},{12,8},{1,5},{5,1},{9,13},{13,9},{2,6},{6,2},{1... | collective-permute-start | bytes 417800 | tf_op jit(solution)/shard_map/ppermute | solution.py:284
  22.3 7.3 %collective-permute-start.5 = (bf16[256,512]{1,0:T(8,128)(2,1)S(1)}, bf16[256,512]{1,0:T(8,128)(2,1)S(1)}, u32[]{:S(2)}, u32[]{:S(2)}) collective-permute-start(bf16[256,512]{1,0:T(8,128)(2,1)S(1)} %forward.4.refs_2_), channel_id=1, source_target_pairs={{0,2},{2,0},{1,3},{3,1},{4,6},{6,4},{5,7},{7,5},{8,10},{10,8},{9,1... | collective-permute-start | bytes 786440 | tf_op jit(solution)/shard_map/ppermute | solution.py:287
  23.9 6.4 %collective-permute-start.3 = (bf16[256,512]{1,0:T(8,128)(2,1)S(1)}, bf16[256,512]{1,0:T(8,128)(2,1)S(1)}, u32[]{:S(2)}, u32[]{:S(2)}) collective-permute-start(bf16[256,512]{1,0:T(8,128)(2,1)S(1)} %both.2.refs_0_), channel_id=1, source_target_pairs={{0,4},{4,0},{8,12},{12,8},{1,5},{5,1},{9,13},{13,9},{2,6},{6,2},{1... | collective-permute-start | bytes 786440 | tf_op jit(solution)/shard_map/ppermute | solution.py:284
  23.9 1.5 %collective-permute-start.10 = (bf16[272,256]{1,0:T(8,128)(2,1)S(1)}, bf16[272,256]{1,0:T(8,128)(2,1)S(1)}, u32[]{:S(2)}, u32[]{:S(2)}) collective-permute-start(bf16[272,256]{1,0:T(8,128)(2,1)S(1)} %collective-permute-done.1.x_ref.refs_3_), channel_id=1, source_target_pairs={{0,1},{1,0},{2,3},{3,2},{4,5},{5,4},{6,7},{7,6},{8,9},{9,8},{10,11... | collective-permute-start | bytes 417800 | tf_op jit(solution)/shard_map/ppermute | solution.py:287
  24.8 1.4 %collective-permute-start.8 = (bf16[272,256]{1,0:T(8,128)(2,1)S(1)}, bf16[272,256]{1,0:T(8,128)(2,1)S(1)}, u32[]{:S(2)}, u32[]{:S(2)}) collective-permute-start(bf16[272,256]{1,0:T(8,128)(2,1)S(1)} %collective-permute-done.6.refs_1_), channel_id=1, source_target_pairs={{0,1},{1,0},{2,3},{3,2},{4,5},{5,4},{6,7},{7,6},{8,9},{9,8},{10,11... | collective-permute-start | bytes 417800 | tf_op jit(solution)/shard_map/ppermute | solution.py:287
  24.8 1.6 %collective-permute-start.9 = (bf16[272,256]{1,0:T(8,128)(2,1)S(1)}, bf16[272,256]{1,0:T(8,128)(2,1)S(1)}, u32[]{:S(2)}, u32[]{:S(2)}) collective-permute-start(bf16[272,256]{1,0:T(8,128)(2,1)S(1)} %collective-permute-done.2.x_ref.refs_2_), channel_id=1, source_target_pairs={{0,1},{1,0},{2,3},{3,2},{4,5},{5,4},{6,7},{7,6},{8,9},{9,8},{10,11... | collective-permute-start | bytes 417800 | tf_op jit(solution)/shard_map/ppermute | solution.py:287
  25.4 5.4 %collective-permute-start.11 = (bf16[256,512]{1,0:T(8,128)(2,1)S(1)}, bf16[256,512]{1,0:T(8,128)(2,1)S(1)}, u32[]{:S(2)}, u32[]{:S(2)}) collective-permute-start(bf16[256,512]{1,0:T(8,128)(2,1)S(1)} %both.2.refs_0_), channel_id=1, source_target_pairs={{0,1},{1,0},{2,3},{3,2},{4,5},{5,4},{6,7},{7,6},{8,9},{9,8},{10,11... | collective-permute-start | bytes 786440 | tf_op jit(solution)/shard_map/ppermute | solution.py:287
  26.2 4.6 %collective-permute-start.13 = (bf16[256,512]{1,0:T(8,128)(2,1)S(1)}, bf16[256,512]{1,0:T(8,128)(2,1)S(1)}, u32[]{:S(2)}, u32[]{:S(2)}) collective-permute-start(bf16[256,512]{1,0:T(8,128)(2,1)S(1)} %forward.4.refs_2_), channel_id=1, source_target_pairs={{0,1},{1,0},{2,3},{3,2},{4,5},{5,4},{6,7},{7,6},{8,9},{9,8},{10,11... | collective-permute-start | bytes 786440 | tf_op jit(solution)/shard_map/ppermute | solution.py:287
  26.4 4.5 %collective-permute-start.14 = (bf16[256,512]{1,0:T(8,128)(2,1)S(1)}, bf16[256,512]{1,0:T(8,128)(2,1)S(1)}, u32[]{:S(2)}, u32[]{:S(2)}) collective-permute-start(bf16[256,512]{1,0:T(8,128)(2,1)S(1)} %both.3.refs_3_), channel_id=1, source_target_pairs={{0,1},{1,0},{2,3},{3,2},{4,5},{5,4},{6,7},{7,6},{8,9},{9,8},{10,11... | collective-permute-start | bytes 786440 | tf_op jit(solution)/shard_map/ppermute | solution.py:287
  30.3 1.5 %collective-permute-start.12 = (bf16[256,512]{1,0:T(8,128)(2,1)S(1)}, bf16[256,512]{1,0:T(8,128)(2,1)S(1)}, u32[]{:S(2)}, u32[]{:S(2)}) collective-permute-start(bf16[256,512]{1,0:T(8,128)(2,1)S(1)} %collective-permute-done.3.refs_1_), channel_id=1, source_target_pairs={{0,1},{1,0},{2,3},{3,2},{4,5},{5,4},{6,7},{7,6},{8,9},{9,8},{10,11... | collective-permute-start | bytes 786440 | tf_op jit(solution)/shard_map/ppermute | solution.py:287
  30.3 1.9 %collective-permute-start.15 = (bf16[256,512]{1,0:T(8,128)(2,1)S(1)}, bf16[256,512]{1,0:T(8,128)(2,1)S(1)}, u32[]{:S(2)}, u32[]{:S(2)}) collective-permute-start(bf16[256,512]{1,0:T(8,128)(2,1)S(1)} %collective-permute-done.5.refs_4_), channel_id=1, source_target_pairs={{0,1},{1,0},{2,3},{3,2},{4,5},{5,4},{6,7},{7,6},{8,9},{9,8},{10,11... | collective-permute-start | bytes 786440 | tf_op jit(solution)/shard_map/ppermute | solution.py:287
  36.9 6.5 %collective-permute-start.16 = (bf16[1024,512]{1,0:T(8,128)(2,1)S(1)}, bf16[1024,512]{1,0:T(8,128)(2,1)S(1)}, u32[]{:S(2)}, u32[]{:S(2)}) collective-permute-start(bf16[1024,512]{1,0:T(8,128)(2,1)S(1)} %contrast.1.grads_ref), channel_id=1, source_target_pairs={{0,1},{1,0},{2,3},{3,2},{4,5},{5,4},{6,7},{7,6},{8,9},{9,8},{10,11... | collective-permute-start | bytes 3145736 | tf_op jit(solution)/shard_map/ppermute | solution.py:287
  37.1 10.2 %collective-permute-start.19 = (bf16[1024,256]{1,0:T(8,128)(2,1)S(1)}, bf16[1024,256]{1,0:T(8,128)(2,1)S(1)}, u32[]{:S(2)}, u32[]{:S(2)}) collective-permute-start(bf16[1024,256]{1,0:T(8,128)(2,1)S(1)} %get-tuple-element.43.goals_ref), channel_id=1, source_target_pairs={{0,1},{1,0},{2,3},{3,2},{4,5},{5,4},{6,7},{7,6},{8,9},{9,8},{10,11... | collective-permute-start | bytes 1572872 | tf_op jit(solution)/shard_map/ppermute | solution.py:287
  46.7 4.9 %collective-permute-start.17 = (bf16[256,1024]{1,0:T(8,128)(2,1)S(1)}, bf16[256,1024]{1,0:T(8,128)(2,1)S(1)}, u32[]{:S(2)}, u32[]{:S(2)}) collective-permute-start(bf16[256,1024]{1,0:T(8,128)(2,1)S(1)} %get-tuple-element.46), channel_id=1, source_target_pairs={{0,1},{1,0},{2,3},{3,2},{4,5},{5,4},{6,7},{7,6},{8,9},{9,8},{10,11... | collective-permute-start | bytes 1572872 | tf_op jit(solution)/shard_map/ppermute | solution.py:287
  46.9 4.7 %collective-permute-start.18 = (bf16[1024,256]{1,0:T(8,128)(2,1)S(1)}, bf16[1024,256]{1,0:T(8,128)(2,1)S(1)}, u32[]{:S(2)}, u32[]{:S(2)}) collective-permute-start(bf16[1024,256]{1,0:T(8,128)(2,1)S(1)} %get-tuple-element.47), channel_id=1, source_target_pairs={{0,1},{1,0},{2,3},{3,2},{4,5},{5,4},{6,7},{7,6},{8,9},{9,8},{10,11... | collective-permute-start | bytes 1572872 | tf_op jit(solution)/shard_map/ppermute | solution.py:287
  51.0 3.2 %collective-permute-start.20 = (bf16[256,1024]{1,0:T(8,128)(2,1)S(1)}, bf16[256,1024]{1,0:T(8,128)(2,1)S(1)}, u32[]{:S(2)}, u32[]{:S(2)}) collective-permute-start(bf16[256,1024]{1,0:T(8,128)(2,1)S(1)} %get-tuple-element.58), channel_id=1, source_target_pairs={{0,1},{1,0},{2,3},{3,2},{4,5},{5,4},{6,7},{7,6},{8,9},{9,8},{10,11... | collective-permute-start | bytes 1572872 | tf_op jit(solution)/shard_map/ppermute | solution.py:287
  51.2 3.0 %collective-permute-start.21 = (bf16[1024,256]{1,0:T(8,128)(2,1)S(1)}, bf16[1024,256]{1,0:T(8,128)(2,1)S(1)}, u32[]{:S(2)}, u32[]{:S(2)}) collective-permute-start(bf16[1024,256]{1,0:T(8,128)(2,1)S(1)} %get-tuple-element.59), channel_id=1, source_target_pairs={{0,1},{1,0},{2,3},{3,2},{4,5},{5,4},{6,7},{7,6},{8,9},{9,8},{10,11... | collective-permute-start | bytes 1572872 | tf_op jit(solution)/shard_map/ppermute | solution.py:287

commit v12 on v11

--- a/solution.py
+++ b/solution.py
@@ -26,11 +26,14 @@
 SMEM = pl.BlockSpec(memory_space=pltpu.SMEM)
 
 
-def kernel(body, name, outs, args, scratch=(), limit=16, pos=None, flops=0, hbm=(), hbm_out=(), aliases={}):
+def kernel(body, name, outs, args, scratch=(), limit=16, pos=False, flops=0, hbm=(), hbm_out=(), aliases={}):
     specs = [HBM if i in hbm else VMEM for i in range(len(args))]
-    if pos is not None:
-        args, specs = (pos, *args), [SMEM, *specs]
-        aliases = {i + 1: o for i, o in aliases.items()}
+    if pos:
+        inner = body
+
+        def body(*refs):
+            inner((lax.axis_index("blk"), lax.axis_index("sub")), *refs)
+
     return pl.pallas_call(
         body,
         in_specs=specs,
@@ -56,14 +59,14 @@
         out_ref[:, k * emb : (k + 1) * emb] = dot(active[...], second[...]).astype(BF)
 
 
-def pack_kernel(n_rep, n_blk, n_sub, pos_ref, x_ref, own_ref, pack_ref):
+def pack_kernel(n_rep, n_blk, n_sub, pos, x_ref, own_ref, pack_ref):
     rows = x_ref.shape[0]
     slab = rows // n_rep
 
     def bits(n):
         return n.bit_length() - 1
 
-    owner = (pos_ref[0] * n_sub + pos_ref[1] + own_ref[0:1, :]) & (n_blk * n_sub - 1)
+    owner = (pos[0] * n_sub + pos[1] + own_ref[0:1, :]) & (n_blk * n_sub - 1)
     place = own_ref[1:2, :]
     batch = ((owner & (n_sub - 1)) << bits(n_rep)) + (place >> bits(slab))
     goal = (((batch << bits(n_blk)) + (owner >> bits(n_sub))) << bits(slab)) + (place & (slab - 1))
@@ -97,9 +100,9 @@
     return kernel(add_kernel, "both", [(part.shape, BF)], (part, there), limit=4)[0]
 
 
-def place_blocks(pos_ref, blocks, put, n_blk, n_rep, slab):
+def place_blocks(pos, blocks, put, n_blk, n_rep, slab):
     for k, block in enumerate(blocks):
-        at = jnp.bitwise_xor(pos_ref[0], k)
+        at = jnp.bitwise_xor(pos[0], k)
         for r in range(n_rep):
             off = (r * n_blk + at) * slab
             put(pl.multiple_of(off, slab), block[r * slab : (r + 1) * slab, :])
@@ -109,7 +112,7 @@
     return jnp.broadcast_to(row, (128, row.shape[1])).T[:, :1]
 
 
-def arrange_kernel(n_blk, n_rep, slab, pos_ref, *refs):
+def arrange_kernel(n_blk, n_rep, slab, pos, *refs):
     mine, other = refs[:n_blk], refs[n_blk : 2 * n_blk]
     rows_mine, rows_other, goals_ref, pick_ref, ep_ref, both_sides, meta = refs[2 * n_blk :]
     half = rows_mine.shape[0]
@@ -121,16 +124,16 @@
             to[pl.ds(off, slab), :] = value
             both_sides[pl.ds(i * half + off, slab), :] = value
 
-        place_blocks(pos_ref, blocks, put, n_blk, n_rep, slab)
+        place_blocks(pos, blocks, put, n_blk, n_rep, slab)
     for k, block in enumerate(mine):
-        at = jnp.bitwise_xor(pos_ref[0], k)
+        at = jnp.bitwise_xor(pos[0], k)
         for r in range(n_rep):
             off = pl.multiple_of((r * n_blk + at) * slab, slab)
             meta[:, pl.ds(off, slab)] = block[n_rep * slab :, r * slab : (r + 1) * slab].astype(F32)
     ep_ref[...] = meta[2:3, :]
     for r in range(n_rep):
         own = slice(r * batch, (r + 1) * batch)
-        goal = column(meta[0:1, own] * 256.0 + meta[1:2, own]).astype(jnp.int32) + pos_ref[1] * half
+        goal = column(meta[0:1, own] * 256.0 + meta[1:2, own]).astype(jnp.int32) + pos[1] * half
         goal = jnp.where(goal >= rows, goal - rows, goal)
         pick_ref[own, :] = jnp.where(
             goal == lax.broadcasted_iota(jnp.int32, (batch, rows), 1), 1.0, 0.0
@@ -138,7 +141,7 @@
     goals_ref[...] = dot(pick_ref[...], both_sides[...]).astype(BF)
 
 
-def contrast_kernel(n_blk, n_rep, slab, scale, pos_ref, *refs):
+def contrast_kernel(n_blk, n_rep, slab, scale, pos, *refs):
     n = n_blk + 1
     mine, other, ep_ref, pick_ref = refs[:n], refs[n : 2 * n], refs[2 * n], refs[2 * n + 1]
     grads_ref, phi_all, psi_all = refs[2 * n + 2 :]
@@ -158,8 +161,8 @@
     def put_other(off, value):
         psi_all[pl.ds(half + off, slab), :] = value[:, emb:]
 
-    place_blocks(pos_ref, sums(mine), put_mine, n_blk, n_rep, slab)
-    place_blocks(pos_ref, sums(other), put_other, n_blk, n_rep, slab)
+    place_blocks(pos, sums(mine), put_mine, n_blk, n_rep, slab)
+    place_blocks(pos, sums(other), put_other, n_blk, n_rep, slab)
     diagonal = lax.broadcasted_iota(jnp.int32, (batch, batch), 0) == lax.broadcasted_iota(
         jnp.int32, (batch, batch), 1
     )
@@ -198,15 +201,15 @@
     return dot(active[...], grad), dot(back[...], rows_ref[...])
 
 
-def mine_kernel(pos_ref, sf, gf, ss, gs, grads_ref, rows_ref, goals_ref, *refs):
+def mine_kernel(pos, sf, gf, ss, gs, grads_ref, rows_ref, goals_ref, *refs):
     outs, (active, back) = refs[:4], refs[4:]
     quarter = active.shape[0]
-    at = pl.multiple_of(pos_ref[1] * quarter, quarter)
+    at = pl.multiple_of(pos[1] * quarter, quarter)
     outs[0][...], outs[1][...] = rows_grads(at, sf, ss, grads_ref, 0, rows_ref, active, back)
     outs[2][...], outs[3][...] = rows_grads(at, gf, gs, grads_ref, 1, goals_ref, active, back)
 
 
-def other_kernel(k, n_put, pos_ref, first, second, grads_ref, rows_ref, sum_second, sum_first, *refs):
+def other_kernel(k, n_put, pos, first, second, grads_ref, rows_ref, sum_second, sum_first, *refs):
     done, outs, puts, (active, back), sems = (
         refs[:n_put],
         refs[n_put : n_put + 4],
@@ -214,11 +217,11 @@
         refs[2 * n_put + 4 : 2 * n_put + 6],
         refs[2 * n_put + 6 :],
     )
-    copies = [put_half(pos_ref[1], x, o, sems[0].at[i]) for i, (x, o) in enumerate(zip(done, puts))]
+    copies = [put_half(pos[1], x, o, sems[0].at[i]) for i, (x, o) in enumerate(zip(done, puts))]
     for c in copies:
         c.start()
     quarter = active.shape[0]
-    at = pl.multiple_of(pos_ref[1] * quarter, quarter)
+    at = pl.multiple_of(pos[1] * quarter, quarter)
     grad_second, grad_first = rows_grads(at, first, second, grads_ref, k, rows_ref, active, back)
     halves = ((sum_first[...] + grad_first).astype(BF).T, (sum_second[...] + grad_second).astype(BF))
     for half, out16, out32 in zip(halves, outs[:2], outs[2:]):
@@ -237,21 +240,21 @@
     return pltpu.make_async_copy(half, to, sem)
 
 
-def finish_kernel(old, new, pos_ref, *refs):
+def finish_kernel(old, new, pos, *refs):
     n = old + new
     halves, outs, scratch, sems = refs[:n], refs[n + old : 2 * n + old], refs[2 * n + old : -1], refs[-1]
-    copies = [put_half(pos_ref[1], x, o, sems.at[old + i]) for i, (x, o) in enumerate(zip(halves[old:], outs[old:]))]
+    copies = [put_half(pos[1], x, o, sems.at[old + i]) for i, (x, o) in enumerate(zip(halves[old:], outs[old:]))]
     for c in copies:
         c.start()
     for i in range(old):
         scratch[i][...] = halves[i][...].astype(F32)
-        copies.append(put_half(1 - pos_ref[1], scratch[i], outs[i], sems.at[i]))
+        copies.append(put_half(1 - pos[1], scratch[i], outs[i], sems.at[i]))
         copies[-1].start()
     for c in copies:
         c.wait()
 
 
-def finish(pos, there, own, wholes, shapes):
+def finish(there, own, wholes, shapes):
     old, new = len(wholes), len(shapes)
     n = old + new
     return kernel(
@@ -260,7 +263,7 @@
         [(w.shape, w.dtype) for w in wholes] + shapes,
         (*there, *own, *wholes),
         [*(pltpu.VMEM(x.shape, F32) for x in there), pltpu.SemaphoreType.DMA((n,))],
-        pos=pos,
+        pos=True,
         hbm=range(n, n + old),
         hbm_out=range(n),
         aliases={n + i: i for i in range(old)},
@@ -272,12 +275,9 @@
 ):
     rows_dev, width = states.shape
     n_blk, n_rep, n_sub = (lax.axis_size(a) for a in ("blk", "rep", "sub"))
-    owners = n_blk * n_sub
     slab = rows_dev // n_rep
-    rows_all = owners * rows_dev
+    rows_all = n_blk * n_sub * rows_dev
     hid, emb = state_second.shape
-    b, s = lax.axis_index("blk"), lax.axis_index("sub")
-    pos = jnp.stack([b, s]).astype(jnp.int32)
     quarter = hid // n_sub
 
     def across(x, k):
@@ -295,7 +295,7 @@
         "pack",
         [((rows_dev + 16, width), BF)],
         (states, jnp.stack([goal_distance.reshape(rows_dev), goal_row, episode])),
-        pos=pos,
+        pos=True,
         limit=4,
         flops=2**32,
     )
@@ -324,7 +324,7 @@
             pltpu.VMEM((rows_all, width), BF),
             pltpu.VMEM((16, rows_all // 2), F32),
         ],
-        pos=pos,
+        pos=True,
     )
     embedded = [sums[0], sums[1], part2, sums[3], after(there2, pick)]
     (grads_mine,) = kernel(
@@ -333,7 +333,7 @@
         [((rows_all // 2, 2 * emb), BF)],
         (*embedded, *(swap(x, "sub") for x in embedded), episodes, pick),
         [pltpu.VMEM((rows_all // 2, emb), BF), pltpu.VMEM((rows_all, emb), BF)],
-        pos=pos,
+        pos=True,
     )
     grads_other = swap(grads_mine, "sub")
     goals_other = swap(goals_mine, "sub")
@@ -347,7 +347,7 @@
         [((quarter, emb), F32), ((quarter, width), F32)] * 2,
         (sf, gf, ss, gs, grads_mine, mine, goals_mine),
         work,
-        pos=pos,
+        pos=True,
         flops=2 * flops,
     )
     halves = [(shape, kind) for kind in (BF, F32) for shape in ((width, quarter), (quarter, emb))]
@@ -358,7 +358,7 @@
         halves,
         (sf, ss, grads_other, other, sums_s2, sums_s1),
         work,
-        pos=pos,
+        pos=True,
         flops=flops,
     )
     state_there = [swap(x, "sub") for x in state_halves]
@@ -368,13 +368,13 @@
         halves + wholes,
         (gf, gs, grads_other, goals_other, sums_g2, sums_g1, state_first_own, state_second_own),
         work + [pltpu.SemaphoreType.DMA((2,))],
-        pos=pos,
+        pos=True,
         flops=flops,
         hbm_out=(4, 5),
     )
     goal_there = [swap(x, "sub") for x in goal_halves]
-    out0, out1, out2, out3 = finish(pos, state_there, (goal_first_own, goal_second_own), (out0, out1), wholes)
-    out2, out3 = finish(pos, goal_there, (), (out2, out3), [])
+    out0, out1, out2, out3 = finish(state_there, (goal_first_own, goal_second_own), (out0, out1), wholes)
+    out2, out3 = finish(goal_there, (), (out2, out3), [])
     return (out0, out1, out2, out3)
 
 

time: 56.5 us -> 52.1 us (0.922)
  Pallas kernels: 29.8 us -> 24.9 us
  waiting for transfers between devices: 6.62 us -> 7.25 us
    pallas_call x13, Pallas kernels: 29.8 us -> 24.9 us  [kernel(): pl.pallas_call(body, in_specs=specs, out_specs=[HBM if i in hbm_out else...]
  transfers between devices with their start and end apart: 22 -> 22, of which waited for: 8 -> 9; matrix products, arithmetic and copies ran while one was open for 0% -> 0% of each run, Pallas kernels for 40% -> 37%
where the time goes in v12:
time: 52.1 us; the launch traced here: 52 us
  Pallas kernels  24.9 us (48%)
  starting transfers between devices  17.2 us (33%)
  waiting for transfers between devices  7.25 us (14%)
  between operations  0.94 us (2%)
  local copies, waits for them, and re-layouts  0.92 us (2%)
  other arithmetic  0.72 us (1%)
    pallas_call x13, Pallas kernels, kernel(): pl.pallas_call(body, in_specs=specs, out_specs=[HBM if i in hbm_out else...  24.9 us
    ppermute x4, starting transfers between devices, across(): return lax.ppermute(x, 'blk', [(i, i ^ k) for i in range(n_blk)])  9.22 us
    ppermute x18, starting transfers between devices, swap(): return lax.ppermute(x, axis, [(0, 1), (1, 0)])  8 us
    ppermute x4, waiting for transfers between devices, across(): return lax.ppermute(x, 'blk', [(i, i ^ k) for i in range(n_blk)])  5.01 us
    ppermute x18, waiting for transfers between devices, swap(): return lax.ppermute(x, axis, [(0, 1), (1, 0)])  2.24 us
  transfers between devices with their start and end apart: 22, of which 9 were waited for; matrix products, arithmetic and copies ran while one was open for 0% of the time, Pallas kernels for 37%

profile of v12, /device:TPU:0, one launch (start us, length us, event | category | flops | bytes accessed | tf_op | source)
XLA Modules:
  0.0 52.0 jit_solution(9542871734203343372)
XLA Ops:
  0.6 0.7 %pad_add_fusion.refs_1_ = s32[3,256]{1,0:T(4,128)S(1)} fusion(s32[1,256]{1,0:T(1,128)} %bitcast.3, s32[1,256]{1,0:T(1,128)} %bitcast.4, s32[1,256]{1,0:T(1,128)} %bitcast.5), kind=kLoop, calls=%fused_computation | loop fusion | flops 1536 | bytes 6144 | tf_op jit(solution)/shard_map/stack | solution.py:297
  1.4 0.0 copy-start.4
  1.4 0.9 %copy-done.4 = bf16[256,256]{1,0:T(8,128)(2,1)S(1)} copy-done((bf16[256,256]{1,0:T(8,128)(2,1)S(1)}, bf16[256,256]{1,0:T(8,128)(2,1)}, u32[]{:S(2)}) %copy-start.4) | copy-done | bytes 131096
  2.3 0.0 copy-start
  2.3 5.1 %collective-permute-start.1 = (bf16[272,256]{1,0:T(8,128)(2,1)S(1)}, bf16[272,256]{1,0:T(8,128)(2,1)S(1)}, u32[]{:S(2)}, u32[]{:S(2)}) collective-permute-start(bf16[272,256]{1,0:T(8,128)(2,1)S(1)} %pack.1.x_ref.refs_0_), channel_id=1, source_target_pairs={{0,12},{4,8},{8,4},{12,0},{1,13},{5,9},{9,5},{13,1},{2,14},{6,10},... | collective-permute-start | bytes 417800 | tf_op jit(solution)/shard_map/ppermute | solution.py:284
  7.4 0.0 copy-done
  7.4 0.0 copy-done.1
  7.4 0.0 copy-done.2
  7.4 0.0 copy-done.3
  7.4 1.4 %forward.3.a_ref = bf16[256,512]{1,0:T(8,128)(2,1)S(1)} custom-call(bf16[272,256]{1,0:T(8,128)(2,1)S(1)} %pack.1.x_ref.refs_0_, bf16[256,2048]{1,0:T(8,128)(2,1)S(1)} %copy-done, bf16[256,2048]{1,0:T(8,128)(2,1)S(1)} %copy-done.2, bf16[2048,256]{1,0:T(8,128)(2,1)S(1)} %copy-done.1, bf16[2048,256]{1,0:T(8,128)(2,1)S(1)} %copy-done.3), custom_call_target="tpu_custom_call" | custom-call | tf_op jit(solution)/shard_map/forward/pallas_call | solution.py:37
  8.8 1.6 %collective-permute-start = (bf16[256,512]{1,0:T(8,128)(2,1)S(1)}, bf16[256,512]{1,0:T(8,128)(2,1)S(1)}, u32[]{:S(2)}, u32[]{:S(2)}) collective-permute-start(bf16[256,512]{1,0:T(8,128)(2,1)S(1)} %forward.3.a_ref), channel_id=1, source_target_pairs={{0,2},{2,0},{1,3},{3,1},{4,6},{6,4},{5,7},{7,5},{8,10},{10,8},{9,1... | collective-permute-start | bytes 786440 | tf_op jit(solution)/shard_map/ppermute | solution.py:287
  10.4 0.8 %collective-permute-done.1.x_ref.refs_3_ = bf16[272,256]{1,0:T(8,128)(2,1)S(1)} collective-permute-done((bf16[272,256]{1,0:T(8,128)(2,1)S(1)}, bf16[272,256]{1,0:T(8,128)(2,1)S(1)}, u32[]{:S(2)}, u32[]{:S(2)}) %collective-permute-start.1) | collective-permute-done | bytes 139296 | tf_op jit(solution)/shard_map/ppermute | solution.py:284
  11.2 3.6 %collective-permute-start.2 = (bf16[272,256]{1,0:T(8,128)(2,1)S(1)}, bf16[272,256]{1,0:T(8,128)(2,1)S(1)}, u32[]{:S(2)}, u32[]{:S(2)}) collective-permute-start(bf16[272,256]{1,0:T(8,128)(2,1)S(1)} %pack.1.x_ref.refs_0_), channel_id=1, source_target_pairs={{0,8},{4,12},{8,0},{12,4},{1,9},{5,13},{9,1},{13,5},{2,10},{6,14},... | collective-permute-start | bytes 417800 | tf_op jit(solution)/shard_map/ppermute | solution.py:284
  14.8 1.4 %forward.5.a_ref = bf16[256,512]{1,0:T(8,128)(2,1)S(1)} custom-call(bf16[272,256]{1,0:T(8,128)(2,1)S(1)} %collective-permute-done.1.x_ref.refs_3_, bf16[256,2048]{1,0:T(8,128)(2,1)S(1)} %copy-done, bf16[256,2048]{1,0:T(8,128)(2,1)S(1)} %copy-done.2, bf16[2048,256]{1,0:T(8,128)(2,1)S(1)} %copy-done.1, bf16[2048,256]{1,0:T(8,128)(2,1)S(1)} %copy-done.3), custom_call_target="tpu_custom_call" | custom-call | tf_op jit(solution)/shard_map/forward/pallas_call | solution.py:37
  16.2 1.6 %collective-permute-start.4 = (bf16[256,512]{1,0:T(8,128)(2,1)S(1)}, bf16[256,512]{1,0:T(8,128)(2,1)S(1)}, u32[]{:S(2)}, u32[]{:S(2)}) collective-permute-start(bf16[256,512]{1,0:T(8,128)(2,1)S(1)} %forward.5.a_ref), channel_id=1, source_target_pairs={{0,2},{2,0},{1,3},{3,1},{4,6},{6,4},{5,7},{7,5},{8,10},{10,8},{9,1... | collective-permute-start | bytes 786440 | tf_op jit(solution)/shard_map/ppermute | solution.py:287
  17.7 0.0 collective-permute-start.7
  17.7 0.5 collective-permute-start.6
  18.2 0.0 collective-permute-done.b_ref
  18.2 0.1 both.2.refs_0_
  18.3 2.0 %collective-permute-done.2.x_ref.refs_2_ = bf16[272,256]{1,0:T(8,128)(2,1)S(1)} collective-permute-done((bf16[272,256]{1,0:T(8,128)(2,1)S(1)}, bf16[272,256]{1,0:T(8,128)(2,1)S(1)}, u32[]{:S(2)}, u32[]{:S(2)}) %collective-permute-start.2) | collective-permute-done | bytes 139296 | tf_op jit(solution)/shard_map/ppermute | solution.py:284
  20.3 1.4 %forward.4.refs_2_ = bf16[256,512]{1,0:T(8,128)(2,1)S(1)} custom-call(bf16[272,256]{1,0:T(8,128)(2,1)S(1)} %collective-permute-done.2.x_ref.refs_2_, bf16[256,2048]{1,0:T(8,128)(2,1)S(1)} %copy-done, bf16[256,2048]{1,0:T(8,128)(2,1)S(1)} %copy-done.2, bf16[2048,256]{1,0:T(8,128)(2,1)S(1)} %copy-done.1, bf16[2048,256]{1,0:T(8,128)(2,1)S(1)} %copy-done.3), custom_call_target="tpu_custom_call" | custom-call | tf_op jit(solution)/shard_map/forward/pallas_call | solution.py:37
  21.7 1.6 %collective-permute-start.5 = (bf16[256,512]{1,0:T(8,128)(2,1)S(1)}, bf16[256,512]{1,0:T(8,128)(2,1)S(1)}, u32[]{:S(2)}, u32[]{:S(2)}) collective-permute-start(bf16[256,512]{1,0:T(8,128)(2,1)S(1)} %forward.4.refs_2_), channel_id=1, source_target_pairs={{0,2},{2,0},{1,3},{3,1},{4,6},{6,4},{5,7},{7,5},{8,10},{10,8},{9,1... | collective-permute-start | bytes 786440 | tf_op jit(solution)/shard_map/ppermute | solution.py:287
  23.3 0.0 collective-permute-start.3
  23.3 0.0 collective-permute-done.7.refs_4_
  23.3 0.0 collective-permute-start.10
  23.3 0.9 %collective-permute-done.6.refs_1_ = bf16[272,256]{1,0:T(8,128)(2,1)S(1)} collective-permute-done((bf16[272,256]{1,0:T(8,128)(2,1)S(1)}, bf16[272,256]{1,0:T(8,128)(2,1)S(1)}, u32[]{:S(2)}, u32[]{:S(2)}) %collective-permute-start.6) | collective-permute-done | bytes 139296 | tf_op jit(solution)/shard_map/ppermute | solution.py:284
  24.2 0.0 collective-permute-start.8
  24.2 0.0 collective-permute-done.4.b_ref
  24.2 0.5 collective-permute-start.9
  24.7 0.1 both.3.refs_3_
  24.8 0.0 collective-permute-done.10.refs_7_
  24.8 0.1 collective-permute-start.11
  24.9 0.7 %collective-permute-done.8.refs_5_ = bf16[272,256]{1,0:T(8,128)(2,1)S(1)} collective-permute-done((bf16[272,256]{1,0:T(8,128)(2,1)S(1)}, bf16[272,256]{1,0:T(8,128)(2,1)S(1)}, u32[]{:S(2)}, u32[]{:S(2)}) %collective-permute-start.8) | collective-permute-done | bytes 139296 | tf_op jit(solution)/shard_map/ppermute | solution.py:287
  25.6 0.1 collective-permute-start.13
  25.7 0.1 collective-permute-done.9.refs_6_
  25.8 0.3 collective-permute-start.14
  26.1 2.3 %arrange.1 = (bf16[1024,256]{1,0:T(8,128)(2,1)S(1)}, bf16[1024,256]{1,0:T(8,128)(2,1)S(1)}, bf16[1024,256]{1,0:T(8,128)(2,1)S(1)}, bf16[1024,2048]{1,0:T(8,128)(2,1)S(1)}, f32[1,1024]{1,0:T(1,128)S(1)}) custom-call(bf16[272,256]{1,0:T(8,128)(2,1)S(1)} %pack.1.x_ref.refs_0_, bf16[272,256]{1,0:T(8,128)(2,1)S(1)} %collective-permute-done.6.refs_1_, ...), custom_call_target="tpu_custom_call" | custom-call | tf_op jit(solution)/shard_map/arrange/pallas_call | solution.py:37
  28.4 0.0 collective-permute-done.5.refs_4_
  28.4 1.3 %collective-permute-done.3.refs_1_ = bf16[256,512]{1,0:T(8,128)(2,1)S(1)} collective-permute-done((bf16[256,512]{1,0:T(8,128)(2,1)S(1)}, bf16[256,512]{1,0:T(8,128)(2,1)S(1)}, u32[]{:S(2)}, u32[]{:S(2)}) %collective-permute-start.3) | collective-permute-done | bytes 262176 | tf_op jit(solution)/shard_map/ppermute | solution.py:284
  29.7 0.0 collective-permute-start.12
  29.7 0.5 collective-permute-start.15
  30.2 0.0 collective-permute-done.11.refs_5_
  30.2 0.0 collective-permute-done.13.refs_7_
  30.2 0.0 collective-permute-done.14.refs_8_
  30.2 1.0 %collective-permute-done.12.refs_6_ = bf16[256,512]{1,0:T(8,128)(2,1)S(1)} collective-permute-done((bf16[256,512]{1,0:T(8,128)(2,1)S(1)}, bf16[256,512]{1,0:T(8,128)(2,1)S(1)}, u32[]{:S(2)}, u32[]{:S(2)}) %collective-permute-start.12) | collective-permute-done | bytes 262176 | tf_op jit(solution)/shard_map/ppermute | solution.py:287
  31.2 0.4 collective-permute-done.15.refs_9_
  31.6 4.1 %contrast.1.refs_4_ = bf16[1024,512]{1,0:T(8,128)(2,1)S(1)} custom-call(bf16[256,512]{1,0:T(8,128)(2,1)S(1)} %both.2.refs_0_, bf16[256,512]{1,0:T(8,128)(2,1)S(1)} %collective-permute-done.3.refs_1_, bf16[256,512]{1,0:T(8,128)(2,1)S(1)} %forward.4.refs_2_, bf16[256,512]{1,0:T(8,128)(2,1)S(1)} %both.3.refs_3_, ...), custom_call_target="tpu_custom_call" | custom-call | tf_op jit(solution)/shard_map/contrast/pallas_call | solution.py:37
  35.7 0.2 collective-permute-start.16
  35.9 0.4 collective-permute-start.19
  36.3 5.2 %mine.1 = (f32[1024,256]{1,0:T(8,128)S(1)}, f32[1024,256]{1,0:T(8,128)S(1)}, f32[1024,256]{1,0:T(8,128)S(1)}, f32[1024,256]{1,0:T(8,128)S(1)}) custom-call(bf16[256,2048]{1,0:T(8,128)(2,1)S(1)} %copy-done, bf16[256,2048]{1,0:T(8,128)(2,1)S(1)} %copy-done.2, bf16[2048,256]{1,0:T(8,128)(2,1)S(1)} %copy-done.1, bf16[2048,256]{1,0:T(8,128)(2,1)S(1)} %copy-done.3, ...), custom_call_target="tpu_custom_call" | custom-call | flops 4294967296 | tf_op jit(solution)/shard_map/mine/pallas_call | solution.py:37
  41.5 0.0 collective-permute-done.16.refs_2_
  41.5 2.7 %other_state.1 = (bf16[256,1024]{1,0:T(8,128)(2,1)S(1)}, bf16[1024,256]{1,0:T(8,128)(2,1)S(1)}, f32[256,1024]{1,0:T(8,128)S(1)}, f32[1024,256]{1,0:T(8,128)S(1)}) custom-call(bf16[256,2048]{1,0:T(8,128)(2,1)S(1)} %copy-done, bf16[2048,256]{1,0:T(8,128)(2,1)S(1)} %copy-done.1, bf16[1024,512]{1,0:T(8,128)(2,1)S(1)} %collective-permute-done.16.refs_2_, ...), custom_call_target="tpu_custom_call" | custom-call | flops 2147483648 | tf_op jit(solution)/shard_map/other_state/pallas_call | solution.py:37
  44.2 0.2 collective-permute-start.17
  44.4 0.4 collective-permute-start.18
  44.8 0.0 collective-permute-done.19.refs_3_
  44.8 2.9 %other_goal.1 = (bf16[256,1024]{1,0:T(8,128)(2,1)S(1)}, bf16[1024,256]{1,0:T(8,128)(2,1)S(1)}, f32[256,1024]{1,0:T(8,128)S(1)}, f32[1024,256]{1,0:T(8,128)S(1)},...) custom-call(bf16[256,2048]{1,0:T(8,128)(2,1)S(1)} %copy-done.2, bf16[2048,256]{1,0:T(8,128)(2,1)S(1)} %copy-done.3, ...), custom_call_target="tpu_custom_call" | custom-call | flops 2147483648 | tf_op jit(solution)/shard_map/other_goal/pallas_call | solution.py:37
  47.7 0.2 collective-permute-start.20
  47.9 0.4 collective-permute-start.21
  48.3 0.0 collective-permute-done.17.refs_0_
  48.3 0.0 collective-permute-done.18.refs_1_
  48.3 2.0 %finish.2 = (f32[256,2048]{1,0:T(8,128)}, f32[2048,256]{1,0:T(8,128)}, f32[256,2048]{1,0:T(8,128)}, f32[2048,256]{1,0:T(8,128)}) custom-call(bf16[256,1024]{1,0:T(8,128)(2,1)S(1)} %collective-permute-done.17.refs_0_, bf16[1024,256]{1,0:T(8,128)(2,1)S(1)} %collective-permute-done.18.refs_1_, ...), custom_call_target="tpu_custom_call", output_to_operand_aliasing={{0}: (4, {}), {1}: (5, {})} | custom-call | tf_op jit(solution)/shard_map/finish/pallas_call | solution.py:37
  50.3 0.0 collective-permute-done.20.refs_0_
  50.3 0.1 collective-permute-done.21.refs_1_
  50.4 1.4 %finish.3 = (f32[256,2048]{1,0:T(8,128)}, f32[2048,256]{1,0:T(8,128)}) custom-call(bf16[256,1024]{1,0:T(8,128)(2,1)S(1)} %collective-permute-done.20.refs_0_, bf16[1024,256]{1,0:T(8,128)(2,1)S(1)} %collective-permute-done.21.refs_1_, f32[256,2048]{1,0:T(8,128)} %get-tuple-element.60.refs_2_, ...), custom_call_target="tpu_custom_call", output_to_operand_aliasing={{0}: (2, {}), {1}: (3, {})} | custom-call | tf_op jit(solution)/shard_map/finish/pallas_call | solution.py:37
  (4 shorter events, 0.0 us)
Async XLA Ops:
  1.4 0.9 %copy-start.4 = (bf16[256,256]{1,0:T(8,128)(2,1)S(1)}, bf16[256,256]{1,0:T(8,128)(2,1)}, u32[]{:S(2)}) copy-start(bf16[256,256]{1,0:T(8,128)(2,1)} %refs_0_.7) | copy-start | bytes 393220
  2.3 5.2 %copy-start = (bf16[256,2048]{1,0:T(8,128)(2,1)S(1)}, bf16[256,2048]{1,0:T(8,128)(2,1)}, u32[]{:S(2)}) copy-start(bf16[256,2048]{1,0:T(8,128)(2,1)} %refs_0_.12) | copy-start | bytes 3145732
  2.3 5.2 %copy-start.1 = (bf16[2048,256]{1,0:T(8,128)(2,1)S(1)}, bf16[2048,256]{1,0:T(8,128)(2,1)}, u32[]{:S(2)}) copy-start(bf16[2048,256]{1,0:T(8,128)(2,1)} %refs_1_.10) | copy-start | bytes 3145732
  2.3 5.2 %copy-start.2 = (bf16[256,2048]{1,0:T(8,128)(2,1)S(1)}, bf16[256,2048]{1,0:T(8,128)(2,1)}, u32[]{:S(2)}) copy-start(bf16[256,2048]{1,0:T(8,128)(2,1)} %refs_0_.13) | copy-start | bytes 3145732
  2.3 5.2 %copy-start.3 = (bf16[2048,256]{1,0:T(8,128)(2,1)S(1)}, bf16[2048,256]{1,0:T(8,128)(2,1)}, u32[]{:S(2)}) copy-start(bf16[2048,256]{1,0:T(8,128)(2,1)} %refs_1_.11) | copy-start | bytes 3145732
  2.3 8.9 %collective-permute-start.1 = (bf16[272,256]{1,0:T(8,128)(2,1)S(1)}, bf16[272,256]{1,0:T(8,128)(2,1)S(1)}, u32[]{:S(2)}, u32[]{:S(2)}) collective-permute-start(bf16[272,256]{1,0:T(8,128)(2,1)S(1)} %pack.1.x_ref.refs_0_), channel_id=1, source_target_pairs={{0,12},{4,8},{8,4},{12,0},{1,13},{5,9},{9,5},{13,1},{2,14},{6,10},... | collective-permute-start | bytes 417800 | tf_op jit(solution)/shard_map/ppermute | solution.py:284
  8.8 9.4 %collective-permute-start = (bf16[256,512]{1,0:T(8,128)(2,1)S(1)}, bf16[256,512]{1,0:T(8,128)(2,1)S(1)}, u32[]{:S(2)}, u32[]{:S(2)}) collective-permute-start(bf16[256,512]{1,0:T(8,128)(2,1)S(1)} %forward.3.a_ref), channel_id=1, source_target_pairs={{0,2},{2,0},{1,3},{3,1},{4,6},{6,4},{5,7},{7,5},{8,10},{10,8},{9,1... | collective-permute-start | bytes 786440 | tf_op jit(solution)/shard_map/ppermute | solution.py:287
  11.2 9.1 %collective-permute-start.2 = (bf16[272,256]{1,0:T(8,128)(2,1)S(1)}, bf16[272,256]{1,0:T(8,128)(2,1)S(1)}, u32[]{:S(2)}, u32[]{:S(2)}) collective-permute-start(bf16[272,256]{1,0:T(8,128)(2,1)S(1)} %pack.1.x_ref.refs_0_), channel_id=1, source_target_pairs={{0,8},{4,12},{8,0},{12,4},{1,9},{5,13},{9,1},{13,5},{2,10},{6,14},... | collective-permute-start | bytes 417800 | tf_op jit(solution)/shard_map/ppermute | solution.py:284
  16.2 8.0 %collective-permute-start.4 = (bf16[256,512]{1,0:T(8,128)(2,1)S(1)}, bf16[256,512]{1,0:T(8,128)(2,1)S(1)}, u32[]{:S(2)}, u32[]{:S(2)}) collective-permute-start(bf16[256,512]{1,0:T(8,128)(2,1)S(1)} %forward.5.a_ref), channel_id=1, source_target_pairs={{0,2},{2,0},{1,3},{3,1},{4,6},{6,4},{5,7},{7,5},{8,10},{10,8},{9,1... | collective-permute-start | bytes 786440 | tf_op jit(solution)/shard_map/ppermute | solution.py:287
  17.7 5.6 %collective-permute-start.7 = (bf16[272,256]{1,0:T(8,128)(2,1)S(1)}, bf16[272,256]{1,0:T(8,128)(2,1)S(1)}, u32[]{:S(2)}, u32[]{:S(2)}) collective-permute-start(bf16[272,256]{1,0:T(8,128)(2,1)S(1)} %pack.1.x_ref.refs_0_), channel_id=1, source_target_pairs={{0,1},{1,0},{2,3},{3,2},{4,5},{5,4},{6,7},{7,6},{8,9},{9,8},{10,11... | collective-permute-start | bytes 417800 | tf_op jit(solution)/shard_map/ppermute | solution.py:287
  17.7 6.5 %collective-permute-start.6 = (bf16[272,256]{1,0:T(8,128)(2,1)S(1)}, bf16[272,256]{1,0:T(8,128)(2,1)S(1)}, u32[]{:S(2)}, u32[]{:S(2)}) collective-permute-start(bf16[272,256]{1,0:T(8,128)(2,1)S(1)} %pack.1.x_ref.refs_0_), channel_id=1, source_target_pairs={{0,4},{4,0},{8,12},{12,8},{1,5},{5,1},{9,13},{13,9},{2,6},{6,2},{1... | collective-permute-start | bytes 417800 | tf_op jit(solution)/shard_map/ppermute | solution.py:284
  21.7 6.7 %collective-permute-start.5 = (bf16[256,512]{1,0:T(8,128)(2,1)S(1)}, bf16[256,512]{1,0:T(8,128)(2,1)S(1)}, u32[]{:S(2)}, u32[]{:S(2)}) collective-permute-start(bf16[256,512]{1,0:T(8,128)(2,1)S(1)} %forward.4.refs_2_), channel_id=1, source_target_pairs={{0,2},{2,0},{1,3},{3,1},{4,6},{6,4},{5,7},{7,5},{8,10},{10,8},{9,1... | collective-permute-start | bytes 786440 | tf_op jit(solution)/shard_map/ppermute | solution.py:287
  23.3 6.4 %collective-permute-start.3 = (bf16[256,512]{1,0:T(8,128)(2,1)S(1)}, bf16[256,512]{1,0:T(8,128)(2,1)S(1)}, u32[]{:S(2)}, u32[]{:S(2)}) collective-permute-start(bf16[256,512]{1,0:T(8,128)(2,1)S(1)} %both.2.refs_0_), channel_id=1, source_target_pairs={{0,4},{4,0},{8,12},{12,8},{1,5},{5,1},{9,13},{13,9},{2,6},{6,2},{1... | collective-permute-start | bytes 786440 | tf_op jit(solution)/shard_map/ppermute | solution.py:284
  23.3 1.5 %collective-permute-start.10 = (bf16[272,256]{1,0:T(8,128)(2,1)S(1)}, bf16[272,256]{1,0:T(8,128)(2,1)S(1)}, u32[]{:S(2)}, u32[]{:S(2)}) collective-permute-start(bf16[272,256]{1,0:T(8,128)(2,1)S(1)} %collective-permute-done.1.x_ref.refs_3_), channel_id=1, source_target_pairs={{0,1},{1,0},{2,3},{3,2},{4,5},{5,4},{6,7},{7,6},{8,9},{9,8},{10,11... | collective-permute-start | bytes 417800 | tf_op jit(solution)/shard_map/ppermute | solution.py:287
  24.2 1.4 %collective-permute-start.8 = (bf16[272,256]{1,0:T(8,128)(2,1)S(1)}, bf16[272,256]{1,0:T(8,128)(2,1)S(1)}, u32[]{:S(2)}, u32[]{:S(2)}) collective-permute-start(bf16[272,256]{1,0:T(8,128)(2,1)S(1)} %collective-permute-done.6.refs_1_), channel_id=1, source_target_pairs={{0,1},{1,0},{2,3},{3,2},{4,5},{5,4},{6,7},{7,6},{8,9},{9,8},{10,11... | collective-permute-start | bytes 417800 | tf_op jit(solution)/shard_map/ppermute | solution.py:287
  24.2 1.6 %collective-permute-start.9 = (bf16[272,256]{1,0:T(8,128)(2,1)S(1)}, bf16[272,256]{1,0:T(8,128)(2,1)S(1)}, u32[]{:S(2)}, u32[]{:S(2)}) collective-permute-start(bf16[272,256]{1,0:T(8,128)(2,1)S(1)} %collective-permute-done.2.x_ref.refs_2_), channel_id=1, source_target_pairs={{0,1},{1,0},{2,3},{3,2},{4,5},{5,4},{6,7},{7,6},{8,9},{9,8},{10,11... | collective-permute-start | bytes 417800 | tf_op jit(solution)/shard_map/ppermute | solution.py:287
  24.8 5.4 %collective-permute-start.11 = (bf16[256,512]{1,0:T(8,128)(2,1)S(1)}, bf16[256,512]{1,0:T(8,128)(2,1)S(1)}, u32[]{:S(2)}, u32[]{:S(2)}) collective-permute-start(bf16[256,512]{1,0:T(8,128)(2,1)S(1)} %both.2.refs_0_), channel_id=1, source_target_pairs={{0,1},{1,0},{2,3},{3,2},{4,5},{5,4},{6,7},{7,6},{8,9},{9,8},{10,11... | collective-permute-start | bytes 786440 | tf_op jit(solution)/shard_map/ppermute | solution.py:287
  25.6 4.6 %collective-permute-start.13 = (bf16[256,512]{1,0:T(8,128)(2,1)S(1)}, bf16[256,512]{1,0:T(8,128)(2,1)S(1)}, u32[]{:S(2)}, u32[]{:S(2)}) collective-permute-start(bf16[256,512]{1,0:T(8,128)(2,1)S(1)} %forward.4.refs_2_), channel_id=1, source_target_pairs={{0,1},{1,0},{2,3},{3,2},{4,5},{5,4},{6,7},{7,6},{8,9},{9,8},{10,11... | collective-permute-start | bytes 786440 | tf_op jit(solution)/shard_map/ppermute | solution.py:287
  25.8 4.5 %collective-permute-start.14 = (bf16[256,512]{1,0:T(8,128)(2,1)S(1)}, bf16[256,512]{1,0:T(8,128)(2,1)S(1)}, u32[]{:S(2)}, u32[]{:S(2)}) collective-permute-start(bf16[256,512]{1,0:T(8,128)(2,1)S(1)} %both.3.refs_3_), channel_id=1, source_target_pairs={{0,1},{1,0},{2,3},{3,2},{4,5},{5,4},{6,7},{7,6},{8,9},{9,8},{10,11... | collective-permute-start | bytes 786440 | tf_op jit(solution)/shard_map/ppermute | solution.py:287
  29.7 1.5 %collective-permute-start.12 = (bf16[256,512]{1,0:T(8,128)(2,1)S(1)}, bf16[256,512]{1,0:T(8,128)(2,1)S(1)}, u32[]{:S(2)}, u32[]{:S(2)}) collective-permute-start(bf16[256,512]{1,0:T(8,128)(2,1)S(1)} %collective-permute-done.3.refs_1_), channel_id=1, source_target_pairs={{0,1},{1,0},{2,3},{3,2},{4,5},{5,4},{6,7},{7,6},{8,9},{9,8},{10,11... | collective-permute-start | bytes 786440 | tf_op jit(solution)/shard_map/ppermute | solution.py:287
  29.7 1.9 %collective-permute-start.15 = (bf16[256,512]{1,0:T(8,128)(2,1)S(1)}, bf16[256,512]{1,0:T(8,128)(2,1)S(1)}, u32[]{:S(2)}, u32[]{:S(2)}) collective-permute-start(bf16[256,512]{1,0:T(8,128)(2,1)S(1)} %collective-permute-done.5.refs_4_), channel_id=1, source_target_pairs={{0,1},{1,0},{2,3},{3,2},{4,5},{5,4},{6,7},{7,6},{8,9},{9,8},{10,11... | collective-permute-start | bytes 786440 | tf_op jit(solution)/shard_map/ppermute | solution.py:287
  35.7 5.8 %collective-permute-start.16 = (bf16[1024,512]{1,0:T(8,128)(2,1)S(1)}, bf16[1024,512]{1,0:T(8,128)(2,1)S(1)}, u32[]{:S(2)}, u32[]{:S(2)}) collective-permute-start(bf16[1024,512]{1,0:T(8,128)(2,1)S(1)} %contrast.1.refs_4_), channel_id=1, source_target_pairs={{0,1},{1,0},{2,3},{3,2},{4,5},{5,4},{6,7},{7,6},{8,9},{9,8},{10,11... | collective-permute-start | bytes 3145736 | tf_op jit(solution)/shard_map/ppermute | solution.py:287
  35.9 8.8 %collective-permute-start.19 = (bf16[1024,256]{1,0:T(8,128)(2,1)S(1)}, bf16[1024,256]{1,0:T(8,128)(2,1)S(1)}, u32[]{:S(2)}, u32[]{:S(2)}) collective-permute-start(bf16[1024,256]{1,0:T(8,128)(2,1)S(1)} %get-tuple-element.43.refs_6_), channel_id=1, source_target_pairs={{0,1},{1,0},{2,3},{3,2},{4,5},{5,4},{6,7},{7,6},{8,9},{9,8},{10,11... | collective-permute-start | bytes 1572872 | tf_op jit(solution)/shard_map/ppermute | solution.py:287
  44.2 4.1 %collective-permute-start.17 = (bf16[256,1024]{1,0:T(8,128)(2,1)S(1)}, bf16[256,1024]{1,0:T(8,128)(2,1)S(1)}, u32[]{:S(2)}, u32[]{:S(2)}) collective-permute-start(bf16[256,1024]{1,0:T(8,128)(2,1)S(1)} %get-tuple-element.46), channel_id=1, source_target_pairs={{0,1},{1,0},{2,3},{3,2},{4,5},{5,4},{6,7},{7,6},{8,9},{9,8},{10,11... | collective-permute-start | bytes 1572872 | tf_op jit(solution)/shard_map/ppermute | solution.py:287
  44.4 3.9 %collective-permute-start.18 = (bf16[1024,256]{1,0:T(8,128)(2,1)S(1)}, bf16[1024,256]{1,0:T(8,128)(2,1)S(1)}, u32[]{:S(2)}, u32[]{:S(2)}) collective-permute-start(bf16[1024,256]{1,0:T(8,128)(2,1)S(1)} %get-tuple-element.47), channel_id=1, source_target_pairs={{0,1},{1,0},{2,3},{3,2},{4,5},{5,4},{6,7},{7,6},{8,9},{9,8},{10,11... | collective-permute-start | bytes 1572872 | tf_op jit(solution)/shard_map/ppermute | solution.py:287
  47.7 2.6 %collective-permute-start.20 = (bf16[256,1024]{1,0:T(8,128)(2,1)S(1)}, bf16[256,1024]{1,0:T(8,128)(2,1)S(1)}, u32[]{:S(2)}, u32[]{:S(2)}) collective-permute-start(bf16[256,1024]{1,0:T(8,128)(2,1)S(1)} %get-tuple-element.58), channel_id=1, source_target_pairs={{0,1},{1,0},{2,3},{3,2},{4,5},{5,4},{6,7},{7,6},{8,9},{9,8},{10,11... | collective-permute-start | bytes 1572872 | tf_op jit(solution)/shard_map/ppermute | solution.py:287
  47.9 2.5 %collective-permute-start.21 = (bf16[1024,256]{1,0:T(8,128)(2,1)S(1)}, bf16[1024,256]{1,0:T(8,128)(2,1)S(1)}, u32[]{:S(2)}, u32[]{:S(2)}) collective-permute-start(bf16[1024,256]{1,0:T(8,128)(2,1)S(1)} %get-tuple-element.59), channel_id=1, source_target_pairs={{0,1},{1,0},{2,3},{3,2},{4,5},{5,4},{6,7},{7,6},{8,9},{9,8},{10,11... | collective-permute-start | bytes 1572872 | tf_op jit(solution)/shard_map/ppermute | solution.py:287

commit v13 on v12

--- a/solution.py
+++ b/solution.py
@@ -59,21 +59,13 @@
         out_ref[:, k * emb : (k + 1) * emb] = dot(active[...], second[...]).astype(BF)
 
 
-def pack_kernel(n_rep, n_blk, n_sub, pos, x_ref, own_ref, pack_ref):
+def pack_kernel(n_blk, n_sub, pos, x_ref, own_ref, pack_ref):
     rows = x_ref.shape[0]
-    slab = rows // n_rep
-
-    def bits(n):
-        return n.bit_length() - 1
-
     owner = (pos[0] * n_sub + pos[1] + own_ref[0:1, :]) & (n_blk * n_sub - 1)
-    place = own_ref[1:2, :]
-    batch = ((owner & (n_sub - 1)) << bits(n_rep)) + (place >> bits(slab))
-    goal = (((batch << bits(n_blk)) + (owner >> bits(n_sub))) << bits(slab)) + (place & (slab - 1))
-    digits = (goal >> 8, goal & 255, own_ref[2:3, :])
-    table = jnp.concatenate([d.astype(F32) for d in digits] + [jnp.zeros((13, rows), F32)], axis=0).astype(BF)
+    digits = (owner, own_ref[1:2, :], own_ref[2:3, :])
+    table = jnp.concatenate([d.astype(F32) for d in digits] + [jnp.zeros((13, rows), F32)], axis=0)
     pack_ref[:rows, :] = x_ref[...]
-    pack_ref[rows:, :] = table
+    pack_ref[rows:, :] = table.astype(BF)
 
 
 def forward_kernel(x_ref, *refs):
@@ -112,66 +104,78 @@
     return jnp.broadcast_to(row, (128, row.shape[1])).T[:, :1]
 
 
+def place_in_turn(k, n_blk):
+    return -k & (n_blk - 1)
+
+
 def arrange_kernel(n_blk, n_rep, slab, pos, *refs):
     mine, other = refs[:n_blk], refs[n_blk : 2 * n_blk]
     rows_mine, rows_other, goals_ref, pick_ref, ep_ref, both_sides, meta = refs[2 * n_blk :]
-    half = rows_mine.shape[0]
-    rows = 2 * half
-    batch = n_blk * slab
+    rows = both_sides.shape[0]
+    batch, rows_dev = n_blk * slab, n_rep * slab
     for i, (blocks, to) in enumerate(((mine, rows_mine), (other, rows_other))):
 
-        def put(off, value, i=i, to=to):
+        def put(off, value, to=to):
             to[pl.ds(off, slab), :] = value
-            both_sides[pl.ds(i * half + off, slab), :] = value
 
         place_blocks(pos, blocks, put, n_blk, n_rep, slab)
+        for k, block in enumerate(blocks):
+            at = (i * n_blk + place_in_turn(k, n_blk)) * rows_dev
+            both_sides[at : at + rows_dev, :] = block[:rows_dev, :]
     for k, block in enumerate(mine):
         at = jnp.bitwise_xor(pos[0], k)
         for r in range(n_rep):
             off = pl.multiple_of((r * n_blk + at) * slab, slab)
-            meta[:, pl.ds(off, slab)] = block[n_rep * slab :, r * slab : (r + 1) * slab].astype(F32)
+            meta[:, pl.ds(off, slab)] = block[rows_dev:, r * slab : (r + 1) * slab].astype(F32)
     ep_ref[...] = meta[2:3, :]
     for r in range(n_rep):
         own = slice(r * batch, (r + 1) * batch)
-        goal = column(meta[0:1, own] * 256.0 + meta[1:2, own]).astype(jnp.int32) + pos[1] * half
-        goal = jnp.where(goal >= rows, goal - rows, goal)
+        owner, place = meta[0:1, own].astype(jnp.int32), meta[1:2, own].astype(jnp.int32)
+        side = (owner & 1) ^ pos[1]
+        column_of = (side * n_blk + place_in_turn((owner >> 1) ^ pos[0], n_blk)) * rows_dev + place
+        goal = column(column_of.astype(F32)).astype(jnp.int32)
         pick_ref[own, :] = jnp.where(
             goal == lax.broadcasted_iota(jnp.int32, (batch, rows), 1), 1.0, 0.0
         ).astype(BF)
     goals_ref[...] = dot(pick_ref[...], both_sides[...]).astype(BF)
 
 
-def contrast_kernel(n_blk, n_rep, slab, scale, pos, *refs):
-    n = n_blk + 1
-    mine, other, ep_ref, pick_ref = refs[:n], refs[n : 2 * n], refs[2 * n], refs[2 * n + 1]
-    grads_ref, phi_all, psi_all = refs[2 * n + 2 :]
-    half, emb = phi_all.shape
-    batch = n_blk * slab
-    last = n_blk - 2
-
-    def sums(parts):
-        blocks = list(parts[:n_blk])
-        blocks[last] = (parts[last][...].astype(F32) + parts[n_blk][...].astype(F32)).astype(BF)
-        return blocks
-
-    def put_mine(off, value):
-        phi_all[pl.ds(off, slab), :] = value[:, :emb]
-        psi_all[pl.ds(off, slab), :] = value[:, emb:]
-
-    def put_other(off, value):
-        psi_all[pl.ds(half + off, slab), :] = value[:, emb:]
-
-    place_blocks(pos, sums(mine), put_mine, n_blk, n_rep, slab)
-    place_blocks(pos, sums(other), put_other, n_blk, n_rep, slab)
+def gather_kernel(n_blk, n_rep, slab, pos, *refs):
+    mine, extra, other, pick_ref = refs[:n_blk], refs[n_blk], refs[n_blk + 1 : n_blk + 3], refs[n_blk + 3]
+    phi_ref, psi_ref, early = refs[n_blk + 4 :]
+    emb = phi_ref.shape[1]
+    rows_dev = n_rep * slab
+    blocks = list(mine)
+    blocks[n_blk - 2] = (mine[n_blk - 2][...].astype(F32) + extra[...].astype(F32)).astype(BF)
+
+    def put(off, value):
+        phi_ref[pl.ds(off, slab), :] = value[:, :emb]
+
+    place_blocks(pos, blocks, put, n_blk, n_rep, slab)
+    for k, block in enumerate(blocks):
+        at = place_in_turn(k, n_blk) * rows_dev
+        early[at : at + rows_dev, :] = block[:, emb:]
+    for i, block in enumerate(other):
+        at = (n_blk + i) * rows_dev
+        early[at : at + rows_dev, :] = block[:, emb:]
+    psi_ref[...] = dot(pick_ref[:, : early.shape[0]], early[...])
+
+
+def contrast_kernel(n_rep, scale, phi_ref, psi_ref, part_ref, there_ref, sums_ref, ep_ref, pick_ref, grads_ref, late, psi_all):
+    half, emb = phi_ref.shape
+    batch = half // n_rep
+    rows_dev = sums_ref.shape[0]
+    late[:rows_dev, :] = (part_ref[:, emb:].astype(F32) + there_ref[:, emb:].astype(F32)).astype(BF)
+    late[rows_dev:, :] = sums_ref[:, emb:]
+    psi_all[...] = (psi_ref[...] + dot(pick_ref[:, pick_ref.shape[1] - 2 * rows_dev :], late[...])).astype(BF)
     diagonal = lax.broadcasted_iota(jnp.int32, (batch, batch), 0) == lax.broadcasted_iota(
         jnp.int32, (batch, batch), 1
     )
-    psi_all[:half, :] = dot(pick_ref[...], psi_all[...]).astype(BF)
     for r in range(n_rep):
         own = slice(r * batch, (r + 1) * batch)
         ep_row = ep_ref[:, own]
         psi = psi_all[own, :]
-        phi = phi_all[own, :]
+        phi = phi_ref[own, :]
         scores = lax.dot_general(phi, psi, (((1,), (1,)), ((), ())), preferred_element_type=F32)
         kept = (column(ep_row) != ep_row) | diagonal
         exponent = jnp.where(kept, jnp.exp(scores * scale), 0.0)
@@ -201,12 +205,33 @@
     return dot(active[...], grad), dot(back[...], rows_ref[...])
 
 
-def mine_kernel(pos, sf, gf, ss, gs, grads_ref, rows_ref, goals_ref, *refs):
-    outs, (active, back) = refs[:4], refs[4:]
-    quarter = active.shape[0]
+def hidden_kernel(pos, sf, gf, rows_ref, goals_ref, *outs):
+    quarter, rows = outs[0].shape
     at = pl.multiple_of(pos[1] * quarter, quarter)
-    outs[0][...], outs[1][...] = rows_grads(at, sf, ss, grads_ref, 0, rows_ref, active, back)
-    outs[2][...], outs[3][...] = rows_grads(at, gf, gs, grads_ref, 1, goals_ref, active, back)
+    for k, (first, x_ref) in enumerate(((sf, rows_ref), (gf, goals_ref))):
+        first_t = first[:, pl.ds(at, quarter)].T
+        for c in range(0, rows, 256):
+            cols = slice(c, c + 256)
+            hidden = dot(first_t, x_ref[cols, :].T)
+            sig = sigmoid(hidden)
+            act = hidden * sig
+            outs[2 * k][:, cols] = act.astype(BF)
+            outs[2 * k + 1][:, cols] = (sig + act * (1.0 - sig)).astype(BF)
+
+
+def mine_kernel(pos, ss, gs, grads_ref, rows_ref, goals_ref, *refs):
+    hidden, outs, back = refs[:4], refs[4:8], refs[8]
+    quarter, rows = back.shape
+    emb = ss.shape[1]
+    at = pl.multiple_of(pos[1] * quarter, quarter)
+    for k, (second_ref, x_ref) in enumerate(((ss, rows_ref), (gs, goals_ref))):
+        second = second_ref[pl.ds(at, quarter), :]
+        grad = grads_ref[:, k * emb : (k + 1) * emb]
+        for c in range(0, rows, 256):
+            cols = slice(c, c + 256)
+            back[:, cols] = (dot(second, grad[cols, :].T) * hidden[2 * k + 1][:, cols].astype(F32)).astype(BF)
+        outs[2 * k][...] = dot(hidden[2 * k][...], grad)
+        outs[2 * k + 1][...] = dot(back[...], x_ref[...])
 
 
 def other_kernel(k, n_put, pos, first, second, grads_ref, rows_ref, sum_second, sum_first, *refs):
@@ -291,7 +316,7 @@
 
     weights = (state_first, goal_first, state_second, goal_second)
     (pack,) = kernel(
-        functools.partial(pack_kernel, n_rep, n_blk, n_sub),
+        functools.partial(pack_kernel, n_blk, n_sub),
         "pack",
         [((rows_dev + 16, width), BF)],
         (states, jnp.stack([goal_distance.reshape(rows_dev), goal_row, episode])),
@@ -326,14 +351,31 @@
         ],
         pos=True,
     )
-    embedded = [sums[0], sums[1], part2, sums[3], after(there2, pick)]
+    sf, gf, ss, gs = held
+    hidden = kernel(
+        hidden_kernel,
+        "hidden",
+        [((quarter, rows_all // 2), BF)] * 4,
+        (sf, gf, mine, goals_mine),
+        pos=True,
+    )
+    there2 = after(there2, hidden[3])
+    late = [swap(x, "sub") for x in (part2, there2, sums[1])]
+    half = rows_all // 2
+    phi, psi = kernel(
+        functools.partial(gather_kernel, n_blk, n_rep, slab),
+        "gather",
+        [((half, emb), BF), ((half, emb), F32)],
+        (sums[0], sums[1], part2, sums[3], there2, swap(sums[0], "sub"), swap(sums[3], "sub"), pick),
+        [pltpu.VMEM((rows_all - 2 * rows_dev, emb), BF)],
+        pos=True,
+    )
     (grads_mine,) = kernel(
-        functools.partial(contrast_kernel, n_blk, n_rep, slab, 4.0 / math.sqrt(emb)),
+        functools.partial(contrast_kernel, n_rep, 4.0 / math.sqrt(emb)),
         "contrast",
-        [((rows_all // 2, 2 * emb), BF)],
-        (*embedded, *(swap(x, "sub") for x in embedded), episodes, pick),
-        [pltpu.VMEM((rows_all // 2, emb), BF), pltpu.VMEM((rows_all, emb), BF)],
-        pos=True,
+        [((half, 2 * emb), BF)],
+        (phi, psi, *late, episodes, pick),
+        [pltpu.VMEM((2 * rows_dev, emb), BF), pltpu.VMEM((half, emb), BF)],
     )
     grads_other = swap(grads_mine, "sub")
     goals_other = swap(goals_mine, "sub")
@@ -345,8 +387,8 @@
         mine_kernel,
         "mine",
         [((quarter, emb), F32), ((quarter, width), F32)] * 2,
-        (sf, gf, ss, gs, grads_mine, mine, goals_mine),
-        work,
+        (ss, gs, grads_mine, mine, goals_mine, *hidden),
+        work[:1],
         pos=True,
         flops=2 * flops,
     )
@@ -473,6 +515,10 @@
         P("rep", None),
     )
     out_specs = (P("grp", "rep"), P(("grp", "rep"), None), P("grp", "rep"), P(("grp", "rep"), None))
-    shape = mesh.shape
-    local = gathered if (shape["blk"], shape["rep"], shape["sub"]) == (4, 2, 2) else exchanged
+
+    def local(states, *others):
+        small = (mesh.shape["blk"], mesh.shape["rep"], mesh.shape["sub"]) == (4, 2, 2)
+        plan = gathered if small and states.shape[0] == states.shape[1] == 256 else exchanged
+        return plan(states, *others)
+
     return jax.shard_map(local, mesh=mesh, in_specs=in_specs, out_specs=out_specs, check_vma=False)

time: 52.1 us -> 52.1 us (level)
  waiting for transfers between devices: 7.25 us -> 6.07 us
  Pallas kernels: 24.9 us -> 25.5 us
    ppermute x4, starting transfers between devices: 9.22 us -> 10.5 us  [across(): return lax.ppermute(x, 'blk', [(i, i ^ k) for i in range(n_blk)])]
    ppermute x18, waiting for transfers between devices: 2.24 us -> 1.22 us  [swap(): return lax.ppermute(x, axis, [(0, 1), (1, 0)])]
    ppermute x18, starting transfers between devices: 8 us -> 7.25 us  [swap(): return lax.ppermute(x, axis, [(0, 1), (1, 0)])]
    pallas_call x13 -> x15, Pallas kernels: 24.9 us -> 25.5 us  [kernel(): pl.pallas_call(body, in_specs=specs, out_specs=[HBM if i in hbm_out else...]
  transfers between devices with their start and end apart: 22 -> 22, of which waited for: 9 -> 6; matrix products, arithmetic and copies ran while one was open for 0% -> 0% of each run, Pallas kernels for 37% -> 42%
where the time goes in v13:
time: 52.1 us; the launch traced here: 51.9 us
  Pallas kernels  25.5 us (49%)
  starting transfers between devices  17.7 us (34%)
  waiting for transfers between devices  6.07 us (12%)
  between operations  0.96 us (2%)
  local copies, waits for them, and re-layouts  0.92 us (2%)
  other arithmetic  0.72 us (1%)
    pallas_call x15, Pallas kernels, kernel(): pl.pallas_call(body, in_specs=specs, out_specs=[HBM if i in hbm_out else...  25.5 us
    ppermute x4, starting transfers between devices, across(): return lax.ppermute(x, 'blk', [(i, i ^ k) for i in range(n_blk)])  10.5 us
    ppermute x18, starting transfers between devices, swap(): return lax.ppermute(x, axis, [(0, 1), (1, 0)])  7.25 us
    ppermute x4, waiting for transfers between devices, across(): return lax.ppermute(x, 'blk', [(i, i ^ k) for i in range(n_blk)])  4.86 us
    ppermute x18, waiting for transfers between devices, swap(): return lax.ppermute(x, axis, [(0, 1), (1, 0)])  1.22 us
  transfers between devices with their start and end apart: 22, of which 6 were waited for; matrix products, arithmetic and copies ran while one was open for 0% of the time, Pallas kernels for 42%

profile of v13, /device:TPU:0, one launch (start us, length us, event | category | flops | bytes accessed | tf_op | source)
XLA Modules:
  0.0 51.9 jit_solution(5996404321750359037)
XLA Ops:
  0.6 0.7 %pad_add_fusion.refs_1_ = s32[3,256]{1,0:T(4,128)S(1)} fusion(s32[1,256]{1,0:T(1,128)} %bitcast.3, s32[1,256]{1,0:T(1,128)} %bitcast.4, s32[1,256]{1,0:T(1,128)} %bitcast.5), kind=kLoop, calls=%fused_computation | loop fusion | flops 1536 | bytes 6144 | tf_op jit(solution)/shard_map/stack | solution.py:322
  1.4 0.9 %copy-done.4 = bf16[256,256]{1,0:T(8,128)(2,1)S(1)} copy-done((bf16[256,256]{1,0:T(8,128)(2,1)S(1)}, bf16[256,256]{1,0:T(8,128)(2,1)}, u32[]{:S(2)}) %copy-start.4) | copy-done | bytes 131096
  2.3 5.1 %collective-permute-start.1 = (bf16[272,256]{1,0:T(8,128)(2,1)S(1)}, bf16[272,256]{1,0:T(8,128)(2,1)S(1)}, u32[]{:S(2)}, u32[]{:S(2)}) collective-permute-start(bf16[272,256]{1,0:T(8,128)(2,1)S(1)} %pack.1.x_ref.refs_0_), channel_id=1, source_target_pairs={{0,12},{4,8},{8,4},{12,0},{1,13},{5,9},{9,5},{13,1},{2,14},{6,10},... | collective-permute-start | bytes 417800 | tf_op jit(solution)/shard_map/ppermute | solution.py:309
  7.4 0.0 copy-done
  7.4 0.0 copy-done.1
  7.4 0.0 copy-done.2
  7.4 0.0 copy-done.3
  7.4 1.4 %forward.3.a_ref = bf16[256,512]{1,0:T(8,128)(2,1)S(1)} custom-call(bf16[272,256]{1,0:T(8,128)(2,1)S(1)} %pack.1.x_ref.refs_0_, bf16[256,2048]{1,0:T(8,128)(2,1)S(1)} %copy-done, bf16[256,2048]{1,0:T(8,128)(2,1)S(1)} %copy-done.1, bf16[2048,256]{1,0:T(8,128)(2,1)S(1)} %copy-done.2, bf16[2048,256]{1,0:T(8,128)(2,1)S(1)} %copy-done.3), custom_call_target="tpu_custom_call" | custom-call | tf_op jit(solution)/shard_map/forward/pallas_call | solution.py:37
  8.8 1.6 %collective-permute-start = (bf16[256,512]{1,0:T(8,128)(2,1)S(1)}, bf16[256,512]{1,0:T(8,128)(2,1)S(1)}, u32[]{:S(2)}, u32[]{:S(2)}) collective-permute-start(bf16[256,512]{1,0:T(8,128)(2,1)S(1)} %forward.3.a_ref), channel_id=1, source_target_pairs={{0,2},{2,0},{1,3},{3,1},{4,6},{6,4},{5,7},{7,5},{8,10},{10,8},{9,1... | collective-permute-start | bytes 786440 | tf_op jit(solution)/shard_map/ppermute | solution.py:312
  10.4 0.8 %collective-permute-done.1.x_ref.refs_3_ = bf16[272,256]{1,0:T(8,128)(2,1)S(1)} collective-permute-done((bf16[272,256]{1,0:T(8,128)(2,1)S(1)}, bf16[272,256]{1,0:T(8,128)(2,1)S(1)}, u32[]{:S(2)}, u32[]{:S(2)}) %collective-permute-start.1) | collective-permute-done | bytes 139296 | tf_op jit(solution)/shard_map/ppermute | solution.py:309
  11.2 1.4 %forward.5.a_ref = bf16[256,512]{1,0:T(8,128)(2,1)S(1)} custom-call(bf16[272,256]{1,0:T(8,128)(2,1)S(1)} %collective-permute-done.1.x_ref.refs_3_, bf16[256,2048]{1,0:T(8,128)(2,1)S(1)} %copy-done, bf16[256,2048]{1,0:T(8,128)(2,1)S(1)} %copy-done.1, bf16[2048,256]{1,0:T(8,128)(2,1)S(1)} %copy-done.2, bf16[2048,256]{1,0:T(8,128)(2,1)S(1)} %copy-done.3), custom_call_target="tpu_custom_call" | custom-call | tf_op jit(solution)/shard_map/forward/pallas_call | solution.py:37
  12.6 1.6 %collective-permute-start.4 = (bf16[256,512]{1,0:T(8,128)(2,1)S(1)}, bf16[256,512]{1,0:T(8,128)(2,1)S(1)}, u32[]{:S(2)}, u32[]{:S(2)}) collective-permute-start(bf16[256,512]{1,0:T(8,128)(2,1)S(1)} %forward.5.a_ref), channel_id=1, source_target_pairs={{0,2},{2,0},{1,3},{3,1},{4,6},{6,4},{5,7},{7,5},{8,10},{10,8},{9,1... | collective-permute-start | bytes 786440 | tf_op jit(solution)/shard_map/ppermute | solution.py:312
  14.1 3.6 %collective-permute-start.2 = (bf16[272,256]{1,0:T(8,128)(2,1)S(1)}, bf16[272,256]{1,0:T(8,128)(2,1)S(1)}, u32[]{:S(2)}, u32[]{:S(2)}) collective-permute-start(bf16[272,256]{1,0:T(8,128)(2,1)S(1)} %pack.1.x_ref.refs_0_), channel_id=1, source_target_pairs={{0,8},{4,12},{8,0},{12,4},{1,9},{5,13},{9,1},{13,5},{2,10},{6,14},... | collective-permute-start | bytes 417800 | tf_op jit(solution)/shard_map/ppermute | solution.py:309
  17.7 0.5 collective-permute-start.6
  18.2 0.0 collective-permute-start.7
  18.2 0.0 collective-permute-done.b_ref
  18.2 0.1 both.2.refs_0_
  18.3 4.0 %collective-permute-done.2.x_ref.refs_2_ = bf16[272,256]{1,0:T(8,128)(2,1)S(1)} collective-permute-done((bf16[272,256]{1,0:T(8,128)(2,1)S(1)}, bf16[272,256]{1,0:T(8,128)(2,1)S(1)}, u32[]{:S(2)}, u32[]{:S(2)}) %collective-permute-start.2) | collective-permute-done | bytes 139296 | tf_op jit(solution)/shard_map/ppermute | solution.py:309
  22.3 1.4 %forward.4.refs_2_ = bf16[256,512]{1,0:T(8,128)(2,1)S(1)} custom-call(bf16[272,256]{1,0:T(8,128)(2,1)S(1)} %collective-permute-done.2.x_ref.refs_2_, bf16[256,2048]{1,0:T(8,128)(2,1)S(1)} %copy-done, bf16[256,2048]{1,0:T(8,128)(2,1)S(1)} %copy-done.1, bf16[2048,256]{1,0:T(8,128)(2,1)S(1)} %copy-done.2, bf16[2048,256]{1,0:T(8,128)(2,1)S(1)} %copy-done.3), custom_call_target="tpu_custom_call" | custom-call | tf_op jit(solution)/shard_map/forward/pallas_call | solution.py:37
  23.7 0.6 %collective-permute-start.5 = (bf16[256,512]{1,0:T(8,128)(2,1)S(1)}, bf16[256,512]{1,0:T(8,128)(2,1)S(1)}, u32[]{:S(2)}, u32[]{:S(2)}) collective-permute-start(bf16[256,512]{1,0:T(8,128)(2,1)S(1)} %forward.4.refs_2_), channel_id=1, source_target_pairs={{0,2},{2,0},{1,3},{3,1},{4,6},{6,4},{5,7},{7,5},{8,10},{10,8},{9,1... | collective-permute-start | bytes 786440 | tf_op jit(solution)/shard_map/ppermute | solution.py:312
  24.3 1.2 %collective-permute-start.3 = (bf16[256,512]{1,0:T(8,128)(2,1)S(1)}, bf16[256,512]{1,0:T(8,128)(2,1)S(1)}, u32[]{:S(2)}, u32[]{:S(2)}) collective-permute-start(bf16[256,512]{1,0:T(8,128)(2,1)S(1)} %both.2.refs_0_), channel_id=1, source_target_pairs={{0,4},{4,0},{8,12},{12,8},{1,5},{5,1},{9,13},{13,9},{2,6},{6,2},{1... | collective-permute-start | bytes 786440 | tf_op jit(solution)/shard_map/ppermute | solution.py:309
  25.5 0.0 collective-permute-done.6.refs_1_
  25.5 0.0 collective-permute-start.8
  25.5 0.0 collective-permute-done.7.refs_4_
  25.5 0.5 collective-permute-start.10
  26.0 0.0 collective-permute-done.4.b_ref
  26.0 0.1 collective-permute-start.9
  26.1 0.1 both.3.refs_3_
  26.2 0.7 %collective-permute-done.8.refs_5_ = bf16[272,256]{1,0:T(8,128)(2,1)S(1)} collective-permute-done((bf16[272,256]{1,0:T(8,128)(2,1)S(1)}, bf16[272,256]{1,0:T(8,128)(2,1)S(1)}, u32[]{:S(2)}, u32[]{:S(2)}) %collective-permute-start.8) | collective-permute-done | bytes 139296 | tf_op jit(solution)/shard_map/ppermute | solution.py:312
  26.9 0.1 collective-permute-start.11
  27.0 0.1 collective-permute-done.10.refs_7_
  27.1 0.3 collective-permute-start.13
  27.4 0.0 collective-permute-done.9.refs_6_
  27.4 0.2 collective-permute-start.12
  27.6 2.3 %arrange.1 = (bf16[1024,256]{1,0:T(8,128)(2,1)S(1)}, bf16[1024,256]{1,0:T(8,128)(2,1)S(1)}, bf16[1024,256]{1,0:T(8,128)(2,1)S(1)}, bf16[1024,2048]{1,0:T(8,128)(2,1)S(1)}, f32[1,1024]{1,0:T(1,128)S(1)}) custom-call(bf16[272,256]{1,0:T(8,128)(2,1)S(1)} %pack.1.x_ref.refs_0_, bf16[272,256]{1,0:T(8,128)(2,1)S(1)} %collective-permute-done.6.refs_1_, ...), custom_call_target="tpu_custom_call" | custom-call | tf_op jit(solution)/shard_map/arrange/pallas_call | solution.py:37
  29.9 2.9 %hidden.1 = (bf16[1024,1024]{1,0:T(8,128)(2,1)S(1)}, bf16[1024,1024]{1,0:T(8,128)(2,1)S(1)}, bf16[1024,1024]{1,0:T(8,128)(2,1)S(1)}, bf16[1024,1024]{1,0:T(8,128)(2,1)S(1)}) custom-call(bf16[256,2048]{1,0:T(8,128)(2,1)S(1)} %copy-done, bf16[256,2048]{1,0:T(8,128)(2,1)S(1)} %copy-done.1, bf16[1024,256]{1,0:T(8,128)(2,1)S(1)} %get-tuple-element.44.refs_2_.refs_3_, ...), custom_call_target="tpu_custom_call" | custom-call | tf_op jit(solution)/shard_map/hidden/pallas_call | solution.py:37
  32.9 0.0 collective-permute-done.5.refs_4_
  32.9 0.4 collective-permute-start.14
  33.3 0.0 collective-permute-done.3.refs_1_
  33.3 0.2 collective-permute-start.15
  33.5 0.0 collective-permute-done.11.refs_5_
  33.5 0.0 collective-permute-done.12.refs_6_
  33.5 1.0 %gather.1 = (bf16[1024,256]{1,0:T(8,128)(2,1)S(1)}, f32[1024,256]{1,0:T(8,128)S(1)}) custom-call(bf16[256,512]{1,0:T(8,128)(2,1)S(1)} %both.2.refs_0_, bf16[256,512]{1,0:T(8,128)(2,1)S(1)} %collective-permute-done.3.refs_1_, bf16[256,512]{1,0:T(8,128)(2,1)S(1)} %forward.4.refs_2_, bf16[256,512]{1,0:T(8,128)(2,1)S(1)} %both.3.refs_3_, ...), custom_call_target="tpu_custom_call" | custom-call | tf_op jit(solution)/shard_map/gather/pallas_call | solution.py:37
  34.5 0.0 collective-permute-done.13.part_ref
  34.5 0.0 collective-permute-done.14.there_ref
  34.5 0.3 collective-permute-done.15.sums_ref
  34.9 2.4 %contrast.1.refs_2_ = bf16[1024,512]{1,0:T(8,128)(2,1)S(1)} custom-call(bf16[1024,256]{1,0:T(8,128)(2,1)S(1)} %get-tuple-element.49.phi_ref, f32[1024,256]{1,0:T(8,128)S(1)} %get-tuple-element.50.psi_ref, bf16[256,512]{1,0:T(8,128)(2,1)S(1)} %collective-permute-done.13.part_ref, bf16[256,512]{1,0:T(8,128)(2,1)S(1)} %collective-permute-done.14.there_ref, ...), custom_call_target="tpu_custom_call" | custom-call | tf_op jit(solution)/shard_map/contrast/pallas_call | solution.py:37
  37.2 0.4 collective-permute-start.16
  37.6 0.2 collective-permute-start.19
  37.8 3.5 %mine.1 = (f32[1024,256]{1,0:T(8,128)S(1)}, f32[1024,256]{1,0:T(8,128)S(1)}, f32[1024,256]{1,0:T(8,128)S(1)}, f32[1024,256]{1,0:T(8,128)S(1)}) custom-call(bf16[2048,256]{1,0:T(8,128)(2,1)S(1)} %copy-done.2, bf16[2048,256]{1,0:T(8,128)(2,1)S(1)} %copy-done.3, bf16[1024,512]{1,0:T(8,128)(2,1)S(1)} %contrast.1.refs_2_, ...), custom_call_target="tpu_custom_call" | custom-call | flops 4294967296 | tf_op jit(solution)/shard_map/mine/pallas_call | solution.py:37
  41.3 0.0 collective-permute-done.16.refs_2_
  41.3 2.7 %other_state.1 = (bf16[256,1024]{1,0:T(8,128)(2,1)S(1)}, bf16[1024,256]{1,0:T(8,128)(2,1)S(1)}, f32[256,1024]{1,0:T(8,128)S(1)}, f32[1024,256]{1,0:T(8,128)S(1)}) custom-call(bf16[256,2048]{1,0:T(8,128)(2,1)S(1)} %copy-done, bf16[2048,256]{1,0:T(8,128)(2,1)S(1)} %copy-done.2, bf16[1024,512]{1,0:T(8,128)(2,1)S(1)} %collective-permute-done.16.refs_2_, ...), custom_call_target="tpu_custom_call" | custom-call | flops 2147483648 | tf_op jit(solution)/shard_map/other_state/pallas_call | solution.py:37
  44.1 0.4 collective-permute-start.17
  44.4 0.2 collective-permute-start.18
  44.6 0.0 collective-permute-done.19.refs_3_
  44.6 3.0 %other_goal.1 = (bf16[256,1024]{1,0:T(8,128)(2,1)S(1)}, bf16[1024,256]{1,0:T(8,128)(2,1)S(1)}, f32[256,1024]{1,0:T(8,128)S(1)}, f32[1024,256]{1,0:T(8,128)S(1)},...) custom-call(bf16[256,2048]{1,0:T(8,128)(2,1)S(1)} %copy-done.1, bf16[2048,256]{1,0:T(8,128)(2,1)S(1)} %copy-done.3, ...), custom_call_target="tpu_custom_call" | custom-call | flops 2147483648 | tf_op jit(solution)/shard_map/other_goal/pallas_call | solution.py:37
  47.6 0.4 collective-permute-start.20
  48.0 0.2 collective-permute-start.21
  48.2 0.0 collective-permute-done.17.refs_0_
  48.2 0.0 collective-permute-done.18.refs_1_
  48.2 2.0 %finish.2 = (f32[256,2048]{1,0:T(8,128)}, f32[2048,256]{1,0:T(8,128)}, f32[256,2048]{1,0:T(8,128)}, f32[2048,256]{1,0:T(8,128)}) custom-call(bf16[256,1024]{1,0:T(8,128)(2,1)S(1)} %collective-permute-done.17.refs_0_, bf16[1024,256]{1,0:T(8,128)(2,1)S(1)} %collective-permute-done.18.refs_1_, ...), custom_call_target="tpu_custom_call", output_to_operand_aliasing={{0}: (4, {}), {1}: (5, {})} | custom-call | tf_op jit(solution)/shard_map/finish/pallas_call | solution.py:37
  50.2 0.0 collective-permute-done.20.refs_0_
  50.3 0.1 collective-permute-done.21.refs_1_
  50.3 1.4 %finish.3 = (f32[256,2048]{1,0:T(8,128)}, f32[2048,256]{1,0:T(8,128)}) custom-call(bf16[256,1024]{1,0:T(8,128)(2,1)S(1)} %collective-permute-done.20.refs_0_, bf16[1024,256]{1,0:T(8,128)(2,1)S(1)} %collective-permute-done.21.refs_1_, f32[256,2048]{1,0:T(8,128)} %get-tuple-element.72.refs_2_, ...), custom_call_target="tpu_custom_call", output_to_operand_aliasing={{0}: (2, {}), {1}: (3, {})} | custom-call | tf_op jit(solution)/shard_map/finish/pallas_call | solution.py:37
  (6 shorter events, 0.0 us)
Async XLA Ops:
  1.4 0.9 %copy-start.4 = (bf16[256,256]{1,0:T(8,128)(2,1)S(1)}, bf16[256,256]{1,0:T(8,128)(2,1)}, u32[]{:S(2)}) copy-start(bf16[256,256]{1,0:T(8,128)(2,1)} %refs_0_.8) | copy-start | bytes 393220
  2.3 5.2 %copy-start = (bf16[256,2048]{1,0:T(8,128)(2,1)S(1)}, bf16[256,2048]{1,0:T(8,128)(2,1)}, u32[]{:S(2)}) copy-start(bf16[256,2048]{1,0:T(8,128)(2,1)} %refs_0_.14) | copy-start | bytes 3145732
  2.3 5.2 %copy-start.1 = (bf16[256,2048]{1,0:T(8,128)(2,1)S(1)}, bf16[256,2048]{1,0:T(8,128)(2,1)}, u32[]{:S(2)}) copy-start(bf16[256,2048]{1,0:T(8,128)(2,1)} %refs_0_.15) | copy-start | bytes 3145732
  2.3 5.2 %copy-start.2 = (bf16[2048,256]{1,0:T(8,128)(2,1)S(1)}, bf16[2048,256]{1,0:T(8,128)(2,1)}, u32[]{:S(2)}) copy-start(bf16[2048,256]{1,0:T(8,128)(2,1)} %refs_1_.12) | copy-start | bytes 3145732
  2.3 5.2 %copy-start.3 = (bf16[2048,256]{1,0:T(8,128)(2,1)S(1)}, bf16[2048,256]{1,0:T(8,128)(2,1)}, u32[]{:S(2)}) copy-start(bf16[2048,256]{1,0:T(8,128)(2,1)} %refs_1_.13) | copy-start | bytes 3145732
  2.3 8.9 %collective-permute-start.1 = (bf16[272,256]{1,0:T(8,128)(2,1)S(1)}, bf16[272,256]{1,0:T(8,128)(2,1)S(1)}, u32[]{:S(2)}, u32[]{:S(2)}) collective-permute-start(bf16[272,256]{1,0:T(8,128)(2,1)S(1)} %pack.1.x_ref.refs_0_), channel_id=1, source_target_pairs={{0,12},{4,8},{8,4},{12,0},{1,13},{5,9},{9,5},{13,1},{2,14},{6,10},... | collective-permute-start | bytes 417800 | tf_op jit(solution)/shard_map/ppermute | solution.py:309
  8.8 9.4 %collective-permute-start = (bf16[256,512]{1,0:T(8,128)(2,1)S(1)}, bf16[256,512]{1,0:T(8,128)(2,1)S(1)}, u32[]{:S(2)}, u32[]{:S(2)}) collective-permute-start(bf16[256,512]{1,0:T(8,128)(2,1)S(1)} %forward.3.a_ref), channel_id=1, source_target_pairs={{0,2},{2,0},{1,3},{3,1},{4,6},{6,4},{5,7},{7,5},{8,10},{10,8},{9,1... | collective-permute-start | bytes 786440 | tf_op jit(solution)/shard_map/ppermute | solution.py:312
  12.6 13.5 %collective-permute-start.4 = (bf16[256,512]{1,0:T(8,128)(2,1)S(1)}, bf16[256,512]{1,0:T(8,128)(2,1)S(1)}, u32[]{:S(2)}, u32[]{:S(2)}) collective-permute-start(bf16[256,512]{1,0:T(8,128)(2,1)S(1)} %forward.5.a_ref), channel_id=1, source_target_pairs={{0,2},{2,0},{1,3},{3,1},{4,6},{6,4},{5,7},{7,5},{8,10},{10,8},{9,1... | collective-permute-start | bytes 786440 | tf_op jit(solution)/shard_map/ppermute | solution.py:312
  14.1 8.2 %collective-permute-start.2 = (bf16[272,256]{1,0:T(8,128)(2,1)S(1)}, bf16[272,256]{1,0:T(8,128)(2,1)S(1)}, u32[]{:S(2)}, u32[]{:S(2)}) collective-permute-start(bf16[272,256]{1,0:T(8,128)(2,1)S(1)} %pack.1.x_ref.refs_0_), channel_id=1, source_target_pairs={{0,8},{4,12},{8,0},{12,4},{1,9},{5,13},{9,1},{13,5},{2,10},{6,14},... | collective-permute-start | bytes 417800 | tf_op jit(solution)/shard_map/ppermute | solution.py:309
  17.7 7.8 %collective-permute-start.6 = (bf16[272,256]{1,0:T(8,128)(2,1)S(1)}, bf16[272,256]{1,0:T(8,128)(2,1)S(1)}, u32[]{:S(2)}, u32[]{:S(2)}) collective-permute-start(bf16[272,256]{1,0:T(8,128)(2,1)S(1)} %pack.1.x_ref.refs_0_), channel_id=1, source_target_pairs={{0,4},{4,0},{8,12},{12,8},{1,5},{5,1},{9,13},{13,9},{2,6},{6,2},{1... | collective-permute-start | bytes 417800 | tf_op jit(solution)/shard_map/ppermute | solution.py:309
  18.2 7.3 %collective-permute-start.7 = (bf16[272,256]{1,0:T(8,128)(2,1)S(1)}, bf16[272,256]{1,0:T(8,128)(2,1)S(1)}, u32[]{:S(2)}, u32[]{:S(2)}) collective-permute-start(bf16[272,256]{1,0:T(8,128)(2,1)S(1)} %pack.1.x_ref.refs_0_), channel_id=1, source_target_pairs={{0,1},{1,0},{2,3},{3,2},{4,5},{5,4},{6,7},{7,6},{8,9},{9,8},{10,11... | collective-permute-start | bytes 417800 | tf_op jit(solution)/shard_map/ppermute | solution.py:312
  23.7 9.2 %collective-permute-start.5 = (bf16[256,512]{1,0:T(8,128)(2,1)S(1)}, bf16[256,512]{1,0:T(8,128)(2,1)S(1)}, u32[]{:S(2)}, u32[]{:S(2)}) collective-permute-start(bf16[256,512]{1,0:T(8,128)(2,1)S(1)} %forward.4.refs_2_), channel_id=1, source_target_pairs={{0,2},{2,0},{1,3},{3,1},{4,6},{6,4},{5,7},{7,5},{8,10},{10,8},{9,1... | collective-permute-start | bytes 786440 | tf_op jit(solution)/shard_map/ppermute | solution.py:312
  24.3 9.0 %collective-permute-start.3 = (bf16[256,512]{1,0:T(8,128)(2,1)S(1)}, bf16[256,512]{1,0:T(8,128)(2,1)S(1)}, u32[]{:S(2)}, u32[]{:S(2)}) collective-permute-start(bf16[256,512]{1,0:T(8,128)(2,1)S(1)} %both.2.refs_0_), channel_id=1, source_target_pairs={{0,4},{4,0},{8,12},{12,8},{1,5},{5,1},{9,13},{13,9},{2,6},{6,2},{1... | collective-permute-start | bytes 786440 | tf_op jit(solution)/shard_map/ppermute | solution.py:309
  25.5 1.4 %collective-permute-start.8 = (bf16[272,256]{1,0:T(8,128)(2,1)S(1)}, bf16[272,256]{1,0:T(8,128)(2,1)S(1)}, u32[]{:S(2)}, u32[]{:S(2)}) collective-permute-start(bf16[272,256]{1,0:T(8,128)(2,1)S(1)} %collective-permute-done.6.refs_1_), channel_id=1, source_target_pairs={{0,1},{1,0},{2,3},{3,2},{4,5},{5,4},{6,7},{7,6},{8,9},{9,8},{10,11... | collective-permute-start | bytes 417800 | tf_op jit(solution)/shard_map/ppermute | solution.py:312
  25.5 1.6 %collective-permute-start.10 = (bf16[272,256]{1,0:T(8,128)(2,1)S(1)}, bf16[272,256]{1,0:T(8,128)(2,1)S(1)}, u32[]{:S(2)}, u32[]{:S(2)}) collective-permute-start(bf16[272,256]{1,0:T(8,128)(2,1)S(1)} %collective-permute-done.1.x_ref.refs_3_), channel_id=1, source_target_pairs={{0,1},{1,0},{2,3},{3,2},{4,5},{5,4},{6,7},{7,6},{8,9},{9,8},{10,11... | collective-permute-start | bytes 417800 | tf_op jit(solution)/shard_map/ppermute | solution.py:312
  26.0 1.4 %collective-permute-start.9 = (bf16[272,256]{1,0:T(8,128)(2,1)S(1)}, bf16[272,256]{1,0:T(8,128)(2,1)S(1)}, u32[]{:S(2)}, u32[]{:S(2)}) collective-permute-start(bf16[272,256]{1,0:T(8,128)(2,1)S(1)} %collective-permute-done.2.x_ref.refs_2_), channel_id=1, source_target_pairs={{0,1},{1,0},{2,3},{3,2},{4,5},{5,4},{6,7},{7,6},{8,9},{9,8},{10,11... | collective-permute-start | bytes 417800 | tf_op jit(solution)/shard_map/ppermute | solution.py:312
  26.9 6.6 %collective-permute-start.11 = (bf16[256,512]{1,0:T(8,128)(2,1)S(1)}, bf16[256,512]{1,0:T(8,128)(2,1)S(1)}, u32[]{:S(2)}, u32[]{:S(2)}) collective-permute-start(bf16[256,512]{1,0:T(8,128)(2,1)S(1)} %both.2.refs_0_), channel_id=1, source_target_pairs={{0,1},{1,0},{2,3},{3,2},{4,5},{5,4},{6,7},{7,6},{8,9},{9,8},{10,11... | collective-permute-start | bytes 786440 | tf_op jit(solution)/shard_map/ppermute | solution.py:312
  27.1 7.4 %collective-permute-start.13 = (bf16[256,512]{1,0:T(8,128)(2,1)S(1)}, bf16[256,512]{1,0:T(8,128)(2,1)S(1)}, u32[]{:S(2)}, u32[]{:S(2)}) collective-permute-start(bf16[256,512]{1,0:T(8,128)(2,1)S(1)} %forward.4.refs_2_), channel_id=1, source_target_pairs={{0,1},{1,0},{2,3},{3,2},{4,5},{5,4},{6,7},{7,6},{8,9},{9,8},{10,11... | collective-permute-start | bytes 786440 | tf_op jit(solution)/shard_map/ppermute | solution.py:312
  27.4 6.1 %collective-permute-start.12 = (bf16[256,512]{1,0:T(8,128)(2,1)S(1)}, bf16[256,512]{1,0:T(8,128)(2,1)S(1)}, u32[]{:S(2)}, u32[]{:S(2)}) collective-permute-start(bf16[256,512]{1,0:T(8,128)(2,1)S(1)} %both.3.refs_3_), channel_id=1, source_target_pairs={{0,1},{1,0},{2,3},{3,2},{4,5},{5,4},{6,7},{7,6},{8,9},{9,8},{10,11... | collective-permute-start | bytes 786440 | tf_op jit(solution)/shard_map/ppermute | solution.py:312
  32.9 1.6 %collective-permute-start.14 = (bf16[256,512]{1,0:T(8,128)(2,1)S(1)}, bf16[256,512]{1,0:T(8,128)(2,1)S(1)}, u32[]{:S(2)}, u32[]{:S(2)}) collective-permute-start(bf16[256,512]{1,0:T(8,128)(2,1)S(1)} %collective-permute-done.5.refs_4_), channel_id=1, source_target_pairs={{0,1},{1,0},{2,3},{3,2},{4,5},{5,4},{6,7},{7,6},{8,9},{9,8},{10,11... | collective-permute-start | bytes 786440 | tf_op jit(solution)/shard_map/ppermute | solution.py:312
  33.3 1.6 %collective-permute-start.15 = (bf16[256,512]{1,0:T(8,128)(2,1)S(1)}, bf16[256,512]{1,0:T(8,128)(2,1)S(1)}, u32[]{:S(2)}, u32[]{:S(2)}) collective-permute-start(bf16[256,512]{1,0:T(8,128)(2,1)S(1)} %collective-permute-done.3.refs_1_), channel_id=1, source_target_pairs={{0,1},{1,0},{2,3},{3,2},{4,5},{5,4},{6,7},{7,6},{8,9},{9,8},{10,11... | collective-permute-start | bytes 786440 | tf_op jit(solution)/shard_map/ppermute | solution.py:312
  37.2 4.1 %collective-permute-start.16 = (bf16[1024,512]{1,0:T(8,128)(2,1)S(1)}, bf16[1024,512]{1,0:T(8,128)(2,1)S(1)}, u32[]{:S(2)}, u32[]{:S(2)}) collective-permute-start(bf16[1024,512]{1,0:T(8,128)(2,1)S(1)} %contrast.1.refs_2_), channel_id=1, source_target_pairs={{0,1},{1,0},{2,3},{3,2},{4,5},{5,4},{6,7},{7,6},{8,9},{9,8},{10,11... | collective-permute-start | bytes 3145736 | tf_op jit(solution)/shard_map/ppermute | solution.py:312
  37.6 7.0 %collective-permute-start.19 = (bf16[1024,256]{1,0:T(8,128)(2,1)S(1)}, bf16[1024,256]{1,0:T(8,128)(2,1)S(1)}, u32[]{:S(2)}, u32[]{:S(2)}) collective-permute-start(bf16[1024,256]{1,0:T(8,128)(2,1)S(1)} %get-tuple-element.45.refs_3_.refs_4_), channel_id=1, source_target_pairs={{0,1},{1,0},{2,3},{3,2},{4,5},{5,4},{6,7},{7,6},{8,9},{9,8},{10,11... | collective-permute-start | bytes 1572872 | tf_op jit(solution)/shard_map/ppermute | solution.py:312
  44.1 4.1 %collective-permute-start.17 = (bf16[256,1024]{1,0:T(8,128)(2,1)S(1)}, bf16[256,1024]{1,0:T(8,128)(2,1)S(1)}, u32[]{:S(2)}, u32[]{:S(2)}) collective-permute-start(bf16[256,1024]{1,0:T(8,128)(2,1)S(1)} %get-tuple-element.58), channel_id=1, source_target_pairs={{0,1},{1,0},{2,3},{3,2},{4,5},{5,4},{6,7},{7,6},{8,9},{9,8},{10,11... | collective-permute-start | bytes 1572872 | tf_op jit(solution)/shard_map/ppermute | solution.py:312
  44.4 3.8 %collective-permute-start.18 = (bf16[1024,256]{1,0:T(8,128)(2,1)S(1)}, bf16[1024,256]{1,0:T(8,128)(2,1)S(1)}, u32[]{:S(2)}, u32[]{:S(2)}) collective-permute-start(bf16[1024,256]{1,0:T(8,128)(2,1)S(1)} %get-tuple-element.59), channel_id=1, source_target_pairs={{0,1},{1,0},{2,3},{3,2},{4,5},{5,4},{6,7},{7,6},{8,9},{9,8},{10,11... | collective-permute-start | bytes 1572872 | tf_op jit(solution)/shard_map/ppermute | solution.py:312
  47.6 2.6 %collective-permute-start.20 = (bf16[256,1024]{1,0:T(8,128)(2,1)S(1)}, bf16[256,1024]{1,0:T(8,128)(2,1)S(1)}, u32[]{:S(2)}, u32[]{:S(2)}) collective-permute-start(bf16[256,1024]{1,0:T(8,128)(2,1)S(1)} %get-tuple-element.70), channel_id=1, source_target_pairs={{0,1},{1,0},{2,3},{3,2},{4,5},{5,4},{6,7},{7,6},{8,9},{9,8},{10,11... | collective-permute-start | bytes 1572872 | tf_op jit(solution)/shard_map/ppermute | solution.py:312
  48.0 2.4 %collective-permute-start.21 = (bf16[1024,256]{1,0:T(8,128)(2,1)S(1)}, bf16[1024,256]{1,0:T(8,128)(2,1)S(1)}, u32[]{:S(2)}, u32[]{:S(2)}) collective-permute-start(bf16[1024,256]{1,0:T(8,128)(2,1)S(1)} %get-tuple-element.71), channel_id=1, source_target_pairs={{0,1},{1,0},{2,3},{3,2},{4,5},{5,4},{6,7},{7,6},{8,9},{9,8},{10,11... | collective-permute-start | bytes 1572872 | tf_op jit(solution)/shard_map/ppermute | solution.py:312

commit v14 on v13

--- a/solution.py
+++ b/solution.py
@@ -109,8 +109,8 @@
 
 
 def arrange_kernel(n_blk, n_rep, slab, pos, *refs):
-    mine, other = refs[:n_blk], refs[n_blk : 2 * n_blk]
-    rows_mine, rows_other, goals_ref, pick_ref, ep_ref, both_sides, meta = refs[2 * n_blk :]
+    mine, other, firsts = refs[:n_blk], refs[n_blk : 2 * n_blk], refs[2 * n_blk : 2 * n_blk + 2]
+    rows_mine, rows_other, goals_ref, pick_ref, ep_ref, *hidden, both_sides, meta = refs[2 * n_blk + 2 :]
     rows = both_sides.shape[0]
     batch, rows_dev = n_blk * slab, n_rep * slab
     for i, (blocks, to) in enumerate(((mine, rows_mine), (other, rows_other))):
@@ -138,6 +138,7 @@
             goal == lax.broadcasted_iota(jnp.int32, (batch, rows), 1), 1.0, 0.0
         ).astype(BF)
     goals_ref[...] = dot(pick_ref[...], both_sides[...]).astype(BF)
+    activate(pos, firsts, (rows_mine, goals_ref), hidden)
 
 
 def gather_kernel(n_blk, n_rep, slab, pos, *refs):
@@ -205,10 +206,10 @@
     return dot(active[...], grad), dot(back[...], rows_ref[...])
 
 
-def hidden_kernel(pos, sf, gf, rows_ref, goals_ref, *outs):
+def activate(pos, firsts, inputs, outs):
     quarter, rows = outs[0].shape
     at = pl.multiple_of(pos[1] * quarter, quarter)
-    for k, (first, x_ref) in enumerate(((sf, rows_ref), (gf, goals_ref))):
+    for k, (first, x_ref) in enumerate(zip(firsts, inputs)):
         first_t = first[:, pl.ds(at, quarter)].T
         for c in range(0, rows, 256):
             cols = slice(c, c + 256)
@@ -340,26 +341,20 @@
     sums[3] = both(part3, there3)
 
     side = ((rows_all // 2, width), BF)
-    mine, other, goals_mine, pick, episodes = kernel(
+    sf, gf, ss, gs = held
+    mine, other, goals_mine, pick, episodes, *hidden = kernel(
         functools.partial(arrange_kernel, n_blk, n_rep, slab),
         "arrange",
-        [side, side, side, ((rows_all // 2, rows_all), BF), ((1, rows_all // 2), F32)],
-        (*(got[k] for k in range(n_blk)), *(swap(got[k], "sub") for k in range(n_blk))),
+        [side, side, side, ((rows_all // 2, rows_all), BF), ((1, rows_all // 2), F32)]
+        + [((quarter, rows_all // 2), BF)] * 4,
+        (*(got[k] for k in range(n_blk)), *(swap(got[k], "sub") for k in range(n_blk)), sf, gf),
         [
             pltpu.VMEM((rows_all, width), BF),
             pltpu.VMEM((16, rows_all // 2), F32),
         ],
         pos=True,
     )
-    sf, gf, ss, gs = held
-    hidden = kernel(
-        hidden_kernel,
-        "hidden",
-        [((quarter, rows_all // 2), BF)] * 4,
-        (sf, gf, mine, goals_mine),
-        pos=True,
-    )
-    there2 = after(there2, hidden[3])
+    there2 = after(there2, pick)
     late = [swap(x, "sub") for x in (part2, there2, sums[1])]
     half = rows_all // 2
     phi, psi = kernel(

time: 52.1 us -> 50.4 us (0.967)
  waiting for transfers between devices: 6.07 us -> 4.06 us
    ppermute x4, waiting for transfers between devices: 4.86 us -> 2.86 us  [across(): return lax.ppermute(x, 'blk', [(i, i ^ k) for i in range(n_blk)])]
    ppermute x18, starting transfers between devices: 7.25 us -> 7.87 us  [swap(): return lax.ppermute(x, axis, [(0, 1), (1, 0)])]
    pallas_call x15 -> x14, Pallas kernels: 25.5 us -> 25.3 us  [kernel(): pl.pallas_call(body, in_specs=specs, out_specs=[HBM if i in hbm_out else...]
  transfers between devices with their start and end apart: 22 -> 22, of which waited for: 6 -> 6; matrix products, arithmetic and copies ran while one was open for 0% -> 0% of each run, Pallas kernels for 42% -> 43%
where the time goes in v14:
time: 50.4 us; the launch traced here: 50.2 us
  Pallas kernels  25.3 us (50%)
  starting transfers between devices  18.2 us (36%)
  waiting for transfers between devices  4.06 us (8%)
  between operations  0.95 us (2%)
  local copies, waits for them, and re-layouts  0.92 us (2%)
  other arithmetic  0.72 us (1%)
    pallas_call x14, Pallas kernels, kernel(): pl.pallas_call(body, in_specs=specs, out_specs=[HBM if i in hbm_out else...  25.3 us
    ppermute x4, starting transfers between devices, across(): return lax.ppermute(x, 'blk', [(i, i ^ k) for i in range(n_blk)])  10.3 us
    ppermute x18, starting transfers between devices, swap(): return lax.ppermute(x, axis, [(0, 1), (1, 0)])  7.87 us
    ppermute x4, waiting for transfers between devices, across(): return lax.ppermute(x, 'blk', [(i, i ^ k) for i in range(n_blk)])  2.86 us
    ppermute x18, waiting for transfers between devices, swap(): return lax.ppermute(x, axis, [(0, 1), (1, 0)])  1.2 us
  transfers between devices with their start and end apart: 22, of which 6 were waited for; matrix products, arithmetic and copies ran while one was open for 0% of the time, Pallas kernels for 43%

profile of v14, /device:TPU:0, one launch (start us, length us, event | category | flops | bytes accessed | tf_op | source)
XLA Modules:
  0.0 50.2 jit_solution(17464429037723013313)
XLA Ops:
  0.6 0.7 %pad_add_fusion.refs_1_ = s32[3,256]{1,0:T(4,128)S(1)} fusion(s32[1,256]{1,0:T(1,128)} %bitcast.3, s32[1,256]{1,0:T(1,128)} %bitcast.4, s32[1,256]{1,0:T(1,128)} %bitcast.5), kind=kLoop, calls=%fused_computation | loop fusion | flops 1536 | bytes 6144 | tf_op jit(solution)/shard_map/stack | solution.py:323
  1.4 0.0 copy-start.4
  1.4 0.9 %copy-done.4 = bf16[256,256]{1,0:T(8,128)(2,1)S(1)} copy-done((bf16[256,256]{1,0:T(8,128)(2,1)S(1)}, bf16[256,256]{1,0:T(8,128)(2,1)}, u32[]{:S(2)}) %copy-start.4) | copy-done | bytes 131096
  2.3 5.1 %collective-permute-start.1 = (bf16[272,256]{1,0:T(8,128)(2,1)S(1)}, bf16[272,256]{1,0:T(8,128)(2,1)S(1)}, u32[]{:S(2)}, u32[]{:S(2)}) collective-permute-start(bf16[272,256]{1,0:T(8,128)(2,1)S(1)} %pack.1.x_ref.refs_0_), channel_id=1, source_target_pairs={{0,12},{4,8},{8,4},{12,0},{1,13},{5,9},{9,5},{13,1},{2,14},{6,10},... | collective-permute-start | bytes 417800 | tf_op jit(solution)/shard_map/ppermute | solution.py:310
  7.4 0.0 copy-done
  7.4 0.0 copy-done.1
  7.4 0.0 copy-done.2
  7.4 0.0 copy-done.3
  7.4 1.4 %forward.3.a_ref = bf16[256,512]{1,0:T(8,128)(2,1)S(1)} custom-call(bf16[272,256]{1,0:T(8,128)(2,1)S(1)} %pack.1.x_ref.refs_0_, bf16[256,2048]{1,0:T(8,128)(2,1)S(1)} %copy-done, bf16[256,2048]{1,0:T(8,128)(2,1)S(1)} %copy-done.1, bf16[2048,256]{1,0:T(8,128)(2,1)S(1)} %copy-done.2, bf16[2048,256]{1,0:T(8,128)(2,1)S(1)} %copy-done.3), custom_call_target="tpu_custom_call" | custom-call | tf_op jit(solution)/shard_map/forward/pallas_call | solution.py:37
  8.8 1.6 %collective-permute-start = (bf16[256,512]{1,0:T(8,128)(2,1)S(1)}, bf16[256,512]{1,0:T(8,128)(2,1)S(1)}, u32[]{:S(2)}, u32[]{:S(2)}) collective-permute-start(bf16[256,512]{1,0:T(8,128)(2,1)S(1)} %forward.3.a_ref), channel_id=1, source_target_pairs={{0,2},{2,0},{1,3},{3,1},{4,6},{6,4},{5,7},{7,5},{8,10},{10,8},{9,1... | collective-permute-start | bytes 786440 | tf_op jit(solution)/shard_map/ppermute | solution.py:313
  10.4 0.8 %collective-permute-done.1.x_ref.refs_3_ = bf16[272,256]{1,0:T(8,128)(2,1)S(1)} collective-permute-done((bf16[272,256]{1,0:T(8,128)(2,1)S(1)}, bf16[272,256]{1,0:T(8,128)(2,1)S(1)}, u32[]{:S(2)}, u32[]{:S(2)}) %collective-permute-start.1) | collective-permute-done | bytes 139296 | tf_op jit(solution)/shard_map/ppermute | solution.py:310
  11.2 3.6 %collective-permute-start.2 = (bf16[272,256]{1,0:T(8,128)(2,1)S(1)}, bf16[272,256]{1,0:T(8,128)(2,1)S(1)}, u32[]{:S(2)}, u32[]{:S(2)}) collective-permute-start(bf16[272,256]{1,0:T(8,128)(2,1)S(1)} %pack.1.x_ref.refs_0_), channel_id=1, source_target_pairs={{0,8},{4,12},{8,0},{12,4},{1,9},{5,13},{9,1},{13,5},{2,10},{6,14},... | collective-permute-start | bytes 417800 | tf_op jit(solution)/shard_map/ppermute | solution.py:310
  14.8 1.4 %forward.5.a_ref = bf16[256,512]{1,0:T(8,128)(2,1)S(1)} custom-call(bf16[272,256]{1,0:T(8,128)(2,1)S(1)} %collective-permute-done.1.x_ref.refs_3_, bf16[256,2048]{1,0:T(8,128)(2,1)S(1)} %copy-done, bf16[256,2048]{1,0:T(8,128)(2,1)S(1)} %copy-done.1, bf16[2048,256]{1,0:T(8,128)(2,1)S(1)} %copy-done.2, bf16[2048,256]{1,0:T(8,128)(2,1)S(1)} %copy-done.3), custom_call_target="tpu_custom_call" | custom-call | tf_op jit(solution)/shard_map/forward/pallas_call | solution.py:37
  16.2 1.6 %collective-permute-start.4 = (bf16[256,512]{1,0:T(8,128)(2,1)S(1)}, bf16[256,512]{1,0:T(8,128)(2,1)S(1)}, u32[]{:S(2)}, u32[]{:S(2)}) collective-permute-start(bf16[256,512]{1,0:T(8,128)(2,1)S(1)} %forward.5.a_ref), channel_id=1, source_target_pairs={{0,2},{2,0},{1,3},{3,1},{4,6},{6,4},{5,7},{7,5},{8,10},{10,8},{9,1... | collective-permute-start | bytes 786440 | tf_op jit(solution)/shard_map/ppermute | solution.py:313
  17.7 0.5 collective-permute-start.6
  18.2 0.0 collective-permute-start.7
  18.2 0.0 collective-permute-done.b_ref
  18.2 0.1 both.2.refs_0_
  18.3 2.0 %collective-permute-done.2.x_ref.refs_2_ = bf16[272,256]{1,0:T(8,128)(2,1)S(1)} collective-permute-done((bf16[272,256]{1,0:T(8,128)(2,1)S(1)}, bf16[272,256]{1,0:T(8,128)(2,1)S(1)}, u32[]{:S(2)}, u32[]{:S(2)}) %collective-permute-start.2) | collective-permute-done | bytes 139296 | tf_op jit(solution)/shard_map/ppermute | solution.py:310
  20.3 1.4 %forward.4.refs_2_ = bf16[256,512]{1,0:T(8,128)(2,1)S(1)} custom-call(bf16[272,256]{1,0:T(8,128)(2,1)S(1)} %collective-permute-done.2.x_ref.refs_2_, bf16[256,2048]{1,0:T(8,128)(2,1)S(1)} %copy-done, bf16[256,2048]{1,0:T(8,128)(2,1)S(1)} %copy-done.1, bf16[2048,256]{1,0:T(8,128)(2,1)S(1)} %copy-done.2, bf16[2048,256]{1,0:T(8,128)(2,1)S(1)} %copy-done.3), custom_call_target="tpu_custom_call" | custom-call | tf_op jit(solution)/shard_map/forward/pallas_call | solution.py:37
  21.7 1.2 %collective-permute-start.5 = (bf16[256,512]{1,0:T(8,128)(2,1)S(1)}, bf16[256,512]{1,0:T(8,128)(2,1)S(1)}, u32[]{:S(2)}, u32[]{:S(2)}) collective-permute-start(bf16[256,512]{1,0:T(8,128)(2,1)S(1)} %forward.4.refs_2_), channel_id=1, source_target_pairs={{0,2},{2,0},{1,3},{3,1},{4,6},{6,4},{5,7},{7,5},{8,10},{10,8},{9,1... | collective-permute-start | bytes 786440 | tf_op jit(solution)/shard_map/ppermute | solution.py:313
  22.9 1.1 %collective-permute-start.3 = (bf16[256,512]{1,0:T(8,128)(2,1)S(1)}, bf16[256,512]{1,0:T(8,128)(2,1)S(1)}, u32[]{:S(2)}, u32[]{:S(2)}) collective-permute-start(bf16[256,512]{1,0:T(8,128)(2,1)S(1)} %both.2.refs_0_), channel_id=1, source_target_pairs={{0,4},{4,0},{8,12},{12,8},{1,5},{5,1},{9,13},{13,9},{2,6},{6,2},{1... | collective-permute-start | bytes 786440 | tf_op jit(solution)/shard_map/ppermute | solution.py:310
  24.1 0.0 collective-permute-done.6.refs_1_
  24.1 0.0 collective-permute-start.8
  24.1 0.0 collective-permute-done.7.refs_4_
  24.1 0.5 %collective-permute-start.10 = (bf16[272,256]{1,0:T(8,128)(2,1)S(1)}, bf16[272,256]{1,0:T(8,128)(2,1)S(1)}, u32[]{:S(2)}, u32[]{:S(2)}) collective-permute-start(bf16[272,256]{1,0:T(8,128)(2,1)S(1)} %collective-permute-done.1.x_ref.refs_3_), channel_id=1, source_target_pairs={{0,1},{1,0},{2,3},{3,2},{4,5},{5,4},{6,7},{7,6},{8,9},{9,8},{10,11... | collective-permute-start | bytes 417800 | tf_op jit(solution)/shard_map/ppermute | solution.py:313
  24.6 0.0 collective-permute-done.4.b_ref
  24.6 0.1 collective-permute-start.9
  24.6 0.1 both.3.refs_3_
  24.7 0.7 %collective-permute-done.8.refs_5_ = bf16[272,256]{1,0:T(8,128)(2,1)S(1)} collective-permute-done((bf16[272,256]{1,0:T(8,128)(2,1)S(1)}, bf16[272,256]{1,0:T(8,128)(2,1)S(1)}, u32[]{:S(2)}, u32[]{:S(2)}) %collective-permute-start.8) | collective-permute-done | bytes 139296 | tf_op jit(solution)/shard_map/ppermute | solution.py:313
  25.4 0.1 collective-permute-start.11
  25.6 0.1 collective-permute-done.10.refs_7_
  25.6 0.3 collective-permute-start.13
  25.9 0.0 collective-permute-done.9.refs_6_
  25.9 0.2 collective-permute-start.12
  26.1 5.0 %arrange.1 = (bf16[1024,256]{1,0:T(8,128)(2,1)S(1)}, bf16[1024,256]{1,0:T(8,128)(2,1)S(1)}, bf16[1024,256]{1,0:T(8,128)(2,1)S(1)}, bf16[1024,2048]{1,0:T(8,128)(...) custom-call(bf16[272,256]{1,0:T(8,128)(2,1)S(1)} %pack.1.x_ref.refs_, ...), custom_call_target="tpu_custom_call" | custom-call | tf_op jit(solution)/shard_map/arrange/pallas_call | solution.py:37
  31.2 0.0 collective-permute-done.5.refs_4_
  31.2 0.4 collective-permute-start.14
  31.5 0.0 collective-permute-done.3.refs_1_
  31.6 0.2 collective-permute-start.15
  31.7 0.0 collective-permute-done.11.refs_5_
  31.8 0.0 collective-permute-done.12.refs_6_
  31.8 1.0 %gather.1 = (bf16[1024,256]{1,0:T(8,128)(2,1)S(1)}, f32[1024,256]{1,0:T(8,128)S(1)}) custom-call(bf16[256,512]{1,0:T(8,128)(2,1)S(1)} %both.2.refs_0_, bf16[256,512]{1,0:T(8,128)(2,1)S(1)} %collective-permute-done.3.refs_1_, bf16[256,512]{1,0:T(8,128)(2,1)S(1)} %forward.4.refs_2_, bf16[256,512]{1,0:T(8,128)(2,1)S(1)} %both.3.refs_3_, ...), custom_call_target="tpu_custom_call" | custom-call | tf_op jit(solution)/shard_map/gather/pallas_call | solution.py:37
  32.8 0.0 collective-permute-done.13.part_ref
  32.8 0.0 collective-permute-done.14.there_ref
  32.8 0.3 collective-permute-done.15.sums_ref
  33.1 2.4 %contrast.1.refs_2_ = bf16[1024,512]{1,0:T(8,128)(2,1)S(1)} custom-call(bf16[1024,256]{1,0:T(8,128)(2,1)S(1)} %get-tuple-element.46.phi_ref, f32[1024,256]{1,0:T(8,128)S(1)} %get-tuple-element.47.psi_ref, bf16[256,512]{1,0:T(8,128)(2,1)S(1)} %collective-permute-done.13.part_ref, bf16[256,512]{1,0:T(8,128)(2,1)S(1)} %collective-permute-done.14.there_ref, ...), custom_call_target="tpu_custom_call" | custom-call | tf_op jit(solution)/shard_map/contrast/pallas_call | solution.py:37
  35.5 0.4 collective-permute-start.16
  35.9 0.2 collective-permute-start.19
  36.1 3.5 %mine.1 = (f32[1024,256]{1,0:T(8,128)S(1)}, f32[1024,256]{1,0:T(8,128)S(1)}, f32[1024,256]{1,0:T(8,128)S(1)}, f32[1024,256]{1,0:T(8,128)S(1)}) custom-call(bf16[2048,256]{1,0:T(8,128)(2,1)S(1)} %copy-done.2, bf16[2048,256]{1,0:T(8,128)(2,1)S(1)} %copy-done.3, bf16[1024,512]{1,0:T(8,128)(2,1)S(1)} %contrast.1.refs_2_, ...), custom_call_target="tpu_custom_call" | custom-call | flops 4294967296 | tf_op jit(solution)/shard_map/mine/pallas_call | solution.py:37
  39.6 0.0 collective-permute-done.16.refs_2_
  39.6 2.7 %other_state.1 = (bf16[256,1024]{1,0:T(8,128)(2,1)S(1)}, bf16[1024,256]{1,0:T(8,128)(2,1)S(1)}, f32[256,1024]{1,0:T(8,128)S(1)}, f32[1024,256]{1,0:T(8,128)S(1)}) custom-call(bf16[256,2048]{1,0:T(8,128)(2,1)S(1)} %copy-done, bf16[2048,256]{1,0:T(8,128)(2,1)S(1)} %copy-done.2, bf16[1024,512]{1,0:T(8,128)(2,1)S(1)} %collective-permute-done.16.refs_2_, ...), custom_call_target="tpu_custom_call" | custom-call | flops 2147483648 | tf_op jit(solution)/shard_map/other_state/pallas_call | solution.py:37
  42.3 0.4 collective-permute-start.17
  42.7 0.2 collective-permute-start.18
  42.9 0.0 collective-permute-done.19.refs_3_
  42.9 3.0 %other_goal.1 = (bf16[256,1024]{1,0:T(8,128)(2,1)S(1)}, bf16[1024,256]{1,0:T(8,128)(2,1)S(1)}, f32[256,1024]{1,0:T(8,128)S(1)}, f32[1024,256]{1,0:T(8,128)S(1)},...) custom-call(bf16[256,2048]{1,0:T(8,128)(2,1)S(1)} %copy-done.1, bf16[2048,256]{1,0:T(8,128)(2,1)S(1)} %copy-done.3, ...), custom_call_target="tpu_custom_call" | custom-call | flops 2147483648 | tf_op jit(solution)/shard_map/other_goal/pallas_call | solution.py:37
  45.9 0.4 collective-permute-start.20
  46.3 0.2 collective-permute-start.21
  46.5 0.0 collective-permute-done.17.refs_0_
  46.5 0.0 collective-permute-done.18.refs_1_
  46.5 2.0 %finish.2 = (f32[256,2048]{1,0:T(8,128)}, f32[2048,256]{1,0:T(8,128)}, f32[256,2048]{1,0:T(8,128)}, f32[2048,256]{1,0:T(8,128)}) custom-call(bf16[256,1024]{1,0:T(8,128)(2,1)S(1)} %collective-permute-done.17.refs_0_, bf16[1024,256]{1,0:T(8,128)(2,1)S(1)} %collective-permute-done.18.refs_1_, ...), custom_call_target="tpu_custom_call", output_to_operand_aliasing={{0}: (4, {}), {1}: (5, {})} | custom-call | tf_op jit(solution)/shard_map/finish/pallas_call | solution.py:37
  48.5 0.0 collective-permute-done.20.refs_0_
  48.5 0.1 collective-permute-done.21.refs_1_
  48.6 1.4 %finish.3 = (f32[256,2048]{1,0:T(8,128)}, f32[2048,256]{1,0:T(8,128)}) custom-call(bf16[256,1024]{1,0:T(8,128)(2,1)S(1)} %collective-permute-done.20.refs_0_, bf16[1024,256]{1,0:T(8,128)(2,1)S(1)} %collective-permute-done.21.refs_1_, f32[256,2048]{1,0:T(8,128)} %get-tuple-element.72.refs_2_, ...), custom_call_target="tpu_custom_call", output_to_operand_aliasing={{0}: (2, {}), {1}: (3, {})} | custom-call | tf_op jit(solution)/shard_map/finish/pallas_call | solution.py:37
  (5 shorter events, 0.0 us)
Async XLA Ops:
  1.4 0.9 %copy-start.4 = (bf16[256,256]{1,0:T(8,128)(2,1)S(1)}, bf16[256,256]{1,0:T(8,128)(2,1)}, u32[]{:S(2)}) copy-start(bf16[256,256]{1,0:T(8,128)(2,1)} %refs_0_.7) | copy-start | bytes 393220
  2.3 5.2 %copy-start = (bf16[256,2048]{1,0:T(8,128)(2,1)S(1)}, bf16[256,2048]{1,0:T(8,128)(2,1)}, u32[]{:S(2)}) copy-start(bf16[256,2048]{1,0:T(8,128)(2,1)} %refs_0_.12) | copy-start | bytes 3145732
  2.3 5.2 %copy-start.1 = (bf16[256,2048]{1,0:T(8,128)(2,1)S(1)}, bf16[256,2048]{1,0:T(8,128)(2,1)}, u32[]{:S(2)}) copy-start(bf16[256,2048]{1,0:T(8,128)(2,1)} %refs_0_.13) | copy-start | bytes 3145732
  2.3 5.2 %copy-start.2 = (bf16[2048,256]{1,0:T(8,128)(2,1)S(1)}, bf16[2048,256]{1,0:T(8,128)(2,1)}, u32[]{:S(2)}) copy-start(bf16[2048,256]{1,0:T(8,128)(2,1)} %refs_1_.10) | copy-start | bytes 3145732
  2.3 5.2 %copy-start.3 = (bf16[2048,256]{1,0:T(8,128)(2,1)S(1)}, bf16[2048,256]{1,0:T(8,128)(2,1)}, u32[]{:S(2)}) copy-start(bf16[2048,256]{1,0:T(8,128)(2,1)} %refs_1_.11) | copy-start | bytes 3145732
  2.3 8.9 %collective-permute-start.1 = (bf16[272,256]{1,0:T(8,128)(2,1)S(1)}, bf16[272,256]{1,0:T(8,128)(2,1)S(1)}, u32[]{:S(2)}, u32[]{:S(2)}) collective-permute-start(bf16[272,256]{1,0:T(8,128)(2,1)S(1)} %pack.1.x_ref.refs_0_), channel_id=1, source_target_pairs={{0,12},{4,8},{8,4},{12,0},{1,13},{5,9},{9,5},{13,1},{2,14},{6,10},... | collective-permute-start | bytes 417800 | tf_op jit(solution)/shard_map/ppermute | solution.py:310
  8.8 9.4 %collective-permute-start = (bf16[256,512]{1,0:T(8,128)(2,1)S(1)}, bf16[256,512]{1,0:T(8,128)(2,1)S(1)}, u32[]{:S(2)}, u32[]{:S(2)}) collective-permute-start(bf16[256,512]{1,0:T(8,128)(2,1)S(1)} %forward.3.a_ref), channel_id=1, source_target_pairs={{0,2},{2,0},{1,3},{3,1},{4,6},{6,4},{5,7},{7,5},{8,10},{10,8},{9,1... | collective-permute-start | bytes 786440 | tf_op jit(solution)/shard_map/ppermute | solution.py:313
  11.2 9.1 %collective-permute-start.2 = (bf16[272,256]{1,0:T(8,128)(2,1)S(1)}, bf16[272,256]{1,0:T(8,128)(2,1)S(1)}, u32[]{:S(2)}, u32[]{:S(2)}) collective-permute-start(bf16[272,256]{1,0:T(8,128)(2,1)S(1)} %pack.1.x_ref.refs_0_), channel_id=1, source_target_pairs={{0,8},{4,12},{8,0},{12,4},{1,9},{5,13},{9,1},{13,5},{2,10},{6,14},... | collective-permute-start | bytes 417800 | tf_op jit(solution)/shard_map/ppermute | solution.py:310
  16.2 8.4 %collective-permute-start.4 = (bf16[256,512]{1,0:T(8,128)(2,1)S(1)}, bf16[256,512]{1,0:T(8,128)(2,1)S(1)}, u32[]{:S(2)}, u32[]{:S(2)}) collective-permute-start(bf16[256,512]{1,0:T(8,128)(2,1)S(1)} %forward.5.a_ref), channel_id=1, source_target_pairs={{0,2},{2,0},{1,3},{3,1},{4,6},{6,4},{5,7},{7,5},{8,10},{10,8},{9,1... | collective-permute-start | bytes 786440 | tf_op jit(solution)/shard_map/ppermute | solution.py:313
  17.7 6.3 %collective-permute-start.6 = (bf16[272,256]{1,0:T(8,128)(2,1)S(1)}, bf16[272,256]{1,0:T(8,128)(2,1)S(1)}, u32[]{:S(2)}, u32[]{:S(2)}) collective-permute-start(bf16[272,256]{1,0:T(8,128)(2,1)S(1)} %pack.1.x_ref.refs_0_), channel_id=1, source_target_pairs={{0,4},{4,0},{8,12},{12,8},{1,5},{5,1},{9,13},{13,9},{2,6},{6,2},{1... | collective-permute-start | bytes 417800 | tf_op jit(solution)/shard_map/ppermute | solution.py:310
  18.2 5.8 %collective-permute-start.7 = (bf16[272,256]{1,0:T(8,128)(2,1)S(1)}, bf16[272,256]{1,0:T(8,128)(2,1)S(1)}, u32[]{:S(2)}, u32[]{:S(2)}) collective-permute-start(bf16[272,256]{1,0:T(8,128)(2,1)S(1)} %pack.1.x_ref.refs_0_), channel_id=1, source_target_pairs={{0,1},{1,0},{2,3},{3,2},{4,5},{5,4},{6,7},{7,6},{8,9},{9,8},{10,11... | collective-permute-start | bytes 417800 | tf_op jit(solution)/shard_map/ppermute | solution.py:313
  21.7 9.4 %collective-permute-start.5 = (bf16[256,512]{1,0:T(8,128)(2,1)S(1)}, bf16[256,512]{1,0:T(8,128)(2,1)S(1)}, u32[]{:S(2)}, u32[]{:S(2)}) collective-permute-start(bf16[256,512]{1,0:T(8,128)(2,1)S(1)} %forward.4.refs_2_), channel_id=1, source_target_pairs={{0,2},{2,0},{1,3},{3,1},{4,6},{6,4},{5,7},{7,5},{8,10},{10,8},{9,1... | collective-permute-start | bytes 786440 | tf_op jit(solution)/shard_map/ppermute | solution.py:313
  22.9 8.6 %collective-permute-start.3 = (bf16[256,512]{1,0:T(8,128)(2,1)S(1)}, bf16[256,512]{1,0:T(8,128)(2,1)S(1)}, u32[]{:S(2)}, u32[]{:S(2)}) collective-permute-start(bf16[256,512]{1,0:T(8,128)(2,1)S(1)} %both.2.refs_0_), channel_id=1, source_target_pairs={{0,4},{4,0},{8,12},{12,8},{1,5},{5,1},{9,13},{13,9},{2,6},{6,2},{1... | collective-permute-start | bytes 786440 | tf_op jit(solution)/shard_map/ppermute | solution.py:310
  24.1 1.4 %collective-permute-start.8 = (bf16[272,256]{1,0:T(8,128)(2,1)S(1)}, bf16[272,256]{1,0:T(8,128)(2,1)S(1)}, u32[]{:S(2)}, u32[]{:S(2)}) collective-permute-start(bf16[272,256]{1,0:T(8,128)(2,1)S(1)} %collective-permute-done.6.refs_1_), channel_id=1, source_target_pairs={{0,1},{1,0},{2,3},{3,2},{4,5},{5,4},{6,7},{7,6},{8,9},{9,8},{10,11... | collective-permute-start | bytes 417800 | tf_op jit(solution)/shard_map/ppermute | solution.py:313
  24.1 1.6 %collective-permute-start.10 = (bf16[272,256]{1,0:T(8,128)(2,1)S(1)}, bf16[272,256]{1,0:T(8,128)(2,1)S(1)}, u32[]{:S(2)}, u32[]{:S(2)}) collective-permute-start(bf16[272,256]{1,0:T(8,128)(2,1)S(1)} %collective-permute-done.1.x_ref.refs_3_), channel_id=1, source_target_pairs={{0,1},{1,0},{2,3},{3,2},{4,5},{5,4},{6,7},{7,6},{8,9},{9,8},{10,11... | collective-permute-start | bytes 417800 | tf_op jit(solution)/shard_map/ppermute | solution.py:313
  24.6 1.4 %collective-permute-start.9 = (bf16[272,256]{1,0:T(8,128)(2,1)S(1)}, bf16[272,256]{1,0:T(8,128)(2,1)S(1)}, u32[]{:S(2)}, u32[]{:S(2)}) collective-permute-start(bf16[272,256]{1,0:T(8,128)(2,1)S(1)} %collective-permute-done.2.x_ref.refs_2_), channel_id=1, source_target_pairs={{0,1},{1,0},{2,3},{3,2},{4,5},{5,4},{6,7},{7,6},{8,9},{9,8},{10,11... | collective-permute-start | bytes 417800 | tf_op jit(solution)/shard_map/ppermute | solution.py:313
  25.4 6.3 %collective-permute-start.11 = (bf16[256,512]{1,0:T(8,128)(2,1)S(1)}, bf16[256,512]{1,0:T(8,128)(2,1)S(1)}, u32[]{:S(2)}, u32[]{:S(2)}) collective-permute-start(bf16[256,512]{1,0:T(8,128)(2,1)S(1)} %both.2.refs_0_), channel_id=1, source_target_pairs={{0,1},{1,0},{2,3},{3,2},{4,5},{5,4},{6,7},{7,6},{8,9},{9,8},{10,11... | collective-permute-start | bytes 786440 | tf_op jit(solution)/shard_map/ppermute | solution.py:313
  25.6 7.2 %collective-permute-start.13 = (bf16[256,512]{1,0:T(8,128)(2,1)S(1)}, bf16[256,512]{1,0:T(8,128)(2,1)S(1)}, u32[]{:S(2)}, u32[]{:S(2)}) collective-permute-start(bf16[256,512]{1,0:T(8,128)(2,1)S(1)} %forward.4.refs_2_), channel_id=1, source_target_pairs={{0,1},{1,0},{2,3},{3,2},{4,5},{5,4},{6,7},{7,6},{8,9},{9,8},{10,11... | collective-permute-start | bytes 786440 | tf_op jit(solution)/shard_map/ppermute | solution.py:313
  25.9 5.8 %collective-permute-start.12 = (bf16[256,512]{1,0:T(8,128)(2,1)S(1)}, bf16[256,512]{1,0:T(8,128)(2,1)S(1)}, u32[]{:S(2)}, u32[]{:S(2)}) collective-permute-start(bf16[256,512]{1,0:T(8,128)(2,1)S(1)} %both.3.refs_3_), channel_id=1, source_target_pairs={{0,1},{1,0},{2,3},{3,2},{4,5},{5,4},{6,7},{7,6},{8,9},{9,8},{10,11... | collective-permute-start | bytes 786440 | tf_op jit(solution)/shard_map/ppermute | solution.py:313
  31.2 1.6 %collective-permute-start.14 = (bf16[256,512]{1,0:T(8,128)(2,1)S(1)}, bf16[256,512]{1,0:T(8,128)(2,1)S(1)}, u32[]{:S(2)}, u32[]{:S(2)}) collective-permute-start(bf16[256,512]{1,0:T(8,128)(2,1)S(1)} %collective-permute-done.5.refs_4_), channel_id=1, source_target_pairs={{0,1},{1,0},{2,3},{3,2},{4,5},{5,4},{6,7},{7,6},{8,9},{9,8},{10,11... | collective-permute-start | bytes 786440 | tf_op jit(solution)/shard_map/ppermute | solution.py:313
  31.6 1.6 %collective-permute-start.15 = (bf16[256,512]{1,0:T(8,128)(2,1)S(1)}, bf16[256,512]{1,0:T(8,128)(2,1)S(1)}, u32[]{:S(2)}, u32[]{:S(2)}) collective-permute-start(bf16[256,512]{1,0:T(8,128)(2,1)S(1)} %collective-permute-done.3.refs_1_), channel_id=1, source_target_pairs={{0,1},{1,0},{2,3},{3,2},{4,5},{5,4},{6,7},{7,6},{8,9},{9,8},{10,11... | collective-permute-start | bytes 786440 | tf_op jit(solution)/shard_map/ppermute | solution.py:313
  35.5 4.1 %collective-permute-start.16 = (bf16[1024,512]{1,0:T(8,128)(2,1)S(1)}, bf16[1024,512]{1,0:T(8,128)(2,1)S(1)}, u32[]{:S(2)}, u32[]{:S(2)}) collective-permute-start(bf16[1024,512]{1,0:T(8,128)(2,1)S(1)} %contrast.1.refs_2_), channel_id=1, source_target_pairs={{0,1},{1,0},{2,3},{3,2},{4,5},{5,4},{6,7},{7,6},{8,9},{9,8},{10,11... | collective-permute-start | bytes 3145736 | tf_op jit(solution)/shard_map/ppermute | solution.py:313
  35.9 7.0 %collective-permute-start.19 = (bf16[1024,256]{1,0:T(8,128)(2,1)S(1)}, bf16[1024,256]{1,0:T(8,128)(2,1)S(1)}, u32[]{:S(2)}, u32[]{:S(2)}) collective-permute-start(bf16[1024,256]{1,0:T(8,128)(2,1)S(1)} %get-tuple-element.51.refs_4_), channel_id=1, source_target_pairs={{0,1},{1,0},{2,3},{3,2},{4,5},{5,4},{6,7},{7,6},{8,9},{9,8},{10,11... | collective-permute-start | bytes 1572872 | tf_op jit(solution)/shard_map/ppermute | solution.py:313
  42.3 4.1 %collective-permute-start.17 = (bf16[256,1024]{1,0:T(8,128)(2,1)S(1)}, bf16[256,1024]{1,0:T(8,128)(2,1)S(1)}, u32[]{:S(2)}, u32[]{:S(2)}) collective-permute-start(bf16[256,1024]{1,0:T(8,128)(2,1)S(1)} %get-tuple-element.58), channel_id=1, source_target_pairs={{0,1},{1,0},{2,3},{3,2},{4,5},{5,4},{6,7},{7,6},{8,9},{9,8},{10,11... | collective-permute-start | bytes 1572872 | tf_op jit(solution)/shard_map/ppermute | solution.py:313
  42.7 3.8 %collective-permute-start.18 = (bf16[1024,256]{1,0:T(8,128)(2,1)S(1)}, bf16[1024,256]{1,0:T(8,128)(2,1)S(1)}, u32[]{:S(2)}, u32[]{:S(2)}) collective-permute-start(bf16[1024,256]{1,0:T(8,128)(2,1)S(1)} %get-tuple-element.59), channel_id=1, source_target_pairs={{0,1},{1,0},{2,3},{3,2},{4,5},{5,4},{6,7},{7,6},{8,9},{9,8},{10,11... | collective-permute-start | bytes 1572872 | tf_op jit(solution)/shard_map/ppermute | solution.py:313
  45.9 2.6 %collective-permute-start.20 = (bf16[256,1024]{1,0:T(8,128)(2,1)S(1)}, bf16[256,1024]{1,0:T(8,128)(2,1)S(1)}, u32[]{:S(2)}, u32[]{:S(2)}) collective-permute-start(bf16[256,1024]{1,0:T(8,128)(2,1)S(1)} %get-tuple-element.70), channel_id=1, source_target_pairs={{0,1},{1,0},{2,3},{3,2},{4,5},{5,4},{6,7},{7,6},{8,9},{9,8},{10,11... | collective-permute-start | bytes 1572872 | tf_op jit(solution)/shard_map/ppermute | solution.py:313
  46.3 2.3 %collective-permute-start.21 = (bf16[1024,256]{1,0:T(8,128)(2,1)S(1)}, bf16[1024,256]{1,0:T(8,128)(2,1)S(1)}, u32[]{:S(2)}, u32[]{:S(2)}) collective-permute-start(bf16[1024,256]{1,0:T(8,128)(2,1)S(1)} %get-tuple-element.71), channel_id=1, source_target_pairs={{0,1},{1,0},{2,3},{3,2},{4,5},{5,4},{6,7},{7,6},{8,9},{9,8},{10,11... | collective-permute-start | bytes 1572872 | tf_op jit(solution)/shard_map/ppermute | solution.py:313

commit v15 on v14

--- a/solution.py
+++ b/solution.py
@@ -59,11 +59,15 @@
         out_ref[:, k * emb : (k + 1) * emb] = dot(active[...], second[...]).astype(BF)
 
 
-def pack_kernel(n_blk, n_sub, pos, x_ref, own_ref, pack_ref):
+def blank_kernel(out_ref):
+    out_ref[...] = jnp.zeros_like(out_ref)
+
+
+def pack_kernel(n_blk, n_sub, pos, blank_ref, x_ref, distance_ref, place_ref, episode_ref, pack_ref):
     rows = x_ref.shape[0]
-    owner = (pos[0] * n_sub + pos[1] + own_ref[0:1, :]) & (n_blk * n_sub - 1)
-    digits = (owner, own_ref[1:2, :], own_ref[2:3, :])
-    table = jnp.concatenate([d.astype(F32) for d in digits] + [jnp.zeros((13, rows), F32)], axis=0)
+    owner = (pos[0] * n_sub + pos[1] + distance_ref[...]) & (n_blk * n_sub - 1)
+    digits = (owner, place_ref[...], episode_ref[...])
+    table = jnp.concatenate([d.astype(F32) for d in digits] + [blank_ref[3:, :]], axis=0)
     pack_ref[:rows, :] = x_ref[...]
     pack_ref[rows:, :] = table.astype(BF)
 
@@ -235,13 +239,18 @@
         outs[2 * k + 1][...] = dot(back[...], x_ref[...])
 
 
+def column_blocks(shape):
+    n, m = shape
+    return [(at, slice(at, at + n)) for at in range(0, m, n)]
+
+
 def other_kernel(k, n_put, pos, first, second, grads_ref, rows_ref, sum_second, sum_first, *refs):
     done, outs, puts, (active, back), sems = (
         refs[:n_put],
-        refs[n_put : n_put + 4],
-        refs[n_put + 4 : 2 * n_put + 4],
-        refs[2 * n_put + 4 : 2 * n_put + 6],
-        refs[2 * n_put + 6 :],
+        refs[n_put : n_put + 3],
+        refs[n_put + 3 : 2 * n_put + 3],
+        refs[2 * n_put + 3 : 2 * n_put + 5],
+        refs[2 * n_put + 5 :],
     )
     copies = [put_half(pos[1], x, o, sems[0].at[i]) for i, (x, o) in enumerate(zip(done, puts))]
     for c in copies:
@@ -249,10 +258,13 @@
     quarter = active.shape[0]
     at = pl.multiple_of(pos[1] * quarter, quarter)
     grad_second, grad_first = rows_grads(at, first, second, grads_ref, k, rows_ref, active, back)
-    halves = ((sum_first[...] + grad_first).astype(BF).T, (sum_second[...] + grad_second).astype(BF))
-    for half, out16, out32 in zip(halves, outs[:2], outs[2:]):
-        out16[...] = half
-        out32[...] = half.astype(F32)
+    first_half, second_half = (sum_first[...] + grad_first).astype(BF).T, (sum_second[...] + grad_second).astype(BF)
+    sent, first_out, second_out = outs
+    sent[:quarter, :] = second_half
+    for at, cols in column_blocks(first_half.shape):
+        sent[quarter + at : quarter + at + first_half.shape[0], :] = first_half[:, cols]
+    first_out[...] = first_half.astype(F32)
+    second_out[...] = second_half.astype(F32)
     for c in copies:
         c.wait()
 
@@ -266,33 +278,40 @@
     return pltpu.make_async_copy(half, to, sem)
 
 
-def finish_kernel(old, new, pos, *refs):
-    n = old + new
-    halves, outs, scratch, sems = refs[:n], refs[n + old : 2 * n + old], refs[2 * n + old : -1], refs[-1]
-    copies = [put_half(pos[1], x, o, sems.at[old + i]) for i, (x, o) in enumerate(zip(halves[old:], outs[old:]))]
+def finish_kernel(new, pos, there_ref, *refs):
+    own, outs, (first, second), sems = refs[:new], refs[new + 2 : 2 * new + 4], refs[2 * new + 4 : 2 * new + 6], refs[-1]
+    copies = [put_half(pos[1], x, o, sems.at[2 + i]) for i, (x, o) in enumerate(zip(own, outs[2:]))]
     for c in copies:
         c.start()
-    for i in range(old):
-        scratch[i][...] = halves[i][...].astype(F32)
-        copies.append(put_half(1 - pos[1], scratch[i], outs[i], sems.at[i]))
-        copies[-1].start()
+    quarter = second.shape[0]
+    second[...] = there_ref[:quarter, :].astype(F32)
+    copies.append(put_half(1 - pos[1], second, outs[1], sems.at[1]))
+    copies[-1].start()
+    for at, cols in column_blocks(first.shape):
+        first[:, cols] = there_ref[quarter + at : quarter + at + first.shape[0], :].astype(F32)
+    copies.append(put_half(1 - pos[1], first, outs[0], sems.at[0]))
+    copies[-1].start()
     for c in copies:
         c.wait()
 
 
 def finish(there, own, wholes, shapes):
-    old, new = len(wholes), len(shapes)
-    n = old + new
+    new = len(shapes)
+    (width, hid), (_, emb) = (w.shape for w in wholes)
     return kernel(
-        functools.partial(finish_kernel, old, new),
+        functools.partial(finish_kernel, new),
         "finish",
         [(w.shape, w.dtype) for w in wholes] + shapes,
-        (*there, *own, *wholes),
-        [*(pltpu.VMEM(x.shape, F32) for x in there), pltpu.SemaphoreType.DMA((n,))],
-        pos=True,
-        hbm=range(n, n + old),
-        hbm_out=range(n),
-        aliases={n + i: i for i in range(old)},
+        (there, *own, *wholes),
+        [
+            pltpu.VMEM((width, hid // 2), F32),
+            pltpu.VMEM((hid // 2, emb), F32),
+            pltpu.SemaphoreType.DMA((2 + new,)),
+        ],
+        pos=True,
+        hbm=(1 + new, 2 + new),
+        hbm_out=range(2 + new),
+        aliases={1 + new: 0, 2 + new: 1},
     )
 
 
@@ -316,11 +335,12 @@
         return lax.optimization_barrier((x, *first))[0]
 
     weights = (state_first, goal_first, state_second, goal_second)
+    (blank,) = kernel(blank_kernel, "blank", [((16, rows_dev), F32)], (), limit=1, flops=2**32)
     (pack,) = kernel(
         functools.partial(pack_kernel, n_blk, n_sub),
         "pack",
         [((rows_dev + 16, width), BF)],
-        (states, jnp.stack([goal_distance.reshape(rows_dev), goal_row, episode])),
+        (blank, states, *(x.reshape(1, rows_dev) for x in (goal_distance, goal_row, episode))),
         pos=True,
         limit=4,
         flops=2**32,
@@ -387,9 +407,9 @@
         pos=True,
         flops=2 * flops,
     )
-    halves = [(shape, kind) for kind in (BF, F32) for shape in ((width, quarter), (quarter, emb))]
+    halves = [((2 * quarter, emb), BF), ((width, quarter), F32), ((quarter, emb), F32)]
     wholes = [((width, hid), F32), ((hid, emb), F32)]
-    *state_halves, state_first_own, state_second_own = kernel(
+    state_halves, state_first_own, state_second_own = kernel(
         functools.partial(other_kernel, 0, 0),
         "other_state",
         halves,
@@ -398,8 +418,8 @@
         pos=True,
         flops=flops,
     )
-    state_there = [swap(x, "sub") for x in state_halves]
-    *goal_halves, goal_first_own, goal_second_own, out0, out1 = kernel(
+    state_there = swap(state_halves, "sub")
+    goal_halves, goal_first_own, goal_second_own, out0, out1 = kernel(
         functools.partial(other_kernel, 1, 2),
         "other_goal",
         halves + wholes,
@@ -407,9 +427,9 @@
         work + [pltpu.SemaphoreType.DMA((2,))],
         pos=True,
         flops=flops,
-        hbm_out=(4, 5),
-    )
-    goal_there = [swap(x, "sub") for x in goal_halves]
+        hbm_out=(3, 4),
+    )
+    goal_there = swap(goal_halves, "sub")
     out0, out1, out2, out3 = finish(state_there, (goal_first_own, goal_second_own), (out0, out1), wholes)
     out2, out3 = finish(goal_there, (), (out2, out3), [])
     return (out0, out1, out2, out3)

time: 50.4 us -> 50 us (level)
  other arithmetic: 0.72 us -> 0 us
    another operation x1 -> x0, other arithmetic: 0.72 us -> none  [gathered(): jnp.stack([goal_distance.reshape(rows_dev), goal_row, episode])]
    ppermute x18 -> x16, starting transfers between devices: 7.87 us -> 7.36 us  [swap(): return lax.ppermute(x, axis, [(0, 1), (1, 0)])]
    pallas_call x14 -> x15, Pallas kernels: 25.3 us -> 25.8 us  [kernel(): pl.pallas_call(body, in_specs=specs, out_specs=[HBM if i in hbm_out else...]
    ppermute x18 -> x16, waiting for transfers between devices: 1.2 us -> 1.53 us  [swap(): return lax.ppermute(x, axis, [(0, 1), (1, 0)])]
  transfers between devices with their start and end apart: 22 -> 20, of which waited for: 6 -> 6; matrix products, arithmetic and copies ran while one was open for 0% -> 0% of each run, Pallas kernels for 43% -> 44%
where the time goes in v15:
time: 50 us; the launch traced here: 49.8 us
  Pallas kernels  25.8 us (52%)
  starting transfers between devices  17.7 us (35%)
  waiting for transfers between devices  4.39 us (9%)
  between operations  0.98 us (2%)
  local copies, waits for them, and re-layouts  0.92 us (2%)
    pallas_call x15, Pallas kernels, kernel(): pl.pallas_call(body, in_specs=specs, out_specs=[HBM if i in hbm_out else...  25.8 us
    ppermute x4, starting transfers between devices, across(): return lax.ppermute(x, 'blk', [(i, i ^ k) for i in range(n_blk)])  10.3 us
    ppermute x16, starting transfers between devices, swap(): return lax.ppermute(x, axis, [(0, 1), (1, 0)])  7.36 us
    ppermute x4, waiting for transfers between devices, across(): return lax.ppermute(x, 'blk', [(i, i ^ k) for i in range(n_blk)])  2.86 us
    ppermute x16, waiting for transfers between devices, swap(): return lax.ppermute(x, axis, [(0, 1), (1, 0)])  1.53 us
  transfers between devices with their start and end apart: 20, of which 6 were waited for; matrix products, arithmetic and copies ran while one was open for 0% of the time, Pallas kernels for 44%

profile of v15, /device:TPU:0, one launch (start us, length us, event | category | flops | bytes accessed | tf_op | source)
XLA Modules:
  0.0 49.8 jit_solution(13713238874610967835)
XLA Ops:
  0.6 0.0 copy-start.5
  0.6 0.0 copy-start.6
  0.7 0.0 copy-start.7
  0.7 0.0 copy-start.4
  0.7 0.6 %copy-done.5 = s32[256,1]{0,1:T(1,128)S(1)} copy-done((s32[256,1]{0,1:T(1,128)S(1)}, s32[256,1]{0,1:T(1,128)}, u32[]{:S(2)}) %copy-start.5) | copy-done | bytes 1048
  1.3 0.0 copy-done.6
  1.3 0.0 copy-done.7
  1.3 0.2 copy-done.4
  1.6 5.1 %collective-permute-start.1 = (bf16[272,256]{1,0:T(8,128)(2,1)S(1)}, bf16[272,256]{1,0:T(8,128)(2,1)S(1)}, u32[]{:S(2)}, u32[]{:S(2)}) collective-permute-start(bf16[272,256]{1,0:T(8,128)(2,1)S(1)} %pack.1.x_ref.refs_0_), channel_id=1, source_target_pairs={{0,12},{4,8},{8,4},{12,0},{1,13},{5,9},{9,5},{13,1},{2,14},{6,10},... | collective-permute-start | bytes 417800 | tf_op jit(solution)/shard_map/ppermute | solution.py:329
  6.7 0.0 copy-done
  6.7 0.0 copy-done.1
  6.7 0.0 copy-done.3
  6.7 1.4 %forward.3.a_ref = bf16[256,512]{1,0:T(8,128)(2,1)S(1)} custom-call(bf16[272,256]{1,0:T(8,128)(2,1)S(1)} %pack.1.x_ref.refs_0_, bf16[256,2048]{1,0:T(8,128)(2,1)S(1)} %copy-done, bf16[256,2048]{1,0:T(8,128)(2,1)S(1)} %copy-done.1, bf16[2048,256]{1,0:T(8,128)(2,1)S(1)} %copy-done.2, bf16[2048,256]{1,0:T(8,128)(2,1)S(1)} %copy-done.3), custom_call_target="tpu_custom_call" | custom-call | tf_op jit(solution)/shard_map/forward/pallas_call | solution.py:37
  8.1 1.6 %collective-permute-start = (bf16[256,512]{1,0:T(8,128)(2,1)S(1)}, bf16[256,512]{1,0:T(8,128)(2,1)S(1)}, u32[]{:S(2)}, u32[]{:S(2)}) collective-permute-start(bf16[256,512]{1,0:T(8,128)(2,1)S(1)} %forward.3.a_ref), channel_id=1, source_target_pairs={{0,2},{2,0},{1,3},{3,1},{4,6},{6,4},{5,7},{7,5},{8,10},{10,8},{9,1... | collective-permute-start | bytes 786440 | tf_op jit(solution)/shard_map/ppermute | solution.py:332
  9.7 0.8 %collective-permute-done.1.x_ref.refs_3_ = bf16[272,256]{1,0:T(8,128)(2,1)S(1)} collective-permute-done((bf16[272,256]{1,0:T(8,128)(2,1)S(1)}, bf16[272,256]{1,0:T(8,128)(2,1)S(1)}, u32[]{:S(2)}, u32[]{:S(2)}) %collective-permute-start.1) | collective-permute-done | bytes 139296 | tf_op jit(solution)/shard_map/ppermute | solution.py:329
  10.5 3.6 %collective-permute-start.2 = (bf16[272,256]{1,0:T(8,128)(2,1)S(1)}, bf16[272,256]{1,0:T(8,128)(2,1)S(1)}, u32[]{:S(2)}, u32[]{:S(2)}) collective-permute-start(bf16[272,256]{1,0:T(8,128)(2,1)S(1)} %pack.1.x_ref.refs_0_), channel_id=1, source_target_pairs={{0,8},{4,12},{8,0},{12,4},{1,9},{5,13},{9,1},{13,5},{2,10},{6,14},... | collective-permute-start | bytes 417800 | tf_op jit(solution)/shard_map/ppermute | solution.py:329
  14.1 1.4 %forward.5.a_ref = bf16[256,512]{1,0:T(8,128)(2,1)S(1)} custom-call(bf16[272,256]{1,0:T(8,128)(2,1)S(1)} %collective-permute-done.1.x_ref.refs_3_, bf16[256,2048]{1,0:T(8,128)(2,1)S(1)} %copy-done, bf16[256,2048]{1,0:T(8,128)(2,1)S(1)} %copy-done.1, bf16[2048,256]{1,0:T(8,128)(2,1)S(1)} %copy-done.2, bf16[2048,256]{1,0:T(8,128)(2,1)S(1)} %copy-done.3), custom_call_target="tpu_custom_call" | custom-call | tf_op jit(solution)/shard_map/forward/pallas_call | solution.py:37
  15.5 1.6 %collective-permute-start.4 = (bf16[256,512]{1,0:T(8,128)(2,1)S(1)}, bf16[256,512]{1,0:T(8,128)(2,1)S(1)}, u32[]{:S(2)}, u32[]{:S(2)}) collective-permute-start(bf16[256,512]{1,0:T(8,128)(2,1)S(1)} %forward.5.a_ref), channel_id=1, source_target_pairs={{0,2},{2,0},{1,3},{3,1},{4,6},{6,4},{5,7},{7,5},{8,10},{10,8},{9,1... | collective-permute-start | bytes 786440 | tf_op jit(solution)/shard_map/ppermute | solution.py:332
  17.1 0.5 collective-permute-start.6
  17.6 0.0 collective-permute-start.7
  17.6 0.0 collective-permute-done.b_ref
  17.6 0.1 both.2.refs_0_
  17.6 2.0 %collective-permute-done.2.x_ref.refs_2_ = bf16[272,256]{1,0:T(8,128)(2,1)S(1)} collective-permute-done((bf16[272,256]{1,0:T(8,128)(2,1)S(1)}, bf16[272,256]{1,0:T(8,128)(2,1)S(1)}, u32[]{:S(2)}, u32[]{:S(2)}) %collective-permute-start.2) | collective-permute-done | bytes 139296 | tf_op jit(solution)/shard_map/ppermute | solution.py:329
  19.7 1.4 %forward.4.refs_2_ = bf16[256,512]{1,0:T(8,128)(2,1)S(1)} custom-call(bf16[272,256]{1,0:T(8,128)(2,1)S(1)} %collective-permute-done.2.x_ref.refs_2_, bf16[256,2048]{1,0:T(8,128)(2,1)S(1)} %copy-done, bf16[256,2048]{1,0:T(8,128)(2,1)S(1)} %copy-done.1, bf16[2048,256]{1,0:T(8,128)(2,1)S(1)} %copy-done.2, bf16[2048,256]{1,0:T(8,128)(2,1)S(1)} %copy-done.3), custom_call_target="tpu_custom_call" | custom-call | tf_op jit(solution)/shard_map/forward/pallas_call | solution.py:37
  21.0 1.2 %collective-permute-start.5 = (bf16[256,512]{1,0:T(8,128)(2,1)S(1)}, bf16[256,512]{1,0:T(8,128)(2,1)S(1)}, u32[]{:S(2)}, u32[]{:S(2)}) collective-permute-start(bf16[256,512]{1,0:T(8,128)(2,1)S(1)} %forward.4.refs_2_), channel_id=1, source_target_pairs={{0,2},{2,0},{1,3},{3,1},{4,6},{6,4},{5,7},{7,5},{8,10},{10,8},{9,1... | collective-permute-start | bytes 786440 | tf_op jit(solution)/shard_map/ppermute | solution.py:332
  22.3 1.1 %collective-permute-start.3 = (bf16[256,512]{1,0:T(8,128)(2,1)S(1)}, bf16[256,512]{1,0:T(8,128)(2,1)S(1)}, u32[]{:S(2)}, u32[]{:S(2)}) collective-permute-start(bf16[256,512]{1,0:T(8,128)(2,1)S(1)} %both.2.refs_0_), channel_id=1, source_target_pairs={{0,4},{4,0},{8,12},{12,8},{1,5},{5,1},{9,13},{13,9},{2,6},{6,2},{1... | collective-permute-start | bytes 786440 | tf_op jit(solution)/shard_map/ppermute | solution.py:329
  23.4 0.0 collective-permute-done.6.refs_1_
  23.4 0.0 collective-permute-start.8
  23.4 0.0 collective-permute-done.7.refs_4_
  23.4 0.5 %collective-permute-start.10 = (bf16[272,256]{1,0:T(8,128)(2,1)S(1)}, bf16[272,256]{1,0:T(8,128)(2,1)S(1)}, u32[]{:S(2)}, u32[]{:S(2)}) collective-permute-start(bf16[272,256]{1,0:T(8,128)(2,1)S(1)} %collective-permute-done.1.x_ref.refs_3_), channel_id=1, source_target_pairs={{0,1},{1,0},{2,3},{3,2},{4,5},{5,4},{6,7},{7,6},{8,9},{9,8},{10,11... | collective-permute-start | bytes 417800 | tf_op jit(solution)/shard_map/ppermute | solution.py:332
  23.9 0.0 collective-permute-done.4.b_ref
  23.9 0.1 collective-permute-start.9
  24.0 0.1 both.3.refs_3_
  24.0 0.7 %collective-permute-done.8.refs_5_ = bf16[272,256]{1,0:T(8,128)(2,1)S(1)} collective-permute-done((bf16[272,256]{1,0:T(8,128)(2,1)S(1)}, bf16[272,256]{1,0:T(8,128)(2,1)S(1)}, u32[]{:S(2)}, u32[]{:S(2)}) %collective-permute-start.8) | collective-permute-done | bytes 139296 | tf_op jit(solution)/shard_map/ppermute | solution.py:332
  24.7 0.1 collective-permute-start.11
  24.9 0.1 collective-permute-done.10.refs_7_
  24.9 0.3 collective-permute-start.13
  25.3 0.0 collective-permute-done.9.refs_6_
  25.3 0.2 collective-permute-start.12
  25.5 5.0 %arrange.1 = (bf16[1024,256]{1,0:T(8,128)(2,1)S(1)}, bf16[1024,256]{1,0:T(8,128)(2,1)S(1)}, bf16[1024,256]{1,0:T(8,128)(2,1)S(1)}, bf16[1024,2048]{1,0:T(8,128)(...) custom-call(bf16[272,256]{1,0:T(8,128)(2,1)S(1)} %pack.1.x_ref.refs_, ...), custom_call_target="tpu_custom_call" | custom-call | tf_op jit(solution)/shard_map/arrange/pallas_call | solution.py:37
  30.5 0.0 collective-permute-done.5.refs_4_
  30.5 0.4 collective-permute-start.14
  30.9 0.0 collective-permute-done.3.refs_1_
  30.9 0.2 collective-permute-start.15
  31.1 0.0 collective-permute-done.11.refs_5_
  31.1 0.0 collective-permute-done.12.refs_6_
  31.1 1.0 %gather.1 = (bf16[1024,256]{1,0:T(8,128)(2,1)S(1)}, f32[1024,256]{1,0:T(8,128)S(1)}) custom-call(bf16[256,512]{1,0:T(8,128)(2,1)S(1)} %both.2.refs_0_, bf16[256,512]{1,0:T(8,128)(2,1)S(1)} %collective-permute-done.3.refs_1_, bf16[256,512]{1,0:T(8,128)(2,1)S(1)} %forward.4.refs_2_, bf16[256,512]{1,0:T(8,128)(2,1)S(1)} %both.3.refs_3_, ...), custom_call_target="tpu_custom_call" | custom-call | tf_op jit(solution)/shard_map/gather/pallas_call | solution.py:37
  32.1 0.0 collective-permute-done.13.part_ref
  32.1 0.0 collective-permute-done.14.there_ref
  32.1 0.3 collective-permute-done.15.sums_ref
  32.5 2.4 %contrast.1.refs_2_ = bf16[1024,512]{1,0:T(8,128)(2,1)S(1)} custom-call(bf16[1024,256]{1,0:T(8,128)(2,1)S(1)} %get-tuple-element.44.phi_ref, f32[1024,256]{1,0:T(8,128)S(1)} %get-tuple-element.45.psi_ref, bf16[256,512]{1,0:T(8,128)(2,1)S(1)} %collective-permute-done.13.part_ref, bf16[256,512]{1,0:T(8,128)(2,1)S(1)} %collective-permute-done.14.there_ref, ...), custom_call_target="tpu_custom_call" | custom-call | tf_op jit(solution)/shard_map/contrast/pallas_call | solution.py:37
  34.8 0.4 collective-permute-start.16
  35.2 0.2 collective-permute-start.18
  35.4 3.5 %mine.1 = (f32[1024,256]{1,0:T(8,128)S(1)}, f32[1024,256]{1,0:T(8,128)S(1)}, f32[1024,256]{1,0:T(8,128)S(1)}, f32[1024,256]{1,0:T(8,128)S(1)}) custom-call(bf16[2048,256]{1,0:T(8,128)(2,1)S(1)} %copy-done.2, bf16[2048,256]{1,0:T(8,128)(2,1)S(1)} %copy-done.3, bf16[1024,512]{1,0:T(8,128)(2,1)S(1)} %contrast.1.refs_2_, ...), custom_call_target="tpu_custom_call" | custom-call | flops 4294967296 | tf_op jit(solution)/shard_map/mine/pallas_call | solution.py:37
  38.9 0.0 collective-permute-done.16.refs_2_
  38.9 2.7 %other_state.1 = (bf16[2048,256]{1,0:T(8,128)(2,1)S(1)}, f32[256,1024]{1,0:T(8,128)S(1)}, f32[1024,256]{1,0:T(8,128)S(1)}) custom-call(bf16[256,2048]{1,0:T(8,128)(2,1)S(1)} %copy-done, bf16[2048,256]{1,0:T(8,128)(2,1)S(1)} %copy-done.2, bf16[1024,512]{1,0:T(8,128)(2,1)S(1)} %collective-permute-done.16.refs_2_, ...), custom_call_target="tpu_custom_call" | custom-call | flops 2147483648 | tf_op jit(solution)/shard_map/other_state/pallas_call | solution.py:37
  41.7 0.4 collective-permute-start.17
  42.0 0.0 collective-permute-done.18.refs_3_
  42.0 3.5 %other_goal.1 = (bf16[2048,256]{1,0:T(8,128)(2,1)S(1)}, f32[256,1024]{1,0:T(8,128)S(1)}, f32[1024,256]{1,0:T(8,128)S(1)}, f32[256,2048]{1,0:T(8,128)}, f32[2048,256]{1,0:T(8,128)}) custom-call(bf16[256,2048]{1,0:T(8,128)(2,1)S(1)} %copy-done.1, bf16[2048,256]{1,0:T(8,128)(2,1)S(1)} %copy-done.3, bf16[1024,512]{1,0:T(8,128)(2,1)S(1)} %collective-permute-done.16.refs_2_, ...), custom_call_target="tpu_custom_call" | custom-call | flops 2147483648 | tf_op jit(solution)/shard_map/other_goal/pallas_call | solution.py:37
  45.5 0.3 collective-permute-start.19
  45.8 0.0 collective-permute-done.17.refs_0_
  45.8 2.0 %finish.2 = (f32[256,2048]{1,0:T(8,128)}, f32[2048,256]{1,0:T(8,128)}, f32[256,2048]{1,0:T(8,128)}, f32[2048,256]{1,0:T(8,128)}) custom-call(bf16[2048,256]{1,0:T(8,128)(2,1)S(1)} %collective-permute-done.17.refs_0_, f32[256,1024]{1,0:T(8,128)S(1)} %get-tuple-element.61.refs_1_, ...), custom_call_target="tpu_custom_call", output_to_operand_aliasing={{0}: (3, {}), {1}: (4, {})} | custom-call | tf_op jit(solution)/shard_map/finish/pallas_call | solution.py:37
  47.8 0.4 collective-permute-done.19.refs_0_
  48.3 1.4 %finish.3 = (f32[256,2048]{1,0:T(8,128)}, f32[2048,256]{1,0:T(8,128)}) custom-call(bf16[2048,256]{1,0:T(8,128)(2,1)S(1)} %collective-permute-done.19.refs_0_, f32[256,2048]{1,0:T(8,128)} %get-tuple-element.68.refs_1_, f32[2048,256]{1,0:T(8,128)} %get-tuple-element.69.refs_2_), custom_call_target="tpu_custom_call", output_to_operand_aliasing={{0}: (1, {}), {1}: (2, {})} | custom-call | tf_op jit(solution)/shard_map/finish/pallas_call | solution.py:37
  (7 shorter events, 0.0 us)
Async XLA Ops:
  0.6 0.7 %copy-start.5 = (s32[256,1]{0,1:T(1,128)S(1)}, s32[256,1]{0,1:T(1,128)}, u32[]{:S(2)}) copy-start(s32[256,1]{0,1:T(1,128)} %param.9) | copy-start | bytes 3076
  0.6 0.7 %copy-start.6 = (s32[256]{0:T(256)S(1)}, s32[256]{0:T(256)}, u32[]{:S(2)}) copy-start(s32[256]{0:T(256)} %param.10) | copy-start | bytes 3076
  0.7 0.7 %copy-start.7 = (s32[256]{0:T(256)S(1)}, s32[256]{0:T(256)}, u32[]{:S(2)}) copy-start(s32[256]{0:T(256)} %param.11) | copy-start | bytes 3076
  0.7 0.9 %copy-start.4 = (bf16[256,256]{1,0:T(8,128)(2,1)S(1)}, bf16[256,256]{1,0:T(8,128)(2,1)}, u32[]{:S(2)}) copy-start(bf16[256,256]{1,0:T(8,128)(2,1)} %refs_1_.7) | copy-start | bytes 393220
  1.6 5.2 %copy-start = (bf16[256,2048]{1,0:T(8,128)(2,1)S(1)}, bf16[256,2048]{1,0:T(8,128)(2,1)}, u32[]{:S(2)}) copy-start(bf16[256,2048]{1,0:T(8,128)(2,1)} %refs_0_.10) | copy-start | bytes 3145732
  1.6 5.2 %copy-start.1 = (bf16[256,2048]{1,0:T(8,128)(2,1)S(1)}, bf16[256,2048]{1,0:T(8,128)(2,1)}, u32[]{:S(2)}) copy-start(bf16[256,2048]{1,0:T(8,128)(2,1)} %refs_0_.11) | copy-start | bytes 3145732
  1.6 5.2 %copy-start.2 = (bf16[2048,256]{1,0:T(8,128)(2,1)S(1)}, bf16[2048,256]{1,0:T(8,128)(2,1)}, u32[]{:S(2)}) copy-start(bf16[2048,256]{1,0:T(8,128)(2,1)} %refs_1_.12) | copy-start | bytes 3145732
  1.6 5.2 %copy-start.3 = (bf16[2048,256]{1,0:T(8,128)(2,1)S(1)}, bf16[2048,256]{1,0:T(8,128)(2,1)}, u32[]{:S(2)}) copy-start(bf16[2048,256]{1,0:T(8,128)(2,1)} %refs_1_.13) | copy-start | bytes 3145732
  1.6 8.9 %collective-permute-start.1 = (bf16[272,256]{1,0:T(8,128)(2,1)S(1)}, bf16[272,256]{1,0:T(8,128)(2,1)S(1)}, u32[]{:S(2)}, u32[]{:S(2)}) collective-permute-start(bf16[272,256]{1,0:T(8,128)(2,1)S(1)} %pack.1.x_ref.refs_0_), channel_id=1, source_target_pairs={{0,12},{4,8},{8,4},{12,0},{1,13},{5,9},{9,5},{13,1},{2,14},{6,10},... | collective-permute-start | bytes 417800 | tf_op jit(solution)/shard_map/ppermute | solution.py:329
  8.1 9.4 %collective-permute-start = (bf16[256,512]{1,0:T(8,128)(2,1)S(1)}, bf16[256,512]{1,0:T(8,128)(2,1)S(1)}, u32[]{:S(2)}, u32[]{:S(2)}) collective-permute-start(bf16[256,512]{1,0:T(8,128)(2,1)S(1)} %forward.3.a_ref), channel_id=1, source_target_pairs={{0,2},{2,0},{1,3},{3,1},{4,6},{6,4},{5,7},{7,5},{8,10},{10,8},{9,1... | collective-permute-start | bytes 786440 | tf_op jit(solution)/shard_map/ppermute | solution.py:332
  10.5 9.1 %collective-permute-start.2 = (bf16[272,256]{1,0:T(8,128)(2,1)S(1)}, bf16[272,256]{1,0:T(8,128)(2,1)S(1)}, u32[]{:S(2)}, u32[]{:S(2)}) collective-permute-start(bf16[272,256]{1,0:T(8,128)(2,1)S(1)} %pack.1.x_ref.refs_0_), channel_id=1, source_target_pairs={{0,8},{4,12},{8,0},{12,4},{1,9},{5,13},{9,1},{13,5},{2,10},{6,14},... | collective-permute-start | bytes 417800 | tf_op jit(solution)/shard_map/ppermute | solution.py:329
  15.5 8.4 %collective-permute-start.4 = (bf16[256,512]{1,0:T(8,128)(2,1)S(1)}, bf16[256,512]{1,0:T(8,128)(2,1)S(1)}, u32[]{:S(2)}, u32[]{:S(2)}) collective-permute-start(bf16[256,512]{1,0:T(8,128)(2,1)S(1)} %forward.5.a_ref), channel_id=1, source_target_pairs={{0,2},{2,0},{1,3},{3,1},{4,6},{6,4},{5,7},{7,5},{8,10},{10,8},{9,1... | collective-permute-start | bytes 786440 | tf_op jit(solution)/shard_map/ppermute | solution.py:332
  17.1 6.3 %collective-permute-start.6 = (bf16[272,256]{1,0:T(8,128)(2,1)S(1)}, bf16[272,256]{1,0:T(8,128)(2,1)S(1)}, u32[]{:S(2)}, u32[]{:S(2)}) collective-permute-start(bf16[272,256]{1,0:T(8,128)(2,1)S(1)} %pack.1.x_ref.refs_0_), channel_id=1, source_target_pairs={{0,4},{4,0},{8,12},{12,8},{1,5},{5,1},{9,13},{13,9},{2,6},{6,2},{1... | collective-permute-start | bytes 417800 | tf_op jit(solution)/shard_map/ppermute | solution.py:329
  17.6 5.8 %collective-permute-start.7 = (bf16[272,256]{1,0:T(8,128)(2,1)S(1)}, bf16[272,256]{1,0:T(8,128)(2,1)S(1)}, u32[]{:S(2)}, u32[]{:S(2)}) collective-permute-start(bf16[272,256]{1,0:T(8,128)(2,1)S(1)} %pack.1.x_ref.refs_0_), channel_id=1, source_target_pairs={{0,1},{1,0},{2,3},{3,2},{4,5},{5,4},{6,7},{7,6},{8,9},{9,8},{10,11... | collective-permute-start | bytes 417800 | tf_op jit(solution)/shard_map/ppermute | solution.py:332
  21.0 9.4 %collective-permute-start.5 = (bf16[256,512]{1,0:T(8,128)(2,1)S(1)}, bf16[256,512]{1,0:T(8,128)(2,1)S(1)}, u32[]{:S(2)}, u32[]{:S(2)}) collective-permute-start(bf16[256,512]{1,0:T(8,128)(2,1)S(1)} %forward.4.refs_2_), channel_id=1, source_target_pairs={{0,2},{2,0},{1,3},{3,1},{4,6},{6,4},{5,7},{7,5},{8,10},{10,8},{9,1... | collective-permute-start | bytes 786440 | tf_op jit(solution)/shard_map/ppermute | solution.py:332
  22.3 8.6 %collective-permute-start.3 = (bf16[256,512]{1,0:T(8,128)(2,1)S(1)}, bf16[256,512]{1,0:T(8,128)(2,1)S(1)}, u32[]{:S(2)}, u32[]{:S(2)}) collective-permute-start(bf16[256,512]{1,0:T(8,128)(2,1)S(1)} %both.2.refs_0_), channel_id=1, source_target_pairs={{0,4},{4,0},{8,12},{12,8},{1,5},{5,1},{9,13},{13,9},{2,6},{6,2},{1... | collective-permute-start | bytes 786440 | tf_op jit(solution)/shard_map/ppermute | solution.py:329
  23.4 1.4 %collective-permute-start.8 = (bf16[272,256]{1,0:T(8,128)(2,1)S(1)}, bf16[272,256]{1,0:T(8,128)(2,1)S(1)}, u32[]{:S(2)}, u32[]{:S(2)}) collective-permute-start(bf16[272,256]{1,0:T(8,128)(2,1)S(1)} %collective-permute-done.6.refs_1_), channel_id=1, source_target_pairs={{0,1},{1,0},{2,3},{3,2},{4,5},{5,4},{6,7},{7,6},{8,9},{9,8},{10,11... | collective-permute-start | bytes 417800 | tf_op jit(solution)/shard_map/ppermute | solution.py:332
  23.4 1.6 %collective-permute-start.10 = (bf16[272,256]{1,0:T(8,128)(2,1)S(1)}, bf16[272,256]{1,0:T(8,128)(2,1)S(1)}, u32[]{:S(2)}, u32[]{:S(2)}) collective-permute-start(bf16[272,256]{1,0:T(8,128)(2,1)S(1)} %collective-permute-done.1.x_ref.refs_3_), channel_id=1, source_target_pairs={{0,1},{1,0},{2,3},{3,2},{4,5},{5,4},{6,7},{7,6},{8,9},{9,8},{10,11... | collective-permute-start | bytes 417800 | tf_op jit(solution)/shard_map/ppermute | solution.py:332
  23.9 1.4 %collective-permute-start.9 = (bf16[272,256]{1,0:T(8,128)(2,1)S(1)}, bf16[272,256]{1,0:T(8,128)(2,1)S(1)}, u32[]{:S(2)}, u32[]{:S(2)}) collective-permute-start(bf16[272,256]{1,0:T(8,128)(2,1)S(1)} %collective-permute-done.2.x_ref.refs_2_), channel_id=1, source_target_pairs={{0,1},{1,0},{2,3},{3,2},{4,5},{5,4},{6,7},{7,6},{8,9},{9,8},{10,11... | collective-permute-start | bytes 417800 | tf_op jit(solution)/shard_map/ppermute | solution.py:332
  24.7 6.3 %collective-permute-start.11 = (bf16[256,512]{1,0:T(8,128)(2,1)S(1)}, bf16[256,512]{1,0:T(8,128)(2,1)S(1)}, u32[]{:S(2)}, u32[]{:S(2)}) collective-permute-start(bf16[256,512]{1,0:T(8,128)(2,1)S(1)} %both.2.refs_0_), channel_id=1, source_target_pairs={{0,1},{1,0},{2,3},{3,2},{4,5},{5,4},{6,7},{7,6},{8,9},{9,8},{10,11... | collective-permute-start | bytes 786440 | tf_op jit(solution)/shard_map/ppermute | solution.py:332
  24.9 7.2 %collective-permute-start.13 = (bf16[256,512]{1,0:T(8,128)(2,1)S(1)}, bf16[256,512]{1,0:T(8,128)(2,1)S(1)}, u32[]{:S(2)}, u32[]{:S(2)}) collective-permute-start(bf16[256,512]{1,0:T(8,128)(2,1)S(1)} %forward.4.refs_2_), channel_id=1, source_target_pairs={{0,1},{1,0},{2,3},{3,2},{4,5},{5,4},{6,7},{7,6},{8,9},{9,8},{10,11... | collective-permute-start | bytes 786440 | tf_op jit(solution)/shard_map/ppermute | solution.py:332
  25.3 5.8 %collective-permute-start.12 = (bf16[256,512]{1,0:T(8,128)(2,1)S(1)}, bf16[256,512]{1,0:T(8,128)(2,1)S(1)}, u32[]{:S(2)}, u32[]{:S(2)}) collective-permute-start(bf16[256,512]{1,0:T(8,128)(2,1)S(1)} %both.3.refs_3_), channel_id=1, source_target_pairs={{0,1},{1,0},{2,3},{3,2},{4,5},{5,4},{6,7},{7,6},{8,9},{9,8},{10,11... | collective-permute-start | bytes 786440 | tf_op jit(solution)/shard_map/ppermute | solution.py:332
  30.5 1.6 %collective-permute-start.14 = (bf16[256,512]{1,0:T(8,128)(2,1)S(1)}, bf16[256,512]{1,0:T(8,128)(2,1)S(1)}, u32[]{:S(2)}, u32[]{:S(2)}) collective-permute-start(bf16[256,512]{1,0:T(8,128)(2,1)S(1)} %collective-permute-done.5.refs_4_), channel_id=1, source_target_pairs={{0,1},{1,0},{2,3},{3,2},{4,5},{5,4},{6,7},{7,6},{8,9},{9,8},{10,11... | collective-permute-start | bytes 786440 | tf_op jit(solution)/shard_map/ppermute | solution.py:332
  30.9 1.6 %collective-permute-start.15 = (bf16[256,512]{1,0:T(8,128)(2,1)S(1)}, bf16[256,512]{1,0:T(8,128)(2,1)S(1)}, u32[]{:S(2)}, u32[]{:S(2)}) collective-permute-start(bf16[256,512]{1,0:T(8,128)(2,1)S(1)} %collective-permute-done.3.refs_1_), channel_id=1, source_target_pairs={{0,1},{1,0},{2,3},{3,2},{4,5},{5,4},{6,7},{7,6},{8,9},{9,8},{10,11... | collective-permute-start | bytes 786440 | tf_op jit(solution)/shard_map/ppermute | solution.py:332
  34.8 4.1 %collective-permute-start.16 = (bf16[1024,512]{1,0:T(8,128)(2,1)S(1)}, bf16[1024,512]{1,0:T(8,128)(2,1)S(1)}, u32[]{:S(2)}, u32[]{:S(2)}) collective-permute-start(bf16[1024,512]{1,0:T(8,128)(2,1)S(1)} %contrast.1.refs_2_), channel_id=1, source_target_pairs={{0,1},{1,0},{2,3},{3,2},{4,5},{5,4},{6,7},{7,6},{8,9},{9,8},{10,11... | collective-permute-start | bytes 3145736 | tf_op jit(solution)/shard_map/ppermute | solution.py:332
  35.2 6.8 %collective-permute-start.18 = (bf16[1024,256]{1,0:T(8,128)(2,1)S(1)}, bf16[1024,256]{1,0:T(8,128)(2,1)S(1)}, u32[]{:S(2)}, u32[]{:S(2)}) collective-permute-start(bf16[1024,256]{1,0:T(8,128)(2,1)S(1)} %get-tuple-element.49.refs_4_), channel_id=1, source_target_pairs={{0,1},{1,0},{2,3},{3,2},{4,5},{5,4},{6,7},{7,6},{8,9},{9,8},{10,11... | collective-permute-start | bytes 1572872 | tf_op jit(solution)/shard_map/ppermute | solution.py:332
  41.7 4.1 %collective-permute-start.17 = (bf16[2048,256]{1,0:T(8,128)(2,1)S(1)}, bf16[2048,256]{1,0:T(8,128)(2,1)S(1)}, u32[]{:S(2)}, u32[]{:S(2)}) collective-permute-start(bf16[2048,256]{1,0:T(8,128)(2,1)S(1)} %get-tuple-element.56), channel_id=1, source_target_pairs={{0,1},{1,0},{2,3},{3,2},{4,5},{5,4},{6,7},{7,6},{8,9},{9,8},{10,11... | collective-permute-start | bytes 3145736 | tf_op jit(solution)/shard_map/ppermute | solution.py:332
  45.5 2.7 %collective-permute-start.19 = (bf16[2048,256]{1,0:T(8,128)(2,1)S(1)}, bf16[2048,256]{1,0:T(8,128)(2,1)S(1)}, u32[]{:S(2)}, u32[]{:S(2)}) collective-permute-start(bf16[2048,256]{1,0:T(8,128)(2,1)S(1)} %get-tuple-element.67), channel_id=1, source_target_pairs={{0,1},{1,0},{2,3},{3,2},{4,5},{5,4},{6,7},{7,6},{8,9},{9,8},{10,11... | collective-permute-start | bytes 3145736 | tf_op jit(solution)/shard_map/ppermute | solution.py:332

commit v16 on v14

--- a/solution.py
+++ b/solution.py
@@ -59,11 +59,15 @@
         out_ref[:, k * emb : (k + 1) * emb] = dot(active[...], second[...]).astype(BF)
 
 
-def pack_kernel(n_blk, n_sub, pos, x_ref, own_ref, pack_ref):
+def blank_kernel(out_ref):
+    out_ref[...] = jnp.zeros_like(out_ref)
+
+
+def pack_kernel(n_blk, n_sub, pos, blank_ref, x_ref, distance_ref, place_ref, episode_ref, pack_ref):
     rows = x_ref.shape[0]
-    owner = (pos[0] * n_sub + pos[1] + own_ref[0:1, :]) & (n_blk * n_sub - 1)
-    digits = (owner, own_ref[1:2, :], own_ref[2:3, :])
-    table = jnp.concatenate([d.astype(F32) for d in digits] + [jnp.zeros((13, rows), F32)], axis=0)
+    owner = (pos[0] * n_sub + pos[1] + distance_ref[...]) & (n_blk * n_sub - 1)
+    digits = (owner, place_ref[...], episode_ref[...])
+    table = jnp.concatenate([d.astype(F32) for d in digits] + [blank_ref[3:, :]], axis=0)
     pack_ref[:rows, :] = x_ref[...]
     pack_ref[rows:, :] = table.astype(BF)
 
@@ -316,11 +320,12 @@
         return lax.optimization_barrier((x, *first))[0]
 
     weights = (state_first, goal_first, state_second, goal_second)
+    (blank,) = kernel(blank_kernel, "blank", [((16, rows_dev), F32)], (), limit=1, flops=2**32)
     (pack,) = kernel(
         functools.partial(pack_kernel, n_blk, n_sub),
         "pack",
         [((rows_dev + 16, width), BF)],
-        (states, jnp.stack([goal_distance.reshape(rows_dev), goal_row, episode])),
+        (blank, states, *(x.reshape(1, rows_dev) for x in (goal_distance, goal_row, episode))),
         pos=True,
         limit=4,
         flops=2**32,
@@ -336,7 +341,9 @@
 
     sums = {0: both(part0, there0)}
     sums[1] = across(after(sums[0], got[2]), 1)
-    part2 = forward(after(got[2], sums[0]), held, rows_dev)
+    others = {k: swap(got[k], "sub") for k in (0, 3)}
+    part2 = forward(after(got[2], sums[0], others[0], others[3]), held, rows_dev)
+    others.update({k: swap(got[k], "sub") for k in (1, 2)})
     there2 = swap(part2, "rep")
     sums[3] = both(part3, there3)
 
@@ -347,7 +354,7 @@
         "arrange",
         [side, side, side, ((rows_all // 2, rows_all), BF), ((1, rows_all // 2), F32)]
         + [((quarter, rows_all // 2), BF)] * 4,
-        (*(got[k] for k in range(n_blk)), *(swap(got[k], "sub") for k in range(n_blk)), sf, gf),
+        (*(got[k] for k in range(n_blk)), *(others[k] for k in range(n_blk)), sf, gf),
         [
             pltpu.VMEM((rows_all, width), BF),
             pltpu.VMEM((16, rows_all // 2), F32),

time: 50.4 us -> 50.2 us (level)
  other arithmetic: 0.72 us -> 0 us
    another operation x1 -> x0, other arithmetic: 0.72 us -> none  [gathered(): jnp.stack([goal_distance.reshape(rows_dev), goal_row, episode])]
    ppermute x18, waiting for transfers between devices: 1.2 us -> 1.89 us  [swap(): return lax.ppermute(x, axis, [(0, 1), (1, 0)])]
    pallas_call x14 -> x15, Pallas kernels: 25.3 us -> 25.3 us  [kernel(): pl.pallas_call(body, in_specs=specs, out_specs=[HBM if i in hbm_out else...]
  transfers between devices with their start and end apart: 22 -> 22, of which waited for: 6 -> 5; matrix products, arithmetic and copies ran while one was open for 0% -> 0% of each run, Pallas kernels for 43% -> 43%
where the time goes in v16:
time: 50.2 us; the launch traced here: 50.1 us
  Pallas kernels  25.3 us (50%)
  starting transfers between devices  18.4 us (37%)
  waiting for transfers between devices  4.41 us (9%)
  between operations  1 us (2%)
  local copies, waits for them, and re-layouts  0.92 us (2%)
    pallas_call x15, Pallas kernels, kernel(): pl.pallas_call(body, in_specs=specs, out_specs=[HBM if i in hbm_out else...  25.3 us
    ppermute x4, starting transfers between devices, across(): return lax.ppermute(x, 'blk', [(i, i ^ k) for i in range(n_blk)])  10.3 us
    ppermute x18, starting transfers between devices, swap(): return lax.ppermute(x, axis, [(0, 1), (1, 0)])  8.14 us
    ppermute x4, waiting for transfers between devices, across(): return lax.ppermute(x, 'blk', [(i, i ^ k) for i in range(n_blk)])  2.52 us
    ppermute x18, waiting for transfers between devices, swap(): return lax.ppermute(x, axis, [(0, 1), (1, 0)])  1.89 us
  transfers between devices with their start and end apart: 22, of which 5 were waited for; matrix products, arithmetic and copies ran while one was open for 0% of the time, Pallas kernels for 43%

profile of v16, /device:TPU:0, one launch (start us, length us, event | category | flops | bytes accessed | tf_op | source)
XLA Modules:
  0.0 50.1 jit_solution(2726829725794260394)
XLA Ops:
  0.6 0.0 copy-start.5
  0.6 0.0 copy-start.6
  0.7 0.6 %copy-done.5 = s32[256,1]{0,1:T(1,128)S(1)} copy-done((s32[256,1]{0,1:T(1,128)S(1)}, s32[256,1]{0,1:T(1,128)}, u32[]{:S(2)}) %copy-start.5) | copy-done | bytes 1048
  1.3 0.0 copy-done.6
  1.3 0.0 copy-done.7
  1.3 0.2 copy-done.4
  1.6 5.1 %collective-permute-start.1 = (bf16[272,256]{1,0:T(8,128)(2,1)S(1)}, bf16[272,256]{1,0:T(8,128)(2,1)S(1)}, u32[]{:S(2)}, u32[]{:S(2)}) collective-permute-start(bf16[272,256]{1,0:T(8,128)(2,1)S(1)} %pack.1.x_ref.refs_0_), channel_id=1, source_target_pairs={{0,12},{4,8},{8,4},{12,0},{1,13},{5,9},{9,5},{13,1},{2,14},{6,10},... | collective-permute-start | bytes 417800 | tf_op jit(solution)/shard_map/ppermute | solution.py:314
  6.7 0.0 copy-done
  6.7 1.4 %forward.3.a_ref = bf16[256,512]{1,0:T(8,128)(2,1)S(1)} custom-call(bf16[272,256]{1,0:T(8,128)(2,1)S(1)} %pack.1.x_ref.refs_0_, bf16[256,2048]{1,0:T(8,128)(2,1)S(1)} %copy-done, bf16[256,2048]{1,0:T(8,128)(2,1)S(1)} %copy-done.1, bf16[2048,256]{1,0:T(8,128)(2,1)S(1)} %copy-done.2, bf16[2048,256]{1,0:T(8,128)(2,1)S(1)} %copy-done.3), custom_call_target="tpu_custom_call" | custom-call | tf_op jit(solution)/shard_map/forward/pallas_call | solution.py:37
  8.1 1.6 %collective-permute-start = (bf16[256,512]{1,0:T(8,128)(2,1)S(1)}, bf16[256,512]{1,0:T(8,128)(2,1)S(1)}, u32[]{:S(2)}, u32[]{:S(2)}) collective-permute-start(bf16[256,512]{1,0:T(8,128)(2,1)S(1)} %forward.3.a_ref), channel_id=1, source_target_pairs={{0,2},{2,0},{1,3},{3,1},{4,6},{6,4},{5,7},{7,5},{8,10},{10,8},{9,1... | collective-permute-start | bytes 786440 | tf_op jit(solution)/shard_map/ppermute | solution.py:317
  9.7 0.0 collective-permute-start.4
  9.7 0.8 %collective-permute-done.1.x_ref.refs_3_ = bf16[272,256]{1,0:T(8,128)(2,1)S(1)} collective-permute-done((bf16[272,256]{1,0:T(8,128)(2,1)S(1)}, bf16[272,256]{1,0:T(8,128)(2,1)S(1)}, u32[]{:S(2)}, u32[]{:S(2)}) %collective-permute-start.1) | collective-permute-done | bytes 139296 | tf_op jit(solution)/shard_map/ppermute | solution.py:314
  10.5 3.6 %collective-permute-start.2 = (bf16[272,256]{1,0:T(8,128)(2,1)S(1)}, bf16[272,256]{1,0:T(8,128)(2,1)S(1)}, u32[]{:S(2)}, u32[]{:S(2)}) collective-permute-start(bf16[272,256]{1,0:T(8,128)(2,1)S(1)} %pack.1.x_ref.refs_0_), channel_id=1, source_target_pairs={{0,8},{4,12},{8,0},{12,4},{1,9},{5,13},{9,1},{13,5},{2,10},{6,14},... | collective-permute-start | bytes 417800 | tf_op jit(solution)/shard_map/ppermute | solution.py:314
  14.1 0.0 collective-permute-start.5
  14.1 0.5 collective-permute-start.8
  14.6 1.4 %forward.5.a_ref = bf16[256,512]{1,0:T(8,128)(2,1)S(1)} custom-call(bf16[272,256]{1,0:T(8,128)(2,1)S(1)} %collective-permute-done.1.x_ref.refs_3_, bf16[256,2048]{1,0:T(8,128)(2,1)S(1)} %copy-done, bf16[256,2048]{1,0:T(8,128)(2,1)S(1)} %copy-done.1, bf16[2048,256]{1,0:T(8,128)(2,1)S(1)} %copy-done.2, bf16[2048,256]{1,0:T(8,128)(2,1)S(1)} %copy-done.3), custom_call_target="tpu_custom_call" | custom-call | tf_op jit(solution)/shard_map/forward/pallas_call | solution.py:37
  16.0 0.0 collective-permute-done.b_ref
  16.0 1.6 %collective-permute-start.6 = (bf16[256,512]{1,0:T(8,128)(2,1)S(1)}, bf16[256,512]{1,0:T(8,128)(2,1)S(1)}, u32[]{:S(2)}, u32[]{:S(2)}) collective-permute-start(bf16[256,512]{1,0:T(8,128)(2,1)S(1)} %forward.5.a_ref), channel_id=1, source_target_pairs={{0,2},{2,0},{1,3},{3,1},{4,6},{6,4},{5,7},{7,5},{8,10},{10,8},{9,1... | collective-permute-start | bytes 786440 | tf_op jit(solution)/shard_map/ppermute | solution.py:317
  17.6 0.1 both.2.refs_0_
  17.6 0.0 collective-permute-done.4.refs_4_
  17.6 1.7 %collective-permute-done.2.x_ref.refs_2_ = bf16[272,256]{1,0:T(8,128)(2,1)S(1)} collective-permute-done((bf16[272,256]{1,0:T(8,128)(2,1)S(1)}, bf16[272,256]{1,0:T(8,128)(2,1)S(1)}, u32[]{:S(2)}, u32[]{:S(2)}) %collective-permute-start.2) | collective-permute-done | bytes 139296 | tf_op jit(solution)/shard_map/ppermute | solution.py:314
  19.3 0.0 collective-permute-done.5.refs_7_
  19.3 1.4 %forward.4.refs_2_ = bf16[256,512]{1,0:T(8,128)(2,1)S(1)} custom-call(bf16[272,256]{1,0:T(8,128)(2,1)S(1)} %collective-permute-done.2.x_ref.refs_2_, bf16[256,2048]{1,0:T(8,128)(2,1)S(1)} %copy-done, bf16[256,2048]{1,0:T(8,128)(2,1)S(1)} %copy-done.1, bf16[2048,256]{1,0:T(8,128)(2,1)S(1)} %copy-done.2, bf16[2048,256]{1,0:T(8,128)(2,1)S(1)} %copy-done.3), custom_call_target="tpu_custom_call" | custom-call | tf_op jit(solution)/shard_map/forward/pallas_call | solution.py:37
  20.7 1.5 %collective-permute-start.7 = (bf16[256,512]{1,0:T(8,128)(2,1)S(1)}, bf16[256,512]{1,0:T(8,128)(2,1)S(1)}, u32[]{:S(2)}, u32[]{:S(2)}) collective-permute-start(bf16[256,512]{1,0:T(8,128)(2,1)S(1)} %forward.4.refs_2_), channel_id=1, source_target_pairs={{0,2},{2,0},{1,3},{3,1},{4,6},{6,4},{5,7},{7,5},{8,10},{10,8},{9,1... | collective-permute-start | bytes 786440 | tf_op jit(solution)/shard_map/ppermute | solution.py:317
  22.3 1.0 %collective-permute-start.3 = (bf16[256,512]{1,0:T(8,128)(2,1)S(1)}, bf16[256,512]{1,0:T(8,128)(2,1)S(1)}, u32[]{:S(2)}, u32[]{:S(2)}) collective-permute-start(bf16[256,512]{1,0:T(8,128)(2,1)S(1)} %both.2.refs_0_), channel_id=1, source_target_pairs={{0,4},{4,0},{8,12},{12,8},{1,5},{5,1},{9,13},{13,9},{2,6},{6,2},{1... | collective-permute-start | bytes 786440 | tf_op jit(solution)/shard_map/ppermute | solution.py:314
  23.3 0.0 collective-permute-done.8.refs_1_
  23.3 0.0 collective-permute-start.9
  23.3 0.5 %collective-permute-start.10 = (bf16[272,256]{1,0:T(8,128)(2,1)S(1)}, bf16[272,256]{1,0:T(8,128)(2,1)S(1)}, u32[]{:S(2)}, u32[]{:S(2)}) collective-permute-start(bf16[272,256]{1,0:T(8,128)(2,1)S(1)} %collective-permute-done.2.x_ref.refs_2_), channel_id=1, source_target_pairs={{0,1},{1,0},{2,3},{3,2},{4,5},{5,4},{6,7},{7,6},{8,9},{9,8},{10,11... | collective-permute-start | bytes 417800 | tf_op jit(solution)/shard_map/ppermute | solution.py:317
  23.8 1.4 %collective-permute-done.6.b_ref = bf16[256,512]{1,0:T(8,128)(2,1)S(1)} collective-permute-done((bf16[256,512]{1,0:T(8,128)(2,1)S(1)}, bf16[256,512]{1,0:T(8,128)(2,1)S(1)}, u32[]{:S(2)}, u32[]{:S(2)}) %collective-permute-start.6) | collective-permute-done | bytes 262176 | tf_op jit(solution)/shard_map/ppermute | solution.py:317
  25.2 0.0 collective-permute-start.11
  25.2 0.1 both.3.refs_3_
  25.3 0.0 collective-permute-done.9.refs_5_
  25.3 0.6 %collective-permute-start.13 = (bf16[256,512]{1,0:T(8,128)(2,1)S(1)}, bf16[256,512]{1,0:T(8,128)(2,1)S(1)}, u32[]{:S(2)}, u32[]{:S(2)}) collective-permute-start(bf16[256,512]{1,0:T(8,128)(2,1)S(1)} %forward.4.refs_2_), channel_id=1, source_target_pairs={{0,1},{1,0},{2,3},{3,2},{4,5},{5,4},{6,7},{7,6},{8,9},{9,8},{10,11... | collective-permute-start | bytes 786440 | tf_op jit(solution)/shard_map/ppermute | solution.py:317
  25.9 0.0 collective-permute-done.10.refs_6_
  25.9 0.1 collective-permute-start.12
  26.0 5.0 %arrange.1 = (bf16[1024,256]{1,0:T(8,128)(2,1)S(1)}, bf16[1024,256]{1,0:T(8,128)(2,1)S(1)}, bf16[1024,256]{1,0:T(8,128)(2,1)S(1)}, bf16[1024,2048]{1,0:T(8,128)(...) custom-call(bf16[272,256]{1,0:T(8,128)(2,1)S(1)} %pack.1.x_ref.refs_, ...), custom_call_target="tpu_custom_call" | custom-call | tf_op jit(solution)/shard_map/arrange/pallas_call | solution.py:37
  31.0 0.0 collective-permute-done.7.refs_4_
  31.0 0.5 collective-permute-start.14
  31.5 0.0 collective-permute-done.3.refs_1_
  31.5 0.1 collective-permute-start.15
  31.6 0.0 collective-permute-done.11.refs_5_
  31.6 0.0 collective-permute-done.12.refs_6_
  31.6 1.0 %gather.1 = (bf16[1024,256]{1,0:T(8,128)(2,1)S(1)}, f32[1024,256]{1,0:T(8,128)S(1)}) custom-call(bf16[256,512]{1,0:T(8,128)(2,1)S(1)} %both.2.refs_0_, bf16[256,512]{1,0:T(8,128)(2,1)S(1)} %collective-permute-done.3.refs_1_, bf16[256,512]{1,0:T(8,128)(2,1)S(1)} %forward.4.refs_2_, bf16[256,512]{1,0:T(8,128)(2,1)S(1)} %both.3.refs_3_, ...), custom_call_target="tpu_custom_call" | custom-call | tf_op jit(solution)/shard_map/gather/pallas_call | solution.py:37
  32.6 0.0 collective-permute-done.13.part_ref
  32.6 0.0 collective-permute-done.14.there_ref
  32.6 0.4 collective-permute-done.15.sums_ref
  33.0 2.4 %contrast.1.refs_2_ = bf16[1024,512]{1,0:T(8,128)(2,1)S(1)} custom-call(bf16[1024,256]{1,0:T(8,128)(2,1)S(1)} %get-tuple-element.46.phi_ref, f32[1024,256]{1,0:T(8,128)S(1)} %get-tuple-element.47.psi_ref, bf16[256,512]{1,0:T(8,128)(2,1)S(1)} %collective-permute-done.13.part_ref, bf16[256,512]{1,0:T(8,128)(2,1)S(1)} %collective-permute-done.14.there_ref, ...), custom_call_target="tpu_custom_call" | custom-call | tf_op jit(solution)/shard_map/contrast/pallas_call | solution.py:37
  35.4 0.4 collective-permute-start.16
  35.8 0.1 collective-permute-start.19
  36.0 3.5 %mine.1 = (f32[1024,256]{1,0:T(8,128)S(1)}, f32[1024,256]{1,0:T(8,128)S(1)}, f32[1024,256]{1,0:T(8,128)S(1)}, f32[1024,256]{1,0:T(8,128)S(1)}) custom-call(bf16[2048,256]{1,0:T(8,128)(2,1)S(1)} %copy-done.2, bf16[2048,256]{1,0:T(8,128)(2,1)S(1)} %copy-done.3, bf16[1024,512]{1,0:T(8,128)(2,1)S(1)} %contrast.1.refs_2_, ...), custom_call_target="tpu_custom_call" | custom-call | flops 4294967296 | tf_op jit(solution)/shard_map/mine/pallas_call | solution.py:37
  39.5 0.0 collective-permute-done.16.refs_2_
  39.5 2.7 %other_state.1 = (bf16[256,1024]{1,0:T(8,128)(2,1)S(1)}, bf16[1024,256]{1,0:T(8,128)(2,1)S(1)}, f32[256,1024]{1,0:T(8,128)S(1)}, f32[1024,256]{1,0:T(8,128)S(1)}) custom-call(bf16[256,2048]{1,0:T(8,128)(2,1)S(1)} %copy-done, bf16[2048,256]{1,0:T(8,128)(2,1)S(1)} %copy-done.2, bf16[1024,512]{1,0:T(8,128)(2,1)S(1)} %collective-permute-done.16.refs_2_, ...), custom_call_target="tpu_custom_call" | custom-call | flops 2147483648 | tf_op jit(solution)/shard_map/other_state/pallas_call | solution.py:37
  42.2 0.4 collective-permute-start.17
  42.7 0.1 collective-permute-start.18
  42.8 0.0 collective-permute-done.19.refs_3_
  42.8 3.0 %other_goal.1 = (bf16[256,1024]{1,0:T(8,128)(2,1)S(1)}, bf16[1024,256]{1,0:T(8,128)(2,1)S(1)}, f32[256,1024]{1,0:T(8,128)S(1)}, f32[1024,256]{1,0:T(8,128)S(1)},...) custom-call(bf16[256,2048]{1,0:T(8,128)(2,1)S(1)} %copy-done.1, bf16[2048,256]{1,0:T(8,128)(2,1)S(1)} %copy-done.3, ...), custom_call_target="tpu_custom_call" | custom-call | flops 2147483648 | tf_op jit(solution)/shard_map/other_goal/pallas_call | solution.py:37
  45.8 0.4 collective-permute-start.20
  46.2 0.1 collective-permute-start.21
  46.3 0.0 collective-permute-done.17.refs_0_
  46.4 0.0 collective-permute-done.18.refs_1_
  46.4 2.0 %finish.2 = (f32[256,2048]{1,0:T(8,128)}, f32[2048,256]{1,0:T(8,128)}, f32[256,2048]{1,0:T(8,128)}, f32[2048,256]{1,0:T(8,128)}) custom-call(bf16[256,1024]{1,0:T(8,128)(2,1)S(1)} %collective-permute-done.17.refs_0_, bf16[1024,256]{1,0:T(8,128)(2,1)S(1)} %collective-permute-done.18.refs_1_, ...), custom_call_target="tpu_custom_call", output_to_operand_aliasing={{0}: (4, {}), {1}: (5, {})} | custom-call | tf_op jit(solution)/shard_map/finish/pallas_call | solution.py:37
  48.4 0.0 collective-permute-done.20.refs_0_
  48.4 0.1 collective-permute-done.21.refs_1_
  48.5 1.4 %finish.3 = (f32[256,2048]{1,0:T(8,128)}, f32[2048,256]{1,0:T(8,128)}) custom-call(bf16[256,1024]{1,0:T(8,128)(2,1)S(1)} %collective-permute-done.20.refs_0_, bf16[1024,256]{1,0:T(8,128)(2,1)S(1)} %collective-permute-done.21.refs_1_, f32[256,2048]{1,0:T(8,128)} %get-tuple-element.72.refs_2_, ...), custom_call_target="tpu_custom_call", output_to_operand_aliasing={{0}: (2, {}), {1}: (3, {})} | custom-call | tf_op jit(solution)/shard_map/finish/pallas_call | solution.py:37
  (11 shorter events, 0.0 us)
Async XLA Ops:
  0.6 0.7 %copy-start.5 = (s32[256,1]{0,1:T(1,128)S(1)}, s32[256,1]{0,1:T(1,128)}, u32[]{:S(2)}) copy-start(s32[256,1]{0,1:T(1,128)} %param.9) | copy-start | bytes 3076
  0.6 0.7 %copy-start.6 = (s32[256]{0:T(256)S(1)}, s32[256]{0:T(256)}, u32[]{:S(2)}) copy-start(s32[256]{0:T(256)} %param.10) | copy-start | bytes 3076
  0.7 0.7 %copy-start.7 = (s32[256]{0:T(256)S(1)}, s32[256]{0:T(256)}, u32[]{:S(2)}) copy-start(s32[256]{0:T(256)} %param.11) | copy-start | bytes 3076
  0.7 0.9 %copy-start.4 = (bf16[256,256]{1,0:T(8,128)(2,1)S(1)}, bf16[256,256]{1,0:T(8,128)(2,1)}, u32[]{:S(2)}) copy-start(bf16[256,256]{1,0:T(8,128)(2,1)} %refs_1_.7) | copy-start | bytes 393220
  1.6 5.2 %copy-start = (bf16[256,2048]{1,0:T(8,128)(2,1)S(1)}, bf16[256,2048]{1,0:T(8,128)(2,1)}, u32[]{:S(2)}) copy-start(bf16[256,2048]{1,0:T(8,128)(2,1)} %refs_0_.10) | copy-start | bytes 3145732
  1.6 5.2 %copy-start.1 = (bf16[256,2048]{1,0:T(8,128)(2,1)S(1)}, bf16[256,2048]{1,0:T(8,128)(2,1)}, u32[]{:S(2)}) copy-start(bf16[256,2048]{1,0:T(8,128)(2,1)} %refs_0_.11) | copy-start | bytes 3145732
  1.6 5.2 %copy-start.2 = (bf16[2048,256]{1,0:T(8,128)(2,1)S(1)}, bf16[2048,256]{1,0:T(8,128)(2,1)}, u32[]{:S(2)}) copy-start(bf16[2048,256]{1,0:T(8,128)(2,1)} %refs_1_.12) | copy-start | bytes 3145732
  1.6 5.2 %copy-start.3 = (bf16[2048,256]{1,0:T(8,128)(2,1)S(1)}, bf16[2048,256]{1,0:T(8,128)(2,1)}, u32[]{:S(2)}) copy-start(bf16[2048,256]{1,0:T(8,128)(2,1)} %refs_1_.13) | copy-start | bytes 3145732
  1.6 8.9 %collective-permute-start.1 = (bf16[272,256]{1,0:T(8,128)(2,1)S(1)}, bf16[272,256]{1,0:T(8,128)(2,1)S(1)}, u32[]{:S(2)}, u32[]{:S(2)}) collective-permute-start(bf16[272,256]{1,0:T(8,128)(2,1)S(1)} %pack.1.x_ref.refs_0_), channel_id=1, source_target_pairs={{0,12},{4,8},{8,4},{12,0},{1,13},{5,9},{9,5},{13,1},{2,14},{6,10},... | collective-permute-start | bytes 417800 | tf_op jit(solution)/shard_map/ppermute | solution.py:314
  8.1 7.9 %collective-permute-start = (bf16[256,512]{1,0:T(8,128)(2,1)S(1)}, bf16[256,512]{1,0:T(8,128)(2,1)S(1)}, u32[]{:S(2)}, u32[]{:S(2)}) collective-permute-start(bf16[256,512]{1,0:T(8,128)(2,1)S(1)} %forward.3.a_ref), channel_id=1, source_target_pairs={{0,2},{2,0},{1,3},{3,1},{4,6},{6,4},{5,7},{7,5},{8,10},{10,8},{9,1... | collective-permute-start | bytes 786440 | tf_op jit(solution)/shard_map/ppermute | solution.py:317
  9.7 7.9 %collective-permute-start.4 = (bf16[272,256]{1,0:T(8,128)(2,1)S(1)}, bf16[272,256]{1,0:T(8,128)(2,1)S(1)}, u32[]{:S(2)}, u32[]{:S(2)}) collective-permute-start(bf16[272,256]{1,0:T(8,128)(2,1)S(1)} %pack.1.x_ref.refs_0_), channel_id=1, source_target_pairs={{0,1},{1,0},{2,3},{3,2},{4,5},{5,4},{6,7},{7,6},{8,9},{9,8},{10,11... | collective-permute-start | bytes 417800 | tf_op jit(solution)/shard_map/ppermute | solution.py:317
  10.5 8.8 %collective-permute-start.2 = (bf16[272,256]{1,0:T(8,128)(2,1)S(1)}, bf16[272,256]{1,0:T(8,128)(2,1)S(1)}, u32[]{:S(2)}, u32[]{:S(2)}) collective-permute-start(bf16[272,256]{1,0:T(8,128)(2,1)S(1)} %pack.1.x_ref.refs_0_), channel_id=1, source_target_pairs={{0,8},{4,12},{8,0},{12,4},{1,9},{5,13},{9,1},{13,5},{2,10},{6,14},... | collective-permute-start | bytes 417800 | tf_op jit(solution)/shard_map/ppermute | solution.py:314
  14.1 5.2 %collective-permute-start.5 = (bf16[272,256]{1,0:T(8,128)(2,1)S(1)}, bf16[272,256]{1,0:T(8,128)(2,1)S(1)}, u32[]{:S(2)}, u32[]{:S(2)}) collective-permute-start(bf16[272,256]{1,0:T(8,128)(2,1)S(1)} %collective-permute-done.1.x_ref.refs_3_), channel_id=1, source_target_pairs={{0,1},{1,0},{2,3},{3,2},{4,5},{5,4},{6,7},{7,6},{8,9},{9,8},{10,11... | collective-permute-start | bytes 417800 | tf_op jit(solution)/shard_map/ppermute | solution.py:317
  14.1 9.2 %collective-permute-start.8 = (bf16[272,256]{1,0:T(8,128)(2,1)S(1)}, bf16[272,256]{1,0:T(8,128)(2,1)S(1)}, u32[]{:S(2)}, u32[]{:S(2)}) collective-permute-start(bf16[272,256]{1,0:T(8,128)(2,1)S(1)} %pack.1.x_ref.refs_0_), channel_id=1, source_target_pairs={{0,4},{4,0},{8,12},{12,8},{1,5},{5,1},{9,13},{13,9},{2,6},{6,2},{1... | collective-permute-start | bytes 417800 | tf_op jit(solution)/shard_map/ppermute | solution.py:314
  16.0 9.2 %collective-permute-start.6 = (bf16[256,512]{1,0:T(8,128)(2,1)S(1)}, bf16[256,512]{1,0:T(8,128)(2,1)S(1)}, u32[]{:S(2)}, u32[]{:S(2)}) collective-permute-start(bf16[256,512]{1,0:T(8,128)(2,1)S(1)} %forward.5.a_ref), channel_id=1, source_target_pairs={{0,2},{2,0},{1,3},{3,1},{4,6},{6,4},{5,7},{7,5},{8,10},{10,8},{9,1... | collective-permute-start | bytes 786440 | tf_op jit(solution)/shard_map/ppermute | solution.py:317
  20.7 10.3 %collective-permute-start.7 = (bf16[256,512]{1,0:T(8,128)(2,1)S(1)}, bf16[256,512]{1,0:T(8,128)(2,1)S(1)}, u32[]{:S(2)}, u32[]{:S(2)}) collective-permute-start(bf16[256,512]{1,0:T(8,128)(2,1)S(1)} %forward.4.refs_2_), channel_id=1, source_target_pairs={{0,2},{2,0},{1,3},{3,1},{4,6},{6,4},{5,7},{7,5},{8,10},{10,8},{9,1... | collective-permute-start | bytes 786440 | tf_op jit(solution)/shard_map/ppermute | solution.py:317
  22.3 9.2 %collective-permute-start.3 = (bf16[256,512]{1,0:T(8,128)(2,1)S(1)}, bf16[256,512]{1,0:T(8,128)(2,1)S(1)}, u32[]{:S(2)}, u32[]{:S(2)}) collective-permute-start(bf16[256,512]{1,0:T(8,128)(2,1)S(1)} %both.2.refs_0_), channel_id=1, source_target_pairs={{0,4},{4,0},{8,12},{12,8},{1,5},{5,1},{9,13},{13,9},{2,6},{6,2},{1... | collective-permute-start | bytes 786440 | tf_op jit(solution)/shard_map/ppermute | solution.py:314
  23.3 2.0 %collective-permute-start.9 = (bf16[272,256]{1,0:T(8,128)(2,1)S(1)}, bf16[272,256]{1,0:T(8,128)(2,1)S(1)}, u32[]{:S(2)}, u32[]{:S(2)}) collective-permute-start(bf16[272,256]{1,0:T(8,128)(2,1)S(1)} %collective-permute-done.8.refs_1_), channel_id=1, source_target_pairs={{0,1},{1,0},{2,3},{3,2},{4,5},{5,4},{6,7},{7,6},{8,9},{9,8},{10,11... | collective-permute-start | bytes 417800 | tf_op jit(solution)/shard_map/ppermute | solution.py:317
  23.3 2.5 %collective-permute-start.10 = (bf16[272,256]{1,0:T(8,128)(2,1)S(1)}, bf16[272,256]{1,0:T(8,128)(2,1)S(1)}, u32[]{:S(2)}, u32[]{:S(2)}) collective-permute-start(bf16[272,256]{1,0:T(8,128)(2,1)S(1)} %collective-permute-done.2.x_ref.refs_2_), channel_id=1, source_target_pairs={{0,1},{1,0},{2,3},{3,2},{4,5},{5,4},{6,7},{7,6},{8,9},{9,8},{10,11... | collective-permute-start | bytes 417800 | tf_op jit(solution)/shard_map/ppermute | solution.py:317
  25.2 6.4 %collective-permute-start.11 = (bf16[256,512]{1,0:T(8,128)(2,1)S(1)}, bf16[256,512]{1,0:T(8,128)(2,1)S(1)}, u32[]{:S(2)}, u32[]{:S(2)}) collective-permute-start(bf16[256,512]{1,0:T(8,128)(2,1)S(1)} %both.2.refs_0_), channel_id=1, source_target_pairs={{0,1},{1,0},{2,3},{3,2},{4,5},{5,4},{6,7},{7,6},{8,9},{9,8},{10,11... | collective-permute-start | bytes 786440 | tf_op jit(solution)/shard_map/ppermute | solution.py:317
  25.3 7.3 %collective-permute-start.13 = (bf16[256,512]{1,0:T(8,128)(2,1)S(1)}, bf16[256,512]{1,0:T(8,128)(2,1)S(1)}, u32[]{:S(2)}, u32[]{:S(2)}) collective-permute-start(bf16[256,512]{1,0:T(8,128)(2,1)S(1)} %forward.4.refs_2_), channel_id=1, source_target_pairs={{0,1},{1,0},{2,3},{3,2},{4,5},{5,4},{6,7},{7,6},{8,9},{9,8},{10,11... | collective-permute-start | bytes 786440 | tf_op jit(solution)/shard_map/ppermute | solution.py:317
  25.9 5.7 %collective-permute-start.12 = (bf16[256,512]{1,0:T(8,128)(2,1)S(1)}, bf16[256,512]{1,0:T(8,128)(2,1)S(1)}, u32[]{:S(2)}, u32[]{:S(2)}) collective-permute-start(bf16[256,512]{1,0:T(8,128)(2,1)S(1)} %both.3.refs_3_), channel_id=1, source_target_pairs={{0,1},{1,0},{2,3},{3,2},{4,5},{5,4},{6,7},{7,6},{8,9},{9,8},{10,11... | collective-permute-start | bytes 786440 | tf_op jit(solution)/shard_map/ppermute | solution.py:317
  31.0 1.7 %collective-permute-start.14 = (bf16[256,512]{1,0:T(8,128)(2,1)S(1)}, bf16[256,512]{1,0:T(8,128)(2,1)S(1)}, u32[]{:S(2)}, u32[]{:S(2)}) collective-permute-start(bf16[256,512]{1,0:T(8,128)(2,1)S(1)} %collective-permute-done.7.refs_4_), channel_id=1, source_target_pairs={{0,1},{1,0},{2,3},{3,2},{4,5},{5,4},{6,7},{7,6},{8,9},{9,8},{10,11... | collective-permute-start | bytes 786440 | tf_op jit(solution)/shard_map/ppermute | solution.py:317
  31.5 1.5 %collective-permute-start.15 = (bf16[256,512]{1,0:T(8,128)(2,1)S(1)}, bf16[256,512]{1,0:T(8,128)(2,1)S(1)}, u32[]{:S(2)}, u32[]{:S(2)}) collective-permute-start(bf16[256,512]{1,0:T(8,128)(2,1)S(1)} %collective-permute-done.3.refs_1_), channel_id=1, source_target_pairs={{0,1},{1,0},{2,3},{3,2},{4,5},{5,4},{6,7},{7,6},{8,9},{9,8},{10,11... | collective-permute-start | bytes 786440 | tf_op jit(solution)/shard_map/ppermute | solution.py:317
  35.4 4.1 %collective-permute-start.16 = (bf16[1024,512]{1,0:T(8,128)(2,1)S(1)}, bf16[1024,512]{1,0:T(8,128)(2,1)S(1)}, u32[]{:S(2)}, u32[]{:S(2)}) collective-permute-start(bf16[1024,512]{1,0:T(8,128)(2,1)S(1)} %contrast.1.refs_2_), channel_id=1, source_target_pairs={{0,1},{1,0},{2,3},{3,2},{4,5},{5,4},{6,7},{7,6},{8,9},{9,8},{10,11... | collective-permute-start | bytes 3145736 | tf_op jit(solution)/shard_map/ppermute | solution.py:317
  35.8 7.0 %collective-permute-start.19 = (bf16[1024,256]{1,0:T(8,128)(2,1)S(1)}, bf16[1024,256]{1,0:T(8,128)(2,1)S(1)}, u32[]{:S(2)}, u32[]{:S(2)}) collective-permute-start(bf16[1024,256]{1,0:T(8,128)(2,1)S(1)} %get-tuple-element.51.refs_4_), channel_id=1, source_target_pairs={{0,1},{1,0},{2,3},{3,2},{4,5},{5,4},{6,7},{7,6},{8,9},{9,8},{10,11... | collective-permute-start | bytes 1572872 | tf_op jit(solution)/shard_map/ppermute | solution.py:317
  42.2 4.1 %collective-permute-start.17 = (bf16[256,1024]{1,0:T(8,128)(2,1)S(1)}, bf16[256,1024]{1,0:T(8,128)(2,1)S(1)}, u32[]{:S(2)}, u32[]{:S(2)}) collective-permute-start(bf16[256,1024]{1,0:T(8,128)(2,1)S(1)} %get-tuple-element.58), channel_id=1, source_target_pairs={{0,1},{1,0},{2,3},{3,2},{4,5},{5,4},{6,7},{7,6},{8,9},{9,8},{10,11... | collective-permute-start | bytes 1572872 | tf_op jit(solution)/shard_map/ppermute | solution.py:317
  42.7 3.7 %collective-permute-start.18 = (bf16[1024,256]{1,0:T(8,128)(2,1)S(1)}, bf16[1024,256]{1,0:T(8,128)(2,1)S(1)}, u32[]{:S(2)}, u32[]{:S(2)}) collective-permute-start(bf16[1024,256]{1,0:T(8,128)(2,1)S(1)} %get-tuple-element.59), channel_id=1, source_target_pairs={{0,1},{1,0},{2,3},{3,2},{4,5},{5,4},{6,7},{7,6},{8,9},{9,8},{10,11... | collective-permute-start | bytes 1572872 | tf_op jit(solution)/shard_map/ppermute | solution.py:317
  45.8 2.6 %collective-permute-start.20 = (bf16[256,1024]{1,0:T(8,128)(2,1)S(1)}, bf16[256,1024]{1,0:T(8,128)(2,1)S(1)}, u32[]{:S(2)}, u32[]{:S(2)}) collective-permute-start(bf16[256,1024]{1,0:T(8,128)(2,1)S(1)} %get-tuple-element.70), channel_id=1, source_target_pairs={{0,1},{1,0},{2,3},{3,2},{4,5},{5,4},{6,7},{7,6},{8,9},{9,8},{10,11... | collective-permute-start | bytes 1572872 | tf_op jit(solution)/shard_map/ppermute | solution.py:317
  46.2 2.3 %collective-permute-start.21 = (bf16[1024,256]{1,0:T(8,128)(2,1)S(1)}, bf16[1024,256]{1,0:T(8,128)(2,1)S(1)}, u32[]{:S(2)}, u32[]{:S(2)}) collective-permute-start(bf16[1024,256]{1,0:T(8,128)(2,1)S(1)} %get-tuple-element.71), channel_id=1, source_target_pairs={{0,1},{1,0},{2,3},{3,2},{4,5},{5,4},{6,7},{7,6},{8,9},{9,8},{10,11... | collective-permute-start | bytes 1572872 | tf_op jit(solution)/shard_map/ppermute | solution.py:317

commit v17 on v16

--- a/solution.py
+++ b/solution.py
@@ -341,9 +341,7 @@
 
     sums = {0: both(part0, there0)}
     sums[1] = across(after(sums[0], got[2]), 1)
-    others = {k: swap(got[k], "sub") for k in (0, 3)}
-    part2 = forward(after(got[2], sums[0], others[0], others[3]), held, rows_dev)
-    others.update({k: swap(got[k], "sub") for k in (1, 2)})
+    part2 = forward(after(got[2], sums[0]), held, rows_dev)
     there2 = swap(part2, "rep")
     sums[3] = both(part3, there3)
 
@@ -354,7 +352,7 @@
         "arrange",
         [side, side, side, ((rows_all // 2, rows_all), BF), ((1, rows_all // 2), F32)]
         + [((quarter, rows_all // 2), BF)] * 4,
-        (*(got[k] for k in range(n_blk)), *(others[k] for k in range(n_blk)), sf, gf),
+        (*(got[k] for k in range(n_blk)), *(swap(got[k], "sub") for k in range(n_blk)), sf, gf),
         [
             pltpu.VMEM((rows_all, width), BF),
             pltpu.VMEM((16, rows_all // 2), F32),

time: 50.2 us -> 49.7 us (0.990)
    ppermute x18, waiting for transfers between devices: 1.89 us -> 1.2 us  [swap(): return lax.ppermute(x, axis, [(0, 1), (1, 0)])]
  transfers between devices with their start and end apart: 22 -> 22, of which waited for: 5 -> 6; matrix products, arithmetic and copies ran while one was open for 0% -> 0% of each run, Pallas kernels for 43% -> 43%
where the time goes in v17:
time: 49.7 us; the launch traced here: 49.5 us
  Pallas kernels  25.3 us (51%)
  starting transfers between devices  18.2 us (37%)
  waiting for transfers between devices  4.06 us (8%)
  between operations  0.99 us (2%)
  local copies, waits for them, and re-layouts  0.92 us (2%)
    pallas_call x15, Pallas kernels, kernel(): pl.pallas_call(body, in_specs=specs, out_specs=[HBM if i in hbm_out else...  25.3 us
    ppermute x4, starting transfers between devices, across(): return lax.ppermute(x, 'blk', [(i, i ^ k) for i in range(n_blk)])  10.3 us
    ppermute x18, starting transfers between devices, swap(): return lax.ppermute(x, axis, [(0, 1), (1, 0)])  7.87 us
    ppermute x4, waiting for transfers between devices, across(): return lax.ppermute(x, 'blk', [(i, i ^ k) for i in range(n_blk)])  2.86 us
    ppermute x18, waiting for transfers between devices, swap(): return lax.ppermute(x, axis, [(0, 1), (1, 0)])  1.2 us
  transfers between devices with their start and end apart: 22, of which 6 were waited for; matrix products, arithmetic and copies ran while one was open for 0% of the time, Pallas kernels for 43%

profile of v17, /device:TPU:0, one launch (start us, length us, event | category | flops | bytes accessed | tf_op | source)
XLA Modules:
  0.0 49.5 jit_solution(13731418951633770152)
XLA Ops:
  0.6 0.0 copy-start.5
  0.6 0.0 copy-start.6
  0.7 0.6 %copy-done.5 = s32[256,1]{0,1:T(1,128)S(1)} copy-done((s32[256,1]{0,1:T(1,128)S(1)}, s32[256,1]{0,1:T(1,128)}, u32[]{:S(2)}) %copy-start.5) | copy-done | bytes 1048
  1.3 0.0 copy-done.6
  1.3 0.0 copy-done.7
  1.3 0.2 copy-done.4
  1.6 5.1 %collective-permute-start.1 = (bf16[272,256]{1,0:T(8,128)(2,1)S(1)}, bf16[272,256]{1,0:T(8,128)(2,1)S(1)}, u32[]{:S(2)}, u32[]{:S(2)}) collective-permute-start(bf16[272,256]{1,0:T(8,128)(2,1)S(1)} %pack.1.x_ref.refs_0_), channel_id=1, source_target_pairs={{0,12},{4,8},{8,4},{12,0},{1,13},{5,9},{9,5},{13,1},{2,14},{6,10},... | collective-permute-start | bytes 417800 | tf_op jit(solution)/shard_map/ppermute | solution.py:314
  6.7 0.0 copy-done.2
  6.7 1.4 %forward.3.a_ref = bf16[256,512]{1,0:T(8,128)(2,1)S(1)} custom-call(bf16[272,256]{1,0:T(8,128)(2,1)S(1)} %pack.1.x_ref.refs_0_, bf16[256,2048]{1,0:T(8,128)(2,1)S(1)} %copy-done, bf16[256,2048]{1,0:T(8,128)(2,1)S(1)} %copy-done.1, bf16[2048,256]{1,0:T(8,128)(2,1)S(1)} %copy-done.2, bf16[2048,256]{1,0:T(8,128)(2,1)S(1)} %copy-done.3), custom_call_target="tpu_custom_call" | custom-call | tf_op jit(solution)/shard_map/forward/pallas_call | solution.py:37
  8.1 1.6 %collective-permute-start = (bf16[256,512]{1,0:T(8,128)(2,1)S(1)}, bf16[256,512]{1,0:T(8,128)(2,1)S(1)}, u32[]{:S(2)}, u32[]{:S(2)}) collective-permute-start(bf16[256,512]{1,0:T(8,128)(2,1)S(1)} %forward.3.a_ref), channel_id=1, source_target_pairs={{0,2},{2,0},{1,3},{3,1},{4,6},{6,4},{5,7},{7,5},{8,10},{10,8},{9,1... | collective-permute-start | bytes 786440 | tf_op jit(solution)/shard_map/ppermute | solution.py:317
  9.7 0.8 %collective-permute-done.1.x_ref.refs_3_ = bf16[272,256]{1,0:T(8,128)(2,1)S(1)} collective-permute-done((bf16[272,256]{1,0:T(8,128)(2,1)S(1)}, bf16[272,256]{1,0:T(8,128)(2,1)S(1)}, u32[]{:S(2)}, u32[]{:S(2)}) %collective-permute-start.1) | collective-permute-done | bytes 139296 | tf_op jit(solution)/shard_map/ppermute | solution.py:314
  10.5 3.6 %collective-permute-start.2 = (bf16[272,256]{1,0:T(8,128)(2,1)S(1)}, bf16[272,256]{1,0:T(8,128)(2,1)S(1)}, u32[]{:S(2)}, u32[]{:S(2)}) collective-permute-start(bf16[272,256]{1,0:T(8,128)(2,1)S(1)} %pack.1.x_ref.refs_0_), channel_id=1, source_target_pairs={{0,8},{4,12},{8,0},{12,4},{1,9},{5,13},{9,1},{13,5},{2,10},{6,14},... | collective-permute-start | bytes 417800 | tf_op jit(solution)/shard_map/ppermute | solution.py:314
  14.1 1.4 %forward.5.a_ref = bf16[256,512]{1,0:T(8,128)(2,1)S(1)} custom-call(bf16[272,256]{1,0:T(8,128)(2,1)S(1)} %collective-permute-done.1.x_ref.refs_3_, bf16[256,2048]{1,0:T(8,128)(2,1)S(1)} %copy-done, bf16[256,2048]{1,0:T(8,128)(2,1)S(1)} %copy-done.1, bf16[2048,256]{1,0:T(8,128)(2,1)S(1)} %copy-done.2, bf16[2048,256]{1,0:T(8,128)(2,1)S(1)} %copy-done.3), custom_call_target="tpu_custom_call" | custom-call | tf_op jit(solution)/shard_map/forward/pallas_call | solution.py:37
  15.5 1.6 %collective-permute-start.4 = (bf16[256,512]{1,0:T(8,128)(2,1)S(1)}, bf16[256,512]{1,0:T(8,128)(2,1)S(1)}, u32[]{:S(2)}, u32[]{:S(2)}) collective-permute-start(bf16[256,512]{1,0:T(8,128)(2,1)S(1)} %forward.5.a_ref), channel_id=1, source_target_pairs={{0,2},{2,0},{1,3},{3,1},{4,6},{6,4},{5,7},{7,5},{8,10},{10,8},{9,1... | collective-permute-start | bytes 786440 | tf_op jit(solution)/shard_map/ppermute | solution.py:317
  17.1 0.5 %collective-permute-start.6 = (bf16[272,256]{1,0:T(8,128)(2,1)S(1)}, bf16[272,256]{1,0:T(8,128)(2,1)S(1)}, u32[]{:S(2)}, u32[]{:S(2)}) collective-permute-start(bf16[272,256]{1,0:T(8,128)(2,1)S(1)} %pack.1.x_ref.refs_0_), channel_id=1, source_target_pairs={{0,4},{4,0},{8,12},{12,8},{1,5},{5,1},{9,13},{13,9},{2,6},{6,2},{1... | collective-permute-start | bytes 417800 | tf_op jit(solution)/shard_map/ppermute | solution.py:314
  17.6 0.0 collective-permute-start.7
  17.6 0.0 collective-permute-done.b_ref
  17.6 0.1 both.2.refs_0_
  17.6 2.0 %collective-permute-done.2.x_ref.refs_2_ = bf16[272,256]{1,0:T(8,128)(2,1)S(1)} collective-permute-done((bf16[272,256]{1,0:T(8,128)(2,1)S(1)}, bf16[272,256]{1,0:T(8,128)(2,1)S(1)}, u32[]{:S(2)}, u32[]{:S(2)}) %collective-permute-start.2) | collective-permute-done | bytes 139296 | tf_op jit(solution)/shard_map/ppermute | solution.py:314
  19.7 1.4 %forward.4.refs_2_ = bf16[256,512]{1,0:T(8,128)(2,1)S(1)} custom-call(bf16[272,256]{1,0:T(8,128)(2,1)S(1)} %collective-permute-done.2.x_ref.refs_2_, bf16[256,2048]{1,0:T(8,128)(2,1)S(1)} %copy-done, bf16[256,2048]{1,0:T(8,128)(2,1)S(1)} %copy-done.1, bf16[2048,256]{1,0:T(8,128)(2,1)S(1)} %copy-done.2, bf16[2048,256]{1,0:T(8,128)(2,1)S(1)} %copy-done.3), custom_call_target="tpu_custom_call" | custom-call | tf_op jit(solution)/shard_map/forward/pallas_call | solution.py:37
  21.0 1.2 %collective-permute-start.5 = (bf16[256,512]{1,0:T(8,128)(2,1)S(1)}, bf16[256,512]{1,0:T(8,128)(2,1)S(1)}, u32[]{:S(2)}, u32[]{:S(2)}) collective-permute-start(bf16[256,512]{1,0:T(8,128)(2,1)S(1)} %forward.4.refs_2_), channel_id=1, source_target_pairs={{0,2},{2,0},{1,3},{3,1},{4,6},{6,4},{5,7},{7,5},{8,10},{10,8},{9,1... | collective-permute-start | bytes 786440 | tf_op jit(solution)/shard_map/ppermute | solution.py:317
  22.3 1.1 %collective-permute-start.3 = (bf16[256,512]{1,0:T(8,128)(2,1)S(1)}, bf16[256,512]{1,0:T(8,128)(2,1)S(1)}, u32[]{:S(2)}, u32[]{:S(2)}) collective-permute-start(bf16[256,512]{1,0:T(8,128)(2,1)S(1)} %both.2.refs_0_), channel_id=1, source_target_pairs={{0,4},{4,0},{8,12},{12,8},{1,5},{5,1},{9,13},{13,9},{2,6},{6,2},{1... | collective-permute-start | bytes 786440 | tf_op jit(solution)/shard_map/ppermute | solution.py:314
  23.4 0.0 collective-permute-done.6.refs_1_
  23.4 0.0 collective-permute-start.8
  23.4 0.0 collective-permute-done.7.refs_4_
  23.4 0.5 %collective-permute-start.10 = (bf16[272,256]{1,0:T(8,128)(2,1)S(1)}, bf16[272,256]{1,0:T(8,128)(2,1)S(1)}, u32[]{:S(2)}, u32[]{:S(2)}) collective-permute-start(bf16[272,256]{1,0:T(8,128)(2,1)S(1)} %collective-permute-done.1.x_ref.refs_3_), channel_id=1, source_target_pairs={{0,1},{1,0},{2,3},{3,2},{4,5},{5,4},{6,7},{7,6},{8,9},{9,8},{10,11... | collective-permute-start | bytes 417800 | tf_op jit(solution)/shard_map/ppermute | solution.py:317
  23.9 0.0 collective-permute-done.4.b_ref
  23.9 0.1 collective-permute-start.9
  24.0 0.1 both.3.refs_3_
  24.0 0.7 %collective-permute-done.8.refs_5_ = bf16[272,256]{1,0:T(8,128)(2,1)S(1)} collective-permute-done((bf16[272,256]{1,0:T(8,128)(2,1)S(1)}, bf16[272,256]{1,0:T(8,128)(2,1)S(1)}, u32[]{:S(2)}, u32[]{:S(2)}) %collective-permute-start.8) | collective-permute-done | bytes 139296 | tf_op jit(solution)/shard_map/ppermute | solution.py:317
  24.7 0.1 collective-permute-start.11
  24.9 0.1 collective-permute-done.10.refs_7_
  24.9 0.3 collective-permute-start.13
  25.3 0.0 collective-permute-done.9.refs_6_
  25.3 0.2 collective-permute-start.12
  25.5 5.0 %arrange.1 = (bf16[1024,256]{1,0:T(8,128)(2,1)S(1)}, bf16[1024,256]{1,0:T(8,128)(2,1)S(1)}, bf16[1024,256]{1,0:T(8,128)(2,1)S(1)}, bf16[1024,2048]{1,0:T(8,128)(...) custom-call(bf16[272,256]{1,0:T(8,128)(2,1)S(1)} %pack.1.x_ref.refs_, ...), custom_call_target="tpu_custom_call" | custom-call | tf_op jit(solution)/shard_map/arrange/pallas_call | solution.py:37
  30.5 0.0 collective-permute-done.5.refs_4_
  30.5 0.4 collective-permute-start.14
  30.9 0.0 collective-permute-done.3.refs_1_
  30.9 0.2 collective-permute-start.15
  31.1 0.0 collective-permute-done.11.refs_5_
  31.1 0.0 collective-permute-done.12.refs_6_
  31.1 1.0 %gather.1 = (bf16[1024,256]{1,0:T(8,128)(2,1)S(1)}, f32[1024,256]{1,0:T(8,128)S(1)}) custom-call(bf16[256,512]{1,0:T(8,128)(2,1)S(1)} %both.2.refs_0_, bf16[256,512]{1,0:T(8,128)(2,1)S(1)} %collective-permute-done.3.refs_1_, bf16[256,512]{1,0:T(8,128)(2,1)S(1)} %forward.4.refs_2_, bf16[256,512]{1,0:T(8,128)(2,1)S(1)} %both.3.refs_3_, ...), custom_call_target="tpu_custom_call" | custom-call | tf_op jit(solution)/shard_map/gather/pallas_call | solution.py:37
  32.1 0.0 collective-permute-done.13.part_ref
  32.1 0.0 collective-permute-done.14.there_ref
  32.1 0.3 collective-permute-done.15.sums_ref
  32.5 2.4 %contrast.1.refs_2_ = bf16[1024,512]{1,0:T(8,128)(2,1)S(1)} custom-call(bf16[1024,256]{1,0:T(8,128)(2,1)S(1)} %get-tuple-element.46.phi_ref, f32[1024,256]{1,0:T(8,128)S(1)} %get-tuple-element.47.psi_ref, bf16[256,512]{1,0:T(8,128)(2,1)S(1)} %collective-permute-done.13.part_ref, bf16[256,512]{1,0:T(8,128)(2,1)S(1)} %collective-permute-done.14.there_ref, ...), custom_call_target="tpu_custom_call" | custom-call | tf_op jit(solution)/shard_map/contrast/pallas_call | solution.py:37
  34.8 0.4 collective-permute-start.16
  35.2 0.2 collective-permute-start.19
  35.4 3.5 %mine.1 = (f32[1024,256]{1,0:T(8,128)S(1)}, f32[1024,256]{1,0:T(8,128)S(1)}, f32[1024,256]{1,0:T(8,128)S(1)}, f32[1024,256]{1,0:T(8,128)S(1)}) custom-call(bf16[2048,256]{1,0:T(8,128)(2,1)S(1)} %copy-done.2, bf16[2048,256]{1,0:T(8,128)(2,1)S(1)} %copy-done.3, bf16[1024,512]{1,0:T(8,128)(2,1)S(1)} %contrast.1.refs_2_, ...), custom_call_target="tpu_custom_call" | custom-call | flops 4294967296 | tf_op jit(solution)/shard_map/mine/pallas_call | solution.py:37
  38.9 0.0 collective-permute-done.16.refs_2_
  38.9 2.7 %other_state.1 = (bf16[256,1024]{1,0:T(8,128)(2,1)S(1)}, bf16[1024,256]{1,0:T(8,128)(2,1)S(1)}, f32[256,1024]{1,0:T(8,128)S(1)}, f32[1024,256]{1,0:T(8,128)S(1)}) custom-call(bf16[256,2048]{1,0:T(8,128)(2,1)S(1)} %copy-done, bf16[2048,256]{1,0:T(8,128)(2,1)S(1)} %copy-done.2, bf16[1024,512]{1,0:T(8,128)(2,1)S(1)} %collective-permute-done.16.refs_2_, ...), custom_call_target="tpu_custom_call" | custom-call | flops 2147483648 | tf_op jit(solution)/shard_map/other_state/pallas_call | solution.py:37
  41.7 0.4 collective-permute-start.17
  42.0 0.2 collective-permute-start.18
  42.2 0.0 collective-permute-done.19.refs_3_
  42.2 3.0 %other_goal.1 = (bf16[256,1024]{1,0:T(8,128)(2,1)S(1)}, bf16[1024,256]{1,0:T(8,128)(2,1)S(1)}, f32[256,1024]{1,0:T(8,128)S(1)}, f32[1024,256]{1,0:T(8,128)S(1)},...) custom-call(bf16[256,2048]{1,0:T(8,128)(2,1)S(1)} %copy-done.1, bf16[2048,256]{1,0:T(8,128)(2,1)S(1)} %copy-done.3, ...), custom_call_target="tpu_custom_call" | custom-call | flops 2147483648 | tf_op jit(solution)/shard_map/other_goal/pallas_call | solution.py:37
  45.2 0.4 collective-permute-start.20
  45.6 0.2 collective-permute-start.21
  45.8 0.0 collective-permute-done.17.refs_0_
  45.8 0.0 collective-permute-done.18.refs_1_
  45.8 2.0 %finish.2 = (f32[256,2048]{1,0:T(8,128)}, f32[2048,256]{1,0:T(8,128)}, f32[256,2048]{1,0:T(8,128)}, f32[2048,256]{1,0:T(8,128)}) custom-call(bf16[256,1024]{1,0:T(8,128)(2,1)S(1)} %collective-permute-done.17.refs_0_, bf16[1024,256]{1,0:T(8,128)(2,1)S(1)} %collective-permute-done.18.refs_1_, ...), custom_call_target="tpu_custom_call", output_to_operand_aliasing={{0}: (4, {}), {1}: (5, {})} | custom-call | tf_op jit(solution)/shard_map/finish/pallas_call | solution.py:37
  47.9 0.0 collective-permute-done.20.refs_0_
  47.9 0.1 collective-permute-done.21.refs_1_
  47.9 1.4 %finish.3 = (f32[256,2048]{1,0:T(8,128)}, f32[2048,256]{1,0:T(8,128)}) custom-call(bf16[256,1024]{1,0:T(8,128)(2,1)S(1)} %collective-permute-done.20.refs_0_, bf16[1024,256]{1,0:T(8,128)(2,1)S(1)} %collective-permute-done.21.refs_1_, f32[256,2048]{1,0:T(8,128)} %get-tuple-element.72.refs_2_, ...), custom_call_target="tpu_custom_call", output_to_operand_aliasing={{0}: (2, {}), {1}: (3, {})} | custom-call | tf_op jit(solution)/shard_map/finish/pallas_call | solution.py:37
  (11 shorter events, 0.0 us)
Async XLA Ops:
  0.6 0.7 %copy-start.5 = (s32[256,1]{0,1:T(1,128)S(1)}, s32[256,1]{0,1:T(1,128)}, u32[]{:S(2)}) copy-start(s32[256,1]{0,1:T(1,128)} %param.9) | copy-start | bytes 3076
  0.6 0.7 %copy-start.6 = (s32[256]{0:T(256)S(1)}, s32[256]{0:T(256)}, u32[]{:S(2)}) copy-start(s32[256]{0:T(256)} %param.10) | copy-start | bytes 3076
  0.7 0.7 %copy-start.7 = (s32[256]{0:T(256)S(1)}, s32[256]{0:T(256)}, u32[]{:S(2)}) copy-start(s32[256]{0:T(256)} %param.11) | copy-start | bytes 3076
  0.7 0.9 %copy-start.4 = (bf16[256,256]{1,0:T(8,128)(2,1)S(1)}, bf16[256,256]{1,0:T(8,128)(2,1)}, u32[]{:S(2)}) copy-start(bf16[256,256]{1,0:T(8,128)(2,1)} %refs_1_.7) | copy-start | bytes 393220
  1.6 5.2 %copy-start = (bf16[256,2048]{1,0:T(8,128)(2,1)S(1)}, bf16[256,2048]{1,0:T(8,128)(2,1)}, u32[]{:S(2)}) copy-start(bf16[256,2048]{1,0:T(8,128)(2,1)} %refs_0_.10) | copy-start | bytes 3145732
  1.6 5.2 %copy-start.1 = (bf16[256,2048]{1,0:T(8,128)(2,1)S(1)}, bf16[256,2048]{1,0:T(8,128)(2,1)}, u32[]{:S(2)}) copy-start(bf16[256,2048]{1,0:T(8,128)(2,1)} %refs_0_.11) | copy-start | bytes 3145732
  1.6 5.2 %copy-start.2 = (bf16[2048,256]{1,0:T(8,128)(2,1)S(1)}, bf16[2048,256]{1,0:T(8,128)(2,1)}, u32[]{:S(2)}) copy-start(bf16[2048,256]{1,0:T(8,128)(2,1)} %refs_1_.12) | copy-start | bytes 3145732
  1.6 5.2 %copy-start.3 = (bf16[2048,256]{1,0:T(8,128)(2,1)S(1)}, bf16[2048,256]{1,0:T(8,128)(2,1)}, u32[]{:S(2)}) copy-start(bf16[2048,256]{1,0:T(8,128)(2,1)} %refs_1_.13) | copy-start | bytes 3145732
  1.6 8.9 %collective-permute-start.1 = (bf16[272,256]{1,0:T(8,128)(2,1)S(1)}, bf16[272,256]{1,0:T(8,128)(2,1)S(1)}, u32[]{:S(2)}, u32[]{:S(2)}) collective-permute-start(bf16[272,256]{1,0:T(8,128)(2,1)S(1)} %pack.1.x_ref.refs_0_), channel_id=1, source_target_pairs={{0,12},{4,8},{8,4},{12,0},{1,13},{5,9},{9,5},{13,1},{2,14},{6,10},... | collective-permute-start | bytes 417800 | tf_op jit(solution)/shard_map/ppermute | solution.py:314
  8.1 9.4 %collective-permute-start = (bf16[256,512]{1,0:T(8,128)(2,1)S(1)}, bf16[256,512]{1,0:T(8,128)(2,1)S(1)}, u32[]{:S(2)}, u32[]{:S(2)}) collective-permute-start(bf16[256,512]{1,0:T(8,128)(2,1)S(1)} %forward.3.a_ref), channel_id=1, source_target_pairs={{0,2},{2,0},{1,3},{3,1},{4,6},{6,4},{5,7},{7,5},{8,10},{10,8},{9,1... | collective-permute-start | bytes 786440 | tf_op jit(solution)/shard_map/ppermute | solution.py:317
  10.5 9.1 %collective-permute-start.2 = (bf16[272,256]{1,0:T(8,128)(2,1)S(1)}, bf16[272,256]{1,0:T(8,128)(2,1)S(1)}, u32[]{:S(2)}, u32[]{:S(2)}) collective-permute-start(bf16[272,256]{1,0:T(8,128)(2,1)S(1)} %pack.1.x_ref.refs_0_), channel_id=1, source_target_pairs={{0,8},{4,12},{8,0},{12,4},{1,9},{5,13},{9,1},{13,5},{2,10},{6,14},... | collective-permute-start | bytes 417800 | tf_op jit(solution)/shard_map/ppermute | solution.py:314
  15.5 8.4 %collective-permute-start.4 = (bf16[256,512]{1,0:T(8,128)(2,1)S(1)}, bf16[256,512]{1,0:T(8,128)(2,1)S(1)}, u32[]{:S(2)}, u32[]{:S(2)}) collective-permute-start(bf16[256,512]{1,0:T(8,128)(2,1)S(1)} %forward.5.a_ref), channel_id=1, source_target_pairs={{0,2},{2,0},{1,3},{3,1},{4,6},{6,4},{5,7},{7,5},{8,10},{10,8},{9,1... | collective-permute-start | bytes 786440 | tf_op jit(solution)/shard_map/ppermute | solution.py:317
  17.1 6.3 %collective-permute-start.6 = (bf16[272,256]{1,0:T(8,128)(2,1)S(1)}, bf16[272,256]{1,0:T(8,128)(2,1)S(1)}, u32[]{:S(2)}, u32[]{:S(2)}) collective-permute-start(bf16[272,256]{1,0:T(8,128)(2,1)S(1)} %pack.1.x_ref.refs_0_), channel_id=1, source_target_pairs={{0,4},{4,0},{8,12},{12,8},{1,5},{5,1},{9,13},{13,9},{2,6},{6,2},{1... | collective-permute-start | bytes 417800 | tf_op jit(solution)/shard_map/ppermute | solution.py:314
  17.6 5.8 %collective-permute-start.7 = (bf16[272,256]{1,0:T(8,128)(2,1)S(1)}, bf16[272,256]{1,0:T(8,128)(2,1)S(1)}, u32[]{:S(2)}, u32[]{:S(2)}) collective-permute-start(bf16[272,256]{1,0:T(8,128)(2,1)S(1)} %pack.1.x_ref.refs_0_), channel_id=1, source_target_pairs={{0,1},{1,0},{2,3},{3,2},{4,5},{5,4},{6,7},{7,6},{8,9},{9,8},{10,11... | collective-permute-start | bytes 417800 | tf_op jit(solution)/shard_map/ppermute | solution.py:317
  21.0 9.4 %collective-permute-start.5 = (bf16[256,512]{1,0:T(8,128)(2,1)S(1)}, bf16[256,512]{1,0:T(8,128)(2,1)S(1)}, u32[]{:S(2)}, u32[]{:S(2)}) collective-permute-start(bf16[256,512]{1,0:T(8,128)(2,1)S(1)} %forward.4.refs_2_), channel_id=1, source_target_pairs={{0,2},{2,0},{1,3},{3,1},{4,6},{6,4},{5,7},{7,5},{8,10},{10,8},{9,1... | collective-permute-start | bytes 786440 | tf_op jit(solution)/shard_map/ppermute | solution.py:317
  22.3 8.6 %collective-permute-start.3 = (bf16[256,512]{1,0:T(8,128)(2,1)S(1)}, bf16[256,512]{1,0:T(8,128)(2,1)S(1)}, u32[]{:S(2)}, u32[]{:S(2)}) collective-permute-start(bf16[256,512]{1,0:T(8,128)(2,1)S(1)} %both.2.refs_0_), channel_id=1, source_target_pairs={{0,4},{4,0},{8,12},{12,8},{1,5},{5,1},{9,13},{13,9},{2,6},{6,2},{1... | collective-permute-start | bytes 786440 | tf_op jit(solution)/shard_map/ppermute | solution.py:314
  23.4 1.4 %collective-permute-start.8 = (bf16[272,256]{1,0:T(8,128)(2,1)S(1)}, bf16[272,256]{1,0:T(8,128)(2,1)S(1)}, u32[]{:S(2)}, u32[]{:S(2)}) collective-permute-start(bf16[272,256]{1,0:T(8,128)(2,1)S(1)} %collective-permute-done.6.refs_1_), channel_id=1, source_target_pairs={{0,1},{1,0},{2,3},{3,2},{4,5},{5,4},{6,7},{7,6},{8,9},{9,8},{10,11... | collective-permute-start | bytes 417800 | tf_op jit(solution)/shard_map/ppermute | solution.py:317
  23.4 1.6 %collective-permute-start.10 = (bf16[272,256]{1,0:T(8,128)(2,1)S(1)}, bf16[272,256]{1,0:T(8,128)(2,1)S(1)}, u32[]{:S(2)}, u32[]{:S(2)}) collective-permute-start(bf16[272,256]{1,0:T(8,128)(2,1)S(1)} %collective-permute-done.1.x_ref.refs_3_), channel_id=1, source_target_pairs={{0,1},{1,0},{2,3},{3,2},{4,5},{5,4},{6,7},{7,6},{8,9},{9,8},{10,11... | collective-permute-start | bytes 417800 | tf_op jit(solution)/shard_map/ppermute | solution.py:317
  23.9 1.4 %collective-permute-start.9 = (bf16[272,256]{1,0:T(8,128)(2,1)S(1)}, bf16[272,256]{1,0:T(8,128)(2,1)S(1)}, u32[]{:S(2)}, u32[]{:S(2)}) collective-permute-start(bf16[272,256]{1,0:T(8,128)(2,1)S(1)} %collective-permute-done.2.x_ref.refs_2_), channel_id=1, source_target_pairs={{0,1},{1,0},{2,3},{3,2},{4,5},{5,4},{6,7},{7,6},{8,9},{9,8},{10,11... | collective-permute-start | bytes 417800 | tf_op jit(solution)/shard_map/ppermute | solution.py:317
  24.7 6.3 %collective-permute-start.11 = (bf16[256,512]{1,0:T(8,128)(2,1)S(1)}, bf16[256,512]{1,0:T(8,128)(2,1)S(1)}, u32[]{:S(2)}, u32[]{:S(2)}) collective-permute-start(bf16[256,512]{1,0:T(8,128)(2,1)S(1)} %both.2.refs_0_), channel_id=1, source_target_pairs={{0,1},{1,0},{2,3},{3,2},{4,5},{5,4},{6,7},{7,6},{8,9},{9,8},{10,11... | collective-permute-start | bytes 786440 | tf_op jit(solution)/shard_map/ppermute | solution.py:317
  24.9 7.2 %collective-permute-start.13 = (bf16[256,512]{1,0:T(8,128)(2,1)S(1)}, bf16[256,512]{1,0:T(8,128)(2,1)S(1)}, u32[]{:S(2)}, u32[]{:S(2)}) collective-permute-start(bf16[256,512]{1,0:T(8,128)(2,1)S(1)} %forward.4.refs_2_), channel_id=1, source_target_pairs={{0,1},{1,0},{2,3},{3,2},{4,5},{5,4},{6,7},{7,6},{8,9},{9,8},{10,11... | collective-permute-start | bytes 786440 | tf_op jit(solution)/shard_map/ppermute | solution.py:317
  25.3 5.8 %collective-permute-start.12 = (bf16[256,512]{1,0:T(8,128)(2,1)S(1)}, bf16[256,512]{1,0:T(8,128)(2,1)S(1)}, u32[]{:S(2)}, u32[]{:S(2)}) collective-permute-start(bf16[256,512]{1,0:T(8,128)(2,1)S(1)} %both.3.refs_3_), channel_id=1, source_target_pairs={{0,1},{1,0},{2,3},{3,2},{4,5},{5,4},{6,7},{7,6},{8,9},{9,8},{10,11... | collective-permute-start | bytes 786440 | tf_op jit(solution)/shard_map/ppermute | solution.py:317
  30.5 1.6 %collective-permute-start.14 = (bf16[256,512]{1,0:T(8,128)(2,1)S(1)}, bf16[256,512]{1,0:T(8,128)(2,1)S(1)}, u32[]{:S(2)}, u32[]{:S(2)}) collective-permute-start(bf16[256,512]{1,0:T(8,128)(2,1)S(1)} %collective-permute-done.5.refs_4_), channel_id=1, source_target_pairs={{0,1},{1,0},{2,3},{3,2},{4,5},{5,4},{6,7},{7,6},{8,9},{9,8},{10,11... | collective-permute-start | bytes 786440 | tf_op jit(solution)/shard_map/ppermute | solution.py:317
  30.9 1.6 %collective-permute-start.15 = (bf16[256,512]{1,0:T(8,128)(2,1)S(1)}, bf16[256,512]{1,0:T(8,128)(2,1)S(1)}, u32[]{:S(2)}, u32[]{:S(2)}) collective-permute-start(bf16[256,512]{1,0:T(8,128)(2,1)S(1)} %collective-permute-done.3.refs_1_), channel_id=1, source_target_pairs={{0,1},{1,0},{2,3},{3,2},{4,5},{5,4},{6,7},{7,6},{8,9},{9,8},{10,11... | collective-permute-start | bytes 786440 | tf_op jit(solution)/shard_map/ppermute | solution.py:317
  34.8 4.1 %collective-permute-start.16 = (bf16[1024,512]{1,0:T(8,128)(2,1)S(1)}, bf16[1024,512]{1,0:T(8,128)(2,1)S(1)}, u32[]{:S(2)}, u32[]{:S(2)}) collective-permute-start(bf16[1024,512]{1,0:T(8,128)(2,1)S(1)} %contrast.1.refs_2_), channel_id=1, source_target_pairs={{0,1},{1,0},{2,3},{3,2},{4,5},{5,4},{6,7},{7,6},{8,9},{9,8},{10,11... | collective-permute-start | bytes 3145736 | tf_op jit(solution)/shard_map/ppermute | solution.py:317
  35.2 7.0 %collective-permute-start.19 = (bf16[1024,256]{1,0:T(8,128)(2,1)S(1)}, bf16[1024,256]{1,0:T(8,128)(2,1)S(1)}, u32[]{:S(2)}, u32[]{:S(2)}) collective-permute-start(bf16[1024,256]{1,0:T(8,128)(2,1)S(1)} %get-tuple-element.51.refs_4_), channel_id=1, source_target_pairs={{0,1},{1,0},{2,3},{3,2},{4,5},{5,4},{6,7},{7,6},{8,9},{9,8},{10,11... | collective-permute-start | bytes 1572872 | tf_op jit(solution)/shard_map/ppermute | solution.py:317
  41.7 4.1 %collective-permute-start.17 = (bf16[256,1024]{1,0:T(8,128)(2,1)S(1)}, bf16[256,1024]{1,0:T(8,128)(2,1)S(1)}, u32[]{:S(2)}, u32[]{:S(2)}) collective-permute-start(bf16[256,1024]{1,0:T(8,128)(2,1)S(1)} %get-tuple-element.58), channel_id=1, source_target_pairs={{0,1},{1,0},{2,3},{3,2},{4,5},{5,4},{6,7},{7,6},{8,9},{9,8},{10,11... | collective-permute-start | bytes 1572872 | tf_op jit(solution)/shard_map/ppermute | solution.py:317
  42.0 3.8 %collective-permute-start.18 = (bf16[1024,256]{1,0:T(8,128)(2,1)S(1)}, bf16[1024,256]{1,0:T(8,128)(2,1)S(1)}, u32[]{:S(2)}, u32[]{:S(2)}) collective-permute-start(bf16[1024,256]{1,0:T(8,128)(2,1)S(1)} %get-tuple-element.59), channel_id=1, source_target_pairs={{0,1},{1,0},{2,3},{3,2},{4,5},{5,4},{6,7},{7,6},{8,9},{9,8},{10,11... | collective-permute-start | bytes 1572872 | tf_op jit(solution)/shard_map/ppermute | solution.py:317
  45.2 2.6 %collective-permute-start.20 = (bf16[256,1024]{1,0:T(8,128)(2,1)S(1)}, bf16[256,1024]{1,0:T(8,128)(2,1)S(1)}, u32[]{:S(2)}, u32[]{:S(2)}) collective-permute-start(bf16[256,1024]{1,0:T(8,128)(2,1)S(1)} %get-tuple-element.70), channel_id=1, source_target_pairs={{0,1},{1,0},{2,3},{3,2},{4,5},{5,4},{6,7},{7,6},{8,9},{9,8},{10,11... | collective-permute-start | bytes 1572872 | tf_op jit(solution)/shard_map/ppermute | solution.py:317
  45.6 2.3 %collective-permute-start.21 = (bf16[1024,256]{1,0:T(8,128)(2,1)S(1)}, bf16[1024,256]{1,0:T(8,128)(2,1)S(1)}, u32[]{:S(2)}, u32[]{:S(2)}) collective-permute-start(bf16[1024,256]{1,0:T(8,128)(2,1)S(1)} %get-tuple-element.71), channel_id=1, source_target_pairs={{0,1},{1,0},{2,3},{3,2},{4,5},{5,4},{6,7},{7,6},{8,9},{9,8},{10,11... | collective-permute-start | bytes 1572872 | tf_op jit(solution)/shard_map/ppermute | solution.py:317

commit v18 on v17

--- a/solution.py
+++ b/solution.py
@@ -176,20 +176,24 @@
     diagonal = lax.broadcasted_iota(jnp.int32, (batch, batch), 0) == lax.broadcasted_iota(
         jnp.int32, (batch, batch), 1
     )
-    for r in range(n_rep):
-        own = slice(r * batch, (r + 1) * batch)
+    batches = [slice(r * batch, (r + 1) * batch) for r in range(n_rep)]
+    scores = [
+        lax.dot_general(phi_ref[own, :], psi_all[own, :], (((1,), (1,)), ((), ())), preferred_element_type=F32)
+        for own in batches
+    ]
+    deltas = []
+    for own, score in zip(batches, scores):
         ep_row = ep_ref[:, own]
-        psi = psi_all[own, :]
-        phi = phi_ref[own, :]
-        scores = lax.dot_general(phi, psi, (((1,), (1,)), ((), ())), preferred_element_type=F32)
         kept = (column(ep_row) != ep_row) | diagonal
-        exponent = jnp.where(kept, jnp.exp(scores * scale), 0.0)
+        exponent = jnp.where(kept, jnp.exp(score * scale), 0.0)
         totals = jnp.sum(exponent, axis=1, keepdims=True)
         power = jnp.where(totals > 1.0, 2.0**-32, 1.0)
         shares = (exponent * power) * (1.0 / (totals * power))
-        delta = jnp.where(diagonal, shares - 1.0, shares).astype(BF)
-        grads_ref[own, :emb] = (dot(delta, psi) * scale).astype(BF)
-        grads_ref[own, emb:] = (dot(delta.T, phi) * scale).astype(BF)
+        deltas.append(jnp.where(diagonal, shares - 1.0, shares).astype(BF))
+    for own, delta in zip(batches, deltas):
+        grads_ref[own, :emb] = (dot(delta, psi_all[own, :]) * scale).astype(BF)
+    for own, delta in zip(batches, deltas):
+        grads_ref[own, emb:] = (dot(delta.T, phi_ref[own, :]) * scale).astype(BF)
 
 
 def rows_grads(at, first_ref, second_ref, grads_ref, k, rows_ref, active, back):

time: 49.7 us -> 49.5 us (level)
  transfers between devices with their start and end apart: 22 -> 22, of which waited for: 6 -> 6; matrix products, arithmetic and copies ran while one was open for 0% -> 0% of each run, Pallas kernels for 43% -> 44%
where the time goes in v18:
time: 49.5 us; the launch traced here: 49.3 us
  Pallas kernels  25.1 us (51%)
  starting transfers between devices  18.2 us (37%)
  waiting for transfers between devices  4.06 us (8%)
  between operations  0.99 us (2%)
  local copies, waits for them, and re-layouts  0.92 us (2%)
    pallas_call x15, Pallas kernels, kernel(): pl.pallas_call(body, in_specs=specs, out_specs=[HBM if i in hbm_out else...  25.1 us
    ppermute x4, starting transfers between devices, across(): return lax.ppermute(x, 'blk', [(i, i ^ k) for i in range(n_blk)])  10.3 us
    ppermute x18, starting transfers between devices, swap(): return lax.ppermute(x, axis, [(0, 1), (1, 0)])  7.87 us
    ppermute x4, waiting for transfers between devices, across(): return lax.ppermute(x, 'blk', [(i, i ^ k) for i in range(n_blk)])  2.86 us
    ppermute x18, waiting for transfers between devices, swap(): return lax.ppermute(x, axis, [(0, 1), (1, 0)])  1.2 us
  transfers between devices with their start and end apart: 22, of which 6 were waited for; matrix products, arithmetic and copies ran while one was open for 0% of the time, Pallas kernels for 44%

profile of v18, /device:TPU:0, one launch (start us, length us, event | category | flops | bytes accessed | tf_op | source)
XLA Modules:
  0.0 49.3 jit_solution(2663940702356224063)
XLA Ops:
  0.6 0.0 copy-start.5
  0.6 0.0 copy-start.6
  0.7 0.0 copy-start.7
  0.7 0.6 %copy-done.5 = s32[256,1]{0,1:T(1,128)S(1)} copy-done((s32[256,1]{0,1:T(1,128)S(1)}, s32[256,1]{0,1:T(1,128)}, u32[]{:S(2)}) %copy-start.5) | copy-done | bytes 1048
  1.3 0.0 copy-done.6
  1.3 0.0 copy-done.7
  1.3 0.2 copy-done.4
  1.6 5.1 %collective-permute-start.1 = (bf16[272,256]{1,0:T(8,128)(2,1)S(1)}, bf16[272,256]{1,0:T(8,128)(2,1)S(1)}, u32[]{:S(2)}, u32[]{:S(2)}) collective-permute-start(bf16[272,256]{1,0:T(8,128)(2,1)S(1)} %pack.1.x_ref.refs_0_), channel_id=1, source_target_pairs={{0,12},{4,8},{8,4},{12,0},{1,13},{5,9},{9,5},{13,1},{2,14},{6,10},... | collective-permute-start | bytes 417800 | tf_op jit(solution)/shard_map/ppermute | solution.py:318
  6.7 1.4 %forward.3.a_ref = bf16[256,512]{1,0:T(8,128)(2,1)S(1)} custom-call(bf16[272,256]{1,0:T(8,128)(2,1)S(1)} %pack.1.x_ref.refs_0_, bf16[256,2048]{1,0:T(8,128)(2,1)S(1)} %copy-done, bf16[256,2048]{1,0:T(8,128)(2,1)S(1)} %copy-done.1, bf16[2048,256]{1,0:T(8,128)(2,1)S(1)} %copy-done.2, bf16[2048,256]{1,0:T(8,128)(2,1)S(1)} %copy-done.3), custom_call_target="tpu_custom_call" | custom-call | tf_op jit(solution)/shard_map/forward/pallas_call | solution.py:37
  8.1 1.6 %collective-permute-start = (bf16[256,512]{1,0:T(8,128)(2,1)S(1)}, bf16[256,512]{1,0:T(8,128)(2,1)S(1)}, u32[]{:S(2)}, u32[]{:S(2)}) collective-permute-start(bf16[256,512]{1,0:T(8,128)(2,1)S(1)} %forward.3.a_ref), channel_id=1, source_target_pairs={{0,2},{2,0},{1,3},{3,1},{4,6},{6,4},{5,7},{7,5},{8,10},{10,8},{9,1... | collective-permute-start | bytes 786440 | tf_op jit(solution)/shard_map/ppermute | solution.py:321
  9.7 0.8 %collective-permute-done.1.x_ref.refs_3_ = bf16[272,256]{1,0:T(8,128)(2,1)S(1)} collective-permute-done((bf16[272,256]{1,0:T(8,128)(2,1)S(1)}, bf16[272,256]{1,0:T(8,128)(2,1)S(1)}, u32[]{:S(2)}, u32[]{:S(2)}) %collective-permute-start.1) | collective-permute-done | bytes 139296 | tf_op jit(solution)/shard_map/ppermute | solution.py:318
  10.5 3.6 %collective-permute-start.2 = (bf16[272,256]{1,0:T(8,128)(2,1)S(1)}, bf16[272,256]{1,0:T(8,128)(2,1)S(1)}, u32[]{:S(2)}, u32[]{:S(2)}) collective-permute-start(bf16[272,256]{1,0:T(8,128)(2,1)S(1)} %pack.1.x_ref.refs_0_), channel_id=1, source_target_pairs={{0,8},{4,12},{8,0},{12,4},{1,9},{5,13},{9,1},{13,5},{2,10},{6,14},... | collective-permute-start | bytes 417800 | tf_op jit(solution)/shard_map/ppermute | solution.py:318
  14.1 1.4 %forward.5.a_ref = bf16[256,512]{1,0:T(8,128)(2,1)S(1)} custom-call(bf16[272,256]{1,0:T(8,128)(2,1)S(1)} %collective-permute-done.1.x_ref.refs_3_, bf16[256,2048]{1,0:T(8,128)(2,1)S(1)} %copy-done, bf16[256,2048]{1,0:T(8,128)(2,1)S(1)} %copy-done.1, bf16[2048,256]{1,0:T(8,128)(2,1)S(1)} %copy-done.2, bf16[2048,256]{1,0:T(8,128)(2,1)S(1)} %copy-done.3), custom_call_target="tpu_custom_call" | custom-call | tf_op jit(solution)/shard_map/forward/pallas_call | solution.py:37
  15.5 1.6 %collective-permute-start.4 = (bf16[256,512]{1,0:T(8,128)(2,1)S(1)}, bf16[256,512]{1,0:T(8,128)(2,1)S(1)}, u32[]{:S(2)}, u32[]{:S(2)}) collective-permute-start(bf16[256,512]{1,0:T(8,128)(2,1)S(1)} %forward.5.a_ref), channel_id=1, source_target_pairs={{0,2},{2,0},{1,3},{3,1},{4,6},{6,4},{5,7},{7,5},{8,10},{10,8},{9,1... | collective-permute-start | bytes 786440 | tf_op jit(solution)/shard_map/ppermute | solution.py:321
  17.1 0.5 %collective-permute-start.6 = (bf16[272,256]{1,0:T(8,128)(2,1)S(1)}, bf16[272,256]{1,0:T(8,128)(2,1)S(1)}, u32[]{:S(2)}, u32[]{:S(2)}) collective-permute-start(bf16[272,256]{1,0:T(8,128)(2,1)S(1)} %pack.1.x_ref.refs_0_), channel_id=1, source_target_pairs={{0,4},{4,0},{8,12},{12,8},{1,5},{5,1},{9,13},{13,9},{2,6},{6,2},{1... | collective-permute-start | bytes 417800 | tf_op jit(solution)/shard_map/ppermute | solution.py:318
  17.6 0.0 collective-permute-start.7
  17.6 0.0 collective-permute-done.b_ref
  17.6 0.1 both.2.refs_0_
  17.6 2.0 %collective-permute-done.2.x_ref.refs_2_ = bf16[272,256]{1,0:T(8,128)(2,1)S(1)} collective-permute-done((bf16[272,256]{1,0:T(8,128)(2,1)S(1)}, bf16[272,256]{1,0:T(8,128)(2,1)S(1)}, u32[]{:S(2)}, u32[]{:S(2)}) %collective-permute-start.2) | collective-permute-done | bytes 139296 | tf_op jit(solution)/shard_map/ppermute | solution.py:318
  19.7 1.4 %forward.4.refs_2_ = bf16[256,512]{1,0:T(8,128)(2,1)S(1)} custom-call(bf16[272,256]{1,0:T(8,128)(2,1)S(1)} %collective-permute-done.2.x_ref.refs_2_, bf16[256,2048]{1,0:T(8,128)(2,1)S(1)} %copy-done, bf16[256,2048]{1,0:T(8,128)(2,1)S(1)} %copy-done.1, bf16[2048,256]{1,0:T(8,128)(2,1)S(1)} %copy-done.2, bf16[2048,256]{1,0:T(8,128)(2,1)S(1)} %copy-done.3), custom_call_target="tpu_custom_call" | custom-call | tf_op jit(solution)/shard_map/forward/pallas_call | solution.py:37
  21.0 1.2 %collective-permute-start.5 = (bf16[256,512]{1,0:T(8,128)(2,1)S(1)}, bf16[256,512]{1,0:T(8,128)(2,1)S(1)}, u32[]{:S(2)}, u32[]{:S(2)}) collective-permute-start(bf16[256,512]{1,0:T(8,128)(2,1)S(1)} %forward.4.refs_2_), channel_id=1, source_target_pairs={{0,2},{2,0},{1,3},{3,1},{4,6},{6,4},{5,7},{7,5},{8,10},{10,8},{9,1... | collective-permute-start | bytes 786440 | tf_op jit(solution)/shard_map/ppermute | solution.py:321
  22.3 1.1 %collective-permute-start.3 = (bf16[256,512]{1,0:T(8,128)(2,1)S(1)}, bf16[256,512]{1,0:T(8,128)(2,1)S(1)}, u32[]{:S(2)}, u32[]{:S(2)}) collective-permute-start(bf16[256,512]{1,0:T(8,128)(2,1)S(1)} %both.2.refs_0_), channel_id=1, source_target_pairs={{0,4},{4,0},{8,12},{12,8},{1,5},{5,1},{9,13},{13,9},{2,6},{6,2},{1... | collective-permute-start | bytes 786440 | tf_op jit(solution)/shard_map/ppermute | solution.py:318
  23.4 0.0 collective-permute-done.6.refs_1_
  23.4 0.0 collective-permute-start.8
  23.4 0.0 collective-permute-done.7.refs_4_
  23.4 0.5 %collective-permute-start.10 = (bf16[272,256]{1,0:T(8,128)(2,1)S(1)}, bf16[272,256]{1,0:T(8,128)(2,1)S(1)}, u32[]{:S(2)}, u32[]{:S(2)}) collective-permute-start(bf16[272,256]{1,0:T(8,128)(2,1)S(1)} %collective-permute-done.1.x_ref.refs_3_), channel_id=1, source_target_pairs={{0,1},{1,0},{2,3},{3,2},{4,5},{5,4},{6,7},{7,6},{8,9},{9,8},{10,11... | collective-permute-start | bytes 417800 | tf_op jit(solution)/shard_map/ppermute | solution.py:321
  23.9 0.0 collective-permute-done.4.b_ref
  23.9 0.1 collective-permute-start.9
  24.0 0.1 both.3.refs_3_
  24.0 0.7 %collective-permute-done.8.refs_5_ = bf16[272,256]{1,0:T(8,128)(2,1)S(1)} collective-permute-done((bf16[272,256]{1,0:T(8,128)(2,1)S(1)}, bf16[272,256]{1,0:T(8,128)(2,1)S(1)}, u32[]{:S(2)}, u32[]{:S(2)}) %collective-permute-start.8) | collective-permute-done | bytes 139296 | tf_op jit(solution)/shard_map/ppermute | solution.py:321
  24.7 0.1 collective-permute-start.11
  24.9 0.1 collective-permute-done.10.refs_7_
  24.9 0.3 collective-permute-start.13
  25.3 0.0 collective-permute-done.9.refs_6_
  25.3 0.2 collective-permute-start.12
  25.5 5.0 %arrange.1 = (bf16[1024,256]{1,0:T(8,128)(2,1)S(1)}, bf16[1024,256]{1,0:T(8,128)(2,1)S(1)}, bf16[1024,256]{1,0:T(8,128)(2,1)S(1)}, bf16[1024,2048]{1,0:T(8,128)(...) custom-call(bf16[272,256]{1,0:T(8,128)(2,1)S(1)} %pack.1.x_ref.refs_, ...), custom_call_target="tpu_custom_call" | custom-call | tf_op jit(solution)/shard_map/arrange/pallas_call | solution.py:37
  30.5 0.0 collective-permute-done.5.refs_4_
  30.5 0.4 collective-permute-start.14
  30.9 0.0 collective-permute-done.3.refs_1_
  30.9 0.2 collective-permute-start.15
  31.1 0.0 collective-permute-done.11.refs_5_
  31.1 0.0 collective-permute-done.12.refs_6_
  31.1 1.0 %gather.1 = (bf16[1024,256]{1,0:T(8,128)(2,1)S(1)}, f32[1024,256]{1,0:T(8,128)S(1)}) custom-call(bf16[256,512]{1,0:T(8,128)(2,1)S(1)} %both.2.refs_0_, bf16[256,512]{1,0:T(8,128)(2,1)S(1)} %collective-permute-done.3.refs_1_, bf16[256,512]{1,0:T(8,128)(2,1)S(1)} %forward.4.refs_2_, bf16[256,512]{1,0:T(8,128)(2,1)S(1)} %both.3.refs_3_, ...), custom_call_target="tpu_custom_call" | custom-call | tf_op jit(solution)/shard_map/gather/pallas_call | solution.py:37
  32.1 0.0 collective-permute-done.13.part_ref
  32.1 0.0 collective-permute-done.14.there_ref
  32.1 0.3 collective-permute-done.15.sums_ref
  32.5 2.2 %contrast.1.refs_2_ = bf16[1024,512]{1,0:T(8,128)(2,1)S(1)} custom-call(bf16[1024,256]{1,0:T(8,128)(2,1)S(1)} %get-tuple-element.46.phi_ref, f32[1024,256]{1,0:T(8,128)S(1)} %get-tuple-element.47.psi_ref, bf16[256,512]{1,0:T(8,128)(2,1)S(1)} %collective-permute-done.13.part_ref, bf16[256,512]{1,0:T(8,128)(2,1)S(1)} %collective-permute-done.14.there_ref, ...), custom_call_target="tpu_custom_call" | custom-call | tf_op jit(solution)/shard_map/contrast/pallas_call | solution.py:37
  34.6 0.4 collective-permute-start.16
  35.0 0.2 collective-permute-start.19
  35.2 3.5 %mine.1 = (f32[1024,256]{1,0:T(8,128)S(1)}, f32[1024,256]{1,0:T(8,128)S(1)}, f32[1024,256]{1,0:T(8,128)S(1)}, f32[1024,256]{1,0:T(8,128)S(1)}) custom-call(bf16[2048,256]{1,0:T(8,128)(2,1)S(1)} %copy-done.2, bf16[2048,256]{1,0:T(8,128)(2,1)S(1)} %copy-done.3, bf16[1024,512]{1,0:T(8,128)(2,1)S(1)} %contrast.1.refs_2_, ...), custom_call_target="tpu_custom_call" | custom-call | flops 4294967296 | tf_op jit(solution)/shard_map/mine/pallas_call | solution.py:37
  38.7 0.0 collective-permute-done.16.refs_2_
  38.7 2.7 %other_state.1 = (bf16[256,1024]{1,0:T(8,128)(2,1)S(1)}, bf16[1024,256]{1,0:T(8,128)(2,1)S(1)}, f32[256,1024]{1,0:T(8,128)S(1)}, f32[1024,256]{1,0:T(8,128)S(1)}) custom-call(bf16[256,2048]{1,0:T(8,128)(2,1)S(1)} %copy-done, bf16[2048,256]{1,0:T(8,128)(2,1)S(1)} %copy-done.2, bf16[1024,512]{1,0:T(8,128)(2,1)S(1)} %collective-permute-done.16.refs_2_, ...), custom_call_target="tpu_custom_call" | custom-call | flops 2147483648 | tf_op jit(solution)/shard_map/other_state/pallas_call | solution.py:37
  41.5 0.4 collective-permute-start.17
  41.8 0.2 collective-permute-start.18
  42.0 0.0 collective-permute-done.19.refs_3_
  42.0 3.0 %other_goal.1 = (bf16[256,1024]{1,0:T(8,128)(2,1)S(1)}, bf16[1024,256]{1,0:T(8,128)(2,1)S(1)}, f32[256,1024]{1,0:T(8,128)S(1)}, f32[1024,256]{1,0:T(8,128)S(1)},...) custom-call(bf16[256,2048]{1,0:T(8,128)(2,1)S(1)} %copy-done.1, bf16[2048,256]{1,0:T(8,128)(2,1)S(1)} %copy-done.3, ...), custom_call_target="tpu_custom_call" | custom-call | flops 2147483648 | tf_op jit(solution)/shard_map/other_goal/pallas_call | solution.py:37
  45.0 0.4 collective-permute-start.20
  45.4 0.2 collective-permute-start.21
  45.6 0.0 collective-permute-done.17.refs_0_
  45.6 0.0 collective-permute-done.18.refs_1_
  45.6 2.0 %finish.2 = (f32[256,2048]{1,0:T(8,128)}, f32[2048,256]{1,0:T(8,128)}, f32[256,2048]{1,0:T(8,128)}, f32[2048,256]{1,0:T(8,128)}) custom-call(bf16[256,1024]{1,0:T(8,128)(2,1)S(1)} %collective-permute-done.17.refs_0_, bf16[1024,256]{1,0:T(8,128)(2,1)S(1)} %collective-permute-done.18.refs_1_, ...), custom_call_target="tpu_custom_call", output_to_operand_aliasing={{0}: (4, {}), {1}: (5, {})} | custom-call | tf_op jit(solution)/shard_map/finish/pallas_call | solution.py:37
  47.7 0.0 collective-permute-done.20.refs_0_
  47.7 0.1 collective-permute-done.21.refs_1_
  47.7 1.4 %finish.3 = (f32[256,2048]{1,0:T(8,128)}, f32[2048,256]{1,0:T(8,128)}) custom-call(bf16[256,1024]{1,0:T(8,128)(2,1)S(1)} %collective-permute-done.20.refs_0_, bf16[1024,256]{1,0:T(8,128)(2,1)S(1)} %collective-permute-done.21.refs_1_, f32[256,2048]{1,0:T(8,128)} %get-tuple-element.72.refs_2_, ...), custom_call_target="tpu_custom_call", output_to_operand_aliasing={{0}: (2, {}), {1}: (3, {})} | custom-call | tf_op jit(solution)/shard_map/finish/pallas_call | solution.py:37
  (11 shorter events, 0.0 us)
Async XLA Ops:
  0.6 0.7 %copy-start.5 = (s32[256,1]{0,1:T(1,128)S(1)}, s32[256,1]{0,1:T(1,128)}, u32[]{:S(2)}) copy-start(s32[256,1]{0,1:T(1,128)} %param.9) | copy-start | bytes 3076
  0.6 0.7 %copy-start.6 = (s32[256]{0:T(256)S(1)}, s32[256]{0:T(256)}, u32[]{:S(2)}) copy-start(s32[256]{0:T(256)} %param.10) | copy-start | bytes 3076
  0.7 0.7 %copy-start.7 = (s32[256]{0:T(256)S(1)}, s32[256]{0:T(256)}, u32[]{:S(2)}) copy-start(s32[256]{0:T(256)} %param.11) | copy-start | bytes 3076
  0.7 0.9 %copy-start.4 = (bf16[256,256]{1,0:T(8,128)(2,1)S(1)}, bf16[256,256]{1,0:T(8,128)(2,1)}, u32[]{:S(2)}) copy-start(bf16[256,256]{1,0:T(8,128)(2,1)} %refs_1_.7) | copy-start | bytes 393220
  1.6 5.2 %copy-start = (bf16[256,2048]{1,0:T(8,128)(2,1)S(1)}, bf16[256,2048]{1,0:T(8,128)(2,1)}, u32[]{:S(2)}) copy-start(bf16[256,2048]{1,0:T(8,128)(2,1)} %refs_0_.10) | copy-start | bytes 3145732
  1.6 5.2 %copy-start.1 = (bf16[256,2048]{1,0:T(8,128)(2,1)S(1)}, bf16[256,2048]{1,0:T(8,128)(2,1)}, u32[]{:S(2)}) copy-start(bf16[256,2048]{1,0:T(8,128)(2,1)} %refs_0_.11) | copy-start | bytes 3145732
  1.6 5.2 %copy-start.2 = (bf16[2048,256]{1,0:T(8,128)(2,1)S(1)}, bf16[2048,256]{1,0:T(8,128)(2,1)}, u32[]{:S(2)}) copy-start(bf16[2048,256]{1,0:T(8,128)(2,1)} %refs_1_.12) | copy-start | bytes 3145732
  1.6 5.2 %copy-start.3 = (bf16[2048,256]{1,0:T(8,128)(2,1)S(1)}, bf16[2048,256]{1,0:T(8,128)(2,1)}, u32[]{:S(2)}) copy-start(bf16[2048,256]{1,0:T(8,128)(2,1)} %refs_1_.13) | copy-start | bytes 3145732
  1.6 8.9 %collective-permute-start.1 = (bf16[272,256]{1,0:T(8,128)(2,1)S(1)}, bf16[272,256]{1,0:T(8,128)(2,1)S(1)}, u32[]{:S(2)}, u32[]{:S(2)}) collective-permute-start(bf16[272,256]{1,0:T(8,128)(2,1)S(1)} %pack.1.x_ref.refs_0_), channel_id=1, source_target_pairs={{0,12},{4,8},{8,4},{12,0},{1,13},{5,9},{9,5},{13,1},{2,14},{6,10},... | collective-permute-start | bytes 417800 | tf_op jit(solution)/shard_map/ppermute | solution.py:318
  8.1 9.4 %collective-permute-start = (bf16[256,512]{1,0:T(8,128)(2,1)S(1)}, bf16[256,512]{1,0:T(8,128)(2,1)S(1)}, u32[]{:S(2)}, u32[]{:S(2)}) collective-permute-start(bf16[256,512]{1,0:T(8,128)(2,1)S(1)} %forward.3.a_ref), channel_id=1, source_target_pairs={{0,2},{2,0},{1,3},{3,1},{4,6},{6,4},{5,7},{7,5},{8,10},{10,8},{9,1... | collective-permute-start | bytes 786440 | tf_op jit(solution)/shard_map/ppermute | solution.py:321
  10.5 9.1 %collective-permute-start.2 = (bf16[272,256]{1,0:T(8,128)(2,1)S(1)}, bf16[272,256]{1,0:T(8,128)(2,1)S(1)}, u32[]{:S(2)}, u32[]{:S(2)}) collective-permute-start(bf16[272,256]{1,0:T(8,128)(2,1)S(1)} %pack.1.x_ref.refs_0_), channel_id=1, source_target_pairs={{0,8},{4,12},{8,0},{12,4},{1,9},{5,13},{9,1},{13,5},{2,10},{6,14},... | collective-permute-start | bytes 417800 | tf_op jit(solution)/shard_map/ppermute | solution.py:318
  15.5 8.4 %collective-permute-start.4 = (bf16[256,512]{1,0:T(8,128)(2,1)S(1)}, bf16[256,512]{1,0:T(8,128)(2,1)S(1)}, u32[]{:S(2)}, u32[]{:S(2)}) collective-permute-start(bf16[256,512]{1,0:T(8,128)(2,1)S(1)} %forward.5.a_ref), channel_id=1, source_target_pairs={{0,2},{2,0},{1,3},{3,1},{4,6},{6,4},{5,7},{7,5},{8,10},{10,8},{9,1... | collective-permute-start | bytes 786440 | tf_op jit(solution)/shard_map/ppermute | solution.py:321
  17.1 6.3 %collective-permute-start.6 = (bf16[272,256]{1,0:T(8,128)(2,1)S(1)}, bf16[272,256]{1,0:T(8,128)(2,1)S(1)}, u32[]{:S(2)}, u32[]{:S(2)}) collective-permute-start(bf16[272,256]{1,0:T(8,128)(2,1)S(1)} %pack.1.x_ref.refs_0_), channel_id=1, source_target_pairs={{0,4},{4,0},{8,12},{12,8},{1,5},{5,1},{9,13},{13,9},{2,6},{6,2},{1... | collective-permute-start | bytes 417800 | tf_op jit(solution)/shard_map/ppermute | solution.py:318
  17.6 5.8 %collective-permute-start.7 = (bf16[272,256]{1,0:T(8,128)(2,1)S(1)}, bf16[272,256]{1,0:T(8,128)(2,1)S(1)}, u32[]{:S(2)}, u32[]{:S(2)}) collective-permute-start(bf16[272,256]{1,0:T(8,128)(2,1)S(1)} %pack.1.x_ref.refs_0_), channel_id=1, source_target_pairs={{0,1},{1,0},{2,3},{3,2},{4,5},{5,4},{6,7},{7,6},{8,9},{9,8},{10,11... | collective-permute-start | bytes 417800 | tf_op jit(solution)/shard_map/ppermute | solution.py:321
  21.0 9.4 %collective-permute-start.5 = (bf16[256,512]{1,0:T(8,128)(2,1)S(1)}, bf16[256,512]{1,0:T(8,128)(2,1)S(1)}, u32[]{:S(2)}, u32[]{:S(2)}) collective-permute-start(bf16[256,512]{1,0:T(8,128)(2,1)S(1)} %forward.4.refs_2_), channel_id=1, source_target_pairs={{0,2},{2,0},{1,3},{3,1},{4,6},{6,4},{5,7},{7,5},{8,10},{10,8},{9,1... | collective-permute-start | bytes 786440 | tf_op jit(solution)/shard_map/ppermute | solution.py:321
  22.3 8.6 %collective-permute-start.3 = (bf16[256,512]{1,0:T(8,128)(2,1)S(1)}, bf16[256,512]{1,0:T(8,128)(2,1)S(1)}, u32[]{:S(2)}, u32[]{:S(2)}) collective-permute-start(bf16[256,512]{1,0:T(8,128)(2,1)S(1)} %both.2.refs_0_), channel_id=1, source_target_pairs={{0,4},{4,0},{8,12},{12,8},{1,5},{5,1},{9,13},{13,9},{2,6},{6,2},{1... | collective-permute-start | bytes 786440 | tf_op jit(solution)/shard_map/ppermute | solution.py:318
  23.4 1.4 %collective-permute-start.8 = (bf16[272,256]{1,0:T(8,128)(2,1)S(1)}, bf16[272,256]{1,0:T(8,128)(2,1)S(1)}, u32[]{:S(2)}, u32[]{:S(2)}) collective-permute-start(bf16[272,256]{1,0:T(8,128)(2,1)S(1)} %collective-permute-done.6.refs_1_), channel_id=1, source_target_pairs={{0,1},{1,0},{2,3},{3,2},{4,5},{5,4},{6,7},{7,6},{8,9},{9,8},{10,11... | collective-permute-start | bytes 417800 | tf_op jit(solution)/shard_map/ppermute | solution.py:321
  23.4 1.6 %collective-permute-start.10 = (bf16[272,256]{1,0:T(8,128)(2,1)S(1)}, bf16[272,256]{1,0:T(8,128)(2,1)S(1)}, u32[]{:S(2)}, u32[]{:S(2)}) collective-permute-start(bf16[272,256]{1,0:T(8,128)(2,1)S(1)} %collective-permute-done.1.x_ref.refs_3_), channel_id=1, source_target_pairs={{0,1},{1,0},{2,3},{3,2},{4,5},{5,4},{6,7},{7,6},{8,9},{9,8},{10,11... | collective-permute-start | bytes 417800 | tf_op jit(solution)/shard_map/ppermute | solution.py:321
  23.9 1.4 %collective-permute-start.9 = (bf16[272,256]{1,0:T(8,128)(2,1)S(1)}, bf16[272,256]{1,0:T(8,128)(2,1)S(1)}, u32[]{:S(2)}, u32[]{:S(2)}) collective-permute-start(bf16[272,256]{1,0:T(8,128)(2,1)S(1)} %collective-permute-done.2.x_ref.refs_2_), channel_id=1, source_target_pairs={{0,1},{1,0},{2,3},{3,2},{4,5},{5,4},{6,7},{7,6},{8,9},{9,8},{10,11... | collective-permute-start | bytes 417800 | tf_op jit(solution)/shard_map/ppermute | solution.py:321
  24.7 6.3 %collective-permute-start.11 = (bf16[256,512]{1,0:T(8,128)(2,1)S(1)}, bf16[256,512]{1,0:T(8,128)(2,1)S(1)}, u32[]{:S(2)}, u32[]{:S(2)}) collective-permute-start(bf16[256,512]{1,0:T(8,128)(2,1)S(1)} %both.2.refs_0_), channel_id=1, source_target_pairs={{0,1},{1,0},{2,3},{3,2},{4,5},{5,4},{6,7},{7,6},{8,9},{9,8},{10,11... | collective-permute-start | bytes 786440 | tf_op jit(solution)/shard_map/ppermute | solution.py:321
  24.9 7.2 %collective-permute-start.13 = (bf16[256,512]{1,0:T(8,128)(2,1)S(1)}, bf16[256,512]{1,0:T(8,128)(2,1)S(1)}, u32[]{:S(2)}, u32[]{:S(2)}) collective-permute-start(bf16[256,512]{1,0:T(8,128)(2,1)S(1)} %forward.4.refs_2_), channel_id=1, source_target_pairs={{0,1},{1,0},{2,3},{3,2},{4,5},{5,4},{6,7},{7,6},{8,9},{9,8},{10,11... | collective-permute-start | bytes 786440 | tf_op jit(solution)/shard_map/ppermute | solution.py:321
  25.3 5.8 %collective-permute-start.12 = (bf16[256,512]{1,0:T(8,128)(2,1)S(1)}, bf16[256,512]{1,0:T(8,128)(2,1)S(1)}, u32[]{:S(2)}, u32[]{:S(2)}) collective-permute-start(bf16[256,512]{1,0:T(8,128)(2,1)S(1)} %both.3.refs_3_), channel_id=1, source_target_pairs={{0,1},{1,0},{2,3},{3,2},{4,5},{5,4},{6,7},{7,6},{8,9},{9,8},{10,11... | collective-permute-start | bytes 786440 | tf_op jit(solution)/shard_map/ppermute | solution.py:321
  30.5 1.6 %collective-permute-start.14 = (bf16[256,512]{1,0:T(8,128)(2,1)S(1)}, bf16[256,512]{1,0:T(8,128)(2,1)S(1)}, u32[]{:S(2)}, u32[]{:S(2)}) collective-permute-start(bf16[256,512]{1,0:T(8,128)(2,1)S(1)} %collective-permute-done.5.refs_4_), channel_id=1, source_target_pairs={{0,1},{1,0},{2,3},{3,2},{4,5},{5,4},{6,7},{7,6},{8,9},{9,8},{10,11... | collective-permute-start | bytes 786440 | tf_op jit(solution)/shard_map/ppermute | solution.py:321
  30.9 1.6 %collective-permute-start.15 = (bf16[256,512]{1,0:T(8,128)(2,1)S(1)}, bf16[256,512]{1,0:T(8,128)(2,1)S(1)}, u32[]{:S(2)}, u32[]{:S(2)}) collective-permute-start(bf16[256,512]{1,0:T(8,128)(2,1)S(1)} %collective-permute-done.3.refs_1_), channel_id=1, source_target_pairs={{0,1},{1,0},{2,3},{3,2},{4,5},{5,4},{6,7},{7,6},{8,9},{9,8},{10,11... | collective-permute-start | bytes 786440 | tf_op jit(solution)/shard_map/ppermute | solution.py:321
  34.6 4.1 %collective-permute-start.16 = (bf16[1024,512]{1,0:T(8,128)(2,1)S(1)}, bf16[1024,512]{1,0:T(8,128)(2,1)S(1)}, u32[]{:S(2)}, u32[]{:S(2)}) collective-permute-start(bf16[1024,512]{1,0:T(8,128)(2,1)S(1)} %contrast.1.refs_2_), channel_id=1, source_target_pairs={{0,1},{1,0},{2,3},{3,2},{4,5},{5,4},{6,7},{7,6},{8,9},{9,8},{10,11... | collective-permute-start | bytes 3145736 | tf_op jit(solution)/shard_map/ppermute | solution.py:321
  35.0 7.0 %collective-permute-start.19 = (bf16[1024,256]{1,0:T(8,128)(2,1)S(1)}, bf16[1024,256]{1,0:T(8,128)(2,1)S(1)}, u32[]{:S(2)}, u32[]{:S(2)}) collective-permute-start(bf16[1024,256]{1,0:T(8,128)(2,1)S(1)} %get-tuple-element.51.refs_4_), channel_id=1, source_target_pairs={{0,1},{1,0},{2,3},{3,2},{4,5},{5,4},{6,7},{7,6},{8,9},{9,8},{10,11... | collective-permute-start | bytes 1572872 | tf_op jit(solution)/shard_map/ppermute | solution.py:321
  41.5 4.1 %collective-permute-start.17 = (bf16[256,1024]{1,0:T(8,128)(2,1)S(1)}, bf16[256,1024]{1,0:T(8,128)(2,1)S(1)}, u32[]{:S(2)}, u32[]{:S(2)}) collective-permute-start(bf16[256,1024]{1,0:T(8,128)(2,1)S(1)} %get-tuple-element.58), channel_id=1, source_target_pairs={{0,1},{1,0},{2,3},{3,2},{4,5},{5,4},{6,7},{7,6},{8,9},{9,8},{10,11... | collective-permute-start | bytes 1572872 | tf_op jit(solution)/shard_map/ppermute | solution.py:321
  41.8 3.8 %collective-permute-start.18 = (bf16[1024,256]{1,0:T(8,128)(2,1)S(1)}, bf16[1024,256]{1,0:T(8,128)(2,1)S(1)}, u32[]{:S(2)}, u32[]{:S(2)}) collective-permute-start(bf16[1024,256]{1,0:T(8,128)(2,1)S(1)} %get-tuple-element.59), channel_id=1, source_target_pairs={{0,1},{1,0},{2,3},{3,2},{4,5},{5,4},{6,7},{7,6},{8,9},{9,8},{10,11... | collective-permute-start | bytes 1572872 | tf_op jit(solution)/shard_map/ppermute | solution.py:321
  45.0 2.6 %collective-permute-start.20 = (bf16[256,1024]{1,0:T(8,128)(2,1)S(1)}, bf16[256,1024]{1,0:T(8,128)(2,1)S(1)}, u32[]{:S(2)}, u32[]{:S(2)}) collective-permute-start(bf16[256,1024]{1,0:T(8,128)(2,1)S(1)} %get-tuple-element.70), channel_id=1, source_target_pairs={{0,1},{1,0},{2,3},{3,2},{4,5},{5,4},{6,7},{7,6},{8,9},{9,8},{10,11... | collective-permute-start | bytes 1572872 | tf_op jit(solution)/shard_map/ppermute | solution.py:321
  45.4 2.3 %collective-permute-start.21 = (bf16[1024,256]{1,0:T(8,128)(2,1)S(1)}, bf16[1024,256]{1,0:T(8,128)(2,1)S(1)}, u32[]{:S(2)}, u32[]{:S(2)}) collective-permute-start(bf16[1024,256]{1,0:T(8,128)(2,1)S(1)} %get-tuple-element.71), channel_id=1, source_target_pairs={{0,1},{1,0},{2,3},{3,2},{4,5},{5,4},{6,7},{7,6},{8,9},{9,8},{10,11... | collective-permute-start | bytes 1572872 | tf_op jit(solution)/shard_map/ppermute | solution.py:321

commit v19 on v18

--- a/solution.py
+++ b/solution.py
@@ -141,8 +141,9 @@
         pick_ref[own, :] = jnp.where(
             goal == lax.broadcasted_iota(jnp.int32, (batch, rows), 1), 1.0, 0.0
         ).astype(BF)
+    activate(pos, firsts[0], rows_mine, hidden[:2])
     goals_ref[...] = dot(pick_ref[...], both_sides[...]).astype(BF)
-    activate(pos, firsts, (rows_mine, goals_ref), hidden)
+    activate(pos, firsts[1], goals_ref, hidden[2:])
 
 
 def gather_kernel(n_blk, n_rep, slab, pos, *refs):
@@ -214,18 +215,17 @@
     return dot(active[...], grad), dot(back[...], rows_ref[...])
 
 
-def activate(pos, firsts, inputs, outs):
+def activate(pos, first, x_ref, outs):
     quarter, rows = outs[0].shape
     at = pl.multiple_of(pos[1] * quarter, quarter)
-    for k, (first, x_ref) in enumerate(zip(firsts, inputs)):
-        first_t = first[:, pl.ds(at, quarter)].T
-        for c in range(0, rows, 256):
-            cols = slice(c, c + 256)
-            hidden = dot(first_t, x_ref[cols, :].T)
-            sig = sigmoid(hidden)
-            act = hidden * sig
-            outs[2 * k][:, cols] = act.astype(BF)
-            outs[2 * k + 1][:, cols] = (sig + act * (1.0 - sig)).astype(BF)
+    first_t = first[:, pl.ds(at, quarter)].T
+    for c in range(0, rows, 256):
+        cols = slice(c, c + 256)
+        hidden = dot(first_t, x_ref[cols, :].T)
+        sig = sigmoid(hidden)
+        act = hidden * sig
+        outs[0][:, cols] = act.astype(BF)
+        outs[1][:, cols] = (sig + act * (1.0 - sig)).astype(BF)
 
 
 def mine_kernel(pos, ss, gs, grads_ref, rows_ref, goals_ref, *refs):

time: 49.5 us -> 49.4 us (level)
  no operation moved by 1% of the time
where the time goes in v19:
time: 49.4 us; the launch traced here: 49.3 us
  Pallas kernels  25.1 us (51%)
  starting transfers between devices  18.2 us (37%)
  waiting for transfers between devices  4.06 us (8%)
  between operations  0.99 us (2%)
  local copies, waits for them, and re-layouts  0.92 us (2%)
    pallas_call x15, Pallas kernels, kernel(): pl.pallas_call(body, in_specs=specs, out_specs=[HBM if i in hbm_out else...  25.1 us
    ppermute x4, starting transfers between devices, across(): return lax.ppermute(x, 'blk', [(i, i ^ k) for i in range(n_blk)])  10.3 us
    ppermute x18, starting transfers between devices, swap(): return lax.ppermute(x, axis, [(0, 1), (1, 0)])  7.87 us
    ppermute x4, waiting for transfers between devices, across(): return lax.ppermute(x, 'blk', [(i, i ^ k) for i in range(n_blk)])  2.86 us
    ppermute x18, waiting for transfers between devices, swap(): return lax.ppermute(x, axis, [(0, 1), (1, 0)])  1.2 us
  transfers between devices with their start and end apart: 22, of which 6 were waited for; matrix products, arithmetic and copies ran while one was open for 0% of the time, Pallas kernels for 44%

profile of v19, /device:TPU:0, one launch (start us, length us, event | category | flops | bytes accessed | tf_op | source)
XLA Modules:
  0.0 49.3 jit_solution(10809761124357078758)
XLA Ops:
  0.6 0.0 copy-start.5
  0.6 0.0 copy-start.6
  0.7 0.6 %copy-done.5 = s32[256,1]{0,1:T(1,128)S(1)} copy-done((s32[256,1]{0,1:T(1,128)S(1)}, s32[256,1]{0,1:T(1,128)}, u32[]{:S(2)}) %copy-start.5) | copy-done | bytes 1048
  1.3 0.0 copy-done.6
  1.3 0.0 copy-done.7
  1.3 0.2 copy-done.4
  1.6 5.1 %collective-permute-start.1 = (bf16[272,256]{1,0:T(8,128)(2,1)S(1)}, bf16[272,256]{1,0:T(8,128)(2,1)S(1)}, u32[]{:S(2)}, u32[]{:S(2)}) collective-permute-start(bf16[272,256]{1,0:T(8,128)(2,1)S(1)} %pack.1.x_ref.refs_0_), channel_id=1, source_target_pairs={{0,12},{4,8},{8,4},{12,0},{1,13},{5,9},{9,5},{13,1},{2,14},{6,10},... | collective-permute-start | bytes 417800 | tf_op jit(solution)/shard_map/ppermute | solution.py:318
  6.7 0.0 copy-done.1
  6.7 1.4 %forward.3.a_ref = bf16[256,512]{1,0:T(8,128)(2,1)S(1)} custom-call(bf16[272,256]{1,0:T(8,128)(2,1)S(1)} %pack.1.x_ref.refs_0_, bf16[256,2048]{1,0:T(8,128)(2,1)S(1)} %copy-done, bf16[256,2048]{1,0:T(8,128)(2,1)S(1)} %copy-done.1, bf16[2048,256]{1,0:T(8,128)(2,1)S(1)} %copy-done.2, bf16[2048,256]{1,0:T(8,128)(2,1)S(1)} %copy-done.3), custom_call_target="tpu_custom_call" | custom-call | tf_op jit(solution)/shard_map/forward/pallas_call | solution.py:37
  8.1 1.6 %collective-permute-start = (bf16[256,512]{1,0:T(8,128)(2,1)S(1)}, bf16[256,512]{1,0:T(8,128)(2,1)S(1)}, u32[]{:S(2)}, u32[]{:S(2)}) collective-permute-start(bf16[256,512]{1,0:T(8,128)(2,1)S(1)} %forward.3.a_ref), channel_id=1, source_target_pairs={{0,2},{2,0},{1,3},{3,1},{4,6},{6,4},{5,7},{7,5},{8,10},{10,8},{9,1... | collective-permute-start | bytes 786440 | tf_op jit(solution)/shard_map/ppermute | solution.py:321
  9.7 0.8 %collective-permute-done.1.x_ref.refs_3_ = bf16[272,256]{1,0:T(8,128)(2,1)S(1)} collective-permute-done((bf16[272,256]{1,0:T(8,128)(2,1)S(1)}, bf16[272,256]{1,0:T(8,128)(2,1)S(1)}, u32[]{:S(2)}, u32[]{:S(2)}) %collective-permute-start.1) | collective-permute-done | bytes 139296 | tf_op jit(solution)/shard_map/ppermute | solution.py:318
  10.5 3.6 %collective-permute-start.2 = (bf16[272,256]{1,0:T(8,128)(2,1)S(1)}, bf16[272,256]{1,0:T(8,128)(2,1)S(1)}, u32[]{:S(2)}, u32[]{:S(2)}) collective-permute-start(bf16[272,256]{1,0:T(8,128)(2,1)S(1)} %pack.1.x_ref.refs_0_), channel_id=1, source_target_pairs={{0,8},{4,12},{8,0},{12,4},{1,9},{5,13},{9,1},{13,5},{2,10},{6,14},... | collective-permute-start | bytes 417800 | tf_op jit(solution)/shard_map/ppermute | solution.py:318
  14.1 1.4 %forward.5.a_ref = bf16[256,512]{1,0:T(8,128)(2,1)S(1)} custom-call(bf16[272,256]{1,0:T(8,128)(2,1)S(1)} %collective-permute-done.1.x_ref.refs_3_, bf16[256,2048]{1,0:T(8,128)(2,1)S(1)} %copy-done, bf16[256,2048]{1,0:T(8,128)(2,1)S(1)} %copy-done.1, bf16[2048,256]{1,0:T(8,128)(2,1)S(1)} %copy-done.2, bf16[2048,256]{1,0:T(8,128)(2,1)S(1)} %copy-done.3), custom_call_target="tpu_custom_call" | custom-call | tf_op jit(solution)/shard_map/forward/pallas_call | solution.py:37
  15.5 1.6 %collective-permute-start.4 = (bf16[256,512]{1,0:T(8,128)(2,1)S(1)}, bf16[256,512]{1,0:T(8,128)(2,1)S(1)}, u32[]{:S(2)}, u32[]{:S(2)}) collective-permute-start(bf16[256,512]{1,0:T(8,128)(2,1)S(1)} %forward.5.a_ref), channel_id=1, source_target_pairs={{0,2},{2,0},{1,3},{3,1},{4,6},{6,4},{5,7},{7,5},{8,10},{10,8},{9,1... | collective-permute-start | bytes 786440 | tf_op jit(solution)/shard_map/ppermute | solution.py:321
  17.1 0.5 %collective-permute-start.6 = (bf16[272,256]{1,0:T(8,128)(2,1)S(1)}, bf16[272,256]{1,0:T(8,128)(2,1)S(1)}, u32[]{:S(2)}, u32[]{:S(2)}) collective-permute-start(bf16[272,256]{1,0:T(8,128)(2,1)S(1)} %pack.1.x_ref.refs_0_), channel_id=1, source_target_pairs={{0,4},{4,0},{8,12},{12,8},{1,5},{5,1},{9,13},{13,9},{2,6},{6,2},{1... | collective-permute-start | bytes 417800 | tf_op jit(solution)/shard_map/ppermute | solution.py:318
  17.6 0.0 collective-permute-start.7
  17.6 0.0 collective-permute-done.b_ref
  17.6 0.1 both.2.refs_0_
  17.6 2.0 %collective-permute-done.2.x_ref.refs_2_ = bf16[272,256]{1,0:T(8,128)(2,1)S(1)} collective-permute-done((bf16[272,256]{1,0:T(8,128)(2,1)S(1)}, bf16[272,256]{1,0:T(8,128)(2,1)S(1)}, u32[]{:S(2)}, u32[]{:S(2)}) %collective-permute-start.2) | collective-permute-done | bytes 139296 | tf_op jit(solution)/shard_map/ppermute | solution.py:318
  19.7 1.4 %forward.4.refs_2_ = bf16[256,512]{1,0:T(8,128)(2,1)S(1)} custom-call(bf16[272,256]{1,0:T(8,128)(2,1)S(1)} %collective-permute-done.2.x_ref.refs_2_, bf16[256,2048]{1,0:T(8,128)(2,1)S(1)} %copy-done, bf16[256,2048]{1,0:T(8,128)(2,1)S(1)} %copy-done.1, bf16[2048,256]{1,0:T(8,128)(2,1)S(1)} %copy-done.2, bf16[2048,256]{1,0:T(8,128)(2,1)S(1)} %copy-done.3), custom_call_target="tpu_custom_call" | custom-call | tf_op jit(solution)/shard_map/forward/pallas_call | solution.py:37
  21.0 1.2 %collective-permute-start.5 = (bf16[256,512]{1,0:T(8,128)(2,1)S(1)}, bf16[256,512]{1,0:T(8,128)(2,1)S(1)}, u32[]{:S(2)}, u32[]{:S(2)}) collective-permute-start(bf16[256,512]{1,0:T(8,128)(2,1)S(1)} %forward.4.refs_2_), channel_id=1, source_target_pairs={{0,2},{2,0},{1,3},{3,1},{4,6},{6,4},{5,7},{7,5},{8,10},{10,8},{9,1... | collective-permute-start | bytes 786440 | tf_op jit(solution)/shard_map/ppermute | solution.py:321
  22.3 1.1 %collective-permute-start.3 = (bf16[256,512]{1,0:T(8,128)(2,1)S(1)}, bf16[256,512]{1,0:T(8,128)(2,1)S(1)}, u32[]{:S(2)}, u32[]{:S(2)}) collective-permute-start(bf16[256,512]{1,0:T(8,128)(2,1)S(1)} %both.2.refs_0_), channel_id=1, source_target_pairs={{0,4},{4,0},{8,12},{12,8},{1,5},{5,1},{9,13},{13,9},{2,6},{6,2},{1... | collective-permute-start | bytes 786440 | tf_op jit(solution)/shard_map/ppermute | solution.py:318
  23.4 0.0 collective-permute-done.6.refs_1_
  23.4 0.0 collective-permute-start.8
  23.4 0.0 collective-permute-done.7.refs_4_
  23.4 0.5 %collective-permute-start.10 = (bf16[272,256]{1,0:T(8,128)(2,1)S(1)}, bf16[272,256]{1,0:T(8,128)(2,1)S(1)}, u32[]{:S(2)}, u32[]{:S(2)}) collective-permute-start(bf16[272,256]{1,0:T(8,128)(2,1)S(1)} %collective-permute-done.1.x_ref.refs_3_), channel_id=1, source_target_pairs={{0,1},{1,0},{2,3},{3,2},{4,5},{5,4},{6,7},{7,6},{8,9},{9,8},{10,11... | collective-permute-start | bytes 417800 | tf_op jit(solution)/shard_map/ppermute | solution.py:321
  23.9 0.0 collective-permute-done.4.b_ref
  23.9 0.1 collective-permute-start.9
  24.0 0.1 both.3.refs_3_
  24.0 0.7 %collective-permute-done.8.refs_5_ = bf16[272,256]{1,0:T(8,128)(2,1)S(1)} collective-permute-done((bf16[272,256]{1,0:T(8,128)(2,1)S(1)}, bf16[272,256]{1,0:T(8,128)(2,1)S(1)}, u32[]{:S(2)}, u32[]{:S(2)}) %collective-permute-start.8) | collective-permute-done | bytes 139296 | tf_op jit(solution)/shard_map/ppermute | solution.py:321
  24.7 0.1 collective-permute-start.11
  24.9 0.1 collective-permute-done.10.refs_7_
  24.9 0.3 collective-permute-start.13
  25.3 0.0 collective-permute-done.9.refs_6_
  25.3 0.2 collective-permute-start.12
  25.5 5.0 %arrange.1 = (bf16[1024,256]{1,0:T(8,128)(2,1)S(1)}, bf16[1024,256]{1,0:T(8,128)(2,1)S(1)}, bf16[1024,256]{1,0:T(8,128)(2,1)S(1)}, bf16[1024,2048]{1,0:T(8,128)(...) custom-call(bf16[272,256]{1,0:T(8,128)(2,1)S(1)} %pack.1.x_ref.refs_, ...), custom_call_target="tpu_custom_call" | custom-call | tf_op jit(solution)/shard_map/arrange/pallas_call | solution.py:37
  30.5 0.0 collective-permute-done.5.refs_4_
  30.5 0.4 collective-permute-start.14
  30.8 0.0 collective-permute-done.3.refs_1_
  30.8 0.2 collective-permute-start.15
  31.0 0.0 collective-permute-done.11.refs_5_
  31.0 0.0 collective-permute-done.12.refs_6_
  31.0 1.0 %gather.1 = (bf16[1024,256]{1,0:T(8,128)(2,1)S(1)}, f32[1024,256]{1,0:T(8,128)S(1)}) custom-call(bf16[256,512]{1,0:T(8,128)(2,1)S(1)} %both.2.refs_0_, bf16[256,512]{1,0:T(8,128)(2,1)S(1)} %collective-permute-done.3.refs_1_, bf16[256,512]{1,0:T(8,128)(2,1)S(1)} %forward.4.refs_2_, bf16[256,512]{1,0:T(8,128)(2,1)S(1)} %both.3.refs_3_, ...), custom_call_target="tpu_custom_call" | custom-call | tf_op jit(solution)/shard_map/gather/pallas_call | solution.py:37
  32.1 0.0 collective-permute-done.13.part_ref
  32.1 0.0 collective-permute-done.14.there_ref
  32.1 0.3 collective-permute-done.15.sums_ref
  32.4 2.2 %contrast.1.refs_2_ = bf16[1024,512]{1,0:T(8,128)(2,1)S(1)} custom-call(bf16[1024,256]{1,0:T(8,128)(2,1)S(1)} %get-tuple-element.46.phi_ref, f32[1024,256]{1,0:T(8,128)S(1)} %get-tuple-element.47.psi_ref, bf16[256,512]{1,0:T(8,128)(2,1)S(1)} %collective-permute-done.13.part_ref, bf16[256,512]{1,0:T(8,128)(2,1)S(1)} %collective-permute-done.14.there_ref, ...), custom_call_target="tpu_custom_call" | custom-call | tf_op jit(solution)/shard_map/contrast/pallas_call | solution.py:37
  34.6 0.4 collective-permute-start.16
  35.0 0.2 collective-permute-start.19
  35.2 3.5 %mine.1 = (f32[1024,256]{1,0:T(8,128)S(1)}, f32[1024,256]{1,0:T(8,128)S(1)}, f32[1024,256]{1,0:T(8,128)S(1)}, f32[1024,256]{1,0:T(8,128)S(1)}) custom-call(bf16[2048,256]{1,0:T(8,128)(2,1)S(1)} %copy-done.2, bf16[2048,256]{1,0:T(8,128)(2,1)S(1)} %copy-done.3, bf16[1024,512]{1,0:T(8,128)(2,1)S(1)} %contrast.1.refs_2_, ...), custom_call_target="tpu_custom_call" | custom-call | flops 4294967296 | tf_op jit(solution)/shard_map/mine/pallas_call | solution.py:37
  38.7 0.0 collective-permute-done.16.refs_2_
  38.7 2.7 %other_state.1 = (bf16[256,1024]{1,0:T(8,128)(2,1)S(1)}, bf16[1024,256]{1,0:T(8,128)(2,1)S(1)}, f32[256,1024]{1,0:T(8,128)S(1)}, f32[1024,256]{1,0:T(8,128)S(1)}) custom-call(bf16[256,2048]{1,0:T(8,128)(2,1)S(1)} %copy-done, bf16[2048,256]{1,0:T(8,128)(2,1)S(1)} %copy-done.2, bf16[1024,512]{1,0:T(8,128)(2,1)S(1)} %collective-permute-done.16.refs_2_, ...), custom_call_target="tpu_custom_call" | custom-call | flops 2147483648 | tf_op jit(solution)/shard_map/other_state/pallas_call | solution.py:37
  41.4 0.4 collective-permute-start.17
  41.8 0.2 collective-permute-start.18
  42.0 0.0 collective-permute-done.19.refs_3_
  42.0 3.0 %other_goal.1 = (bf16[256,1024]{1,0:T(8,128)(2,1)S(1)}, bf16[1024,256]{1,0:T(8,128)(2,1)S(1)}, f32[256,1024]{1,0:T(8,128)S(1)}, f32[1024,256]{1,0:T(8,128)S(1)},...) custom-call(bf16[256,2048]{1,0:T(8,128)(2,1)S(1)} %copy-done.1, bf16[2048,256]{1,0:T(8,128)(2,1)S(1)} %copy-done.3, ...), custom_call_target="tpu_custom_call" | custom-call | flops 2147483648 | tf_op jit(solution)/shard_map/other_goal/pallas_call | solution.py:37
  45.0 0.4 collective-permute-start.20
  45.4 0.2 collective-permute-start.21
  45.6 0.0 collective-permute-done.17.refs_0_
  45.6 0.0 collective-permute-done.18.refs_1_
  45.6 2.0 %finish.2 = (f32[256,2048]{1,0:T(8,128)}, f32[2048,256]{1,0:T(8,128)}, f32[256,2048]{1,0:T(8,128)}, f32[2048,256]{1,0:T(8,128)}) custom-call(bf16[256,1024]{1,0:T(8,128)(2,1)S(1)} %collective-permute-done.17.refs_0_, bf16[1024,256]{1,0:T(8,128)(2,1)S(1)} %collective-permute-done.18.refs_1_, ...), custom_call_target="tpu_custom_call", output_to_operand_aliasing={{0}: (4, {}), {1}: (5, {})} | custom-call | tf_op jit(solution)/shard_map/finish/pallas_call | solution.py:37
  47.6 0.0 collective-permute-done.20.refs_0_
  47.6 0.1 collective-permute-done.21.refs_1_
  47.7 1.4 %finish.3 = (f32[256,2048]{1,0:T(8,128)}, f32[2048,256]{1,0:T(8,128)}) custom-call(bf16[256,1024]{1,0:T(8,128)(2,1)S(1)} %collective-permute-done.20.refs_0_, bf16[1024,256]{1,0:T(8,128)(2,1)S(1)} %collective-permute-done.21.refs_1_, f32[256,2048]{1,0:T(8,128)} %get-tuple-element.72.refs_2_, ...), custom_call_target="tpu_custom_call", output_to_operand_aliasing={{0}: (2, {}), {1}: (3, {})} | custom-call | tf_op jit(solution)/shard_map/finish/pallas_call | solution.py:37
  (11 shorter events, 0.0 us)
Async XLA Ops:
  0.6 0.7 %copy-start.5 = (s32[256,1]{0,1:T(1,128)S(1)}, s32[256,1]{0,1:T(1,128)}, u32[]{:S(2)}) copy-start(s32[256,1]{0,1:T(1,128)} %param.9) | copy-start | bytes 3076
  0.6 0.7 %copy-start.6 = (s32[256]{0:T(256)S(1)}, s32[256]{0:T(256)}, u32[]{:S(2)}) copy-start(s32[256]{0:T(256)} %param.10) | copy-start | bytes 3076
  0.7 0.7 %copy-start.7 = (s32[256]{0:T(256)S(1)}, s32[256]{0:T(256)}, u32[]{:S(2)}) copy-start(s32[256]{0:T(256)} %param.11) | copy-start | bytes 3076
  0.7 0.9 %copy-start.4 = (bf16[256,256]{1,0:T(8,128)(2,1)S(1)}, bf16[256,256]{1,0:T(8,128)(2,1)}, u32[]{:S(2)}) copy-start(bf16[256,256]{1,0:T(8,128)(2,1)} %refs_1_.7) | copy-start | bytes 393220
  1.6 5.2 %copy-start = (bf16[256,2048]{1,0:T(8,128)(2,1)S(1)}, bf16[256,2048]{1,0:T(8,128)(2,1)}, u32[]{:S(2)}) copy-start(bf16[256,2048]{1,0:T(8,128)(2,1)} %refs_0_.10) | copy-start | bytes 3145732
  1.6 5.2 %copy-start.1 = (bf16[256,2048]{1,0:T(8,128)(2,1)S(1)}, bf16[256,2048]{1,0:T(8,128)(2,1)}, u32[]{:S(2)}) copy-start(bf16[256,2048]{1,0:T(8,128)(2,1)} %refs_0_.11) | copy-start | bytes 3145732
  1.6 5.2 %copy-start.2 = (bf16[2048,256]{1,0:T(8,128)(2,1)S(1)}, bf16[2048,256]{1,0:T(8,128)(2,1)}, u32[]{:S(2)}) copy-start(bf16[2048,256]{1,0:T(8,128)(2,1)} %refs_1_.12) | copy-start | bytes 3145732
  1.6 5.2 %copy-start.3 = (bf16[2048,256]{1,0:T(8,128)(2,1)S(1)}, bf16[2048,256]{1,0:T(8,128)(2,1)}, u32[]{:S(2)}) copy-start(bf16[2048,256]{1,0:T(8,128)(2,1)} %refs_1_.13) | copy-start | bytes 3145732
  1.6 8.9 %collective-permute-start.1 = (bf16[272,256]{1,0:T(8,128)(2,1)S(1)}, bf16[272,256]{1,0:T(8,128)(2,1)S(1)}, u32[]{:S(2)}, u32[]{:S(2)}) collective-permute-start(bf16[272,256]{1,0:T(8,128)(2,1)S(1)} %pack.1.x_ref.refs_0_), channel_id=1, source_target_pairs={{0,12},{4,8},{8,4},{12,0},{1,13},{5,9},{9,5},{13,1},{2,14},{6,10},... | collective-permute-start | bytes 417800 | tf_op jit(solution)/shard_map/ppermute | solution.py:318
  8.1 9.4 %collective-permute-start = (bf16[256,512]{1,0:T(8,128)(2,1)S(1)}, bf16[256,512]{1,0:T(8,128)(2,1)S(1)}, u32[]{:S(2)}, u32[]{:S(2)}) collective-permute-start(bf16[256,512]{1,0:T(8,128)(2,1)S(1)} %forward.3.a_ref), channel_id=1, source_target_pairs={{0,2},{2,0},{1,3},{3,1},{4,6},{6,4},{5,7},{7,5},{8,10},{10,8},{9,1... | collective-permute-start | bytes 786440 | tf_op jit(solution)/shard_map/ppermute | solution.py:321
  10.5 9.1 %collective-permute-start.2 = (bf16[272,256]{1,0:T(8,128)(2,1)S(1)}, bf16[272,256]{1,0:T(8,128)(2,1)S(1)}, u32[]{:S(2)}, u32[]{:S(2)}) collective-permute-start(bf16[272,256]{1,0:T(8,128)(2,1)S(1)} %pack.1.x_ref.refs_0_), channel_id=1, source_target_pairs={{0,8},{4,12},{8,0},{12,4},{1,9},{5,13},{9,1},{13,5},{2,10},{6,14},... | collective-permute-start | bytes 417800 | tf_op jit(solution)/shard_map/ppermute | solution.py:318
  15.5 8.4 %collective-permute-start.4 = (bf16[256,512]{1,0:T(8,128)(2,1)S(1)}, bf16[256,512]{1,0:T(8,128)(2,1)S(1)}, u32[]{:S(2)}, u32[]{:S(2)}) collective-permute-start(bf16[256,512]{1,0:T(8,128)(2,1)S(1)} %forward.5.a_ref), channel_id=1, source_target_pairs={{0,2},{2,0},{1,3},{3,1},{4,6},{6,4},{5,7},{7,5},{8,10},{10,8},{9,1... | collective-permute-start | bytes 786440 | tf_op jit(solution)/shard_map/ppermute | solution.py:321
  17.1 6.3 %collective-permute-start.6 = (bf16[272,256]{1,0:T(8,128)(2,1)S(1)}, bf16[272,256]{1,0:T(8,128)(2,1)S(1)}, u32[]{:S(2)}, u32[]{:S(2)}) collective-permute-start(bf16[272,256]{1,0:T(8,128)(2,1)S(1)} %pack.1.x_ref.refs_0_), channel_id=1, source_target_pairs={{0,4},{4,0},{8,12},{12,8},{1,5},{5,1},{9,13},{13,9},{2,6},{6,2},{1... | collective-permute-start | bytes 417800 | tf_op jit(solution)/shard_map/ppermute | solution.py:318
  17.6 5.8 %collective-permute-start.7 = (bf16[272,256]{1,0:T(8,128)(2,1)S(1)}, bf16[272,256]{1,0:T(8,128)(2,1)S(1)}, u32[]{:S(2)}, u32[]{:S(2)}) collective-permute-start(bf16[272,256]{1,0:T(8,128)(2,1)S(1)} %pack.1.x_ref.refs_0_), channel_id=1, source_target_pairs={{0,1},{1,0},{2,3},{3,2},{4,5},{5,4},{6,7},{7,6},{8,9},{9,8},{10,11... | collective-permute-start | bytes 417800 | tf_op jit(solution)/shard_map/ppermute | solution.py:321
  21.0 9.4 %collective-permute-start.5 = (bf16[256,512]{1,0:T(8,128)(2,1)S(1)}, bf16[256,512]{1,0:T(8,128)(2,1)S(1)}, u32[]{:S(2)}, u32[]{:S(2)}) collective-permute-start(bf16[256,512]{1,0:T(8,128)(2,1)S(1)} %forward.4.refs_2_), channel_id=1, source_target_pairs={{0,2},{2,0},{1,3},{3,1},{4,6},{6,4},{5,7},{7,5},{8,10},{10,8},{9,1... | collective-permute-start | bytes 786440 | tf_op jit(solution)/shard_map/ppermute | solution.py:321
  22.3 8.6 %collective-permute-start.3 = (bf16[256,512]{1,0:T(8,128)(2,1)S(1)}, bf16[256,512]{1,0:T(8,128)(2,1)S(1)}, u32[]{:S(2)}, u32[]{:S(2)}) collective-permute-start(bf16[256,512]{1,0:T(8,128)(2,1)S(1)} %both.2.refs_0_), channel_id=1, source_target_pairs={{0,4},{4,0},{8,12},{12,8},{1,5},{5,1},{9,13},{13,9},{2,6},{6,2},{1... | collective-permute-start | bytes 786440 | tf_op jit(solution)/shard_map/ppermute | solution.py:318
  23.4 1.4 %collective-permute-start.8 = (bf16[272,256]{1,0:T(8,128)(2,1)S(1)}, bf16[272,256]{1,0:T(8,128)(2,1)S(1)}, u32[]{:S(2)}, u32[]{:S(2)}) collective-permute-start(bf16[272,256]{1,0:T(8,128)(2,1)S(1)} %collective-permute-done.6.refs_1_), channel_id=1, source_target_pairs={{0,1},{1,0},{2,3},{3,2},{4,5},{5,4},{6,7},{7,6},{8,9},{9,8},{10,11... | collective-permute-start | bytes 417800 | tf_op jit(solution)/shard_map/ppermute | solution.py:321
  23.4 1.6 %collective-permute-start.10 = (bf16[272,256]{1,0:T(8,128)(2,1)S(1)}, bf16[272,256]{1,0:T(8,128)(2,1)S(1)}, u32[]{:S(2)}, u32[]{:S(2)}) collective-permute-start(bf16[272,256]{1,0:T(8,128)(2,1)S(1)} %collective-permute-done.1.x_ref.refs_3_), channel_id=1, source_target_pairs={{0,1},{1,0},{2,3},{3,2},{4,5},{5,4},{6,7},{7,6},{8,9},{9,8},{10,11... | collective-permute-start | bytes 417800 | tf_op jit(solution)/shard_map/ppermute | solution.py:321
  23.9 1.4 %collective-permute-start.9 = (bf16[272,256]{1,0:T(8,128)(2,1)S(1)}, bf16[272,256]{1,0:T(8,128)(2,1)S(1)}, u32[]{:S(2)}, u32[]{:S(2)}) collective-permute-start(bf16[272,256]{1,0:T(8,128)(2,1)S(1)} %collective-permute-done.2.x_ref.refs_2_), channel_id=1, source_target_pairs={{0,1},{1,0},{2,3},{3,2},{4,5},{5,4},{6,7},{7,6},{8,9},{9,8},{10,11... | collective-permute-start | bytes 417800 | tf_op jit(solution)/shard_map/ppermute | solution.py:321
  24.7 6.3 %collective-permute-start.11 = (bf16[256,512]{1,0:T(8,128)(2,1)S(1)}, bf16[256,512]{1,0:T(8,128)(2,1)S(1)}, u32[]{:S(2)}, u32[]{:S(2)}) collective-permute-start(bf16[256,512]{1,0:T(8,128)(2,1)S(1)} %both.2.refs_0_), channel_id=1, source_target_pairs={{0,1},{1,0},{2,3},{3,2},{4,5},{5,4},{6,7},{7,6},{8,9},{9,8},{10,11... | collective-permute-start | bytes 786440 | tf_op jit(solution)/shard_map/ppermute | solution.py:321
  24.9 7.1 %collective-permute-start.13 = (bf16[256,512]{1,0:T(8,128)(2,1)S(1)}, bf16[256,512]{1,0:T(8,128)(2,1)S(1)}, u32[]{:S(2)}, u32[]{:S(2)}) collective-permute-start(bf16[256,512]{1,0:T(8,128)(2,1)S(1)} %forward.4.refs_2_), channel_id=1, source_target_pairs={{0,1},{1,0},{2,3},{3,2},{4,5},{5,4},{6,7},{7,6},{8,9},{9,8},{10,11... | collective-permute-start | bytes 786440 | tf_op jit(solution)/shard_map/ppermute | solution.py:321
  25.3 5.8 %collective-permute-start.12 = (bf16[256,512]{1,0:T(8,128)(2,1)S(1)}, bf16[256,512]{1,0:T(8,128)(2,1)S(1)}, u32[]{:S(2)}, u32[]{:S(2)}) collective-permute-start(bf16[256,512]{1,0:T(8,128)(2,1)S(1)} %both.3.refs_3_), channel_id=1, source_target_pairs={{0,1},{1,0},{2,3},{3,2},{4,5},{5,4},{6,7},{7,6},{8,9},{9,8},{10,11... | collective-permute-start | bytes 786440 | tf_op jit(solution)/shard_map/ppermute | solution.py:321
  30.5 1.6 %collective-permute-start.14 = (bf16[256,512]{1,0:T(8,128)(2,1)S(1)}, bf16[256,512]{1,0:T(8,128)(2,1)S(1)}, u32[]{:S(2)}, u32[]{:S(2)}) collective-permute-start(bf16[256,512]{1,0:T(8,128)(2,1)S(1)} %collective-permute-done.5.refs_4_), channel_id=1, source_target_pairs={{0,1},{1,0},{2,3},{3,2},{4,5},{5,4},{6,7},{7,6},{8,9},{9,8},{10,11... | collective-permute-start | bytes 786440 | tf_op jit(solution)/shard_map/ppermute | solution.py:321
  30.8 1.6 %collective-permute-start.15 = (bf16[256,512]{1,0:T(8,128)(2,1)S(1)}, bf16[256,512]{1,0:T(8,128)(2,1)S(1)}, u32[]{:S(2)}, u32[]{:S(2)}) collective-permute-start(bf16[256,512]{1,0:T(8,128)(2,1)S(1)} %collective-permute-done.3.refs_1_), channel_id=1, source_target_pairs={{0,1},{1,0},{2,3},{3,2},{4,5},{5,4},{6,7},{7,6},{8,9},{9,8},{10,11... | collective-permute-start | bytes 786440 | tf_op jit(solution)/shard_map/ppermute | solution.py:321
  34.6 4.1 %collective-permute-start.16 = (bf16[1024,512]{1,0:T(8,128)(2,1)S(1)}, bf16[1024,512]{1,0:T(8,128)(2,1)S(1)}, u32[]{:S(2)}, u32[]{:S(2)}) collective-permute-start(bf16[1024,512]{1,0:T(8,128)(2,1)S(1)} %contrast.1.refs_2_), channel_id=1, source_target_pairs={{0,1},{1,0},{2,3},{3,2},{4,5},{5,4},{6,7},{7,6},{8,9},{9,8},{10,11... | collective-permute-start | bytes 3145736 | tf_op jit(solution)/shard_map/ppermute | solution.py:321
  35.0 7.0 %collective-permute-start.19 = (bf16[1024,256]{1,0:T(8,128)(2,1)S(1)}, bf16[1024,256]{1,0:T(8,128)(2,1)S(1)}, u32[]{:S(2)}, u32[]{:S(2)}) collective-permute-start(bf16[1024,256]{1,0:T(8,128)(2,1)S(1)} %get-tuple-element.51.refs_4_), channel_id=1, source_target_pairs={{0,1},{1,0},{2,3},{3,2},{4,5},{5,4},{6,7},{7,6},{8,9},{9,8},{10,11... | collective-permute-start | bytes 1572872 | tf_op jit(solution)/shard_map/ppermute | solution.py:321
  41.4 4.1 %collective-permute-start.17 = (bf16[256,1024]{1,0:T(8,128)(2,1)S(1)}, bf16[256,1024]{1,0:T(8,128)(2,1)S(1)}, u32[]{:S(2)}, u32[]{:S(2)}) collective-permute-start(bf16[256,1024]{1,0:T(8,128)(2,1)S(1)} %get-tuple-element.58), channel_id=1, source_target_pairs={{0,1},{1,0},{2,3},{3,2},{4,5},{5,4},{6,7},{7,6},{8,9},{9,8},{10,11... | collective-permute-start | bytes 1572872 | tf_op jit(solution)/shard_map/ppermute | solution.py:321
  41.8 3.8 %collective-permute-start.18 = (bf16[1024,256]{1,0:T(8,128)(2,1)S(1)}, bf16[1024,256]{1,0:T(8,128)(2,1)S(1)}, u32[]{:S(2)}, u32[]{:S(2)}) collective-permute-start(bf16[1024,256]{1,0:T(8,128)(2,1)S(1)} %get-tuple-element.59), channel_id=1, source_target_pairs={{0,1},{1,0},{2,3},{3,2},{4,5},{5,4},{6,7},{7,6},{8,9},{9,8},{10,11... | collective-permute-start | bytes 1572872 | tf_op jit(solution)/shard_map/ppermute | solution.py:321
  45.0 2.6 %collective-permute-start.20 = (bf16[256,1024]{1,0:T(8,128)(2,1)S(1)}, bf16[256,1024]{1,0:T(8,128)(2,1)S(1)}, u32[]{:S(2)}, u32[]{:S(2)}) collective-permute-start(bf16[256,1024]{1,0:T(8,128)(2,1)S(1)} %get-tuple-element.70), channel_id=1, source_target_pairs={{0,1},{1,0},{2,3},{3,2},{4,5},{5,4},{6,7},{7,6},{8,9},{9,8},{10,11... | collective-permute-start | bytes 1572872 | tf_op jit(solution)/shard_map/ppermute | solution.py:321
  45.4 2.3 %collective-permute-start.21 = (bf16[1024,256]{1,0:T(8,128)(2,1)S(1)}, bf16[1024,256]{1,0:T(8,128)(2,1)S(1)}, u32[]{:S(2)}, u32[]{:S(2)}) collective-permute-start(bf16[1024,256]{1,0:T(8,128)(2,1)S(1)} %get-tuple-element.71), channel_id=1, source_target_pairs={{0,1},{1,0},{2,3},{3,2},{4,5},{5,4},{6,7},{7,6},{8,9},{9,8},{10,11... | collective-permute-start | bytes 1572872 | tf_op jit(solution)/shard_map/ppermute | solution.py:321

commit v20 on v19

--- a/solution.py
+++ b/solution.py
@@ -236,10 +236,10 @@
     for k, (second_ref, x_ref) in enumerate(((ss, rows_ref), (gs, goals_ref))):
         second = second_ref[pl.ds(at, quarter), :]
         grad = grads_ref[:, k * emb : (k + 1) * emb]
+        outs[2 * k][...] = dot(hidden[2 * k][...], grad)
         for c in range(0, rows, 256):
             cols = slice(c, c + 256)
             back[:, cols] = (dot(second, grad[cols, :].T) * hidden[2 * k + 1][:, cols].astype(F32)).astype(BF)
-        outs[2 * k][...] = dot(hidden[2 * k][...], grad)
         outs[2 * k + 1][...] = dot(back[...], x_ref[...])
 
 

time: 49.4 us -> 49.8 us (level)
  no operation moved by 1% of the time
where the time goes in v20:
time: 49.8 us; the launch traced here: 49.6 us
  Pallas kernels  25.4 us (51%)
  starting transfers between devices  18.2 us (37%)
  waiting for transfers between devices  4.06 us (8%)
  between operations  0.99 us (2%)
  local copies, waits for them, and re-layouts  0.92 us (2%)
    pallas_call x15, Pallas kernels, kernel(): pl.pallas_call(body, in_specs=specs, out_specs=[HBM if i in hbm_out else...  25.4 us
    ppermute x4, starting transfers between devices, across(): return lax.ppermute(x, 'blk', [(i, i ^ k) for i in range(n_blk)])  10.3 us
    ppermute x18, starting transfers between devices, swap(): return lax.ppermute(x, axis, [(0, 1), (1, 0)])  7.87 us
    ppermute x4, waiting for transfers between devices, across(): return lax.ppermute(x, 'blk', [(i, i ^ k) for i in range(n_blk)])  2.86 us
    ppermute x18, waiting for transfers between devices, swap(): return lax.ppermute(x, axis, [(0, 1), (1, 0)])  1.2 us
  transfers between devices with their start and end apart: 22, of which 6 were waited for; matrix products, arithmetic and copies ran while one was open for 0% of the time, Pallas kernels for 44%

profile of v20, /device:TPU:0, one launch (start us, length us, event | category | flops | bytes accessed | tf_op | source)
XLA Modules:
  0.0 49.6 jit_solution(15551712981684482657)
XLA Ops:
  0.6 0.0 copy-start.5
  0.6 0.0 copy-start.6
  0.7 0.6 %copy-done.5 = s32[256,1]{0,1:T(1,128)S(1)} copy-done((s32[256,1]{0,1:T(1,128)S(1)}, s32[256,1]{0,1:T(1,128)}, u32[]{:S(2)}) %copy-start.5) | copy-done | bytes 1048
  1.3 0.0 copy-done.6
  1.3 0.0 copy-done.7
  1.3 0.2 copy-done.4
  1.6 5.1 %collective-permute-start.1 = (bf16[272,256]{1,0:T(8,128)(2,1)S(1)}, bf16[272,256]{1,0:T(8,128)(2,1)S(1)}, u32[]{:S(2)}, u32[]{:S(2)}) collective-permute-start(bf16[272,256]{1,0:T(8,128)(2,1)S(1)} %pack.1.x_ref.refs_0_), channel_id=1, source_target_pairs={{0,12},{4,8},{8,4},{12,0},{1,13},{5,9},{9,5},{13,1},{2,14},{6,10},... | collective-permute-start | bytes 417800 | tf_op jit(solution)/shard_map/ppermute | solution.py:318
  6.7 0.0 copy-done.1
  6.7 1.4 %forward.3.a_ref = bf16[256,512]{1,0:T(8,128)(2,1)S(1)} custom-call(bf16[272,256]{1,0:T(8,128)(2,1)S(1)} %pack.1.x_ref.refs_0_, bf16[256,2048]{1,0:T(8,128)(2,1)S(1)} %copy-done, bf16[256,2048]{1,0:T(8,128)(2,1)S(1)} %copy-done.1, bf16[2048,256]{1,0:T(8,128)(2,1)S(1)} %copy-done.2, bf16[2048,256]{1,0:T(8,128)(2,1)S(1)} %copy-done.3), custom_call_target="tpu_custom_call" | custom-call | tf_op jit(solution)/shard_map/forward/pallas_call | solution.py:37
  8.1 1.6 %collective-permute-start = (bf16[256,512]{1,0:T(8,128)(2,1)S(1)}, bf16[256,512]{1,0:T(8,128)(2,1)S(1)}, u32[]{:S(2)}, u32[]{:S(2)}) collective-permute-start(bf16[256,512]{1,0:T(8,128)(2,1)S(1)} %forward.3.a_ref), channel_id=1, source_target_pairs={{0,2},{2,0},{1,3},{3,1},{4,6},{6,4},{5,7},{7,5},{8,10},{10,8},{9,1... | collective-permute-start | bytes 786440 | tf_op jit(solution)/shard_map/ppermute | solution.py:321
  9.7 0.8 %collective-permute-done.1.x_ref.refs_3_ = bf16[272,256]{1,0:T(8,128)(2,1)S(1)} collective-permute-done((bf16[272,256]{1,0:T(8,128)(2,1)S(1)}, bf16[272,256]{1,0:T(8,128)(2,1)S(1)}, u32[]{:S(2)}, u32[]{:S(2)}) %collective-permute-start.1) | collective-permute-done | bytes 139296 | tf_op jit(solution)/shard_map/ppermute | solution.py:318
  10.5 3.6 %collective-permute-start.2 = (bf16[272,256]{1,0:T(8,128)(2,1)S(1)}, bf16[272,256]{1,0:T(8,128)(2,1)S(1)}, u32[]{:S(2)}, u32[]{:S(2)}) collective-permute-start(bf16[272,256]{1,0:T(8,128)(2,1)S(1)} %pack.1.x_ref.refs_0_), channel_id=1, source_target_pairs={{0,8},{4,12},{8,0},{12,4},{1,9},{5,13},{9,1},{13,5},{2,10},{6,14},... | collective-permute-start | bytes 417800 | tf_op jit(solution)/shard_map/ppermute | solution.py:318
  14.1 1.4 %forward.5.a_ref = bf16[256,512]{1,0:T(8,128)(2,1)S(1)} custom-call(bf16[272,256]{1,0:T(8,128)(2,1)S(1)} %collective-permute-done.1.x_ref.refs_3_, bf16[256,2048]{1,0:T(8,128)(2,1)S(1)} %copy-done, bf16[256,2048]{1,0:T(8,128)(2,1)S(1)} %copy-done.1, bf16[2048,256]{1,0:T(8,128)(2,1)S(1)} %copy-done.2, bf16[2048,256]{1,0:T(8,128)(2,1)S(1)} %copy-done.3), custom_call_target="tpu_custom_call" | custom-call | tf_op jit(solution)/shard_map/forward/pallas_call | solution.py:37
  15.5 1.6 %collective-permute-start.4 = (bf16[256,512]{1,0:T(8,128)(2,1)S(1)}, bf16[256,512]{1,0:T(8,128)(2,1)S(1)}, u32[]{:S(2)}, u32[]{:S(2)}) collective-permute-start(bf16[256,512]{1,0:T(8,128)(2,1)S(1)} %forward.5.a_ref), channel_id=1, source_target_pairs={{0,2},{2,0},{1,3},{3,1},{4,6},{6,4},{5,7},{7,5},{8,10},{10,8},{9,1... | collective-permute-start | bytes 786440 | tf_op jit(solution)/shard_map/ppermute | solution.py:321
  17.1 0.5 %collective-permute-start.6 = (bf16[272,256]{1,0:T(8,128)(2,1)S(1)}, bf16[272,256]{1,0:T(8,128)(2,1)S(1)}, u32[]{:S(2)}, u32[]{:S(2)}) collective-permute-start(bf16[272,256]{1,0:T(8,128)(2,1)S(1)} %pack.1.x_ref.refs_0_), channel_id=1, source_target_pairs={{0,4},{4,0},{8,12},{12,8},{1,5},{5,1},{9,13},{13,9},{2,6},{6,2},{1... | collective-permute-start | bytes 417800 | tf_op jit(solution)/shard_map/ppermute | solution.py:318
  17.6 0.0 collective-permute-start.7
  17.6 0.0 collective-permute-done.b_ref
  17.6 0.1 both.2.refs_0_
  17.6 2.0 %collective-permute-done.2.x_ref.refs_2_ = bf16[272,256]{1,0:T(8,128)(2,1)S(1)} collective-permute-done((bf16[272,256]{1,0:T(8,128)(2,1)S(1)}, bf16[272,256]{1,0:T(8,128)(2,1)S(1)}, u32[]{:S(2)}, u32[]{:S(2)}) %collective-permute-start.2) | collective-permute-done | bytes 139296 | tf_op jit(solution)/shard_map/ppermute | solution.py:318
  19.7 1.4 %forward.4.refs_2_ = bf16[256,512]{1,0:T(8,128)(2,1)S(1)} custom-call(bf16[272,256]{1,0:T(8,128)(2,1)S(1)} %collective-permute-done.2.x_ref.refs_2_, bf16[256,2048]{1,0:T(8,128)(2,1)S(1)} %copy-done, bf16[256,2048]{1,0:T(8,128)(2,1)S(1)} %copy-done.1, bf16[2048,256]{1,0:T(8,128)(2,1)S(1)} %copy-done.2, bf16[2048,256]{1,0:T(8,128)(2,1)S(1)} %copy-done.3), custom_call_target="tpu_custom_call" | custom-call | tf_op jit(solution)/shard_map/forward/pallas_call | solution.py:37
  21.0 1.2 %collective-permute-start.5 = (bf16[256,512]{1,0:T(8,128)(2,1)S(1)}, bf16[256,512]{1,0:T(8,128)(2,1)S(1)}, u32[]{:S(2)}, u32[]{:S(2)}) collective-permute-start(bf16[256,512]{1,0:T(8,128)(2,1)S(1)} %forward.4.refs_2_), channel_id=1, source_target_pairs={{0,2},{2,0},{1,3},{3,1},{4,6},{6,4},{5,7},{7,5},{8,10},{10,8},{9,1... | collective-permute-start | bytes 786440 | tf_op jit(solution)/shard_map/ppermute | solution.py:321
  22.3 1.1 %collective-permute-start.3 = (bf16[256,512]{1,0:T(8,128)(2,1)S(1)}, bf16[256,512]{1,0:T(8,128)(2,1)S(1)}, u32[]{:S(2)}, u32[]{:S(2)}) collective-permute-start(bf16[256,512]{1,0:T(8,128)(2,1)S(1)} %both.2.refs_0_), channel_id=1, source_target_pairs={{0,4},{4,0},{8,12},{12,8},{1,5},{5,1},{9,13},{13,9},{2,6},{6,2},{1... | collective-permute-start | bytes 786440 | tf_op jit(solution)/shard_map/ppermute | solution.py:318
  23.4 0.0 collective-permute-done.6.refs_1_
  23.4 0.0 collective-permute-start.8
  23.4 0.0 collective-permute-done.7.refs_4_
  23.4 0.5 %collective-permute-start.10 = (bf16[272,256]{1,0:T(8,128)(2,1)S(1)}, bf16[272,256]{1,0:T(8,128)(2,1)S(1)}, u32[]{:S(2)}, u32[]{:S(2)}) collective-permute-start(bf16[272,256]{1,0:T(8,128)(2,1)S(1)} %collective-permute-done.1.x_ref.refs_3_), channel_id=1, source_target_pairs={{0,1},{1,0},{2,3},{3,2},{4,5},{5,4},{6,7},{7,6},{8,9},{9,8},{10,11... | collective-permute-start | bytes 417800 | tf_op jit(solution)/shard_map/ppermute | solution.py:321
  23.9 0.0 collective-permute-done.4.b_ref
  23.9 0.1 collective-permute-start.9
  24.0 0.1 both.3.refs_3_
  24.0 0.7 %collective-permute-done.8.refs_5_ = bf16[272,256]{1,0:T(8,128)(2,1)S(1)} collective-permute-done((bf16[272,256]{1,0:T(8,128)(2,1)S(1)}, bf16[272,256]{1,0:T(8,128)(2,1)S(1)}, u32[]{:S(2)}, u32[]{:S(2)}) %collective-permute-start.8) | collective-permute-done | bytes 139296 | tf_op jit(solution)/shard_map/ppermute | solution.py:321
  24.7 0.1 collective-permute-start.11
  24.9 0.1 collective-permute-done.10.refs_7_
  24.9 0.3 collective-permute-start.13
  25.3 0.0 collective-permute-done.9.refs_6_
  25.3 0.2 collective-permute-start.12
  25.5 5.0 %arrange.1 = (bf16[1024,256]{1,0:T(8,128)(2,1)S(1)}, bf16[1024,256]{1,0:T(8,128)(2,1)S(1)}, bf16[1024,256]{1,0:T(8,128)(2,1)S(1)}, bf16[1024,2048]{1,0:T(8,128)(...) custom-call(bf16[272,256]{1,0:T(8,128)(2,1)S(1)} %pack.1.x_ref.refs_, ...), custom_call_target="tpu_custom_call" | custom-call | tf_op jit(solution)/shard_map/arrange/pallas_call | solution.py:37
  30.5 0.0 collective-permute-done.5.refs_4_
  30.5 0.4 collective-permute-start.14
  30.8 0.0 collective-permute-done.3.refs_1_
  30.8 0.2 collective-permute-start.15
  31.0 0.0 collective-permute-done.11.refs_5_
  31.0 0.0 collective-permute-done.12.refs_6_
  31.0 1.0 %gather.1 = (bf16[1024,256]{1,0:T(8,128)(2,1)S(1)}, f32[1024,256]{1,0:T(8,128)S(1)}) custom-call(bf16[256,512]{1,0:T(8,128)(2,1)S(1)} %both.2.refs_0_, bf16[256,512]{1,0:T(8,128)(2,1)S(1)} %collective-permute-done.3.refs_1_, bf16[256,512]{1,0:T(8,128)(2,1)S(1)} %forward.4.refs_2_, bf16[256,512]{1,0:T(8,128)(2,1)S(1)} %both.3.refs_3_, ...), custom_call_target="tpu_custom_call" | custom-call | tf_op jit(solution)/shard_map/gather/pallas_call | solution.py:37
  32.1 0.0 collective-permute-done.13.part_ref
  32.1 0.0 collective-permute-done.14.there_ref
  32.1 0.3 collective-permute-done.15.sums_ref
  32.4 2.2 %contrast.1.refs_2_ = bf16[1024,512]{1,0:T(8,128)(2,1)S(1)} custom-call(bf16[1024,256]{1,0:T(8,128)(2,1)S(1)} %get-tuple-element.46.phi_ref, f32[1024,256]{1,0:T(8,128)S(1)} %get-tuple-element.47.psi_ref, bf16[256,512]{1,0:T(8,128)(2,1)S(1)} %collective-permute-done.13.part_ref, bf16[256,512]{1,0:T(8,128)(2,1)S(1)} %collective-permute-done.14.there_ref, ...), custom_call_target="tpu_custom_call" | custom-call | tf_op jit(solution)/shard_map/contrast/pallas_call | solution.py:37
  34.6 0.4 collective-permute-start.16
  35.0 0.2 collective-permute-start.19
  35.2 3.8 %mine.1 = (f32[1024,256]{1,0:T(8,128)S(1)}, f32[1024,256]{1,0:T(8,128)S(1)}, f32[1024,256]{1,0:T(8,128)S(1)}, f32[1024,256]{1,0:T(8,128)S(1)}) custom-call(bf16[2048,256]{1,0:T(8,128)(2,1)S(1)} %copy-done.2, bf16[2048,256]{1,0:T(8,128)(2,1)S(1)} %copy-done.3, bf16[1024,512]{1,0:T(8,128)(2,1)S(1)} %contrast.1.refs_2_, ...), custom_call_target="tpu_custom_call" | custom-call | flops 4294967296 | tf_op jit(solution)/shard_map/mine/pallas_call | solution.py:37
  39.0 0.0 collective-permute-done.16.refs_2_
  39.0 2.7 %other_state.1 = (bf16[256,1024]{1,0:T(8,128)(2,1)S(1)}, bf16[1024,256]{1,0:T(8,128)(2,1)S(1)}, f32[256,1024]{1,0:T(8,128)S(1)}, f32[1024,256]{1,0:T(8,128)S(1)}) custom-call(bf16[256,2048]{1,0:T(8,128)(2,1)S(1)} %copy-done, bf16[2048,256]{1,0:T(8,128)(2,1)S(1)} %copy-done.2, bf16[1024,512]{1,0:T(8,128)(2,1)S(1)} %collective-permute-done.16.refs_2_, ...), custom_call_target="tpu_custom_call" | custom-call | flops 2147483648 | tf_op jit(solution)/shard_map/other_state/pallas_call | solution.py:37
  41.8 0.4 collective-permute-start.17
  42.1 0.2 collective-permute-start.18
  42.3 0.0 collective-permute-done.19.refs_3_
  42.3 3.0 %other_goal.1 = (bf16[256,1024]{1,0:T(8,128)(2,1)S(1)}, bf16[1024,256]{1,0:T(8,128)(2,1)S(1)}, f32[256,1024]{1,0:T(8,128)S(1)}, f32[1024,256]{1,0:T(8,128)S(1)},...) custom-call(bf16[256,2048]{1,0:T(8,128)(2,1)S(1)} %copy-done.1, bf16[2048,256]{1,0:T(8,128)(2,1)S(1)} %copy-done.3, ...), custom_call_target="tpu_custom_call" | custom-call | flops 2147483648 | tf_op jit(solution)/shard_map/other_goal/pallas_call | solution.py:37
  45.3 0.4 collective-permute-start.20
  45.7 0.2 collective-permute-start.21
  45.9 0.0 collective-permute-done.17.refs_0_
  45.9 0.0 collective-permute-done.18.refs_1_
  45.9 2.0 %finish.2 = (f32[256,2048]{1,0:T(8,128)}, f32[2048,256]{1,0:T(8,128)}, f32[256,2048]{1,0:T(8,128)}, f32[2048,256]{1,0:T(8,128)}) custom-call(bf16[256,1024]{1,0:T(8,128)(2,1)S(1)} %collective-permute-done.17.refs_0_, bf16[1024,256]{1,0:T(8,128)(2,1)S(1)} %collective-permute-done.18.refs_1_, ...), custom_call_target="tpu_custom_call", output_to_operand_aliasing={{0}: (4, {}), {1}: (5, {})} | custom-call | tf_op jit(solution)/shard_map/finish/pallas_call | solution.py:37
  48.0 0.0 collective-permute-done.20.refs_0_
  48.0 0.1 collective-permute-done.21.refs_1_
  48.0 1.4 %finish.3 = (f32[256,2048]{1,0:T(8,128)}, f32[2048,256]{1,0:T(8,128)}) custom-call(bf16[256,1024]{1,0:T(8,128)(2,1)S(1)} %collective-permute-done.20.refs_0_, bf16[1024,256]{1,0:T(8,128)(2,1)S(1)} %collective-permute-done.21.refs_1_, f32[256,2048]{1,0:T(8,128)} %get-tuple-element.72.refs_2_, ...), custom_call_target="tpu_custom_call", output_to_operand_aliasing={{0}: (2, {}), {1}: (3, {})} | custom-call | tf_op jit(solution)/shard_map/finish/pallas_call | solution.py:37
  (11 shorter events, 0.0 us)
Async XLA Ops:
  0.6 0.7 %copy-start.5 = (s32[256,1]{0,1:T(1,128)S(1)}, s32[256,1]{0,1:T(1,128)}, u32[]{:S(2)}) copy-start(s32[256,1]{0,1:T(1,128)} %param.9) | copy-start | bytes 3076
  0.6 0.7 %copy-start.6 = (s32[256]{0:T(256)S(1)}, s32[256]{0:T(256)}, u32[]{:S(2)}) copy-start(s32[256]{0:T(256)} %param.10) | copy-start | bytes 3076
  0.7 0.7 %copy-start.7 = (s32[256]{0:T(256)S(1)}, s32[256]{0:T(256)}, u32[]{:S(2)}) copy-start(s32[256]{0:T(256)} %param.11) | copy-start | bytes 3076
  0.7 0.9 %copy-start.4 = (bf16[256,256]{1,0:T(8,128)(2,1)S(1)}, bf16[256,256]{1,0:T(8,128)(2,1)}, u32[]{:S(2)}) copy-start(bf16[256,256]{1,0:T(8,128)(2,1)} %refs_1_.7) | copy-start | bytes 393220
  1.6 5.2 %copy-start = (bf16[256,2048]{1,0:T(8,128)(2,1)S(1)}, bf16[256,2048]{1,0:T(8,128)(2,1)}, u32[]{:S(2)}) copy-start(bf16[256,2048]{1,0:T(8,128)(2,1)} %refs_0_.10) | copy-start | bytes 3145732
  1.6 5.2 %copy-start.1 = (bf16[256,2048]{1,0:T(8,128)(2,1)S(1)}, bf16[256,2048]{1,0:T(8,128)(2,1)}, u32[]{:S(2)}) copy-start(bf16[256,2048]{1,0:T(8,128)(2,1)} %refs_0_.11) | copy-start | bytes 3145732
  1.6 5.2 %copy-start.2 = (bf16[2048,256]{1,0:T(8,128)(2,1)S(1)}, bf16[2048,256]{1,0:T(8,128)(2,1)}, u32[]{:S(2)}) copy-start(bf16[2048,256]{1,0:T(8,128)(2,1)} %refs_1_.12) | copy-start | bytes 3145732
  1.6 5.2 %copy-start.3 = (bf16[2048,256]{1,0:T(8,128)(2,1)S(1)}, bf16[2048,256]{1,0:T(8,128)(2,1)}, u32[]{:S(2)}) copy-start(bf16[2048,256]{1,0:T(8,128)(2,1)} %refs_1_.13) | copy-start | bytes 3145732
  1.6 8.9 %collective-permute-start.1 = (bf16[272,256]{1,0:T(8,128)(2,1)S(1)}, bf16[272,256]{1,0:T(8,128)(2,1)S(1)}, u32[]{:S(2)}, u32[]{:S(2)}) collective-permute-start(bf16[272,256]{1,0:T(8,128)(2,1)S(1)} %pack.1.x_ref.refs_0_), channel_id=1, source_target_pairs={{0,12},{4,8},{8,4},{12,0},{1,13},{5,9},{9,5},{13,1},{2,14},{6,10},... | collective-permute-start | bytes 417800 | tf_op jit(solution)/shard_map/ppermute | solution.py:318
  8.1 9.4 %collective-permute-start = (bf16[256,512]{1,0:T(8,128)(2,1)S(1)}, bf16[256,512]{1,0:T(8,128)(2,1)S(1)}, u32[]{:S(2)}, u32[]{:S(2)}) collective-permute-start(bf16[256,512]{1,0:T(8,128)(2,1)S(1)} %forward.3.a_ref), channel_id=1, source_target_pairs={{0,2},{2,0},{1,3},{3,1},{4,6},{6,4},{5,7},{7,5},{8,10},{10,8},{9,1... | collective-permute-start | bytes 786440 | tf_op jit(solution)/shard_map/ppermute | solution.py:321
  10.5 9.1 %collective-permute-start.2 = (bf16[272,256]{1,0:T(8,128)(2,1)S(1)}, bf16[272,256]{1,0:T(8,128)(2,1)S(1)}, u32[]{:S(2)}, u32[]{:S(2)}) collective-permute-start(bf16[272,256]{1,0:T(8,128)(2,1)S(1)} %pack.1.x_ref.refs_0_), channel_id=1, source_target_pairs={{0,8},{4,12},{8,0},{12,4},{1,9},{5,13},{9,1},{13,5},{2,10},{6,14},... | collective-permute-start | bytes 417800 | tf_op jit(solution)/shard_map/ppermute | solution.py:318
  15.5 8.4 %collective-permute-start.4 = (bf16[256,512]{1,0:T(8,128)(2,1)S(1)}, bf16[256,512]{1,0:T(8,128)(2,1)S(1)}, u32[]{:S(2)}, u32[]{:S(2)}) collective-permute-start(bf16[256,512]{1,0:T(8,128)(2,1)S(1)} %forward.5.a_ref), channel_id=1, source_target_pairs={{0,2},{2,0},{1,3},{3,1},{4,6},{6,4},{5,7},{7,5},{8,10},{10,8},{9,1... | collective-permute-start | bytes 786440 | tf_op jit(solution)/shard_map/ppermute | solution.py:321
  17.1 6.3 %collective-permute-start.6 = (bf16[272,256]{1,0:T(8,128)(2,1)S(1)}, bf16[272,256]{1,0:T(8,128)(2,1)S(1)}, u32[]{:S(2)}, u32[]{:S(2)}) collective-permute-start(bf16[272,256]{1,0:T(8,128)(2,1)S(1)} %pack.1.x_ref.refs_0_), channel_id=1, source_target_pairs={{0,4},{4,0},{8,12},{12,8},{1,5},{5,1},{9,13},{13,9},{2,6},{6,2},{1... | collective-permute-start | bytes 417800 | tf_op jit(solution)/shard_map/ppermute | solution.py:318
  17.6 5.8 %collective-permute-start.7 = (bf16[272,256]{1,0:T(8,128)(2,1)S(1)}, bf16[272,256]{1,0:T(8,128)(2,1)S(1)}, u32[]{:S(2)}, u32[]{:S(2)}) collective-permute-start(bf16[272,256]{1,0:T(8,128)(2,1)S(1)} %pack.1.x_ref.refs_0_), channel_id=1, source_target_pairs={{0,1},{1,0},{2,3},{3,2},{4,5},{5,4},{6,7},{7,6},{8,9},{9,8},{10,11... | collective-permute-start | bytes 417800 | tf_op jit(solution)/shard_map/ppermute | solution.py:321
  21.0 9.4 %collective-permute-start.5 = (bf16[256,512]{1,0:T(8,128)(2,1)S(1)}, bf16[256,512]{1,0:T(8,128)(2,1)S(1)}, u32[]{:S(2)}, u32[]{:S(2)}) collective-permute-start(bf16[256,512]{1,0:T(8,128)(2,1)S(1)} %forward.4.refs_2_), channel_id=1, source_target_pairs={{0,2},{2,0},{1,3},{3,1},{4,6},{6,4},{5,7},{7,5},{8,10},{10,8},{9,1... | collective-permute-start | bytes 786440 | tf_op jit(solution)/shard_map/ppermute | solution.py:321
  22.3 8.6 %collective-permute-start.3 = (bf16[256,512]{1,0:T(8,128)(2,1)S(1)}, bf16[256,512]{1,0:T(8,128)(2,1)S(1)}, u32[]{:S(2)}, u32[]{:S(2)}) collective-permute-start(bf16[256,512]{1,0:T(8,128)(2,1)S(1)} %both.2.refs_0_), channel_id=1, source_target_pairs={{0,4},{4,0},{8,12},{12,8},{1,5},{5,1},{9,13},{13,9},{2,6},{6,2},{1... | collective-permute-start | bytes 786440 | tf_op jit(solution)/shard_map/ppermute | solution.py:318
  23.4 1.4 %collective-permute-start.8 = (bf16[272,256]{1,0:T(8,128)(2,1)S(1)}, bf16[272,256]{1,0:T(8,128)(2,1)S(1)}, u32[]{:S(2)}, u32[]{:S(2)}) collective-permute-start(bf16[272,256]{1,0:T(8,128)(2,1)S(1)} %collective-permute-done.6.refs_1_), channel_id=1, source_target_pairs={{0,1},{1,0},{2,3},{3,2},{4,5},{5,4},{6,7},{7,6},{8,9},{9,8},{10,11... | collective-permute-start | bytes 417800 | tf_op jit(solution)/shard_map/ppermute | solution.py:321
  23.4 1.6 %collective-permute-start.10 = (bf16[272,256]{1,0:T(8,128)(2,1)S(1)}, bf16[272,256]{1,0:T(8,128)(2,1)S(1)}, u32[]{:S(2)}, u32[]{:S(2)}) collective-permute-start(bf16[272,256]{1,0:T(8,128)(2,1)S(1)} %collective-permute-done.1.x_ref.refs_3_), channel_id=1, source_target_pairs={{0,1},{1,0},{2,3},{3,2},{4,5},{5,4},{6,7},{7,6},{8,9},{9,8},{10,11... | collective-permute-start | bytes 417800 | tf_op jit(solution)/shard_map/ppermute | solution.py:321
  23.9 1.4 %collective-permute-start.9 = (bf16[272,256]{1,0:T(8,128)(2,1)S(1)}, bf16[272,256]{1,0:T(8,128)(2,1)S(1)}, u32[]{:S(2)}, u32[]{:S(2)}) collective-permute-start(bf16[272,256]{1,0:T(8,128)(2,1)S(1)} %collective-permute-done.2.x_ref.refs_2_), channel_id=1, source_target_pairs={{0,1},{1,0},{2,3},{3,2},{4,5},{5,4},{6,7},{7,6},{8,9},{9,8},{10,11... | collective-permute-start | bytes 417800 | tf_op jit(solution)/shard_map/ppermute | solution.py:321
  24.7 6.3 %collective-permute-start.11 = (bf16[256,512]{1,0:T(8,128)(2,1)S(1)}, bf16[256,512]{1,0:T(8,128)(2,1)S(1)}, u32[]{:S(2)}, u32[]{:S(2)}) collective-permute-start(bf16[256,512]{1,0:T(8,128)(2,1)S(1)} %both.2.refs_0_), channel_id=1, source_target_pairs={{0,1},{1,0},{2,3},{3,2},{4,5},{5,4},{6,7},{7,6},{8,9},{9,8},{10,11... | collective-permute-start | bytes 786440 | tf_op jit(solution)/shard_map/ppermute | solution.py:321
  24.9 7.1 %collective-permute-start.13 = (bf16[256,512]{1,0:T(8,128)(2,1)S(1)}, bf16[256,512]{1,0:T(8,128)(2,1)S(1)}, u32[]{:S(2)}, u32[]{:S(2)}) collective-permute-start(bf16[256,512]{1,0:T(8,128)(2,1)S(1)} %forward.4.refs_2_), channel_id=1, source_target_pairs={{0,1},{1,0},{2,3},{3,2},{4,5},{5,4},{6,7},{7,6},{8,9},{9,8},{10,11... | collective-permute-start | bytes 786440 | tf_op jit(solution)/shard_map/ppermute | solution.py:321
  25.3 5.8 %collective-permute-start.12 = (bf16[256,512]{1,0:T(8,128)(2,1)S(1)}, bf16[256,512]{1,0:T(8,128)(2,1)S(1)}, u32[]{:S(2)}, u32[]{:S(2)}) collective-permute-start(bf16[256,512]{1,0:T(8,128)(2,1)S(1)} %both.3.refs_3_), channel_id=1, source_target_pairs={{0,1},{1,0},{2,3},{3,2},{4,5},{5,4},{6,7},{7,6},{8,9},{9,8},{10,11... | collective-permute-start | bytes 786440 | tf_op jit(solution)/shard_map/ppermute | solution.py:321
  30.5 1.6 %collective-permute-start.14 = (bf16[256,512]{1,0:T(8,128)(2,1)S(1)}, bf16[256,512]{1,0:T(8,128)(2,1)S(1)}, u32[]{:S(2)}, u32[]{:S(2)}) collective-permute-start(bf16[256,512]{1,0:T(8,128)(2,1)S(1)} %collective-permute-done.5.refs_4_), channel_id=1, source_target_pairs={{0,1},{1,0},{2,3},{3,2},{4,5},{5,4},{6,7},{7,6},{8,9},{9,8},{10,11... | collective-permute-start | bytes 786440 | tf_op jit(solution)/shard_map/ppermute | solution.py:321
  30.8 1.6 %collective-permute-start.15 = (bf16[256,512]{1,0:T(8,128)(2,1)S(1)}, bf16[256,512]{1,0:T(8,128)(2,1)S(1)}, u32[]{:S(2)}, u32[]{:S(2)}) collective-permute-start(bf16[256,512]{1,0:T(8,128)(2,1)S(1)} %collective-permute-done.3.refs_1_), channel_id=1, source_target_pairs={{0,1},{1,0},{2,3},{3,2},{4,5},{5,4},{6,7},{7,6},{8,9},{9,8},{10,11... | collective-permute-start | bytes 786440 | tf_op jit(solution)/shard_map/ppermute | solution.py:321
  34.6 4.4 %collective-permute-start.16 = (bf16[1024,512]{1,0:T(8,128)(2,1)S(1)}, bf16[1024,512]{1,0:T(8,128)(2,1)S(1)}, u32[]{:S(2)}, u32[]{:S(2)}) collective-permute-start(bf16[1024,512]{1,0:T(8,128)(2,1)S(1)} %contrast.1.refs_2_), channel_id=1, source_target_pairs={{0,1},{1,0},{2,3},{3,2},{4,5},{5,4},{6,7},{7,6},{8,9},{9,8},{10,11... | collective-permute-start | bytes 3145736 | tf_op jit(solution)/shard_map/ppermute | solution.py:321
  35.0 7.3 %collective-permute-start.19 = (bf16[1024,256]{1,0:T(8,128)(2,1)S(1)}, bf16[1024,256]{1,0:T(8,128)(2,1)S(1)}, u32[]{:S(2)}, u32[]{:S(2)}) collective-permute-start(bf16[1024,256]{1,0:T(8,128)(2,1)S(1)} %get-tuple-element.51.refs_4_), channel_id=1, source_target_pairs={{0,1},{1,0},{2,3},{3,2},{4,5},{5,4},{6,7},{7,6},{8,9},{9,8},{10,11... | collective-permute-start | bytes 1572872 | tf_op jit(solution)/shard_map/ppermute | solution.py:321
  41.8 4.1 %collective-permute-start.17 = (bf16[256,1024]{1,0:T(8,128)(2,1)S(1)}, bf16[256,1024]{1,0:T(8,128)(2,1)S(1)}, u32[]{:S(2)}, u32[]{:S(2)}) collective-permute-start(bf16[256,1024]{1,0:T(8,128)(2,1)S(1)} %get-tuple-element.58), channel_id=1, source_target_pairs={{0,1},{1,0},{2,3},{3,2},{4,5},{5,4},{6,7},{7,6},{8,9},{9,8},{10,11... | collective-permute-start | bytes 1572872 | tf_op jit(solution)/shard_map/ppermute | solution.py:321
  42.1 3.8 %collective-permute-start.18 = (bf16[1024,256]{1,0:T(8,128)(2,1)S(1)}, bf16[1024,256]{1,0:T(8,128)(2,1)S(1)}, u32[]{:S(2)}, u32[]{:S(2)}) collective-permute-start(bf16[1024,256]{1,0:T(8,128)(2,1)S(1)} %get-tuple-element.59), channel_id=1, source_target_pairs={{0,1},{1,0},{2,3},{3,2},{4,5},{5,4},{6,7},{7,6},{8,9},{9,8},{10,11... | collective-permute-start | bytes 1572872 | tf_op jit(solution)/shard_map/ppermute | solution.py:321
  45.3 2.6 %collective-permute-start.20 = (bf16[256,1024]{1,0:T(8,128)(2,1)S(1)}, bf16[256,1024]{1,0:T(8,128)(2,1)S(1)}, u32[]{:S(2)}, u32[]{:S(2)}) collective-permute-start(bf16[256,1024]{1,0:T(8,128)(2,1)S(1)} %get-tuple-element.70), channel_id=1, source_target_pairs={{0,1},{1,0},{2,3},{3,2},{4,5},{5,4},{6,7},{7,6},{8,9},{9,8},{10,11... | collective-permute-start | bytes 1572872 | tf_op jit(solution)/shard_map/ppermute | solution.py:321
  45.7 2.3 %collective-permute-start.21 = (bf16[1024,256]{1,0:T(8,128)(2,1)S(1)}, bf16[1024,256]{1,0:T(8,128)(2,1)S(1)}, u32[]{:S(2)}, u32[]{:S(2)}) collective-permute-start(bf16[1024,256]{1,0:T(8,128)(2,1)S(1)} %get-tuple-element.71), channel_id=1, source_target_pairs={{0,1},{1,0},{2,3},{3,2},{4,5},{5,4},{6,7},{7,6},{8,9},{9,8},{10,11... | collective-permute-start | bytes 1572872 | tf_op jit(solution)/shard_map/ppermute | solution.py:321
